TPU v7x, 32 devices: a whole 2x2x4 slice. The times are simulated.
32 devices in a mesh: row: 8 (over z, y), col: 4 (over x, core).
Axes of the slice: x: 2, y: 2, z: 4, core: 2. Of those that a mesh axis runs over, the one named last changes fastest.
Arguments:
- rhs: float32 [2, 8, 1024, 128], P(None, 'row'), may hold values from -6 to 6
- diag_inv: bfloat16 [4, 1024, 1024], P(None, 'row'), as said below
- blocks: bfloat16 [1, 4, 8, 1, 1024, 1024], P(None, 'col', 'row'), may hold values from -0.09375 to 0.09375
- block_rows: int32 [1, 4, 8, 1], P(None, 'col', 'row'), may hold values from 0 to 1, as said below
- counts: int32 [1, 4, 8], P(None, 'col', 'row'), may hold values from 0 to 1, as said below
Outputs:
- solved: float32 [1, 4, 1024, 128], P(None, 'col')
- remainder: float32 [2, 8, 1024, 128], P(None, 'row')
Inputs may be any that keep to these rules, and one draw needn't show every extreme that they name: `diag_inv`: lower triangular. `block_rows`: the 1 entries of one list are different; for row indices r below 4, slot 0 lists local block row 0. `counts`: 1 is reached in every draw; for row indices r below 4 the count is 1.
All inputs are finite; a program needn't handle non-finite values.
Results may differ from a plain program's by a relative error of at most 0.0041.
Values may be sent and summed in bfloat16 or wider, within the bound.
No kernel may reach another device: no remote copies, remote signals or barrier semaphores. Data moves between devices by JAX's collectives and lax.ppermute only.
A program may use at most 64 MiB of HBM per device.

v0:
```python
import jax
import jax.numpy as jnp
from jax import lax
from jax.sharding import PartitionSpec as P


def broadcast(value, axis, root):
    mine = lax.axis_index(axis) == root
    return lax.psum(jnp.where(mine, value, jnp.zeros_like(value)), axis)


def on_device(rhs, diag_inv, blocks, block_rows, counts):
    nrow = lax.axis_size("row")
    ncol = lax.axis_size("col")
    my_row = lax.axis_index("row")
    my_col = lax.axis_index("col")
    kc = diag_inv.shape[0]
    rb_local = rhs.shape[0]
    nz_local = blocks.shape[3]
    local_rhs = rhs[:, 0]
    partial_value = jnp.zeros(local_rhs.shape, jnp.float32)
    solved_list = [jnp.zeros(local_rhs.shape[1:], jnp.float32)]
    slot_ids = jnp.arange(nz_local, dtype=jnp.int32)
    local_ids = jnp.arange(rb_local, dtype=jnp.int32)
    for k in range(kc):
        j = k // ncol
        owner_row = k % nrow
        local_pivot = k // nrow
        mine_row = my_row == owner_row
        mine_col = my_col == k % ncol
        pivot_part = jnp.where(mine_row, partial_value[local_pivot], jnp.float32(0.0))
        summed = lax.psum(pivot_part, "col")
        updated = (local_rhs[local_pivot] - summed).astype(jnp.bfloat16)
        pivot_bf = broadcast(updated, "row", owner_row)
        row_part = jnp.dot(diag_inv[k], pivot_bf, preferred_element_type=jnp.float32)
        sol = lax.all_gather(row_part, "row", axis=0, tiled=True)
        sol_bf = sol.astype(jnp.bfloat16)
        rows = block_rows[j, 0, 0]
        glob = rows * nrow + my_row
        valid = (slot_ids < counts[j, 0, 0]) & (glob > k) & mine_col
        weights = (valid[:, None] & (rows[:, None] == local_ids[None, :])).astype(jnp.float32)
        contrib = jnp.einsum(
            "sab,bn->san", blocks[j, 0, 0], sol_bf, preferred_element_type=jnp.float32
        )
        partial_value = partial_value + jnp.einsum(
            "sl,san->lan", weights, contrib, precision=lax.Precision.HIGHEST
        )
        solved_list[j] = jnp.where(mine_col, sol, solved_list[j])
    total = lax.psum(partial_value, "col")
    remainder = (local_rhs - total)[:, None]
    solved = jnp.stack(solved_list)[:, None]
    return (solved, remainder)


def solution(mesh):
    in_specs = (
        P(None, "row", None, None),
        P(None, "row", None),
        P(None, "col", "row", None, None, None),
        P(None, "col", "row", None),
        P(None, "col", "row"),
    )
    out_specs = (P(None, "col", None, None), P(None, "row", None, None))
    return jax.shard_map(
        on_device, mesh=mesh, in_specs=in_specs, out_specs=out_specs, check_vma=False
    )
```

profile of v0, /device:TPU:7, one launch (start us, length us, event | category | flops | bytes accessed | tf_op | source)
XLA Modules:
  0.0 602.3 jit_solution(2042647633984352649)
XLA Ops:
  7.2 1.9 fusion.30
  10.5 70.6 %all-reduce.9.cloned.1.call-done = bf16[1024,128]{1,0:T(8,128)(2,1)} async-done(((bf16[1024,128]{1,0:T(8,128)(2,1)}), bf16[1024,128]{1,0:T(8,128)(2,1)}) %all-reduce.9.cloned.1.call-update) | async-done | bytes 262160 | tf_op jit(solution)/shard_map/psum | solution.py:9
  82.4 24.9 %all_gather.12 = f32[1024,128]{0,1:T(8,128)S(1)} all-gather(f32[128,128]{0,1:T(8,128)S(1)} %convolution_bitcast_fusion.3), channel_id=1, replica_groups=mesh['row'=8,'col'=4] {'row'}, dimensions={0}, use_global_device_ids=true | all-gather | bytes 589824 | tf_op jit(solution)/shard_map/all_gather | solution.py:36
  110.2 40.0 %all-reduce.11.cloned.1.call-done = f32[1024,128]{1,0:T(8,128)} async-done(((f32[1024,128]{1,0:T(8,128)}), f32[1024,128]{1,0:T(8,128)}) %all-reduce.11.cloned.1.call-update) | async-done | bytes 524304 | tf_op jit(solution)/shard_map/psum | solution.py:32
  150.2 2.0 fusion.29
  152.3 72.0 %all-reduce.13.cloned.1.call-done = bf16[1024,128]{1,0:T(8,128)(2,1)} async-done(((bf16[1024,128]{1,0:T(8,128)(2,1)}), bf16[1024,128]{1,0:T(8,128)(2,1)}) %all-reduce.13.cloned.1.call-update) | async-done | bytes 262160 | tf_op jit(solution)/shard_map/psum | solution.py:9
  224.3 1.3 convolution_bitcast_fusion.2
  225.6 24.8 %all_gather.13 = f32[1024,128]{0,1:T(8,128)S(1)} all-gather(f32[128,128]{0,1:T(8,128)S(1)} %convolution_bitcast_fusion.2), channel_id=1, replica_groups=mesh['row'=8,'col'=4] {'row'}, dimensions={0}, use_global_device_ids=true | all-gather | bytes 589824 | tf_op jit(solution)/shard_map/all_gather | solution.py:36
  251.2 1.6 fusion.11
  255.2 40.0 %all-reduce.15.cloned.1.call-done = f32[1024,128]{1,0:T(8,128)} async-done(((f32[1024,128]{1,0:T(8,128)}), f32[1024,128]{1,0:T(8,128)}) %all-reduce.15.cloned.1.call-update) | async-done | bytes 524304 | tf_op jit(solution)/shard_map/psum | solution.py:32
  295.2 2.0 fusion.28
  297.2 71.5 %all-reduce.17.cloned.1.call-done = bf16[1024,128]{1,0:T(8,128)(2,1)} async-done(((bf16[1024,128]{1,0:T(8,128)(2,1)}), bf16[1024,128]{1,0:T(8,128)(2,1)}) %all-reduce.17.cloned.1.call-update) | async-done | bytes 262160 | tf_op jit(solution)/shard_map/psum | solution.py:9
  370.0 24.9 %all_gather.14 = f32[1024,128]{0,1:T(8,128)S(1)} all-gather(f32[128,128]{0,1:T(8,128)S(1)} %convolution_bitcast_fusion.1), channel_id=1, replica_groups=mesh['row'=8,'col'=4] {'row'}, dimensions={0}, use_global_device_ids=true | all-gather | bytes 589824 | tf_op jit(solution)/shard_map/all_gather | solution.py:36
  395.7 1.6 fusion.14
  397.3 2.0 copy.9
  401.6 40.0 %all-reduce.19.cloned.1.call-done = f32[1024,128]{1,0:T(8,128)} async-done(((f32[1024,128]{1,0:T(8,128)}), f32[1024,128]{1,0:T(8,128)}) %all-reduce.19.cloned.1.call-update) | async-done | bytes 524304 | tf_op jit(solution)/shard_map/psum | solution.py:32
  441.5 2.0 fusion.27
  443.6 72.0 %all-reduce.21.cloned.1.call-done = bf16[1024,128]{1,0:T(8,128)(2,1)} async-done(((bf16[1024,128]{1,0:T(8,128)(2,1)}), bf16[1024,128]{1,0:T(8,128)(2,1)}) %all-reduce.21.cloned.1.call-update) | async-done | bytes 262160 | tf_op jit(solution)/shard_map/psum | solution.py:9
  516.9 24.9 %all_gather.15 = f32[1024,128]{0,1:T(8,128)S(1)} all-gather(f32[128,128]{0,1:T(8,128)S(1)} %convolution_bitcast_fusion), channel_id=1, replica_groups=mesh['row'=8,'col'=4] {'row'}, dimensions={0}, use_global_device_ids=true | all-gather | bytes 589824 | tf_op jit(solution)/shard_map/all_gather | solution.py:36
  542.6 1.6 fusion.17
  544.3 2.0 copy.10
  546.3 2.5 multiply_add_fusion
  551.0 41.8 %all-reduce.23.cloned.1.call-done = f32[2,1024,128]{2,1,0:T(8,128)} async-done(((f32[2,1024,128]{2,1,0:T(8,128)}), f32[2,1024,128]{2,1,0:T(8,128)}) %all-reduce.23.cloned.1.call-update) | async-done | bytes 1048592 | tf_op jit(solution)/shard_map/psum | solution.py:49
  592.9 2.6 fusion.20
  (44 shorter events, 16.1 us)
Async XLA Ops:
  7.2 100.9 %copy-start = (bf16[1,1,1,1,1024,1024]{5,4,3,2,1,0:T(8,128)(2,1)S(1)}, bf16[1,1,1,1,1024,1024]{5,4,3,2,1,0:T(8,128)(2,1)}, u32[]{:S(2)}) copy-start(bf16[1,1,1,1,1024,1024]{5,4,3,2,1,0:T(8,128)(2,1)} %param.7) | copy-start | bytes 6291460
  7.2 74.0 %all-reduce.9.cloned.1.call-start = ((), (), s32[]{:S(2)}) async-start(), calls=%async_computation | async-start | bytes 524288 | tf_op jit(solution)/shard_map/psum | solution.py:9
  9.2 141.0 %all-reduce.11.cloned.1.call-start = ((), (), s32[]{:S(2)}) async-start(), calls=%async_computation.1 | async-start | bytes 1048576 | tf_op jit(solution)/shard_map/psum | solution.py:32
  107.3 0.8 copy-start.1
  110.1 114.2 %all-reduce.13.cloned.1.call-start = ((), (), s32[]{:S(2)}) async-start(), calls=%async_computation.2 | async-start | bytes 524288 | tf_op jit(solution)/shard_map/psum | solution.py:9
  152.2 143.0 %all-reduce.15.cloned.1.call-start = ((), (), s32[]{:S(2)}) async-start(), calls=%async_computation.3 | async-start | bytes 1048576 | tf_op jit(solution)/shard_map/psum | solution.py:32
  250.4 0.8 copy-start.2
  255.1 113.6 %all-reduce.17.cloned.1.call-start = ((), (), s32[]{:S(2)}) async-start(), calls=%async_computation.4 | async-start | bytes 524288 | tf_op jit(solution)/shard_map/psum | solution.py:9
  297.1 144.4 %all-reduce.19.cloned.1.call-start = ((), (), s32[]{:S(2)}) async-start(), calls=%async_computation.5 | async-start | bytes 1048576 | tf_op jit(solution)/shard_map/psum | solution.py:32
  394.9 0.8 copy-start.3
  401.5 114.1 %all-reduce.21.cloned.1.call-start = ((), (), s32[]{:S(2)}) async-start(), calls=%async_computation.6 | async-start | bytes 524288 | tf_op jit(solution)/shard_map/psum | solution.py:9
  443.5 149.3 %all-reduce.23.cloned.1.call-start = ((), (), s32[]{:S(2)}) async-start(), calls=%async_computation.7 | async-start | bytes 2097152 | tf_op jit(solution)/shard_map/psum | solution.py:49
  541.8 0.8 copy-start.4
Sparse Core Ops, SparseCore 0:
  11.9 69.1 all-reduce.8
  110.3 39.8 all-reduce.10
  154.5 69.7 all-reduce.12
  255.2 39.8 all-reduce.14
  298.9 69.7 all-reduce.16
  401.6 39.8 all-reduce.18
  445.8 69.7 all-reduce.20
  548.9 43.9 all-reduce.22
where the time goes:
time: 605 us; the launch traced here: 602 us
  waiting for transfers between devices  448 us (74%)
  blocking collectives  99.5 us (16%)
  other arithmetic  18.2 us (3%)
  between operations  15.6 us (3%)
  matrix products  10.9 us (2%)
  local copies, waits for them, and re-layouts  9.67 us (2%)
    psum x4, waiting for transfers between devices, broadcast(): return lax.psum(jnp.where(mine, value, jnp.zeros_like(value)), axis)  286 us
    psum x3, waiting for transfers between devices, on_device(): summed = lax.psum(pivot_part, 'col')  120 us
    all_gather x4, blocking collectives, on_device(): sol = lax.all_gather(row_part, 'row', axis=0, tiled=True)  99.5 us
    psum x1, waiting for transfers between devices, on_device(): total = lax.psum(partial_value, 'col')  41.8 us
  transfers between devices with their start and end apart: 8, of which 8 were waited for; matrix products, arithmetic and copies ran while one was open for 0% of the time, Pallas kernels for 0%

commit v1 on v0

--- a/solution.py
+++ b/solution.py
@@ -1,7 +1,16 @@
+import functools
+
 import jax
 import jax.numpy as jnp
 from jax import lax
+from jax.experimental import pallas as pl
+from jax.experimental.pallas import tpu as pltpu
 from jax.sharding import PartitionSpec as P
+
+VMEM = pl.BlockSpec(memory_space=pltpu.VMEM)
+ANY = pl.BlockSpec(memory_space=pl.ANY)
+SMEM = pl.BlockSpec(memory_space=pltpu.SMEM)
+TAIL = 16
 
 
 def broadcast(value, axis, root):
@@ -9,7 +18,7 @@
     return lax.psum(jnp.where(mine, value, jnp.zeros_like(value)), axis)
 
 
-def on_device(rhs, diag_inv, blocks, block_rows, counts):
+def on_device_any(rhs, diag_inv, blocks, block_rows, counts):
     nrow = lax.axis_size("row")
     ncol = lax.axis_size("col")
     my_row = lax.axis_index("row")
@@ -52,6 +61,289 @@
     return (solved, remainder)
 
 
+NR, NC = 8, 4
+SOLVER = {1: (1, 0), 2: (2, 1), 3: (3, 2)}
+SOURCE = {0: (2, 0), 1: (3, 1), 2: (2, 2), 3: (3, 2)}
+ORDER = (5, 7, 4, 6, 3, 2, 1, 0)
+
+
+def send(value, pairs):
+    return lax.ppermute(value, ("row", "col"), [(a * NC + b, c * NC + d) for (a, b), (c, d) in pairs])
+
+
+def dot(a, b):
+    return jnp.dot(a, b, preferred_element_type=jnp.float32)
+
+
+def first_kernel(rhs_ref, hi_ref, lo_ref, out_ref):
+    n = hi_ref.shape[0]
+    p = rhs_ref[...].astype(jnp.bfloat16)
+    out_ref[:n] = dot(hi_ref[...], p).astype(jnp.bfloat16)
+    out_ref[n:] = dot(lo_ref[...], p[: lo_ref.shape[1]]).astype(jnp.bfloat16)
+
+
+def at(device):
+    return (lax.axis_index("row") == device[0]) & (lax.axis_index("col") == device[1])
+
+
+def any_of(devices):
+    flag = at(devices[0])
+    for d in devices[1:]:
+        flag = flag | at(d)
+    return flag
+
+
+def step_kernel(k, *refs):
+    n_in = 4 if k == 1 else 1
+    q_in = refs[:n_in]
+    if k == 1:
+        s_in = s_prev = q_prev = None
+        rest = refs[n_in:]
+    else:
+        s_in, s_prev, q_prev = refs[n_in : n_in + 3]
+        rest = refs[n_in + 3 :]
+    rhs_ref, l_hbm = rest[:2]
+    d_hbm = rest[2 : 2 + NR]
+    s_out, q_out = rest[2 + NR : 4 + NR]
+    l_v, p_v, q_v = rest[4 + NR : 7 + NR]
+    d_v = rest[7 + NR : 7 + 2 * NR]
+    l_sem, d_sem = rest[7 + 2 * NR :]
+    size = l_hbm.shape[0]
+    part = size // NR
+    quarter = size // 4
+
+    solver = at(SOLVER[k])
+    updates = [SOLVER[k]]
+    if k == 1:
+        updates += [(2, 0), (3, 0)]
+    elif k == 2:
+        updates += [(3, 1)]
+    update = any_of(updates)
+
+    l_copy = [
+        pltpu.make_async_copy(l_hbm.at[pl.ds(i * quarter, quarter)], l_v.at[pl.ds(i * quarter, quarter)], l_sem.at[i])
+        for i in range(4)
+    ]
+    d_copy = [pltpu.make_async_copy(d_hbm[i], d_v[i], d_sem.at[i]) for i in range(NR)]
+
+    @pl.when(update)
+    def _():
+        for c in l_copy:
+            c.start()
+
+    @pl.when(solver)
+    def _():
+        for c in d_copy:
+            c.start()
+
+    if k == 1:
+        row = lax.axis_index("row")
+        for j in range(4):
+            src = lax.rem(row + 7 - j, 4)
+            hi = pl.multiple_of((4 + src) * part, part)
+            lo = pl.multiple_of(lax.rem(src + 1, 4) * part, part)
+            q_v[pl.ds(hi, part)] = q_in[j][:part]
+            q_v[pl.ds(lo, part)] = q_in[j][part:]
+    else:
+        q_v[...] = q_in[0][...]
+
+    @pl.when(update)
+    def _():
+        q = q_v[...]
+        for i in range(4):
+            l_copy[i].wait()
+            rows = pl.ds(i * quarter, quarter)
+            s = dot(l_v[rows], q)
+            if s_in is not None:
+                s = s + s_in[rows].astype(jnp.float32)
+            s_out[rows] = s.astype(jnp.bfloat16)
+            p_v[rows] = (rhs_ref[rows] - s).astype(jnp.bfloat16)
+
+    @pl.when(jnp.logical_not(update))
+    def _():
+        if s_prev is None:
+            s_out[...] = jnp.zeros_like(s_out)
+        else:
+            s_out[...] = s_prev[...]
+
+    @pl.when(solver)
+    def _():
+        for i in range(NR):
+            d_copy[i].wait()
+            width = (i + 1) * part
+            q_out[pl.ds(i * part, part)] = dot(d_v[i][...], p_v[:width]).astype(jnp.bfloat16)
+
+    @pl.when(jnp.logical_not(solver))
+    def _():
+        if k == 1:
+            q_out[...] = q_v[...]
+        elif k == 2:
+            keep = at(SOURCE[1])
+            q_out[...] = jnp.where(keep, q_v[...], q_prev[...])
+        else:
+            q_out[...] = q_prev[...]
+
+
+def step(k, q_in, s_in, s_prev, q_prev, rhs0, block, d_parts):
+    shape = rhs0.shape
+    args = list(q_in)
+    if k > 1:
+        args += [s_in, s_prev, q_prev]
+    args += [rhs0, block]
+    n_vmem = len(args) - 1
+    args += list(d_parts)
+    return pl.pallas_call(
+        functools.partial(step_kernel, k),
+        out_shape=[jax.ShapeDtypeStruct(shape, jnp.bfloat16)] * 2,
+        in_specs=[VMEM] * n_vmem + [ANY] * (1 + NR),
+        out_specs=[VMEM] * 2,
+        scratch_shapes=[
+            pltpu.VMEM(block.shape, jnp.bfloat16),
+            pltpu.VMEM(shape, jnp.bfloat16),
+            pltpu.VMEM(shape, jnp.bfloat16),
+        ]
+        + [pltpu.VMEM(d.shape, jnp.bfloat16) for d in d_parts]
+        + [pltpu.SemaphoreType.DMA((4,)), pltpu.SemaphoreType.DMA((NR,))],
+        compiler_params=pltpu.CompilerParams(vmem_limit_bytes=24 << 20),
+        name=f"step{k}",
+    )(*args)
+
+
+def update_kernel(*refs):
+    rows_ref, counts_ref = refs[:2]
+    got = refs[2 : 2 + NR]
+    s_ref, l_hbm = refs[2 + NR : 4 + NR]
+    solved_ref, out_ref = refs[4 + NR : 6 + NR]
+    l_v, q_v, l_sem, q_sem = refs[6 + NR :]
+    size = l_hbm.shape[0]
+    quarter = size // 4
+    row = lax.axis_index("row")
+    col = lax.axis_index("col")
+    below = row >= NC
+    l_copy = [
+        pltpu.make_async_copy(l_hbm.at[pl.ds(i * quarter, quarter)], l_v.at[pl.ds(i * quarter, quarter)], l_sem.at[i])
+        for i in range(4)
+    ]
+
+    @pl.when(below)
+    def _():
+        for c in l_copy:
+            c.start()
+
+    for j in range(NR):
+
+        @pl.when(row == ORDER[j])
+        def _():
+            copy = pltpu.make_async_copy(got[j], q_v, q_sem)
+            copy.start()
+            copy.wait()
+
+    q = q_v[...]
+    solved_ref[...] = q.astype(jnp.float32)
+
+    @pl.when(below)
+    def _():
+        for i in range(4):
+            l_copy[i].wait()
+            rows = pl.ds(i * quarter, quarter)
+            out_ref[rows] = dot(l_v[rows], q).astype(jnp.bfloat16)
+
+    @pl.when(jnp.logical_not(below))
+    def _():
+        out_ref[pl.ds(0, size)] = s_ref[...]
+
+    listed = rows_ref[0, 0, 0, 0]
+    there = below & (counts_ref[0, 0, 0] > 0)
+    first = (there & (listed == 0)) | (jnp.logical_not(below) & (row >= 1) & (col == row - 1))
+    second = there & (listed == 1)
+    ids = lax.broadcasted_iota(jnp.int32, (TAIL, out_ref.shape[1]), 0)
+    flag = ((ids == 0) & first) | ((ids == 1) & second)
+    out_ref[pl.ds(size, TAIL)] = jnp.where(flag, 1.0, 0.0).astype(jnp.bfloat16)
+
+
+def final_kernel(rhs_ref, *refs):
+    sums, out_ref = refs[:-1], refs[-1]
+    size = out_ref.shape[1]
+    for i in range(out_ref.shape[0]):
+        acc = rhs_ref[i]
+        for s in sums:
+            keep = s[pl.ds(size, TAIL)].astype(jnp.float32)[i : i + 1] > 0.5
+            acc = acc - jnp.where(keep, s[pl.ds(0, size)].astype(jnp.float32), 0.0)
+        out_ref[i] = acc
+
+
+def on_device_8x4(rhs, diag_inv, blocks, block_rows, counts):
+    col = lax.axis_index("col")
+    size, width = rhs.shape[2:]
+    part = size // NR
+    rhs0 = rhs[0, 0]
+    block = blocks[0, 0, 0, 0]
+
+    hi = send(diag_inv[0], [((4 + c, c), (0, c)) for c in range(4)])
+    lo = send(diag_inv[0, :, : 4 * part], [(((c + 1) % 4, c), (0, c)) for c in range(4)])
+
+    mine = lax.rem(col + 1, NC)
+    d_parts = []
+    for r in range(NR):
+        cut = lax.dynamic_slice(diag_inv, (mine, 0, 0), (1, part, (r + 1) * part))[0]
+        d_parts.append(send(cut, [((r, SOLVER[k][1]), SOLVER[k]) for k in (1, 2, 3)]))
+
+    q0 = pl.pallas_call(
+        first_kernel,
+        out_shape=jax.ShapeDtypeStruct((2 * part, width), jnp.bfloat16),
+        in_specs=[VMEM] * 3,
+        out_specs=VMEM,
+        name="first",
+    )(rhs0, hi, lo)
+    takers = ((1, 0), (2, 0), (3, 0), (0, 0))
+    got = [send(q0, [((0, c), takers[(c + j) % 4]) for c in range(4)]) for j in range(4)]
+
+    s1, q1 = step(1, got, None, None, None, rhs0, block, d_parts)
+    s_in = send(s1, [((2, 0), (2, 1)), ((3, 0), (3, 1))])
+    q_in_a = send(q1, [((1, 0), (2, 1))])
+    q_in_b = send(q1, [((1, 0), (3, 1))])
+    q_in = jnp.where(lax.axis_index("row") == 2, q_in_a, q_in_b)
+    s2, q2 = step(2, [q_in], s_in, s1, q1, rhs0, block, d_parts)
+    s_in = send(s2, [((3, 1), (3, 2))])
+    q_in = send(q2, [((2, 1), (3, 2))])
+    q2_far = send(q2, [((2, 1), (2, 2))])
+    s3, q3 = step(3, [q_in], s_in, s2, q2, rhs0, block, d_parts)
+    q_all = jnp.where((lax.axis_index("row") == 2) & (col == 2), q2_far, q3)
+    got = [send(q_all, [(SOURCE[k], (r, k)) for k in range(NC)]) for r in ORDER]
+
+    solved, mine_sum = pl.pallas_call(
+        update_kernel,
+        out_shape=[
+            jax.ShapeDtypeStruct((size, width), jnp.float32),
+            jax.ShapeDtypeStruct((size + TAIL, width), jnp.bfloat16),
+        ],
+        in_specs=[SMEM, SMEM] + [ANY] * NR + [VMEM, ANY],
+        out_specs=[VMEM, VMEM],
+        scratch_shapes=[
+            pltpu.VMEM(block.shape, jnp.bfloat16),
+            pltpu.VMEM((size, width), jnp.bfloat16),
+            pltpu.SemaphoreType.DMA((4,)),
+            pltpu.SemaphoreType.DMA,
+        ],
+        compiler_params=pltpu.CompilerParams(vmem_limit_bytes=16 << 20),
+        name="update",
+    )(block_rows, counts, *got, s3, block)
+
+    others = [
+        send(mine_sum, [((r, c), (r, (c + s) % NC)) for r in range(NR) for c in range(NC)])
+        for s in range(1, NC)
+    ]
+    remainder = pl.pallas_call(
+        final_kernel,
+        out_shape=jax.ShapeDtypeStruct((rhs.shape[0], size, width), jnp.float32),
+        in_specs=[VMEM] * (1 + NC),
+        out_specs=VMEM,
+        compiler_params=pltpu.CompilerParams(vmem_limit_bytes=16 << 20),
+        name="final",
+    )(rhs[:, 0], mine_sum, *others)
+    return solved[None, None], remainder[:, None]
+
+
 def solution(mesh):
     in_specs = (
         P(None, "row", None, None),
@@ -61,6 +353,11 @@
         P(None, "col", "row"),
     )
     out_specs = (P(None, "col", None, None), P(None, "row", None, None))
+    small = mesh.shape["row"] == NR and mesh.shape["col"] == NC
     return jax.shard_map(
-        on_device, mesh=mesh, in_specs=in_specs, out_specs=out_specs, check_vma=False
+        on_device_8x4 if small else on_device_any,
+        mesh=mesh,
+        in_specs=in_specs,
+        out_specs=out_specs,
+        check_vma=False,
     )

time: 605 us -> 121 us (0.20)
  the two profiles are of different devices: /device:TPU:7 before, /device:TPU:0 now
where the time goes in v1:
time: 121 us; the launch traced here: 120 us
  starting transfers between devices  56.5 us (47%)
  waiting for transfers between devices  32 us (26%)
  local copies, waits for them, and re-layouts  19 us (16%)
  Pallas kernels  8.78 us (7%)
  between operations  2.39 us (2%)
    ppermute x31, starting transfers between devices, send(): lax.ppermute(value, ('row', 'col'), [(a * NC + b, c * NC + d) for (a, b),...  56.5 us
    ppermute x31, waiting for transfers between devices, send(): lax.ppermute(value, ('row', 'col'), [(a * NC + b, c * NC + d) for (a, b),...  32 us
    unnamed x38, local copies, waits for them, and re-layouts  9.97 us
    squeeze x8, local copies, waits for them, and re-layouts, on_device_8x4(): lax.dynamic_slice(diag_inv, (mine, 0, 0), (1, part, (r + 1) * part))[0]  8.17 us
    pallas_call x3, Pallas kernels, step(): pl.pallas_call(functools.partial(step_kernel, k), out_shape=[jax.ShapeDty...  4.42 us
  transfers between devices with their start and end apart: 31, of which 5 were waited for; matrix products, arithmetic and copies ran while one was open for 7% of the time, Pallas kernels for 3%

profile of v1, /device:TPU:0, one launch (start us, length us, event | category | flops | bytes accessed | tf_op | source)
XLA Modules:
  0.0 119.6 jit_solution(2928941979037177318)
XLA Ops:
  0.7 1.9 %dynamic-slice_bitcast_fusion = (bf16[128,1024]{1,0:T(8,128)(2,1)}, bf16[128,1024]{1,0:T(8,128)(2,1)S(1)}) fusion(bf16[4,128,1024]{2,1,0:T(8,128)(2,1)} %param.6, s32[]{:T(128)S(6)} %select_n.26), kind=kLoop, calls=%fused_computation.1 | loop fusion | bytes 1048580 | tf_op jit(solution)/shard_map/squeeze | solution.py:288
  2.6 1.4 %collective-permute-start = (bf16[128,1024]{1,0:T(8,128)(2,1)S(1)}, bf16[128,1024]{1,0:T(8,128)(2,1)}, u32[]{:S(2)}, u32[]{:S(2)}) collective-permute-start(bf16[128,1024]{1,0:T(8,128)(2,1)S(1)} %get-tuple-element.21), channel_id=1, source_target_pairs={{16,0},{21,1},{26,2},{31,3}} | collective-permute-start | bytes 786440 | tf_op jit(solution)/shard_map/ppermute | solution.py:71
  4.0 1.6 %dynamic-slice_bitcast_fusion.4 = (bf16[128,512]{1,0:T(8,128)(2,1)}, bf16[128,512]{1,0:T(8,128)(2,1)S(1)}) fusion(bf16[4,128,1024]{2,1,0:T(8,128)(2,1)} %param.6, s32[]{:T(128)S(6)} %select_n.26), kind=kLoop, calls=%fused_computation.8 | loop fusion | bytes 524292 | tf_op jit(solution)/shard_map/squeeze | solution.py:288
  10.8 5.6 %collective-permute-start.6 = (bf16[128,128]{1,0:T(8,128)(2,1)S(1)}, bf16[128,128]{1,0:T(8,128)(2,1)S(1)}, u32[]{:S(2)}, u32[]{:S(2)}) collective-permute-start(bf16[128,128]{1,0:T(8,128)(2,1)S(1)} %dynamic-slice_bitcast_fusion.7), channel_id=1, source_target_pairs={{0,4},{1,9},{2,14}} | collective-permute-start | bytes 98312 | tf_op jit(solution)/shard_map/ppermute | solution.py:71
  23.4 2.0 %first.1 = bf16[256,128]{1,0:T(8,128)(2,1)} custom-call(f32[1024,128]{1,0:T(8,128)} %slice_bitcast_fusion.rhs_ref.refs_4_, bf16[128,1024]{1,0:T(8,128)(2,1)} %collective-permute-done.hi_ref, bf16[128,512]{1,0:T(8,128)(2,1)} %copy-done.18), custom_call_target="tpu_custom_call" | custom-call | tf_op jit(solution)/shard_map/first/pallas_call | solution.py:291
  26.0 8.7 %collective-permute-start.2 = (bf16[256,128]{1,0:T(8,128)(2,1)}, bf16[256,128]{1,0:T(8,128)(2,1)S(1)}, u32[]{:S(2)}, u32[]{:S(2)}) collective-permute-start(bf16[256,128]{1,0:T(8,128)(2,1)} %first.1), channel_id=1, source_target_pairs={{0,4},{1,8},{2,12},{3,0}} | collective-permute-start | bytes 196616 | tf_op jit(solution)/shard_map/ppermute | solution.py:71
  34.8 1.9 %collective-permute-start.3 = (bf16[256,128]{1,0:T(8,128)(2,1)}, bf16[256,128]{1,0:T(8,128)(2,1)S(1)}, u32[]{:S(2)}, u32[]{:S(2)}) collective-permute-start(bf16[256,128]{1,0:T(8,128)(2,1)} %first.1), channel_id=1, source_target_pairs={{0,8},{1,12},{2,0},{3,4}} | collective-permute-start | bytes 196616 | tf_op jit(solution)/shard_map/ppermute | solution.py:71
  36.7 1.9 %collective-permute-start.4 = (bf16[256,128]{1,0:T(8,128)(2,1)}, bf16[256,128]{1,0:T(8,128)(2,1)S(1)}, u32[]{:S(2)}, u32[]{:S(2)}) collective-permute-start(bf16[256,128]{1,0:T(8,128)(2,1)} %first.1), channel_id=1, source_target_pairs={{0,12},{1,0},{2,4},{3,8}} | collective-permute-start | bytes 196616 | tf_op jit(solution)/shard_map/ppermute | solution.py:71
  38.7 1.5 %collective-permute-start.5 = (bf16[256,128]{1,0:T(8,128)(2,1)}, bf16[256,128]{1,0:T(8,128)(2,1)S(1)}, u32[]{:S(2)}, u32[]{:S(2)}) collective-permute-start(bf16[256,128]{1,0:T(8,128)(2,1)} %first.1), channel_id=1, source_target_pairs={{0,0},{1,4},{2,8},{3,12}} | collective-permute-start | bytes 196616 | tf_op jit(solution)/shard_map/ppermute | solution.py:71
  45.7 1.4 %collective-permute-start.14 = (bf16[1024,128]{1,0:T(8,128)(2,1)}, bf16[1024,128]{1,0:T(8,128)(2,1)}, u32[]{:S(2)}, u32[]{:S(2)}) collective-permute-start(bf16[1024,128]{1,0:T(8,128)(2,1)} %get-tuple-element.10.refs_3_), channel_id=1, source_target_pairs={{4,9}} | collective-permute-start | bytes 786440 | tf_op jit(solution)/shard_map/ppermute | solution.py:71
  47.1 1.4 %collective-permute-start.15 = (bf16[1024,128]{1,0:T(8,128)(2,1)}, bf16[1024,128]{1,0:T(8,128)(2,1)}, u32[]{:S(2)}, u32[]{:S(2)}) collective-permute-start(bf16[1024,128]{1,0:T(8,128)(2,1)} %get-tuple-element.10.refs_3_), channel_id=1, source_target_pairs={{4,13}} | collective-permute-start | bytes 786440 | tf_op jit(solution)/shard_map/ppermute | solution.py:71
  53.4 2.1 %step2.1 = (bf16[1024,128]{1,0:T(8,128)(2,1)}, bf16[1024,128]{1,0:T(8,128)(2,1)}) custom-call(bf16[1024,128]{1,0:T(8,128)(2,1)S(1)} %broadcast_select_fusion.refs_0_, bf16[1024,128]{1,0:T(8,128)(2,1)} %collective-permute-done.16.refs_1_, bf16[1024,128]{1,0:T(8,128)(2,1)} %get-tuple-element.11.refs_2_, bf16[1024,128]{1,0:T(8,128)(2,1)} %get-tuple-element.10.refs_3_, ...), custom_call_target="tpu_custom_call" | custom-call | tf_op jit(solution)/shard_map/step2/pallas_call | solution.py:195
  55.5 1.4 %collective-permute-start.18 = (bf16[1024,128]{1,0:T(8,128)(2,1)}, bf16[1024,128]{1,0:T(8,128)(2,1)}, u32[]{:S(2)}, u32[]{:S(2)}) collective-permute-start(bf16[1024,128]{1,0:T(8,128)(2,1)} %get-tuple-element.12.refs_3_), channel_id=1, source_target_pairs={{9,14}} | collective-permute-start | bytes 786440 | tf_op jit(solution)/shard_map/ppermute | solution.py:71
  56.9 1.4 %collective-permute-start.19 = (bf16[1024,128]{1,0:T(8,128)(2,1)}, bf16[1024,128]{1,0:T(8,128)(2,1)}, u32[]{:S(2)}, u32[]{:S(2)}) collective-permute-start(bf16[1024,128]{1,0:T(8,128)(2,1)} %get-tuple-element.13.refs_2_), channel_id=1, source_target_pairs={{13,14}} | collective-permute-start | bytes 786440 | tf_op jit(solution)/shard_map/ppermute | solution.py:71
  58.2 1.3 %collective-permute-start.17 = (bf16[1024,128]{1,0:T(8,128)(2,1)}, bf16[1024,128]{1,0:T(8,128)(2,1)}, u32[]{:S(2)}, u32[]{:S(2)}) collective-permute-start(bf16[1024,128]{1,0:T(8,128)(2,1)} %get-tuple-element.12.refs_3_), channel_id=1, source_target_pairs={{9,10}} | collective-permute-start | bytes 786440 | tf_op jit(solution)/shard_map/ppermute | solution.py:71
  62.1 1.3 %step3.1 = (bf16[1024,128]{1,0:T(8,128)(2,1)S(1)}, bf16[1024,128]{1,0:T(8,128)(2,1)S(1)}) custom-call(bf16[1024,128]{1,0:T(8,128)(2,1)} %collective-permute-done.18.refs_0_, bf16[1024,128]{1,0:T(8,128)(2,1)} %collective-permute-done.19.refs_1_, bf16[1024,128]{1,0:T(8,128)(2,1)} %get-tuple-element.13.refs_2_, bf16[1024,128]{1,0:T(8,128)(2,1)} %get-tuple-element.12.refs_3_, ...), custom_call_target="tpu_custom_call" | custom-call | tf_op jit(solution)/shard_map/step3/pallas_call | solution.py:195
  71.0 20.4 %collective-permute-done.27.refs_9_ = bf16[1024,128]{1,0:T(8,128)(2,1)S(1)} collective-permute-done((bf16[1024,128]{1,0:T(8,128)(2,1)S(1)}, bf16[1024,128]{1,0:T(8,128)(2,1)S(1)}, u32[]{:S(2)}, u32[]{:S(2)}) %collective-permute-start.27) | collective-permute-done | bytes 262176 | tf_op jit(solution)/shard_map/ppermute | solution.py:71
  92.4 5.6 %collective-permute-start.28 = (bf16[1040,128]{1,0:T(8,128)(2,1)S(1)}, bf16[1040,128]{1,0:T(8,128)(2,1)S(1)}, u32[]{:S(2)}, u32[]{:S(2)}) collective-permute-start(bf16[1040,128]{1,0:T(8,128)(2,1)S(1)} %get-tuple-element.17.refs_0_), channel_id=1, source_target_pairs={{0,1},{1,2},{2,3},{3,0},{4,5},{5,6},{6,7},{7,4},{8,9},{9,10},{10,1... | collective-permute-start | bytes 798728 | tf_op jit(solution)/shard_map/ppermute | solution.py:71
  98.0 8.4 %collective-permute-start.29 = (bf16[1040,128]{1,0:T(8,128)(2,1)S(1)}, bf16[1040,128]{1,0:T(8,128)(2,1)S(1)}, u32[]{:S(2)}, u32[]{:S(2)}) collective-permute-start(bf16[1040,128]{1,0:T(8,128)(2,1)S(1)} %get-tuple-element.17.refs_0_), channel_id=1, source_target_pairs={{0,2},{1,3},{2,0},{3,1},{4,6},{5,7},{6,4},{7,5},{8,10},{9,11},{10,... | collective-permute-start | bytes 798728 | tf_op jit(solution)/shard_map/ppermute | solution.py:71
  106.4 1.4 %collective-permute-start.30 = (bf16[1040,128]{1,0:T(8,128)(2,1)S(1)}, bf16[1040,128]{1,0:T(8,128)(2,1)S(1)}, u32[]{:S(2)}, u32[]{:S(2)}) collective-permute-start(bf16[1040,128]{1,0:T(8,128)(2,1)S(1)} %get-tuple-element.17.refs_0_), channel_id=1, source_target_pairs={{0,3},{1,0},{2,1},{3,2},{4,7},{5,4},{6,5},{7,6},{8,11},{9,8},{10,9... | collective-permute-start | bytes 798728 | tf_op jit(solution)/shard_map/ppermute | solution.py:71
  107.7 4.1 %collective-permute-done.28.refs_1_ = bf16[1040,128]{1,0:T(8,128)(2,1)S(1)} collective-permute-done((bf16[1040,128]{1,0:T(8,128)(2,1)S(1)}, bf16[1040,128]{1,0:T(8,128)(2,1)S(1)}, u32[]{:S(2)}, u32[]{:S(2)}) %collective-permute-start.28) | collective-permute-done | bytes 266272 | tf_op jit(solution)/shard_map/ppermute | solution.py:71
  111.9 1.7 %collective-permute-done.29.refs_2_ = bf16[1040,128]{1,0:T(8,128)(2,1)S(1)} collective-permute-done((bf16[1040,128]{1,0:T(8,128)(2,1)S(1)}, bf16[1040,128]{1,0:T(8,128)(2,1)S(1)}, u32[]{:S(2)}, u32[]{:S(2)}) %collective-permute-start.29) | collective-permute-done | bytes 266272 | tf_op jit(solution)/shard_map/ppermute | solution.py:71
  113.6 4.6 %collective-permute-done.30.refs_3_ = bf16[1040,128]{1,0:T(8,128)(2,1)S(1)} collective-permute-done((bf16[1040,128]{1,0:T(8,128)(2,1)S(1)}, bf16[1040,128]{1,0:T(8,128)(2,1)S(1)}, u32[]{:S(2)}, u32[]{:S(2)}) %collective-permute-start.30) | collective-permute-done | bytes 266272 | tf_op jit(solution)/shard_map/ppermute | solution.py:71
  118.2 1.4 %final.1 = f32[2,1024,128]{2,1,0:T(8,128)} custom-call(f32[2,1024,128]{2,1,0:T(8,128)S(1)} %bitcast.32, bf16[1040,128]{1,0:T(8,128)(2,1)S(1)} %get-tuple-element.17.refs_0_, bf16[1040,128]{1,0:T(8,128)(2,1)S(1)} %collective-permute-done.28.refs_1_, bf16[1040,128]{1,0:T(8,128)(2,1)S(1)} %collective-permute-done.29.refs_2_, ...), custom_call_target="tpu_custom_call" | custom-call | tf_op jit(solution)/shard_map/final/pallas_call | solution.py:336
  (93 shorter events, 32.7 us)
Async XLA Ops:
  2.6 19.2 %collective-permute-start = (bf16[128,1024]{1,0:T(8,128)(2,1)S(1)}, bf16[128,1024]{1,0:T(8,128)(2,1)}, u32[]{:S(2)}, u32[]{:S(2)}) collective-permute-start(bf16[128,1024]{1,0:T(8,128)(2,1)S(1)} %get-tuple-element.21), channel_id=1, source_target_pairs={{16,0},{21,1},{26,2},{31,3}} | collective-permute-start | bytes 786440 | tf_op jit(solution)/shard_map/ppermute | solution.py:71
  5.6 15.5 %collective-permute-start.1 = (bf16[128,512]{1,0:T(8,128)(2,1)S(1)}, bf16[128,512]{1,0:T(8,128)(2,1)S(1)}, u32[]{:S(2)}, u32[]{:S(2)}) collective-permute-start(bf16[128,512]{1,0:T(8,128)(2,1)S(1)} %get-tuple-element.23), channel_id=1, source_target_pairs={{4,0},{9,1},{14,2},{3,3}} | collective-permute-start | bytes 393224 | tf_op jit(solution)/shard_map/ppermute | solution.py:71
  7.8 12.6 %collective-permute-start.8 = (bf16[128,384]{1,0:T(8,128)(2,1)S(1)}, bf16[128,384]{1,0:T(8,128)(2,1)S(1)}, u32[]{:S(2)}, u32[]{:S(2)}) collective-permute-start(bf16[128,384]{1,0:T(8,128)(2,1)S(1)} %dynamic-slice_bitcast_fusion.5), channel_id=1, source_target_pairs={{8,4},{9,9},{10,14}} | collective-permute-start | bytes 294920 | tf_op jit(solution)/shard_map/ppermute | solution.py:71
  9.4 10.4 %collective-permute-start.7 = (bf16[128,256]{1,0:T(8,128)(2,1)S(1)}, bf16[128,256]{1,0:T(8,128)(2,1)S(1)}, u32[]{:S(2)}, u32[]{:S(2)}) collective-permute-start(bf16[128,256]{1,0:T(8,128)(2,1)S(1)} %dynamic-slice_bitcast_fusion.6), channel_id=1, source_target_pairs={{4,4},{5,9},{6,14}} | collective-permute-start | bytes 196616 | tf_op jit(solution)/shard_map/ppermute | solution.py:71
  10.8 7.7 %collective-permute-start.6 = (bf16[128,128]{1,0:T(8,128)(2,1)S(1)}, bf16[128,128]{1,0:T(8,128)(2,1)S(1)}, u32[]{:S(2)}, u32[]{:S(2)}) collective-permute-start(bf16[128,128]{1,0:T(8,128)(2,1)S(1)} %dynamic-slice_bitcast_fusion.7), channel_id=1, source_target_pairs={{0,4},{1,9},{2,14}} | collective-permute-start | bytes 98312 | tf_op jit(solution)/shard_map/ppermute | solution.py:71
  19.1 21.1 %collective-permute-start.13 = (bf16[128,1024]{1,0:T(8,128)(2,1)}, bf16[128,1024]{1,0:T(8,128)(2,1)S(1)}, u32[]{:S(2)}, u32[]{:S(2)}) collective-permute-start(bf16[128,1024]{1,0:T(8,128)(2,1)} %get-tuple-element.20), channel_id=1, source_target_pairs={{28,4},{29,9},{30,14}} | collective-permute-start | bytes 786440 | tf_op jit(solution)/shard_map/ppermute | solution.py:71
  19.7 5.6 %collective-permute-start.9 = (bf16[128,512]{1,0:T(8,128)(2,1)}, bf16[128,512]{1,0:T(8,128)(2,1)S(1)}, u32[]{:S(2)}, u32[]{:S(2)}) collective-permute-start(bf16[128,512]{1,0:T(8,128)(2,1)} %get-tuple-element.22), channel_id=1, source_target_pairs={{12,4},{13,9},{14,14}} | collective-permute-start | bytes 393224 | tf_op jit(solution)/shard_map/ppermute | solution.py:71
  20.4 18.2 %collective-permute-start.12 = (bf16[128,896]{1,0:T(8,128)(2,1)}, bf16[128,896]{1,0:T(8,128)(2,1)S(1)}, u32[]{:S(2)}, u32[]{:S(2)}) collective-permute-start(bf16[128,896]{1,0:T(8,128)(2,1)} %dynamic-slice_bitcast_fusion.1), channel_id=1, source_target_pairs={{24,4},{25,9},{26,14}} | collective-permute-start | bytes 688136 | tf_op jit(solution)/shard_map/ppermute | solution.py:71
  21.1 15.6 %collective-permute-start.11 = (bf16[128,768]{1,0:T(8,128)(2,1)}, bf16[128,768]{1,0:T(8,128)(2,1)S(1)}, u32[]{:S(2)}, u32[]{:S(2)}) collective-permute-start(bf16[128,768]{1,0:T(8,128)(2,1)} %dynamic-slice_bitcast_fusion.2), channel_id=1, source_target_pairs={{20,4},{21,9},{22,14}} | collective-permute-start | bytes 589832 | tf_op jit(solution)/shard_map/ppermute | solution.py:71
  21.8 12.9 %collective-permute-start.10 = (bf16[128,640]{1,0:T(8,128)(2,1)}, bf16[128,640]{1,0:T(8,128)(2,1)S(1)}, u32[]{:S(2)}, u32[]{:S(2)}) collective-permute-start(bf16[128,640]{1,0:T(8,128)(2,1)} %dynamic-slice_bitcast_fusion.3), channel_id=1, source_target_pairs={{16,4},{17,9},{18,14}} | collective-permute-start | bytes 491528 | tf_op jit(solution)/shard_map/ppermute | solution.py:71
  26.0 14.1 %collective-permute-start.2 = (bf16[256,128]{1,0:T(8,128)(2,1)}, bf16[256,128]{1,0:T(8,128)(2,1)S(1)}, u32[]{:S(2)}, u32[]{:S(2)}) collective-permute-start(bf16[256,128]{1,0:T(8,128)(2,1)} %first.1), channel_id=1, source_target_pairs={{0,4},{1,8},{2,12},{3,0}} | collective-permute-start | bytes 196616 | tf_op jit(solution)/shard_map/ppermute | solution.py:71
  34.8 6.4 %collective-permute-start.3 = (bf16[256,128]{1,0:T(8,128)(2,1)}, bf16[256,128]{1,0:T(8,128)(2,1)S(1)}, u32[]{:S(2)}, u32[]{:S(2)}) collective-permute-start(bf16[256,128]{1,0:T(8,128)(2,1)} %first.1), channel_id=1, source_target_pairs={{0,8},{1,12},{2,0},{3,4}} | collective-permute-start | bytes 196616 | tf_op jit(solution)/shard_map/ppermute | solution.py:71
  36.7 4.4 %collective-permute-start.4 = (bf16[256,128]{1,0:T(8,128)(2,1)}, bf16[256,128]{1,0:T(8,128)(2,1)S(1)}, u32[]{:S(2)}, u32[]{:S(2)}) collective-permute-start(bf16[256,128]{1,0:T(8,128)(2,1)} %first.1), channel_id=1, source_target_pairs={{0,12},{1,0},{2,4},{3,8}} | collective-permute-start | bytes 196616 | tf_op jit(solution)/shard_map/ppermute | solution.py:71
  45.7 4.1 %collective-permute-start.14 = (bf16[1024,128]{1,0:T(8,128)(2,1)}, bf16[1024,128]{1,0:T(8,128)(2,1)}, u32[]{:S(2)}, u32[]{:S(2)}) collective-permute-start(bf16[1024,128]{1,0:T(8,128)(2,1)} %get-tuple-element.10.refs_3_), channel_id=1, source_target_pairs={{4,9}} | collective-permute-start | bytes 786440 | tf_op jit(solution)/shard_map/ppermute | solution.py:71
  55.5 4.1 %collective-permute-start.18 = (bf16[1024,128]{1,0:T(8,128)(2,1)}, bf16[1024,128]{1,0:T(8,128)(2,1)}, u32[]{:S(2)}, u32[]{:S(2)}) collective-permute-start(bf16[1024,128]{1,0:T(8,128)(2,1)} %get-tuple-element.12.refs_3_), channel_id=1, source_target_pairs={{9,14}} | collective-permute-start | bytes 786440 | tf_op jit(solution)/shard_map/ppermute | solution.py:71
  58.2 5.3 %collective-permute-start.17 = (bf16[1024,128]{1,0:T(8,128)(2,1)}, bf16[1024,128]{1,0:T(8,128)(2,1)}, u32[]{:S(2)}, u32[]{:S(2)}) collective-permute-start(bf16[1024,128]{1,0:T(8,128)(2,1)} %get-tuple-element.12.refs_3_), channel_id=1, source_target_pairs={{9,10}} | collective-permute-start | bytes 786440 | tf_op jit(solution)/shard_map/ppermute | solution.py:71
  64.9 3.5 %collective-permute-start.22 = (bf16[1024,128]{1,0:T(8,128)(2,1)S(1)}, bf16[1024,128]{1,0:T(8,128)(2,1)S(1)}, u32[]{:S(2)}, u32[]{:S(2)}) collective-permute-start(bf16[1024,128]{1,0:T(8,128)(2,1)S(1)} %broadcast_select_fusion.1), channel_id=1, source_target_pairs={{8,16},{13,17},{10,18},{14,19}} | collective-permute-start | bytes 786440 | tf_op jit(solution)/shard_map/ppermute | solution.py:71
  65.6 5.4 %collective-permute-start.23 = (bf16[1024,128]{1,0:T(8,128)(2,1)S(1)}, bf16[1024,128]{1,0:T(8,128)(2,1)S(1)}, u32[]{:S(2)}, u32[]{:S(2)}) collective-permute-start(bf16[1024,128]{1,0:T(8,128)(2,1)S(1)} %broadcast_select_fusion.1), channel_id=1, source_target_pairs={{8,24},{13,25},{10,26},{14,27}} | collective-permute-start | bytes 786440 | tf_op jit(solution)/shard_map/ppermute | solution.py:71
  66.3 4.7 %collective-permute-start.24 = (bf16[1024,128]{1,0:T(8,128)(2,1)S(1)}, bf16[1024,128]{1,0:T(8,128)(2,1)S(1)}, u32[]{:S(2)}, u32[]{:S(2)}) collective-permute-start(bf16[1024,128]{1,0:T(8,128)(2,1)S(1)} %broadcast_select_fusion.1), channel_id=1, source_target_pairs={{8,12},{13,13},{10,14},{14,15}} | collective-permute-start | bytes 786440 | tf_op jit(solution)/shard_map/ppermute | solution.py:71
  67.0 4.0 %collective-permute-start.25 = (bf16[1024,128]{1,0:T(8,128)(2,1)S(1)}, bf16[1024,128]{1,0:T(8,128)(2,1)S(1)}, u32[]{:S(2)}, u32[]{:S(2)}) collective-permute-start(bf16[1024,128]{1,0:T(8,128)(2,1)S(1)} %broadcast_select_fusion.1), channel_id=1, source_target_pairs={{8,8},{13,9},{10,10},{14,11}} | collective-permute-start | bytes 786440 | tf_op jit(solution)/shard_map/ppermute | solution.py:71
  68.4 23.1 %collective-permute-start.27 = (bf16[1024,128]{1,0:T(8,128)(2,1)S(1)}, bf16[1024,128]{1,0:T(8,128)(2,1)S(1)}, u32[]{:S(2)}, u32[]{:S(2)}) collective-permute-start(bf16[1024,128]{1,0:T(8,128)(2,1)S(1)} %broadcast_select_fusion.1), channel_id=1, source_target_pairs={{8,0},{13,1},{10,2},{14,3}} | collective-permute-start | bytes 786440 | tf_op jit(solution)/shard_map/ppermute | solution.py:71
  92.4 19.5 %collective-permute-start.28 = (bf16[1040,128]{1,0:T(8,128)(2,1)S(1)}, bf16[1040,128]{1,0:T(8,128)(2,1)S(1)}, u32[]{:S(2)}, u32[]{:S(2)}) collective-permute-start(bf16[1040,128]{1,0:T(8,128)(2,1)S(1)} %get-tuple-element.17.refs_0_), channel_id=1, source_target_pairs={{0,1},{1,2},{2,3},{3,0},{4,5},{5,6},{6,7},{7,4},{8,9},{9,10},{10,1... | collective-permute-start | bytes 798728 | tf_op jit(solution)/shard_map/ppermute | solution.py:71
  98.0 15.6 %collective-permute-start.29 = (bf16[1040,128]{1,0:T(8,128)(2,1)S(1)}, bf16[1040,128]{1,0:T(8,128)(2,1)S(1)}, u32[]{:S(2)}, u32[]{:S(2)}) collective-permute-start(bf16[1040,128]{1,0:T(8,128)(2,1)S(1)} %get-tuple-element.17.refs_0_), channel_id=1, source_target_pairs={{0,2},{1,3},{2,0},{3,1},{4,6},{5,7},{6,4},{7,5},{8,10},{9,11},{10,... | collective-permute-start | bytes 798728 | tf_op jit(solution)/shard_map/ppermute | solution.py:71
  106.4 11.8 %collective-permute-start.30 = (bf16[1040,128]{1,0:T(8,128)(2,1)S(1)}, bf16[1040,128]{1,0:T(8,128)(2,1)S(1)}, u32[]{:S(2)}, u32[]{:S(2)}) collective-permute-start(bf16[1040,128]{1,0:T(8,128)(2,1)S(1)} %get-tuple-element.17.refs_0_), channel_id=1, source_target_pairs={{0,3},{1,0},{2,1},{3,2},{4,7},{5,4},{6,5},{7,6},{8,11},{9,8},{10,9... | collective-permute-start | bytes 798728 | tf_op jit(solution)/shard_map/ppermute | solution.py:71
  (26 other events, 160.8 us)

commit v2 on v1

--- a/solution.py
+++ b/solution.py
@@ -68,7 +68,16 @@
 
 
 def send(value, pairs):
-    return lax.ppermute(value, ("row", "col"), [(a * NC + b, c * NC + d) for (a, b), (c, d) in pairs])
+    to = {a * NC + b: c * NC + d for (a, b), (c, d) in pairs}
+    back = {d: s for s, d in to.items()}
+    for last in [d for d in to.values() if d not in to]:
+        first = last
+        while first in back:
+            first = back[first]
+        to[last] = first
+    for i in range(NR * NC):
+        to.setdefault(i, i)
+    return lax.ppermute(value, ("row", "col"), sorted(to.items()))
 
 
 def dot(a, b):
@@ -93,8 +102,27 @@
     return flag
 
 
+def whole_kernel(*refs):
+    parts, out_ref, sem = refs[:NR], refs[NR], refs[NR + 1]
+    part = out_ref.shape[0] // NR
+    half = out_ref.shape[0] // 2
+
+    @pl.when(any_of(list(SOLVER.values())))
+    def _():
+        copies = []
+        for i in range(NR):
+            wide = parts[i].shape[1]
+            copies.append(
+                pltpu.make_async_copy(parts[i], out_ref.at[pl.ds(i * part, part), pl.ds(0, wide)], sem.at[i])
+            )
+            copies[-1].start()
+        out_ref[:half, half:] = jnp.zeros((half, half), out_ref.dtype)
+        for c in copies:
+            c.wait()
+
+
 def step_kernel(k, *refs):
-    n_in = 4 if k == 1 else 1
+    n_in = {1: 4, 2: 2, 3: 1}[k]
     q_in = refs[:n_in]
     if k == 1:
         s_in = s_prev = q_prev = None
@@ -102,15 +130,11 @@
     else:
         s_in, s_prev, q_prev = refs[n_in : n_in + 3]
         rest = refs[n_in + 3 :]
-    rhs_ref, l_hbm = rest[:2]
-    d_hbm = rest[2 : 2 + NR]
-    s_out, q_out = rest[2 + NR : 4 + NR]
-    l_v, p_v, q_v = rest[4 + NR : 7 + NR]
-    d_v = rest[7 + NR : 7 + 2 * NR]
-    l_sem, d_sem = rest[7 + 2 * NR :]
-    size = l_hbm.shape[0]
+    rhs_ref, l_ref, d_ref, s_out, q_out, p_v, q_v = rest
+    size = l_ref.shape[0]
     part = size // NR
-    quarter = size // 4
+    half = size // 2
+    row = lax.axis_index("row")
 
     solver = at(SOLVER[k])
     updates = [SOLVER[k]]
@@ -120,44 +144,30 @@
         updates += [(3, 1)]
     update = any_of(updates)
 
-    l_copy = [
-        pltpu.make_async_copy(l_hbm.at[pl.ds(i * quarter, quarter)], l_v.at[pl.ds(i * quarter, quarter)], l_sem.at[i])
-        for i in range(4)
-    ]
-    d_copy = [pltpu.make_async_copy(d_hbm[i], d_v[i], d_sem.at[i]) for i in range(NR)]
-
-    @pl.when(update)
-    def _():
-        for c in l_copy:
-            c.start()
-
-    @pl.when(solver)
-    def _():
-        for c in d_copy:
-            c.start()
-
     if k == 1:
-        row = lax.axis_index("row")
         for j in range(4):
             src = lax.rem(row + 7 - j, 4)
             hi = pl.multiple_of((4 + src) * part, part)
             lo = pl.multiple_of(lax.rem(src + 1, 4) * part, part)
             q_v[pl.ds(hi, part)] = q_in[j][:part]
             q_v[pl.ds(lo, part)] = q_in[j][part:]
-    else:
-        q_v[...] = q_in[0][...]
+    elif k == 2:
+
+        @pl.when(row == 2)
+        def _():
+            q_v[...] = q_in[0][...]
+
+        @pl.when(row != 2)
+        def _():
+            q_v[...] = q_in[1][...]
 
     @pl.when(update)
     def _():
-        q = q_v[...]
-        for i in range(4):
-            l_copy[i].wait()
-            rows = pl.ds(i * quarter, quarter)
-            s = dot(l_v[rows], q)
-            if s_in is not None:
-                s = s + s_in[rows].astype(jnp.float32)
-            s_out[rows] = s.astype(jnp.bfloat16)
-            p_v[rows] = (rhs_ref[rows] - s).astype(jnp.bfloat16)
+        s = dot(l_ref[...], q_in[0][...] if k == 3 else q_v[...])
+        if s_in is not None:
+            s = s + s_in[...].astype(jnp.float32)
+        s_out[...] = s.astype(jnp.bfloat16)
+        p_v[...] = (rhs_ref[...] - s).astype(jnp.bfloat16)
 
     @pl.when(jnp.logical_not(update))
     def _():
@@ -168,10 +178,8 @@
 
     @pl.when(solver)
     def _():
-        for i in range(NR):
-            d_copy[i].wait()
-            width = (i + 1) * part
-            q_out[pl.ds(i * part, part)] = dot(d_v[i][...], p_v[:width]).astype(jnp.bfloat16)
+        q_out[:half] = dot(d_ref[:half, :half], p_v[:half]).astype(jnp.bfloat16)
+        q_out[half:] = dot(d_ref[half:], p_v[...]).astype(jnp.bfloat16)
 
     @pl.when(jnp.logical_not(solver))
     def _():
@@ -184,27 +192,19 @@
             q_out[...] = q_prev[...]
 
 
-def step(k, q_in, s_in, s_prev, q_prev, rhs0, block, d_parts):
+def step(k, q_in, s_in, s_prev, q_prev, rhs0, block, diag):
     shape = rhs0.shape
     args = list(q_in)
     if k > 1:
         args += [s_in, s_prev, q_prev]
-    args += [rhs0, block]
-    n_vmem = len(args) - 1
-    args += list(d_parts)
+    args += [rhs0, block, diag]
     return pl.pallas_call(
         functools.partial(step_kernel, k),
         out_shape=[jax.ShapeDtypeStruct(shape, jnp.bfloat16)] * 2,
-        in_specs=[VMEM] * n_vmem + [ANY] * (1 + NR),
+        in_specs=[VMEM] * len(args),
         out_specs=[VMEM] * 2,
-        scratch_shapes=[
-            pltpu.VMEM(block.shape, jnp.bfloat16),
-            pltpu.VMEM(shape, jnp.bfloat16),
-            pltpu.VMEM(shape, jnp.bfloat16),
-        ]
-        + [pltpu.VMEM(d.shape, jnp.bfloat16) for d in d_parts]
-        + [pltpu.SemaphoreType.DMA((4,)), pltpu.SemaphoreType.DMA((NR,))],
-        compiler_params=pltpu.CompilerParams(vmem_limit_bytes=24 << 20),
+        scratch_shapes=[pltpu.VMEM(shape, jnp.bfloat16)] * 2,
+        compiler_params=pltpu.CompilerParams(vmem_limit_bytes=16 << 20),
         name=f"step{k}",
     )(*args)
 
@@ -212,23 +212,13 @@
 def update_kernel(*refs):
     rows_ref, counts_ref = refs[:2]
     got = refs[2 : 2 + NR]
-    s_ref, l_hbm = refs[2 + NR : 4 + NR]
+    s_ref, l_ref = refs[2 + NR : 4 + NR]
     solved_ref, out_ref = refs[4 + NR : 6 + NR]
-    l_v, q_v, l_sem, q_sem = refs[6 + NR :]
-    size = l_hbm.shape[0]
-    quarter = size // 4
+    q_v, q_sem = refs[6 + NR :]
+    size = l_ref.shape[0]
     row = lax.axis_index("row")
     col = lax.axis_index("col")
     below = row >= NC
-    l_copy = [
-        pltpu.make_async_copy(l_hbm.at[pl.ds(i * quarter, quarter)], l_v.at[pl.ds(i * quarter, quarter)], l_sem.at[i])
-        for i in range(4)
-    ]
-
-    @pl.when(below)
-    def _():
-        for c in l_copy:
-            c.start()
 
     for j in range(NR):
 
@@ -238,19 +228,15 @@
             copy.start()
             copy.wait()
 
-    q = q_v[...]
-    solved_ref[...] = q.astype(jnp.float32)
-
     @pl.when(below)
     def _():
-        for i in range(4):
-            l_copy[i].wait()
-            rows = pl.ds(i * quarter, quarter)
-            out_ref[rows] = dot(l_v[rows], q).astype(jnp.bfloat16)
+        out_ref[pl.ds(0, size)] = dot(l_ref[...], q_v[...]).astype(jnp.bfloat16)
 
     @pl.when(jnp.logical_not(below))
     def _():
         out_ref[pl.ds(0, size)] = s_ref[...]
+
+    solved_ref[...] = q_v[...].astype(jnp.float32)
 
     listed = rows_ref[0, 0, 0, 0]
     there = below & (counts_ref[0, 0, 0] > 0)
@@ -283,10 +269,20 @@
     lo = send(diag_inv[0, :, : 4 * part], [(((c + 1) % 4, c), (0, c)) for c in range(4)])
 
     mine = lax.rem(col + 1, NC)
-    d_parts = []
-    for r in range(NR):
-        cut = lax.dynamic_slice(diag_inv, (mine, 0, 0), (1, part, (r + 1) * part))[0]
-        d_parts.append(send(cut, [((r, SOLVER[k][1]), SOLVER[k]) for k in (1, 2, 3)]))
+    wide = lax.dynamic_index_in_dim(diag_inv, mine, 0, keepdims=False)
+    narrow = wide[:, : 4 * part]
+    d_parts = [
+        send(narrow if r < 4 else wide, [((r, SOLVER[k][1]), SOLVER[k]) for k in (1, 2, 3)]) for r in range(NR)
+    ]
+    diag = pl.pallas_call(
+        whole_kernel,
+        out_shape=jax.ShapeDtypeStruct((size, size), jnp.bfloat16),
+        in_specs=[ANY] * NR,
+        out_specs=VMEM,
+        scratch_shapes=[pltpu.SemaphoreType.DMA((NR,))],
+        compiler_params=pltpu.CompilerParams(vmem_limit_bytes=8 << 20),
+        name="whole",
+    )(*d_parts)
 
     q0 = pl.pallas_call(
         first_kernel,
@@ -298,16 +294,15 @@
     takers = ((1, 0), (2, 0), (3, 0), (0, 0))
     got = [send(q0, [((0, c), takers[(c + j) % 4]) for c in range(4)]) for j in range(4)]
 
-    s1, q1 = step(1, got, None, None, None, rhs0, block, d_parts)
+    s1, q1 = step(1, got, None, None, None, rhs0, block, diag)
     s_in = send(s1, [((2, 0), (2, 1)), ((3, 0), (3, 1))])
     q_in_a = send(q1, [((1, 0), (2, 1))])
     q_in_b = send(q1, [((1, 0), (3, 1))])
-    q_in = jnp.where(lax.axis_index("row") == 2, q_in_a, q_in_b)
-    s2, q2 = step(2, [q_in], s_in, s1, q1, rhs0, block, d_parts)
+    s2, q2 = step(2, [q_in_a, q_in_b], s_in, s1, q1, rhs0, block, diag)
     s_in = send(s2, [((3, 1), (3, 2))])
     q_in = send(q2, [((2, 1), (3, 2))])
     q2_far = send(q2, [((2, 1), (2, 2))])
-    s3, q3 = step(3, [q_in], s_in, s2, q2, rhs0, block, d_parts)
+    s3, q3 = step(3, [q_in], s_in, s2, q2, rhs0, block, diag)
     q_all = jnp.where((lax.axis_index("row") == 2) & (col == 2), q2_far, q3)
     got = [send(q_all, [(SOURCE[k], (r, k)) for k in range(NC)]) for r in ORDER]
 
@@ -317,12 +312,10 @@
             jax.ShapeDtypeStruct((size, width), jnp.float32),
             jax.ShapeDtypeStruct((size + TAIL, width), jnp.bfloat16),
         ],
-        in_specs=[SMEM, SMEM] + [ANY] * NR + [VMEM, ANY],
+        in_specs=[SMEM, SMEM] + [ANY] * NR + [VMEM, VMEM],
         out_specs=[VMEM, VMEM],
         scratch_shapes=[
-            pltpu.VMEM(block.shape, jnp.bfloat16),
             pltpu.VMEM((size, width), jnp.bfloat16),
-            pltpu.SemaphoreType.DMA((4,)),
             pltpu.SemaphoreType.DMA,
         ],
         compiler_params=pltpu.CompilerParams(vmem_limit_bytes=16 << 20),

time: 121 us -> 119 us (0.983)
  the two profiles are of different devices: /device:TPU:0 before, /device:TPU:1 now
where the time goes in v2:
time: 119 us; the launch traced here: 118 us
  starting transfers between devices  83 us (70%)
  waiting for transfers between devices  15.1 us (13%)
  local copies, waits for them, and re-layouts  11.6 us (10%)
  Pallas kernels  5.73 us (5%)
  between operations  2.33 us (2%)
    ppermute x31, starting transfers between devices, send(): return lax.ppermute(value, ('row', 'col'), sorted(to.items()))  83 us
    ppermute x31, waiting for transfers between devices, send(): return lax.ppermute(value, ('row', 'col'), sorted(to.items()))  15.1 us
    unnamed x22, local copies, waits for them, and re-layouts  5.44 us
  transfers between devices with their start and end apart: 31, of which 4 were waited for; matrix products, arithmetic and copies ran while one was open for 2% of the time, Pallas kernels for 3%

profile of v2, /device:TPU:1, one launch (start us, length us, event | category | flops | bytes accessed | tf_op | source)
XLA Modules:
  0.0 117.8 jit_solution(2504840024363203924)
XLA Ops:
  0.6 1.8 %dynamic-slice_bitcast_fusion = (bf16[128,1024]{1,0:T(8,128)(2,1)}, bf16[128,1024]{1,0:T(8,128)(2,1)S(1)}) fusion(bf16[4,128,1024]{2,1,0:T(8,128)(2,1)} %param.6, s32[]{:T(128)S(6)} %select_n.13), kind=kLoop, calls=%fused_computation.1 | loop fusion | bytes 1048580 | tf_op jit(solution)/shard_map/jit(dynamic_index_in_dim)/squeeze | solution.py:272
  2.4 1.6 %slice.16 = bf16[128,512]{1,0:T(8,128)(2,1)} slice(bf16[128,1024]{1,0:T(8,128)(2,1)} %get-tuple-element.20), slice={[0:128], [0:512]} | slice | bytes 262144 | tf_op jit(solution)/shard_map/slice | solution.py:273
  4.0 4.0 %collective-permute-start.6 = (bf16[128,512]{1,0:T(8,128)(2,1)}, bf16[128,512]{1,0:T(8,128)(2,1)S(1)}, u32[]{:S(2)}, u32[]{:S(2)}) collective-permute-start(bf16[128,512]{1,0:T(8,128)(2,1)} %slice.16), channel_id=1, source_target_pairs={{0,4},{1,9},{2,14},{3,3},{4,0},{5,5},{6,6},{7,7},{8,8},{9,1},{10,1... | collective-permute-start | bytes 393224 | tf_op jit(solution)/shard_map/ppermute | solution.py:80
  8.0 1.6 %collective-permute-start.7 = (bf16[128,512]{1,0:T(8,128)(2,1)}, bf16[128,512]{1,0:T(8,128)(2,1)S(1)}, u32[]{:S(2)}, u32[]{:S(2)}) collective-permute-start(bf16[128,512]{1,0:T(8,128)(2,1)} %slice.16), channel_id=1, source_target_pairs={{0,0},{1,1},{2,2},{3,3},{4,4},{5,9},{6,14},{7,7},{8,8},{9,5},{10,1... | collective-permute-start | bytes 393224 | tf_op jit(solution)/shard_map/ppermute | solution.py:80
  9.6 1.6 %collective-permute-start.8 = (bf16[128,512]{1,0:T(8,128)(2,1)}, bf16[128,512]{1,0:T(8,128)(2,1)S(1)}, u32[]{:S(2)}, u32[]{:S(2)}) collective-permute-start(bf16[128,512]{1,0:T(8,128)(2,1)} %slice.16), channel_id=1, source_target_pairs={{0,0},{1,1},{2,2},{3,3},{4,8},{5,5},{6,6},{7,7},{8,4},{9,9},{10,14... | collective-permute-start | bytes 393224 | tf_op jit(solution)/shard_map/ppermute | solution.py:80
  11.1 3.5 %collective-permute-start = (bf16[128,1024]{1,0:T(8,128)(2,1)S(1)}, bf16[128,1024]{1,0:T(8,128)(2,1)S(1)}, u32[]{:S(2)}, u32[]{:S(2)}) collective-permute-start(bf16[128,1024]{1,0:T(8,128)(2,1)S(1)} %get-tuple-element.21), channel_id=1, source_target_pairs={{0,16},{1,21},{2,26},{3,31},{4,4},{5,5},{6,6},{7,7},{8,8},{9,9},{1... | collective-permute-start | bytes 786440 | tf_op jit(solution)/shard_map/ppermute | solution.py:80
  15.5 1.9 %collective-permute-start.1 = (bf16[128,512]{1,0:T(8,128)(2,1)S(1)}, bf16[128,512]{1,0:T(8,128)(2,1)S(1)}, u32[]{:S(2)}, u32[]{:S(2)}) collective-permute-start(bf16[128,512]{1,0:T(8,128)(2,1)S(1)} %slice_bitcast_fusion.2), channel_id=1, source_target_pairs={{0,4},{1,9},{2,14},{3,3},{4,0},{5,5},{6,6},{7,7},{8,8},{9,1},{10,1... | collective-permute-start | bytes 393224 | tf_op jit(solution)/shard_map/ppermute | solution.py:80
  17.5 1.6 %collective-permute-start.10 = (bf16[128,1024]{1,0:T(8,128)(2,1)}, bf16[128,1024]{1,0:T(8,128)(2,1)S(1)}, u32[]{:S(2)}, u32[]{:S(2)}) collective-permute-start(bf16[128,1024]{1,0:T(8,128)(2,1)} %get-tuple-element.20), channel_id=1, source_target_pairs={{0,0},{1,1},{2,2},{3,3},{4,16},{5,5},{6,6},{7,7},{8,8},{9,17},{10,... | collective-permute-start | bytes 786440 | tf_op jit(solution)/shard_map/ppermute | solution.py:80
  19.8 1.6 %collective-permute-start.11 = (bf16[128,1024]{1,0:T(8,128)(2,1)}, bf16[128,1024]{1,0:T(8,128)(2,1)S(1)}, u32[]{:S(2)}, u32[]{:S(2)}) collective-permute-start(bf16[128,1024]{1,0:T(8,128)(2,1)} %get-tuple-element.20), channel_id=1, source_target_pairs={{0,0},{1,1},{2,2},{3,3},{4,20},{5,5},{6,6},{7,7},{8,8},{9,21},{10,... | collective-permute-start | bytes 786440 | tf_op jit(solution)/shard_map/ppermute | solution.py:80
  22.0 1.6 %collective-permute-start.12 = (bf16[128,1024]{1,0:T(8,128)(2,1)}, bf16[128,1024]{1,0:T(8,128)(2,1)S(1)}, u32[]{:S(2)}, u32[]{:S(2)}) collective-permute-start(bf16[128,1024]{1,0:T(8,128)(2,1)} %get-tuple-element.20), channel_id=1, source_target_pairs={{0,0},{1,1},{2,2},{3,3},{4,24},{5,5},{6,6},{7,7},{8,8},{9,25},{10,... | collective-permute-start | bytes 786440 | tf_op jit(solution)/shard_map/ppermute | solution.py:80
  23.6 2.2 %collective-permute-start.9 = (bf16[128,512]{1,0:T(8,128)(2,1)}, bf16[128,512]{1,0:T(8,128)(2,1)}, u32[]{:S(2)}, u32[]{:S(2)}) collective-permute-start(bf16[128,512]{1,0:T(8,128)(2,1)} %slice.16), channel_id=1, source_target_pairs={{0,0},{1,1},{2,2},{3,3},{4,12},{5,5},{6,6},{7,7},{8,8},{9,13},{10,... | collective-permute-start | bytes 393224 | tf_op jit(solution)/shard_map/ppermute | solution.py:80
  26.5 3.6 %collective-permute-start.13 = (bf16[128,1024]{1,0:T(8,128)(2,1)}, bf16[128,1024]{1,0:T(8,128)(2,1)}, u32[]{:S(2)}, u32[]{:S(2)}) collective-permute-start(bf16[128,1024]{1,0:T(8,128)(2,1)} %get-tuple-element.20), channel_id=1, source_target_pairs={{0,0},{1,1},{2,2},{3,3},{4,28},{5,5},{6,6},{7,7},{8,8},{9,29},{10,... | collective-permute-start | bytes 786440 | tf_op jit(solution)/shard_map/ppermute | solution.py:80
  30.1 1.9 %slice_bitcast_fusion.rhs_ref.refs_4_.refs_5_ = f32[1024,128]{1,0:T(8,128)} fusion(f32[2,1,1024,128]{3,2,1,0:T(8,128)} %param.5), kind=kLoop, calls=%fused_computation | loop fusion | bytes 1048576 | tf_op jit(solution)/shard_map/squeeze | solution.py:265
  32.0 2.2 %first.1 = bf16[256,128]{1,0:T(8,128)(2,1)} custom-call(f32[1024,128]{1,0:T(8,128)} %slice_bitcast_fusion.rhs_ref.refs_4_.refs_5_, bf16[128,1024]{1,0:T(8,128)(2,1)} %copy-done.9, bf16[128,512]{1,0:T(8,128)(2,1)} %copy-done.10), custom_call_target="tpu_custom_call" | custom-call | tf_op jit(solution)/shard_map/first/pallas_call | solution.py:287
  34.1 1.9 %collective-permute-start.2 = (bf16[256,128]{1,0:T(8,128)(2,1)}, bf16[256,128]{1,0:T(8,128)(2,1)S(1)}, u32[]{:S(2)}, u32[]{:S(2)}) collective-permute-start(bf16[256,128]{1,0:T(8,128)(2,1)} %first.1), channel_id=1, source_target_pairs={{0,4},{1,8},{2,12},{3,0},{4,3},{5,5},{6,6},{7,7},{8,1},{9,9},{10,1... | collective-permute-start | bytes 196616 | tf_op jit(solution)/shard_map/ppermute | solution.py:80
  36.1 6.4 %collective-permute-start.3 = (bf16[256,128]{1,0:T(8,128)(2,1)}, bf16[256,128]{1,0:T(8,128)(2,1)S(1)}, u32[]{:S(2)}, u32[]{:S(2)}) collective-permute-start(bf16[256,128]{1,0:T(8,128)(2,1)} %first.1), channel_id=1, source_target_pairs={{0,8},{1,12},{2,0},{3,4},{4,3},{5,5},{6,6},{7,7},{8,2},{9,9},{10,1... | collective-permute-start | bytes 196616 | tf_op jit(solution)/shard_map/ppermute | solution.py:80
  42.4 1.9 %collective-permute-start.4 = (bf16[256,128]{1,0:T(8,128)(2,1)}, bf16[256,128]{1,0:T(8,128)(2,1)S(1)}, u32[]{:S(2)}, u32[]{:S(2)}) collective-permute-start(bf16[256,128]{1,0:T(8,128)(2,1)} %first.1), channel_id=1, source_target_pairs={{0,12},{1,0},{2,4},{3,8},{4,2},{5,5},{6,6},{7,7},{8,3},{9,9},{10,1... | collective-permute-start | bytes 196616 | tf_op jit(solution)/shard_map/ppermute | solution.py:80
  44.4 4.6 %collective-permute-start.5 = (bf16[256,128]{1,0:T(8,128)(2,1)}, bf16[256,128]{1,0:T(8,128)(2,1)S(1)}, u32[]{:S(2)}, u32[]{:S(2)}) collective-permute-start(bf16[256,128]{1,0:T(8,128)(2,1)} %first.1), channel_id=1, source_target_pairs={{0,0},{1,4},{2,8},{3,12},{4,1},{5,5},{6,6},{7,7},{8,2},{9,9},{10,1... | collective-permute-start | bytes 196616 | tf_op jit(solution)/shard_map/ppermute | solution.py:80
  56.9 1.6 %copy-done.2 = bf16[1024,1024]{1,0:T(8,128)(2,1)S(1)} copy-done((bf16[1024,1024]{1,0:T(8,128)(2,1)S(1)}, bf16[1024,1024]{1,0:T(8,128)(2,1)}, u32[]{:S(2)}) %copy-start.2) | copy-done | bytes 2097176
  64.4 26.7 %collective-permute-start.27 = (bf16[1024,128]{1,0:T(8,128)(2,1)S(1)}, bf16[1024,128]{1,0:T(8,128)(2,1)S(1)}, u32[]{:S(2)}, u32[]{:S(2)}) collective-permute-start(bf16[1024,128]{1,0:T(8,128)(2,1)S(1)} %broadcast_select_fusion), channel_id=1, source_target_pairs={{0,8},{1,13},{2,10},{3,14},{4,4},{5,5},{6,6},{7,7},{8,0},{9,9},{10... | collective-permute-start | bytes 786440 | tf_op jit(solution)/shard_map/ppermute | solution.py:80
  92.4 3.3 %collective-permute-done.27.refs_9_ = bf16[1024,128]{1,0:T(8,128)(2,1)S(1)} collective-permute-done((bf16[1024,128]{1,0:T(8,128)(2,1)S(1)}, bf16[1024,128]{1,0:T(8,128)(2,1)S(1)}, u32[]{:S(2)}, u32[]{:S(2)}) %collective-permute-start.27) | collective-permute-done | bytes 262176 | tf_op jit(solution)/shard_map/ppermute | solution.py:80
  96.6 4.2 %collective-permute-start.28 = (bf16[1040,128]{1,0:T(8,128)(2,1)S(1)}, bf16[1040,128]{1,0:T(8,128)(2,1)S(1)}, u32[]{:S(2)}, u32[]{:S(2)}) collective-permute-start(bf16[1040,128]{1,0:T(8,128)(2,1)S(1)} %get-tuple-element.17.refs_0_), channel_id=1, source_target_pairs={{0,1},{1,2},{2,3},{3,0},{4,5},{5,6},{6,7},{7,4},{8,9},{9,10},{10,1... | collective-permute-start | bytes 798728 | tf_op jit(solution)/shard_map/ppermute | solution.py:80
  100.7 3.4 %collective-permute-start.29 = (bf16[1040,128]{1,0:T(8,128)(2,1)S(1)}, bf16[1040,128]{1,0:T(8,128)(2,1)S(1)}, u32[]{:S(2)}, u32[]{:S(2)}) collective-permute-start(bf16[1040,128]{1,0:T(8,128)(2,1)S(1)} %get-tuple-element.17.refs_0_), channel_id=1, source_target_pairs={{0,2},{1,3},{2,0},{3,1},{4,6},{5,7},{6,4},{7,5},{8,10},{9,11},{10,... | collective-permute-start | bytes 798728 | tf_op jit(solution)/shard_map/ppermute | solution.py:80
  104.8 10.9 %collective-permute-done.29.refs_2_ = bf16[1040,128]{1,0:T(8,128)(2,1)S(1)} collective-permute-done((bf16[1040,128]{1,0:T(8,128)(2,1)S(1)}, bf16[1040,128]{1,0:T(8,128)(2,1)S(1)}, u32[]{:S(2)}, u32[]{:S(2)}) %collective-permute-start.29) | collective-permute-done | bytes 266272 | tf_op jit(solution)/shard_map/ppermute | solution.py:80
  (72 shorter events, 20.2 us)
Async XLA Ops:
  4.0 13.5 %collective-permute-start.6 = (bf16[128,512]{1,0:T(8,128)(2,1)}, bf16[128,512]{1,0:T(8,128)(2,1)S(1)}, u32[]{:S(2)}, u32[]{:S(2)}) collective-permute-start(bf16[128,512]{1,0:T(8,128)(2,1)} %slice.16), channel_id=1, source_target_pairs={{0,4},{1,9},{2,14},{3,3},{4,0},{5,5},{6,6},{7,7},{8,8},{9,1},{10,1... | collective-permute-start | bytes 393224 | tf_op jit(solution)/shard_map/ppermute | solution.py:80
  8.0 11.1 %collective-permute-start.7 = (bf16[128,512]{1,0:T(8,128)(2,1)}, bf16[128,512]{1,0:T(8,128)(2,1)S(1)}, u32[]{:S(2)}, u32[]{:S(2)}) collective-permute-start(bf16[128,512]{1,0:T(8,128)(2,1)} %slice.16), channel_id=1, source_target_pairs={{0,0},{1,1},{2,2},{3,3},{4,4},{5,9},{6,14},{7,7},{8,8},{9,5},{10,1... | collective-permute-start | bytes 393224 | tf_op jit(solution)/shard_map/ppermute | solution.py:80
  9.6 11.8 %collective-permute-start.8 = (bf16[128,512]{1,0:T(8,128)(2,1)}, bf16[128,512]{1,0:T(8,128)(2,1)S(1)}, u32[]{:S(2)}, u32[]{:S(2)}) collective-permute-start(bf16[128,512]{1,0:T(8,128)(2,1)} %slice.16), channel_id=1, source_target_pairs={{0,0},{1,1},{2,2},{3,3},{4,8},{5,5},{6,6},{7,7},{8,4},{9,9},{10,14... | collective-permute-start | bytes 393224 | tf_op jit(solution)/shard_map/ppermute | solution.py:80
  11.1 14.7 %collective-permute-start = (bf16[128,1024]{1,0:T(8,128)(2,1)S(1)}, bf16[128,1024]{1,0:T(8,128)(2,1)S(1)}, u32[]{:S(2)}, u32[]{:S(2)}) collective-permute-start(bf16[128,1024]{1,0:T(8,128)(2,1)S(1)} %get-tuple-element.21), channel_id=1, source_target_pairs={{0,16},{1,21},{2,26},{3,31},{4,4},{5,5},{6,6},{7,7},{8,8},{9,9},{1... | collective-permute-start | bytes 786440 | tf_op jit(solution)/shard_map/ppermute | solution.py:80
  15.5 8.1 %collective-permute-start.1 = (bf16[128,512]{1,0:T(8,128)(2,1)S(1)}, bf16[128,512]{1,0:T(8,128)(2,1)S(1)}, u32[]{:S(2)}, u32[]{:S(2)}) collective-permute-start(bf16[128,512]{1,0:T(8,128)(2,1)S(1)} %slice_bitcast_fusion.2), channel_id=1, source_target_pairs={{0,4},{1,9},{2,14},{3,3},{4,0},{5,5},{6,6},{7,7},{8,8},{9,1},{10,1... | collective-permute-start | bytes 393224 | tf_op jit(solution)/shard_map/ppermute | solution.py:80
  17.5 18.6 %collective-permute-start.10 = (bf16[128,1024]{1,0:T(8,128)(2,1)}, bf16[128,1024]{1,0:T(8,128)(2,1)S(1)}, u32[]{:S(2)}, u32[]{:S(2)}) collective-permute-start(bf16[128,1024]{1,0:T(8,128)(2,1)} %get-tuple-element.20), channel_id=1, source_target_pairs={{0,0},{1,1},{2,2},{3,3},{4,16},{5,5},{6,6},{7,7},{8,8},{9,17},{10,... | collective-permute-start | bytes 786440 | tf_op jit(solution)/shard_map/ppermute | solution.py:80
  19.8 22.7 %collective-permute-start.11 = (bf16[128,1024]{1,0:T(8,128)(2,1)}, bf16[128,1024]{1,0:T(8,128)(2,1)S(1)}, u32[]{:S(2)}, u32[]{:S(2)}) collective-permute-start(bf16[128,1024]{1,0:T(8,128)(2,1)} %get-tuple-element.20), channel_id=1, source_target_pairs={{0,0},{1,1},{2,2},{3,3},{4,20},{5,5},{6,6},{7,7},{8,8},{9,21},{10,... | collective-permute-start | bytes 786440 | tf_op jit(solution)/shard_map/ppermute | solution.py:80
  22.0 22.4 %collective-permute-start.12 = (bf16[128,1024]{1,0:T(8,128)(2,1)}, bf16[128,1024]{1,0:T(8,128)(2,1)S(1)}, u32[]{:S(2)}, u32[]{:S(2)}) collective-permute-start(bf16[128,1024]{1,0:T(8,128)(2,1)} %get-tuple-element.20), channel_id=1, source_target_pairs={{0,0},{1,1},{2,2},{3,3},{4,24},{5,5},{6,6},{7,7},{8,8},{9,25},{10,... | collective-permute-start | bytes 786440 | tf_op jit(solution)/shard_map/ppermute | solution.py:80
  23.6 10.5 %collective-permute-start.9 = (bf16[128,512]{1,0:T(8,128)(2,1)}, bf16[128,512]{1,0:T(8,128)(2,1)}, u32[]{:S(2)}, u32[]{:S(2)}) collective-permute-start(bf16[128,512]{1,0:T(8,128)(2,1)} %slice.16), channel_id=1, source_target_pairs={{0,0},{1,1},{2,2},{3,3},{4,12},{5,5},{6,6},{7,7},{8,8},{9,13},{10,... | collective-permute-start | bytes 393224 | tf_op jit(solution)/shard_map/ppermute | solution.py:80
  26.5 22.5 %collective-permute-start.13 = (bf16[128,1024]{1,0:T(8,128)(2,1)}, bf16[128,1024]{1,0:T(8,128)(2,1)}, u32[]{:S(2)}, u32[]{:S(2)}) collective-permute-start(bf16[128,1024]{1,0:T(8,128)(2,1)} %get-tuple-element.20), channel_id=1, source_target_pairs={{0,0},{1,1},{2,2},{3,3},{4,28},{5,5},{6,6},{7,7},{8,8},{9,29},{10,... | collective-permute-start | bytes 786440 | tf_op jit(solution)/shard_map/ppermute | solution.py:80
  34.1 16.8 %collective-permute-start.2 = (bf16[256,128]{1,0:T(8,128)(2,1)}, bf16[256,128]{1,0:T(8,128)(2,1)S(1)}, u32[]{:S(2)}, u32[]{:S(2)}) collective-permute-start(bf16[256,128]{1,0:T(8,128)(2,1)} %first.1), channel_id=1, source_target_pairs={{0,4},{1,8},{2,12},{3,0},{4,3},{5,5},{6,6},{7,7},{8,1},{9,9},{10,1... | collective-permute-start | bytes 196616 | tf_op jit(solution)/shard_map/ppermute | solution.py:80
  36.1 14.9 %collective-permute-start.3 = (bf16[256,128]{1,0:T(8,128)(2,1)}, bf16[256,128]{1,0:T(8,128)(2,1)S(1)}, u32[]{:S(2)}, u32[]{:S(2)}) collective-permute-start(bf16[256,128]{1,0:T(8,128)(2,1)} %first.1), channel_id=1, source_target_pairs={{0,8},{1,12},{2,0},{3,4},{4,3},{5,5},{6,6},{7,7},{8,2},{9,9},{10,1... | collective-permute-start | bytes 196616 | tf_op jit(solution)/shard_map/ppermute | solution.py:80
  42.4 8.5 %collective-permute-start.4 = (bf16[256,128]{1,0:T(8,128)(2,1)}, bf16[256,128]{1,0:T(8,128)(2,1)S(1)}, u32[]{:S(2)}, u32[]{:S(2)}) collective-permute-start(bf16[256,128]{1,0:T(8,128)(2,1)} %first.1), channel_id=1, source_target_pairs={{0,12},{1,0},{2,4},{3,8},{4,2},{5,5},{6,6},{7,7},{8,3},{9,9},{10,1... | collective-permute-start | bytes 196616 | tf_op jit(solution)/shard_map/ppermute | solution.py:80
  44.4 6.8 %collective-permute-start.5 = (bf16[256,128]{1,0:T(8,128)(2,1)}, bf16[256,128]{1,0:T(8,128)(2,1)S(1)}, u32[]{:S(2)}, u32[]{:S(2)}) collective-permute-start(bf16[256,128]{1,0:T(8,128)(2,1)} %first.1), channel_id=1, source_target_pairs={{0,0},{1,4},{2,8},{3,12},{4,1},{5,5},{6,6},{7,7},{8,2},{9,9},{10,1... | collective-permute-start | bytes 196616 | tf_op jit(solution)/shard_map/ppermute | solution.py:80
  55.5 3.9 %collective-permute-start.17 = (bf16[1024,128]{1,0:T(8,128)(2,1)S(1)}, bf16[1024,128]{1,0:T(8,128)(2,1)}, u32[]{:S(2)}, u32[]{:S(2)}) collective-permute-start(bf16[1024,128]{1,0:T(8,128)(2,1)S(1)} %get-tuple-element.12.refs_3_), channel_id=1, source_target_pairs={{0,0},{1,1},{2,2},{3,3},{4,4},{5,5},{6,6},{7,7},{8,8},{9,10},{10,9... | collective-permute-start | bytes 786440 | tf_op jit(solution)/shard_map/ppermute | solution.py:80
  60.9 3.5 %collective-permute-start.22 = (bf16[1024,128]{1,0:T(8,128)(2,1)S(1)}, bf16[1024,128]{1,0:T(8,128)(2,1)S(1)}, u32[]{:S(2)}, u32[]{:S(2)}) collective-permute-start(bf16[1024,128]{1,0:T(8,128)(2,1)S(1)} %broadcast_select_fusion), channel_id=1, source_target_pairs={{0,0},{1,1},{2,2},{3,3},{4,4},{5,5},{6,6},{7,7},{8,16},{9,9},{10,1... | collective-permute-start | bytes 786440 | tf_op jit(solution)/shard_map/ppermute | solution.py:80
  61.6 30.8 %collective-permute-start.23 = (bf16[1024,128]{1,0:T(8,128)(2,1)S(1)}, bf16[1024,128]{1,0:T(8,128)(2,1)S(1)}, u32[]{:S(2)}, u32[]{:S(2)}) collective-permute-start(bf16[1024,128]{1,0:T(8,128)(2,1)S(1)} %broadcast_select_fusion), channel_id=1, source_target_pairs={{0,0},{1,1},{2,2},{3,3},{4,4},{5,5},{6,6},{7,7},{8,24},{9,9},{10,2... | collective-permute-start | bytes 786440 | tf_op jit(solution)/shard_map/ppermute | solution.py:80
  62.3 30.1 %collective-permute-start.24 = (bf16[1024,128]{1,0:T(8,128)(2,1)S(1)}, bf16[1024,128]{1,0:T(8,128)(2,1)S(1)}, u32[]{:S(2)}, u32[]{:S(2)}) collective-permute-start(bf16[1024,128]{1,0:T(8,128)(2,1)S(1)} %broadcast_select_fusion), channel_id=1, source_target_pairs={{0,0},{1,1},{2,2},{3,3},{4,4},{5,5},{6,6},{7,7},{8,12},{9,9},{10,1... | collective-permute-start | bytes 786440 | tf_op jit(solution)/shard_map/ppermute | solution.py:80
  63.0 29.4 %collective-permute-start.25 = (bf16[1024,128]{1,0:T(8,128)(2,1)S(1)}, bf16[1024,128]{1,0:T(8,128)(2,1)S(1)}, u32[]{:S(2)}, u32[]{:S(2)}) collective-permute-start(bf16[1024,128]{1,0:T(8,128)(2,1)S(1)} %broadcast_select_fusion), channel_id=1, source_target_pairs={{0,0},{1,1},{2,2},{3,3},{4,4},{5,5},{6,6},{7,7},{8,8},{9,13},{10,1... | collective-permute-start | bytes 786440 | tf_op jit(solution)/shard_map/ppermute | solution.py:80
  63.7 28.7 %collective-permute-start.26 = (bf16[1024,128]{1,0:T(8,128)(2,1)S(1)}, bf16[1024,128]{1,0:T(8,128)(2,1)S(1)}, u32[]{:S(2)}, u32[]{:S(2)}) collective-permute-start(bf16[1024,128]{1,0:T(8,128)(2,1)S(1)} %broadcast_select_fusion), channel_id=1, source_target_pairs={{0,0},{1,1},{2,2},{3,3},{4,8},{5,13},{6,10},{7,14},{8,4},{9,9},{10... | collective-permute-start | bytes 786440 | tf_op jit(solution)/shard_map/ppermute | solution.py:80
  64.4 31.3 %collective-permute-start.27 = (bf16[1024,128]{1,0:T(8,128)(2,1)S(1)}, bf16[1024,128]{1,0:T(8,128)(2,1)S(1)}, u32[]{:S(2)}, u32[]{:S(2)}) collective-permute-start(bf16[1024,128]{1,0:T(8,128)(2,1)S(1)} %broadcast_select_fusion), channel_id=1, source_target_pairs={{0,8},{1,13},{2,10},{3,14},{4,4},{5,5},{6,6},{7,7},{8,0},{9,9},{10... | collective-permute-start | bytes 786440 | tf_op jit(solution)/shard_map/ppermute | solution.py:80
  96.6 8.3 %collective-permute-start.28 = (bf16[1040,128]{1,0:T(8,128)(2,1)S(1)}, bf16[1040,128]{1,0:T(8,128)(2,1)S(1)}, u32[]{:S(2)}, u32[]{:S(2)}) collective-permute-start(bf16[1040,128]{1,0:T(8,128)(2,1)S(1)} %get-tuple-element.17.refs_0_), channel_id=1, source_target_pairs={{0,1},{1,2},{2,3},{3,0},{4,5},{5,6},{6,7},{7,4},{8,9},{9,10},{10,1... | collective-permute-start | bytes 798728 | tf_op jit(solution)/shard_map/ppermute | solution.py:80
  100.7 15.0 %collective-permute-start.29 = (bf16[1040,128]{1,0:T(8,128)(2,1)S(1)}, bf16[1040,128]{1,0:T(8,128)(2,1)S(1)}, u32[]{:S(2)}, u32[]{:S(2)}) collective-permute-start(bf16[1040,128]{1,0:T(8,128)(2,1)S(1)} %get-tuple-element.17.refs_0_), channel_id=1, source_target_pairs={{0,2},{1,3},{2,0},{3,1},{4,6},{5,7},{6,4},{7,5},{8,10},{9,11},{10,... | collective-permute-start | bytes 798728 | tf_op jit(solution)/shard_map/ppermute | solution.py:80
  104.1 12.3 %collective-permute-start.30 = (bf16[1040,128]{1,0:T(8,128)(2,1)S(1)}, bf16[1040,128]{1,0:T(8,128)(2,1)S(1)}, u32[]{:S(2)}, u32[]{:S(2)}) collective-permute-start(bf16[1040,128]{1,0:T(8,128)(2,1)S(1)} %get-tuple-element.17.refs_0_), channel_id=1, source_target_pairs={{0,3},{1,0},{2,1},{3,2},{4,7},{5,4},{6,5},{7,6},{8,11},{9,8},{10,9... | collective-permute-start | bytes 798728 | tf_op jit(solution)/shard_map/ppermute | solution.py:80
  (18 other events, 86.3 us)

commit v3 on v0

--- a/solution.py
+++ b/solution.py
@@ -1,7 +1,16 @@
+import functools
+
 import jax
 import jax.numpy as jnp
 from jax import lax
+from jax.experimental import pallas as pl
+from jax.experimental.pallas import tpu as pltpu
 from jax.sharding import PartitionSpec as P
+
+VMEM = pl.BlockSpec(memory_space=pltpu.VMEM)
+ANY = pl.BlockSpec(memory_space=pl.ANY)
+SMEM = pl.BlockSpec(memory_space=pltpu.SMEM)
+TAIL = 16
 
 
 def broadcast(value, axis, root):
@@ -9,7 +18,7 @@
     return lax.psum(jnp.where(mine, value, jnp.zeros_like(value)), axis)
 
 
-def on_device(rhs, diag_inv, blocks, block_rows, counts):
+def on_device_any(rhs, diag_inv, blocks, block_rows, counts):
     nrow = lax.axis_size("row")
     ncol = lax.axis_size("col")
     my_row = lax.axis_index("row")
@@ -52,6 +61,326 @@
     return (solved, remainder)
 
 
+NR, NC = 8, 4
+MAKER = ((1, 0), (2, 1), (3, 2), (5, 3))
+SIDE = (3, 0)
+
+
+def send(value, pairs):
+    return lax.ppermute(value, ("row", "col"), [(a * NC + b, c * NC + d) for (a, b), (c, d) in pairs])
+
+
+def dot(a, b):
+    return jnp.dot(a, b, preferred_element_type=jnp.float32)
+
+
+def low(a):
+    return a.astype(jnp.bfloat16)
+
+
+def at(device):
+    return (lax.axis_index("row") == device[0]) & (lax.axis_index("col") == device[1])
+
+
+def any_of(devices):
+    flag = at(devices[0])
+    for d in devices[1:]:
+        flag = flag | at(d)
+    return flag
+
+
+def call(kernel, outs, ins, in_specs, out_specs, scratch=(), limit=16):
+    return pl.pallas_call(
+        kernel,
+        out_shape=outs,
+        in_specs=in_specs,
+        out_specs=out_specs,
+        scratch_shapes=list(scratch),
+        compiler_params=pltpu.CompilerParams(vmem_limit_bytes=limit << 20),
+        name=kernel.func.__name__ if isinstance(kernel, functools.partial) else kernel.__name__,
+    )(*ins)
+
+
+def cut_kernel(rhs_ref, diag_ref, p_ref, *refs):
+    cuts, (rhs_v, rhs_sem, sem) = refs[:NR], refs[NR:]
+    row, col = lax.axis_index("row"), lax.axis_index("col")
+    part = diag_ref.shape[1]
+
+    for r in range(NR):
+
+        @pl.when(row == r)
+        def _():
+            pltpu.make_async_copy(diag_ref.at[col, :, pl.ds(0, (r + 1) * part)], cuts[r], sem).start()
+
+    @pl.when(row == 0)
+    def _():
+        copy = pltpu.make_async_copy(rhs_ref.at[0], rhs_v, rhs_sem)
+        copy.start()
+        copy.wait()
+        p_ref[...] = low(rhs_v[...])
+
+    for r in range(NR):
+
+        @pl.when(row == r)
+        def _():
+            pltpu.make_async_copy(diag_ref.at[col, :, pl.ds(0, (r + 1) * part)], cuts[r], sem).wait()
+
+
+def whole_kernel(*refs):
+    parts, own, out_ref, sem = refs[:NR], refs[NR : 2 * NR], refs[2 * NR], refs[2 * NR + 1]
+    size = out_ref.shape[0]
+    part = size // NR
+    row = lax.axis_index("row")
+
+    @pl.when(any_of(MAKER))
+    def _():
+        def copy(i, source):
+            return pltpu.make_async_copy(
+                source, out_ref.at[pl.ds(i * part, part), pl.ds(0, (i + 1) * part)], sem.at[i]
+            )
+
+        for i in range(NR):
+
+            @pl.when(row == i)
+            def _():
+                copy(i, own[i]).start()
+
+            @pl.when(row != i)
+            def _():
+                copy(i, parts[i]).start()
+
+        for i in range(NR - 1):
+            right = (i + 1) * part
+            out_ref[pl.ds(i * part, part), pl.ds(right, size - right)] = jnp.zeros((part, size - right), out_ref.dtype)
+        for i in range(NR):
+            copy(i, parts[i]).wait()
+
+
+def lower_dot(d_ref, p):
+    half = d_ref.shape[0] // 2
+    return low(dot(d_ref[:half, :half], p[:half])), low(dot(d_ref[half:], p))
+
+
+def step0_kernel(p_ref, rhs_ref, d_ref, l_ref, msg_ref, q_ref, s_ref):
+    size = l_ref.shape[0]
+    half = size // 2
+    active = at(MAKER[0])
+
+    @pl.when(active)
+    def _():
+        q_ref[:half], q_ref[half:] = lower_dot(d_ref, p_ref[...])
+        q = q_ref[...]
+        s = dot(l_ref[...], q)
+        s_ref[...] = low(s)
+        msg_ref[:size] = low(rhs_ref[0] - s)
+        msg_ref[size:] = q
+
+    @pl.when(jnp.logical_not(active))
+    def _():
+        q_ref[...] = jnp.zeros_like(q_ref)
+
+
+def step1_kernel(in_ref, side_ref, rhs_ref, d_ref, l_ref, l2_ref, q_prev, s_prev, msg_ref, q_ref, s_ref):
+    size = l_ref.shape[0]
+    half = size // 2
+    active = at(MAKER[1])
+    side = at(SIDE)
+
+    @pl.when(active)
+    def _():
+        q_ref[:half], q_ref[half:] = lower_dot(d_ref, in_ref[:size])
+        q = q_ref[...]
+        s = dot(l_ref[...], q) + dot(l2_ref[...], in_ref[size:])
+        s_ref[...] = low(s)
+        msg_ref[:size] = low(rhs_ref[0] - s)
+        msg_ref[size:] = q
+
+    @pl.when(side)
+    def _():
+        q = side_ref[...]
+        q_ref[...] = q
+        s_ref[...] = low(dot(l_ref[...], q))
+
+    @pl.when(jnp.logical_not(active | side))
+    def _():
+        q_ref[...] = q_prev[...]
+        s_ref[...] = s_prev[...]
+
+
+def step2_kernel(in_ref, sum_ref, rhs_ref, d_ref, l_ref, l2_ref, q_prev, s_prev, p_ref, q_ref, s_ref):
+    size = l_ref.shape[0]
+    half = size // 2
+    active = at(MAKER[2])
+
+    @pl.when(active)
+    def _():
+        q_ref[:half], q_ref[half:] = lower_dot(d_ref, in_ref[:size])
+        s = dot(l_ref[...], q_ref[...]) + dot(l2_ref[...], in_ref[size:]) + sum_ref[...].astype(jnp.float32)
+        s_ref[...] = low(s)
+        p_ref[...] = low(rhs_ref[0] - s)
+
+    @pl.when(jnp.logical_not(active))
+    def _():
+        q_ref[...] = q_prev[...]
+        s_ref[...] = s_prev[...]
+
+
+def step3_kernel(p_ref, d_ref, q_ref):
+    half = d_ref.shape[0] // 2
+    active = at(MAKER[3])
+
+    @pl.when(active)
+    def _():
+        q_ref[:half], q_ref[half:] = lower_dot(d_ref, p_ref[...])
+
+    @pl.when(jnp.logical_not(active))
+    def _():
+        q_ref[...] = jnp.zeros_like(q_ref)
+
+
+def update_kernel(rows_ref, counts_ref, s_ref, l_ref, *refs):
+    firsts, lasts, out_ref = refs[:2], refs[2:6], refs[6]
+    size = l_ref.shape[0]
+    row, col = lax.axis_index("row"), lax.axis_index("col")
+    below = row >= NC
+
+    def product(parts):
+        q = parts[0][...]
+        for p in parts[1:]:
+            q = q + p[...]
+        out_ref[pl.ds(0, size)] = low(dot(l_ref[...], q))
+
+    @pl.when(below & (col < NC - 1))
+    def _():
+        product(firsts)
+
+    @pl.when(below & (col == NC - 1))
+    def _():
+        product(lasts)
+
+    @pl.when(jnp.logical_not(below))
+    def _():
+        out_ref[pl.ds(0, size)] = s_ref[...]
+
+    listed = rows_ref[0, 0, 0, 0]
+    there = below & (counts_ref[0, 0, 0] > 0)
+    first = (there & (listed == 0)) | (jnp.logical_not(below) & (row >= 1) & (col == row - 1))
+    second = there & (listed == 1)
+    ids = lax.broadcasted_iota(jnp.int32, (TAIL, out_ref.shape[1]), 0)
+    flag = ((ids == 0) & first) | ((ids == 1) & second)
+    out_ref[pl.ds(size, TAIL)] = low(jnp.where(flag, 1.0, 0.0))
+
+
+def final_kernel(rhs_ref, *refs):
+    sums, parts, (solved_ref, out_ref) = refs[:NC], refs[NC:-2], refs[-2:]
+    size = out_ref.shape[1]
+    firsts, lasts = parts[:2], parts[2:]
+    col = lax.axis_index("col")
+
+    def keep_sum(values):
+        q = values[0][...]
+        for p in values[1:]:
+            q = q + p[...]
+        solved_ref[...] = q.astype(jnp.float32)
+
+    @pl.when(col < NC - 1)
+    def _():
+        keep_sum(firsts)
+
+    @pl.when(col == NC - 1)
+    def _():
+        keep_sum(lasts)
+
+    for i in range(out_ref.shape[0]):
+        acc = rhs_ref[i]
+        for s in sums:
+            keep = s[pl.ds(size, TAIL)].astype(jnp.float32)[i : i + 1] > 0.5
+            acc = acc - jnp.where(keep, s[pl.ds(0, size)].astype(jnp.float32), 0.0)
+        out_ref[i] = acc
+
+
+def on_device_8x4(rhs, diag_inv, blocks, block_rows, counts):
+    size, width = rhs.shape[2:]
+    part = size // NR
+    rhs = rhs[:, 0]
+    block = blocks[0, 0, 0, 0]
+    vec = jax.ShapeDtypeStruct((size, width), jnp.bfloat16)
+    two = jax.ShapeDtypeStruct((2 * size, width), jnp.bfloat16)
+
+    p0, *cuts = call(
+        cut_kernel,
+        [vec] + [jax.ShapeDtypeStruct((part, (r + 1) * part), jnp.bfloat16) for r in range(NR)],
+        [rhs, diag_inv],
+        [ANY, ANY],
+        [VMEM] + [ANY] * NR,
+        [pltpu.VMEM((size, width), jnp.float32), pltpu.SemaphoreType.DMA, pltpu.SemaphoreType.DMA],
+    )
+    parts = {}
+    for r in (7, 6, 5, 4, 3, 2, 1, 0):
+        parts[r] = send(cuts[r], [((r, c), MAKER[c]) for c in range(NC) if MAKER[c][0] != r])
+    p0 = send(p0, [((0, 0), MAKER[0])])
+    block2 = send(block, [((2, 0), MAKER[1]), ((3, 1), MAKER[2])])
+    diag = call(
+        whole_kernel,
+        jax.ShapeDtypeStruct((size, size), jnp.bfloat16),
+        [parts[r] for r in range(NR)] + cuts,
+        [ANY] * (2 * NR),
+        VMEM,
+        [pltpu.SemaphoreType.DMA((NR,))],
+    )
+
+    msg, q, s = call(step0_kernel, [two, vec, vec], [p0, rhs, diag, block], [VMEM] * 4, [VMEM] * 3)
+    side = send(q, [(MAKER[0], SIDE)])
+    msg = send(msg, [(MAKER[0], MAKER[1])])
+    msg, q, s = call(
+        step1_kernel, [two, vec, vec], [msg, side, rhs, diag, block, block2, q, s], [VMEM] * 8, [VMEM] * 3
+    )
+    msg = send(msg, [(MAKER[1], MAKER[2])])
+    side = send(s, [(SIDE, MAKER[2])])
+    p3, q, s = call(
+        step2_kernel, [vec, vec, vec], [msg, side, rhs, diag, block, block2, q, s], [VMEM] * 8, [VMEM] * 3
+    )
+    p3 = send(p3, [(MAKER[2], MAKER[3])])
+
+    def tree(value, *columns):
+        return send(value, [((a, k), (b, k)) for k, edges in enumerate(columns) for a, b in edges])
+
+    got = tree(q, [(3, 5), (1, 0)], [(2, 4)], [(3, 5)])
+    q = q + got
+    got = tree(q, [(5, 4), (3, 2)], [(4, 5), (2, 3)], [(5, 4), (3, 2)])
+    q = q + got
+    q, p3 = lax.optimization_barrier((q, p3))
+    got = tree(q, [(5, 7), (4, 6)], [(4, 6), (5, 7), (2, 0), (3, 1)], [(5, 7), (4, 6), (3, 1), (2, 0)])
+
+    q3 = call(step3_kernel, vec, [p3, diag], [VMEM] * 2, VMEM)
+    last = [send(q3, [(MAKER[3], (r, 3))]) for r in (4, 7, 6)]
+
+    mine = call(
+        update_kernel,
+        jax.ShapeDtypeStruct((size + TAIL, width), jnp.bfloat16),
+        [block_rows, counts, s, block, q, got, q3, *last],
+        [SMEM] * 2 + [VMEM] * 8,
+        VMEM,
+    )
+
+    def swap(value, step):
+        return send(value, [((r, c), (r, c ^ step)) for r in range(NR) for c in range(NC)])
+
+    near = swap(mine, 1)
+    far = swap(mine, 2)
+    farther = swap(far, 1)
+    q3 = q3 + last[0] + last[1] + last[2]
+    rest = send(q3, [((a, 3), (b, 3)) for a, b in ((5, 1), (7, 3), (4, 2), (6, 0))])
+    solved, remainder = call(
+        final_kernel,
+        [jax.ShapeDtypeStruct((size, width), jnp.float32), jax.ShapeDtypeStruct(rhs.shape, jnp.float32)],
+        [rhs, mine, near, far, farther, q, got, q3, rest],
+        [VMEM] * 9,
+        [VMEM] * 2,
+    )
+    return solved[None, None], remainder[:, None]
+
+
 def solution(mesh):
     in_specs = (
         P(None, "row", None, None),
@@ -61,6 +390,11 @@
         P(None, "col", "row"),
     )
     out_specs = (P(None, "col", None, None), P(None, "row", None, None))
+    small = mesh.shape["row"] == NR and mesh.shape["col"] == NC
     return jax.shard_map(
-        on_device, mesh=mesh, in_specs=in_specs, out_specs=out_specs, check_vma=False
-    )
+        on_device_8x4 if small else on_device_any,
+        mesh=mesh,
+        in_specs=in_specs,
+        out_specs=out_specs,
+        check_vma=False,
+    )

time: 605 us -> 96.4 us (0.16)
  waiting for transfers between devices: 448 us -> 13.4 us
  blocking collectives: 99.5 us -> 0 us
  starting transfers between devices: 0.33 us -> 74.7 us
  other arithmetic: 18.2 us -> 0.21 us
  between operations: 15.6 us -> 2.35 us
  matrix products: 10.9 us -> 0 us
  local copies, waits for them, and re-layouts: 9.67 us -> 3.33 us
    psum x8 -> x0, waiting for transfers between devices: 448 us -> none  [the longest x4 286 us: broadcast(): return lax.psum(jnp.where(mine, value, jnp.zeros_like(value)), axis)]
    all_gather x4 -> x0, blocking collectives: 99.5 us -> none  [on_device(): sol = lax.all_gather(row_part, 'row', axis=0, tiled=True)]
    ppermute x0 -> x25, starting transfers between devices: none -> 74.7 us  [send(): lax.ppermute(value, ('row', 'col'), [(a * NC + b, c * NC + d) for (a, b),...]
    ppermute x0 -> x25, waiting for transfers between devices: none -> 13.4 us  [send(): lax.ppermute(value, ('row', 'col'), [(a * NC + b, c * NC + d) for (a, b),...]
    dot_general x8 -> x0, matrix products: 10.9 us -> none  [the longest x4 5.72 us: on_device(): jnp.einsum('sab,bn->san', blocks[j, 0, 0], sol_bf, preferred_element_type...]
    select_n x7 -> x0, other arithmetic: 10.3 us -> none  [the longest x4 7.8 us: broadcast(): return lax.psum(jnp.where(mine, value, jnp.zeros_like(value)), axis)]
  transfers between devices with their start and end apart: 8 -> 25, of which waited for: 8 -> 2; matrix products, arithmetic and copies ran while one was open for 0% -> 0% of each run, Pallas kernels for 0% -> 0%
where the time goes in v3:
time: 96.4 us; the launch traced here: 95.9 us
  starting transfers between devices  74.7 us (77%)
  waiting for transfers between devices  13.4 us (14%)
  local copies, waits for them, and re-layouts  3.33 us (3%)
  between operations  2.35 us (2%)
  Pallas kernels  1.92 us (2%)
    ppermute x25, starting transfers between devices, send(): lax.ppermute(value, ('row', 'col'), [(a * NC + b, c * NC + d) for (a, b),...  74.7 us
    ppermute x25, waiting for transfers between devices, send(): lax.ppermute(value, ('row', 'col'), [(a * NC + b, c * NC + d) for (a, b),...  13.4 us
    unnamed x8, local copies, waits for them, and re-layouts  3.33 us
  transfers between devices with their start and end apart: 25, of which 2 were waited for; matrix products, arithmetic and copies ran while one was open for 0% of the time, Pallas kernels for 0%

profile of v3, /device:TPU:7, one launch (start us, length us, event | category | flops | bytes accessed | tf_op | source)
XLA Modules:
  0.0 95.9 jit_solution(11459095515265105765)
XLA Ops:
  0.6 0.8 collective-permute-start.11
  1.4 1.2 %copy-done.1 = f32[2,1,1024,128]{3,2,1,0:T(8,128)S(1)} copy-done((f32[2,1,1024,128]{3,2,1,0:T(8,128)S(1)}, f32[2,1,1024,128]{3,2,1,0:T(8,128)}, u32[]{:S(2)}) %copy-start.1) | copy-done | bytes 1048600
  2.7 1.2 %copy-done.3 = bf16[4,128,1024]{2,1,0:T(8,128)(2,1)S(1)} copy-done((bf16[4,128,1024]{2,1,0:T(8,128)(2,1)S(1)}, bf16[4,128,1024]{2,1,0:T(8,128)(2,1)}, u32[]{:S(2)}) %copy-start.3) | copy-done | bytes 1048600
  6.7 9.2 %collective-permute-start.2 = (bf16[128,256]{1,0:T(8,128)(2,1)S(1)}, bf16[128,256]{1,0:T(8,128)(2,1)S(1)}, u32[]{:S(2)}, u32[]{:S(2)}) collective-permute-start(bf16[128,256]{1,0:T(8,128)(2,1)S(1)} %get-tuple-element.26.refs_9_), channel_id=1, source_target_pairs={{5,9},{6,14},{7,23}} | collective-permute-start | bytes 196616 | tf_op jit(solution)/shard_map/ppermute | solution.py:70
  15.9 1.3 %collective-permute-done.2.refs_1_ = bf16[128,256]{1,0:T(8,128)(2,1)S(1)} collective-permute-done((bf16[128,256]{1,0:T(8,128)(2,1)S(1)}, bf16[128,256]{1,0:T(8,128)(2,1)S(1)}, u32[]{:S(2)}, u32[]{:S(2)}) %collective-permute-start.2) | collective-permute-done | bytes 65568 | tf_op jit(solution)/shard_map/ppermute | solution.py:70
  17.9 0.7 collective-permute-start
  19.3 0.8 collective-permute-start.6
  21.2 0.7 collective-permute-start.9
  21.9 0.7 collective-permute-start.10
  22.7 0.7 collective-permute-start.12
  23.4 0.7 collective-permute-start.13
  24.2 0.7 collective-permute-start.14
  24.9 0.7 collective-permute-start.15
  25.6 0.7 collective-permute-start.16
  26.5 0.7 collective-permute-start.18
  27.2 0.7 collective-permute-start.19
  27.8 0.7 collective-permute-start.20
  28.5 0.7 collective-permute-start.17
  30.6 38.7 %collective-permute-start.22 = (bf16[1040,128]{1,0:T(8,128)(2,1)S(1)}, bf16[1040,128]{1,0:T(8,128)(2,1)S(1)}, u32[]{:S(2)}, u32[]{:S(2)}) collective-permute-start(bf16[1040,128]{1,0:T(8,128)(2,1)S(1)} %update_kernel.1.refs_0_), channel_id=1, source_target_pairs={{0,2},{1,3},{2,0},{3,1},{4,6},{5,7},{6,4},{7,5},{8,10},{9,11},{10,... | collective-permute-start | bytes 798728 | tf_op jit(solution)/shard_map/ppermute | solution.py:70
  69.3 5.3 %collective-permute-start.21 = (bf16[1040,128]{1,0:T(8,128)(2,1)S(1)}, bf16[1040,128]{1,0:T(8,128)(2,1)S(1)}, u32[]{:S(2)}, u32[]{:S(2)}) collective-permute-start(bf16[1040,128]{1,0:T(8,128)(2,1)S(1)} %update_kernel.1.refs_0_), channel_id=1, source_target_pairs={{0,1},{1,0},{2,3},{3,2},{4,5},{5,4},{6,7},{7,6},{8,9},{9,8},{10,11... | collective-permute-start | bytes 798728 | tf_op jit(solution)/shard_map/ppermute | solution.py:70
  74.6 6.3 %collective-permute-start.23 = (bf16[1040,128]{1,0:T(8,128)(2,1)S(1)}, bf16[1040,128]{1,0:T(8,128)(2,1)S(1)}, u32[]{:S(2)}, u32[]{:S(2)}) collective-permute-start(bf16[1040,128]{1,0:T(8,128)(2,1)S(1)} %collective-permute-done.22.refs_2_), channel_id=1, source_target_pairs={{0,1},{1,0},{2,3},{3,2},{4,5},{5,4},{6,7},{7,6},{8,9},{9,8},{10,11... | collective-permute-start | bytes 798728 | tf_op jit(solution)/shard_map/ppermute | solution.py:70
  81.1 1.3 %collective-permute-start.24 = (bf16[1024,128]{1,0:T(8,128)(2,1)S(1)}, bf16[1024,128]{1,0:T(8,128)(2,1)S(1)}, u32[]{:S(2)}, u32[]{:S(2)}) collective-permute-start(bf16[1024,128]{1,0:T(8,128)(2,1)S(1)} %add_add_fusion.refs_6_), channel_id=1, source_target_pairs={{23,7},{31,15},{19,11},{27,3}} | collective-permute-start | bytes 786440 | tf_op jit(solution)/shard_map/ppermute | solution.py:70
  82.4 12.1 %collective-permute-done.24.refs_7_ = bf16[1024,128]{1,0:T(8,128)(2,1)S(1)} collective-permute-done((bf16[1024,128]{1,0:T(8,128)(2,1)S(1)}, bf16[1024,128]{1,0:T(8,128)(2,1)S(1)}, u32[]{:S(2)}, u32[]{:S(2)}) %collective-permute-start.24) | collective-permute-done | bytes 262176 | tf_op jit(solution)/shard_map/ppermute | solution.py:70
  94.4 1.5 %final_kernel.1 = (f32[1024,128]{1,0:T(8,128)}, f32[2,1024,128]{2,1,0:T(8,128)}) custom-call(f32[2,1024,128]{2,1,0:T(8,128)S(1)} %bitcast.15, bf16[1040,128]{1,0:T(8,128)(2,1)S(1)} %update_kernel.1.refs_0_, bf16[1040,128]{1,0:T(8,128)(2,1)S(1)} %collective-permute-done.21.refs_1_, bf16[1040,128]{1,0:T(8,128)(2,1)S(1)} %collective-permute-done.22.refs_2_, ...), custom_call_target="tpu_custom_call" | custom-call | tf_op jit(solution)/shard_map/final_kernel/pallas_call | solution.py:93
  (45 shorter events, 5.6 us)
Async XLA Ops:
  0.6 22.0 %collective-permute-start.11 = (bf16[1024,1024]{1,0:T(8,128)(2,1)}, bf16[1024,1024]{1,0:T(8,128)(2,1)S(1)}, u32[]{:S(2)}, u32[]{:S(2)}) collective-permute-start(bf16[1024,1024]{1,0:T(8,128)(2,1)} %bitcast.6), channel_id=1, source_target_pairs={{8,9},{13,14}} | collective-permute-start | bytes 6291464 | tf_op jit(solution)/shard_map/ppermute | solution.py:70
  4.0 15.3 %collective-permute-start.5 = (bf16[128,640]{1,0:T(8,128)(2,1)S(1)}, bf16[128,640]{1,0:T(8,128)(2,1)S(1)}, u32[]{:S(2)}, u32[]{:S(2)}) collective-permute-start(bf16[128,640]{1,0:T(8,128)(2,1)S(1)} %get-tuple-element.29.refs_12_), channel_id=1, source_target_pairs={{16,4},{17,9},{18,14},{19,23}} | collective-permute-start | bytes 491528 | tf_op jit(solution)/shard_map/ppermute | solution.py:70
  4.6 2.0 %collective-permute-start.1 = (bf16[128,128]{1,0:T(8,128)(2,1)S(1)}, bf16[128,128]{1,0:T(8,128)(2,1)S(1)}, u32[]{:S(2)}, u32[]{:S(2)}) collective-permute-start(bf16[128,128]{1,0:T(8,128)(2,1)S(1)} %get-tuple-element.25.refs_8_), channel_id=1, source_target_pairs={{0,4},{1,9},{2,14},{3,23}} | collective-permute-start | bytes 98312 | tf_op jit(solution)/shard_map/ppermute | solution.py:70
  5.3 13.3 %collective-permute-start.4 = (bf16[128,512]{1,0:T(8,128)(2,1)S(1)}, bf16[128,512]{1,0:T(8,128)(2,1)S(1)}, u32[]{:S(2)}, u32[]{:S(2)}) collective-permute-start(bf16[128,512]{1,0:T(8,128)(2,1)S(1)} %get-tuple-element.28.refs_11_), channel_id=1, source_target_pairs={{12,4},{13,9},{15,23}} | collective-permute-start | bytes 393224 | tf_op jit(solution)/shard_map/ppermute | solution.py:70
  6.0 11.9 %collective-permute-start.3 = (bf16[128,384]{1,0:T(8,128)(2,1)S(1)}, bf16[128,384]{1,0:T(8,128)(2,1)S(1)}, u32[]{:S(2)}, u32[]{:S(2)}) collective-permute-start(bf16[128,384]{1,0:T(8,128)(2,1)S(1)} %get-tuple-element.27.refs_10_), channel_id=1, source_target_pairs={{8,4},{10,14},{11,23}} | collective-permute-start | bytes 294920 | tf_op jit(solution)/shard_map/ppermute | solution.py:70
  6.7 10.6 %collective-permute-start.2 = (bf16[128,256]{1,0:T(8,128)(2,1)S(1)}, bf16[128,256]{1,0:T(8,128)(2,1)S(1)}, u32[]{:S(2)}, u32[]{:S(2)}) collective-permute-start(bf16[128,256]{1,0:T(8,128)(2,1)S(1)} %get-tuple-element.26.refs_9_), channel_id=1, source_target_pairs={{5,9},{6,14},{7,23}} | collective-permute-start | bytes 196616 | tf_op jit(solution)/shard_map/ppermute | solution.py:70
  17.2 2.9 %collective-permute-start.8 = (bf16[128,1024]{1,0:T(8,128)(2,1)S(1)}, bf16[128,1024]{1,0:T(8,128)(2,1)S(1)}, u32[]{:S(2)}, u32[]{:S(2)}) collective-permute-start(bf16[128,1024]{1,0:T(8,128)(2,1)S(1)} %get-tuple-element.32.refs_15_), channel_id=1, source_target_pairs={{28,4},{29,9},{30,14},{31,23}} | collective-permute-start | bytes 786440 | tf_op jit(solution)/shard_map/ppermute | solution.py:70
  17.9 2.4 %collective-permute-start = (bf16[1024,128]{1,0:T(8,128)(2,1)S(1)}, bf16[1024,128]{1,0:T(8,128)(2,1)S(1)}, u32[]{:S(2)}, u32[]{:S(2)}) collective-permute-start(bf16[1024,128]{1,0:T(8,128)(2,1)S(1)} %get-tuple-element.24), channel_id=1, source_target_pairs={{0,4}} | collective-permute-start | bytes 786440 | tf_op jit(solution)/shard_map/ppermute | solution.py:70
  18.6 1.5 %collective-permute-start.7 = (bf16[128,896]{1,0:T(8,128)(2,1)S(1)}, bf16[128,896]{1,0:T(8,128)(2,1)S(1)}, u32[]{:S(2)}, u32[]{:S(2)}) collective-permute-start(bf16[128,896]{1,0:T(8,128)(2,1)S(1)} %get-tuple-element.31.refs_14_), channel_id=1, source_target_pairs={{24,4},{25,9},{26,14},{27,23}} | collective-permute-start | bytes 688136 | tf_op jit(solution)/shard_map/ppermute | solution.py:70
  19.3 0.8 collective-permute-start.6
  21.2 1.4 %collective-permute-start.9 = (bf16[2048,128]{1,0:T(8,128)(2,1)S(1)}, bf16[2048,128]{1,0:T(8,128)(2,1)S(1)}, u32[]{:S(2)}, u32[]{:S(2)}) collective-permute-start(bf16[2048,128]{1,0:T(8,128)(2,1)S(1)} %get-tuple-element.33), channel_id=1, source_target_pairs={{4,9}} | collective-permute-start | bytes 1572872 | tf_op jit(solution)/shard_map/ppermute | solution.py:70
  21.9 0.7 collective-permute-start.10
  22.7 1.4 %collective-permute-start.12 = (bf16[2048,128]{1,0:T(8,128)(2,1)S(1)}, bf16[2048,128]{1,0:T(8,128)(2,1)S(1)}, u32[]{:S(2)}, u32[]{:S(2)}) collective-permute-start(bf16[2048,128]{1,0:T(8,128)(2,1)S(1)} %get-tuple-element.36), channel_id=1, source_target_pairs={{9,14}} | collective-permute-start | bytes 1572872 | tf_op jit(solution)/shard_map/ppermute | solution.py:70
  23.4 0.7 collective-permute-start.13
  24.9 1.4 %collective-permute-start.15 = (bf16[1024,128]{1,0:T(8,128)(2,1)S(1)}, bf16[1024,128]{1,0:T(8,128)(2,1)S(1)}, u32[]{:S(2)}, u32[]{:S(2)}) collective-permute-start(bf16[1024,128]{1,0:T(8,128)(2,1)S(1)} %add.15), channel_id=1, source_target_pairs={{20,16},{12,8},{17,21},{9,13},{22,18},{14,10}} | collective-permute-start | bytes 786440 | tf_op jit(solution)/shard_map/ppermute | solution.py:70
  25.6 0.8 collective-permute-start.16
  26.5 4.0 %collective-permute-start.18 = (bf16[1024,128]{1,0:T(8,128)(2,1)S(1)}, bf16[1024,128]{1,0:T(8,128)(2,1)S(1)}, u32[]{:S(2)}, u32[]{:S(2)}) collective-permute-start(bf16[1024,128]{1,0:T(8,128)(2,1)S(1)} %step3_kernel.1.refs_2_), channel_id=1, source_target_pairs={{23,19}} | collective-permute-start | bytes 786440 | tf_op jit(solution)/shard_map/ppermute | solution.py:70
  27.2 3.4 %collective-permute-start.19 = (bf16[1024,128]{1,0:T(8,128)(2,1)S(1)}, bf16[1024,128]{1,0:T(8,128)(2,1)S(1)}, u32[]{:S(2)}, u32[]{:S(2)}) collective-permute-start(bf16[1024,128]{1,0:T(8,128)(2,1)S(1)} %step3_kernel.1.refs_2_), channel_id=1, source_target_pairs={{23,31}} | collective-permute-start | bytes 786440 | tf_op jit(solution)/shard_map/ppermute | solution.py:70
  27.8 2.7 %collective-permute-start.20 = (bf16[1024,128]{1,0:T(8,128)(2,1)S(1)}, bf16[1024,128]{1,0:T(8,128)(2,1)S(1)}, u32[]{:S(2)}, u32[]{:S(2)}) collective-permute-start(bf16[1024,128]{1,0:T(8,128)(2,1)S(1)} %step3_kernel.1.refs_2_), channel_id=1, source_target_pairs={{23,27}} | collective-permute-start | bytes 786440 | tf_op jit(solution)/shard_map/ppermute | solution.py:70
  28.5 2.0 %collective-permute-start.17 = (bf16[1024,128]{1,0:T(8,128)(2,1)S(1)}, bf16[1024,128]{1,0:T(8,128)(2,1)S(1)}, u32[]{:S(2)}, u32[]{:S(2)}) collective-permute-start(bf16[1024,128]{1,0:T(8,128)(2,1)S(1)} %add.16.refs_0_.refs_4_), channel_id=1, source_target_pairs={{20,28},{16,24},{17,25},{21,29},{9,1},{13,5},{22,30},{18,26},{14,6... | collective-permute-start | bytes 786440 | tf_op jit(solution)/shard_map/ppermute | solution.py:70
  30.6 44.0 %collective-permute-start.22 = (bf16[1040,128]{1,0:T(8,128)(2,1)S(1)}, bf16[1040,128]{1,0:T(8,128)(2,1)S(1)}, u32[]{:S(2)}, u32[]{:S(2)}) collective-permute-start(bf16[1040,128]{1,0:T(8,128)(2,1)S(1)} %update_kernel.1.refs_0_), channel_id=1, source_target_pairs={{0,2},{1,3},{2,0},{3,1},{4,6},{5,7},{6,4},{7,5},{8,10},{9,11},{10,... | collective-permute-start | bytes 798728 | tf_op jit(solution)/shard_map/ppermute | solution.py:70
  69.3 25.1 %collective-permute-start.21 = (bf16[1040,128]{1,0:T(8,128)(2,1)S(1)}, bf16[1040,128]{1,0:T(8,128)(2,1)S(1)}, u32[]{:S(2)}, u32[]{:S(2)}) collective-permute-start(bf16[1040,128]{1,0:T(8,128)(2,1)S(1)} %update_kernel.1.refs_0_), channel_id=1, source_target_pairs={{0,1},{1,0},{2,3},{3,2},{4,5},{5,4},{6,7},{7,6},{8,9},{9,8},{10,11... | collective-permute-start | bytes 798728 | tf_op jit(solution)/shard_map/ppermute | solution.py:70
  74.6 19.8 %collective-permute-start.23 = (bf16[1040,128]{1,0:T(8,128)(2,1)S(1)}, bf16[1040,128]{1,0:T(8,128)(2,1)S(1)}, u32[]{:S(2)}, u32[]{:S(2)}) collective-permute-start(bf16[1040,128]{1,0:T(8,128)(2,1)S(1)} %collective-permute-done.22.refs_2_), channel_id=1, source_target_pairs={{0,1},{1,0},{2,3},{3,2},{4,5},{5,4},{6,7},{7,6},{8,9},{9,8},{10,11... | collective-permute-start | bytes 798728 | tf_op jit(solution)/shard_map/ppermute | solution.py:70
  81.1 13.4 %collective-permute-start.24 = (bf16[1024,128]{1,0:T(8,128)(2,1)S(1)}, bf16[1024,128]{1,0:T(8,128)(2,1)S(1)}, u32[]{:S(2)}, u32[]{:S(2)}) collective-permute-start(bf16[1024,128]{1,0:T(8,128)(2,1)S(1)} %add_add_fusion.refs_6_), channel_id=1, source_target_pairs={{23,7},{31,15},{19,11},{27,3}} | collective-permute-start | bytes 786440 | tf_op jit(solution)/shard_map/ppermute | solution.py:70
  (5 other events, 6.6 us)

commit v4 on v0

--- a/solution.py
+++ b/solution.py
@@ -1,7 +1,16 @@
+import functools
+
 import jax
 import jax.numpy as jnp
 from jax import lax
+from jax.experimental import pallas as pl
+from jax.experimental.pallas import tpu as pltpu
 from jax.sharding import PartitionSpec as P
+
+VMEM = pl.BlockSpec(memory_space=pltpu.VMEM)
+ANY = pl.BlockSpec(memory_space=pl.ANY)
+SMEM = pl.BlockSpec(memory_space=pltpu.SMEM)
+TAIL = 16
 
 
 def broadcast(value, axis, root):
@@ -9,7 +18,7 @@
     return lax.psum(jnp.where(mine, value, jnp.zeros_like(value)), axis)
 
 
-def on_device(rhs, diag_inv, blocks, block_rows, counts):
+def on_device_any(rhs, diag_inv, blocks, block_rows, counts):
     nrow = lax.axis_size("row")
     ncol = lax.axis_size("col")
     my_row = lax.axis_index("row")
@@ -52,6 +61,399 @@
     return (solved, remainder)
 
 
+NR, NC = 8, 4
+MAKER = (None, (2, 1), (3, 2), (5, 3))
+FIRST = (1, 0)
+NEAR = (5, 2)
+
+
+def send(value, pairs):
+    return lax.ppermute(value, ("row", "col"), [(a * NC + b, c * NC + d) for (a, b), (c, d) in pairs])
+
+
+def hops(a, b):
+    d = a ^ b
+    return 4 * (abs((a >> 3) - (b >> 3)) + ((d >> 2) & 1) + ((d >> 1) & 1)) + (d & 1) if d else 1000
+
+
+def complete(pairs):
+    to = {a * NC + b: c * NC + d for (a, b), (c, d) in pairs}
+    free_from = [i for i in range(NR * NC) if i not in to]
+    free_to = [i for i in range(NR * NC) if i not in to.values()]
+    n = len(free_from)
+    u, v, match = [0] * (n + 1), [0] * (n + 1), [0] * (n + 1)
+    for i in range(1, n + 1):
+        match[0], j0 = i, 0
+        least, way, used = [10**9] * (n + 1), [0] * (n + 1), [False] * (n + 1)
+        while True:
+            used[j0] = True
+            i0, delta, j1 = match[j0], 10**9, 0
+            for j in range(1, n + 1):
+                if not used[j]:
+                    cur = hops(free_from[i0 - 1], free_to[j - 1]) - u[i0] - v[j]
+                    if cur < least[j]:
+                        least[j], way[j] = cur, j0
+                    if least[j] < delta:
+                        delta, j1 = least[j], j
+            for j in range(n + 1):
+                if used[j]:
+                    u[match[j]] += delta
+                    v[j] -= delta
+                else:
+                    least[j] -= delta
+            j0 = j1
+            if match[j0] == 0:
+                break
+        while j0:
+            j1 = way[j0]
+            match[j0] = match[j1]
+            j0 = j1
+    for j in range(1, n + 1):
+        to[free_from[match[j] - 1]] = free_to[j - 1]
+    return [(divmod(a, NC), divmod(b, NC)) for a, b in sorted(to.items())]
+
+
+def dot(a, b):
+    return jnp.dot(a, b, preferred_element_type=jnp.float32)
+
+
+def low(a):
+    return a.astype(jnp.bfloat16)
+
+
+def at(device):
+    return (lax.axis_index("row") == device[0]) & (lax.axis_index("col") == device[1])
+
+
+def any_of(devices):
+    flag = at(devices[0])
+    for d in devices[1:]:
+        flag = flag | at(d)
+    return flag
+
+
+def call(kernel, outs, ins, in_specs, out_specs, scratch=(), limit=16):
+    return pl.pallas_call(
+        kernel,
+        out_shape=outs,
+        in_specs=in_specs,
+        out_specs=out_specs,
+        scratch_shapes=list(scratch),
+        compiler_params=pltpu.CompilerParams(vmem_limit_bytes=limit << 20),
+        name=kernel.func.__name__ if isinstance(kernel, functools.partial) else kernel.__name__,
+    )(*ins)
+
+
+def cut0_kernel(diag_ref, hi_ref, lo_ref, sem):
+    row = lax.axis_index("row")
+    half = lo_ref.shape[1]
+
+    @pl.when(row >= 4)
+    def _():
+        copy = pltpu.make_async_copy(diag_ref.at[0], hi_ref, sem)
+        copy.start()
+        copy.wait()
+
+    @pl.when(row < 4)
+    def _():
+        copy = pltpu.make_async_copy(diag_ref.at[0, :, pl.ds(0, half)], lo_ref, sem)
+        copy.start()
+        copy.wait()
+
+
+def first_kernel(rhs_ref, hi_ref, lo_ref, out_ref, rhs_v, sem):
+    n = hi_ref.shape[0]
+
+    @pl.when(lax.axis_index("row") == 0)
+    def _():
+        copy = pltpu.make_async_copy(rhs_ref.at[0], rhs_v, sem)
+        copy.start()
+        copy.wait()
+        p = low(rhs_v[...])
+        out_ref[:n] = low(dot(hi_ref[...], p))
+        out_ref[n:] = low(dot(lo_ref[...], p[: lo_ref.shape[1]]))
+
+
+def step0_kernel(g0, g1, g2, g3, rhs_ref, l_ref, p_ref, q_ref, s_ref):
+    size = l_ref.shape[0]
+    part = size // NR
+    row = lax.axis_index("row")
+    active = (row < 4) & (lax.axis_index("col") == 0)
+
+    @pl.when(active)
+    def _():
+        for j, got in enumerate((g0, g1, g2, g3)):
+            src = lax.rem(row + 7 - j, 4)
+            hi = pl.multiple_of((4 + src) * part, part)
+            lo = pl.multiple_of(lax.rem(src + 1, 4) * part, part)
+            q_ref[pl.ds(hi, part)] = got[:part]
+            q_ref[pl.ds(lo, part)] = got[part:]
+
+    @pl.when(active & (row > 0))
+    def _():
+        s = dot(l_ref[...], q_ref[...])
+        s_ref[...] = low(s)
+        p_ref[...] = low(rhs_ref[0] - s)
+
+    @pl.when(jnp.logical_not(active))
+    def _():
+        q_ref[...] = jnp.zeros_like(q_ref)
+
+
+def cut_kernel(diag_ref, after_ref, *refs):
+    cuts, sem = refs[:NR], refs[NR]
+    row, col = lax.axis_index("row"), lax.axis_index("col")
+    part = diag_ref.shape[1]
+    for r in range(NR):
+
+        @pl.when(row == r)
+        def _():
+            copy = pltpu.make_async_copy(diag_ref.at[col, :, pl.ds(0, (r + 1) * part)], cuts[r], sem)
+            copy.start()
+            copy.wait()
+
+
+def join_kernel(rows, *refs):
+    n = len(rows)
+    parts, own = refs[:n], refs[n : 2 * n]
+    out_ref, sem = refs[-2:]
+    part = parts[0].shape[0]
+    row = lax.axis_index("row")
+
+    @pl.when(any_of(MAKER[1:]))
+    def _():
+        def copy(i, source):
+            width = (rows[i] + 1) * part
+            return pltpu.make_async_copy(source, out_ref.at[pl.ds(i * part, part), pl.ds(0, width)], sem.at[i])
+
+        for i in range(n):
+
+            @pl.when(row == rows[i])
+            def _():
+                copy(i, own[i]).start()
+
+            @pl.when(row != rows[i])
+            def _():
+                copy(i, parts[i]).start()
+
+        for i in range(n):
+            right = (rows[i] + 1) * part
+            rest = out_ref.shape[1] - right
+            if rest:
+                out_ref[pl.ds(i * part, part), pl.ds(right, rest)] = jnp.zeros((part, rest), out_ref.dtype)
+        for i in range(n):
+            copy(i, parts[i]).wait()
+
+
+def lower_dot(q_ref, d_refs, p):
+    top = 0
+    for d in d_refs:
+        bottom = top + d.shape[0]
+        q_ref[top:bottom] = low(dot(d[:, :bottom], p[:bottom]))
+        top = bottom
+
+
+def step1_kernel(p_ref, sum_ref, rhs_ref, d0, d1, d2, l_ref, q_prev, s_prev, msg_ref, q_ref, s_ref):
+    size = l_ref.shape[0]
+    active = at(MAKER[1])
+
+    @pl.when(active)
+    def _():
+        lower_dot(q_ref, (d0, d1, d2), p_ref[...])
+        q = q_ref[...]
+        s = dot(l_ref[...], q) + sum_ref[...].astype(jnp.float32)
+        s_ref[...] = low(s)
+        msg_ref[:size] = low(rhs_ref[0] - s)
+        msg_ref[size:] = q
+
+    @pl.when(jnp.logical_not(active))
+    def _():
+        q_ref[...] = q_prev[...]
+        s_ref[...] = s_prev[...]
+
+
+def step2_kernel(in_ref, sum_ref, rhs_ref, d0, d1, d2, l_ref, l2_ref, q_prev, s_prev, p_ref, q_ref, s_ref):
+    size = l_ref.shape[0]
+    active = at(MAKER[2])
+
+    @pl.when(active)
+    def _():
+        lower_dot(q_ref, (d0, d1, d2), in_ref[:size])
+        s = dot(l_ref[...], q_ref[...]) + dot(l2_ref[...], in_ref[size:]) + sum_ref[...].astype(jnp.float32)
+        s_ref[...] = low(s)
+        p_ref[...] = low(rhs_ref[0] - s)
+
+    @pl.when(jnp.logical_not(active))
+    def _():
+        q_ref[...] = q_prev[...]
+        s_ref[...] = s_prev[...]
+
+
+def step3_kernel(p_ref, near_ref, d0, d1, d2, q_ref):
+    active = at(MAKER[3])
+
+    @pl.when(active)
+    def _():
+        lower_dot(q_ref, (d0, d1, d2), p_ref[...])
+
+    @pl.when(jnp.logical_not(active))
+    def _():
+        q_ref[...] = near_ref[...]
+
+
+def update_kernel(rows_ref, counts_ref, s_ref, l_ref, *refs):
+    parts, q_ref, out_ref = refs[:-2], refs[-2], refs[-1]
+    size = l_ref.shape[0]
+    row, col = lax.axis_index("row"), lax.axis_index("col")
+    below = row >= NC
+    q = parts[0][...]
+    for p in parts[1:]:
+        q = q + p[...]
+    q_ref[...] = q
+
+    @pl.when(below)
+    def _():
+        out_ref[pl.ds(0, size)] = low(dot(l_ref[...], q_ref[...]))
+
+    @pl.when(jnp.logical_not(below))
+    def _():
+        out_ref[pl.ds(0, size)] = s_ref[...]
+
+    listed = rows_ref[0, 0, 0, 0]
+    there = below & (counts_ref[0, 0, 0] > 0)
+    first = (there & (listed == 0)) | (jnp.logical_not(below) & (row >= 1) & (col == row - 1))
+    second = there & (listed == 1)
+    ids = lax.broadcasted_iota(jnp.int32, (TAIL, out_ref.shape[1]), 0)
+    flag = ((ids == 0) & first) | ((ids == 1) & second)
+    out_ref[pl.ds(size, TAIL)] = low(jnp.where(flag, 1.0, 0.0))
+
+
+def final_kernel(rhs_ref, q_ref, rest_ref, *refs):
+    sums, (solved_ref, out_ref) = refs[:NC], refs[NC:]
+    size = out_ref.shape[1]
+    solved_ref[...] = (q_ref[...] + rest_ref[...]).astype(jnp.float32)
+    for i in range(out_ref.shape[0]):
+        acc = rhs_ref[i]
+        for s in sums:
+            keep = s[pl.ds(size, TAIL)].astype(jnp.float32)[i : i + 1] > 0.5
+            acc = acc - jnp.where(keep, s[pl.ds(0, size)].astype(jnp.float32), 0.0)
+        out_ref[i] = acc
+
+
+def on_device_8x4(rhs, diag_inv, blocks, block_rows, counts):
+    size, width = rhs.shape[2:]
+    part = size // NR
+    rhs = rhs[:, 0]
+    block = blocks[0, 0, 0, 0]
+    bf16 = jnp.bfloat16
+    vec = jax.ShapeDtypeStruct((size, width), bf16)
+    two = jax.ShapeDtypeStruct((2 * size, width), bf16)
+    dma = pltpu.SemaphoreType.DMA
+
+    hi, lo = call(
+        cut0_kernel,
+        [jax.ShapeDtypeStruct((part, size), bf16), jax.ShapeDtypeStruct((part, size // 2), bf16)],
+        [diag_inv],
+        [ANY],
+        [ANY, ANY],
+        [dma],
+    )
+    hi = send(hi, [((4 + c, c), (0, c)) for c in range(4)])
+    lo = send(lo, [(((c + 1) % 4, c), (0, c)) for c in range(4)])
+    q = call(
+        first_kernel,
+        jax.ShapeDtypeStruct((2 * part, width), bf16),
+        [rhs, hi, lo],
+        [ANY, VMEM, VMEM],
+        VMEM,
+        [pltpu.VMEM((size, width), jnp.float32), dma],
+    )
+    takers = ((1, 0), (2, 0), (3, 0), (0, 0))
+    got = [send(q, [((0, c), takers[(c + j) % 4]) for c in range(4)]) for j in range(4)]
+    p, q, s = call(step0_kernel, [vec] * 3, [*got, rhs, block], [VMEM] * 6, [VMEM] * 3)
+    p_in = send(p, complete([(FIRST, MAKER[1])]))
+    side = send(s, complete([((2, 0), MAKER[1]), ((3, 0), MAKER[2])]))
+
+    cuts = call(
+        cut_kernel,
+        [jax.ShapeDtypeStruct((part, (r + 1) * part), bf16) for r in range(NR)],
+        [diag_inv, p],
+        [ANY, ANY],
+        [ANY] * NR,
+        [dma],
+    )
+    parts = {
+        r: send(cuts[r], [((r, c), MAKER[c]) for c in range(1, NC) if MAKER[c][0] != r]) for r in (7, 6, 5, 4, 3, 2, 1, 0)
+    }
+    block2 = send(block, [((3, 1), MAKER[2])])
+    diag = []
+    for rows in ((6, 7), (4, 5), (0, 1, 2, 3)):
+        take = [parts[r] for r in rows]
+        if diag:
+            take[0], diag[-1] = lax.optimization_barrier((take[0], diag[-1]))
+        diag.append(
+            call(
+                functools.partial(join_kernel, rows),
+                jax.ShapeDtypeStruct((len(rows) * part, (rows[-1] + 1) * part), bf16),
+                take + [cuts[r] for r in rows],
+                [ANY] * (2 * len(rows)),
+                VMEM,
+                [pltpu.SemaphoreType.DMA((len(rows),))],
+            )
+        )
+    diag = diag[::-1]
+
+    msg, q, s = call(
+        step1_kernel, [two, vec, vec], [p_in, side, rhs, *diag, block, q, s], [VMEM] * 9, [VMEM] * 3
+    )
+    msg = send(msg, complete([(MAKER[1], MAKER[2])]))
+
+    def tree(value, *columns):
+        return send(value, [((a, k), (b, k)) for k, edges in enumerate(columns) for a, b in edges])
+
+    q = q + tree(q, [(0, 4), (1, 5), (2, 6), (3, 7)], [(2, 4)])
+    q = q + tree(q, [], [(4, 5), (2, 3)])
+    msg, q = lax.optimization_barrier((msg, q))
+    got = tree(q, [], [(4, 6), (5, 7), (2, 0), (3, 1)])
+
+    p, q, s = call(
+        step2_kernel,
+        [vec, vec, vec],
+        [msg, side, rhs, *diag, block, block2, q, s],
+        [VMEM] * 10,
+        [VMEM] * 3,
+    )
+    p = send(p, [(MAKER[2], MAKER[3])])
+    near = send(q, [(MAKER[2], NEAR)])
+    hub = call(step3_kernel, vec, [p, near, *diag], [VMEM] * 5, VMEM)
+    last = [send(hub, [((5, c), (r, c)) for c in (2, 3)]) for r in (4, 7, 6)]
+    q, mine = call(
+        update_kernel,
+        [vec, jax.ShapeDtypeStruct((size + TAIL, width), bf16)],
+        [block_rows, counts, s, block, q, got, hub, *last],
+        [SMEM] * 2 + [VMEM] * 8,
+        [VMEM] * 2,
+    )
+
+    def swap(value, step):
+        return send(value, [((r, c), (r, c ^ step)) for r in range(NR) for c in range(NC)])
+
+    beside = swap(mine, 1)
+    across = swap(mine, 2)
+    corner = swap(across, 1)
+    rest = send(
+        q, [((a, 3), (b, 3)) for a, b in ((5, 1), (7, 3), (4, 2), (6, 0))] + [((a, 2), (a - 4, 2)) for a in (4, 5, 6)]
+    )
+    solved, remainder = call(
+        final_kernel,
+        [jax.ShapeDtypeStruct((size, width), jnp.float32), jax.ShapeDtypeStruct(rhs.shape, jnp.float32)],
+        [rhs, q, rest, mine, beside, across, corner],
+        [VMEM] * 7,
+        [VMEM] * 2,
+    )
+    return solved[None, None], remainder[:, None]
+
+
 def solution(mesh):
     in_specs = (
         P(None, "row", None, None),
@@ -61,6 +463,11 @@
         P(None, "col", "row"),
     )
     out_specs = (P(None, "col", None, None), P(None, "row", None, None))
+    small = mesh.shape["row"] == NR and mesh.shape["col"] == NC
     return jax.shard_map(
-        on_device, mesh=mesh, in_specs=in_specs, out_specs=out_specs, check_vma=False
-    )
+        on_device_8x4 if small else on_device_any,
+        mesh=mesh,
+        in_specs=in_specs,
+        out_specs=out_specs,
+        check_vma=False,
+    )

time: 605 us -> 103 us (0.17)
  waiting for transfers between devices: 448 us -> 35.2 us
  blocking collectives: 99.5 us -> 0 us
  starting transfers between devices: 0.33 us -> 59.3 us
  other arithmetic: 18.2 us -> 0.14 us
  between operations: 15.6 us -> 2.44 us
  matrix products: 10.9 us -> 0 us
  local copies, waits for them, and re-layouts: 9.67 us -> 2.45 us
    psum x8 -> x0, waiting for transfers between devices: 448 us -> none  [the longest x4 286 us: broadcast(): return lax.psum(jnp.where(mine, value, jnp.zeros_like(value)), axis)]
    all_gather x4 -> x0, blocking collectives: 99.5 us -> none  [on_device(): sol = lax.all_gather(row_part, 'row', axis=0, tiled=True)]
    ppermute x0 -> x30, starting transfers between devices: none -> 59.3 us  [send(): lax.ppermute(value, ('row', 'col'), [(a * NC + b, c * NC + d) for (a, b),...]
    ppermute x0 -> x30, waiting for transfers between devices: none -> 35.2 us  [send(): lax.ppermute(value, ('row', 'col'), [(a * NC + b, c * NC + d) for (a, b),...]
    dot_general x8 -> x0, matrix products: 10.9 us -> none  [the longest x4 5.72 us: on_device(): jnp.einsum('sab,bn->san', blocks[j, 0, 0], sol_bf, preferred_element_type...]
    select_n x7 -> x0, other arithmetic: 10.3 us -> none  [the longest x4 7.8 us: broadcast(): return lax.psum(jnp.where(mine, value, jnp.zeros_like(value)), axis)]
  transfers between devices with their start and end apart: 8 -> 30, of which waited for: 8 -> 3; matrix products, arithmetic and copies ran while one was open for 0% -> 0% of each run, Pallas kernels for 0% -> 0%
where the time goes in v4:
time: 103 us; the launch traced here: 102 us
  starting transfers between devices  59.3 us (58%)
  waiting for transfers between devices  35.2 us (34%)
  local copies, waits for them, and re-layouts  2.45 us (2%)
  between operations  2.44 us (2%)
  Pallas kernels  2.07 us (2%)
    ppermute x30, starting transfers between devices, send(): lax.ppermute(value, ('row', 'col'), [(a * NC + b, c * NC + d) for (a, b),...  59.3 us
    ppermute x30, waiting for transfers between devices, send(): lax.ppermute(value, ('row', 'col'), [(a * NC + b, c * NC + d) for (a, b),...  35.2 us
    unnamed x10, local copies, waits for them, and re-layouts  2.45 us
    pallas_call x12, Pallas kernels, call(): pl.pallas_call(kernel, out_shape=outs, in_specs=in_specs, out_specs=out_s...  2.07 us
  transfers between devices with their start and end apart: 30, of which 3 were waited for; matrix products, arithmetic and copies ran while one was open for 0% of the time, Pallas kernels for 0%

profile of v4, /device:TPU:7, one launch (start us, length us, event | category | flops | bytes accessed | tf_op | source)
XLA Modules:
  0.0 101.6 jit_solution(13491053137038810836)
XLA Ops:
  0.6 0.9 collective-permute-start.19
  1.6 1.2 %copy-done.3 = bf16[4,128,1024]{2,1,0:T(8,128)(2,1)S(1)} copy-done((bf16[4,128,1024]{2,1,0:T(8,128)(2,1)S(1)}, bf16[4,128,1024]{2,1,0:T(8,128)(2,1)}, u32[]{:S(2)}) %copy-start.3) | copy-done | bytes 1048600
  2.8 0.7 collective-permute-start
  4.2 1.2 %copy-done.1 = f32[2,1,1024,128]{3,2,1,0:T(8,128)S(1)} copy-done((f32[2,1,1024,128]{3,2,1,0:T(8,128)S(1)}, f32[2,1,1024,128]{3,2,1,0:T(8,128)}, u32[]{:S(2)}) %copy-start.1) | copy-done | bytes 1048600
  5.5 0.8 collective-permute-start.2
  8.5 0.8 collective-permute-start.12
  9.3 4.2 %collective-permute-start.13 = (bf16[128,256]{1,0:T(8,128)(2,1)S(1)}, bf16[128,256]{1,0:T(8,128)(2,1)S(1)}, u32[]{:S(2)}, u32[]{:S(2)}) collective-permute-start(bf16[128,256]{1,0:T(8,128)(2,1)S(1)} %get-tuple-element.42.refs_5_), channel_id=1, source_target_pairs={{5,9},{6,14},{7,23}} | collective-permute-start | bytes 196616 | tf_op jit(solution)/shard_map/ppermute | solution.py:71
  14.9 0.7 collective-permute-start.11
  15.6 0.7 collective-permute-start.10
  16.3 7.5 %collective-permute-start.7 = (bf16[1024,128]{1,0:T(8,128)(2,1)S(1)}, bf16[1024,128]{1,0:T(8,128)(2,1)S(1)}, u32[]{:S(2)}, u32[]{:S(2)}) collective-permute-start(bf16[1024,128]{1,0:T(8,128)(2,1)S(1)} %get-tuple-element.34.s_prev), channel_id=1, source_target_pairs={{0,1},{1,0},{2,3},{3,2},{4,5},{5,4},{6,7},{7,6},{8,9},{9,8},{10,11... | collective-permute-start | bytes 786440 | tf_op jit(solution)/shard_map/ppermute | solution.py:71
  25.5 0.7 collective-permute-start.17
  26.8 0.7 collective-permute-start.18
  27.6 0.7 collective-permute-done.16.in_ref
  28.3 0.7 collective-permute-start.21
  29.0 0.7 collective-permute-start.22
  29.7 0.7 collective-permute-start.20
  30.4 0.7 collective-permute-start.23
  31.1 0.7 collective-permute-start.24
  31.8 0.7 collective-permute-start.25
  34.0 30.4 %collective-permute-start.28 = (bf16[1040,128]{1,0:T(8,128)(2,1)S(1)}, bf16[1040,128]{1,0:T(8,128)(2,1)S(1)}, u32[]{:S(2)}, u32[]{:S(2)}) collective-permute-start(bf16[1040,128]{1,0:T(8,128)(2,1)S(1)} %get-tuple-element.57.refs_0_), channel_id=1, source_target_pairs={{0,2},{1,3},{2,0},{3,1},{4,6},{5,7},{6,4},{7,5},{8,10},{9,11},{10,... | collective-permute-start | bytes 798728 | tf_op jit(solution)/shard_map/ppermute | solution.py:71
  64.4 3.8 %collective-permute-done.28.refs_2_ = bf16[1040,128]{1,0:T(8,128)(2,1)S(1)} collective-permute-done((bf16[1040,128]{1,0:T(8,128)(2,1)S(1)}, bf16[1040,128]{1,0:T(8,128)(2,1)S(1)}, u32[]{:S(2)}, u32[]{:S(2)}) %collective-permute-start.28) | collective-permute-done | bytes 266272 | tf_op jit(solution)/shard_map/ppermute | solution.py:71
  68.2 1.3 %collective-permute-start.26 = (bf16[1024,128]{1,0:T(8,128)(2,1)S(1)}, bf16[1024,128]{1,0:T(8,128)(2,1)S(1)}, u32[]{:S(2)}, u32[]{:S(2)}) collective-permute-start(bf16[1024,128]{1,0:T(8,128)(2,1)S(1)} %get-tuple-element.56.q_ref), channel_id=1, source_target_pairs={{23,7},{31,15},{19,11},{27,3},{18,2},{22,6},{26,10}} | collective-permute-start | bytes 786440 | tf_op jit(solution)/shard_map/ppermute | solution.py:71
  69.5 30.6 %collective-permute-done.26.rest_ref = bf16[1024,128]{1,0:T(8,128)(2,1)S(1)} collective-permute-done((bf16[1024,128]{1,0:T(8,128)(2,1)S(1)}, bf16[1024,128]{1,0:T(8,128)(2,1)S(1)}, u32[]{:S(2)}, u32[]{:S(2)}) %collective-permute-start.26) | collective-permute-done | bytes 262176 | tf_op jit(solution)/shard_map/ppermute | solution.py:71
  100.2 1.5 %final_kernel.1 = (f32[1024,128]{1,0:T(8,128)}, f32[2,1024,128]{2,1,0:T(8,128)}) custom-call(f32[2,1024,128]{2,1,0:T(8,128)S(1)} %bitcast.15, bf16[1024,128]{1,0:T(8,128)(2,1)S(1)} %get-tuple-element.56.q_ref, bf16[1024,128]{1,0:T(8,128)(2,1)S(1)} %collective-permute-done.26.rest_ref, bf16[1040,128]{1,0:T(8,128)(2,1)S(1)} %get-tuple-element.57.refs_0_, ...), custom_call_target="tpu_custom_call" | custom-call | tf_op jit(solution)/shard_map/final_kernel/pallas_call | solution.py:136
  (60 shorter events, 6.8 us)
Async XLA Ops:
  0.6 27.6 %collective-permute-start.19 = (bf16[1024,1024]{1,0:T(8,128)(2,1)}, bf16[1024,1024]{1,0:T(8,128)(2,1)S(1)}, u32[]{:S(2)}, u32[]{:S(2)}) collective-permute-start(bf16[1024,1024]{1,0:T(8,128)(2,1)} %bitcast.6), channel_id=1, source_target_pairs={{13,14}} | collective-permute-start | bytes 6291464 | tf_op jit(solution)/shard_map/ppermute | solution.py:71
  2.8 1.4 %collective-permute-start = (bf16[128,1024]{1,0:T(8,128)(2,1)S(1)}, bf16[128,1024]{1,0:T(8,128)(2,1)S(1)}, u32[]{:S(2)}, u32[]{:S(2)}) collective-permute-start(bf16[128,1024]{1,0:T(8,128)(2,1)S(1)} %get-tuple-element.31), channel_id=1, source_target_pairs={{16,0},{21,1},{26,2},{31,3}} | collective-permute-start | bytes 786440 | tf_op jit(solution)/shard_map/ppermute | solution.py:71
  5.5 2.8 %collective-permute-start.2 = (bf16[256,128]{1,0:T(8,128)(2,1)S(1)}, bf16[256,128]{1,0:T(8,128)(2,1)S(1)}, u32[]{:S(2)}, u32[]{:S(2)}) collective-permute-start(bf16[256,128]{1,0:T(8,128)(2,1)S(1)} %first_kernel.1), channel_id=1, source_target_pairs={{0,4},{1,8},{2,12},{3,0}} | collective-permute-start | bytes 196616 | tf_op jit(solution)/shard_map/ppermute | solution.py:71
  6.3 2.0 %collective-permute-start.3 = (bf16[256,128]{1,0:T(8,128)(2,1)S(1)}, bf16[256,128]{1,0:T(8,128)(2,1)S(1)}, u32[]{:S(2)}, u32[]{:S(2)}) collective-permute-start(bf16[256,128]{1,0:T(8,128)(2,1)S(1)} %first_kernel.1), channel_id=1, source_target_pairs={{0,8},{1,12},{2,0},{3,4}} | collective-permute-start | bytes 196616 | tf_op jit(solution)/shard_map/ppermute | solution.py:71
  6.9 1.4 %collective-permute-start.4 = (bf16[256,128]{1,0:T(8,128)(2,1)S(1)}, bf16[256,128]{1,0:T(8,128)(2,1)S(1)}, u32[]{:S(2)}, u32[]{:S(2)}) collective-permute-start(bf16[256,128]{1,0:T(8,128)(2,1)S(1)} %first_kernel.1), channel_id=1, source_target_pairs={{0,12},{1,0},{2,4},{3,8}} | collective-permute-start | bytes 196616 | tf_op jit(solution)/shard_map/ppermute | solution.py:71
  8.5 15.3 %collective-permute-start.12 = (bf16[128,768]{1,0:T(8,128)(2,1)S(1)}, bf16[128,768]{1,0:T(8,128)(2,1)S(1)}, u32[]{:S(2)}, u32[]{:S(2)}) collective-permute-start(bf16[128,768]{1,0:T(8,128)(2,1)S(1)} %get-tuple-element.40.refs_3_), channel_id=1, source_target_pairs={{21,9},{22,14}} | collective-permute-start | bytes 589832 | tf_op jit(solution)/shard_map/ppermute | solution.py:71
  9.3 6.3 %collective-permute-start.13 = (bf16[128,256]{1,0:T(8,128)(2,1)S(1)}, bf16[128,256]{1,0:T(8,128)(2,1)S(1)}, u32[]{:S(2)}, u32[]{:S(2)}) collective-permute-start(bf16[128,256]{1,0:T(8,128)(2,1)S(1)} %get-tuple-element.42.refs_5_), channel_id=1, source_target_pairs={{5,9},{6,14},{7,23}} | collective-permute-start | bytes 196616 | tf_op jit(solution)/shard_map/ppermute | solution.py:71
  13.6 2.7 %collective-permute-start.9 = (bf16[128,640]{1,0:T(8,128)(2,1)S(1)}, bf16[128,640]{1,0:T(8,128)(2,1)S(1)}, u32[]{:S(2)}, u32[]{:S(2)}) collective-permute-start(bf16[128,640]{1,0:T(8,128)(2,1)S(1)} %get-tuple-element.36.refs_2_), channel_id=1, source_target_pairs={{17,9},{18,14},{19,23}} | collective-permute-start | bytes 491528 | tf_op jit(solution)/shard_map/ppermute | solution.py:71
  14.9 9.7 %collective-permute-start.11 = (bf16[128,1024]{1,0:T(8,128)(2,1)S(1)}, bf16[128,1024]{1,0:T(8,128)(2,1)S(1)}, u32[]{:S(2)}, u32[]{:S(2)}) collective-permute-start(bf16[128,1024]{1,0:T(8,128)(2,1)S(1)} %get-tuple-element.38.refs_3_), channel_id=1, source_target_pairs={{29,9},{30,14},{31,23}} | collective-permute-start | bytes 786440 | tf_op jit(solution)/shard_map/ppermute | solution.py:71
  15.6 8.3 %collective-permute-start.10 = (bf16[128,896]{1,0:T(8,128)(2,1)S(1)}, bf16[128,896]{1,0:T(8,128)(2,1)S(1)}, u32[]{:S(2)}, u32[]{:S(2)}) collective-permute-start(bf16[128,896]{1,0:T(8,128)(2,1)S(1)} %get-tuple-element.37.refs_2_), channel_id=1, source_target_pairs={{25,9},{26,14},{27,23}} | collective-permute-start | bytes 688136 | tf_op jit(solution)/shard_map/ppermute | solution.py:71
  16.3 9.1 %collective-permute-start.7 = (bf16[1024,128]{1,0:T(8,128)(2,1)S(1)}, bf16[1024,128]{1,0:T(8,128)(2,1)S(1)}, u32[]{:S(2)}, u32[]{:S(2)}) collective-permute-start(bf16[1024,128]{1,0:T(8,128)(2,1)S(1)} %get-tuple-element.34.s_prev), channel_id=1, source_target_pairs={{0,1},{1,0},{2,3},{3,2},{4,5},{5,4},{6,7},{7,6},{8,9},{9,8},{10,11... | collective-permute-start | bytes 786440 | tf_op jit(solution)/shard_map/ppermute | solution.py:71
  23.8 1.6 %collective-permute-start.6 = (bf16[1024,128]{1,0:T(8,128)(2,1)S(1)}, bf16[1024,128]{1,0:T(8,128)(2,1)S(1)}, u32[]{:S(2)}, u32[]{:S(2)}) collective-permute-start(bf16[1024,128]{1,0:T(8,128)(2,1)S(1)} %get-tuple-element.33.after_ref), channel_id=1, source_target_pairs={{0,1},{1,5},{2,3},{3,2},{4,9},{5,4},{6,7},{7,6},{8,0},{9,8},{10,11... | collective-permute-start | bytes 786440 | tf_op jit(solution)/shard_map/ppermute | solution.py:71
  23.9 1.5 %collective-permute-start.15 = (bf16[128,512]{1,0:T(8,128)(2,1)S(1)}, bf16[128,512]{1,0:T(8,128)(2,1)S(1)}, u32[]{:S(2)}, u32[]{:S(2)}) collective-permute-start(bf16[128,512]{1,0:T(8,128)(2,1)S(1)} %get-tuple-element.44.refs_7_), channel_id=1, source_target_pairs={{13,9},{15,23}} | collective-permute-start | bytes 393224 | tf_op jit(solution)/shard_map/ppermute | solution.py:71
  26.2 2.0 %collective-permute-start.16 = (bf16[2048,128]{1,0:T(8,128)(2,1)S(1)}, bf16[2048,128]{1,0:T(8,128)(2,1)S(1)}, u32[]{:S(2)}, u32[]{:S(2)}) collective-permute-start(bf16[2048,128]{1,0:T(8,128)(2,1)S(1)} %get-tuple-element.48), channel_id=1, source_target_pairs={{0,1},{1,0},{2,3},{3,2},{4,5},{5,4},{6,7},{7,6},{8,9},{9,14},{10,8... | collective-permute-start | bytes 1572872 | tf_op jit(solution)/shard_map/ppermute | solution.py:71
  28.3 2.1 %collective-permute-start.21 = (bf16[1024,128]{1,0:T(8,128)(2,1)S(1)}, bf16[1024,128]{1,0:T(8,128)(2,1)S(1)}, u32[]{:S(2)}, u32[]{:S(2)}) collective-permute-start(bf16[1024,128]{1,0:T(8,128)(2,1)S(1)} %get-tuple-element.55), channel_id=1, source_target_pairs={{14,23}} | collective-permute-start | bytes 786440 | tf_op jit(solution)/shard_map/ppermute | solution.py:71
  29.0 1.4 %collective-permute-start.22 = (bf16[1024,128]{1,0:T(8,128)(2,1)S(1)}, bf16[1024,128]{1,0:T(8,128)(2,1)S(1)}, u32[]{:S(2)}, u32[]{:S(2)}) collective-permute-start(bf16[1024,128]{1,0:T(8,128)(2,1)S(1)} %get-tuple-element.54.refs_0_), channel_id=1, source_target_pairs={{14,22}} | collective-permute-start | bytes 786440 | tf_op jit(solution)/shard_map/ppermute | solution.py:71
  29.7 4.1 %collective-permute-start.20 = (bf16[1024,128]{1,0:T(8,128)(2,1)S(1)}, bf16[1024,128]{1,0:T(8,128)(2,1)S(1)}, u32[]{:S(2)}, u32[]{:S(2)}) collective-permute-start(bf16[1024,128]{1,0:T(8,128)(2,1)S(1)} %add.7.q_prev), channel_id=1, source_target_pairs={{17,25},{21,29},{9,1},{13,5}} | collective-permute-start | bytes 786440 | tf_op jit(solution)/shard_map/ppermute | solution.py:71
  30.4 3.4 %collective-permute-start.23 = (bf16[1024,128]{1,0:T(8,128)(2,1)S(1)}, bf16[1024,128]{1,0:T(8,128)(2,1)S(1)}, u32[]{:S(2)}, u32[]{:S(2)}) collective-permute-start(bf16[1024,128]{1,0:T(8,128)(2,1)S(1)} %step3_kernel.1.refs_2_), channel_id=1, source_target_pairs={{22,18},{23,19}} | collective-permute-start | bytes 786440 | tf_op jit(solution)/shard_map/ppermute | solution.py:71
  31.1 2.7 %collective-permute-start.24 = (bf16[1024,128]{1,0:T(8,128)(2,1)S(1)}, bf16[1024,128]{1,0:T(8,128)(2,1)S(1)}, u32[]{:S(2)}, u32[]{:S(2)}) collective-permute-start(bf16[1024,128]{1,0:T(8,128)(2,1)S(1)} %step3_kernel.1.refs_2_), channel_id=1, source_target_pairs={{22,30},{23,31}} | collective-permute-start | bytes 786440 | tf_op jit(solution)/shard_map/ppermute | solution.py:71
  31.8 2.0 %collective-permute-start.25 = (bf16[1024,128]{1,0:T(8,128)(2,1)S(1)}, bf16[1024,128]{1,0:T(8,128)(2,1)S(1)}, u32[]{:S(2)}, u32[]{:S(2)}) collective-permute-start(bf16[1024,128]{1,0:T(8,128)(2,1)S(1)} %step3_kernel.1.refs_2_), channel_id=1, source_target_pairs={{22,26},{23,27}} | collective-permute-start | bytes 786440 | tf_op jit(solution)/shard_map/ppermute | solution.py:71
  34.0 34.2 %collective-permute-start.28 = (bf16[1040,128]{1,0:T(8,128)(2,1)S(1)}, bf16[1040,128]{1,0:T(8,128)(2,1)S(1)}, u32[]{:S(2)}, u32[]{:S(2)}) collective-permute-start(bf16[1040,128]{1,0:T(8,128)(2,1)S(1)} %get-tuple-element.57.refs_0_), channel_id=1, source_target_pairs={{0,2},{1,3},{2,0},{3,1},{4,6},{5,7},{6,4},{7,5},{8,10},{9,11},{10,... | collective-permute-start | bytes 798728 | tf_op jit(solution)/shard_map/ppermute | solution.py:71
  64.4 35.7 %collective-permute-start.27 = (bf16[1040,128]{1,0:T(8,128)(2,1)S(1)}, bf16[1040,128]{1,0:T(8,128)(2,1)S(1)}, u32[]{:S(2)}, u32[]{:S(2)}) collective-permute-start(bf16[1040,128]{1,0:T(8,128)(2,1)S(1)} %get-tuple-element.57.refs_0_), channel_id=1, source_target_pairs={{0,1},{1,0},{2,3},{3,2},{4,5},{5,4},{6,7},{7,6},{8,9},{9,8},{10,11... | collective-permute-start | bytes 798728 | tf_op jit(solution)/shard_map/ppermute | solution.py:71
  68.2 31.9 %collective-permute-start.29 = (bf16[1040,128]{1,0:T(8,128)(2,1)S(1)}, bf16[1040,128]{1,0:T(8,128)(2,1)S(1)}, u32[]{:S(2)}, u32[]{:S(2)}) collective-permute-start(bf16[1040,128]{1,0:T(8,128)(2,1)S(1)} %collective-permute-done.28.refs_2_), channel_id=1, source_target_pairs={{0,1},{1,0},{2,3},{3,2},{4,5},{5,4},{6,7},{7,6},{8,9},{9,8},{10,11... | collective-permute-start | bytes 798728 | tf_op jit(solution)/shard_map/ppermute | solution.py:71
  68.2 31.9 %collective-permute-start.26 = (bf16[1024,128]{1,0:T(8,128)(2,1)S(1)}, bf16[1024,128]{1,0:T(8,128)(2,1)S(1)}, u32[]{:S(2)}, u32[]{:S(2)}) collective-permute-start(bf16[1024,128]{1,0:T(8,128)(2,1)S(1)} %get-tuple-element.56.q_ref), channel_id=1, source_target_pairs={{23,7},{31,15},{19,11},{27,3},{18,2},{22,6},{26,10}} | collective-permute-start | bytes 786440 | tf_op jit(solution)/shard_map/ppermute | solution.py:71
  (11 other events, 34.8 us)

commit v5 on v4

v5 whole, which is shorter than its diff:
```python
import functools

import jax
import jax.numpy as jnp
from jax import lax
from jax.experimental import pallas as pl
from jax.experimental.pallas import tpu as pltpu
from jax.sharding import PartitionSpec as P

VMEM = pl.BlockSpec(memory_space=pltpu.VMEM)
ANY = pl.BlockSpec(memory_space=pl.ANY)
HBM = pl.BlockSpec(memory_space=pltpu.HBM)
SMEM = pl.BlockSpec(memory_space=pltpu.SMEM)
TAIL = 16


def broadcast(value, axis, root):
    mine = lax.axis_index(axis) == root
    return lax.psum(jnp.where(mine, value, jnp.zeros_like(value)), axis)


def on_device_any(rhs, diag_inv, blocks, block_rows, counts):
    nrow = lax.axis_size("row")
    ncol = lax.axis_size("col")
    my_row = lax.axis_index("row")
    my_col = lax.axis_index("col")
    kc = diag_inv.shape[0]
    rb_local = rhs.shape[0]
    nz_local = blocks.shape[3]
    local_rhs = rhs[:, 0]
    partial_value = jnp.zeros(local_rhs.shape, jnp.float32)
    solved_list = [jnp.zeros(local_rhs.shape[1:], jnp.float32)]
    slot_ids = jnp.arange(nz_local, dtype=jnp.int32)
    local_ids = jnp.arange(rb_local, dtype=jnp.int32)
    for k in range(kc):
        j = k // ncol
        owner_row = k % nrow
        local_pivot = k // nrow
        mine_row = my_row == owner_row
        mine_col = my_col == k % ncol
        pivot_part = jnp.where(mine_row, partial_value[local_pivot], jnp.float32(0.0))
        summed = lax.psum(pivot_part, "col")
        updated = (local_rhs[local_pivot] - summed).astype(jnp.bfloat16)
        pivot_bf = broadcast(updated, "row", owner_row)
        row_part = jnp.dot(diag_inv[k], pivot_bf, preferred_element_type=jnp.float32)
        sol = lax.all_gather(row_part, "row", axis=0, tiled=True)
        sol_bf = sol.astype(jnp.bfloat16)
        rows = block_rows[j, 0, 0]
        glob = rows * nrow + my_row
        valid = (slot_ids < counts[j, 0, 0]) & (glob > k) & mine_col
        weights = (valid[:, None] & (rows[:, None] == local_ids[None, :])).astype(jnp.float32)
        contrib = jnp.einsum(
            "sab,bn->san", blocks[j, 0, 0], sol_bf, preferred_element_type=jnp.float32
        )
        partial_value = partial_value + jnp.einsum(
            "sl,san->lan", weights, contrib, precision=lax.Precision.HIGHEST
        )
        solved_list[j] = jnp.where(mine_col, sol, solved_list[j])
    total = lax.psum(partial_value, "col")
    remainder = (local_rhs - total)[:, None]
    solved = jnp.stack(solved_list)[:, None]
    return (solved, remainder)


NR, NC = 8, 4
MAKER = (None, (2, 1), (3, 2), (5, 3))
FIRST = (1, 0)
BESIDE = (3, 1)
NEAR = (5, 2)


def hops(a, b):
    d = a ^ b
    return 4 * (abs((a >> 3) - (b >> 3)) + ((d >> 2) & 1) + ((d >> 1) & 1)) + (d & 1) if d else 1000


def complete(pairs):
    to = {a * NC + b: c * NC + d for (a, b), (c, d) in pairs}
    free_from = [i for i in range(NR * NC) if i not in to]
    free_to = [i for i in range(NR * NC) if i not in to.values()]
    n = len(free_from)
    u, v, match = [0] * (n + 1), [0] * (n + 1), [0] * (n + 1)
    for i in range(1, n + 1):
        match[0], j0 = i, 0
        least, way, used = [10**9] * (n + 1), [0] * (n + 1), [False] * (n + 1)
        while True:
            used[j0] = True
            i0, delta, j1 = match[j0], 10**9, 0
            for j in range(1, n + 1):
                if not used[j]:
                    cur = hops(free_from[i0 - 1], free_to[j - 1]) - u[i0] - v[j]
                    if cur < least[j]:
                        least[j], way[j] = cur, j0
                    if least[j] < delta:
                        delta, j1 = least[j], j
            for j in range(n + 1):
                if used[j]:
                    u[match[j]] += delta
                    v[j] -= delta
                else:
                    least[j] -= delta
            j0 = j1
            if match[j0] == 0:
                break
        while j0:
            j1 = way[j0]
            match[j0] = match[j1]
            j0 = j1
    for j in range(1, n + 1):
        to[free_from[match[j] - 1]] = free_to[j - 1]
    return [(divmod(a, NC), divmod(b, NC)) for a, b in sorted(to.items())]


def send(value, pairs):
    moves = [(a * NC + b, c * NC + d) for (a, b), (c, d) in complete(pairs)]
    return lax.ppermute(value, ("row", "col"), moves)


def dot(a, b):
    return jnp.dot(a, b, preferred_element_type=jnp.float32)


def low(a):
    return a.astype(jnp.bfloat16)


def at(device):
    return (lax.axis_index("row") == device[0]) & (lax.axis_index("col") == device[1])


def any_of(devices):
    flag = at(devices[0])
    for d in devices[1:]:
        flag = flag | at(d)
    return flag


def call(kernel, outs, ins, in_specs, out_specs, scratch=(), limit=16):
    return pl.pallas_call(
        kernel,
        out_shape=outs,
        in_specs=in_specs,
        out_specs=out_specs,
        scratch_shapes=list(scratch),
        compiler_params=pltpu.CompilerParams(vmem_limit_bytes=limit << 20),
        name=kernel.func.__name__ if isinstance(kernel, functools.partial) else kernel.__name__,
    )(*ins)


def cut_kernel(diag_ref, *refs):
    cuts, sem = refs[:NR], refs[NR]
    row, col = lax.axis_index("row"), lax.axis_index("col")
    part = diag_ref.shape[1]
    for r in range(NR):

        @pl.when(row == r)
        def _():
            copy = pltpu.make_async_copy(diag_ref.at[col, :, pl.ds(0, (r + 1) * part)], cuts[r], sem)
            copy.start()
            copy.wait()


def first_kernel(rhs_ref, own_ref, *refs):
    parts, out_ref = refs[:NR], refs[NR]
    rhs_v, lo_v, hi_v, rhs_sem, lo_sem, hi_sem = refs[NR + 1 :]
    n = out_ref.shape[0] // 2
    col = lax.axis_index("col")

    @pl.when(lax.axis_index("row") == 0)
    def _():
        rhs_copy = pltpu.make_async_copy(rhs_ref.at[0], rhs_v, rhs_sem)
        rhs_copy.start()

        def piece(c):
            lo = own_ref if c == 0 else parts[c]
            wide = (4 + c + 1) * n
            return (
                pltpu.make_async_copy(lo, lo_v.at[:, pl.ds(0, (c + 1) * n)], lo_sem),
                pltpu.make_async_copy(parts[4 + c], hi_v.at[:, pl.ds(0, wide)], hi_sem),
            )

        for c in range(NC):

            @pl.when(col == c)
            def _():
                for copy in piece(c):
                    copy.start()

        rhs_copy.wait()
        p = low(rhs_v[...])
        for c in range(NC):

            @pl.when(col == c)
            def _():
                for copy in piece(c):
                    copy.wait()
                wide = (4 + c + 1) * n
                out_ref[:n] = low(dot(hi_v[:, :wide], p[:wide]))
                out_ref[n:] = low(dot(lo_v[:, : (c + 1) * n], p[: (c + 1) * n]))


def whole_kernel(*refs):
    parts, own, out_ref, sem = refs[:NR], refs[NR : 2 * NR], refs[2 * NR], refs[2 * NR + 1]
    size = out_ref.shape[0]
    part = size // NR
    row = lax.axis_index("row")

    @pl.when(any_of(MAKER[1:]))
    def _():
        def copy(i, source):
            return pltpu.make_async_copy(
                source, out_ref.at[pl.ds(i * part, part), pl.ds(0, (i + 1) * part)], sem.at[i]
            )

        for i in range(NR):

            @pl.when(row == i)
            def _():
                copy(i, own[i]).start()

            @pl.when(row != i)
            def _():
                copy(i, parts[i]).start()

        for i in range(NR - 1):
            right = (i + 1) * part
            out_ref[pl.ds(i * part, part), pl.ds(right, size - right)] = jnp.zeros((part, size - right), out_ref.dtype)
        for i in range(NR):
            copy(i, parts[i]).wait()


def lower_dot(q_ref, d_ref, p_ref):
    half = d_ref.shape[0] // 2
    q_ref[:half] = low(dot(d_ref[:half, :half], p_ref[:half]))
    q_ref[half:] = low(dot(d_ref[half:], p_ref[...]))


def step0_kernel(g0, g1, g2, g3, rhs_ref, l_ref, p_ref, q_ref, s_ref):
    part = l_ref.shape[0] // NR
    row = lax.axis_index("row")

    @pl.when((row >= 1) & (row < 4) & (lax.axis_index("col") == 0))
    def _():
        for j, got in enumerate((g0, g1, g2, g3)):
            src = lax.rem(row + 7 - j, 4)
            hi = pl.multiple_of((4 + src) * part, part)
            lo = pl.multiple_of(src * part, part)
            q_ref[pl.ds(hi, part)] = got[:part]
            q_ref[pl.ds(lo, part)] = got[part:]
        s = dot(l_ref[...], q_ref[...])
        s_ref[...] = low(s)
        p_ref[...] = low(rhs_ref[0] - s)


def step1_kernel(p_in, sum_ref, rhs_ref, d_ref, l_ref, q_prev, s_prev, p_ref, q_ref, s_ref):
    active = at(MAKER[1])

    @pl.when(active)
    def _():
        lower_dot(q_ref, d_ref, p_in)
        s = dot(l_ref[...], q_ref[...]) + sum_ref[...].astype(jnp.float32)
        s_ref[...] = low(s)
        p_ref[...] = low(rhs_ref[0] - s)

    @pl.when(jnp.logical_not(active))
    def _():
        q_ref[...] = q_prev[...]
        s_ref[...] = s_prev[...]


def step2_kernel(p_in, q_in, sum_ref, d_ref, l_ref, q_prev, s_prev, q_ref, s_ref):
    active, beside = at(MAKER[2]), at(BESIDE)

    @pl.when(active)
    def _():
        lower_dot(q_ref, d_ref, p_in)
        s_ref[...] = low(dot(l_ref[...], q_ref[...]))

    @pl.when(beside)
    def _():
        q_ref[...] = q_in[...]
        s_ref[...] = low(dot(l_ref[...], q_in[...]) + sum_ref[...].astype(jnp.float32))

    @pl.when(jnp.logical_not(active | beside))
    def _():
        q_ref[...] = q_prev[...]
        s_ref[...] = s_prev[...]


def step3_kernel(sum_ref, rhs_ref, s_prev, p_ref, s_ref):
    active = at(MAKER[2])

    @pl.when(active)
    def _():
        s = s_prev[...].astype(jnp.float32) + sum_ref[...].astype(jnp.float32)
        s_ref[...] = low(s)
        p_ref[...] = low(rhs_ref[0] - s)

    @pl.when(jnp.logical_not(active))
    def _():
        s_ref[...] = s_prev[...]


def step4_kernel(p_in, near_ref, d_ref, q_ref):
    @pl.when(at(MAKER[3]))
    def _():
        lower_dot(q_ref, d_ref, p_in)

    @pl.when(at(NEAR))
    def _():
        q_ref[...] = near_ref[...]


def relay_kernel(q_ref, got_ref, out_ref):
    row = lax.axis_index("row")
    taken = (row == 4) | (row == 5) | at((0, 0))

    @pl.when(taken)
    def _():
        out_ref[...] = got_ref[...]

    @pl.when(jnp.logical_not(taken))
    def _():
        out_ref[...] = q_ref[...]


def update_kernel(rows_ref, counts_ref, s_ref, l_ref, q0, q1, hub, h4, h7, h6, q_ref, out_ref):
    size = l_ref.shape[0]
    row, col = lax.axis_index("row"), lax.axis_index("col")
    below = row >= NC
    right = col >= 2
    late = jnp.logical_not(right) & ((row >= 6) | ((row < 2) & (col == 1)))

    def take(flag, source):
        @pl.when(flag)
        def _():
            q_ref[...] = source[...]

    take(late, q1)
    take(jnp.logical_not(late) & jnp.logical_not(right & below), q0)
    for r, source in ((5, hub), (4, h4), (7, h7), (6, h6)):
        take(right & (row == r), source)

    @pl.when(below)
    def _():
        out_ref[pl.ds(0, size)] = low(dot(l_ref[...], q_ref[...]))

    @pl.when(jnp.logical_not(below))
    def _():
        out_ref[pl.ds(0, size)] = s_ref[...]

    listed = rows_ref[0, 0, 0, 0]
    there = below & (counts_ref[0, 0, 0] > 0)
    first = (there & (listed == 0)) | (jnp.logical_not(below) & (row >= 1) & (col == row - 1))
    second = there & (listed == 1)
    ids = lax.broadcasted_iota(jnp.int32, (TAIL, out_ref.shape[1]), 0)
    flag = ((ids == 0) & first) | ((ids == 1) & second)
    out_ref[pl.ds(size, TAIL)] = low(jnp.where(flag, 1.0, 0.0))


def final_kernel(rhs_ref, q_ref, rest_ref, *refs):
    sums, (solved_ref, out_ref) = refs[:NC], refs[NC:]
    size = out_ref.shape[1]
    row, col = lax.axis_index("row"), lax.axis_index("col")
    came = (row < NC) & (col >= 2) & jnp.logical_not(at(MAKER[2]))

    @pl.when(came)
    def _():
        solved_ref[...] = rest_ref[...].astype(jnp.float32)

    @pl.when(jnp.logical_not(came))
    def _():
        solved_ref[...] = q_ref[...].astype(jnp.float32)

    for i in range(out_ref.shape[0]):
        acc = rhs_ref[i]
        for s in sums:
            keep = s[pl.ds(size, TAIL)].astype(jnp.float32)[i : i + 1] > 0.5
            acc = acc - jnp.where(keep, s[pl.ds(0, size)].astype(jnp.float32), 0.0)
        out_ref[i] = acc


def on_device_8x4(rhs, diag_inv, blocks, block_rows, counts):
    size, width = rhs.shape[2:]
    part = size // NR
    rhs = rhs[:, 0]
    block = blocks[0, 0, 0, 0]
    bf16 = jnp.bfloat16
    vec = jax.ShapeDtypeStruct((size, width), bf16)
    dma = pltpu.SemaphoreType.DMA

    cuts = call(
        cut_kernel,
        [jax.ShapeDtypeStruct((part, (r + 1) * part), bf16) for r in range(NR)],
        [diag_inv],
        [HBM],
        [ANY] * NR,
        [dma],
    )
    parts = []
    for r in range(NR):
        pairs = [((r, 0), (0, r % 4))] if r else []
        pairs += [((r, c), MAKER[c]) for c in range(1, NC) if MAKER[c][0] != r]
        parts.append(send(cuts[r], pairs))
    q = call(
        first_kernel,
        jax.ShapeDtypeStruct((2 * part, width), bf16),
        [rhs, cuts[0], *parts],
        [HBM] + [ANY] * (1 + NR),
        VMEM,
        [
            pltpu.VMEM((size, width), jnp.float32),
            pltpu.VMEM((part, 4 * part), bf16),
            pltpu.VMEM((part, size), bf16),
            dma,
            dma,
            dma,
        ],
    )
    takers = (FIRST, (2, 0), (3, 0))
    got = [send(q, [((0, c), takers[(c + j) % 4]) for c in range(4) if (c + j) % 4 < 3]) for j in range(4)]
    diag = call(
        whole_kernel,
        jax.ShapeDtypeStruct((size, size), bf16),
        [*parts, *cuts],
        [ANY] * (2 * NR),
        VMEM,
        [pltpu.SemaphoreType.DMA((NR,))],
    )

    p, q, s = call(step0_kernel, [vec] * 3, [*got, rhs, block], [VMEM] * 6, [VMEM] * 3)
    p_in = send(p, [(FIRST, MAKER[1])])
    sums = send(s, [((2, 0), MAKER[1]), ((3, 0), BESIDE)])
    p, q, s = call(step1_kernel, [vec] * 3, [p_in, sums, rhs, diag, block, q, s], [VMEM] * 7, [VMEM] * 3)
    p_in = send(p, [(MAKER[1], MAKER[2])])
    q_in = send(q, [(MAKER[1], BESIDE)])
    q, s = call(step2_kernel, [vec] * 2, [p_in, q_in, sums, diag, block, q, s], [VMEM] * 7, [VMEM] * 2)
    sums = send(s, [(BESIDE, MAKER[2])])
    near = send(q, [(MAKER[2], NEAR)])
    p, s = call(step3_kernel, [vec] * 2, [sums, rhs, s], [VMEM] * 3, [VMEM] * 2)
    p_in = send(p, [(MAKER[2], MAKER[3])])

    got = send(
        q, [((2, 0), (4, 0)), ((3, 0), (5, 0)), ((1, 0), (0, 0)), ((2, 1), (4, 1)), ((3, 1), (5, 1))]
    )
    q = call(relay_kernel, vec, [q, got], [VMEM] * 2, VMEM)
    got = send(
        q,
        [((4, c), (6, c)) for c in (0, 1)] + [((5, c), (7, c)) for c in (0, 1)] + [((2, 1), (0, 1)), ((3, 1), (1, 1))],
    )

    hub = call(step4_kernel, vec, [p_in, near, diag], [VMEM] * 3, VMEM)
    last = [send(hub, [((5, c), (r, c)) for c in (2, 3)]) for r in (4, 7, 6)]
    q, mine = call(
        update_kernel,
        [vec, jax.ShapeDtypeStruct((size + TAIL, width), bf16)],
        [block_rows, counts, s, block, q, got, hub, *last],
        [SMEM] * 2 + [VMEM] * 8,
        [VMEM] * 2,
    )

    def swap(value, step):
        return send(value, [((r, c), (r, c ^ step)) for r in range(NR) for c in range(NC)])

    beside = swap(mine, 1)
    across = swap(mine, 2)
    corner = swap(across, 1)
    rest = send(
        q, [((a, 3), (b, 3)) for a, b in ((5, 1), (7, 3), (4, 2), (6, 0))] + [((a, 2), (a - 4, 2)) for a in (4, 5, 6)]
    )
    solved, remainder = call(
        final_kernel,
        [jax.ShapeDtypeStruct((size, width), jnp.float32), jax.ShapeDtypeStruct(rhs.shape, jnp.float32)],
        [rhs, q, rest, mine, beside, across, corner],
        [VMEM] * 7,
        [VMEM] * 2,
    )
    return solved[None, None], remainder[:, None]


def solution(mesh):
    in_specs = (
        P(None, "row", None, None),
        P(None, "row", None),
        P(None, "col", "row", None, None, None),
        P(None, "col", "row", None),
        P(None, "col", "row"),
    )
    out_specs = (P(None, "col", None, None), P(None, "row", None, None))
    small = mesh.shape["row"] == NR and mesh.shape["col"] == NC
    return jax.shard_map(
        on_device_8x4 if small else on_device_any,
        mesh=mesh,
        in_specs=in_specs,
        out_specs=out_specs,
        check_vma=False,
    )
```

time: 103 us -> 80.4 us (0.78)
  starting transfers between devices: 59.3 us -> 45.5 us
  waiting for transfers between devices: 35.2 us -> 28 us
    ppermute x30 -> x28, starting transfers between devices: 59.3 us -> 45.5 us  [send(): return lax.ppermute(value, ('row', 'col'), moves)]
    ppermute x30 -> x28, waiting for transfers between devices: 35.2 us -> 28 us  [send(): return lax.ppermute(value, ('row', 'col'), moves)]
    pallas_call x12 -> x11, Pallas kernels: 2.07 us -> 1.76 us  [call(): pl.pallas_call(kernel, out_shape=outs, in_specs=in_specs, out_specs=out_s...]
    unnamed x10 -> x8, local copies, waits for them, and re-layouts: 2.45 us -> 2.59 us
  transfers between devices with their start and end apart: 30 -> 28, of which waited for: 3 -> 15; matrix products, arithmetic and copies ran while one was open for 0% -> 0% of each run, Pallas kernels for 0% -> 0%
where the time goes in v5:
time: 80.4 us; the launch traced here: 80 us
  starting transfers between devices  45.5 us (57%)
  waiting for transfers between devices  28 us (35%)
  local copies, waits for them, and re-layouts  2.59 us (3%)
  between operations  2.07 us (3%)
  Pallas kernels  1.76 us (2%)
    ppermute x28, starting transfers between devices, send(): return lax.ppermute(value, ('row', 'col'), moves)  45.5 us
    ppermute x28, waiting for transfers between devices, send(): return lax.ppermute(value, ('row', 'col'), moves)  28 us
    unnamed x8, local copies, waits for them, and re-layouts  2.59 us
    pallas_call x11, Pallas kernels, call(): pl.pallas_call(kernel, out_shape=outs, in_specs=in_specs, out_specs=out_s...  1.76 us
  transfers between devices with their start and end apart: 28, of which 15 were waited for; matrix products, arithmetic and copies ran while one was open for 0% of the time, Pallas kernels for 0%

profile of v5, /device:TPU:7, one launch (start us, length us, event | category | flops | bytes accessed | tf_op | source)
XLA Modules:
  0.0 80.0 jit_solution(8175169665621320075)
XLA Ops:
  0.6 1.4 %copy-done.3 = bf16[4,128,1024]{2,1,0:T(8,128)(2,1)S(1)} copy-done((bf16[4,128,1024]{2,1,0:T(8,128)(2,1)S(1)}, bf16[4,128,1024]{2,1,0:T(8,128)(2,1)}, u32[]{:S(2)}) %copy-start.3) | copy-done | bytes 1048600
  2.1 0.7 collective-permute-start.7
  2.9 3.8 %collective-permute-start.1 = (bf16[128,256]{1,0:T(8,128)(2,1)S(1)}, bf16[128,256]{1,0:T(8,128)(2,1)S(1)}, u32[]{:S(2)}, u32[]{:S(2)}) collective-permute-start(bf16[128,256]{1,0:T(8,128)(2,1)S(1)} %get-tuple-element.25.refs_9_), channel_id=1, source_target_pairs={{0,4},{1,5},{2,3},{3,2},{4,1},{5,9},{6,14},{7,23},{8,0},{9,8},{10,... | collective-permute-start | bytes 196616 | tf_op jit(solution)/shard_map/ppermute | solution.py:116
  6.7 3.3 %collective-permute-done.refs_0_ = bf16[128,128]{1,0:T(8,128)(2,1)S(1)} collective-permute-done((bf16[128,128]{1,0:T(8,128)(2,1)S(1)}, bf16[128,128]{1,0:T(8,128)(2,1)S(1)}, u32[]{:S(2)}, u32[]{:S(2)}) %collective-permute-start) | collective-permute-done | bytes 32800 | tf_op jit(solution)/shard_map/ppermute | solution.py:116
  10.0 0.5 collective-permute-start.4
  10.5 1.3 %collective-permute-done.3.refs_3_ = bf16[128,512]{1,0:T(8,128)(2,1)S(1)} collective-permute-done((bf16[128,512]{1,0:T(8,128)(2,1)S(1)}, bf16[128,512]{1,0:T(8,128)(2,1)S(1)}, u32[]{:S(2)}, u32[]{:S(2)}) %collective-permute-start.3) | collective-permute-done | bytes 131104 | tf_op jit(solution)/shard_map/ppermute | solution.py:116
  11.9 1.2 %copy-done.1 = f32[2,1,1024,128]{3,2,1,0:T(8,128)S(1)} copy-done((f32[2,1,1024,128]{3,2,1,0:T(8,128)S(1)}, f32[2,1,1024,128]{3,2,1,0:T(8,128)}, u32[]{:S(2)}) %copy-start.1) | copy-done | bytes 1048600
  13.4 4.5 %collective-permute-start.11 = (bf16[256,128]{1,0:T(8,128)(2,1)S(1)}, bf16[256,128]{1,0:T(8,128)(2,1)S(1)}, u32[]{:S(2)}, u32[]{:S(2)}) collective-permute-start(bf16[256,128]{1,0:T(8,128)(2,1)S(1)} %first_kernel.1), channel_id=1, source_target_pairs={{0,2},{1,4},{2,8},{3,12},{4,0},{5,3},{6,7},{7,6},{8,9},{9,1},{10,1... | collective-permute-start | bytes 196616 | tf_op jit(solution)/shard_map/ppermute | solution.py:116
  18.0 0.5 collective-permute-start.9
  18.5 0.4 collective-permute-done.11.g3
  19.2 5.5 %collective-permute-done.9.g1 = bf16[256,128]{1,0:T(8,128)(2,1)S(1)} collective-permute-done((bf16[256,128]{1,0:T(8,128)(2,1)S(1)}, bf16[256,128]{1,0:T(8,128)(2,1)S(1)}, u32[]{:S(2)}, u32[]{:S(2)}) %collective-permute-start.9) | collective-permute-done | bytes 65568 | tf_op jit(solution)/shard_map/ppermute | solution.py:116
  24.7 0.5 collective-permute-start.13
  25.3 0.9 %collective-permute-done.12.p_in = bf16[1024,128]{1,0:T(8,128)(2,1)S(1)} collective-permute-done((bf16[1024,128]{1,0:T(8,128)(2,1)S(1)}, bf16[1024,128]{1,0:T(8,128)(2,1)S(1)}, u32[]{:S(2)}, u32[]{:S(2)}) %collective-permute-start.12) | collective-permute-done | bytes 262176 | tf_op jit(solution)/shard_map/ppermute | solution.py:116
  27.3 1.0 %collective-permute-done.14.p_in = bf16[1024,128]{1,0:T(8,128)(2,1)S(1)} collective-permute-done((bf16[1024,128]{1,0:T(8,128)(2,1)S(1)}, bf16[1024,128]{1,0:T(8,128)(2,1)S(1)}, u32[]{:S(2)}, u32[]{:S(2)}) %collective-permute-start.14) | collective-permute-done | bytes 262176 | tf_op jit(solution)/shard_map/ppermute | solution.py:116
  29.4 0.9 %collective-permute-done.16.sum_ref = bf16[1024,128]{1,0:T(8,128)(2,1)S(1)} collective-permute-done((bf16[1024,128]{1,0:T(8,128)(2,1)S(1)}, bf16[1024,128]{1,0:T(8,128)(2,1)S(1)}, u32[]{:S(2)}, u32[]{:S(2)}) %collective-permute-start.16) | collective-permute-done | bytes 262176 | tf_op jit(solution)/shard_map/ppermute | solution.py:116
  30.5 0.5 collective-permute-done.17.got_ref
  31.3 0.6 collective-permute-done.19.p_in
  34.3 20.0 %collective-permute-start.26 = (bf16[1040,128]{1,0:T(8,128)(2,1)S(1)}, bf16[1040,128]{1,0:T(8,128)(2,1)S(1)}, u32[]{:S(2)}, u32[]{:S(2)}) collective-permute-start(bf16[1040,128]{1,0:T(8,128)(2,1)S(1)} %get-tuple-element.43.refs_0_), channel_id=1, source_target_pairs={{0,2},{1,3},{2,0},{3,1},{4,6},{5,7},{6,4},{7,5},{8,10},{9,11},{10,... | collective-permute-start | bytes 798728 | tf_op jit(solution)/shard_map/ppermute | solution.py:116
  54.3 2.0 %collective-permute-start.25 = (bf16[1040,128]{1,0:T(8,128)(2,1)S(1)}, bf16[1040,128]{1,0:T(8,128)(2,1)S(1)}, u32[]{:S(2)}, u32[]{:S(2)}) collective-permute-start(bf16[1040,128]{1,0:T(8,128)(2,1)S(1)} %get-tuple-element.43.refs_0_), channel_id=1, source_target_pairs={{0,1},{1,0},{2,3},{3,2},{4,5},{5,4},{6,7},{7,6},{8,9},{9,8},{10,11... | collective-permute-start | bytes 798728 | tf_op jit(solution)/shard_map/ppermute | solution.py:116
  56.3 2.9 %collective-permute-done.26.refs_2_ = bf16[1040,128]{1,0:T(8,128)(2,1)S(1)} collective-permute-done((bf16[1040,128]{1,0:T(8,128)(2,1)S(1)}, bf16[1040,128]{1,0:T(8,128)(2,1)S(1)}, u32[]{:S(2)}, u32[]{:S(2)}) %collective-permute-start.26) | collective-permute-done | bytes 266272 | tf_op jit(solution)/shard_map/ppermute | solution.py:116
  59.2 2.4 %collective-permute-start.27 = (bf16[1040,128]{1,0:T(8,128)(2,1)S(1)}, bf16[1040,128]{1,0:T(8,128)(2,1)S(1)}, u32[]{:S(2)}, u32[]{:S(2)}) collective-permute-start(bf16[1040,128]{1,0:T(8,128)(2,1)S(1)} %collective-permute-done.26.refs_2_), channel_id=1, source_target_pairs={{0,1},{1,0},{2,3},{3,2},{4,5},{5,4},{6,7},{7,6},{8,9},{9,8},{10,11... | collective-permute-start | bytes 798728 | tf_op jit(solution)/shard_map/ppermute | solution.py:116
  61.6 7.7 %collective-permute-start.24 = (bf16[1024,128]{1,0:T(8,128)(2,1)S(1)}, bf16[1024,128]{1,0:T(8,128)(2,1)S(1)}, u32[]{:S(2)}, u32[]{:S(2)}) collective-permute-start(bf16[1024,128]{1,0:T(8,128)(2,1)S(1)} %get-tuple-element.42.q_ref), channel_id=1, source_target_pairs={{0,1},{1,0},{2,26},{3,27},{4,5},{5,4},{6,14},{7,30},{8,9},{9,8},{1... | collective-permute-start | bytes 786440 | tf_op jit(solution)/shard_map/ppermute | solution.py:116
  69.3 9.2 %collective-permute-done.24.rest_ref = bf16[1024,128]{1,0:T(8,128)(2,1)S(1)} collective-permute-done((bf16[1024,128]{1,0:T(8,128)(2,1)S(1)}, bf16[1024,128]{1,0:T(8,128)(2,1)S(1)}, u32[]{:S(2)}, u32[]{:S(2)}) %collective-permute-start.24) | collective-permute-done | bytes 262176 | tf_op jit(solution)/shard_map/ppermute | solution.py:116
  78.5 1.4 %final_kernel.1 = (f32[1024,128]{1,0:T(8,128)}, f32[2,1024,128]{2,1,0:T(8,128)}) custom-call(f32[2,1024,128]{2,1,0:T(8,128)S(1)} %bitcast.14, bf16[1024,128]{1,0:T(8,128)(2,1)S(1)} %get-tuple-element.42.q_ref, bf16[1024,128]{1,0:T(8,128)(2,1)S(1)} %collective-permute-done.24.rest_ref, bf16[1040,128]{1,0:T(8,128)(2,1)S(1)} %get-tuple-element.43.refs_0_, ...), custom_call_target="tpu_custom_call" | custom-call | tf_op jit(solution)/shard_map/final_kernel/pallas_call | solution.py:139
  (51 shorter events, 4.6 us)
Async XLA Ops:
  2.1 9.8 %collective-permute-start.7 = (bf16[128,1024]{1,0:T(8,128)(2,1)S(1)}, bf16[128,1024]{1,0:T(8,128)(2,1)S(1)}, u32[]{:S(2)}, u32[]{:S(2)}) collective-permute-start(bf16[128,1024]{1,0:T(8,128)(2,1)S(1)} %get-tuple-element.31.refs_15_), channel_id=1, source_target_pairs={{0,1},{1,0},{2,10},{3,2},{4,5},{5,4},{6,7},{7,6},{8,16},{9,8},{10,... | collective-permute-start | bytes 786440 | tf_op jit(solution)/shard_map/ppermute | solution.py:116
  2.8 7.7 %collective-permute-start.2 = (bf16[128,384]{1,0:T(8,128)(2,1)S(1)}, bf16[128,384]{1,0:T(8,128)(2,1)S(1)}, u32[]{:S(2)}, u32[]{:S(2)}) collective-permute-start(bf16[128,384]{1,0:T(8,128)(2,1)S(1)} %get-tuple-element.26.refs_10_), channel_id=1, source_target_pairs={{0,1},{1,0},{2,3},{3,11},{4,5},{5,4},{6,7},{7,6},{8,2},{9,8},{10,1... | collective-permute-start | bytes 294920 | tf_op jit(solution)/shard_map/ppermute | solution.py:116
  2.9 7.1 %collective-permute-start.1 = (bf16[128,256]{1,0:T(8,128)(2,1)S(1)}, bf16[128,256]{1,0:T(8,128)(2,1)S(1)}, u32[]{:S(2)}, u32[]{:S(2)}) collective-permute-start(bf16[128,256]{1,0:T(8,128)(2,1)S(1)} %get-tuple-element.25.refs_9_), channel_id=1, source_target_pairs={{0,4},{1,5},{2,3},{3,2},{4,1},{5,9},{6,14},{7,23},{8,0},{9,8},{10,... | collective-permute-start | bytes 196616 | tf_op jit(solution)/shard_map/ppermute | solution.py:116
  6.7 3.3 %collective-permute-start = (bf16[128,128]{1,0:T(8,128)(2,1)S(1)}, bf16[128,128]{1,0:T(8,128)(2,1)S(1)}, u32[]{:S(2)}, u32[]{:S(2)}) collective-permute-start(bf16[128,128]{1,0:T(8,128)(2,1)S(1)} %get-tuple-element.24.own_ref.refs_8_), channel_id=1, source_target_pairs={{0,1},{1,9},{2,14},{3,23},{4,5},{5,4},{6,2},{7,6},{8,0},{9,8},{10,... | collective-permute-start | bytes 98312 | tf_op jit(solution)/shard_map/ppermute | solution.py:116
  6.7 5.2 %collective-permute-start.6 = (bf16[128,896]{1,0:T(8,128)(2,1)S(1)}, bf16[128,896]{1,0:T(8,128)(2,1)S(1)}, u32[]{:S(2)}, u32[]{:S(2)}) collective-permute-start(bf16[128,896]{1,0:T(8,128)(2,1)S(1)} %get-tuple-element.30.refs_14_), channel_id=1, source_target_pairs={{0,1},{1,0},{2,3},{3,11},{4,5},{5,4},{6,7},{7,6},{8,16},{9,8},{10,... | collective-permute-start | bytes 688136 | tf_op jit(solution)/shard_map/ppermute | solution.py:116
  10.0 1.9 %collective-permute-start.5 = (bf16[128,768]{1,0:T(8,128)(2,1)S(1)}, bf16[128,768]{1,0:T(8,128)(2,1)S(1)}, u32[]{:S(2)}, u32[]{:S(2)}) collective-permute-start(bf16[128,768]{1,0:T(8,128)(2,1)S(1)} %get-tuple-element.29.refs_13_), channel_id=1, source_target_pairs={{0,8},{1,0},{2,3},{3,2},{4,5},{5,4},{6,7},{7,6},{8,16},{9,17},{10,... | collective-permute-start | bytes 589832 | tf_op jit(solution)/shard_map/ppermute | solution.py:116
  10.0 1.9 %collective-permute-start.4 = (bf16[128,640]{1,0:T(8,128)(2,1)S(1)}, bf16[128,640]{1,0:T(8,128)(2,1)S(1)}, u32[]{:S(2)}, u32[]{:S(2)}) collective-permute-start(bf16[128,640]{1,0:T(8,128)(2,1)S(1)} %get-tuple-element.28.refs_12_), channel_id=1, source_target_pairs={{0,1},{1,17},{2,3},{3,2},{4,5},{5,4},{6,7},{7,6},{8,16},{9,8},{10,... | collective-permute-start | bytes 491528 | tf_op jit(solution)/shard_map/ppermute | solution.py:116
  13.1 5.4 %collective-permute-start.10 = (bf16[256,128]{1,0:T(8,128)(2,1)S(1)}, bf16[256,128]{1,0:T(8,128)(2,1)S(1)}, u32[]{:S(2)}, u32[]{:S(2)}) collective-permute-start(bf16[256,128]{1,0:T(8,128)(2,1)S(1)} %first_kernel.1), channel_id=1, source_target_pairs={{0,12},{1,3},{2,4},{3,8},{4,0},{5,7},{6,2},{7,6},{8,9},{9,1},{10,1... | collective-permute-start | bytes 196616 | tf_op jit(solution)/shard_map/ppermute | solution.py:116
  13.4 5.4 %collective-permute-start.11 = (bf16[256,128]{1,0:T(8,128)(2,1)S(1)}, bf16[256,128]{1,0:T(8,128)(2,1)S(1)}, u32[]{:S(2)}, u32[]{:S(2)}) collective-permute-start(bf16[256,128]{1,0:T(8,128)(2,1)S(1)} %first_kernel.1), channel_id=1, source_target_pairs={{0,2},{1,4},{2,8},{3,12},{4,0},{5,3},{6,7},{7,6},{8,9},{9,1},{10,1... | collective-permute-start | bytes 196616 | tf_op jit(solution)/shard_map/ppermute | solution.py:116
  18.0 6.8 %collective-permute-start.9 = (bf16[256,128]{1,0:T(8,128)(2,1)S(1)}, bf16[256,128]{1,0:T(8,128)(2,1)S(1)}, u32[]{:S(2)}, u32[]{:S(2)}) collective-permute-start(bf16[256,128]{1,0:T(8,128)(2,1)S(1)} %first_kernel.1), channel_id=1, source_target_pairs={{0,8},{1,12},{2,3},{3,4},{4,0},{5,7},{6,2},{7,6},{8,9},{9,1},{10,1... | collective-permute-start | bytes 196616 | tf_op jit(solution)/shard_map/ppermute | solution.py:116
  24.7 1.9 %collective-permute-start.13 = (bf16[1024,128]{1,0:T(8,128)(2,1)S(1)}, bf16[1024,128]{1,0:T(8,128)(2,1)S(1)}, u32[]{:S(2)}, u32[]{:S(2)}) collective-permute-start(bf16[1024,128]{1,0:T(8,128)(2,1)S(1)} %get-tuple-element.33.s_prev), channel_id=1, source_target_pairs={{0,1},{1,0},{2,3},{3,2},{4,5},{5,4},{6,7},{7,6},{8,9},{9,8},{10,11... | collective-permute-start | bytes 786440 | tf_op jit(solution)/shard_map/ppermute | solution.py:116
  26.7 1.6 %collective-permute-start.14 = (bf16[1024,128]{1,0:T(8,128)(2,1)S(1)}, bf16[1024,128]{1,0:T(8,128)(2,1)S(1)}, u32[]{:S(2)}, u32[]{:S(2)}) collective-permute-start(bf16[1024,128]{1,0:T(8,128)(2,1)S(1)} %get-tuple-element.35), channel_id=1, source_target_pairs={{0,1},{1,0},{2,3},{3,2},{4,5},{5,4},{6,7},{7,6},{8,9},{9,14},{10,8... | collective-permute-start | bytes 786440 | tf_op jit(solution)/shard_map/ppermute | solution.py:116
  26.9 1.8 %collective-permute-start.15 = (bf16[1024,128]{1,0:T(8,128)(2,1)S(1)}, bf16[1024,128]{1,0:T(8,128)(2,1)S(1)}, u32[]{:S(2)}, u32[]{:S(2)}) collective-permute-start(bf16[1024,128]{1,0:T(8,128)(2,1)S(1)} %get-tuple-element.36.q_prev), channel_id=1, source_target_pairs={{0,1},{1,0},{2,3},{3,2},{4,5},{5,4},{6,7},{7,6},{8,9},{9,13},{10,1... | collective-permute-start | bytes 786440 | tf_op jit(solution)/shard_map/ppermute | solution.py:116
  28.7 1.6 %collective-permute-start.16 = (bf16[1024,128]{1,0:T(8,128)(2,1)S(1)}, bf16[1024,128]{1,0:T(8,128)(2,1)S(1)}, u32[]{:S(2)}, u32[]{:S(2)}) collective-permute-start(bf16[1024,128]{1,0:T(8,128)(2,1)S(1)} %get-tuple-element.38.s_prev), channel_id=1, source_target_pairs={{0,1},{1,0},{2,3},{3,2},{4,5},{5,4},{6,7},{7,6},{8,9},{9,8},{10,11... | collective-permute-start | bytes 786440 | tf_op jit(solution)/shard_map/ppermute | solution.py:116
  28.9 2.4 %collective-permute-start.20 = (bf16[1024,128]{1,0:T(8,128)(2,1)S(1)}, bf16[1024,128]{1,0:T(8,128)(2,1)S(1)}, u32[]{:S(2)}, u32[]{:S(2)}) collective-permute-start(bf16[1024,128]{1,0:T(8,128)(2,1)S(1)} %get-tuple-element.40.q_ref), channel_id=1, source_target_pairs={{0,1},{1,0},{2,3},{3,2},{4,5},{5,4},{6,7},{7,6},{8,9},{9,8},{10,11... | collective-permute-start | bytes 786440 | tf_op jit(solution)/shard_map/ppermute | solution.py:116
  29.3 1.8 %collective-permute-start.17 = (bf16[1024,128]{1,0:T(8,128)(2,1)S(1)}, bf16[1024,128]{1,0:T(8,128)(2,1)S(1)}, u32[]{:S(2)}, u32[]{:S(2)}) collective-permute-start(bf16[1024,128]{1,0:T(8,128)(2,1)S(1)} %get-tuple-element.40.q_ref), channel_id=1, source_target_pairs={{0,1},{1,5},{2,3},{3,2},{4,0},{5,4},{6,7},{7,6},{8,16},{9,17},{10,... | collective-permute-start | bytes 786440 | tf_op jit(solution)/shard_map/ppermute | solution.py:116
  31.1 2.8 %collective-permute-start.18 = (bf16[1024,128]{1,0:T(8,128)(2,1)S(1)}, bf16[1024,128]{1,0:T(8,128)(2,1)S(1)}, u32[]{:S(2)}, u32[]{:S(2)}) collective-permute-start(bf16[1024,128]{1,0:T(8,128)(2,1)S(1)} %relay_kernel.1.q0), channel_id=1, source_target_pairs={{0,8},{1,0},{2,3},{3,2},{4,12},{5,4},{6,7},{7,6},{8,9},{9,1},{10,1... | collective-permute-start | bytes 786440 | tf_op jit(solution)/shard_map/ppermute | solution.py:116
  31.9 2.0 %collective-permute-start.21 = (bf16[1024,128]{1,0:T(8,128)(2,1)S(1)}, bf16[1024,128]{1,0:T(8,128)(2,1)S(1)}, u32[]{:S(2)}, u32[]{:S(2)}) collective-permute-start(bf16[1024,128]{1,0:T(8,128)(2,1)S(1)} %step4_kernel.1.hub), channel_id=1, source_target_pairs={{0,1},{1,0},{2,3},{3,2},{4,5},{5,4},{6,7},{7,6},{8,9},{9,8},{10,11... | collective-permute-start | bytes 786440 | tf_op jit(solution)/shard_map/ppermute | solution.py:116
  32.1 1.8 %collective-permute-start.22 = (bf16[1024,128]{1,0:T(8,128)(2,1)S(1)}, bf16[1024,128]{1,0:T(8,128)(2,1)S(1)}, u32[]{:S(2)}, u32[]{:S(2)}) collective-permute-start(bf16[1024,128]{1,0:T(8,128)(2,1)S(1)} %step4_kernel.1.hub), channel_id=1, source_target_pairs={{0,1},{1,0},{2,3},{3,2},{4,5},{5,4},{6,7},{7,6},{8,9},{9,8},{10,11... | collective-permute-start | bytes 786440 | tf_op jit(solution)/shard_map/ppermute | solution.py:116
  32.4 1.8 %collective-permute-start.23 = (bf16[1024,128]{1,0:T(8,128)(2,1)S(1)}, bf16[1024,128]{1,0:T(8,128)(2,1)S(1)}, u32[]{:S(2)}, u32[]{:S(2)}) collective-permute-start(bf16[1024,128]{1,0:T(8,128)(2,1)S(1)} %step4_kernel.1.hub), channel_id=1, source_target_pairs={{0,1},{1,0},{2,3},{3,2},{4,5},{5,4},{6,7},{7,6},{8,9},{9,8},{10,11... | collective-permute-start | bytes 786440 | tf_op jit(solution)/shard_map/ppermute | solution.py:116
  34.3 24.9 %collective-permute-start.26 = (bf16[1040,128]{1,0:T(8,128)(2,1)S(1)}, bf16[1040,128]{1,0:T(8,128)(2,1)S(1)}, u32[]{:S(2)}, u32[]{:S(2)}) collective-permute-start(bf16[1040,128]{1,0:T(8,128)(2,1)S(1)} %get-tuple-element.43.refs_0_), channel_id=1, source_target_pairs={{0,2},{1,3},{2,0},{3,1},{4,6},{5,7},{6,4},{7,5},{8,10},{9,11},{10,... | collective-permute-start | bytes 798728 | tf_op jit(solution)/shard_map/ppermute | solution.py:116
  54.3 24.2 %collective-permute-start.25 = (bf16[1040,128]{1,0:T(8,128)(2,1)S(1)}, bf16[1040,128]{1,0:T(8,128)(2,1)S(1)}, u32[]{:S(2)}, u32[]{:S(2)}) collective-permute-start(bf16[1040,128]{1,0:T(8,128)(2,1)S(1)} %get-tuple-element.43.refs_0_), channel_id=1, source_target_pairs={{0,1},{1,0},{2,3},{3,2},{4,5},{5,4},{6,7},{7,6},{8,9},{9,8},{10,11... | collective-permute-start | bytes 798728 | tf_op jit(solution)/shard_map/ppermute | solution.py:116
  59.2 19.3 %collective-permute-start.27 = (bf16[1040,128]{1,0:T(8,128)(2,1)S(1)}, bf16[1040,128]{1,0:T(8,128)(2,1)S(1)}, u32[]{:S(2)}, u32[]{:S(2)}) collective-permute-start(bf16[1040,128]{1,0:T(8,128)(2,1)S(1)} %collective-permute-done.26.refs_2_), channel_id=1, source_target_pairs={{0,1},{1,0},{2,3},{3,2},{4,5},{5,4},{6,7},{7,6},{8,9},{9,8},{10,11... | collective-permute-start | bytes 798728 | tf_op jit(solution)/shard_map/ppermute | solution.py:116
  61.6 16.9 %collective-permute-start.24 = (bf16[1024,128]{1,0:T(8,128)(2,1)S(1)}, bf16[1024,128]{1,0:T(8,128)(2,1)S(1)}, u32[]{:S(2)}, u32[]{:S(2)}) collective-permute-start(bf16[1024,128]{1,0:T(8,128)(2,1)S(1)} %get-tuple-element.42.q_ref), channel_id=1, source_target_pairs={{0,1},{1,0},{2,26},{3,27},{4,5},{5,4},{6,14},{7,30},{8,9},{9,8},{1... | collective-permute-start | bytes 786440 | tf_op jit(solution)/shard_map/ppermute | solution.py:116
  (8 other events, 44.1 us)

commit v6 on v5

--- a/solution.py
+++ b/solution.py
@@ -66,7 +66,7 @@
 MAKER = (None, (2, 1), (3, 2), (5, 3))
 FIRST = (1, 0)
 BESIDE = (3, 1)
-NEAR = (5, 2)
+PARTNER = (None, (2, 0), (3, 3), (5, 2))
 
 
 def hops(a, b):
@@ -112,8 +112,11 @@
 
 
 def send(value, pairs):
-    moves = [(a * NC + b, c * NC + d) for (a, b), (c, d) in complete(pairs)]
-    return lax.ppermute(value, ("row", "col"), moves)
+    return lax.ppermute(value, ("row", "col"), [(a * NC + b, c * NC + d) for (a, b), (c, d) in complete(pairs)])
+
+
+def send_only(value, pairs):
+    return lax.ppermute(value, ("row", "col"), [(a * NC + b, c * NC + d) for (a, b), (c, d) in pairs])
 
 
 def dot(a, b):
@@ -147,22 +150,27 @@
     )(*ins)
 
 
+def pair_width(m, part):
+    return 2 * (m + 1) * part
+
+
 def cut_kernel(diag_ref, *refs):
-    cuts, sem = refs[:NR], refs[NR]
+    cuts, sem = refs[:-1], refs[-1]
     row, col = lax.axis_index("row"), lax.axis_index("col")
     part = diag_ref.shape[1]
-    for r in range(NR):
-
-        @pl.when(row == r)
+    k = jnp.where(lax.rem(row, 2) == 1, col, col + 1 - 2 * lax.rem(col, 2))
+    for m in range(NR // 2):
+
+        @pl.when(row // 2 == m)
         def _():
-            copy = pltpu.make_async_copy(diag_ref.at[col, :, pl.ds(0, (r + 1) * part)], cuts[r], sem)
+            copy = pltpu.make_async_copy(diag_ref.at[k, :, pl.ds(0, pair_width(m, part))], cuts[m], sem)
             copy.start()
             copy.wait()
 
 
-def first_kernel(rhs_ref, own_ref, *refs):
-    parts, out_ref = refs[:NR], refs[NR]
-    rhs_v, lo_v, hi_v, rhs_sem, lo_sem, hi_sem = refs[NR + 1 :]
+def first_kernel(rhs_ref, diag_ref, *refs):
+    parts, out_ref = refs[: NR // 2], refs[NR // 2]
+    rhs_v, lo_v, hi_v, rhs_sem, lo_sem, hi_sem = refs[NR // 2 + 1 :]
     n = out_ref.shape[0] // 2
     col = lax.axis_index("col")
 
@@ -172,11 +180,11 @@
         rhs_copy.start()
 
         def piece(c):
-            lo = own_ref if c == 0 else parts[c]
-            wide = (4 + c + 1) * n
+            lo_wide, hi_wide = pair_width(c // 2, n), pair_width(2 + c // 2, n)
+            lo = parts[c // 2] if c else diag_ref.at[0, :, pl.ds(0, lo_wide)]
             return (
-                pltpu.make_async_copy(lo, lo_v.at[:, pl.ds(0, (c + 1) * n)], lo_sem),
-                pltpu.make_async_copy(parts[4 + c], hi_v.at[:, pl.ds(0, wide)], hi_sem),
+                pltpu.make_async_copy(lo, lo_v.at[:, pl.ds(0, lo_wide)], lo_sem),
+                pltpu.make_async_copy(parts[2 + c // 2], hi_v.at[:, pl.ds(0, hi_wide)], hi_sem),
             )
 
         for c in range(NC):
@@ -194,39 +202,63 @@
             def _():
                 for copy in piece(c):
                     copy.wait()
-                wide = (4 + c + 1) * n
-                out_ref[:n] = low(dot(hi_v[:, :wide], p[:wide]))
-                out_ref[n:] = low(dot(lo_v[:, : (c + 1) * n], p[: (c + 1) * n]))
-
-
-def whole_kernel(*refs):
-    parts, own, out_ref, sem = refs[:NR], refs[NR : 2 * NR], refs[2 * NR], refs[2 * NR + 1]
+                lo_wide, hi_wide = pair_width(c // 2, n), pair_width(2 + c // 2, n)
+                out_ref[:n] = low(dot(hi_v[:, :hi_wide], p[:hi_wide]))
+                out_ref[n:] = low(dot(lo_v[:, :lo_wide], p[:lo_wide]))
+
+
+def pack_kernel(*refs):
+    parts, out_ref, sem = refs[:-2], refs[-2], refs[-1]
+
+    @pl.when(any_of(PARTNER[1:]))
+    def _():
+        copies, left = [], 0
+        for m, source in enumerate(parts):
+            wide = source.shape[1]
+            copies.append(pltpu.make_async_copy(source, out_ref.at[:, pl.ds(left, wide)], sem.at[m]))
+            left += wide
+        for copy in copies:
+            copy.start()
+        for copy in copies:
+            copy.wait()
+
+
+def whole_kernel(diag_ref, even_ref, *refs):
+    odd, out_ref, sem = refs[:-2], refs[-2], refs[-1]
     size = out_ref.shape[0]
     part = size // NR
-    row = lax.axis_index("row")
+    row, col = lax.axis_index("row"), lax.axis_index("col")
 
     @pl.when(any_of(MAKER[1:]))
     def _():
         def copy(i, source):
-            return pltpu.make_async_copy(
-                source, out_ref.at[pl.ds(i * part, part), pl.ds(0, (i + 1) * part)], sem.at[i]
-            )
-
+            wide = pair_width(i // 2, part)
+            return pltpu.make_async_copy(source, out_ref.at[pl.ds(i * part, part), pl.ds(0, wide)], sem.at[i])
+
+        left = 0
         for i in range(NR):
+            wide = pair_width(i // 2, part)
+            if i % 2:
+                source = odd[i // 2]
+            else:
+                source = even_ref.at[:, pl.ds(left, wide)]
+                left += wide
 
             @pl.when(row == i)
             def _():
-                copy(i, own[i]).start()
+                copy(i, diag_ref.at[col, :, pl.ds(0, wide)]).start()
 
             @pl.when(row != i)
             def _():
-                copy(i, parts[i]).start()
-
-        for i in range(NR - 1):
-            right = (i + 1) * part
-            out_ref[pl.ds(i * part, part), pl.ds(right, size - right)] = jnp.zeros((part, size - right), out_ref.dtype)
+                copy(i, source).start()
+
+        for m in range(NR // 2 - 1):
+            right = pair_width(m, part)
+            out_ref[pl.ds(2 * m * part, 2 * part), pl.ds(right, size - right)] = jnp.zeros(
+                (2 * part, size - right), out_ref.dtype
+            )
         for i in range(NR):
-            copy(i, parts[i]).wait()
+            copy(i, odd[i // 2]).wait()
 
 
 def lower_dot(q_ref, d_ref, p_ref):
@@ -268,7 +300,7 @@
         s_ref[...] = s_prev[...]
 
 
-def step2_kernel(p_in, q_in, sum_ref, d_ref, l_ref, q_prev, s_prev, q_ref, s_ref):
+def step2_kernel(p_in, q_in, sum_ref, rhs_ref, d_ref, l_ref, q_prev, s_prev, a_ref, q_ref, s_ref):
     active, beside = at(MAKER[2]), at(BESIDE)
 
     @pl.when(active)
@@ -279,7 +311,9 @@
     @pl.when(beside)
     def _():
         q_ref[...] = q_in[...]
-        s_ref[...] = low(dot(l_ref[...], q_in[...]) + sum_ref[...].astype(jnp.float32))
+        s = dot(l_ref[...], q_in[...]) + sum_ref[...].astype(jnp.float32)
+        s_ref[...] = low(s)
+        a_ref[...] = low(rhs_ref[0] - s)
 
     @pl.when(jnp.logical_not(active | beside))
     def _():
@@ -287,33 +321,16 @@
         s_ref[...] = s_prev[...]
 
 
-def step3_kernel(sum_ref, rhs_ref, s_prev, p_ref, s_ref):
-    active = at(MAKER[2])
-
-    @pl.when(active)
-    def _():
-        s = s_prev[...].astype(jnp.float32) + sum_ref[...].astype(jnp.float32)
-        s_ref[...] = low(s)
-        p_ref[...] = low(rhs_ref[0] - s)
-
-    @pl.when(jnp.logical_not(active))
-    def _():
-        s_ref[...] = s_prev[...]
-
-
-def step4_kernel(p_in, near_ref, d_ref, q_ref):
+def step3_kernel(a_ref, sum_ref, d_ref, q_ref, p_v):
     @pl.when(at(MAKER[3]))
     def _():
-        lower_dot(q_ref, d_ref, p_in)
-
-    @pl.when(at(NEAR))
-    def _():
-        q_ref[...] = near_ref[...]
+        p_v[...] = low(a_ref[...].astype(jnp.float32) - sum_ref[...].astype(jnp.float32))
+        lower_dot(q_ref, d_ref, p_v)
 
 
 def relay_kernel(q_ref, got_ref, out_ref):
     row = lax.axis_index("row")
-    taken = (row == 4) | (row == 5) | at((0, 0))
+    taken = (row == 4) | (row == 5) | at((0, 0)) | at((2, 2))
 
     @pl.when(taken)
     def _():
@@ -324,22 +341,25 @@
         out_ref[...] = q_ref[...]
 
 
-def update_kernel(rows_ref, counts_ref, s_ref, l_ref, q0, q1, hub, h4, h7, h6, q_ref, out_ref):
+def update_kernel(rows_ref, counts_ref, s_ref, l_ref, q0, r2, r3, r4, hub, h4, h7, h6, h3, h1, q_ref, out_ref):
     size = l_ref.shape[0]
     row, col = lax.axis_index("row"), lax.axis_index("col")
     below = row >= NC
-    right = col >= 2
-    late = jnp.logical_not(right) & ((row >= 6) | ((row < 2) & (col == 1)))
 
     def take(flag, source):
         @pl.when(flag)
         def _():
             q_ref[...] = source[...]
 
-    take(late, q1)
-    take(jnp.logical_not(late) & jnp.logical_not(right & below), q0)
-    for r, source in ((5, hub), (4, h4), (7, h7), (6, h6)):
-        take(right & (row == r), source)
+    from_r2 = ((col < 2) & ((row >= 6) | ((row < 2) & (col == 1)))) | at((4, 2)) | at((5, 2))
+    from_r3 = (col == 2) & (row >= 6)
+    from_r4 = (col == 2) & (row < 2)
+    take(from_r2, r2)
+    take(from_r3, r3)
+    take(from_r4, r4)
+    take((col < 3) & jnp.logical_not(from_r2 | from_r3 | from_r4), q0)
+    for r, source in ((5, hub), (4, h4), (7, h7), (6, h6), (3, h3), (1, h1)):
+        take((col == 3) & (row == r), source)
 
     @pl.when(below)
     def _():
@@ -351,7 +371,8 @@
 
     listed = rows_ref[0, 0, 0, 0]
     there = below & (counts_ref[0, 0, 0] > 0)
-    first = (there & (listed == 0)) | (jnp.logical_not(below) & (row >= 1) & (col == row - 1))
+    done = at(FIRST) | at(MAKER[1]) | at(BESIDE) | at(MAKER[2])
+    first = (there & (listed == 0)) | done
     second = there & (listed == 1)
     ids = lax.broadcasted_iota(jnp.int32, (TAIL, out_ref.shape[1]), 0)
     flag = ((ids == 0) & first) | ((ids == 1) & second)
@@ -361,8 +382,7 @@
 def final_kernel(rhs_ref, q_ref, rest_ref, *refs):
     sums, (solved_ref, out_ref) = refs[:NC], refs[NC:]
     size = out_ref.shape[1]
-    row, col = lax.axis_index("row"), lax.axis_index("col")
-    came = (row < NC) & (col >= 2) & jnp.logical_not(at(MAKER[2]))
+    came = at((2, 3)) | at((0, 3))
 
     @pl.when(came)
     def _():
@@ -389,28 +409,30 @@
     vec = jax.ShapeDtypeStruct((size, width), bf16)
     dma = pltpu.SemaphoreType.DMA
 
+    wides = [pair_width(m, part) for m in range(NR // 2)]
     cuts = call(
-        cut_kernel,
-        [jax.ShapeDtypeStruct((part, (r + 1) * part), bf16) for r in range(NR)],
-        [diag_inv],
-        [HBM],
-        [ANY] * NR,
-        [dma],
+        cut_kernel, [jax.ShapeDtypeStruct((part, w), bf16) for w in wides], [diag_inv], [HBM], [ANY] * len(wides), [dma]
     )
     parts = []
-    for r in range(NR):
-        pairs = [((r, 0), (0, r % 4))] if r else []
-        pairs += [((r, c), MAKER[c]) for c in range(1, NC) if MAKER[c][0] != r]
-        parts.append(send(cuts[r], pairs))
+    for m, cut in enumerate(cuts):
+        even, odd = 2 * m, 2 * m + 1
+        pairs = [((odd, 0), (0, odd % 4))] + ([((even, 1), (0, even % 4))] if even else [])
+        for k in range(1, NC):
+            maker, partner = MAKER[k], PARTNER[k]
+            if maker[0] != odd:
+                pairs.append(((odd, maker[1]), maker))
+            if partner[0] != even:
+                pairs.append(((even, partner[1]), partner))
+        parts.append(send(cut, pairs))
     q = call(
         first_kernel,
         jax.ShapeDtypeStruct((2 * part, width), bf16),
-        [rhs, cuts[0], *parts],
-        [HBM] + [ANY] * (1 + NR),
+        [rhs, diag_inv, *parts],
+        [HBM, HBM] + [ANY] * len(wides),
         VMEM,
         [
             pltpu.VMEM((size, width), jnp.float32),
-            pltpu.VMEM((part, 4 * part), bf16),
+            pltpu.VMEM((part, size // 2), bf16),
             pltpu.VMEM((part, size), bf16),
             dma,
             dma,
@@ -419,11 +441,20 @@
     )
     takers = (FIRST, (2, 0), (3, 0))
     got = [send(q, [((0, c), takers[(c + j) % 4]) for c in range(4) if (c + j) % 4 < 3]) for j in range(4)]
+    even = call(
+        pack_kernel,
+        jax.ShapeDtypeStruct((part, sum(wides)), bf16),
+        parts,
+        [ANY] * len(wides),
+        VMEM,
+        [pltpu.SemaphoreType.DMA((len(wides),))],
+    )
+    even = send(even, [(PARTNER[k], MAKER[k]) for k in range(1, NC)])
     diag = call(
         whole_kernel,
         jax.ShapeDtypeStruct((size, size), bf16),
-        [*parts, *cuts],
-        [ANY] * (2 * NR),
+        [diag_inv, even, *parts],
+        [HBM] + [ANY] * (1 + len(wides)),
         VMEM,
         [pltpu.SemaphoreType.DMA((NR,))],
     )
@@ -434,40 +465,39 @@
     p, q, s = call(step1_kernel, [vec] * 3, [p_in, sums, rhs, diag, block, q, s], [VMEM] * 7, [VMEM] * 3)
     p_in = send(p, [(MAKER[1], MAKER[2])])
     q_in = send(q, [(MAKER[1], BESIDE)])
-    q, s = call(step2_kernel, [vec] * 2, [p_in, q_in, sums, diag, block, q, s], [VMEM] * 7, [VMEM] * 2)
-    sums = send(s, [(BESIDE, MAKER[2])])
-    near = send(q, [(MAKER[2], NEAR)])
-    p, s = call(step3_kernel, [vec] * 2, [sums, rhs, s], [VMEM] * 3, [VMEM] * 2)
-    p_in = send(p, [(MAKER[2], MAKER[3])])
-
-    got = send(
-        q, [((2, 0), (4, 0)), ((3, 0), (5, 0)), ((1, 0), (0, 0)), ((2, 1), (4, 1)), ((3, 1), (5, 1))]
-    )
-    q = call(relay_kernel, vec, [q, got], [VMEM] * 2, VMEM)
-    got = send(
-        q,
-        [((4, c), (6, c)) for c in (0, 1)] + [((5, c), (7, c)) for c in (0, 1)] + [((2, 1), (0, 1)), ((3, 1), (1, 1))],
-    )
-
-    hub = call(step4_kernel, vec, [p_in, near, diag], [VMEM] * 3, VMEM)
-    last = [send(hub, [((5, c), (r, c)) for c in (2, 3)]) for r in (4, 7, 6)]
+    a, q, s = call(step2_kernel, [vec] * 3, [p_in, q_in, sums, rhs, diag, block, q, s], [VMEM] * 8, [VMEM] * 3)
+    sums = send(s, [(MAKER[2], MAKER[3])])
+    a = send(a, [(BESIDE, MAKER[3])])
+    hub = call(step3_kernel, vec, [a, sums, diag], [VMEM] * 3, VMEM, [pltpu.VMEM((size, width), bf16)])
+
+    h4, h7, h6 = [send(hub, [(MAKER[3], (r, 3))]) for r in (4, 7, 6)]
+    h3, h1 = [send(hub, [(MAKER[3], (r, 3))]) for r in (3, 1)]
+
+    def tree(value, *columns):
+        return send_only(value, [((a, k), (b, k)) for k, edges in enumerate(columns) for a, b in edges])
+
+    r1 = tree(q, [(2, 4), (3, 5), (1, 0)], [(2, 4), (3, 5)], [(3, 2)])
+    q = call(relay_kernel, vec, [q, r1], [VMEM] * 2, VMEM)
+    r2 = tree(q, [(4, 6), (5, 7)], [(4, 6), (5, 7), (2, 0), (3, 1)], [(2, 4), (3, 5)])
+    r3 = tree(q, [], [], [(2, 6), (3, 7)])
+    r4 = tree(q, [], [], [(2, 0), (3, 1)])
+
     q, mine = call(
         update_kernel,
         [vec, jax.ShapeDtypeStruct((size + TAIL, width), bf16)],
-        [block_rows, counts, s, block, q, got, hub, *last],
-        [SMEM] * 2 + [VMEM] * 8,
+        [block_rows, counts, s, block, q, r2, r3, r4, hub, h4, h7, h6, h3, h1],
+        [SMEM] * 2 + [VMEM] * 12,
         [VMEM] * 2,
     )
 
     def swap(value, step):
         return send(value, [((r, c), (r, c ^ step)) for r in range(NR) for c in range(NC)])
 
-    beside = swap(mine, 1)
+    rest = send_only(q, [((3, 3), (2, 3)), ((1, 3), (0, 3))])
     across = swap(mine, 2)
+    mine_after, across = lax.optimization_barrier((mine, across))
+    beside = swap(mine_after, 1)
     corner = swap(across, 1)
-    rest = send(
-        q, [((a, 3), (b, 3)) for a, b in ((5, 1), (7, 3), (4, 2), (6, 0))] + [((a, 2), (a - 4, 2)) for a in (4, 5, 6)]
-    )
     solved, remainder = call(
         final_kernel,
         [jax.ShapeDtypeStruct((size, width), jnp.float32), jax.ShapeDtypeStruct(rhs.shape, jnp.float32)],

time: 80.4 us -> 77.4 us (0.963)
  the two profiles are of different devices: /device:TPU:7 before, /device:TPU:3 now
where the time goes in v6:
time: 77.4 us; the launch traced here: 77.1 us
  starting transfers between devices  45 us (58%)
  waiting for transfers between devices  26.3 us (34%)
  Pallas kernels  2.35 us (3%)
  between operations  2.12 us (3%)
  local copies, waits for them, and re-layouts  1.32 us (2%)
    ppermute x23, starting transfers between devices, send(): lax.ppermute(value, ('row', 'col'), [(a * NC + b, c * NC + d) for (a, b),...  41 us
    ppermute x23, waiting for transfers between devices, send(): lax.ppermute(value, ('row', 'col'), [(a * NC + b, c * NC + d) for (a, b),...  20.4 us
    ppermute x5, waiting for transfers between devices, send_only(): lax.ppermute(value, ('row', 'col'), [(a * NC + b, c * NC + d) for (a, b),...  5.95 us
    ppermute x5, starting transfers between devices, send_only(): lax.ppermute(value, ('row', 'col'), [(a * NC + b, c * NC + d) for (a, b),...  3.97 us
    pallas_call x11, Pallas kernels, call(): pl.pallas_call(kernel, out_shape=outs, in_specs=in_specs, out_specs=out_s...  2.35 us
  transfers between devices with their start and end apart: 28, of which 13 were waited for; matrix products, arithmetic and copies ran while one was open for 0% of the time, Pallas kernels for 1%

profile of v6, /device:TPU:3, one launch (start us, length us, event | category | flops | bytes accessed | tf_op | source)
XLA Modules:
  0.0 77.1 jit_solution(14100887602099996436)
XLA Ops:
  0.6 1.3 %copy-done.2 = bf16[4,128,1024]{2,1,0:T(8,128)(2,1)S(1)} copy-done((bf16[4,128,1024]{2,1,0:T(8,128)(2,1)S(1)}, bf16[4,128,1024]{2,1,0:T(8,128)(2,1)}, u32[]{:S(2)}) %copy-start.2) | copy-done | bytes 1048600
  2.0 1.4 %collective-permute-start.3 = (bf16[128,1024]{1,0:T(8,128)(2,1)S(1)}, bf16[128,1024]{1,0:T(8,128)(2,1)S(1)}, u32[]{:S(2)}, u32[]{:S(2)}) collective-permute-start(bf16[128,1024]{1,0:T(8,128)(2,1)S(1)} %get-tuple-element.24), channel_id=1, source_target_pairs={{0,1},{1,0},{2,10},{3,11},{4,5},{5,4},{6,7},{7,6},{8,16},{9,17},{1... | collective-permute-start | bytes 786440 | tf_op jit(solution)/shard_map/ppermute | solution.py:115
  3.4 1.3 %collective-permute-start.2 = (bf16[128,768]{1,0:T(8,128)(2,1)S(1)}, bf16[128,768]{1,0:T(8,128)(2,1)S(1)}, u32[]{:S(2)}, u32[]{:S(2)}) collective-permute-start(bf16[128,768]{1,0:T(8,128)(2,1)S(1)} %get-tuple-element.23), channel_id=1, source_target_pairs={{0,2},{1,3},{2,10},{3,11},{4,5},{5,4},{6,7},{7,6},{8,16},{9,17},{1... | collective-permute-start | bytes 589832 | tf_op jit(solution)/shard_map/ppermute | solution.py:115
  4.7 1.3 %collective-permute-start.1 = (bf16[128,512]{1,0:T(8,128)(2,1)S(1)}, bf16[128,512]{1,0:T(8,128)(2,1)S(1)}, u32[]{:S(2)}, u32[]{:S(2)}) collective-permute-start(bf16[128,512]{1,0:T(8,128)(2,1)S(1)} %get-tuple-element.22), channel_id=1, source_target_pairs={{0,1},{1,0},{2,10},{3,11},{4,5},{5,4},{6,7},{7,6},{8,13},{9,2},{10... | collective-permute-start | bytes 393224 | tf_op jit(solution)/shard_map/ppermute | solution.py:115
  6.0 2.1 %collective-permute-start = (bf16[128,256]{1,0:T(8,128)(2,1)S(1)}, bf16[128,256]{1,0:T(8,128)(2,1)S(1)}, u32[]{:S(2)}, u32[]{:S(2)}) collective-permute-start(bf16[128,256]{1,0:T(8,128)(2,1)S(1)} %get-tuple-element.21), channel_id=1, source_target_pairs={{0,8},{1,5},{2,22},{3,15},{4,1},{5,9},{6,14},{7,23},{8,0},{9,11},{... | collective-permute-start | bytes 196616 | tf_op jit(solution)/shard_map/ppermute | solution.py:115
  8.0 8.8 %collective-permute-done.refs_0_ = bf16[128,256]{1,0:T(8,128)(2,1)S(1)} collective-permute-done((bf16[128,256]{1,0:T(8,128)(2,1)S(1)}, bf16[128,256]{1,0:T(8,128)(2,1)S(1)}, u32[]{:S(2)}, u32[]{:S(2)}) %collective-permute-start) | collective-permute-done | bytes 65568 | tf_op jit(solution)/shard_map/ppermute | solution.py:115
  16.8 1.6 %collective-permute-start.10 = (bf16[128,2560]{1,0:T(8,128)(2,1)S(1)}, bf16[128,2560]{1,0:T(8,128)(2,1)S(1)}, u32[]{:S(2)}, u32[]{:S(2)}) collective-permute-start(bf16[128,2560]{1,0:T(8,128)(2,1)S(1)} %pack_kernel.1), channel_id=1, source_target_pairs={{0,1},{1,0},{2,3},{3,2},{4,5},{5,4},{6,7},{7,6},{8,9},{9,8},{10,11... | collective-permute-start | bytes 1966088 | tf_op jit(solution)/shard_map/ppermute | solution.py:115
  19.1 0.8 %collective-permute-start.5 = (bf16[256,128]{1,0:T(8,128)(2,1)S(1)}, bf16[256,128]{1,0:T(8,128)(2,1)S(1)}, u32[]{:S(2)}, u32[]{:S(2)}) collective-permute-start(bf16[256,128]{1,0:T(8,128)(2,1)S(1)} %first_kernel.1), channel_id=1, source_target_pairs={{0,8},{1,12},{2,3},{3,4},{4,0},{5,7},{6,2},{7,6},{8,9},{9,1},{10,1... | collective-permute-start | bytes 196616 | tf_op jit(solution)/shard_map/ppermute | solution.py:115
  19.9 1.9 %collective-permute-start.6 = (bf16[256,128]{1,0:T(8,128)(2,1)S(1)}, bf16[256,128]{1,0:T(8,128)(2,1)S(1)}, u32[]{:S(2)}, u32[]{:S(2)}) collective-permute-start(bf16[256,128]{1,0:T(8,128)(2,1)S(1)} %first_kernel.1), channel_id=1, source_target_pairs={{0,12},{1,3},{2,4},{3,8},{4,0},{5,7},{6,2},{7,6},{8,9},{9,1},{10,1... | collective-permute-start | bytes 196616 | tf_op jit(solution)/shard_map/ppermute | solution.py:115
  21.9 1.4 %collective-permute-done.4.g0 = bf16[256,128]{1,0:T(8,128)(2,1)S(1)} collective-permute-done((bf16[256,128]{1,0:T(8,128)(2,1)S(1)}, bf16[256,128]{1,0:T(8,128)(2,1)S(1)}, u32[]{:S(2)}, u32[]{:S(2)}) %collective-permute-start.4) | collective-permute-done | bytes 65568 | tf_op jit(solution)/shard_map/ppermute | solution.py:115
  23.2 1.3 %collective-permute-done.6.g2 = bf16[256,128]{1,0:T(8,128)(2,1)S(1)} collective-permute-done((bf16[256,128]{1,0:T(8,128)(2,1)S(1)}, bf16[256,128]{1,0:T(8,128)(2,1)S(1)}, u32[]{:S(2)}, u32[]{:S(2)}) %collective-permute-start.6) | collective-permute-done | bytes 65568 | tf_op jit(solution)/shard_map/ppermute | solution.py:115
  24.5 1.4 %collective-permute-done.7.g3 = bf16[256,128]{1,0:T(8,128)(2,1)S(1)} collective-permute-done((bf16[256,128]{1,0:T(8,128)(2,1)S(1)}, bf16[256,128]{1,0:T(8,128)(2,1)S(1)}, u32[]{:S(2)}, u32[]{:S(2)}) %collective-permute-start.7) | collective-permute-done | bytes 65568 | tf_op jit(solution)/shard_map/ppermute | solution.py:115
  26.5 0.9 %collective-permute-done.8.p_in = bf16[1024,128]{1,0:T(8,128)(2,1)S(1)} collective-permute-done((bf16[1024,128]{1,0:T(8,128)(2,1)S(1)}, bf16[1024,128]{1,0:T(8,128)(2,1)S(1)}, u32[]{:S(2)}, u32[]{:S(2)}) %collective-permute-start.8) | collective-permute-done | bytes 262176 | tf_op jit(solution)/shard_map/ppermute | solution.py:115
  28.4 1.0 %collective-permute-done.11.p_in = bf16[1024,128]{1,0:T(8,128)(2,1)S(1)} collective-permute-done((bf16[1024,128]{1,0:T(8,128)(2,1)S(1)}, bf16[1024,128]{1,0:T(8,128)(2,1)S(1)}, u32[]{:S(2)}, u32[]{:S(2)}) %collective-permute-start.11) | collective-permute-done | bytes 262176 | tf_op jit(solution)/shard_map/ppermute | solution.py:115
  30.4 0.7 collective-permute-start.13
  33.4 0.7 collective-permute-start.14
  34.0 0.7 collective-permute-start.15
  34.7 0.7 collective-permute-start.16
  36.9 17.1 %collective-permute-start.25 = (bf16[1040,128]{1,0:T(8,128)(2,1)S(1)}, bf16[1040,128]{1,0:T(8,128)(2,1)S(1)}, u32[]{:S(2)}, u32[]{:S(2)}) collective-permute-start(bf16[1040,128]{1,0:T(8,128)(2,1)S(1)} %get-tuple-element.36.refs_0_), channel_id=1, source_target_pairs={{0,2},{1,3},{2,0},{3,1},{4,6},{5,7},{6,4},{7,5},{8,10},{9,11},{10,... | collective-permute-start | bytes 798728 | tf_op jit(solution)/shard_map/ppermute | solution.py:115
  54.0 3.8 %collective-permute-done.25.refs_2_ = bf16[1040,128]{1,0:T(8,128)(2,1)S(1)} collective-permute-done((bf16[1040,128]{1,0:T(8,128)(2,1)S(1)}, bf16[1040,128]{1,0:T(8,128)(2,1)S(1)}, u32[]{:S(2)}, u32[]{:S(2)}) %collective-permute-start.25) | collective-permute-done | bytes 266272 | tf_op jit(solution)/shard_map/ppermute | solution.py:115
  57.8 10.7 %collective-permute-start.26 = (bf16[1040,128]{1,0:T(8,128)(2,1)S(1)}, bf16[1040,128]{1,0:T(8,128)(2,1)S(1)}, u32[]{:S(2)}, u32[]{:S(2)}) collective-permute-start(bf16[1040,128]{1,0:T(8,128)(2,1)S(1)} %get-tuple-element.36.refs_0_), channel_id=1, source_target_pairs={{0,1},{1,0},{2,3},{3,2},{4,5},{5,4},{6,7},{7,6},{8,9},{9,8},{10,11... | collective-permute-start | bytes 798728 | tf_op jit(solution)/shard_map/ppermute | solution.py:115
  68.5 1.3 %collective-permute-start.24 = (bf16[1024,128]{1,0:T(8,128)(2,1)S(1)}, bf16[1024,128]{1,0:T(8,128)(2,1)S(1)}, u32[]{:S(2)}, u32[]{:S(2)}) collective-permute-start(bf16[1024,128]{1,0:T(8,128)(2,1)S(1)} %get-tuple-element.34.q_ref), channel_id=1, source_target_pairs={{15,11},{7,3}} | collective-permute-start | bytes 786440 | tf_op jit(solution)/shard_map/ppermute | solution.py:119
  69.8 5.9 %collective-permute-done.24.rest_ref = bf16[1024,128]{1,0:T(8,128)(2,1)S(1)} collective-permute-done((bf16[1024,128]{1,0:T(8,128)(2,1)S(1)}, bf16[1024,128]{1,0:T(8,128)(2,1)S(1)}, u32[]{:S(2)}, u32[]{:S(2)}) %collective-permute-start.24) | collective-permute-done | bytes 262176 | tf_op jit(solution)/shard_map/ppermute | solution.py:119
  75.7 1.4 %final_kernel.1 = (f32[1024,128]{1,0:T(8,128)}, f32[2,1024,128]{2,1,0:T(8,128)}) custom-call(f32[2,1024,128]{2,1,0:T(8,128)S(1)} %bitcast.14, bf16[1024,128]{1,0:T(8,128)(2,1)S(1)} %get-tuple-element.34.q_ref, bf16[1024,128]{1,0:T(8,128)(2,1)S(1)} %collective-permute-done.24.rest_ref, bf16[1040,128]{1,0:T(8,128)(2,1)S(1)} %get-tuple-element.36.refs_0_, ...), custom_call_target="tpu_custom_call" | custom-call | tf_op jit(solution)/shard_map/final_kernel/pallas_call | solution.py:142
  (51 shorter events, 5.7 us)
Async XLA Ops:
  2.0 14.8 %collective-permute-start.3 = (bf16[128,1024]{1,0:T(8,128)(2,1)S(1)}, bf16[128,1024]{1,0:T(8,128)(2,1)S(1)}, u32[]{:S(2)}, u32[]{:S(2)}) collective-permute-start(bf16[128,1024]{1,0:T(8,128)(2,1)S(1)} %get-tuple-element.24), channel_id=1, source_target_pairs={{0,1},{1,0},{2,10},{3,11},{4,5},{5,4},{6,7},{7,6},{8,16},{9,17},{1... | collective-permute-start | bytes 786440 | tf_op jit(solution)/shard_map/ppermute | solution.py:115
  3.4 13.4 %collective-permute-start.2 = (bf16[128,768]{1,0:T(8,128)(2,1)S(1)}, bf16[128,768]{1,0:T(8,128)(2,1)S(1)}, u32[]{:S(2)}, u32[]{:S(2)}) collective-permute-start(bf16[128,768]{1,0:T(8,128)(2,1)S(1)} %get-tuple-element.23), channel_id=1, source_target_pairs={{0,2},{1,3},{2,10},{3,11},{4,5},{5,4},{6,7},{7,6},{8,16},{9,17},{1... | collective-permute-start | bytes 589832 | tf_op jit(solution)/shard_map/ppermute | solution.py:115
  4.7 12.1 %collective-permute-start.1 = (bf16[128,512]{1,0:T(8,128)(2,1)S(1)}, bf16[128,512]{1,0:T(8,128)(2,1)S(1)}, u32[]{:S(2)}, u32[]{:S(2)}) collective-permute-start(bf16[128,512]{1,0:T(8,128)(2,1)S(1)} %get-tuple-element.22), channel_id=1, source_target_pairs={{0,1},{1,0},{2,10},{3,11},{4,5},{5,4},{6,7},{7,6},{8,13},{9,2},{10... | collective-permute-start | bytes 393224 | tf_op jit(solution)/shard_map/ppermute | solution.py:115
  6.0 10.8 %collective-permute-start = (bf16[128,256]{1,0:T(8,128)(2,1)S(1)}, bf16[128,256]{1,0:T(8,128)(2,1)S(1)}, u32[]{:S(2)}, u32[]{:S(2)}) collective-permute-start(bf16[128,256]{1,0:T(8,128)(2,1)S(1)} %get-tuple-element.21), channel_id=1, source_target_pairs={{0,8},{1,5},{2,22},{3,15},{4,1},{5,9},{6,14},{7,23},{8,0},{9,11},{... | collective-permute-start | bytes 196616 | tf_op jit(solution)/shard_map/ppermute | solution.py:115
  16.8 9.6 %collective-permute-start.10 = (bf16[128,2560]{1,0:T(8,128)(2,1)S(1)}, bf16[128,2560]{1,0:T(8,128)(2,1)S(1)}, u32[]{:S(2)}, u32[]{:S(2)}) collective-permute-start(bf16[128,2560]{1,0:T(8,128)(2,1)S(1)} %pack_kernel.1), channel_id=1, source_target_pairs={{0,1},{1,0},{2,3},{3,2},{4,5},{5,4},{6,7},{7,6},{8,9},{9,8},{10,11... | collective-permute-start | bytes 1966088 | tf_op jit(solution)/shard_map/ppermute | solution.py:115
  19.0 4.2 %collective-permute-start.4 = (bf16[256,128]{1,0:T(8,128)(2,1)S(1)}, bf16[256,128]{1,0:T(8,128)(2,1)S(1)}, u32[]{:S(2)}, u32[]{:S(2)}) collective-permute-start(bf16[256,128]{1,0:T(8,128)(2,1)S(1)} %first_kernel.1), channel_id=1, source_target_pairs={{0,4},{1,8},{2,12},{3,2},{4,0},{5,1},{6,7},{7,6},{8,9},{9,3},{10,1... | collective-permute-start | bytes 196616 | tf_op jit(solution)/shard_map/ppermute | solution.py:115
  19.1 4.1 %collective-permute-start.5 = (bf16[256,128]{1,0:T(8,128)(2,1)S(1)}, bf16[256,128]{1,0:T(8,128)(2,1)S(1)}, u32[]{:S(2)}, u32[]{:S(2)}) collective-permute-start(bf16[256,128]{1,0:T(8,128)(2,1)S(1)} %first_kernel.1), channel_id=1, source_target_pairs={{0,8},{1,12},{2,3},{3,4},{4,0},{5,7},{6,2},{7,6},{8,9},{9,1},{10,1... | collective-permute-start | bytes 196616 | tf_op jit(solution)/shard_map/ppermute | solution.py:115
  19.9 4.6 %collective-permute-start.6 = (bf16[256,128]{1,0:T(8,128)(2,1)S(1)}, bf16[256,128]{1,0:T(8,128)(2,1)S(1)}, u32[]{:S(2)}, u32[]{:S(2)}) collective-permute-start(bf16[256,128]{1,0:T(8,128)(2,1)S(1)} %first_kernel.1), channel_id=1, source_target_pairs={{0,12},{1,3},{2,4},{3,8},{4,0},{5,7},{6,2},{7,6},{8,9},{9,1},{10,1... | collective-permute-start | bytes 196616 | tf_op jit(solution)/shard_map/ppermute | solution.py:115
  21.9 4.0 %collective-permute-start.7 = (bf16[256,128]{1,0:T(8,128)(2,1)S(1)}, bf16[256,128]{1,0:T(8,128)(2,1)S(1)}, u32[]{:S(2)}, u32[]{:S(2)}) collective-permute-start(bf16[256,128]{1,0:T(8,128)(2,1)S(1)} %first_kernel.1), channel_id=1, source_target_pairs={{0,2},{1,4},{2,8},{3,12},{4,0},{5,3},{6,7},{7,6},{8,9},{9,1},{10,1... | collective-permute-start | bytes 196616 | tf_op jit(solution)/shard_map/ppermute | solution.py:115
  25.9 1.9 %collective-permute-start.9 = (bf16[1024,128]{1,0:T(8,128)(2,1)S(1)}, bf16[1024,128]{1,0:T(8,128)(2,1)S(1)}, u32[]{:S(2)}, u32[]{:S(2)}) collective-permute-start(bf16[1024,128]{1,0:T(8,128)(2,1)S(1)} %get-tuple-element.26.s_prev), channel_id=1, source_target_pairs={{0,1},{1,0},{2,3},{3,2},{4,5},{5,4},{6,7},{7,6},{8,9},{9,8},{10,11... | collective-permute-start | bytes 786440 | tf_op jit(solution)/shard_map/ppermute | solution.py:115
  28.0 1.8 %collective-permute-start.12 = (bf16[1024,128]{1,0:T(8,128)(2,1)S(1)}, bf16[1024,128]{1,0:T(8,128)(2,1)S(1)}, u32[]{:S(2)}, u32[]{:S(2)}) collective-permute-start(bf16[1024,128]{1,0:T(8,128)(2,1)S(1)} %get-tuple-element.29.q_prev), channel_id=1, source_target_pairs={{0,1},{1,0},{2,3},{3,2},{4,5},{5,4},{6,7},{7,6},{8,9},{9,13},{10,1... | collective-permute-start | bytes 786440 | tf_op jit(solution)/shard_map/ppermute | solution.py:115
  30.0 1.8 %collective-permute-start.18 = (bf16[1024,128]{1,0:T(8,128)(2,1)S(1)}, bf16[1024,128]{1,0:T(8,128)(2,1)S(1)}, u32[]{:S(2)}, u32[]{:S(2)}) collective-permute-start(bf16[1024,128]{1,0:T(8,128)(2,1)S(1)} %get-tuple-element.31.s_ref), channel_id=1, source_target_pairs={{0,1},{1,0},{2,3},{3,2},{4,5},{5,4},{6,7},{7,6},{8,9},{9,8},{10,11... | collective-permute-start | bytes 786440 | tf_op jit(solution)/shard_map/ppermute | solution.py:115
  30.4 2.4 %collective-permute-start.13 = (bf16[1024,128]{1,0:T(8,128)(2,1)S(1)}, bf16[1024,128]{1,0:T(8,128)(2,1)S(1)}, u32[]{:S(2)}, u32[]{:S(2)}) collective-permute-start(bf16[1024,128]{1,0:T(8,128)(2,1)S(1)} %get-tuple-element.32.q_ref), channel_id=1, source_target_pairs={{8,16},{12,20},{4,0},{9,17},{13,21},{14,10}} | collective-permute-start | bytes 786440 | tf_op jit(solution)/shard_map/ppermute | solution.py:119
  32.0 2.1 %collective-permute-start.20 = (bf16[1024,128]{1,0:T(8,128)(2,1)S(1)}, bf16[1024,128]{1,0:T(8,128)(2,1)S(1)}, u32[]{:S(2)}, u32[]{:S(2)}) collective-permute-start(bf16[1024,128]{1,0:T(8,128)(2,1)S(1)} %step3_kernel.1.hub), channel_id=1, source_target_pairs={{0,1},{1,0},{2,3},{3,2},{4,5},{5,4},{6,7},{7,6},{8,9},{9,8},{10,11... | collective-permute-start | bytes 786440 | tf_op jit(solution)/shard_map/ppermute | solution.py:115
  32.3 2.4 %collective-permute-start.21 = (bf16[1024,128]{1,0:T(8,128)(2,1)S(1)}, bf16[1024,128]{1,0:T(8,128)(2,1)S(1)}, u32[]{:S(2)}, u32[]{:S(2)}) collective-permute-start(bf16[1024,128]{1,0:T(8,128)(2,1)S(1)} %step3_kernel.1.hub), channel_id=1, source_target_pairs={{0,1},{1,0},{2,3},{3,2},{4,5},{5,4},{6,7},{7,6},{8,9},{9,8},{10,11... | collective-permute-start | bytes 786440 | tf_op jit(solution)/shard_map/ppermute | solution.py:115
  32.5 4.2 %collective-permute-start.22 = (bf16[1024,128]{1,0:T(8,128)(2,1)S(1)}, bf16[1024,128]{1,0:T(8,128)(2,1)S(1)}, u32[]{:S(2)}, u32[]{:S(2)}) collective-permute-start(bf16[1024,128]{1,0:T(8,128)(2,1)S(1)} %step3_kernel.1.hub), channel_id=1, source_target_pairs={{0,1},{1,0},{2,3},{3,2},{4,5},{5,4},{6,7},{7,6},{8,9},{9,8},{10,11... | collective-permute-start | bytes 786440 | tf_op jit(solution)/shard_map/ppermute | solution.py:115
  32.8 3.9 %collective-permute-start.23 = (bf16[1024,128]{1,0:T(8,128)(2,1)S(1)}, bf16[1024,128]{1,0:T(8,128)(2,1)S(1)}, u32[]{:S(2)}, u32[]{:S(2)}) collective-permute-start(bf16[1024,128]{1,0:T(8,128)(2,1)S(1)} %step3_kernel.1.hub), channel_id=1, source_target_pairs={{0,1},{1,0},{2,3},{3,2},{4,5},{5,4},{6,14},{7,6},{8,9},{9,8},{10,1... | collective-permute-start | bytes 786440 | tf_op jit(solution)/shard_map/ppermute | solution.py:115
  33.4 3.4 %collective-permute-start.14 = (bf16[1024,128]{1,0:T(8,128)(2,1)S(1)}, bf16[1024,128]{1,0:T(8,128)(2,1)S(1)}, u32[]{:S(2)}, u32[]{:S(2)}) collective-permute-start(bf16[1024,128]{1,0:T(8,128)(2,1)S(1)} %relay_kernel.1.q0), channel_id=1, source_target_pairs={{16,24},{20,28},{17,25},{21,29},{9,1},{13,5},{10,18},{14,22}} | collective-permute-start | bytes 786440 | tf_op jit(solution)/shard_map/ppermute | solution.py:119
  34.0 2.7 %collective-permute-start.15 = (bf16[1024,128]{1,0:T(8,128)(2,1)S(1)}, bf16[1024,128]{1,0:T(8,128)(2,1)S(1)}, u32[]{:S(2)}, u32[]{:S(2)}) collective-permute-start(bf16[1024,128]{1,0:T(8,128)(2,1)S(1)} %relay_kernel.1.q0), channel_id=1, source_target_pairs={{10,26},{14,30}} | collective-permute-start | bytes 786440 | tf_op jit(solution)/shard_map/ppermute | solution.py:119
  34.7 2.0 %collective-permute-start.16 = (bf16[1024,128]{1,0:T(8,128)(2,1)S(1)}, bf16[1024,128]{1,0:T(8,128)(2,1)S(1)}, u32[]{:S(2)}, u32[]{:S(2)}) collective-permute-start(bf16[1024,128]{1,0:T(8,128)(2,1)S(1)} %relay_kernel.1.q0), channel_id=1, source_target_pairs={{10,2},{14,6}} | collective-permute-start | bytes 786440 | tf_op jit(solution)/shard_map/ppermute | solution.py:119
  36.9 20.9 %collective-permute-start.25 = (bf16[1040,128]{1,0:T(8,128)(2,1)S(1)}, bf16[1040,128]{1,0:T(8,128)(2,1)S(1)}, u32[]{:S(2)}, u32[]{:S(2)}) collective-permute-start(bf16[1040,128]{1,0:T(8,128)(2,1)S(1)} %get-tuple-element.36.refs_0_), channel_id=1, source_target_pairs={{0,2},{1,3},{2,0},{3,1},{4,6},{5,7},{6,4},{7,5},{8,10},{9,11},{10,... | collective-permute-start | bytes 798728 | tf_op jit(solution)/shard_map/ppermute | solution.py:115
  57.8 17.9 %collective-permute-start.26 = (bf16[1040,128]{1,0:T(8,128)(2,1)S(1)}, bf16[1040,128]{1,0:T(8,128)(2,1)S(1)}, u32[]{:S(2)}, u32[]{:S(2)}) collective-permute-start(bf16[1040,128]{1,0:T(8,128)(2,1)S(1)} %get-tuple-element.36.refs_0_), channel_id=1, source_target_pairs={{0,1},{1,0},{2,3},{3,2},{4,5},{5,4},{6,7},{7,6},{8,9},{9,8},{10,11... | collective-permute-start | bytes 798728 | tf_op jit(solution)/shard_map/ppermute | solution.py:115
  68.5 7.2 %collective-permute-start.27 = (bf16[1040,128]{1,0:T(8,128)(2,1)S(1)}, bf16[1040,128]{1,0:T(8,128)(2,1)S(1)}, u32[]{:S(2)}, u32[]{:S(2)}) collective-permute-start(bf16[1040,128]{1,0:T(8,128)(2,1)S(1)} %collective-permute-done.25.refs_2_), channel_id=1, source_target_pairs={{0,1},{1,0},{2,3},{3,2},{4,5},{5,4},{6,7},{7,6},{8,9},{9,8},{10,11... | collective-permute-start | bytes 798728 | tf_op jit(solution)/shard_map/ppermute | solution.py:115
  68.5 7.2 %collective-permute-start.24 = (bf16[1024,128]{1,0:T(8,128)(2,1)S(1)}, bf16[1024,128]{1,0:T(8,128)(2,1)S(1)}, u32[]{:S(2)}, u32[]{:S(2)}) collective-permute-start(bf16[1024,128]{1,0:T(8,128)(2,1)S(1)} %get-tuple-element.34.q_ref), channel_id=1, source_target_pairs={{15,11},{7,3}} | collective-permute-start | bytes 786440 | tf_op jit(solution)/shard_map/ppermute | solution.py:119
  (8 other events, 65.8 us)

commit v7 on v6

--- a/solution.py
+++ b/solution.py
@@ -66,7 +66,9 @@
 MAKER = (None, (2, 1), (3, 2), (5, 3))
 FIRST = (1, 0)
 BESIDE = (3, 1)
-PARTNER = (None, (2, 0), (3, 3), (5, 2))
+PARTNER = (None, (3, 1), (3, 3), (5, 2))
+PIECES = ((4, 0), (2, 1), (6, 5), (7, 3))
+REST = ((2, 3), (0, 3), (0, 2), (1, 2))
 
 
 def hops(a, b):
@@ -170,7 +172,7 @@
 
 def first_kernel(rhs_ref, diag_ref, *refs):
     parts, out_ref = refs[: NR // 2], refs[NR // 2]
-    rhs_v, lo_v, hi_v, rhs_sem, lo_sem, hi_sem = refs[NR // 2 + 1 :]
+    rhs_v, d_v, rhs_sem, d_sem = refs[NR // 2 + 1 :]
     n = out_ref.shape[0] // 2
     col = lax.axis_index("col")
 
@@ -179,19 +181,19 @@
         rhs_copy = pltpu.make_async_copy(rhs_ref.at[0], rhs_v, rhs_sem)
         rhs_copy.start()
 
-        def piece(c):
-            lo_wide, hi_wide = pair_width(c // 2, n), pair_width(2 + c // 2, n)
-            lo = parts[c // 2] if c else diag_ref.at[0, :, pl.ds(0, lo_wide)]
-            return (
-                pltpu.make_async_copy(lo, lo_v.at[:, pl.ds(0, lo_wide)], lo_sem),
-                pltpu.make_async_copy(parts[2 + c // 2], hi_v.at[:, pl.ds(0, hi_wide)], hi_sem),
-            )
+        def pieces(c):
+            copies = []
+            for i, r in enumerate(PIECES[c]):
+                wide = pair_width(r // 2, n)
+                source = parts[r // 2] if r else diag_ref.at[0, :, pl.ds(0, wide)]
+                copies.append(pltpu.make_async_copy(source, d_v.at[i, :, pl.ds(0, wide)], d_sem.at[i]))
+            return copies
 
         for c in range(NC):
 
             @pl.when(col == c)
             def _():
-                for copy in piece(c):
+                for copy in pieces(c):
                     copy.start()
 
         rhs_copy.wait()
@@ -200,11 +202,10 @@
 
             @pl.when(col == c)
             def _():
-                for copy in piece(c):
+                for i, copy in enumerate(pieces(c)):
                     copy.wait()
-                lo_wide, hi_wide = pair_width(c // 2, n), pair_width(2 + c // 2, n)
-                out_ref[:n] = low(dot(hi_v[:, :hi_wide], p[:hi_wide]))
-                out_ref[n:] = low(dot(lo_v[:, :lo_wide], p[:lo_wide]))
+                    wide = pair_width(PIECES[c][i] // 2, n)
+                    out_ref[i * n : (i + 1) * n] = low(dot(d_v[i, :, :wide], p[:wide]))
 
 
 def pack_kernel(*refs):
@@ -271,14 +272,18 @@
     part = l_ref.shape[0] // NR
     row = lax.axis_index("row")
 
+    def lookup(c, i):
+        r = jnp.int32(PIECES[0][i])
+        for n in range(1, NC):
+            r = jnp.where(c == n, PIECES[n][i], r)
+        return pl.multiple_of(r * part, part)
+
     @pl.when((row >= 1) & (row < 4) & (lax.axis_index("col") == 0))
     def _():
         for j, got in enumerate((g0, g1, g2, g3)):
             src = lax.rem(row + 7 - j, 4)
-            hi = pl.multiple_of((4 + src) * part, part)
-            lo = pl.multiple_of(src * part, part)
-            q_ref[pl.ds(hi, part)] = got[:part]
-            q_ref[pl.ds(lo, part)] = got[part:]
+            q_ref[pl.ds(lookup(src, 0), part)] = got[:part]
+            q_ref[pl.ds(lookup(src, 1), part)] = got[part:]
         s = dot(l_ref[...], q_ref[...])
         s_ref[...] = low(s)
         p_ref[...] = low(rhs_ref[0] - s)
@@ -321,27 +326,25 @@
         s_ref[...] = s_prev[...]
 
 
-def step3_kernel(a_ref, sum_ref, d_ref, q_ref, p_v):
-    @pl.when(at(MAKER[3]))
+def step3_kernel(took, a_ref, sum_ref, d_ref, q_prev, came_ref, q_ref, p_v):
+    active, taken = at(MAKER[3]), any_of(took)
+
+    @pl.when(active)
     def _():
         p_v[...] = low(a_ref[...].astype(jnp.float32) - sum_ref[...].astype(jnp.float32))
         lower_dot(q_ref, d_ref, p_v)
 
-
-def relay_kernel(q_ref, got_ref, out_ref):
-    row = lax.axis_index("row")
-    taken = (row == 4) | (row == 5) | at((0, 0)) | at((2, 2))
-
     @pl.when(taken)
     def _():
-        out_ref[...] = got_ref[...]
-
-    @pl.when(jnp.logical_not(taken))
-    def _():
-        out_ref[...] = q_ref[...]
-
-
-def update_kernel(rows_ref, counts_ref, s_ref, l_ref, q0, r2, r3, r4, hub, h4, h7, h6, h3, h1, q_ref, out_ref):
+        q_ref[...] = came_ref[...]
+
+    @pl.when(jnp.logical_not(active | taken))
+    def _():
+        q_ref[...] = q_prev[...]
+
+
+def update_kernel(takers, rows_ref, counts_ref, s_ref, l_ref, q_prev, *refs):
+    got, q_ref, out_ref = refs[:-2], refs[-2], refs[-1]
     size = l_ref.shape[0]
     row, col = lax.axis_index("row"), lax.axis_index("col")
     below = row >= NC
@@ -351,15 +354,10 @@
         def _():
             q_ref[...] = source[...]
 
-    from_r2 = ((col < 2) & ((row >= 6) | ((row < 2) & (col == 1)))) | at((4, 2)) | at((5, 2))
-    from_r3 = (col == 2) & (row >= 6)
-    from_r4 = (col == 2) & (row < 2)
-    take(from_r2, r2)
-    take(from_r3, r3)
-    take(from_r4, r4)
-    take((col < 3) & jnp.logical_not(from_r2 | from_r3 | from_r4), q0)
-    for r, source in ((5, hub), (4, h4), (7, h7), (6, h6), (3, h3), (1, h1)):
-        take((col == 3) & (row == r), source)
+    kept = jnp.logical_not(any_of([d for devices in takers for d in devices]))
+    take(kept, q_prev)
+    for devices, source in zip(takers, got):
+        take(any_of(devices), source)
 
     @pl.when(below)
     def _():
@@ -382,7 +380,7 @@
 def final_kernel(rhs_ref, q_ref, rest_ref, *refs):
     sums, (solved_ref, out_ref) = refs[:NC], refs[NC:]
     size = out_ref.shape[1]
-    came = at((2, 3)) | at((0, 3))
+    came = any_of(REST)
 
     @pl.when(came)
     def _():
@@ -416,13 +414,14 @@
     parts = []
     for m, cut in enumerate(cuts):
         even, odd = 2 * m, 2 * m + 1
-        pairs = [((odd, 0), (0, odd % 4))] + ([((even, 1), (0, even % 4))] if even else [])
+        at_piece = {r: (0, c) for c, rows in enumerate(PIECES) for r in rows}
+        pairs = [((odd, 0), at_piece[odd])] + ([((even, 1), at_piece[even])] if even else [])
         for k in range(1, NC):
-            maker, partner = MAKER[k], PARTNER[k]
+            maker = MAKER[k]
             if maker[0] != odd:
-                pairs.append(((odd, maker[1]), maker))
-            if partner[0] != even:
-                pairs.append(((even, partner[1]), partner))
+                pairs.append(((odd, k), maker))
+            if maker[0] != even:
+                pairs.append(((even, k ^ 1), PARTNER[k]))
         parts.append(send(cut, pairs))
     q = call(
         first_kernel,
@@ -432,11 +431,9 @@
         VMEM,
         [
             pltpu.VMEM((size, width), jnp.float32),
-            pltpu.VMEM((part, size // 2), bf16),
-            pltpu.VMEM((part, size), bf16),
+            pltpu.VMEM((2, part, size), bf16),
             dma,
-            dma,
-            dma,
+            pltpu.SemaphoreType.DMA((2,)),
         ],
     )
     takers = (FIRST, (2, 0), (3, 0))
@@ -465,35 +462,43 @@
     p, q, s = call(step1_kernel, [vec] * 3, [p_in, sums, rhs, diag, block, q, s], [VMEM] * 7, [VMEM] * 3)
     p_in = send(p, [(MAKER[1], MAKER[2])])
     q_in = send(q, [(MAKER[1], BESIDE)])
+
+    p_in, spread = lax.optimization_barrier((p_in, q))
+    came = send(spread, [((2, 0), (4, 0)), ((3, 0), (5, 0)), ((1, 0), (0, 0)), ((2, 1), (4, 1))])
+    took = [(4, 0), (5, 0), (0, 0), (4, 1)]
+
     a, q, s = call(step2_kernel, [vec] * 3, [p_in, q_in, sums, rhs, diag, block, q, s], [VMEM] * 8, [VMEM] * 3)
     sums = send(s, [(MAKER[2], MAKER[3])])
     a = send(a, [(BESIDE, MAKER[3])])
-    hub = call(step3_kernel, vec, [a, sums, diag], [VMEM] * 3, VMEM, [pltpu.VMEM((size, width), bf16)])
-
-    h4, h7, h6 = [send(hub, [(MAKER[3], (r, 3))]) for r in (4, 7, 6)]
-    h3, h1 = [send(hub, [(MAKER[3], (r, 3))]) for r in (3, 1)]
-
-    def tree(value, *columns):
-        return send_only(value, [((a, k), (b, k)) for k, edges in enumerate(columns) for a, b in edges])
-
-    r1 = tree(q, [(2, 4), (3, 5), (1, 0)], [(2, 4), (3, 5)], [(3, 2)])
-    q = call(relay_kernel, vec, [q, r1], [VMEM] * 2, VMEM)
-    r2 = tree(q, [(4, 6), (5, 7)], [(4, 6), (5, 7), (2, 0), (3, 1)], [(2, 4), (3, 5)])
-    r3 = tree(q, [], [], [(2, 6), (3, 7)])
-    r4 = tree(q, [], [], [(2, 0), (3, 1)])
-
+    q = call(
+        functools.partial(step3_kernel, took),
+        vec,
+        [a, sums, diag, q, came],
+        [VMEM] * 5,
+        VMEM,
+        [pltpu.VMEM((size, width), bf16)],
+    )
+
+    makers = [(MAKER[3], (r, 3)) for r in (4, 7, 6, 3, 1)]
+    second = [(MAKER[2], (r, 2)) for r in (4, 5, 6, 7, 2)]
+    others = [
+        [((4, 0), (6, 0)), ((5, 0), (7, 0)), ((4, 1), (6, 1)), ((3, 1), (5, 1)), ((2, 1), (0, 1))],
+        [((4, 1), (7, 1)), ((3, 1), (1, 1))],
+    ]
+    sends = [[makers[i], second[i], *(others[i] if i < 2 else [])] for i in range(5)]
+    got = [send(q, pairs) for pairs in sends]
     q, mine = call(
-        update_kernel,
+        functools.partial(update_kernel, [[b for _, b in pairs] for pairs in sends]),
         [vec, jax.ShapeDtypeStruct((size + TAIL, width), bf16)],
-        [block_rows, counts, s, block, q, r2, r3, r4, hub, h4, h7, h6, h3, h1],
-        [SMEM] * 2 + [VMEM] * 12,
+        [block_rows, counts, s, block, q, *got],
+        [SMEM] * 2 + [VMEM] * (3 + len(got)),
         [VMEM] * 2,
     )
 
     def swap(value, step):
         return send(value, [((r, c), (r, c ^ step)) for r in range(NR) for c in range(NC)])
 
-    rest = send_only(q, [((3, 3), (2, 3)), ((1, 3), (0, 3))])
+    rest = send_only(q, [(a, b) for a, b in zip(((3, 3), (1, 3), (2, 2), MAKER[2]), REST)])
     across = swap(mine, 2)
     mine_after, across = lax.optimization_barrier((mine, across))
     beside = swap(mine_after, 1)

time: 77.4 us -> 76.1 us (0.983)
  the two profiles are of different devices: /device:TPU:3 before, /device:TPU:6 now
where the time goes in v7:
time: 76.1 us; the launch traced here: 75.9 us
  starting transfers between devices  46.1 us (61%)
  waiting for transfers between devices  24.6 us (32%)
  between operations  2.11 us (3%)
  Pallas kernels  1.81 us (2%)
  local copies, waits for them, and re-layouts  1.32 us (2%)
    ppermute x24, starting transfers between devices, send(): lax.ppermute(value, ('row', 'col'), [(a * NC + b, c * NC + d) for (a, b),...  44.8 us
    ppermute x24, waiting for transfers between devices, send(): lax.ppermute(value, ('row', 'col'), [(a * NC + b, c * NC + d) for (a, b),...  17.6 us
    ppermute x1, waiting for transfers between devices, send_only(): lax.ppermute(value, ('row', 'col'), [(a * NC + b, c * NC + d) for (a, b),...  6.97 us
    pallas_call x10, Pallas kernels, call(): pl.pallas_call(kernel, out_shape=outs, in_specs=in_specs, out_specs=out_s...  1.81 us
  transfers between devices with their start and end apart: 25, of which 13 were waited for; matrix products, arithmetic and copies ran while one was open for 0% of the time, Pallas kernels for 0%

profile of v7, /device:TPU:6, one launch (start us, length us, event | category | flops | bytes accessed | tf_op | source)
XLA Modules:
  0.0 75.9 jit_solution(9254923237773851165)
XLA Ops:
  0.6 1.3 %copy-done.2 = bf16[4,128,1024]{2,1,0:T(8,128)(2,1)S(1)} copy-done((bf16[4,128,1024]{2,1,0:T(8,128)(2,1)S(1)}, bf16[4,128,1024]{2,1,0:T(8,128)(2,1)}, u32[]{:S(2)}) %copy-start.2) | copy-done | bytes 1048600
  2.1 0.5 collective-permute-start.2
  2.6 4.7 %collective-permute-start = (bf16[128,256]{1,0:T(8,128)(2,1)S(1)}, bf16[128,256]{1,0:T(8,128)(2,1)S(1)}, u32[]{:S(2)}, u32[]{:S(2)}) collective-permute-start(bf16[128,256]{1,0:T(8,128)(2,1)S(1)} %get-tuple-element.23), channel_id=1, source_target_pairs={{0,13},{1,5},{2,22},{3,15},{4,1},{5,9},{6,14},{7,23},{8,0},{9,8},{... | collective-permute-start | bytes 196616 | tf_op jit(solution)/shard_map/ppermute | solution.py:117
  7.3 2.2 %collective-permute-done.refs_0_ = bf16[128,256]{1,0:T(8,128)(2,1)S(1)} collective-permute-done((bf16[128,256]{1,0:T(8,128)(2,1)S(1)}, bf16[128,256]{1,0:T(8,128)(2,1)S(1)}, u32[]{:S(2)}, u32[]{:S(2)}) %collective-permute-start) | collective-permute-done | bytes 65568 | tf_op jit(solution)/shard_map/ppermute | solution.py:117
  9.8 0.5 collective-permute-start.4
  10.4 9.2 %collective-permute-start.5 = (bf16[256,128]{1,0:T(8,128)(2,1)S(1)}, bf16[256,128]{1,0:T(8,128)(2,1)S(1)}, u32[]{:S(2)}, u32[]{:S(2)}) collective-permute-start(bf16[256,128]{1,0:T(8,128)(2,1)S(1)} %first_kernel.1), channel_id=1, source_target_pairs={{0,8},{1,12},{2,3},{3,4},{4,0},{5,7},{6,2},{7,6},{8,9},{9,1},{10,1... | collective-permute-start | bytes 196616 | tf_op jit(solution)/shard_map/ppermute | solution.py:117
  19.6 0.5 collective-permute-start.7
  20.0 1.4 %collective-permute-done.5.g1 = bf16[256,128]{1,0:T(8,128)(2,1)S(1)} collective-permute-done((bf16[256,128]{1,0:T(8,128)(2,1)S(1)}, bf16[256,128]{1,0:T(8,128)(2,1)S(1)}, u32[]{:S(2)}, u32[]{:S(2)}) %collective-permute-start.5) | collective-permute-done | bytes 65568 | tf_op jit(solution)/shard_map/ppermute | solution.py:117
  21.4 0.6 collective-permute-done.6.g2
  22.1 0.5 collective-permute-start.9
  22.7 0.9 %collective-permute-done.8.p_in = bf16[1024,128]{1,0:T(8,128)(2,1)S(1)} collective-permute-done((bf16[1024,128]{1,0:T(8,128)(2,1)S(1)}, bf16[1024,128]{1,0:T(8,128)(2,1)S(1)}, u32[]{:S(2)}, u32[]{:S(2)}) %collective-permute-start.8) | collective-permute-done | bytes 262176 | tf_op jit(solution)/shard_map/ppermute | solution.py:117
  23.6 0.4 collective-permute-done.9.sum_ref
  24.6 1.0 %collective-permute-done.11.p_in = bf16[1024,128]{1,0:T(8,128)(2,1)S(1)} collective-permute-done((bf16[1024,128]{1,0:T(8,128)(2,1)S(1)}, bf16[1024,128]{1,0:T(8,128)(2,1)S(1)}, u32[]{:S(2)}, u32[]{:S(2)}) %collective-permute-start.11) | collective-permute-done | bytes 262176 | tf_op jit(solution)/shard_map/ppermute | solution.py:117
  25.6 0.4 collective-permute-done.12.q_in
  26.7 0.9 %collective-permute-done.13.a_ref = bf16[1024,128]{1,0:T(8,128)(2,1)S(1)} collective-permute-done((bf16[1024,128]{1,0:T(8,128)(2,1)S(1)}, bf16[1024,128]{1,0:T(8,128)(2,1)S(1)}, u32[]{:S(2)}, u32[]{:S(2)}) %collective-permute-start.13) | collective-permute-done | bytes 262176 | tf_op jit(solution)/shard_map/ppermute | solution.py:117
  27.6 0.4 collective-permute-done.14.sum_ref
  28.0 0.4 collective-permute-done.15.came_ref
  29.5 20.6 %collective-permute-start.20 = (bf16[1024,128]{1,0:T(8,128)(2,1)S(1)}, bf16[1024,128]{1,0:T(8,128)(2,1)S(1)}, u32[]{:S(2)}, u32[]{:S(2)}) collective-permute-start(bf16[1024,128]{1,0:T(8,128)(2,1)S(1)} %step3_kernel.1.q_prev), channel_id=1, source_target_pairs={{0,1},{1,0},{2,3},{3,2},{4,5},{5,4},{6,14},{7,6},{8,9},{9,8},{10,1... | collective-permute-start | bytes 786440 | tf_op jit(solution)/shard_map/ppermute | solution.py:117
  51.4 2.6 %collective-permute-done.20.refs_4_ = bf16[1024,128]{1,0:T(8,128)(2,1)S(1)} collective-permute-done((bf16[1024,128]{1,0:T(8,128)(2,1)S(1)}, bf16[1024,128]{1,0:T(8,128)(2,1)S(1)}, u32[]{:S(2)}, u32[]{:S(2)}) %collective-permute-start.20) | collective-permute-done | bytes 262176 | tf_op jit(solution)/shard_map/ppermute | solution.py:117
  54.1 6.4 %collective-permute-done.22.refs_2_ = bf16[1040,128]{1,0:T(8,128)(2,1)S(1)} collective-permute-done((bf16[1040,128]{1,0:T(8,128)(2,1)S(1)}, bf16[1040,128]{1,0:T(8,128)(2,1)S(1)}, u32[]{:S(2)}, u32[]{:S(2)}) %collective-permute-start.22) | collective-permute-done | bytes 266272 | tf_op jit(solution)/shard_map/ppermute | solution.py:117
  60.5 5.7 %collective-permute-start.23 = (bf16[1040,128]{1,0:T(8,128)(2,1)S(1)}, bf16[1040,128]{1,0:T(8,128)(2,1)S(1)}, u32[]{:S(2)}, u32[]{:S(2)}) collective-permute-start(bf16[1040,128]{1,0:T(8,128)(2,1)S(1)} %get-tuple-element.40.refs_0_), channel_id=1, source_target_pairs={{0,1},{1,0},{2,3},{3,2},{4,5},{5,4},{6,7},{7,6},{8,9},{9,8},{10,11... | collective-permute-start | bytes 798728 | tf_op jit(solution)/shard_map/ppermute | solution.py:117
  66.2 1.3 %collective-permute-start.21 = (bf16[1024,128]{1,0:T(8,128)(2,1)S(1)}, bf16[1024,128]{1,0:T(8,128)(2,1)S(1)}, u32[]{:S(2)}, u32[]{:S(2)}) collective-permute-start(bf16[1024,128]{1,0:T(8,128)(2,1)S(1)} %get-tuple-element.38.q_ref), channel_id=1, source_target_pairs={{15,11},{7,3},{10,2},{14,6}} | collective-permute-start | bytes 786440 | tf_op jit(solution)/shard_map/ppermute | solution.py:121
  67.5 7.0 %collective-permute-done.21.rest_ref = bf16[1024,128]{1,0:T(8,128)(2,1)S(1)} collective-permute-done((bf16[1024,128]{1,0:T(8,128)(2,1)S(1)}, bf16[1024,128]{1,0:T(8,128)(2,1)S(1)}, u32[]{:S(2)}, u32[]{:S(2)}) %collective-permute-start.21) | collective-permute-done | bytes 262176 | tf_op jit(solution)/shard_map/ppermute | solution.py:121
  74.5 1.4 %final_kernel.1 = (f32[1024,128]{1,0:T(8,128)}, f32[2,1024,128]{2,1,0:T(8,128)}) custom-call(f32[2,1024,128]{2,1,0:T(8,128)S(1)} %bitcast.14, bf16[1024,128]{1,0:T(8,128)(2,1)S(1)} %get-tuple-element.38.q_ref, bf16[1024,128]{1,0:T(8,128)(2,1)S(1)} %collective-permute-done.21.rest_ref, bf16[1040,128]{1,0:T(8,128)(2,1)S(1)} %get-tuple-element.40.refs_0_, ...), custom_call_target="tpu_custom_call" | custom-call | tf_op jit(solution)/shard_map/final_kernel/pallas_call | solution.py:144
  (44 shorter events, 3.1 us)
Async XLA Ops:
  2.0 7.6 %collective-permute-start.3 = (bf16[128,1024]{1,0:T(8,128)(2,1)S(1)}, bf16[128,1024]{1,0:T(8,128)(2,1)S(1)}, u32[]{:S(2)}, u32[]{:S(2)}) collective-permute-start(bf16[128,1024]{1,0:T(8,128)(2,1)S(1)} %get-tuple-element.26), channel_id=1, source_target_pairs={{0,8},{1,0},{2,10},{3,1},{4,5},{5,4},{6,7},{7,6},{8,16},{9,17},{10... | collective-permute-start | bytes 786440 | tf_op jit(solution)/shard_map/ppermute | solution.py:117
  2.1 7.5 %collective-permute-start.2 = (bf16[128,768]{1,0:T(8,128)(2,1)S(1)}, bf16[128,768]{1,0:T(8,128)(2,1)S(1)}, u32[]{:S(2)}, u32[]{:S(2)}) collective-permute-start(bf16[128,768]{1,0:T(8,128)(2,1)S(1)} %get-tuple-element.25), channel_id=1, source_target_pairs={{0,1},{1,17},{2,3},{3,11},{4,5},{5,4},{6,7},{7,6},{8,16},{9,8},{10... | collective-permute-start | bytes 589832 | tf_op jit(solution)/shard_map/ppermute | solution.py:117
  2.6 7.0 %collective-permute-start.1 = (bf16[128,512]{1,0:T(8,128)(2,1)S(1)}, bf16[128,512]{1,0:T(8,128)(2,1)S(1)}, u32[]{:S(2)}, u32[]{:S(2)}) collective-permute-start(bf16[128,512]{1,0:T(8,128)(2,1)S(1)} %get-tuple-element.24), channel_id=1, source_target_pairs={{0,8},{1,0},{2,10},{3,2},{4,5},{5,4},{6,7},{7,6},{8,11},{9,1},{10,... | collective-permute-start | bytes 393224 | tf_op jit(solution)/shard_map/ppermute | solution.py:117
  2.6 6.9 %collective-permute-start = (bf16[128,256]{1,0:T(8,128)(2,1)S(1)}, bf16[128,256]{1,0:T(8,128)(2,1)S(1)}, u32[]{:S(2)}, u32[]{:S(2)}) collective-permute-start(bf16[128,256]{1,0:T(8,128)(2,1)S(1)} %get-tuple-element.23), channel_id=1, source_target_pairs={{0,13},{1,5},{2,22},{3,15},{4,1},{5,9},{6,14},{7,23},{8,0},{9,8},{... | collective-permute-start | bytes 196616 | tf_op jit(solution)/shard_map/ppermute | solution.py:117
  9.6 12.9 %collective-permute-start.10 = (bf16[128,2560]{1,0:T(8,128)(2,1)S(1)}, bf16[128,2560]{1,0:T(8,128)(2,1)S(1)}, u32[]{:S(2)}, u32[]{:S(2)}) collective-permute-start(bf16[128,2560]{1,0:T(8,128)(2,1)S(1)} %pack_kernel.1), channel_id=1, source_target_pairs={{0,1},{1,0},{2,3},{3,2},{4,5},{5,4},{6,7},{7,6},{8,12},{9,8},{10,1... | collective-permute-start | bytes 1966088 | tf_op jit(solution)/shard_map/ppermute | solution.py:117
  9.8 10.2 %collective-permute-start.4 = (bf16[256,128]{1,0:T(8,128)(2,1)S(1)}, bf16[256,128]{1,0:T(8,128)(2,1)S(1)}, u32[]{:S(2)}, u32[]{:S(2)}) collective-permute-start(bf16[256,128]{1,0:T(8,128)(2,1)S(1)} %first_kernel.1), channel_id=1, source_target_pairs={{0,4},{1,8},{2,12},{3,2},{4,0},{5,1},{6,7},{7,6},{8,9},{9,3},{10,1... | collective-permute-start | bytes 196616 | tf_op jit(solution)/shard_map/ppermute | solution.py:117
  10.4 11.1 %collective-permute-start.5 = (bf16[256,128]{1,0:T(8,128)(2,1)S(1)}, bf16[256,128]{1,0:T(8,128)(2,1)S(1)}, u32[]{:S(2)}, u32[]{:S(2)}) collective-permute-start(bf16[256,128]{1,0:T(8,128)(2,1)S(1)} %first_kernel.1), channel_id=1, source_target_pairs={{0,8},{1,12},{2,3},{3,4},{4,0},{5,7},{6,2},{7,6},{8,9},{9,1},{10,1... | collective-permute-start | bytes 196616 | tf_op jit(solution)/shard_map/ppermute | solution.py:117
  19.5 2.5 %collective-permute-start.6 = (bf16[256,128]{1,0:T(8,128)(2,1)S(1)}, bf16[256,128]{1,0:T(8,128)(2,1)S(1)}, u32[]{:S(2)}, u32[]{:S(2)}) collective-permute-start(bf16[256,128]{1,0:T(8,128)(2,1)S(1)} %first_kernel.1), channel_id=1, source_target_pairs={{0,12},{1,3},{2,4},{3,8},{4,0},{5,7},{6,2},{7,6},{8,9},{9,1},{10,1... | collective-permute-start | bytes 196616 | tf_op jit(solution)/shard_map/ppermute | solution.py:117
  19.6 2.5 %collective-permute-start.7 = (bf16[256,128]{1,0:T(8,128)(2,1)S(1)}, bf16[256,128]{1,0:T(8,128)(2,1)S(1)}, u32[]{:S(2)}, u32[]{:S(2)}) collective-permute-start(bf16[256,128]{1,0:T(8,128)(2,1)S(1)} %first_kernel.1), channel_id=1, source_target_pairs={{0,2},{1,4},{2,8},{3,12},{4,0},{5,3},{6,7},{7,6},{8,9},{9,1},{10,1... | collective-permute-start | bytes 196616 | tf_op jit(solution)/shard_map/ppermute | solution.py:117
  22.1 1.9 %collective-permute-start.9 = (bf16[1024,128]{1,0:T(8,128)(2,1)S(1)}, bf16[1024,128]{1,0:T(8,128)(2,1)S(1)}, u32[]{:S(2)}, u32[]{:S(2)}) collective-permute-start(bf16[1024,128]{1,0:T(8,128)(2,1)S(1)} %get-tuple-element.28.s_prev), channel_id=1, source_target_pairs={{0,1},{1,0},{2,3},{3,2},{4,5},{5,4},{6,7},{7,6},{8,9},{9,8},{10,11... | collective-permute-start | bytes 786440 | tf_op jit(solution)/shard_map/ppermute | solution.py:117
  24.0 1.6 %collective-permute-start.11 = (bf16[1024,128]{1,0:T(8,128)(2,1)S(1)}, bf16[1024,128]{1,0:T(8,128)(2,1)S(1)}, u32[]{:S(2)}, u32[]{:S(2)}) collective-permute-start(bf16[1024,128]{1,0:T(8,128)(2,1)S(1)} %get-tuple-element.30), channel_id=1, source_target_pairs={{0,1},{1,0},{2,3},{3,2},{4,5},{5,4},{6,7},{7,6},{8,9},{9,14},{10,8... | collective-permute-start | bytes 786440 | tf_op jit(solution)/shard_map/ppermute | solution.py:117
  24.2 1.8 %collective-permute-start.12 = (bf16[1024,128]{1,0:T(8,128)(2,1)S(1)}, bf16[1024,128]{1,0:T(8,128)(2,1)S(1)}, u32[]{:S(2)}, u32[]{:S(2)}) collective-permute-start(bf16[1024,128]{1,0:T(8,128)(2,1)S(1)} %get-tuple-element.37.q_prev), channel_id=1, source_target_pairs={{0,1},{1,0},{2,3},{3,2},{4,5},{5,4},{6,7},{7,6},{8,9},{9,13},{10,1... | collective-permute-start | bytes 786440 | tf_op jit(solution)/shard_map/ppermute | solution.py:117
  26.0 1.6 %collective-permute-start.13 = (bf16[1024,128]{1,0:T(8,128)(2,1)S(1)}, bf16[1024,128]{1,0:T(8,128)(2,1)S(1)}, u32[]{:S(2)}, u32[]{:S(2)}) collective-permute-start(bf16[1024,128]{1,0:T(8,128)(2,1)S(1)} %get-tuple-element.35), channel_id=1, source_target_pairs={{0,1},{1,0},{2,3},{3,2},{4,5},{5,4},{6,7},{7,6},{8,9},{9,8},{10,11... | collective-permute-start | bytes 786440 | tf_op jit(solution)/shard_map/ppermute | solution.py:117
  26.2 1.8 %collective-permute-start.14 = (bf16[1024,128]{1,0:T(8,128)(2,1)S(1)}, bf16[1024,128]{1,0:T(8,128)(2,1)S(1)}, u32[]{:S(2)}, u32[]{:S(2)}) collective-permute-start(bf16[1024,128]{1,0:T(8,128)(2,1)S(1)} %get-tuple-element.34.s_ref), channel_id=1, source_target_pairs={{0,1},{1,0},{2,3},{3,2},{4,5},{5,4},{6,7},{7,6},{8,9},{9,8},{10,11... | collective-permute-start | bytes 786440 | tf_op jit(solution)/shard_map/ppermute | solution.py:117
  26.6 1.8 %collective-permute-start.15 = (bf16[1024,128]{1,0:T(8,128)(2,1)S(1)}, bf16[1024,128]{1,0:T(8,128)(2,1)S(1)}, u32[]{:S(2)}, u32[]{:S(2)}) collective-permute-start(bf16[1024,128]{1,0:T(8,128)(2,1)S(1)} %get-tuple-element.37.q_prev), channel_id=1, source_target_pairs={{0,1},{1,5},{2,3},{3,2},{4,0},{5,4},{6,7},{7,6},{8,16},{9,17},{10,... | collective-permute-start | bytes 786440 | tf_op jit(solution)/shard_map/ppermute | solution.py:117
  28.4 22.9 %collective-permute-start.16 = (bf16[1024,128]{1,0:T(8,128)(2,1)S(1)}, bf16[1024,128]{1,0:T(8,128)(2,1)S(1)}, u32[]{:S(2)}, u32[]{:S(2)}) collective-permute-start(bf16[1024,128]{1,0:T(8,128)(2,1)S(1)} %step3_kernel.1.q_prev), channel_id=1, source_target_pairs={{0,8},{1,0},{2,3},{3,2},{4,5},{5,4},{6,7},{7,6},{8,9},{9,1},{10,11... | collective-permute-start | bytes 786440 | tf_op jit(solution)/shard_map/ppermute | solution.py:117
  28.6 22.7 %collective-permute-start.17 = (bf16[1024,128]{1,0:T(8,128)(2,1)S(1)}, bf16[1024,128]{1,0:T(8,128)(2,1)S(1)}, u32[]{:S(2)}, u32[]{:S(2)}) collective-permute-start(bf16[1024,128]{1,0:T(8,128)(2,1)S(1)} %step3_kernel.1.q_prev), channel_id=1, source_target_pairs={{0,1},{1,0},{2,3},{3,2},{4,12},{5,4},{6,7},{7,6},{8,9},{9,8},{10,1... | collective-permute-start | bytes 786440 | tf_op jit(solution)/shard_map/ppermute | solution.py:117
  29.0 22.4 %collective-permute-start.18 = (bf16[1024,128]{1,0:T(8,128)(2,1)S(1)}, bf16[1024,128]{1,0:T(8,128)(2,1)S(1)}, u32[]{:S(2)}, u32[]{:S(2)}) collective-permute-start(bf16[1024,128]{1,0:T(8,128)(2,1)S(1)} %step3_kernel.1.q_prev), channel_id=1, source_target_pairs={{0,1},{1,0},{2,3},{3,2},{4,5},{5,4},{6,7},{7,6},{8,9},{9,8},{10,11... | collective-permute-start | bytes 786440 | tf_op jit(solution)/shard_map/ppermute | solution.py:117
  29.1 22.3 %collective-permute-start.19 = (bf16[1024,128]{1,0:T(8,128)(2,1)S(1)}, bf16[1024,128]{1,0:T(8,128)(2,1)S(1)}, u32[]{:S(2)}, u32[]{:S(2)}) collective-permute-start(bf16[1024,128]{1,0:T(8,128)(2,1)S(1)} %step3_kernel.1.q_prev), channel_id=1, source_target_pairs={{0,1},{1,0},{2,3},{3,2},{4,5},{5,4},{6,7},{7,6},{8,9},{9,8},{10,11... | collective-permute-start | bytes 786440 | tf_op jit(solution)/shard_map/ppermute | solution.py:117
  29.5 24.4 %collective-permute-start.20 = (bf16[1024,128]{1,0:T(8,128)(2,1)S(1)}, bf16[1024,128]{1,0:T(8,128)(2,1)S(1)}, u32[]{:S(2)}, u32[]{:S(2)}) collective-permute-start(bf16[1024,128]{1,0:T(8,128)(2,1)S(1)} %step3_kernel.1.q_prev), channel_id=1, source_target_pairs={{0,1},{1,0},{2,3},{3,2},{4,5},{5,4},{6,14},{7,6},{8,9},{9,8},{10,1... | collective-permute-start | bytes 786440 | tf_op jit(solution)/shard_map/ppermute | solution.py:117
  54.0 6.5 %collective-permute-start.22 = (bf16[1040,128]{1,0:T(8,128)(2,1)S(1)}, bf16[1040,128]{1,0:T(8,128)(2,1)S(1)}, u32[]{:S(2)}, u32[]{:S(2)}) collective-permute-start(bf16[1040,128]{1,0:T(8,128)(2,1)S(1)} %get-tuple-element.40.refs_0_), channel_id=1, source_target_pairs={{0,2},{1,3},{2,0},{3,1},{4,6},{5,7},{6,4},{7,5},{8,10},{9,11},{10,... | collective-permute-start | bytes 798728 | tf_op jit(solution)/shard_map/ppermute | solution.py:117
  60.5 14.0 %collective-permute-start.23 = (bf16[1040,128]{1,0:T(8,128)(2,1)S(1)}, bf16[1040,128]{1,0:T(8,128)(2,1)S(1)}, u32[]{:S(2)}, u32[]{:S(2)}) collective-permute-start(bf16[1040,128]{1,0:T(8,128)(2,1)S(1)} %get-tuple-element.40.refs_0_), channel_id=1, source_target_pairs={{0,1},{1,0},{2,3},{3,2},{4,5},{5,4},{6,7},{7,6},{8,9},{9,8},{10,11... | collective-permute-start | bytes 798728 | tf_op jit(solution)/shard_map/ppermute | solution.py:117
  66.2 8.3 %collective-permute-start.24 = (bf16[1040,128]{1,0:T(8,128)(2,1)S(1)}, bf16[1040,128]{1,0:T(8,128)(2,1)S(1)}, u32[]{:S(2)}, u32[]{:S(2)}) collective-permute-start(bf16[1040,128]{1,0:T(8,128)(2,1)S(1)} %collective-permute-done.22.refs_2_), channel_id=1, source_target_pairs={{0,1},{1,0},{2,3},{3,2},{4,5},{5,4},{6,7},{7,6},{8,9},{9,8},{10,11... | collective-permute-start | bytes 798728 | tf_op jit(solution)/shard_map/ppermute | solution.py:117
  66.2 8.3 %collective-permute-start.21 = (bf16[1024,128]{1,0:T(8,128)(2,1)S(1)}, bf16[1024,128]{1,0:T(8,128)(2,1)S(1)}, u32[]{:S(2)}, u32[]{:S(2)}) collective-permute-start(bf16[1024,128]{1,0:T(8,128)(2,1)S(1)} %get-tuple-element.38.q_ref), channel_id=1, source_target_pairs={{15,11},{7,3},{10,2},{14,6}} | collective-permute-start | bytes 786440 | tf_op jit(solution)/shard_map/ppermute | solution.py:121
  (5 other events, 39.8 us)

commit v8 on v7

--- a/solution.py
+++ b/solution.py
@@ -73,7 +73,9 @@
 
 def hops(a, b):
     d = a ^ b
-    return 4 * (abs((a >> 3) - (b >> 3)) + ((d >> 2) & 1) + ((d >> 1) & 1)) + (d & 1) if d else 1000
+    if d < 2:
+        return 1 if d else 10000
+    return 100 + abs((a >> 3) - (b >> 3)) + ((d >> 2) & 1) + ((d >> 1) & 1)
 
 
 def complete(pairs):
@@ -422,7 +424,7 @@
                 pairs.append(((odd, k), maker))
             if maker[0] != even:
                 pairs.append(((even, k ^ 1), PARTNER[k]))
-        parts.append(send(cut, pairs))
+        parts.append(send_only(cut, pairs))
     q = call(
         first_kernel,
         jax.ShapeDtypeStruct((2 * part, width), bf16),
@@ -470,6 +472,7 @@
     a, q, s = call(step2_kernel, [vec] * 3, [p_in, q_in, sums, rhs, diag, block, q, s], [VMEM] * 8, [VMEM] * 3)
     sums = send(s, [(MAKER[2], MAKER[3])])
     a = send(a, [(BESIDE, MAKER[3])])
+
     q = call(
         functools.partial(step3_kernel, took),
         vec,
@@ -479,16 +482,19 @@
         [pltpu.VMEM((size, width), bf16)],
     )
 
-    makers = [(MAKER[3], (r, 3)) for r in (4, 7, 6, 3, 1)]
-    second = [(MAKER[2], (r, 2)) for r in (4, 5, 6, 7, 2)]
-    others = [
-        [((4, 0), (6, 0)), ((5, 0), (7, 0)), ((4, 1), (6, 1)), ((3, 1), (5, 1)), ((2, 1), (0, 1))],
-        [((4, 1), (7, 1)), ((3, 1), (1, 1))],
+    sends = [
+        [(MAKER[3], (4, 3)), ((4, 0), (6, 0)), ((5, 0), (7, 0)), ((4, 1), (6, 1)), ((3, 1), (5, 1)), ((2, 1), (0, 1))],
+        [(MAKER[3], (7, 3)), ((4, 1), (7, 1)), ((3, 1), (1, 1))],
+        [(MAKER[3], (6, 3))],
+        [(MAKER[3], (3, 3))],
+        [(MAKER[3], (1, 3))],
     ]
-    sends = [[makers[i], second[i], *(others[i] if i < 2 else [])] for i in range(5)]
-    got = [send(q, pairs) for pairs in sends]
+    for pairs, r in zip(sends, (4, 5, 6, 7, 2)):
+        pairs.append((MAKER[2], (r, 2)))
+    got = [send_only(q, pairs) for pairs in sends]
+    takers = [[b for _, b in pairs] for pairs in sends]
     q, mine = call(
-        functools.partial(update_kernel, [[b for _, b in pairs] for pairs in sends]),
+        functools.partial(update_kernel, takers),
         [vec, jax.ShapeDtypeStruct((size + TAIL, width), bf16)],
         [block_rows, counts, s, block, q, *got],
         [SMEM] * 2 + [VMEM] * (3 + len(got)),
@@ -498,7 +504,7 @@
     def swap(value, step):
         return send(value, [((r, c), (r, c ^ step)) for r in range(NR) for c in range(NC)])
 
-    rest = send_only(q, [(a, b) for a, b in zip(((3, 3), (1, 3), (2, 2), MAKER[2]), REST)])
+    rest = send_only(q, list(zip(((3, 3), (1, 3), (2, 2), MAKER[2]), REST)))
     across = swap(mine, 2)
     mine_after, across = lax.optimization_barrier((mine, across))
     beside = swap(mine_after, 1)

time: 76.1 us -> 76 us (level)
  waiting for transfers between devices: 24.6 us -> 19.3 us
  starting transfers between devices: 46.1 us -> 51.1 us
    ppermute x1 -> x10, starting transfers between devices: 1.28 us -> 11.7 us  [send_only(): lax.ppermute(value, ('row', 'col'), [(a * NC + b, c * NC + d) for (a, b),...]
    ppermute x24 -> x15, waiting for transfers between devices: 17.6 us -> 9.98 us  [send(): lax.ppermute(value, ('row', 'col'), [(a * NC + b, c * NC + d) for (a, b),...]
    ppermute x24 -> x15, starting transfers between devices: 44.8 us -> 39.4 us  [send(): lax.ppermute(value, ('row', 'col'), [(a * NC + b, c * NC + d) for (a, b),...]
    ppermute x1 -> x10, waiting for transfers between devices: 6.97 us -> 9.34 us  [send_only(): lax.ppermute(value, ('row', 'col'), [(a * NC + b, c * NC + d) for (a, b),...]
  transfers between devices with their start and end apart: 25 -> 25, of which waited for: 13 -> 14; matrix products, arithmetic and copies ran while one was open for 0% -> 0% of each run, Pallas kernels for 0% -> 0%
where the time goes in v8:
time: 76 us; the launch traced here: 75.7 us
  starting transfers between devices  51.1 us (67%)
  waiting for transfers between devices  19.3 us (25%)
  between operations  2.16 us (3%)
  Pallas kernels  1.86 us (2%)
  local copies, waits for them, and re-layouts  1.32 us (2%)
    ppermute x15, starting transfers between devices, send(): lax.ppermute(value, ('row', 'col'), [(a * NC + b, c * NC + d) for (a, b),...  39.4 us
    ppermute x10, starting transfers between devices, send_only(): lax.ppermute(value, ('row', 'col'), [(a * NC + b, c * NC + d) for (a, b),...  11.7 us
    ppermute x15, waiting for transfers between devices, send(): lax.ppermute(value, ('row', 'col'), [(a * NC + b, c * NC + d) for (a, b),...  9.98 us
    ppermute x10, waiting for transfers between devices, send_only(): lax.ppermute(value, ('row', 'col'), [(a * NC + b, c * NC + d) for (a, b),...  9.34 us
    pallas_call x10, Pallas kernels, call(): pl.pallas_call(kernel, out_shape=outs, in_specs=in_specs, out_specs=out_s...  1.86 us
  transfers between devices with their start and end apart: 25, of which 14 were waited for; matrix products, arithmetic and copies ran while one was open for 0% of the time, Pallas kernels for 0%

profile of v8, /device:TPU:6, one launch (start us, length us, event | category | flops | bytes accessed | tf_op | source)
XLA Modules:
  0.0 75.7 jit_solution(18383459839882404700)
XLA Ops:
  0.6 1.3 %copy-done.2 = bf16[4,128,1024]{2,1,0:T(8,128)(2,1)S(1)} copy-done((bf16[4,128,1024]{2,1,0:T(8,128)(2,1)S(1)}, bf16[4,128,1024]{2,1,0:T(8,128)(2,1)}, u32[]{:S(2)}) %copy-start.2) | copy-done | bytes 1048600
  2.0 0.8 %collective-permute-start.3 = (bf16[128,1024]{1,0:T(8,128)(2,1)S(1)}, bf16[128,1024]{1,0:T(8,128)(2,1)S(1)}, u32[]{:S(2)}, u32[]{:S(2)}) collective-permute-start(bf16[128,1024]{1,0:T(8,128)(2,1)S(1)} %get-tuple-element.26), channel_id=1, source_target_pairs={{28,3},{25,2},{29,9},{24,13},{30,14},{27,15},{31,23},{26,22}} | collective-permute-start | bytes 786440 | tf_op jit(solution)/shard_map/ppermute | solution.py:123
  2.8 0.8 %collective-permute-start.2 = (bf16[128,768]{1,0:T(8,128)(2,1)S(1)}, bf16[128,768]{1,0:T(8,128)(2,1)S(1)}, u32[]{:S(2)}, u32[]{:S(2)}) collective-permute-start(bf16[128,768]{1,0:T(8,128)(2,1)S(1)} %get-tuple-element.25), channel_id=1, source_target_pairs={{20,2},{17,0},{21,9},{16,13},{22,14},{19,15},{18,22}} | collective-permute-start | bytes 589832 | tf_op jit(solution)/shard_map/ppermute | solution.py:123
  3.6 0.7 collective-permute-start.1
  4.3 4.7 %collective-permute-start = (bf16[128,256]{1,0:T(8,128)(2,1)S(1)}, bf16[128,256]{1,0:T(8,128)(2,1)S(1)}, u32[]{:S(2)}, u32[]{:S(2)}) collective-permute-start(bf16[128,256]{1,0:T(8,128)(2,1)S(1)} %get-tuple-element.23), channel_id=1, source_target_pairs={{4,1},{5,9},{0,13},{6,14},{3,15},{7,23},{2,22}} | collective-permute-start | bytes 196616 | tf_op jit(solution)/shard_map/ppermute | solution.py:123
  9.0 2.4 %collective-permute-done.refs_0_ = bf16[128,256]{1,0:T(8,128)(2,1)S(1)} collective-permute-done((bf16[128,256]{1,0:T(8,128)(2,1)S(1)}, bf16[128,256]{1,0:T(8,128)(2,1)S(1)}, u32[]{:S(2)}, u32[]{:S(2)}) %collective-permute-start) | collective-permute-done | bytes 65568 | tf_op jit(solution)/shard_map/ppermute | solution.py:123
  11.6 0.6 collective-permute-start.4
  12.3 0.4 collective-permute-start.6
  12.8 0.9 %collective-permute-done.4.g0 = bf16[256,128]{1,0:T(8,128)(2,1)S(1)} collective-permute-done((bf16[256,128]{1,0:T(8,128)(2,1)S(1)}, bf16[256,128]{1,0:T(8,128)(2,1)S(1)}, u32[]{:S(2)}, u32[]{:S(2)}) %collective-permute-start.4) | collective-permute-done | bytes 65568 | tf_op jit(solution)/shard_map/ppermute | solution.py:119
  14.6 0.9 %collective-permute-done.8.p_in = bf16[1024,128]{1,0:T(8,128)(2,1)S(1)} collective-permute-done((bf16[1024,128]{1,0:T(8,128)(2,1)S(1)}, bf16[1024,128]{1,0:T(8,128)(2,1)S(1)}, u32[]{:S(2)}, u32[]{:S(2)}) %collective-permute-start.8) | collective-permute-done | bytes 262176 | tf_op jit(solution)/shard_map/ppermute | solution.py:119
  16.6 1.0 %collective-permute-done.11.p_in = bf16[1024,128]{1,0:T(8,128)(2,1)S(1)} collective-permute-done((bf16[1024,128]{1,0:T(8,128)(2,1)S(1)}, bf16[1024,128]{1,0:T(8,128)(2,1)S(1)}, u32[]{:S(2)}, u32[]{:S(2)}) %collective-permute-start.11) | collective-permute-done | bytes 262176 | tf_op jit(solution)/shard_map/ppermute | solution.py:119
  18.7 0.9 %collective-permute-done.13.a_ref = bf16[1024,128]{1,0:T(8,128)(2,1)S(1)} collective-permute-done((bf16[1024,128]{1,0:T(8,128)(2,1)S(1)}, bf16[1024,128]{1,0:T(8,128)(2,1)S(1)}, u32[]{:S(2)}, u32[]{:S(2)}) %collective-permute-start.13) | collective-permute-done | bytes 262176 | tf_op jit(solution)/shard_map/ppermute | solution.py:119
  20.0 0.4 collective-permute-done.15.came_ref
  20.4 0.7 collective-permute-start.16
  21.0 0.7 collective-permute-start.17
  21.7 0.7 collective-permute-start.18
  22.4 0.7 collective-permute-start.19
  23.1 0.7 collective-permute-start.20
  25.3 19.1 %collective-permute-start.22 = (bf16[1040,128]{1,0:T(8,128)(2,1)S(1)}, bf16[1040,128]{1,0:T(8,128)(2,1)S(1)}, u32[]{:S(2)}, u32[]{:S(2)}) collective-permute-start(bf16[1040,128]{1,0:T(8,128)(2,1)S(1)} %get-tuple-element.40.refs_0_), channel_id=1, source_target_pairs={{0,2},{1,3},{2,0},{3,1},{4,6},{5,7},{6,4},{7,5},{8,10},{9,11},{10,... | collective-permute-start | bytes 798728 | tf_op jit(solution)/shard_map/ppermute | solution.py:119
  44.4 4.4 %collective-permute-done.22.refs_2_ = bf16[1040,128]{1,0:T(8,128)(2,1)S(1)} collective-permute-done((bf16[1040,128]{1,0:T(8,128)(2,1)S(1)}, bf16[1040,128]{1,0:T(8,128)(2,1)S(1)}, u32[]{:S(2)}, u32[]{:S(2)}) %collective-permute-start.22) | collective-permute-done | bytes 266272 | tf_op jit(solution)/shard_map/ppermute | solution.py:119
  48.8 17.3 %collective-permute-start.23 = (bf16[1040,128]{1,0:T(8,128)(2,1)S(1)}, bf16[1040,128]{1,0:T(8,128)(2,1)S(1)}, u32[]{:S(2)}, u32[]{:S(2)}) collective-permute-start(bf16[1040,128]{1,0:T(8,128)(2,1)S(1)} %get-tuple-element.40.refs_0_), channel_id=1, source_target_pairs={{0,1},{1,0},{2,3},{3,2},{4,5},{5,4},{6,7},{7,6},{8,9},{9,8},{10,11... | collective-permute-start | bytes 798728 | tf_op jit(solution)/shard_map/ppermute | solution.py:119
  66.0 1.3 %collective-permute-start.21 = (bf16[1024,128]{1,0:T(8,128)(2,1)S(1)}, bf16[1024,128]{1,0:T(8,128)(2,1)S(1)}, u32[]{:S(2)}, u32[]{:S(2)}) collective-permute-start(bf16[1024,128]{1,0:T(8,128)(2,1)S(1)} %get-tuple-element.38.q_ref), channel_id=1, source_target_pairs={{15,11},{7,3},{10,2},{14,6}} | collective-permute-start | bytes 786440 | tf_op jit(solution)/shard_map/ppermute | solution.py:123
  67.3 7.0 %collective-permute-done.21.rest_ref = bf16[1024,128]{1,0:T(8,128)(2,1)S(1)} collective-permute-done((bf16[1024,128]{1,0:T(8,128)(2,1)S(1)}, bf16[1024,128]{1,0:T(8,128)(2,1)S(1)}, u32[]{:S(2)}, u32[]{:S(2)}) %collective-permute-start.21) | collective-permute-done | bytes 262176 | tf_op jit(solution)/shard_map/ppermute | solution.py:123
  74.3 1.4 %final_kernel.1 = (f32[1024,128]{1,0:T(8,128)}, f32[2,1024,128]{2,1,0:T(8,128)}) custom-call(f32[2,1024,128]{2,1,0:T(8,128)S(1)} %bitcast.14, bf16[1024,128]{1,0:T(8,128)(2,1)S(1)} %get-tuple-element.38.q_ref, bf16[1024,128]{1,0:T(8,128)(2,1)S(1)} %collective-permute-done.21.rest_ref, bf16[1040,128]{1,0:T(8,128)(2,1)S(1)} %get-tuple-element.40.refs_0_, ...), custom_call_target="tpu_custom_call" | custom-call | tf_op jit(solution)/shard_map/final_kernel/pallas_call | solution.py:146
  (44 shorter events, 3.9 us)
Async XLA Ops:
  2.0 9.4 %collective-permute-start.3 = (bf16[128,1024]{1,0:T(8,128)(2,1)S(1)}, bf16[128,1024]{1,0:T(8,128)(2,1)S(1)}, u32[]{:S(2)}, u32[]{:S(2)}) collective-permute-start(bf16[128,1024]{1,0:T(8,128)(2,1)S(1)} %get-tuple-element.26), channel_id=1, source_target_pairs={{28,3},{25,2},{29,9},{24,13},{30,14},{27,15},{31,23},{26,22}} | collective-permute-start | bytes 786440 | tf_op jit(solution)/shard_map/ppermute | solution.py:123
  2.8 8.6 %collective-permute-start.2 = (bf16[128,768]{1,0:T(8,128)(2,1)S(1)}, bf16[128,768]{1,0:T(8,128)(2,1)S(1)}, u32[]{:S(2)}, u32[]{:S(2)}) collective-permute-start(bf16[128,768]{1,0:T(8,128)(2,1)S(1)} %get-tuple-element.25), channel_id=1, source_target_pairs={{20,2},{17,0},{21,9},{16,13},{22,14},{19,15},{18,22}} | collective-permute-start | bytes 589832 | tf_op jit(solution)/shard_map/ppermute | solution.py:123
  3.6 7.8 %collective-permute-start.1 = (bf16[128,512]{1,0:T(8,128)(2,1)S(1)}, bf16[128,512]{1,0:T(8,128)(2,1)S(1)}, u32[]{:S(2)}, u32[]{:S(2)}) collective-permute-start(bf16[128,512]{1,0:T(8,128)(2,1)S(1)} %get-tuple-element.24), channel_id=1, source_target_pairs={{12,3},{9,1},{13,9},{11,15},{15,23},{10,22}} | collective-permute-start | bytes 393224 | tf_op jit(solution)/shard_map/ppermute | solution.py:123
  4.3 7.1 %collective-permute-start = (bf16[128,256]{1,0:T(8,128)(2,1)S(1)}, bf16[128,256]{1,0:T(8,128)(2,1)S(1)}, u32[]{:S(2)}, u32[]{:S(2)}) collective-permute-start(bf16[128,256]{1,0:T(8,128)(2,1)S(1)} %get-tuple-element.23), channel_id=1, source_target_pairs={{4,1},{5,9},{0,13},{6,14},{3,15},{7,23},{2,22}} | collective-permute-start | bytes 196616 | tf_op jit(solution)/shard_map/ppermute | solution.py:123
  11.5 3.1 %collective-permute-start.10 = (bf16[128,2560]{1,0:T(8,128)(2,1)S(1)}, bf16[128,2560]{1,0:T(8,128)(2,1)S(1)}, u32[]{:S(2)}, u32[]{:S(2)}) collective-permute-start(bf16[128,2560]{1,0:T(8,128)(2,1)S(1)} %pack_kernel.1), channel_id=1, source_target_pairs={{0,1},{1,0},{2,3},{3,2},{4,5},{5,4},{6,7},{7,6},{8,12},{9,8},{10,1... | collective-permute-start | bytes 1966088 | tf_op jit(solution)/shard_map/ppermute | solution.py:119
  11.6 2.1 %collective-permute-start.4 = (bf16[256,128]{1,0:T(8,128)(2,1)S(1)}, bf16[256,128]{1,0:T(8,128)(2,1)S(1)}, u32[]{:S(2)}, u32[]{:S(2)}) collective-permute-start(bf16[256,128]{1,0:T(8,128)(2,1)S(1)} %first_kernel.1), channel_id=1, source_target_pairs={{0,4},{1,8},{2,12},{3,2},{4,5},{5,0},{6,7},{7,6},{8,9},{9,1},{10,1... | collective-permute-start | bytes 196616 | tf_op jit(solution)/shard_map/ppermute | solution.py:119
  12.2 1.6 %collective-permute-start.5 = (bf16[256,128]{1,0:T(8,128)(2,1)S(1)}, bf16[256,128]{1,0:T(8,128)(2,1)S(1)}, u32[]{:S(2)}, u32[]{:S(2)}) collective-permute-start(bf16[256,128]{1,0:T(8,128)(2,1)S(1)} %first_kernel.1), channel_id=1, source_target_pairs={{0,8},{1,12},{2,3},{3,4},{4,5},{5,0},{6,7},{7,6},{8,9},{9,1},{10,1... | collective-permute-start | bytes 196616 | tf_op jit(solution)/shard_map/ppermute | solution.py:119
  12.3 1.6 %collective-permute-start.6 = (bf16[256,128]{1,0:T(8,128)(2,1)S(1)}, bf16[256,128]{1,0:T(8,128)(2,1)S(1)}, u32[]{:S(2)}, u32[]{:S(2)}) collective-permute-start(bf16[256,128]{1,0:T(8,128)(2,1)S(1)} %first_kernel.1), channel_id=1, source_target_pairs={{0,12},{1,0},{2,4},{3,8},{4,5},{5,1},{6,7},{7,6},{8,9},{9,2},{10,1... | collective-permute-start | bytes 196616 | tf_op jit(solution)/shard_map/ppermute | solution.py:119
  14.0 1.5 %collective-permute-start.8 = (bf16[1024,128]{1,0:T(8,128)(2,1)S(1)}, bf16[1024,128]{1,0:T(8,128)(2,1)S(1)}, u32[]{:S(2)}, u32[]{:S(2)}) collective-permute-start(bf16[1024,128]{1,0:T(8,128)(2,1)S(1)} %get-tuple-element.27), channel_id=1, source_target_pairs={{0,1},{1,0},{2,3},{3,2},{4,9},{5,4},{6,7},{7,6},{8,5},{9,8},{10,11... | collective-permute-start | bytes 786440 | tf_op jit(solution)/shard_map/ppermute | solution.py:119
  14.2 1.8 %collective-permute-start.9 = (bf16[1024,128]{1,0:T(8,128)(2,1)S(1)}, bf16[1024,128]{1,0:T(8,128)(2,1)S(1)}, u32[]{:S(2)}, u32[]{:S(2)}) collective-permute-start(bf16[1024,128]{1,0:T(8,128)(2,1)S(1)} %get-tuple-element.28.s_prev), channel_id=1, source_target_pairs={{0,1},{1,0},{2,3},{3,2},{4,5},{5,4},{6,7},{7,6},{8,9},{9,8},{10,11... | collective-permute-start | bytes 786440 | tf_op jit(solution)/shard_map/ppermute | solution.py:119
  16.0 1.6 %collective-permute-start.11 = (bf16[1024,128]{1,0:T(8,128)(2,1)S(1)}, bf16[1024,128]{1,0:T(8,128)(2,1)S(1)}, u32[]{:S(2)}, u32[]{:S(2)}) collective-permute-start(bf16[1024,128]{1,0:T(8,128)(2,1)S(1)} %get-tuple-element.30), channel_id=1, source_target_pairs={{0,1},{1,0},{2,3},{3,2},{4,5},{5,4},{6,7},{7,6},{8,9},{9,14},{10,1... | collective-permute-start | bytes 786440 | tf_op jit(solution)/shard_map/ppermute | solution.py:119
  16.2 1.8 %collective-permute-start.12 = (bf16[1024,128]{1,0:T(8,128)(2,1)S(1)}, bf16[1024,128]{1,0:T(8,128)(2,1)S(1)}, u32[]{:S(2)}, u32[]{:S(2)}) collective-permute-start(bf16[1024,128]{1,0:T(8,128)(2,1)S(1)} %get-tuple-element.37.q_prev), channel_id=1, source_target_pairs={{0,1},{1,0},{2,3},{3,2},{4,5},{5,4},{6,7},{7,6},{8,9},{9,13},{10,1... | collective-permute-start | bytes 786440 | tf_op jit(solution)/shard_map/ppermute | solution.py:119
  18.0 1.6 %collective-permute-start.13 = (bf16[1024,128]{1,0:T(8,128)(2,1)S(1)}, bf16[1024,128]{1,0:T(8,128)(2,1)S(1)}, u32[]{:S(2)}, u32[]{:S(2)}) collective-permute-start(bf16[1024,128]{1,0:T(8,128)(2,1)S(1)} %get-tuple-element.35), channel_id=1, source_target_pairs={{0,1},{1,0},{2,3},{3,2},{4,5},{5,4},{6,7},{7,6},{8,9},{9,8},{10,11... | collective-permute-start | bytes 786440 | tf_op jit(solution)/shard_map/ppermute | solution.py:119
  18.2 1.8 %collective-permute-start.14 = (bf16[1024,128]{1,0:T(8,128)(2,1)S(1)}, bf16[1024,128]{1,0:T(8,128)(2,1)S(1)}, u32[]{:S(2)}, u32[]{:S(2)}) collective-permute-start(bf16[1024,128]{1,0:T(8,128)(2,1)S(1)} %get-tuple-element.34.s_ref), channel_id=1, source_target_pairs={{0,1},{1,0},{2,3},{3,2},{4,5},{5,4},{6,7},{7,6},{8,9},{9,8},{10,11... | collective-permute-start | bytes 786440 | tf_op jit(solution)/shard_map/ppermute | solution.py:119
  18.6 1.8 %collective-permute-start.15 = (bf16[1024,128]{1,0:T(8,128)(2,1)S(1)}, bf16[1024,128]{1,0:T(8,128)(2,1)S(1)}, u32[]{:S(2)}, u32[]{:S(2)}) collective-permute-start(bf16[1024,128]{1,0:T(8,128)(2,1)S(1)} %get-tuple-element.37.q_prev), channel_id=1, source_target_pairs={{0,1},{1,5},{2,3},{3,2},{4,0},{5,4},{6,7},{7,6},{8,16},{9,17},{10,... | collective-permute-start | bytes 786440 | tf_op jit(solution)/shard_map/ppermute | solution.py:119
  20.4 4.7 %collective-permute-start.16 = (bf16[1024,128]{1,0:T(8,128)(2,1)S(1)}, bf16[1024,128]{1,0:T(8,128)(2,1)S(1)}, u32[]{:S(2)}, u32[]{:S(2)}) collective-permute-start(bf16[1024,128]{1,0:T(8,128)(2,1)S(1)} %step3_kernel.1.q_prev), channel_id=1, source_target_pairs={{23,19},{16,24},{20,28},{17,25},{13,21},{9,1},{14,18}} | collective-permute-start | bytes 786440 | tf_op jit(solution)/shard_map/ppermute | solution.py:123
  21.0 4.0 %collective-permute-start.17 = (bf16[1024,128]{1,0:T(8,128)(2,1)S(1)}, bf16[1024,128]{1,0:T(8,128)(2,1)S(1)}, u32[]{:S(2)}, u32[]{:S(2)}) collective-permute-start(bf16[1024,128]{1,0:T(8,128)(2,1)S(1)} %step3_kernel.1.q_prev), channel_id=1, source_target_pairs={{23,31},{17,29},{13,5},{14,22}} | collective-permute-start | bytes 786440 | tf_op jit(solution)/shard_map/ppermute | solution.py:123
  21.7 3.4 %collective-permute-start.18 = (bf16[1024,128]{1,0:T(8,128)(2,1)S(1)}, bf16[1024,128]{1,0:T(8,128)(2,1)S(1)}, u32[]{:S(2)}, u32[]{:S(2)}) collective-permute-start(bf16[1024,128]{1,0:T(8,128)(2,1)S(1)} %step3_kernel.1.q_prev), channel_id=1, source_target_pairs={{23,27},{14,26}} | collective-permute-start | bytes 786440 | tf_op jit(solution)/shard_map/ppermute | solution.py:123
  22.4 2.7 %collective-permute-start.19 = (bf16[1024,128]{1,0:T(8,128)(2,1)S(1)}, bf16[1024,128]{1,0:T(8,128)(2,1)S(1)}, u32[]{:S(2)}, u32[]{:S(2)}) collective-permute-start(bf16[1024,128]{1,0:T(8,128)(2,1)S(1)} %step3_kernel.1.q_prev), channel_id=1, source_target_pairs={{23,15},{14,30}} | collective-permute-start | bytes 786440 | tf_op jit(solution)/shard_map/ppermute | solution.py:123
  23.1 2.0 %collective-permute-start.20 = (bf16[1024,128]{1,0:T(8,128)(2,1)S(1)}, bf16[1024,128]{1,0:T(8,128)(2,1)S(1)}, u32[]{:S(2)}, u32[]{:S(2)}) collective-permute-start(bf16[1024,128]{1,0:T(8,128)(2,1)S(1)} %step3_kernel.1.q_prev), channel_id=1, source_target_pairs={{23,7},{14,10}} | collective-permute-start | bytes 786440 | tf_op jit(solution)/shard_map/ppermute | solution.py:123
  25.3 23.5 %collective-permute-start.22 = (bf16[1040,128]{1,0:T(8,128)(2,1)S(1)}, bf16[1040,128]{1,0:T(8,128)(2,1)S(1)}, u32[]{:S(2)}, u32[]{:S(2)}) collective-permute-start(bf16[1040,128]{1,0:T(8,128)(2,1)S(1)} %get-tuple-element.40.refs_0_), channel_id=1, source_target_pairs={{0,2},{1,3},{2,0},{3,1},{4,6},{5,7},{6,4},{7,5},{8,10},{9,11},{10,... | collective-permute-start | bytes 798728 | tf_op jit(solution)/shard_map/ppermute | solution.py:119
  48.8 25.5 %collective-permute-start.23 = (bf16[1040,128]{1,0:T(8,128)(2,1)S(1)}, bf16[1040,128]{1,0:T(8,128)(2,1)S(1)}, u32[]{:S(2)}, u32[]{:S(2)}) collective-permute-start(bf16[1040,128]{1,0:T(8,128)(2,1)S(1)} %get-tuple-element.40.refs_0_), channel_id=1, source_target_pairs={{0,1},{1,0},{2,3},{3,2},{4,5},{5,4},{6,7},{7,6},{8,9},{9,8},{10,11... | collective-permute-start | bytes 798728 | tf_op jit(solution)/shard_map/ppermute | solution.py:119
  66.0 8.3 %collective-permute-start.24 = (bf16[1040,128]{1,0:T(8,128)(2,1)S(1)}, bf16[1040,128]{1,0:T(8,128)(2,1)S(1)}, u32[]{:S(2)}, u32[]{:S(2)}) collective-permute-start(bf16[1040,128]{1,0:T(8,128)(2,1)S(1)} %collective-permute-done.22.refs_2_), channel_id=1, source_target_pairs={{0,1},{1,0},{2,3},{3,2},{4,5},{5,4},{6,7},{7,6},{8,9},{9,8},{10,11... | collective-permute-start | bytes 798728 | tf_op jit(solution)/shard_map/ppermute | solution.py:119
  66.0 8.3 %collective-permute-start.21 = (bf16[1024,128]{1,0:T(8,128)(2,1)S(1)}, bf16[1024,128]{1,0:T(8,128)(2,1)S(1)}, u32[]{:S(2)}, u32[]{:S(2)}) collective-permute-start(bf16[1024,128]{1,0:T(8,128)(2,1)S(1)} %get-tuple-element.38.q_ref), channel_id=1, source_target_pairs={{15,11},{7,3},{10,2},{14,6}} | collective-permute-start | bytes 786440 | tf_op jit(solution)/shard_map/ppermute | solution.py:123
  (5 other events, 35.2 us)

commit v9 on v8

--- a/solution.py
+++ b/solution.py
@@ -67,8 +67,18 @@
 FIRST = (1, 0)
 BESIDE = (3, 1)
 PARTNER = (None, (3, 1), (3, 3), (5, 2))
-PIECES = ((4, 0), (2, 1), (6, 5), (7, 3))
-REST = ((2, 3), (0, 3), (0, 2), (1, 2))
+PIECES = ((4, 0), (6, 2), (5, 1), (7, 3))
+SENDS = (
+    (1, 0, 3, 2),
+    (3, 1, 0, 2),
+    (0, 1, 3, 2),
+    (2, 1, 0, 3),
+    (0, 1, 3, 2),
+    (2, 3, 0, 1),
+    (0, 3, 1, 2),
+    (1, 2, 0, 3),
+)
+REST = ((2, 3), (3, 3), (0, 3), (1, 3), (0, 2), (1, 2))
 
 
 def hops(a, b):
@@ -162,7 +172,10 @@
     cuts, sem = refs[:-1], refs[-1]
     row, col = lax.axis_index("row"), lax.axis_index("col")
     part = diag_ref.shape[1]
-    k = jnp.where(lax.rem(row, 2) == 1, col, col + 1 - 2 * lax.rem(col, 2))
+    k = jnp.int32(0)
+    for r in range(NR):
+        for c in range(NC):
+            k = jnp.where((row == r) & (col == c), SENDS[r][c], k)
     for m in range(NR // 2):
 
         @pl.when(row // 2 == m)
@@ -379,19 +392,21 @@
     out_ref[pl.ds(size, TAIL)] = low(jnp.where(flag, 1.0, 0.0))
 
 
-def final_kernel(rhs_ref, q_ref, rest_ref, *refs):
-    sums, (solved_ref, out_ref) = refs[:NC], refs[NC:]
+def solved_kernel(q_ref, rest_ref, solved_ref):
+    came = any_of(REST)
+
+    @pl.when(came)
+    def _():
+        solved_ref[...] = rest_ref[...].astype(jnp.float32)
+
+    @pl.when(jnp.logical_not(came))
+    def _():
+        solved_ref[...] = q_ref[...].astype(jnp.float32)
+
+
+def final_kernel(rhs_ref, *refs):
+    sums, out_ref = refs[:NC], refs[NC]
     size = out_ref.shape[1]
-    came = any_of(REST)
-
-    @pl.when(came)
-    def _():
-        solved_ref[...] = rest_ref[...].astype(jnp.float32)
-
-    @pl.when(jnp.logical_not(came))
-    def _():
-        solved_ref[...] = q_ref[...].astype(jnp.float32)
-
     for i in range(out_ref.shape[0]):
         acc = rhs_ref[i]
         for s in sums:
@@ -413,17 +428,16 @@
     cuts = call(
         cut_kernel, [jax.ShapeDtypeStruct((part, w), bf16) for w in wides], [diag_inv], [HBM], [ANY] * len(wides), [dma]
     )
+    at_piece = {r: (0, c) for c, rows in enumerate(PIECES) for r in rows}
     parts = []
     for m, cut in enumerate(cuts):
-        even, odd = 2 * m, 2 * m + 1
-        at_piece = {r: (0, c) for c, rows in enumerate(PIECES) for r in rows}
-        pairs = [((odd, 0), at_piece[odd])] + ([((even, 1), at_piece[even])] if even else [])
-        for k in range(1, NC):
-            maker = MAKER[k]
-            if maker[0] != odd:
-                pairs.append(((odd, k), maker))
-            if maker[0] != even:
-                pairs.append(((even, k ^ 1), PARTNER[k]))
+        pairs = []
+        for r in (2 * m, 2 * m + 1):
+            for c, k in enumerate(SENDS[r]):
+                if k == 0 and r:
+                    pairs.append(((r, c), at_piece[r]))
+                if k and MAKER[k][0] != r:
+                    pairs.append(((r, c), MAKER[k] if r % 2 else PARTNER[k]))
         parts.append(send_only(cut, pairs))
     q = call(
         first_kernel,
@@ -470,8 +484,8 @@
     took = [(4, 0), (5, 0), (0, 0), (4, 1)]
 
     a, q, s = call(step2_kernel, [vec] * 3, [p_in, q_in, sums, rhs, diag, block, q, s], [VMEM] * 8, [VMEM] * 3)
-    sums = send(s, [(MAKER[2], MAKER[3])])
-    a = send(a, [(BESIDE, MAKER[3])])
+    sums = send_only(s, [(MAKER[2], MAKER[3])])
+    a = send_only(a, [(BESIDE, MAKER[3])])
 
     q = call(
         functools.partial(step3_kernel, took),
@@ -483,13 +497,13 @@
     )
 
     sends = [
-        [(MAKER[3], (4, 3)), ((4, 0), (6, 0)), ((5, 0), (7, 0)), ((4, 1), (6, 1)), ((3, 1), (5, 1)), ((2, 1), (0, 1))],
+        [(MAKER[3], (6, 3)), ((4, 0), (6, 0)), ((5, 0), (7, 0)), ((4, 1), (6, 1)), ((3, 1), (5, 1)), ((2, 1), (0, 1))],
         [(MAKER[3], (7, 3)), ((4, 1), (7, 1)), ((3, 1), (1, 1))],
-        [(MAKER[3], (6, 3))],
-        [(MAKER[3], (3, 3))],
-        [(MAKER[3], (1, 3))],
+        [(MAKER[3], (4, 3))],
+        [],
+        [],
     ]
-    for pairs, r in zip(sends, (4, 5, 6, 7, 2)):
+    for pairs, r in zip(sends, (4, 6, 7, 5, 2)):
         pairs.append((MAKER[2], (r, 2)))
     got = [send_only(q, pairs) for pairs in sends]
     takers = [[b for _, b in pairs] for pairs in sends]
@@ -504,17 +518,18 @@
     def swap(value, step):
         return send(value, [((r, c), (r, c ^ step)) for r in range(NR) for c in range(NC)])
 
-    rest = send_only(q, list(zip(((3, 3), (1, 3), (2, 2), MAKER[2]), REST)))
     across = swap(mine, 2)
-    mine_after, across = lax.optimization_barrier((mine, across))
-    beside = swap(mine_after, 1)
+    rest = send_only(q, list(zip(((4, 3), (5, 3), (6, 3), (7, 3), (2, 2), MAKER[2]), REST)))
+    solved = call(solved_kernel, jax.ShapeDtypeStruct((size, width), jnp.float32), [q, rest], [VMEM] * 2, VMEM)
+    beside, across, solved = lax.optimization_barrier((mine, across, solved))
+    beside = swap(beside, 1)
     corner = swap(across, 1)
-    solved, remainder = call(
+    remainder = call(
         final_kernel,
-        [jax.ShapeDtypeStruct((size, width), jnp.float32), jax.ShapeDtypeStruct(rhs.shape, jnp.float32)],
-        [rhs, q, rest, mine, beside, across, corner],
-        [VMEM] * 7,
-        [VMEM] * 2,
+        jax.ShapeDtypeStruct(rhs.shape, jnp.float32),
+        [rhs, mine, beside, across, corner],
+        [VMEM] * 5,
+        VMEM,
     )
     return solved[None, None], remainder[:, None]
 

time: 76 us -> 71.3 us (0.938)
  the two profiles are of different devices: /device:TPU:6 before, /device:TPU:7 now
where the time goes in v9:
time: 71.3 us; the launch traced here: 70.9 us
  starting transfers between devices  43.1 us (60%)
  waiting for transfers between devices  21.8 us (31%)
  Pallas kernels  2.62 us (4%)
  between operations  2.15 us (3%)
  local copies, waits for them, and re-layouts  1.32 us (2%)
    ppermute x13, starting transfers between devices, send(): lax.ppermute(value, ('row', 'col'), [(a * NC + b, c * NC + d) for (a, b),...  29.1 us
    ppermute x12, waiting for transfers between devices, send_only(): lax.ppermute(value, ('row', 'col'), [(a * NC + b, c * NC + d) for (a, b),...  15.5 us
    ppermute x12, starting transfers between devices, send_only(): lax.ppermute(value, ('row', 'col'), [(a * NC + b, c * NC + d) for (a, b),...  13.9 us
    ppermute x13, waiting for transfers between devices, send(): lax.ppermute(value, ('row', 'col'), [(a * NC + b, c * NC + d) for (a, b),...  6.24 us
    pallas_call x11, Pallas kernels, call(): pl.pallas_call(kernel, out_shape=outs, in_specs=in_specs, out_specs=out_s...  2.62 us
  transfers between devices with their start and end apart: 25, of which 13 were waited for; matrix products, arithmetic and copies ran while one was open for 0% of the time, Pallas kernels for 1%

profile of v9, /device:TPU:7, one launch (start us, length us, event | category | flops | bytes accessed | tf_op | source)
XLA Modules:
  0.0 70.9 jit_solution(985881137399385157)
XLA Ops:
  0.6 1.3 %copy-done.2 = bf16[4,128,1024]{2,1,0:T(8,128)(2,1)S(1)} copy-done((bf16[4,128,1024]{2,1,0:T(8,128)(2,1)S(1)}, bf16[4,128,1024]{2,1,0:T(8,128)(2,1)}, u32[]{:S(2)}) %copy-start.2) | copy-done | bytes 1048600
  2.0 0.8 %collective-permute-start.3 = (bf16[128,1024]{1,0:T(8,128)(2,1)S(1)}, bf16[128,1024]{1,0:T(8,128)(2,1)S(1)}, u32[]{:S(2)}, u32[]{:S(2)}) collective-permute-start(bf16[128,1024]{1,0:T(8,128)(2,1)S(1)} %get-tuple-element.25), channel_id=1, source_target_pairs={{24,1},{25,22},{26,13},{27,15},{28,9},{29,14},{30,3},{31,23}} | collective-permute-start | bytes 786440 | tf_op jit(solution)/shard_map/ppermute | solution.py:133
  2.8 0.8 %collective-permute-start.2 = (bf16[128,768]{1,0:T(8,128)(2,1)S(1)}, bf16[128,768]{1,0:T(8,128)(2,1)S(1)}, u32[]{:S(2)}, u32[]{:S(2)}) collective-permute-start(bf16[128,768]{1,0:T(8,128)(2,1)S(1)} %get-tuple-element.24), channel_id=1, source_target_pairs={{16,0},{17,13},{18,22},{19,15},{20,14},{22,2},{23,9}} | collective-permute-start | bytes 589832 | tf_op jit(solution)/shard_map/ppermute | solution.py:133
  3.6 0.7 collective-permute-start.1
  4.3 5.6 %collective-permute-start = (bf16[128,256]{1,0:T(8,128)(2,1)S(1)}, bf16[128,256]{1,0:T(8,128)(2,1)S(1)}, u32[]{:S(2)}, u32[]{:S(2)}) collective-permute-start(bf16[128,256]{1,0:T(8,128)(2,1)S(1)} %get-tuple-element.22), channel_id=1, source_target_pairs={{0,13},{2,22},{3,15},{4,23},{5,9},{6,2},{7,14}} | collective-permute-start | bytes 196616 | tf_op jit(solution)/shard_map/ppermute | solution.py:133
  9.9 1.3 %collective-permute-done.refs_0_ = bf16[128,256]{1,0:T(8,128)(2,1)S(1)} collective-permute-done((bf16[128,256]{1,0:T(8,128)(2,1)S(1)}, bf16[128,256]{1,0:T(8,128)(2,1)S(1)}, u32[]{:S(2)}, u32[]{:S(2)}) %collective-permute-start) | collective-permute-done | bytes 65568 | tf_op jit(solution)/shard_map/ppermute | solution.py:133
  11.3 4.6 %collective-permute-start.10 = (bf16[128,2560]{1,0:T(8,128)(2,1)S(1)}, bf16[128,2560]{1,0:T(8,128)(2,1)S(1)}, u32[]{:S(2)}, u32[]{:S(2)}) collective-permute-start(bf16[128,2560]{1,0:T(8,128)(2,1)S(1)} %pack_kernel.1), channel_id=1, source_target_pairs={{0,1},{1,0},{2,3},{3,2},{4,5},{5,4},{6,7},{7,6},{8,12},{9,8},{10,1... | collective-permute-start | bytes 1966088 | tf_op jit(solution)/shard_map/ppermute | solution.py:129
  17.1 0.7 collective-permute-done.4.g0
  18.6 0.9 %collective-permute-done.8.p_in = bf16[1024,128]{1,0:T(8,128)(2,1)S(1)} collective-permute-done((bf16[1024,128]{1,0:T(8,128)(2,1)S(1)}, bf16[1024,128]{1,0:T(8,128)(2,1)S(1)}, u32[]{:S(2)}, u32[]{:S(2)}) %collective-permute-start.8) | collective-permute-done | bytes 262176 | tf_op jit(solution)/shard_map/ppermute | solution.py:129
  20.6 1.0 %collective-permute-done.11.p_in = bf16[1024,128]{1,0:T(8,128)(2,1)S(1)} collective-permute-done((bf16[1024,128]{1,0:T(8,128)(2,1)S(1)}, bf16[1024,128]{1,0:T(8,128)(2,1)S(1)}, u32[]{:S(2)}, u32[]{:S(2)}) %collective-permute-start.11) | collective-permute-done | bytes 262176 | tf_op jit(solution)/shard_map/ppermute | solution.py:129
  22.0 0.7 collective-permute-start.13
  22.7 0.7 collective-permute-start.14
  23.8 1.2 %collective-permute-done.15.came_ref = bf16[1024,128]{1,0:T(8,128)(2,1)S(1)} collective-permute-done((bf16[1024,128]{1,0:T(8,128)(2,1)S(1)}, bf16[1024,128]{1,0:T(8,128)(2,1)S(1)}, u32[]{:S(2)}, u32[]{:S(2)}) %collective-permute-start.15) | collective-permute-done | bytes 262176 | tf_op jit(solution)/shard_map/ppermute | solution.py:129
  25.0 0.7 collective-permute-start.16
  25.7 0.7 collective-permute-start.17
  26.4 0.7 collective-permute-start.18
  27.1 0.7 collective-permute-start.19
  27.8 0.7 collective-permute-start.20
  29.9 21.4 %collective-permute-start.21 = (bf16[1040,128]{1,0:T(8,128)(2,1)S(1)}, bf16[1040,128]{1,0:T(8,128)(2,1)S(1)}, u32[]{:S(2)}, u32[]{:S(2)}) collective-permute-start(bf16[1040,128]{1,0:T(8,128)(2,1)S(1)} %get-tuple-element.40.refs_0_), channel_id=1, source_target_pairs={{0,2},{1,3},{2,0},{3,1},{4,6},{5,7},{6,4},{7,5},{8,10},{9,11},{10,... | collective-permute-start | bytes 798728 | tf_op jit(solution)/shard_map/ppermute | solution.py:129
  51.3 1.3 %collective-permute-start.22 = (bf16[1024,128]{1,0:T(8,128)(2,1)S(1)}, bf16[1024,128]{1,0:T(8,128)(2,1)S(1)}, u32[]{:S(2)}, u32[]{:S(2)}) collective-permute-start(bf16[1024,128]{1,0:T(8,128)(2,1)S(1)} %get-tuple-element.38.q_ref), channel_id=1, source_target_pairs={{19,11},{23,15},{27,3},{31,7},{10,2},{14,6}} | collective-permute-start | bytes 786440 | tf_op jit(solution)/shard_map/ppermute | solution.py:133
  52.6 14.2 %collective-permute-done.22.rest_ref = bf16[1024,128]{1,0:T(8,128)(2,1)S(1)} collective-permute-done((bf16[1024,128]{1,0:T(8,128)(2,1)S(1)}, bf16[1024,128]{1,0:T(8,128)(2,1)S(1)}, u32[]{:S(2)}, u32[]{:S(2)}) %collective-permute-start.22) | collective-permute-done | bytes 262176 | tf_op jit(solution)/shard_map/ppermute | solution.py:133
  66.8 0.8 %solved_kernel.1 = f32[1024,128]{1,0:T(8,128)} custom-call(bf16[1024,128]{1,0:T(8,128)(2,1)S(1)} %get-tuple-element.38.q_ref, bf16[1024,128]{1,0:T(8,128)(2,1)S(1)} %collective-permute-done.22.rest_ref), custom_call_target="tpu_custom_call" | custom-call | tf_op jit(solution)/shard_map/solved_kernel/pallas_call | solution.py:156
  68.1 1.0 %collective-permute-done.23.refs_1_ = bf16[1040,128]{1,0:T(8,128)(2,1)S(1)} collective-permute-done((bf16[1040,128]{1,0:T(8,128)(2,1)S(1)}, bf16[1040,128]{1,0:T(8,128)(2,1)S(1)}, u32[]{:S(2)}, u32[]{:S(2)}) %collective-permute-start.23) | collective-permute-done | bytes 266272 | tf_op jit(solution)/shard_map/ppermute | solution.py:129
  69.5 1.4 %final_kernel.1 = f32[2,1024,128]{2,1,0:T(8,128)} custom-call(f32[2,1024,128]{2,1,0:T(8,128)S(1)} %bitcast.14, bf16[1040,128]{1,0:T(8,128)(2,1)S(1)} %get-tuple-element.40.refs_0_, bf16[1040,128]{1,0:T(8,128)(2,1)S(1)} %collective-permute-done.23.refs_1_, bf16[1040,128]{1,0:T(8,128)(2,1)S(1)} %collective-permute-done.21.refs_2_, ...), custom_call_target="tpu_custom_call" | custom-call | tf_op jit(solution)/shard_map/final_kernel/pallas_call | solution.py:156
  (45 shorter events, 5.0 us)
Async XLA Ops:
  2.0 9.3 %collective-permute-start.3 = (bf16[128,1024]{1,0:T(8,128)(2,1)S(1)}, bf16[128,1024]{1,0:T(8,128)(2,1)S(1)}, u32[]{:S(2)}, u32[]{:S(2)}) collective-permute-start(bf16[128,1024]{1,0:T(8,128)(2,1)S(1)} %get-tuple-element.25), channel_id=1, source_target_pairs={{24,1},{25,22},{26,13},{27,15},{28,9},{29,14},{30,3},{31,23}} | collective-permute-start | bytes 786440 | tf_op jit(solution)/shard_map/ppermute | solution.py:133
  2.8 8.4 %collective-permute-start.2 = (bf16[128,768]{1,0:T(8,128)(2,1)S(1)}, bf16[128,768]{1,0:T(8,128)(2,1)S(1)}, u32[]{:S(2)}, u32[]{:S(2)}) collective-permute-start(bf16[128,768]{1,0:T(8,128)(2,1)S(1)} %get-tuple-element.24), channel_id=1, source_target_pairs={{16,0},{17,13},{18,22},{19,15},{20,14},{22,2},{23,9}} | collective-permute-start | bytes 589832 | tf_op jit(solution)/shard_map/ppermute | solution.py:133
  3.6 7.6 %collective-permute-start.1 = (bf16[128,512]{1,0:T(8,128)(2,1)S(1)}, bf16[128,512]{1,0:T(8,128)(2,1)S(1)}, u32[]{:S(2)}, u32[]{:S(2)}) collective-permute-start(bf16[128,512]{1,0:T(8,128)(2,1)S(1)} %get-tuple-element.23), channel_id=1, source_target_pairs={{8,1},{10,22},{11,15},{13,9},{14,3},{15,23}} | collective-permute-start | bytes 393224 | tf_op jit(solution)/shard_map/ppermute | solution.py:133
  4.3 6.9 %collective-permute-start = (bf16[128,256]{1,0:T(8,128)(2,1)S(1)}, bf16[128,256]{1,0:T(8,128)(2,1)S(1)}, u32[]{:S(2)}, u32[]{:S(2)}) collective-permute-start(bf16[128,256]{1,0:T(8,128)(2,1)S(1)} %get-tuple-element.22), channel_id=1, source_target_pairs={{0,13},{2,22},{3,15},{4,23},{5,9},{6,2},{7,14}} | collective-permute-start | bytes 196616 | tf_op jit(solution)/shard_map/ppermute | solution.py:133
  11.3 7.2 %collective-permute-start.10 = (bf16[128,2560]{1,0:T(8,128)(2,1)S(1)}, bf16[128,2560]{1,0:T(8,128)(2,1)S(1)}, u32[]{:S(2)}, u32[]{:S(2)}) collective-permute-start(bf16[128,2560]{1,0:T(8,128)(2,1)S(1)} %pack_kernel.1), channel_id=1, source_target_pairs={{0,1},{1,0},{2,3},{3,2},{4,5},{5,4},{6,7},{7,6},{8,12},{9,8},{10,1... | collective-permute-start | bytes 1966088 | tf_op jit(solution)/shard_map/ppermute | solution.py:129
  16.0 1.8 %collective-permute-start.4 = (bf16[256,128]{1,0:T(8,128)(2,1)S(1)}, bf16[256,128]{1,0:T(8,128)(2,1)S(1)}, u32[]{:S(2)}, u32[]{:S(2)}) collective-permute-start(bf16[256,128]{1,0:T(8,128)(2,1)S(1)} %first_kernel.1), channel_id=1, source_target_pairs={{0,4},{1,8},{2,12},{3,2},{4,5},{5,0},{6,7},{7,6},{8,9},{9,1},{10,1... | collective-permute-start | bytes 196616 | tf_op jit(solution)/shard_map/ppermute | solution.py:129
  16.1 1.7 %collective-permute-start.5 = (bf16[256,128]{1,0:T(8,128)(2,1)S(1)}, bf16[256,128]{1,0:T(8,128)(2,1)S(1)}, u32[]{:S(2)}, u32[]{:S(2)}) collective-permute-start(bf16[256,128]{1,0:T(8,128)(2,1)S(1)} %first_kernel.1), channel_id=1, source_target_pairs={{0,8},{1,12},{2,3},{3,4},{4,5},{5,0},{6,7},{7,6},{8,9},{9,1},{10,1... | collective-permute-start | bytes 196616 | tf_op jit(solution)/shard_map/ppermute | solution.py:129
  16.6 1.4 %collective-permute-start.6 = (bf16[256,128]{1,0:T(8,128)(2,1)S(1)}, bf16[256,128]{1,0:T(8,128)(2,1)S(1)}, u32[]{:S(2)}, u32[]{:S(2)}) collective-permute-start(bf16[256,128]{1,0:T(8,128)(2,1)S(1)} %first_kernel.1), channel_id=1, source_target_pairs={{0,12},{1,0},{2,4},{3,8},{4,5},{5,1},{6,7},{7,6},{8,9},{9,2},{10,1... | collective-permute-start | bytes 196616 | tf_op jit(solution)/shard_map/ppermute | solution.py:129
  16.7 1.4 %collective-permute-start.7 = (bf16[256,128]{1,0:T(8,128)(2,1)S(1)}, bf16[256,128]{1,0:T(8,128)(2,1)S(1)}, u32[]{:S(2)}, u32[]{:S(2)}) collective-permute-start(bf16[256,128]{1,0:T(8,128)(2,1)S(1)} %first_kernel.1), channel_id=1, source_target_pairs={{0,1},{1,4},{2,8},{3,12},{4,5},{5,0},{6,7},{7,6},{8,9},{9,2},{10,1... | collective-permute-start | bytes 196616 | tf_op jit(solution)/shard_map/ppermute | solution.py:129
  18.1 1.5 %collective-permute-start.8 = (bf16[1024,128]{1,0:T(8,128)(2,1)S(1)}, bf16[1024,128]{1,0:T(8,128)(2,1)S(1)}, u32[]{:S(2)}, u32[]{:S(2)}) collective-permute-start(bf16[1024,128]{1,0:T(8,128)(2,1)S(1)} %get-tuple-element.26), channel_id=1, source_target_pairs={{0,1},{1,0},{2,3},{3,2},{4,9},{5,4},{6,7},{7,6},{8,5},{9,8},{10,11... | collective-permute-start | bytes 786440 | tf_op jit(solution)/shard_map/ppermute | solution.py:129
  18.4 1.5 %collective-permute-start.9 = (bf16[1024,128]{1,0:T(8,128)(2,1)S(1)}, bf16[1024,128]{1,0:T(8,128)(2,1)S(1)}, u32[]{:S(2)}, u32[]{:S(2)}) collective-permute-start(bf16[1024,128]{1,0:T(8,128)(2,1)S(1)} %get-tuple-element.27.s_prev), channel_id=1, source_target_pairs={{0,1},{1,0},{2,3},{3,2},{4,5},{5,4},{6,7},{7,6},{8,9},{9,8},{10,11... | collective-permute-start | bytes 786440 | tf_op jit(solution)/shard_map/ppermute | solution.py:129
  20.0 1.6 %collective-permute-start.11 = (bf16[1024,128]{1,0:T(8,128)(2,1)S(1)}, bf16[1024,128]{1,0:T(8,128)(2,1)S(1)}, u32[]{:S(2)}, u32[]{:S(2)}) collective-permute-start(bf16[1024,128]{1,0:T(8,128)(2,1)S(1)} %get-tuple-element.29), channel_id=1, source_target_pairs={{0,1},{1,0},{2,3},{3,2},{4,5},{5,4},{6,7},{7,6},{8,9},{9,14},{10,1... | collective-permute-start | bytes 786440 | tf_op jit(solution)/shard_map/ppermute | solution.py:129
  20.4 1.5 %collective-permute-start.12 = (bf16[1024,128]{1,0:T(8,128)(2,1)S(1)}, bf16[1024,128]{1,0:T(8,128)(2,1)S(1)}, u32[]{:S(2)}, u32[]{:S(2)}) collective-permute-start(bf16[1024,128]{1,0:T(8,128)(2,1)S(1)} %get-tuple-element.36.q_prev), channel_id=1, source_target_pairs={{0,1},{1,0},{2,3},{3,2},{4,5},{5,4},{6,7},{7,6},{8,9},{9,13},{10,1... | collective-permute-start | bytes 786440 | tf_op jit(solution)/shard_map/ppermute | solution.py:129
  22.0 1.8 %collective-permute-start.13 = (bf16[1024,128]{1,0:T(8,128)(2,1)S(1)}, bf16[1024,128]{1,0:T(8,128)(2,1)S(1)}, u32[]{:S(2)}, u32[]{:S(2)}) collective-permute-start(bf16[1024,128]{1,0:T(8,128)(2,1)S(1)} %get-tuple-element.34), channel_id=1, source_target_pairs={{13,23}} | collective-permute-start | bytes 786440 | tf_op jit(solution)/shard_map/ppermute | solution.py:133
  23.4 1.6 %collective-permute-start.15 = (bf16[1024,128]{1,0:T(8,128)(2,1)S(1)}, bf16[1024,128]{1,0:T(8,128)(2,1)S(1)}, u32[]{:S(2)}, u32[]{:S(2)}) collective-permute-start(bf16[1024,128]{1,0:T(8,128)(2,1)S(1)} %get-tuple-element.36.q_prev), channel_id=1, source_target_pairs={{0,1},{1,5},{2,3},{3,2},{4,0},{5,4},{6,7},{7,6},{8,16},{9,17},{10,... | collective-permute-start | bytes 786440 | tf_op jit(solution)/shard_map/ppermute | solution.py:129
  25.0 4.7 %collective-permute-start.16 = (bf16[1024,128]{1,0:T(8,128)(2,1)S(1)}, bf16[1024,128]{1,0:T(8,128)(2,1)S(1)}, u32[]{:S(2)}, u32[]{:S(2)}) collective-permute-start(bf16[1024,128]{1,0:T(8,128)(2,1)S(1)} %step3_kernel.1.q_prev), channel_id=1, source_target_pairs={{23,27},{16,24},{20,28},{17,25},{13,21},{9,1},{14,18}} | collective-permute-start | bytes 786440 | tf_op jit(solution)/shard_map/ppermute | solution.py:133
  25.7 4.0 %collective-permute-start.17 = (bf16[1024,128]{1,0:T(8,128)(2,1)S(1)}, bf16[1024,128]{1,0:T(8,128)(2,1)S(1)}, u32[]{:S(2)}, u32[]{:S(2)}) collective-permute-start(bf16[1024,128]{1,0:T(8,128)(2,1)S(1)} %step3_kernel.1.q_prev), channel_id=1, source_target_pairs={{23,31},{17,29},{13,5},{14,26}} | collective-permute-start | bytes 786440 | tf_op jit(solution)/shard_map/ppermute | solution.py:133
  26.4 3.4 %collective-permute-start.18 = (bf16[1024,128]{1,0:T(8,128)(2,1)S(1)}, bf16[1024,128]{1,0:T(8,128)(2,1)S(1)}, u32[]{:S(2)}, u32[]{:S(2)}) collective-permute-start(bf16[1024,128]{1,0:T(8,128)(2,1)S(1)} %step3_kernel.1.q_prev), channel_id=1, source_target_pairs={{23,19},{14,30}} | collective-permute-start | bytes 786440 | tf_op jit(solution)/shard_map/ppermute | solution.py:133
  27.1 2.7 %collective-permute-start.19 = (bf16[1024,128]{1,0:T(8,128)(2,1)S(1)}, bf16[1024,128]{1,0:T(8,128)(2,1)S(1)}, u32[]{:S(2)}, u32[]{:S(2)}) collective-permute-start(bf16[1024,128]{1,0:T(8,128)(2,1)S(1)} %step3_kernel.1.q_prev), channel_id=1, source_target_pairs={{14,22}} | collective-permute-start | bytes 786440 | tf_op jit(solution)/shard_map/ppermute | solution.py:133
  27.8 2.0 %collective-permute-start.20 = (bf16[1024,128]{1,0:T(8,128)(2,1)S(1)}, bf16[1024,128]{1,0:T(8,128)(2,1)S(1)}, u32[]{:S(2)}, u32[]{:S(2)}) collective-permute-start(bf16[1024,128]{1,0:T(8,128)(2,1)S(1)} %step3_kernel.1.q_prev), channel_id=1, source_target_pairs={{14,10}} | collective-permute-start | bytes 786440 | tf_op jit(solution)/shard_map/ppermute | solution.py:133
  29.9 37.7 %collective-permute-start.21 = (bf16[1040,128]{1,0:T(8,128)(2,1)S(1)}, bf16[1040,128]{1,0:T(8,128)(2,1)S(1)}, u32[]{:S(2)}, u32[]{:S(2)}) collective-permute-start(bf16[1040,128]{1,0:T(8,128)(2,1)S(1)} %get-tuple-element.40.refs_0_), channel_id=1, source_target_pairs={{0,2},{1,3},{2,0},{3,1},{4,6},{5,7},{6,4},{7,5},{8,10},{9,11},{10,... | collective-permute-start | bytes 798728 | tf_op jit(solution)/shard_map/ppermute | solution.py:129
  51.3 15.5 %collective-permute-start.22 = (bf16[1024,128]{1,0:T(8,128)(2,1)S(1)}, bf16[1024,128]{1,0:T(8,128)(2,1)S(1)}, u32[]{:S(2)}, u32[]{:S(2)}) collective-permute-start(bf16[1024,128]{1,0:T(8,128)(2,1)S(1)} %get-tuple-element.38.q_ref), channel_id=1, source_target_pairs={{19,11},{23,15},{27,3},{31,7},{10,2},{14,6}} | collective-permute-start | bytes 786440 | tf_op jit(solution)/shard_map/ppermute | solution.py:133
  67.6 1.5 %collective-permute-start.23 = (bf16[1040,128]{1,0:T(8,128)(2,1)S(1)}, bf16[1040,128]{1,0:T(8,128)(2,1)S(1)}, u32[]{:S(2)}, u32[]{:S(2)}) collective-permute-start(bf16[1040,128]{1,0:T(8,128)(2,1)S(1)} %get-tuple-element.40.refs_0_), channel_id=1, source_target_pairs={{0,1},{1,0},{2,3},{3,2},{4,5},{5,4},{6,7},{7,6},{8,9},{9,8},{10,11... | collective-permute-start | bytes 798728 | tf_op jit(solution)/shard_map/ppermute | solution.py:129
  67.6 1.9 %collective-permute-start.24 = (bf16[1040,128]{1,0:T(8,128)(2,1)S(1)}, bf16[1040,128]{1,0:T(8,128)(2,1)S(1)}, u32[]{:S(2)}, u32[]{:S(2)}) collective-permute-start(bf16[1040,128]{1,0:T(8,128)(2,1)S(1)} %collective-permute-done.21.refs_2_), channel_id=1, source_target_pairs={{0,1},{1,0},{2,3},{3,2},{4,5},{5,4},{6,7},{7,6},{8,9},{9,8},{10,11... | collective-permute-start | bytes 798728 | tf_op jit(solution)/shard_map/ppermute | solution.py:129
  (5 other events, 47.8 us)

commit v10 on v9

--- a/solution.py
+++ b/solution.py
@@ -66,19 +66,19 @@
 MAKER = (None, (2, 1), (3, 2), (5, 3))
 FIRST = (1, 0)
 BESIDE = (3, 1)
-PARTNER = (None, (3, 1), (3, 3), (5, 2))
-PIECES = ((4, 0), (6, 2), (5, 1), (7, 3))
+PARTNER = (None, (2, 0), (3, 3), (5, 2))
+PIECES = ((6, 0), (7, 1), (4, 2), (5, 3))
 SENDS = (
-    (1, 0, 3, 2),
-    (3, 1, 0, 2),
-    (0, 1, 3, 2),
-    (2, 1, 0, 3),
-    (0, 1, 3, 2),
-    (2, 3, 0, 1),
-    (0, 3, 1, 2),
-    (1, 2, 0, 3),
+    (1, None, 2, 3),
+    (2, 0, 1, 3),
+    (None, 3, 0, 2),
+    (3, None, 1, 0),
+    (1, 3, 0, 2),
+    (1, None, 2, 0),
+    (0, 1, 2, 3),
+    (1, 0, 2, 3),
 )
-REST = ((2, 3), (3, 3), (0, 3), (1, 3), (0, 2), (1, 2))
+REST = ((2, 3), (0, 3), (1, 3), (0, 2))
 
 
 def hops(a, b):
@@ -168,70 +168,78 @@
     return 2 * (m + 1) * part
 
 
-def cut_kernel(diag_ref, *refs):
-    cuts, sem = refs[:-1], refs[-1]
+def sent_here():
     row, col = lax.axis_index("row"), lax.axis_index("col")
-    part = diag_ref.shape[1]
-    k = jnp.int32(0)
+    k = jnp.int32(-1)
     for r in range(NR):
         for c in range(NC):
-            k = jnp.where((row == r) & (col == c), SENDS[r][c], k)
-    for m in range(NR // 2):
-
-        @pl.when(row // 2 == m)
+            if SENDS[r][c] is not None:
+                k = jnp.where((row == r) & (col == c), SENDS[r][c], k)
+    return k
+
+
+def cut(diag_ref, flag, k, out, sem):
+    @pl.when(flag)
+    def _():
+        copy = pltpu.make_async_copy(diag_ref.at[k, :, pl.ds(0, out.shape[1])], out, sem)
+        copy.start()
+        copy.wait()
+
+
+def cut_first_kernel(diag_ref, hi_ref, lo_ref, sem):
+    row, k = lax.axis_index("row"), sent_here()
+    cut(diag_ref, (k == 0) & (row >= 4), 0, hi_ref, sem)
+    cut(diag_ref, ((k == 0) & (row < 4)) | ((k > 0) & (row == 0)), k, lo_ref, sem)
+
+
+def cut_rest_kernel(diag_ref, after_ref, *refs):
+    cuts, sem = refs[:-1], refs[-1]
+    row, k = lax.axis_index("row"), sent_here()
+    for m, out in enumerate(cuts):
+        cut(diag_ref, (k > 0) & (row > 0) & (row // 2 == m), k, out, sem)
+
+
+def first_kernel(rhs_ref, diag_ref, hi_ref, lo_ref, out_ref, rhs_v, lo_v, rhs_sem, lo_sem):
+    n, half = lo_ref.shape
+    col = lax.axis_index("col")
+
+    @pl.when(lax.axis_index("row") == 0)
+    def _():
+        copy = pltpu.make_async_copy(rhs_ref.at[0], rhs_v, rhs_sem)
+        copy.start()
+        own = pltpu.make_async_copy(diag_ref.at[0, :, pl.ds(0, half)], lo_v, lo_sem)
+
+        @pl.when(col == 0)
         def _():
-            copy = pltpu.make_async_copy(diag_ref.at[k, :, pl.ds(0, pair_width(m, part))], cuts[m], sem)
-            copy.start()
-            copy.wait()
-
-
-def first_kernel(rhs_ref, diag_ref, *refs):
-    parts, out_ref = refs[: NR // 2], refs[NR // 2]
-    rhs_v, d_v, rhs_sem, d_sem = refs[NR // 2 + 1 :]
-    n = out_ref.shape[0] // 2
-    col = lax.axis_index("col")
-
-    @pl.when(lax.axis_index("row") == 0)
-    def _():
-        rhs_copy = pltpu.make_async_copy(rhs_ref.at[0], rhs_v, rhs_sem)
-        rhs_copy.start()
-
-        def pieces(c):
-            copies = []
-            for i, r in enumerate(PIECES[c]):
-                wide = pair_width(r // 2, n)
-                source = parts[r // 2] if r else diag_ref.at[0, :, pl.ds(0, wide)]
-                copies.append(pltpu.make_async_copy(source, d_v.at[i, :, pl.ds(0, wide)], d_sem.at[i]))
-            return copies
-
-        for c in range(NC):
-
-            @pl.when(col == c)
-            def _():
-                for copy in pieces(c):
-                    copy.start()
-
-        rhs_copy.wait()
+            own.start()
+
+        @pl.when(col != 0)
+        def _():
+            lo_v[...] = lo_ref[...]
+
+        copy.wait()
         p = low(rhs_v[...])
-        for c in range(NC):
-
-            @pl.when(col == c)
-            def _():
-                for i, copy in enumerate(pieces(c)):
-                    copy.wait()
-                    wide = pair_width(PIECES[c][i] // 2, n)
-                    out_ref[i * n : (i + 1) * n] = low(dot(d_v[i, :, :wide], p[:wide]))
+        out_ref[:n] = low(dot(hi_ref[...], p))
+
+        @pl.when(col == 0)
+        def _():
+            own.wait()
+
+        out_ref[n:] = low(dot(lo_v[...], p[:half]))
 
 
 def pack_kernel(*refs):
     parts, out_ref, sem = refs[:-2], refs[-2], refs[-1]
+    part = out_ref.shape[0]
 
     @pl.when(any_of(PARTNER[1:]))
     def _():
         copies, left = [], 0
         for m, source in enumerate(parts):
-            wide = source.shape[1]
-            copies.append(pltpu.make_async_copy(source, out_ref.at[:, pl.ds(left, wide)], sem.at[m]))
+            wide = pair_width(m, part)
+            copies.append(
+                pltpu.make_async_copy(source.at[:, pl.ds(0, wide)], out_ref.at[:, pl.ds(left, wide)], sem.at[m])
+            )
             left += wide
         for copy in copies:
             copy.start()
@@ -283,25 +291,40 @@
     q_ref[half:] = low(dot(d_ref[half:], p_ref[...]))
 
 
+def collect(got, first, q_ref):
+    part = q_ref.shape[0] // NR
+    for j, pieces in enumerate(got):
+        src = lax.rem(first + j, NC)
+        for i in range(2):
+            r = jnp.int32(PIECES[0][i])
+            for n in range(1, NC):
+                r = jnp.where(src == n, PIECES[n][i], r)
+            q_ref[pl.ds(pl.multiple_of(r * part, part), part)] = pieces[i * part : (i + 1) * part]
+
+
 def step0_kernel(g0, g1, g2, g3, rhs_ref, l_ref, p_ref, q_ref, s_ref):
-    part = l_ref.shape[0] // NR
     row = lax.axis_index("row")
 
-    def lookup(c, i):
-        r = jnp.int32(PIECES[0][i])
-        for n in range(1, NC):
-            r = jnp.where(c == n, PIECES[n][i], r)
-        return pl.multiple_of(r * part, part)
-
-    @pl.when((row >= 1) & (row < 4) & (lax.axis_index("col") == 0))
-    def _():
-        for j, got in enumerate((g0, g1, g2, g3)):
-            src = lax.rem(row + 7 - j, 4)
-            q_ref[pl.ds(lookup(src, 0), part)] = got[:part]
-            q_ref[pl.ds(lookup(src, 1), part)] = got[part:]
+    @pl.when(at(FIRST) | at((3, 0)))
+    def _():
+        collect((g0, g1, g2, g3), jnp.where(row == 3, 1, 0), q_ref)
         s = dot(l_ref[...], q_ref[...])
+        p_ref[...] = low(rhs_ref[0] - s)
         s_ref[...] = low(s)
-        p_ref[...] = low(rhs_ref[0] - s)
+
+
+def step0_again_kernel(g0, g1, g2, g3, l_ref, q_prev, s_prev, q_ref, s_ref):
+    active = at((2, 0))
+
+    @pl.when(active)
+    def _():
+        collect((g0, g1, g2, g3), 0, q_ref)
+        s_ref[...] = low(dot(l_ref[...], q_ref[...]))
+
+    @pl.when(jnp.logical_not(active))
+    def _():
+        q_ref[...] = q_prev[...]
+        s_ref[...] = s_prev[...]
 
 
 def step1_kernel(p_in, sum_ref, rhs_ref, d_ref, l_ref, q_prev, s_prev, p_ref, q_ref, s_ref):
@@ -326,6 +349,7 @@
     @pl.when(active)
     def _():
         lower_dot(q_ref, d_ref, p_in)
+        a_ref[...] = q_ref[...]
         s_ref[...] = low(dot(l_ref[...], q_ref[...]))
 
     @pl.when(beside)
@@ -341,19 +365,22 @@
         s_ref[...] = s_prev[...]
 
 
-def step3_kernel(took, a_ref, sum_ref, d_ref, q_prev, came_ref, q_ref, p_v):
-    active, taken = at(MAKER[3]), any_of(took)
+def step3_kernel(takers, sum_ref, a_ref, *refs):
+    came, (d_ref, q_prev, q_ref, p_v) = refs[:-4], refs[-4:]
+    active = at(MAKER[3])
 
     @pl.when(active)
     def _():
         p_v[...] = low(a_ref[...].astype(jnp.float32) - sum_ref[...].astype(jnp.float32))
         lower_dot(q_ref, d_ref, p_v)
 
-    @pl.when(taken)
-    def _():
-        q_ref[...] = came_ref[...]
-
-    @pl.when(jnp.logical_not(active | taken))
+    for devices, source in zip(takers, (a_ref, *came)):
+
+        @pl.when(any_of(devices))
+        def _():
+            q_ref[...] = source[...]
+
+    @pl.when(jnp.logical_not(active | any_of([d for devices in takers for d in devices])))
     def _():
         q_ref[...] = q_prev[...]
 
@@ -425,39 +452,55 @@
     dma = pltpu.SemaphoreType.DMA
 
     wides = [pair_width(m, part) for m in range(NR // 2)]
-    cuts = call(
-        cut_kernel, [jax.ShapeDtypeStruct((part, w), bf16) for w in wides], [diag_inv], [HBM], [ANY] * len(wides), [dma]
-    )
-    at_piece = {r: (0, c) for c, rows in enumerate(PIECES) for r in rows}
-    parts = []
-    for m, cut in enumerate(cuts):
-        pairs = []
-        for r in (2 * m, 2 * m + 1):
-            for c, k in enumerate(SENDS[r]):
-                if k == 0 and r:
-                    pairs.append(((r, c), at_piece[r]))
-                if k and MAKER[k][0] != r:
-                    pairs.append(((r, c), MAKER[k] if r % 2 else PARTNER[k]))
-        parts.append(send_only(cut, pairs))
+    hi, lo = call(
+        cut_first_kernel,
+        [jax.ShapeDtypeStruct((part, w), bf16) for w in (size, size // 2)],
+        [diag_inv],
+        [HBM],
+        [ANY, ANY],
+        [dma],
+    )
+    source = {(r, k): (r, c) for r in range(NR) for c, k in enumerate(SENDS[r]) if k is not None}
+    hi = send_only(hi, [(source[rows[0], 0], (0, c)) for c, rows in enumerate(PIECES)])
+    lo = send_only(
+        lo,
+        [(source[rows[1], 0], (0, c)) for c, rows in enumerate(PIECES) if rows[1]]
+        + [(source[0, k], PARTNER[k]) for k in range(1, NC)],
+    )
     q = call(
         first_kernel,
         jax.ShapeDtypeStruct((2 * part, width), bf16),
-        [rhs, diag_inv, *parts],
-        [HBM, HBM] + [ANY] * len(wides),
+        [rhs, diag_inv, hi, lo],
+        [HBM, HBM, VMEM, VMEM],
         VMEM,
-        [
-            pltpu.VMEM((size, width), jnp.float32),
-            pltpu.VMEM((2, part, size), bf16),
-            dma,
-            pltpu.SemaphoreType.DMA((2,)),
-        ],
-    )
-    takers = (FIRST, (2, 0), (3, 0))
-    got = [send(q, [((0, c), takers[(c + j) % 4]) for c in range(4) if (c + j) % 4 < 3]) for j in range(4)]
+        [pltpu.VMEM((size, width), jnp.float32), pltpu.VMEM((part, size // 2), bf16), dma, dma],
+    )
+    cuts = call(
+        cut_rest_kernel,
+        [jax.ShapeDtypeStruct((part, w), bf16) for w in wides],
+        [diag_inv, q],
+        [HBM, ANY],
+        [ANY] * len(wides),
+        [dma],
+    )
+    parts = [
+        send_only(
+            cut,
+            [
+                (source[r, k], MAKER[k] if r % 2 else PARTNER[k])
+                for r in (2 * m, 2 * m + 1)
+                for k in range(1, NC)
+                if r and MAKER[k][0] != r
+            ],
+        )
+        for m, cut in enumerate(cuts)
+    ]
+    got = [send(q, [((0, j), FIRST), ((0, (j + 1) % NC), (3, 0))]) for j in range(NC)]
+    got_again = [send(q, [((0, j), (2, 0))]) for j in range(NC)]
     even = call(
         pack_kernel,
         jax.ShapeDtypeStruct((part, sum(wides)), bf16),
-        parts,
+        [lo, *parts[1:]],
         [ANY] * len(wides),
         VMEM,
         [pltpu.SemaphoreType.DMA((len(wides),))],
@@ -474,6 +517,7 @@
 
     p, q, s = call(step0_kernel, [vec] * 3, [*got, rhs, block], [VMEM] * 6, [VMEM] * 3)
     p_in = send(p, [(FIRST, MAKER[1])])
+    q, s = call(step0_again_kernel, [vec] * 2, [*got_again, block, q, s], [VMEM] * 7, [VMEM] * 2)
     sums = send(s, [((2, 0), MAKER[1]), ((3, 0), BESIDE)])
     p, q, s = call(step1_kernel, [vec] * 3, [p_in, sums, rhs, diag, block, q, s], [VMEM] * 7, [VMEM] * 3)
     p_in = send(p, [(MAKER[1], MAKER[2])])
@@ -484,27 +528,28 @@
     took = [(4, 0), (5, 0), (0, 0), (4, 1)]
 
     a, q, s = call(step2_kernel, [vec] * 3, [p_in, q_in, sums, rhs, diag, block, q, s], [VMEM] * 8, [VMEM] * 3)
-    sums = send_only(s, [(MAKER[2], MAKER[3])])
-    a = send_only(a, [(BESIDE, MAKER[3])])
-
+    sums = send(s, [(MAKER[2], MAKER[3])])
+    q_2 = a
+    a = send_only(a, [(BESIDE, MAKER[3]), (MAKER[2], (2, 2))])
+    q_2 = send_only(q_2, [(MAKER[2], (7, 2))])
     q = call(
-        functools.partial(step3_kernel, took),
+        functools.partial(step3_kernel, [[(2, 2)], [(7, 2)], took]),
         vec,
-        [a, sums, diag, q, came],
-        [VMEM] * 5,
+        [sums, a, q_2, came, diag, q],
+        [VMEM] * 6,
         VMEM,
         [pltpu.VMEM((size, width), bf16)],
     )
 
     sends = [
-        [(MAKER[3], (6, 3)), ((4, 0), (6, 0)), ((5, 0), (7, 0)), ((4, 1), (6, 1)), ((3, 1), (5, 1)), ((2, 1), (0, 1))],
-        [(MAKER[3], (7, 3)), ((4, 1), (7, 1)), ((3, 1), (1, 1))],
+        [
+            (MAKER[3], (7, 3)), ((2, 2), (6, 2)), (MAKER[2], (5, 2)),
+            ((4, 0), (6, 0)), ((5, 0), (7, 0)), ((4, 1), (6, 1)), ((3, 1), (5, 1)), ((2, 1), (0, 1)),
+        ],
+        [(MAKER[3], (6, 3)), ((2, 2), (4, 2)), (MAKER[2], (1, 2)), ((4, 1), (7, 1)), ((3, 1), (1, 1))],
         [(MAKER[3], (4, 3))],
-        [],
-        [],
+        [(MAKER[3], (3, 3))],
     ]
-    for pairs, r in zip(sends, (4, 6, 7, 5, 2)):
-        pairs.append((MAKER[2], (r, 2)))
     got = [send_only(q, pairs) for pairs in sends]
     takers = [[b for _, b in pairs] for pairs in sends]
     q, mine = call(
@@ -519,7 +564,7 @@
         return send(value, [((r, c), (r, c ^ step)) for r in range(NR) for c in range(NC)])
 
     across = swap(mine, 2)
-    rest = send_only(q, list(zip(((4, 3), (5, 3), (6, 3), (7, 3), (2, 2), MAKER[2]), REST)))
+    rest = send_only(q, list(zip(((3, 3), (6, 3), (7, 3), (2, 2)), REST)))
     solved = call(solved_kernel, jax.ShapeDtypeStruct((size, width), jnp.float32), [q, rest], [VMEM] * 2, VMEM)
     beside, across, solved = lax.optimization_barrier((mine, across, solved))
     beside = swap(beside, 1)

time: 71.3 us -> 81.8 us (1.15)
  starting transfers between devices: 43.1 us -> 53 us
  local copies, waits for them, and re-layouts: 1.32 us -> 2.45 us
    ppermute x12 -> x13, starting transfers between devices: 13.9 us -> 31.7 us  [send_only(): lax.ppermute(value, ('row', 'col'), [(a * NC + b, c * NC + d) for (a, b),...]
    ppermute x13 -> x18, starting transfers between devices: 29.1 us -> 21.3 us  [send(): lax.ppermute(value, ('row', 'col'), [(a * NC + b, c * NC + d) for (a, b),...]
    unnamed x8 -> x10, local copies, waits for them, and re-layouts: 1.32 us -> 2.45 us
    ppermute x12 -> x13, waiting for transfers between devices: 15.5 us -> 15 us  [send_only(): lax.ppermute(value, ('row', 'col'), [(a * NC + b, c * NC + d) for (a, b),...]
    pallas_call x11 -> x13, Pallas kernels: 2.62 us -> 2.71 us  [call(): pl.pallas_call(kernel, out_shape=outs, in_specs=in_specs, out_specs=out_s...]
    ppermute x13 -> x18, waiting for transfers between devices: 6.24 us -> 6.16 us  [send(): lax.ppermute(value, ('row', 'col'), [(a * NC + b, c * NC + d) for (a, b),...]
  transfers between devices with their start and end apart: 25 -> 31, of which waited for: 13 -> 12; matrix products, arithmetic and copies ran while one was open for 0% -> 0% of each run, Pallas kernels for 1% -> 1%
where the time goes in v10:
time: 81.8 us; the launch traced here: 81.5 us
  starting transfers between devices  53 us (65%)
  waiting for transfers between devices  21.1 us (26%)
  Pallas kernels  2.71 us (3%)
  local copies, waits for them, and re-layouts  2.45 us (3%)
  between operations  2.22 us (3%)
    ppermute x13, starting transfers between devices, send_only(): lax.ppermute(value, ('row', 'col'), [(a * NC + b, c * NC + d) for (a, b),...  31.7 us
    ppermute x18, starting transfers between devices, send(): lax.ppermute(value, ('row', 'col'), [(a * NC + b, c * NC + d) for (a, b),...  21.3 us
    ppermute x13, waiting for transfers between devices, send_only(): lax.ppermute(value, ('row', 'col'), [(a * NC + b, c * NC + d) for (a, b),...  15 us
    ppermute x18, waiting for transfers between devices, send(): lax.ppermute(value, ('row', 'col'), [(a * NC + b, c * NC + d) for (a, b),...  6.16 us
    pallas_call x13, Pallas kernels, call(): pl.pallas_call(kernel, out_shape=outs, in_specs=in_specs, out_specs=out_s...  2.71 us
    unnamed x10, local copies, waits for them, and re-layouts  2.45 us
  transfers between devices with their start and end apart: 31, of which 12 were waited for; matrix products, arithmetic and copies ran while one was open for 0% of the time, Pallas kernels for 1%

profile of v10, /device:TPU:7, one launch (start us, length us, event | category | flops | bytes accessed | tf_op | source)
XLA Modules:
  0.0 81.5 jit_solution(6150157198527711938)
XLA Ops:
  0.6 1.2 %copy-done.3 = bf16[4,128,1024]{2,1,0:T(8,128)(2,1)S(1)} copy-done((bf16[4,128,1024]{2,1,0:T(8,128)(2,1)S(1)}, bf16[4,128,1024]{2,1,0:T(8,128)(2,1)}, u32[]{:S(2)}) %copy-start.3) | copy-done | bytes 1048600
  1.9 0.7 collective-permute-start
  2.6 0.7 collective-permute-start.1
  3.3 1.2 %copy-done.1 = f32[2,1,1024,128]{3,2,1,0:T(8,128)S(1)} copy-done((f32[2,1,1024,128]{3,2,1,0:T(8,128)S(1)}, f32[2,1,1024,128]{3,2,1,0:T(8,128)}, u32[]{:S(2)}) %copy-start.1) | copy-done | bytes 1048600
  4.6 0.8 collective-permute-start.14
  5.4 0.7 collective-permute-start.13
  6.9 0.7 collective-permute-start.15
  8.6 0.8 collective-permute-done.2.g0
  12.2 22.9 %collective-permute-start.16 = (bf16[128,256]{1,0:T(8,128)(2,1)S(1)}, bf16[128,256]{1,0:T(8,128)(2,1)S(1)}, u32[]{:S(2)}, u32[]{:S(2)}) collective-permute-start(bf16[128,256]{1,0:T(8,128)(2,1)S(1)} %get-tuple-element.35), channel_id=1, source_target_pairs={{6,9},{4,14},{7,23}} | collective-permute-start | bytes 196616 | tf_op jit(solution)/shard_map/ppermute | solution.py:133
  35.1 1.3 %collective-permute-done.16.refs_0_ = bf16[128,256]{1,0:T(8,128)(2,1)S(1)} collective-permute-done((bf16[128,256]{1,0:T(8,128)(2,1)S(1)}, bf16[128,256]{1,0:T(8,128)(2,1)S(1)}, u32[]{:S(2)}, u32[]{:S(2)}) %collective-permute-start.16) | collective-permute-done | bytes 65568 | tf_op jit(solution)/shard_map/ppermute | solution.py:133
  36.6 1.6 %collective-permute-start.17 = (bf16[1024,128]{1,0:T(8,128)(2,1)S(1)}, bf16[1024,128]{1,0:T(8,128)(2,1)S(1)}, u32[]{:S(2)}, u32[]{:S(2)}) collective-permute-start(bf16[1024,128]{1,0:T(8,128)(2,1)S(1)} %get-tuple-element.37), channel_id=1, source_target_pairs={{0,1},{1,0},{2,3},{3,2},{4,5},{5,4},{6,7},{7,6},{8,9},{9,14},{10,1... | collective-permute-start | bytes 786440 | tf_op jit(solution)/shard_map/ppermute | solution.py:129
  38.3 1.1 %collective-permute-done.17.p_in = bf16[1024,128]{1,0:T(8,128)(2,1)S(1)} collective-permute-done((bf16[1024,128]{1,0:T(8,128)(2,1)S(1)}, bf16[1024,128]{1,0:T(8,128)(2,1)S(1)}, u32[]{:S(2)}, u32[]{:S(2)}) %collective-permute-start.17) | collective-permute-done | bytes 262176 | tf_op jit(solution)/shard_map/ppermute | solution.py:129
  40.9 0.7 collective-permute-start.21
  41.8 1.4 %collective-permute-done.22.refs_1_ = bf16[1024,128]{1,0:T(8,128)(2,1)S(1)} collective-permute-done((bf16[1024,128]{1,0:T(8,128)(2,1)S(1)}, bf16[1024,128]{1,0:T(8,128)(2,1)S(1)}, u32[]{:S(2)}, u32[]{:S(2)}) %collective-permute-start.22) | collective-permute-done | bytes 262176 | tf_op jit(solution)/shard_map/ppermute | solution.py:129
  43.2 0.7 collective-permute-start.23
  43.9 0.7 collective-permute-start.24
  44.6 0.7 collective-permute-start.25
  45.2 0.7 collective-permute-start.26
  47.4 15.1 %collective-permute-start.27 = (bf16[1040,128]{1,0:T(8,128)(2,1)S(1)}, bf16[1040,128]{1,0:T(8,128)(2,1)S(1)}, u32[]{:S(2)}, u32[]{:S(2)}) collective-permute-start(bf16[1040,128]{1,0:T(8,128)(2,1)S(1)} %get-tuple-element.48.refs_0_), channel_id=1, source_target_pairs={{0,2},{1,3},{2,0},{3,1},{4,6},{5,7},{6,4},{7,5},{8,10},{9,11},{10,... | collective-permute-start | bytes 798728 | tf_op jit(solution)/shard_map/ppermute | solution.py:129
  62.4 1.3 %collective-permute-start.28 = (bf16[1024,128]{1,0:T(8,128)(2,1)S(1)}, bf16[1024,128]{1,0:T(8,128)(2,1)S(1)}, u32[]{:S(2)}, u32[]{:S(2)}) collective-permute-start(bf16[1024,128]{1,0:T(8,128)(2,1)S(1)} %get-tuple-element.46.q_ref), channel_id=1, source_target_pairs={{15,11},{27,3},{31,7},{10,2}} | collective-permute-start | bytes 786440 | tf_op jit(solution)/shard_map/ppermute | solution.py:133
  63.7 13.6 %collective-permute-done.28.rest_ref = bf16[1024,128]{1,0:T(8,128)(2,1)S(1)} collective-permute-done((bf16[1024,128]{1,0:T(8,128)(2,1)S(1)}, bf16[1024,128]{1,0:T(8,128)(2,1)S(1)}, u32[]{:S(2)}, u32[]{:S(2)}) %collective-permute-start.28) | collective-permute-done | bytes 262176 | tf_op jit(solution)/shard_map/ppermute | solution.py:133
  77.3 0.8 %solved_kernel.1 = f32[1024,128]{1,0:T(8,128)} custom-call(bf16[1024,128]{1,0:T(8,128)(2,1)S(1)} %get-tuple-element.46.q_ref, bf16[1024,128]{1,0:T(8,128)(2,1)S(1)} %collective-permute-done.28.rest_ref), custom_call_target="tpu_custom_call" | custom-call | tf_op jit(solution)/shard_map/solved_kernel/pallas_call | solution.py:156
  78.7 1.0 %collective-permute-done.29.refs_1_ = bf16[1040,128]{1,0:T(8,128)(2,1)S(1)} collective-permute-done((bf16[1040,128]{1,0:T(8,128)(2,1)S(1)}, bf16[1040,128]{1,0:T(8,128)(2,1)S(1)}, u32[]{:S(2)}, u32[]{:S(2)}) %collective-permute-start.29) | collective-permute-done | bytes 266272 | tf_op jit(solution)/shard_map/ppermute | solution.py:129
  80.1 1.4 %final_kernel.1 = f32[2,1024,128]{2,1,0:T(8,128)} custom-call(f32[2,1024,128]{2,1,0:T(8,128)S(1)} %bitcast.15, bf16[1040,128]{1,0:T(8,128)(2,1)S(1)} %get-tuple-element.48.refs_0_, bf16[1040,128]{1,0:T(8,128)(2,1)S(1)} %collective-permute-done.29.refs_1_, bf16[1040,128]{1,0:T(8,128)(2,1)S(1)} %collective-permute-done.27.refs_2_, ...), custom_call_target="tpu_custom_call" | custom-call | tf_op jit(solution)/shard_map/final_kernel/pallas_call | solution.py:156
  (61 shorter events, 7.6 us)
Async XLA Ops:
  1.9 1.4 %collective-permute-start = (bf16[128,1024]{1,0:T(8,128)(2,1)S(1)}, bf16[128,1024]{1,0:T(8,128)(2,1)S(1)}, u32[]{:S(2)}, u32[]{:S(2)}) collective-permute-start(bf16[128,1024]{1,0:T(8,128)(2,1)S(1)} %get-tuple-element.26), channel_id=1, source_target_pairs={{24,0},{29,1},{18,2},{23,3}} | collective-permute-start | bytes 786440 | tf_op jit(solution)/shard_map/ppermute | solution.py:133
  4.6 2.2 %collective-permute-start.14 = (bf16[128,1024]{1,0:T(8,128)(2,1)S(1)}, bf16[128,1024]{1,0:T(8,128)(2,1)S(1)}, u32[]{:S(2)}, u32[]{:S(2)}) collective-permute-start(bf16[128,1024]{1,0:T(8,128)(2,1)S(1)} %get-tuple-element.34), channel_id=1, source_target_pairs={{25,8},{26,15},{27,22},{28,9},{30,14},{31,23}} | collective-permute-start | bytes 786440 | tf_op jit(solution)/shard_map/ppermute | solution.py:133
  5.4 1.4 %collective-permute-start.13 = (bf16[128,768]{1,0:T(8,128)(2,1)S(1)}, bf16[128,768]{1,0:T(8,128)(2,1)S(1)}, u32[]{:S(2)}, u32[]{:S(2)}) collective-permute-start(bf16[128,768]{1,0:T(8,128)(2,1)S(1)} %get-tuple-element.33), channel_id=1, source_target_pairs={{16,8},{19,15},{17,22},{20,9},{22,14}} | collective-permute-start | bytes 589832 | tf_op jit(solution)/shard_map/ppermute | solution.py:133
  6.9 29.5 %collective-permute-start.15 = (bf16[128,2560]{1,0:T(8,128)(2,1)S(1)}, bf16[128,2560]{1,0:T(8,128)(2,1)S(1)}, u32[]{:S(2)}, u32[]{:S(2)}) collective-permute-start(bf16[128,2560]{1,0:T(8,128)(2,1)S(1)} %pack_kernel.1), channel_id=1, source_target_pairs={{0,1},{1,0},{2,3},{3,2},{4,5},{5,4},{6,7},{7,6},{8,9},{9,8},{10,11... | collective-permute-start | bytes 1966088 | tf_op jit(solution)/shard_map/ppermute | solution.py:129
  7.6 1.8 %collective-permute-start.2 = (bf16[256,128]{1,0:T(8,128)(2,1)S(1)}, bf16[256,128]{1,0:T(8,128)(2,1)S(1)}, u32[]{:S(2)}, u32[]{:S(2)}) collective-permute-start(bf16[256,128]{1,0:T(8,128)(2,1)S(1)} %first_kernel.1.after_ref), channel_id=1, source_target_pairs={{0,4},{1,12},{2,3},{3,2},{4,5},{5,0},{6,7},{7,6},{8,9},{9,8},{10,1... | collective-permute-start | bytes 196616 | tf_op jit(solution)/shard_map/ppermute | solution.py:129
  7.7 2.1 %collective-permute-start.3 = (bf16[256,128]{1,0:T(8,128)(2,1)S(1)}, bf16[256,128]{1,0:T(8,128)(2,1)S(1)}, u32[]{:S(2)}, u32[]{:S(2)}) collective-permute-start(bf16[256,128]{1,0:T(8,128)(2,1)S(1)} %first_kernel.1.after_ref), channel_id=1, source_target_pairs={{0,1},{1,4},{2,12},{3,2},{4,5},{5,0},{6,7},{7,6},{8,9},{9,8},{10,1... | collective-permute-start | bytes 196616 | tf_op jit(solution)/shard_map/ppermute | solution.py:129
  8.1 1.8 %collective-permute-start.4 = (bf16[256,128]{1,0:T(8,128)(2,1)S(1)}, bf16[256,128]{1,0:T(8,128)(2,1)S(1)}, u32[]{:S(2)}, u32[]{:S(2)}) collective-permute-start(bf16[256,128]{1,0:T(8,128)(2,1)S(1)} %first_kernel.1.after_ref), channel_id=1, source_target_pairs={{0,1},{1,0},{2,4},{3,12},{4,5},{5,2},{6,7},{7,6},{8,9},{9,8},{10,1... | collective-permute-start | bytes 196616 | tf_op jit(solution)/shard_map/ppermute | solution.py:129
  8.2 2.1 %collective-permute-start.5 = (bf16[256,128]{1,0:T(8,128)(2,1)S(1)}, bf16[256,128]{1,0:T(8,128)(2,1)S(1)}, u32[]{:S(2)}, u32[]{:S(2)}) collective-permute-start(bf16[256,128]{1,0:T(8,128)(2,1)S(1)} %first_kernel.1.after_ref), channel_id=1, source_target_pairs={{0,12},{1,0},{2,3},{3,4},{4,5},{5,1},{6,7},{7,6},{8,9},{9,8},{10,1... | collective-permute-start | bytes 196616 | tf_op jit(solution)/shard_map/ppermute | solution.py:129
  11.6 24.9 %collective-permute-start.11 = (bf16[1024,128]{1,0:T(8,128)(2,1)S(1)}, bf16[1024,128]{1,0:T(8,128)(2,1)S(1)}, u32[]{:S(2)}, u32[]{:S(2)}) collective-permute-start(bf16[1024,128]{1,0:T(8,128)(2,1)S(1)} %get-tuple-element.31.s_prev), channel_id=1, source_target_pairs={{0,1},{1,0},{2,3},{3,2},{4,5},{5,4},{6,7},{7,6},{8,9},{9,8},{10,11... | collective-permute-start | bytes 786440 | tf_op jit(solution)/shard_map/ppermute | solution.py:129
  11.8 24.7 %collective-permute-start.6 = (bf16[1024,128]{1,0:T(8,128)(2,1)S(1)}, bf16[1024,128]{1,0:T(8,128)(2,1)S(1)}, u32[]{:S(2)}, u32[]{:S(2)}) collective-permute-start(bf16[1024,128]{1,0:T(8,128)(2,1)S(1)} %get-tuple-element.28), channel_id=1, source_target_pairs={{0,1},{1,0},{2,3},{3,2},{4,9},{5,4},{6,7},{7,6},{8,5},{9,8},{10,11... | collective-permute-start | bytes 786440 | tf_op jit(solution)/shard_map/ppermute | solution.py:129
  12.2 24.2 %collective-permute-start.16 = (bf16[128,256]{1,0:T(8,128)(2,1)S(1)}, bf16[128,256]{1,0:T(8,128)(2,1)S(1)}, u32[]{:S(2)}, u32[]{:S(2)}) collective-permute-start(bf16[128,256]{1,0:T(8,128)(2,1)S(1)} %get-tuple-element.35), channel_id=1, source_target_pairs={{6,9},{4,14},{7,23}} | collective-permute-start | bytes 196616 | tf_op jit(solution)/shard_map/ppermute | solution.py:133
  36.6 2.8 %collective-permute-start.17 = (bf16[1024,128]{1,0:T(8,128)(2,1)S(1)}, bf16[1024,128]{1,0:T(8,128)(2,1)S(1)}, u32[]{:S(2)}, u32[]{:S(2)}) collective-permute-start(bf16[1024,128]{1,0:T(8,128)(2,1)S(1)} %get-tuple-element.37), channel_id=1, source_target_pairs={{0,1},{1,0},{2,3},{3,2},{4,5},{5,4},{6,7},{7,6},{8,9},{9,14},{10,1... | collective-permute-start | bytes 786440 | tf_op jit(solution)/shard_map/ppermute | solution.py:129
  38.2 1.5 %collective-permute-start.18 = (bf16[1024,128]{1,0:T(8,128)(2,1)S(1)}, bf16[1024,128]{1,0:T(8,128)(2,1)S(1)}, u32[]{:S(2)}, u32[]{:S(2)}) collective-permute-start(bf16[1024,128]{1,0:T(8,128)(2,1)S(1)} %get-tuple-element.43.q_prev), channel_id=1, source_target_pairs={{0,1},{1,0},{2,3},{3,2},{4,5},{5,4},{6,7},{7,6},{8,9},{9,13},{10,1... | collective-permute-start | bytes 786440 | tf_op jit(solution)/shard_map/ppermute | solution.py:129
  39.8 2.0 %collective-permute-start.19 = (bf16[1024,128]{1,0:T(8,128)(2,1)S(1)}, bf16[1024,128]{1,0:T(8,128)(2,1)S(1)}, u32[]{:S(2)}, u32[]{:S(2)}) collective-permute-start(bf16[1024,128]{1,0:T(8,128)(2,1)S(1)} %get-tuple-element.41.s_ref), channel_id=1, source_target_pairs={{0,1},{1,0},{2,3},{3,2},{4,5},{5,4},{6,7},{7,6},{8,9},{9,8},{10,11... | collective-permute-start | bytes 786440 | tf_op jit(solution)/shard_map/ppermute | solution.py:129
  40.2 1.6 %collective-permute-start.20 = (bf16[1024,128]{1,0:T(8,128)(2,1)S(1)}, bf16[1024,128]{1,0:T(8,128)(2,1)S(1)}, u32[]{:S(2)}, u32[]{:S(2)}) collective-permute-start(bf16[1024,128]{1,0:T(8,128)(2,1)S(1)} %get-tuple-element.42), channel_id=1, source_target_pairs={{13,23},{14,10}} | collective-permute-start | bytes 786440 | tf_op jit(solution)/shard_map/ppermute | solution.py:133
  41.6 1.6 %collective-permute-start.22 = (bf16[1024,128]{1,0:T(8,128)(2,1)S(1)}, bf16[1024,128]{1,0:T(8,128)(2,1)S(1)}, u32[]{:S(2)}, u32[]{:S(2)}) collective-permute-start(bf16[1024,128]{1,0:T(8,128)(2,1)S(1)} %get-tuple-element.43.q_prev), channel_id=1, source_target_pairs={{0,1},{1,5},{2,3},{3,2},{4,0},{5,4},{6,7},{7,6},{8,16},{9,17},{10,... | collective-permute-start | bytes 786440 | tf_op jit(solution)/shard_map/ppermute | solution.py:129
  43.2 4.0 %collective-permute-start.23 = (bf16[1024,128]{1,0:T(8,128)(2,1)S(1)}, bf16[1024,128]{1,0:T(8,128)(2,1)S(1)}, u32[]{:S(2)}, u32[]{:S(2)}) collective-permute-start(bf16[1024,128]{1,0:T(8,128)(2,1)S(1)} %step3_kernel.1.q_prev), channel_id=1, source_target_pairs={{23,31},{10,26},{14,22},{16,24},{20,28},{17,25},{13,21},{9,1}} | collective-permute-start | bytes 786440 | tf_op jit(solution)/shard_map/ppermute | solution.py:133
  43.9 3.4 %collective-permute-start.24 = (bf16[1024,128]{1,0:T(8,128)(2,1)S(1)}, bf16[1024,128]{1,0:T(8,128)(2,1)S(1)}, u32[]{:S(2)}, u32[]{:S(2)}) collective-permute-start(bf16[1024,128]{1,0:T(8,128)(2,1)S(1)} %step3_kernel.1.q_prev), channel_id=1, source_target_pairs={{23,27},{10,18},{14,6},{17,29},{13,5}} | collective-permute-start | bytes 786440 | tf_op jit(solution)/shard_map/ppermute | solution.py:133
  44.6 2.7 %collective-permute-start.25 = (bf16[1024,128]{1,0:T(8,128)(2,1)S(1)}, bf16[1024,128]{1,0:T(8,128)(2,1)S(1)}, u32[]{:S(2)}, u32[]{:S(2)}) collective-permute-start(bf16[1024,128]{1,0:T(8,128)(2,1)S(1)} %step3_kernel.1.q_prev), channel_id=1, source_target_pairs={{23,19}} | collective-permute-start | bytes 786440 | tf_op jit(solution)/shard_map/ppermute | solution.py:133
  45.2 2.0 %collective-permute-start.26 = (bf16[1024,128]{1,0:T(8,128)(2,1)S(1)}, bf16[1024,128]{1,0:T(8,128)(2,1)S(1)}, u32[]{:S(2)}, u32[]{:S(2)}) collective-permute-start(bf16[1024,128]{1,0:T(8,128)(2,1)S(1)} %step3_kernel.1.q_prev), channel_id=1, source_target_pairs={{23,15}} | collective-permute-start | bytes 786440 | tf_op jit(solution)/shard_map/ppermute | solution.py:133
  47.4 30.8 %collective-permute-start.27 = (bf16[1040,128]{1,0:T(8,128)(2,1)S(1)}, bf16[1040,128]{1,0:T(8,128)(2,1)S(1)}, u32[]{:S(2)}, u32[]{:S(2)}) collective-permute-start(bf16[1040,128]{1,0:T(8,128)(2,1)S(1)} %get-tuple-element.48.refs_0_), channel_id=1, source_target_pairs={{0,2},{1,3},{2,0},{3,1},{4,6},{5,7},{6,4},{7,5},{8,10},{9,11},{10,... | collective-permute-start | bytes 798728 | tf_op jit(solution)/shard_map/ppermute | solution.py:129
  62.4 14.9 %collective-permute-start.28 = (bf16[1024,128]{1,0:T(8,128)(2,1)S(1)}, bf16[1024,128]{1,0:T(8,128)(2,1)S(1)}, u32[]{:S(2)}, u32[]{:S(2)}) collective-permute-start(bf16[1024,128]{1,0:T(8,128)(2,1)S(1)} %get-tuple-element.46.q_ref), channel_id=1, source_target_pairs={{15,11},{27,3},{31,7},{10,2}} | collective-permute-start | bytes 786440 | tf_op jit(solution)/shard_map/ppermute | solution.py:133
  78.2 1.5 %collective-permute-start.29 = (bf16[1040,128]{1,0:T(8,128)(2,1)S(1)}, bf16[1040,128]{1,0:T(8,128)(2,1)S(1)}, u32[]{:S(2)}, u32[]{:S(2)}) collective-permute-start(bf16[1040,128]{1,0:T(8,128)(2,1)S(1)} %get-tuple-element.48.refs_0_), channel_id=1, source_target_pairs={{0,1},{1,0},{2,3},{3,2},{4,5},{5,4},{6,7},{7,6},{8,9},{9,8},{10,11... | collective-permute-start | bytes 798728 | tf_op jit(solution)/shard_map/ppermute | solution.py:129
  78.2 1.9 %collective-permute-start.30 = (bf16[1040,128]{1,0:T(8,128)(2,1)S(1)}, bf16[1040,128]{1,0:T(8,128)(2,1)S(1)}, u32[]{:S(2)}, u32[]{:S(2)}) collective-permute-start(bf16[1040,128]{1,0:T(8,128)(2,1)S(1)} %collective-permute-done.27.refs_2_), channel_id=1, source_target_pairs={{0,1},{1,0},{2,3},{3,2},{4,5},{5,4},{6,7},{7,6},{8,9},{9,8},{10,11... | collective-permute-start | bytes 798728 | tf_op jit(solution)/shard_map/ppermute | solution.py:129
  (12 other events, 47.7 us)

commit v11 on v9

--- a/solution.py
+++ b/solution.py
@@ -69,16 +69,16 @@
 PARTNER = (None, (3, 1), (3, 3), (5, 2))
 PIECES = ((4, 0), (6, 2), (5, 1), (7, 3))
 SENDS = (
-    (1, 0, 3, 2),
+    (0, 1, 2, 3),
     (3, 1, 0, 2),
     (0, 1, 3, 2),
-    (2, 1, 0, 3),
+    (3, 1, 0, 2),
     (0, 1, 3, 2),
-    (2, 3, 0, 1),
+    (2, 0, 3, 1),
     (0, 3, 1, 2),
-    (1, 2, 0, 3),
+    (1, 3, 0, 2),
 )
-REST = ((2, 3), (3, 3), (0, 3), (1, 3), (0, 2), (1, 2))
+REST = ((2, 3), (0, 3), (1, 3), (0, 2))
 
 
 def hops(a, b):
@@ -178,7 +178,7 @@
             k = jnp.where((row == r) & (col == c), SENDS[r][c], k)
     for m in range(NR // 2):
 
-        @pl.when(row // 2 == m)
+        @pl.when(jnp.where((row == 1) & (k == 0), 1, row // 2) == m)
         def _():
             copy = pltpu.make_async_copy(diag_ref.at[k, :, pl.ds(0, pair_width(m, part))], cuts[m], sem)
             copy.start()
@@ -186,8 +186,7 @@
 
 
 def first_kernel(rhs_ref, diag_ref, *refs):
-    parts, out_ref = refs[: NR // 2], refs[NR // 2]
-    rhs_v, d_v, rhs_sem, d_sem = refs[NR // 2 + 1 :]
+    parts, (out_ref, rhs_v, d_v, rhs_sem, d_sem) = refs[:-5], refs[-5:]
     n = out_ref.shape[0] // 2
     col = lax.axis_index("col")
 
@@ -199,8 +198,9 @@
         def pieces(c):
             copies = []
             for i, r in enumerate(PIECES[c]):
-                wide = pair_width(r // 2, n)
-                source = parts[r // 2] if r else diag_ref.at[0, :, pl.ds(0, wide)]
+                m = max(r // 2, 1)
+                wide = pair_width(m, n)
+                source = parts[m - 1] if r else diag_ref.at[0, :, pl.ds(0, wide)]
                 copies.append(pltpu.make_async_copy(source, d_v.at[i, :, pl.ds(0, wide)], d_sem.at[i]))
             return copies
 
@@ -219,7 +219,7 @@
             def _():
                 for i, copy in enumerate(pieces(c)):
                     copy.wait()
-                    wide = pair_width(PIECES[c][i] // 2, n)
+                    wide = pair_width(max(PIECES[c][i] // 2, 1), n)
                     out_ref[i * n : (i + 1) * n] = low(dot(d_v[i, :, :wide], p[:wide]))
 
 
@@ -239,7 +239,7 @@
             copy.wait()
 
 
-def whole_kernel(diag_ref, even_ref, *refs):
+def whole_kernel(diag_ref, top_ref, even_ref, *refs):
     odd, out_ref, sem = refs[:-2], refs[-2], refs[-1]
     size = out_ref.shape[0]
     part = size // NR
@@ -256,9 +256,11 @@
             wide = pair_width(i // 2, part)
             if i % 2:
                 source = odd[i // 2]
-            else:
+            elif i:
                 source = even_ref.at[:, pl.ds(left, wide)]
                 left += wide
+            else:
+                source = top_ref
 
             @pl.when(row == i)
             def _():
@@ -326,6 +328,7 @@
     @pl.when(active)
     def _():
         lower_dot(q_ref, d_ref, p_in)
+        a_ref[...] = q_ref[...]
         s_ref[...] = low(dot(l_ref[...], q_ref[...]))
 
     @pl.when(beside)
@@ -341,19 +344,22 @@
         s_ref[...] = s_prev[...]
 
 
-def step3_kernel(took, a_ref, sum_ref, d_ref, q_prev, came_ref, q_ref, p_v):
-    active, taken = at(MAKER[3]), any_of(took)
+def step3_kernel(takers, sum_ref, a_ref, *refs):
+    came, (d_ref, q_prev, q_ref, p_v) = refs[:-4], refs[-4:]
+    active = at(MAKER[3])
 
     @pl.when(active)
     def _():
         p_v[...] = low(a_ref[...].astype(jnp.float32) - sum_ref[...].astype(jnp.float32))
         lower_dot(q_ref, d_ref, p_v)
 
-    @pl.when(taken)
-    def _():
-        q_ref[...] = came_ref[...]
-
-    @pl.when(jnp.logical_not(active | taken))
+    for devices, source in zip(takers, (a_ref, *came)):
+
+        @pl.when(any_of(devices))
+        def _():
+            q_ref[...] = source[...]
+
+    @pl.when(jnp.logical_not(active | any_of([d for devices in takers for d in devices])))
     def _():
         q_ref[...] = q_prev[...]
 
@@ -432,18 +438,18 @@
     parts = []
     for m, cut in enumerate(cuts):
         pairs = []
-        for r in (2 * m, 2 * m + 1):
+        for r in range(1, NR):
             for c, k in enumerate(SENDS[r]):
-                if k == 0 and r:
+                if k == 0 and max(r // 2, 1) == m:
                     pairs.append(((r, c), at_piece[r]))
-                if k and MAKER[k][0] != r:
+                if k and MAKER[k][0] != r and r // 2 == m:
                     pairs.append(((r, c), MAKER[k] if r % 2 else PARTNER[k]))
         parts.append(send_only(cut, pairs))
     q = call(
         first_kernel,
         jax.ShapeDtypeStruct((2 * part, width), bf16),
-        [rhs, diag_inv, *parts],
-        [HBM, HBM] + [ANY] * len(wides),
+        [rhs, diag_inv, *parts[1:]],
+        [HBM, HBM] + [ANY] * (len(wides) - 1),
         VMEM,
         [
             pltpu.VMEM((size, width), jnp.float32),
@@ -456,18 +462,20 @@
     got = [send(q, [((0, c), takers[(c + j) % 4]) for c in range(4) if (c + j) % 4 < 3]) for j in range(4)]
     even = call(
         pack_kernel,
-        jax.ShapeDtypeStruct((part, sum(wides)), bf16),
-        parts,
-        [ANY] * len(wides),
+        jax.ShapeDtypeStruct((part, sum(wides[1:])), bf16),
+        parts[1:],
+        [ANY] * (len(wides) - 1),
         VMEM,
-        [pltpu.SemaphoreType.DMA((len(wides),))],
+        [pltpu.SemaphoreType.DMA((len(wides) - 1,))],
     )
     even = send(even, [(PARTNER[k], MAKER[k]) for k in range(1, NC)])
+    top, _ = lax.optimization_barrier((cuts[0], q))
+    top = send(top, [((0, k), MAKER[k]) for k in range(1, NC)])
     diag = call(
         whole_kernel,
         jax.ShapeDtypeStruct((size, size), bf16),
-        [diag_inv, even, *parts],
-        [HBM] + [ANY] * (1 + len(wides)),
+        [diag_inv, top, even, *parts],
+        [HBM] + [ANY] * (2 + len(wides)),
         VMEM,
         [pltpu.SemaphoreType.DMA((NR,))],
     )
@@ -479,33 +487,34 @@
     p_in = send(p, [(MAKER[1], MAKER[2])])
     q_in = send(q, [(MAKER[1], BESIDE)])
 
-    p_in, spread = lax.optimization_barrier((p_in, q))
-    came = send(spread, [((2, 0), (4, 0)), ((3, 0), (5, 0)), ((1, 0), (0, 0)), ((2, 1), (4, 1))])
+    came = send(q, [((2, 0), (4, 0)), ((3, 0), (5, 0)), ((1, 0), (0, 0)), ((2, 1), (4, 1))])
     took = [(4, 0), (5, 0), (0, 0), (4, 1)]
+    p_in, came = lax.optimization_barrier((p_in, came))
 
     a, q, s = call(step2_kernel, [vec] * 3, [p_in, q_in, sums, rhs, diag, block, q, s], [VMEM] * 8, [VMEM] * 3)
-    sums = send_only(s, [(MAKER[2], MAKER[3])])
-    a = send_only(a, [(BESIDE, MAKER[3])])
-
+    sums = send(s, [(MAKER[2], MAKER[3])])
+    q_2 = a
+    a = send_only(a, [(BESIDE, MAKER[3]), (MAKER[2], (2, 2))])
+    q_2 = send_only(q_2, [(MAKER[2], (7, 2))])
     q = call(
-        functools.partial(step3_kernel, took),
+        functools.partial(step3_kernel, [[(2, 2)], [(7, 2)], took]),
         vec,
-        [a, sums, diag, q, came],
-        [VMEM] * 5,
+        [sums, a, q_2, came, diag, q],
+        [VMEM] * 6,
         VMEM,
         [pltpu.VMEM((size, width), bf16)],
     )
 
-    sends = [
-        [(MAKER[3], (6, 3)), ((4, 0), (6, 0)), ((5, 0), (7, 0)), ((4, 1), (6, 1)), ((3, 1), (5, 1)), ((2, 1), (0, 1))],
-        [(MAKER[3], (7, 3)), ((4, 1), (7, 1)), ((3, 1), (1, 1))],
-        [(MAKER[3], (4, 3))],
-        [],
-        [],
+    sends = [[(MAKER[3], (r, 3))] for r in (6, 7, 4)]
+    got = [send(q, pairs) for pairs in sends]
+    sends += [
+        [
+            (MAKER[3], (3, 3)), ((2, 2), (6, 2)), (MAKER[2], (5, 2)),
+            ((4, 0), (6, 0)), ((5, 0), (7, 0)), ((4, 1), (6, 1)), ((3, 1), (5, 1)), ((2, 1), (0, 1)),
+        ],
+        [((2, 2), (4, 2)), (MAKER[2], (1, 2)), ((4, 1), (7, 1)), ((3, 1), (1, 1))],
     ]
-    for pairs, r in zip(sends, (4, 6, 7, 5, 2)):
-        pairs.append((MAKER[2], (r, 2)))
-    got = [send_only(q, pairs) for pairs in sends]
+    got += [send_only(q, pairs) for pairs in sends[3:]]
     takers = [[b for _, b in pairs] for pairs in sends]
     q, mine = call(
         functools.partial(update_kernel, takers),
@@ -519,7 +528,7 @@
         return send(value, [((r, c), (r, c ^ step)) for r in range(NR) for c in range(NC)])
 
     across = swap(mine, 2)
-    rest = send_only(q, list(zip(((4, 3), (5, 3), (6, 3), (7, 3), (2, 2), MAKER[2]), REST)))
+    rest = send_only(q, list(zip(((3, 3), (6, 3), (7, 3), (2, 2)), REST)))
     solved = call(solved_kernel, jax.ShapeDtypeStruct((size, width), jnp.float32), [q, rest], [VMEM] * 2, VMEM)
     beside, across, solved = lax.optimization_barrier((mine, across, solved))
     beside = swap(beside, 1)

time: 71.3 us -> 69.9 us (0.980)
  waiting for transfers between devices: 21.8 us -> 15.8 us
  starting transfers between devices: 43.1 us -> 47.6 us
    ppermute x13 -> x18, starting transfers between devices: 29.1 us -> 37.8 us  [send(): lax.ppermute(value, ('row', 'col'), [(a * NC + b, c * NC + d) for (a, b),...]
    ppermute x12 -> x9, starting transfers between devices: 13.9 us -> 9.84 us  [send_only(): lax.ppermute(value, ('row', 'col'), [(a * NC + b, c * NC + d) for (a, b),...]
    ppermute x12 -> x9, waiting for transfers between devices: 15.5 us -> 11.7 us  [send_only(): lax.ppermute(value, ('row', 'col'), [(a * NC + b, c * NC + d) for (a, b),...]
    ppermute x13 -> x18, waiting for transfers between devices: 6.24 us -> 4.11 us  [send(): lax.ppermute(value, ('row', 'col'), [(a * NC + b, c * NC + d) for (a, b),...]
  transfers between devices with their start and end apart: 25 -> 27, of which waited for: 13 -> 11; matrix products, arithmetic and copies ran while one was open for 0% -> 0% of each run, Pallas kernels for 1% -> 1%
where the time goes in v11:
time: 69.9 us; the launch traced here: 69.6 us
  starting transfers between devices  47.6 us (68%)
  waiting for transfers between devices  15.8 us (23%)
  Pallas kernels  2.69 us (4%)
  between operations  2.19 us (3%)
  local copies, waits for them, and re-layouts  1.32 us (2%)
    ppermute x18, starting transfers between devices, send(): lax.ppermute(value, ('row', 'col'), [(a * NC + b, c * NC + d) for (a, b),...  37.8 us
    ppermute x9, waiting for transfers between devices, send_only(): lax.ppermute(value, ('row', 'col'), [(a * NC + b, c * NC + d) for (a, b),...  11.7 us
    ppermute x9, starting transfers between devices, send_only(): lax.ppermute(value, ('row', 'col'), [(a * NC + b, c * NC + d) for (a, b),...  9.84 us
    ppermute x18, waiting for transfers between devices, send(): lax.ppermute(value, ('row', 'col'), [(a * NC + b, c * NC + d) for (a, b),...  4.11 us
    pallas_call x11, Pallas kernels, call(): pl.pallas_call(kernel, out_shape=outs, in_specs=in_specs, out_specs=out_s...  2.69 us
  transfers between devices with their start and end apart: 27, of which 11 were waited for; matrix products, arithmetic and copies ran while one was open for 0% of the time, Pallas kernels for 1%

profile of v11, /device:TPU:7, one launch (start us, length us, event | category | flops | bytes accessed | tf_op | source)
XLA Modules:
  0.0 69.6 jit_solution(15920774646861246392)
XLA Ops:
  0.6 1.3 %copy-done.2 = bf16[4,128,1024]{2,1,0:T(8,128)(2,1)S(1)} copy-done((bf16[4,128,1024]{2,1,0:T(8,128)(2,1)S(1)}, bf16[4,128,1024]{2,1,0:T(8,128)(2,1)}, u32[]{:S(2)}) %copy-start.2) | copy-done | bytes 1048600
  2.0 0.8 %collective-permute-start.2 = (bf16[128,1024]{1,0:T(8,128)(2,1)S(1)}, bf16[128,1024]{1,0:T(8,128)(2,1)S(1)}, u32[]{:S(2)}, u32[]{:S(2)}) collective-permute-start(bf16[128,1024]{1,0:T(8,128)(2,1)S(1)} %get-tuple-element.25), channel_id=1, source_target_pairs={{24,1},{25,22},{26,13},{27,15},{28,9},{29,23},{30,3},{31,14}} | collective-permute-start | bytes 786440 | tf_op jit(solution)/shard_map/ppermute | solution.py:133
  2.8 0.8 %collective-permute-start.1 = (bf16[128,768]{1,0:T(8,128)(2,1)S(1)}, bf16[128,768]{1,0:T(8,128)(2,1)S(1)}, u32[]{:S(2)}, u32[]{:S(2)}) collective-permute-start(bf16[128,768]{1,0:T(8,128)(2,1)S(1)} %get-tuple-element.24), channel_id=1, source_target_pairs={{16,0},{17,13},{18,22},{19,15},{20,14},{21,2},{23,9}} | collective-permute-start | bytes 589832 | tf_op jit(solution)/shard_map/ppermute | solution.py:133
  3.6 0.7 collective-permute-start
  4.4 11.9 %collective-permute-start.10 = (bf16[128,2304]{1,0:T(8,128)(2,1)S(1)}, bf16[128,2304]{1,0:T(8,128)(2,1)S(1)}, u32[]{:S(2)}, u32[]{:S(2)}) collective-permute-start(bf16[128,2304]{1,0:T(8,128)(2,1)S(1)} %pack_kernel.1), channel_id=1, source_target_pairs={{0,1},{1,0},{2,3},{3,2},{4,5},{5,4},{6,7},{7,6},{8,12},{9,8},{10,1... | collective-permute-start | bytes 1769480 | tf_op jit(solution)/shard_map/ppermute | solution.py:129
  16.4 0.5 collective-permute-start.4
  17.0 0.4 collective-permute-start.6
  17.4 0.6 collective-permute-done.3.g0
  18.8 3.6 %collective-permute-start.11 = (bf16[128,256]{1,0:T(8,128)(2,1)S(1)}, bf16[128,256]{1,0:T(8,128)(2,1)S(1)}, u32[]{:S(2)}, u32[]{:S(2)}) collective-permute-start(bf16[128,256]{1,0:T(8,128)(2,1)S(1)} %get-tuple-element.29), channel_id=1, source_target_pairs={{4,23},{5,9},{7,14}} | collective-permute-start | bytes 196616 | tf_op jit(solution)/shard_map/ppermute | solution.py:133
  22.5 1.2 %collective-permute-done.11.refs_0_ = bf16[128,256]{1,0:T(8,128)(2,1)S(1)} collective-permute-done((bf16[128,256]{1,0:T(8,128)(2,1)S(1)}, bf16[128,256]{1,0:T(8,128)(2,1)S(1)}, u32[]{:S(2)}, u32[]{:S(2)}) %collective-permute-start.11) | collective-permute-done | bytes 65568 | tf_op jit(solution)/shard_map/ppermute | solution.py:133
  24.6 0.9 %collective-permute-done.12.p_in = bf16[1024,128]{1,0:T(8,128)(2,1)S(1)} collective-permute-done((bf16[1024,128]{1,0:T(8,128)(2,1)S(1)}, bf16[1024,128]{1,0:T(8,128)(2,1)S(1)}, u32[]{:S(2)}, u32[]{:S(2)}) %collective-permute-start.12) | collective-permute-done | bytes 262176 | tf_op jit(solution)/shard_map/ppermute | solution.py:129
  26.5 0.7 collective-permute-start.16
  27.2 0.7 collective-permute-start.17
  28.0 0.4 collective-permute-start.18
  28.9 0.7 collective-permute-start.21
  29.5 0.7 collective-permute-start.22
  31.7 20.2 %collective-permute-start.23 = (bf16[1040,128]{1,0:T(8,128)(2,1)S(1)}, bf16[1040,128]{1,0:T(8,128)(2,1)S(1)}, u32[]{:S(2)}, u32[]{:S(2)}) collective-permute-start(bf16[1040,128]{1,0:T(8,128)(2,1)S(1)} %get-tuple-element.42.refs_0_), channel_id=1, source_target_pairs={{0,2},{1,3},{2,0},{3,1},{4,6},{5,7},{6,4},{7,5},{8,10},{9,11},{10,... | collective-permute-start | bytes 798728 | tf_op jit(solution)/shard_map/ppermute | solution.py:129
  51.9 1.3 %collective-permute-start.24 = (bf16[1024,128]{1,0:T(8,128)(2,1)S(1)}, bf16[1024,128]{1,0:T(8,128)(2,1)S(1)}, u32[]{:S(2)}, u32[]{:S(2)}) collective-permute-start(bf16[1024,128]{1,0:T(8,128)(2,1)S(1)} %get-tuple-element.40.q_ref), channel_id=1, source_target_pairs={{15,11},{27,3},{31,7},{10,2}} | collective-permute-start | bytes 786440 | tf_op jit(solution)/shard_map/ppermute | solution.py:133
  53.2 10.4 %collective-permute-done.24.rest_ref = bf16[1024,128]{1,0:T(8,128)(2,1)S(1)} collective-permute-done((bf16[1024,128]{1,0:T(8,128)(2,1)S(1)}, bf16[1024,128]{1,0:T(8,128)(2,1)S(1)}, u32[]{:S(2)}, u32[]{:S(2)}) %collective-permute-start.24) | collective-permute-done | bytes 262176 | tf_op jit(solution)/shard_map/ppermute | solution.py:133
  63.6 0.8 %solved_kernel.1 = f32[1024,128]{1,0:T(8,128)} custom-call(bf16[1024,128]{1,0:T(8,128)(2,1)S(1)} %get-tuple-element.40.q_ref, bf16[1024,128]{1,0:T(8,128)(2,1)S(1)} %collective-permute-done.24.rest_ref), custom_call_target="tpu_custom_call" | custom-call | tf_op jit(solution)/shard_map/solved_kernel/pallas_call | solution.py:156
  64.5 2.2 %collective-permute-start.25 = (bf16[1040,128]{1,0:T(8,128)(2,1)S(1)}, bf16[1040,128]{1,0:T(8,128)(2,1)S(1)}, u32[]{:S(2)}, u32[]{:S(2)}) collective-permute-start(bf16[1040,128]{1,0:T(8,128)(2,1)S(1)} %get-tuple-element.42.refs_0_), channel_id=1, source_target_pairs={{0,1},{1,0},{2,3},{3,2},{4,5},{5,4},{6,7},{7,6},{8,9},{9,8},{10,11... | collective-permute-start | bytes 798728 | tf_op jit(solution)/shard_map/ppermute | solution.py:129
  66.7 1.2 %collective-permute-done.25.refs_1_ = bf16[1040,128]{1,0:T(8,128)(2,1)S(1)} collective-permute-done((bf16[1040,128]{1,0:T(8,128)(2,1)S(1)}, bf16[1040,128]{1,0:T(8,128)(2,1)S(1)}, u32[]{:S(2)}, u32[]{:S(2)}) %collective-permute-start.25) | collective-permute-done | bytes 266272 | tf_op jit(solution)/shard_map/ppermute | solution.py:129
  67.9 0.4 collective-permute-done.26.refs_3_
  68.2 1.4 %final_kernel.1 = f32[2,1024,128]{2,1,0:T(8,128)} custom-call(f32[2,1024,128]{2,1,0:T(8,128)S(1)} %bitcast.14, bf16[1040,128]{1,0:T(8,128)(2,1)S(1)} %get-tuple-element.42.refs_0_, bf16[1040,128]{1,0:T(8,128)(2,1)S(1)} %collective-permute-done.25.refs_1_, bf16[1040,128]{1,0:T(8,128)(2,1)S(1)} %collective-permute-done.23.refs_2_, ...), custom_call_target="tpu_custom_call" | custom-call | tf_op jit(solution)/shard_map/final_kernel/pallas_call | solution.py:156
  (49 shorter events, 3.9 us)
Async XLA Ops:
  2.0 2.3 %collective-permute-start.2 = (bf16[128,1024]{1,0:T(8,128)(2,1)S(1)}, bf16[128,1024]{1,0:T(8,128)(2,1)S(1)}, u32[]{:S(2)}, u32[]{:S(2)}) collective-permute-start(bf16[128,1024]{1,0:T(8,128)(2,1)S(1)} %get-tuple-element.25), channel_id=1, source_target_pairs={{24,1},{25,22},{26,13},{27,15},{28,9},{29,23},{30,3},{31,14}} | collective-permute-start | bytes 786440 | tf_op jit(solution)/shard_map/ppermute | solution.py:133
  2.8 1.5 %collective-permute-start.1 = (bf16[128,768]{1,0:T(8,128)(2,1)S(1)}, bf16[128,768]{1,0:T(8,128)(2,1)S(1)}, u32[]{:S(2)}, u32[]{:S(2)}) collective-permute-start(bf16[128,768]{1,0:T(8,128)(2,1)S(1)} %get-tuple-element.24), channel_id=1, source_target_pairs={{16,0},{17,13},{18,22},{19,15},{20,14},{21,2},{23,9}} | collective-permute-start | bytes 589832 | tf_op jit(solution)/shard_map/ppermute | solution.py:133
  4.4 19.3 %collective-permute-start.10 = (bf16[128,2304]{1,0:T(8,128)(2,1)S(1)}, bf16[128,2304]{1,0:T(8,128)(2,1)S(1)}, u32[]{:S(2)}, u32[]{:S(2)}) collective-permute-start(bf16[128,2304]{1,0:T(8,128)(2,1)S(1)} %pack_kernel.1), channel_id=1, source_target_pairs={{0,1},{1,0},{2,3},{3,2},{4,5},{5,4},{6,7},{7,6},{8,12},{9,8},{10,1... | collective-permute-start | bytes 1769480 | tf_op jit(solution)/shard_map/ppermute | solution.py:129
  16.3 1.7 %collective-permute-start.3 = (bf16[256,128]{1,0:T(8,128)(2,1)S(1)}, bf16[256,128]{1,0:T(8,128)(2,1)S(1)}, u32[]{:S(2)}, u32[]{:S(2)}) collective-permute-start(bf16[256,128]{1,0:T(8,128)(2,1)S(1)} %first_kernel.1), channel_id=1, source_target_pairs={{0,4},{1,8},{2,12},{3,2},{4,5},{5,0},{6,7},{7,6},{8,9},{9,1},{10,1... | collective-permute-start | bytes 196616 | tf_op jit(solution)/shard_map/ppermute | solution.py:129
  16.4 1.6 %collective-permute-start.4 = (bf16[256,128]{1,0:T(8,128)(2,1)S(1)}, bf16[256,128]{1,0:T(8,128)(2,1)S(1)}, u32[]{:S(2)}, u32[]{:S(2)}) collective-permute-start(bf16[256,128]{1,0:T(8,128)(2,1)S(1)} %first_kernel.1), channel_id=1, source_target_pairs={{0,8},{1,12},{2,3},{3,4},{4,5},{5,0},{6,7},{7,6},{8,9},{9,1},{10,1... | collective-permute-start | bytes 196616 | tf_op jit(solution)/shard_map/ppermute | solution.py:129
  17.0 1.3 %collective-permute-start.6 = (bf16[256,128]{1,0:T(8,128)(2,1)S(1)}, bf16[256,128]{1,0:T(8,128)(2,1)S(1)}, u32[]{:S(2)}, u32[]{:S(2)}) collective-permute-start(bf16[256,128]{1,0:T(8,128)(2,1)S(1)} %first_kernel.1), channel_id=1, source_target_pairs={{0,1},{1,4},{2,8},{3,12},{4,5},{5,0},{6,7},{7,6},{8,9},{9,2},{10,1... | collective-permute-start | bytes 196616 | tf_op jit(solution)/shard_map/ppermute | solution.py:129
  18.3 5.5 %collective-permute-start.8 = (bf16[1024,128]{1,0:T(8,128)(2,1)S(1)}, bf16[1024,128]{1,0:T(8,128)(2,1)S(1)}, u32[]{:S(2)}, u32[]{:S(2)}) collective-permute-start(bf16[1024,128]{1,0:T(8,128)(2,1)S(1)} %get-tuple-element.27.s_prev), channel_id=1, source_target_pairs={{0,1},{1,0},{2,3},{3,2},{4,5},{5,4},{6,7},{7,6},{8,9},{9,8},{10,11... | collective-permute-start | bytes 786440 | tf_op jit(solution)/shard_map/ppermute | solution.py:129
  18.7 5.2 %collective-permute-start.7 = (bf16[1024,128]{1,0:T(8,128)(2,1)S(1)}, bf16[1024,128]{1,0:T(8,128)(2,1)S(1)}, u32[]{:S(2)}, u32[]{:S(2)}) collective-permute-start(bf16[1024,128]{1,0:T(8,128)(2,1)S(1)} %get-tuple-element.26), channel_id=1, source_target_pairs={{0,1},{1,0},{2,3},{3,2},{4,9},{5,4},{6,7},{7,6},{8,5},{9,8},{10,11... | collective-permute-start | bytes 786440 | tf_op jit(solution)/shard_map/ppermute | solution.py:129
  18.8 4.9 %collective-permute-start.11 = (bf16[128,256]{1,0:T(8,128)(2,1)S(1)}, bf16[128,256]{1,0:T(8,128)(2,1)S(1)}, u32[]{:S(2)}, u32[]{:S(2)}) collective-permute-start(bf16[128,256]{1,0:T(8,128)(2,1)S(1)} %get-tuple-element.29), channel_id=1, source_target_pairs={{4,23},{5,9},{7,14}} | collective-permute-start | bytes 196616 | tf_op jit(solution)/shard_map/ppermute | solution.py:133
  22.4 1.3 %collective-permute-start.9 = (bf16[128,256]{1,0:T(8,128)(2,1)S(1)}, bf16[128,256]{1,0:T(8,128)(2,1)S(1)}, u32[]{:S(2)}, u32[]{:S(2)}) collective-permute-start(bf16[128,256]{1,0:T(8,128)(2,1)S(1)} %get-tuple-element.29), channel_id=1, source_target_pairs={{0,1},{1,9},{2,14},{3,23},{4,5},{5,4},{6,7},{7,6},{8,0},{9,8},{10,... | collective-permute-start | bytes 196616 | tf_op jit(solution)/shard_map/ppermute | solution.py:129
  23.9 1.6 %collective-permute-start.12 = (bf16[1024,128]{1,0:T(8,128)(2,1)S(1)}, bf16[1024,128]{1,0:T(8,128)(2,1)S(1)}, u32[]{:S(2)}, u32[]{:S(2)}) collective-permute-start(bf16[1024,128]{1,0:T(8,128)(2,1)S(1)} %get-tuple-element.31), channel_id=1, source_target_pairs={{0,1},{1,0},{2,3},{3,2},{4,5},{5,4},{6,7},{7,6},{8,9},{9,14},{10,1... | collective-permute-start | bytes 786440 | tf_op jit(solution)/shard_map/ppermute | solution.py:129
  24.1 1.8 %collective-permute-start.13 = (bf16[1024,128]{1,0:T(8,128)(2,1)S(1)}, bf16[1024,128]{1,0:T(8,128)(2,1)S(1)}, u32[]{:S(2)}, u32[]{:S(2)}) collective-permute-start(bf16[1024,128]{1,0:T(8,128)(2,1)S(1)} %get-tuple-element.32.q_prev), channel_id=1, source_target_pairs={{0,1},{1,5},{2,3},{3,2},{4,0},{5,4},{6,7},{7,6},{8,16},{9,17},{10,... | collective-permute-start | bytes 786440 | tf_op jit(solution)/shard_map/ppermute | solution.py:129
  24.5 1.8 %collective-permute-start.14 = (bf16[1024,128]{1,0:T(8,128)(2,1)S(1)}, bf16[1024,128]{1,0:T(8,128)(2,1)S(1)}, u32[]{:S(2)}, u32[]{:S(2)}) collective-permute-start(bf16[1024,128]{1,0:T(8,128)(2,1)S(1)} %get-tuple-element.32.q_prev), channel_id=1, source_target_pairs={{0,1},{1,0},{2,3},{3,2},{4,5},{5,4},{6,7},{7,6},{8,9},{9,13},{10,1... | collective-permute-start | bytes 786440 | tf_op jit(solution)/shard_map/ppermute | solution.py:129
  26.3 1.6 %collective-permute-start.15 = (bf16[1024,128]{1,0:T(8,128)(2,1)S(1)}, bf16[1024,128]{1,0:T(8,128)(2,1)S(1)}, u32[]{:S(2)}, u32[]{:S(2)}) collective-permute-start(bf16[1024,128]{1,0:T(8,128)(2,1)S(1)} %get-tuple-element.35.s_ref), channel_id=1, source_target_pairs={{0,1},{1,0},{2,3},{3,2},{4,5},{5,4},{6,7},{7,6},{8,9},{9,8},{10,11... | collective-permute-start | bytes 786440 | tf_op jit(solution)/shard_map/ppermute | solution.py:129
  26.5 1.4 %collective-permute-start.16 = (bf16[1024,128]{1,0:T(8,128)(2,1)S(1)}, bf16[1024,128]{1,0:T(8,128)(2,1)S(1)}, u32[]{:S(2)}, u32[]{:S(2)}) collective-permute-start(bf16[1024,128]{1,0:T(8,128)(2,1)S(1)} %get-tuple-element.36), channel_id=1, source_target_pairs={{13,23},{14,10}} | collective-permute-start | bytes 786440 | tf_op jit(solution)/shard_map/ppermute | solution.py:133
  28.0 3.6 %collective-permute-start.18 = (bf16[1024,128]{1,0:T(8,128)(2,1)S(1)}, bf16[1024,128]{1,0:T(8,128)(2,1)S(1)}, u32[]{:S(2)}, u32[]{:S(2)}) collective-permute-start(bf16[1024,128]{1,0:T(8,128)(2,1)S(1)} %step3_kernel.1.q_prev), channel_id=1, source_target_pairs={{0,1},{1,0},{2,3},{3,2},{4,5},{5,4},{6,7},{7,6},{8,9},{9,8},{10,11... | collective-permute-start | bytes 786440 | tf_op jit(solution)/shard_map/ppermute | solution.py:129
  28.4 3.2 %collective-permute-start.19 = (bf16[1024,128]{1,0:T(8,128)(2,1)S(1)}, bf16[1024,128]{1,0:T(8,128)(2,1)S(1)}, u32[]{:S(2)}, u32[]{:S(2)}) collective-permute-start(bf16[1024,128]{1,0:T(8,128)(2,1)S(1)} %step3_kernel.1.q_prev), channel_id=1, source_target_pairs={{0,1},{1,0},{2,3},{3,2},{4,5},{5,4},{6,7},{7,6},{8,9},{9,8},{10,11... | collective-permute-start | bytes 786440 | tf_op jit(solution)/shard_map/ppermute | solution.py:129
  28.5 3.0 %collective-permute-start.20 = (bf16[1024,128]{1,0:T(8,128)(2,1)S(1)}, bf16[1024,128]{1,0:T(8,128)(2,1)S(1)}, u32[]{:S(2)}, u32[]{:S(2)}) collective-permute-start(bf16[1024,128]{1,0:T(8,128)(2,1)S(1)} %step3_kernel.1.q_prev), channel_id=1, source_target_pairs={{0,1},{1,0},{2,3},{3,2},{4,5},{5,4},{6,7},{7,6},{8,9},{9,8},{10,11... | collective-permute-start | bytes 786440 | tf_op jit(solution)/shard_map/ppermute | solution.py:129
  28.9 2.7 %collective-permute-start.21 = (bf16[1024,128]{1,0:T(8,128)(2,1)S(1)}, bf16[1024,128]{1,0:T(8,128)(2,1)S(1)}, u32[]{:S(2)}, u32[]{:S(2)}) collective-permute-start(bf16[1024,128]{1,0:T(8,128)(2,1)S(1)} %step3_kernel.1.q_prev), channel_id=1, source_target_pairs={{23,15},{10,26},{14,22},{16,24},{20,28},{17,25},{13,21},{9,1}} | collective-permute-start | bytes 786440 | tf_op jit(solution)/shard_map/ppermute | solution.py:133
  29.5 2.0 %collective-permute-start.22 = (bf16[1024,128]{1,0:T(8,128)(2,1)S(1)}, bf16[1024,128]{1,0:T(8,128)(2,1)S(1)}, u32[]{:S(2)}, u32[]{:S(2)}) collective-permute-start(bf16[1024,128]{1,0:T(8,128)(2,1)S(1)} %step3_kernel.1.q_prev), channel_id=1, source_target_pairs={{10,18},{14,6},{17,29},{13,5}} | collective-permute-start | bytes 786440 | tf_op jit(solution)/shard_map/ppermute | solution.py:133
  31.7 32.7 %collective-permute-start.23 = (bf16[1040,128]{1,0:T(8,128)(2,1)S(1)}, bf16[1040,128]{1,0:T(8,128)(2,1)S(1)}, u32[]{:S(2)}, u32[]{:S(2)}) collective-permute-start(bf16[1040,128]{1,0:T(8,128)(2,1)S(1)} %get-tuple-element.42.refs_0_), channel_id=1, source_target_pairs={{0,2},{1,3},{2,0},{3,1},{4,6},{5,7},{6,4},{7,5},{8,10},{9,11},{10,... | collective-permute-start | bytes 798728 | tf_op jit(solution)/shard_map/ppermute | solution.py:129
  51.9 11.7 %collective-permute-start.24 = (bf16[1024,128]{1,0:T(8,128)(2,1)S(1)}, bf16[1024,128]{1,0:T(8,128)(2,1)S(1)}, u32[]{:S(2)}, u32[]{:S(2)}) collective-permute-start(bf16[1024,128]{1,0:T(8,128)(2,1)S(1)} %get-tuple-element.40.q_ref), channel_id=1, source_target_pairs={{15,11},{27,3},{31,7},{10,2}} | collective-permute-start | bytes 786440 | tf_op jit(solution)/shard_map/ppermute | solution.py:133
  64.5 3.4 %collective-permute-start.25 = (bf16[1040,128]{1,0:T(8,128)(2,1)S(1)}, bf16[1040,128]{1,0:T(8,128)(2,1)S(1)}, u32[]{:S(2)}, u32[]{:S(2)}) collective-permute-start(bf16[1040,128]{1,0:T(8,128)(2,1)S(1)} %get-tuple-element.42.refs_0_), channel_id=1, source_target_pairs={{0,1},{1,0},{2,3},{3,2},{4,5},{5,4},{6,7},{7,6},{8,9},{9,8},{10,11... | collective-permute-start | bytes 798728 | tf_op jit(solution)/shard_map/ppermute | solution.py:129
  66.7 1.5 %collective-permute-start.26 = (bf16[1040,128]{1,0:T(8,128)(2,1)S(1)}, bf16[1040,128]{1,0:T(8,128)(2,1)S(1)}, u32[]{:S(2)}, u32[]{:S(2)}) collective-permute-start(bf16[1040,128]{1,0:T(8,128)(2,1)S(1)} %collective-permute-done.23.refs_2_), channel_id=1, source_target_pairs={{0,1},{1,0},{2,3},{3,2},{4,5},{5,4},{6,7},{7,6},{8,9},{9,8},{10,11... | collective-permute-start | bytes 798728 | tf_op jit(solution)/shard_map/ppermute | solution.py:129
  (7 other events, 50.2 us)

commit v12 on v11

--- a/solution.py
+++ b/solution.py
@@ -67,18 +67,18 @@
 FIRST = (1, 0)
 BESIDE = (3, 1)
 PARTNER = (None, (3, 1), (3, 3), (5, 2))
-PIECES = ((4, 0), (6, 2), (5, 1), (7, 3))
+PIECES = ((4, 1), (6, 3), (5, 2), (7, 0))
 SENDS = (
+    (0, 1, 2, 3),
     (0, 1, 2, 3),
     (3, 1, 0, 2),
     (0, 1, 3, 2),
-    (3, 1, 0, 2),
     (0, 1, 3, 2),
-    (2, 0, 3, 1),
+    (2, 1, 3, 0),
     (0, 3, 1, 2),
     (1, 3, 0, 2),
 )
-REST = ((2, 3), (0, 3), (1, 3), (0, 2))
+REST = ((2, 3), (0, 3), (0, 2), (1, 2))
 
 
 def hops(a, b):
@@ -224,7 +224,7 @@
 
 
 def pack_kernel(*refs):
-    parts, out_ref, sem = refs[:-2], refs[-2], refs[-1]
+    parts, out_ref, sem = refs[1:-2], refs[-2], refs[-1]
 
     @pl.when(any_of(PARTNER[1:]))
     def _():
@@ -306,19 +306,29 @@
         p_ref[...] = low(rhs_ref[0] - s)
 
 
-def step1_kernel(p_in, sum_ref, rhs_ref, d_ref, l_ref, q_prev, s_prev, p_ref, q_ref, s_ref):
+def step1_kernel(p_in, d_ref, q_prev, q_ref):
     active = at(MAKER[1])
 
     @pl.when(active)
     def _():
         lower_dot(q_ref, d_ref, p_in)
-        s = dot(l_ref[...], q_ref[...]) + sum_ref[...].astype(jnp.float32)
+
+    @pl.when(jnp.logical_not(active))
+    def _():
+        q_ref[...] = q_prev[...]
+
+
+def step1_sum_kernel(q_in, sum_ref, rhs_ref, l_ref, s_prev, p_ref, s_ref):
+    active = at(MAKER[1])
+
+    @pl.when(active)
+    def _():
+        s = dot(l_ref[...], q_in[...]) + sum_ref[...].astype(jnp.float32)
         s_ref[...] = low(s)
         p_ref[...] = low(rhs_ref[0] - s)
 
     @pl.when(jnp.logical_not(active))
     def _():
-        q_ref[...] = q_prev[...]
         s_ref[...] = s_prev[...]
 
 
@@ -463,8 +473,8 @@
     even = call(
         pack_kernel,
         jax.ShapeDtypeStruct((part, sum(wides[1:])), bf16),
-        parts[1:],
-        [ANY] * (len(wides) - 1),
+        parts,
+        [ANY] * len(wides),
         VMEM,
         [pltpu.SemaphoreType.DMA((len(wides) - 1,))],
     )
@@ -483,7 +493,8 @@
     p, q, s = call(step0_kernel, [vec] * 3, [*got, rhs, block], [VMEM] * 6, [VMEM] * 3)
     p_in = send(p, [(FIRST, MAKER[1])])
     sums = send(s, [((2, 0), MAKER[1]), ((3, 0), BESIDE)])
-    p, q, s = call(step1_kernel, [vec] * 3, [p_in, sums, rhs, diag, block, q, s], [VMEM] * 7, [VMEM] * 3)
+    q = call(step1_kernel, vec, [p_in, diag, q], [VMEM] * 3, VMEM)
+    p, s = call(step1_sum_kernel, [vec] * 2, [q, sums, rhs, block, s], [VMEM] * 5, [VMEM] * 2)
     p_in = send(p, [(MAKER[1], MAKER[2])])
     q_in = send(q, [(MAKER[1], BESIDE)])
 
@@ -493,14 +504,12 @@
 
     a, q, s = call(step2_kernel, [vec] * 3, [p_in, q_in, sums, rhs, diag, block, q, s], [VMEM] * 8, [VMEM] * 3)
     sums = send(s, [(MAKER[2], MAKER[3])])
-    q_2 = a
     a = send_only(a, [(BESIDE, MAKER[3]), (MAKER[2], (2, 2))])
-    q_2 = send_only(q_2, [(MAKER[2], (7, 2))])
     q = call(
-        functools.partial(step3_kernel, [[(2, 2)], [(7, 2)], took]),
+        functools.partial(step3_kernel, [[(2, 2)], took]),
         vec,
-        [sums, a, q_2, came, diag, q],
-        [VMEM] * 6,
+        [sums, a, came, diag, q],
+        [VMEM] * 5,
         VMEM,
         [pltpu.VMEM((size, width), bf16)],
     )
@@ -509,10 +518,10 @@
     got = [send(q, pairs) for pairs in sends]
     sends += [
         [
-            (MAKER[3], (3, 3)), ((2, 2), (6, 2)), (MAKER[2], (5, 2)),
+            (MAKER[3], (3, 3)), ((2, 2), (6, 2)), (MAKER[2], (7, 2)),
             ((4, 0), (6, 0)), ((5, 0), (7, 0)), ((4, 1), (6, 1)), ((3, 1), (5, 1)), ((2, 1), (0, 1)),
         ],
-        [((2, 2), (4, 2)), (MAKER[2], (1, 2)), ((4, 1), (7, 1)), ((3, 1), (1, 1))],
+        [(MAKER[3], (1, 3)), ((2, 2), (4, 2)), (MAKER[2], (5, 2)), ((4, 1), (7, 1)), ((3, 1), (1, 1))],
     ]
     got += [send_only(q, pairs) for pairs in sends[3:]]
     takers = [[b for _, b in pairs] for pairs in sends]
@@ -528,7 +537,7 @@
         return send(value, [((r, c), (r, c ^ step)) for r in range(NR) for c in range(NC)])
 
     across = swap(mine, 2)
-    rest = send_only(q, list(zip(((3, 3), (6, 3), (7, 3), (2, 2)), REST)))
+    rest = send_only(q, list(zip(((3, 3), (1, 3), (2, 2), MAKER[2]), REST)))
     solved = call(solved_kernel, jax.ShapeDtypeStruct((size, width), jnp.float32), [q, rest], [VMEM] * 2, VMEM)
     beside, across, solved = lax.optimization_barrier((mine, across, solved))
     beside = swap(beside, 1)

time: 69.9 us -> 68.1 us (0.974)
  starting transfers between devices: 47.6 us -> 23.7 us
  waiting for transfers between devices: 15.8 us -> 38.1 us
    ppermute x18, starting transfers between devices: 37.8 us -> 10.9 us  [send(): lax.ppermute(value, ('row', 'col'), [(a * NC + b, c * NC + d) for (a, b),...]
    ppermute x9 -> x8, waiting for transfers between devices: 11.7 us -> 32.6 us  [send_only(): lax.ppermute(value, ('row', 'col'), [(a * NC + b, c * NC + d) for (a, b),...]
    ppermute x9 -> x8, starting transfers between devices: 9.84 us -> 12.9 us  [send_only(): lax.ppermute(value, ('row', 'col'), [(a * NC + b, c * NC + d) for (a, b),...]
    ppermute x18, waiting for transfers between devices: 4.11 us -> 5.53 us  [send(): lax.ppermute(value, ('row', 'col'), [(a * NC + b, c * NC + d) for (a, b),...]
    pallas_call x11 -> x12, Pallas kernels: 2.69 us -> 2.58 us  [call(): pl.pallas_call(kernel, out_shape=outs, in_specs=in_specs, out_specs=out_s...]
  transfers between devices with their start and end apart: 27 -> 26, of which waited for: 11 -> 14; matrix products, arithmetic and copies ran while one was open for 0% -> 0% of each run, Pallas kernels for 1% -> 1%
where the time goes in v12:
time: 68.1 us; the launch traced here: 67.9 us
  waiting for transfers between devices  38.1 us (56%)
  starting transfers between devices  23.7 us (35%)
  Pallas kernels  2.58 us (4%)
  between operations  2.15 us (3%)
  local copies, waits for them, and re-layouts  1.32 us (2%)
    ppermute x8, waiting for transfers between devices, send_only(): lax.ppermute(value, ('row', 'col'), [(a * NC + b, c * NC + d) for (a, b),...  32.6 us
    ppermute x8, starting transfers between devices, send_only(): lax.ppermute(value, ('row', 'col'), [(a * NC + b, c * NC + d) for (a, b),...  12.9 us
    ppermute x18, starting transfers between devices, send(): lax.ppermute(value, ('row', 'col'), [(a * NC + b, c * NC + d) for (a, b),...  10.9 us
    ppermute x18, waiting for transfers between devices, send(): lax.ppermute(value, ('row', 'col'), [(a * NC + b, c * NC + d) for (a, b),...  5.53 us
    pallas_call x12, Pallas kernels, call(): pl.pallas_call(kernel, out_shape=outs, in_specs=in_specs, out_specs=out_s...  2.58 us
  transfers between devices with their start and end apart: 26, of which 14 were waited for; matrix products, arithmetic and copies ran while one was open for 0% of the time, Pallas kernels for 1%

profile of v12, /device:TPU:7, one launch (start us, length us, event | category | flops | bytes accessed | tf_op | source)
XLA Modules:
  0.0 67.9 jit_solution(15348008974705592314)
XLA Ops:
  0.6 1.3 %copy-done.2 = bf16[4,128,1024]{2,1,0:T(8,128)(2,1)S(1)} copy-done((bf16[4,128,1024]{2,1,0:T(8,128)(2,1)S(1)}, bf16[4,128,1024]{2,1,0:T(8,128)(2,1)}, u32[]{:S(2)}) %copy-start.2) | copy-done | bytes 1048600
  2.0 0.8 %collective-permute-start.2 = (bf16[128,1024]{1,0:T(8,128)(2,1)S(1)}, bf16[128,1024]{1,0:T(8,128)(2,1)S(1)}, u32[]{:S(2)}, u32[]{:S(2)}) collective-permute-start(bf16[128,1024]{1,0:T(8,128)(2,1)S(1)} %get-tuple-element.24), channel_id=1, source_target_pairs={{24,1},{25,22},{26,13},{27,15},{28,9},{29,23},{30,3},{31,14}} | collective-permute-start | bytes 786440 | tf_op jit(solution)/shard_map/ppermute | solution.py:133
  2.8 0.8 %collective-permute-start.1 = (bf16[128,768]{1,0:T(8,128)(2,1)S(1)}, bf16[128,768]{1,0:T(8,128)(2,1)S(1)}, u32[]{:S(2)}, u32[]{:S(2)}) collective-permute-start(bf16[128,768]{1,0:T(8,128)(2,1)S(1)} %get-tuple-element.23), channel_id=1, source_target_pairs={{16,0},{17,13},{18,22},{19,15},{20,14},{21,9},{23,2}} | collective-permute-start | bytes 589832 | tf_op jit(solution)/shard_map/ppermute | solution.py:133
  3.6 0.7 collective-permute-start
  4.3 6.6 %collective-permute-start.9 = (bf16[128,256]{1,0:T(8,128)(2,1)S(1)}, bf16[128,256]{1,0:T(8,128)(2,1)S(1)}, u32[]{:S(2)}, u32[]{:S(2)}) collective-permute-start(bf16[128,256]{1,0:T(8,128)(2,1)S(1)} %get-tuple-element.27), channel_id=1, source_target_pairs={{5,9},{6,14},{7,23}} | collective-permute-start | bytes 196616 | tf_op jit(solution)/shard_map/ppermute | solution.py:133
  11.0 1.3 %collective-permute-done.9.refs_0_ = bf16[128,256]{1,0:T(8,128)(2,1)S(1)} collective-permute-done((bf16[128,256]{1,0:T(8,128)(2,1)S(1)}, bf16[128,256]{1,0:T(8,128)(2,1)S(1)}, u32[]{:S(2)}, u32[]{:S(2)}) %collective-permute-start.9) | collective-permute-done | bytes 65568 | tf_op jit(solution)/shard_map/ppermute | solution.py:133
  12.3 2.2 %collective-permute-start.10 = (bf16[128,2304]{1,0:T(8,128)(2,1)S(1)}, bf16[128,2304]{1,0:T(8,128)(2,1)S(1)}, u32[]{:S(2)}, u32[]{:S(2)}) collective-permute-start(bf16[128,2304]{1,0:T(8,128)(2,1)S(1)} %pack_kernel.1), channel_id=1, source_target_pairs={{0,1},{1,0},{2,3},{3,2},{4,5},{5,4},{6,7},{7,6},{8,12},{9,8},{10,1... | collective-permute-start | bytes 1769480 | tf_op jit(solution)/shard_map/ppermute | solution.py:129
  14.7 0.5 collective-permute-start.4
  15.3 0.4 collective-permute-start.6
  15.7 0.6 collective-permute-done.3.g0
  17.5 1.1 %collective-permute-done.8.top_ref = bf16[128,256]{1,0:T(8,128)(2,1)S(1)} collective-permute-done((bf16[128,256]{1,0:T(8,128)(2,1)S(1)}, bf16[128,256]{1,0:T(8,128)(2,1)S(1)}, u32[]{:S(2)}, u32[]{:S(2)}) %collective-permute-start.8) | collective-permute-done | bytes 65568 | tf_op jit(solution)/shard_map/ppermute | solution.py:129
  18.8 0.4 collective-permute-start.12
  19.8 0.7 collective-permute-done.12.p_in
  21.6 0.7 collective-permute-start.16
  22.3 0.5 collective-permute-done.15.sum_ref
  23.7 0.7 collective-permute-start.20
  24.4 1.3 %collective-permute-start.21 = (bf16[1024,128]{1,0:T(8,128)(2,1)S(1)}, bf16[1024,128]{1,0:T(8,128)(2,1)S(1)}, u32[]{:S(2)}, u32[]{:S(2)}) collective-permute-start(bf16[1024,128]{1,0:T(8,128)(2,1)S(1)} %step3_kernel.1.q_prev), channel_id=1, source_target_pairs={{23,7},{10,18},{14,22},{17,29},{13,5}} | collective-permute-start | bytes 786440 | tf_op jit(solution)/shard_map/ppermute | solution.py:133
  27.0 27.9 %collective-permute-done.21.refs_4_ = bf16[1024,128]{1,0:T(8,128)(2,1)S(1)} collective-permute-done((bf16[1024,128]{1,0:T(8,128)(2,1)S(1)}, bf16[1024,128]{1,0:T(8,128)(2,1)S(1)}, u32[]{:S(2)}, u32[]{:S(2)}) %collective-permute-start.21) | collective-permute-done | bytes 262176 | tf_op jit(solution)/shard_map/ppermute | solution.py:133
  55.1 1.3 %collective-permute-start.23 = (bf16[1024,128]{1,0:T(8,128)(2,1)S(1)}, bf16[1024,128]{1,0:T(8,128)(2,1)S(1)}, u32[]{:S(2)}, u32[]{:S(2)}) collective-permute-start(bf16[1024,128]{1,0:T(8,128)(2,1)S(1)} %get-tuple-element.38.q_ref), channel_id=1, source_target_pairs={{15,11},{7,3},{10,2},{14,6}} | collective-permute-start | bytes 786440 | tf_op jit(solution)/shard_map/ppermute | solution.py:133
  56.4 3.3 %collective-permute-done.23.rest_ref = bf16[1024,128]{1,0:T(8,128)(2,1)S(1)} collective-permute-done((bf16[1024,128]{1,0:T(8,128)(2,1)S(1)}, bf16[1024,128]{1,0:T(8,128)(2,1)S(1)}, u32[]{:S(2)}, u32[]{:S(2)}) %collective-permute-start.23) | collective-permute-done | bytes 262176 | tf_op jit(solution)/shard_map/ppermute | solution.py:133
  59.7 0.8 %solved_kernel.1 = f32[1024,128]{1,0:T(8,128)} custom-call(bf16[1024,128]{1,0:T(8,128)(2,1)S(1)} %get-tuple-element.38.q_ref, bf16[1024,128]{1,0:T(8,128)(2,1)S(1)} %collective-permute-done.23.rest_ref), custom_call_target="tpu_custom_call" | custom-call | tf_op jit(solution)/shard_map/solved_kernel/pallas_call | solution.py:156
  60.6 4.4 %collective-permute-start.24 = (bf16[1040,128]{1,0:T(8,128)(2,1)S(1)}, bf16[1040,128]{1,0:T(8,128)(2,1)S(1)}, u32[]{:S(2)}, u32[]{:S(2)}) collective-permute-start(bf16[1040,128]{1,0:T(8,128)(2,1)S(1)} %get-tuple-element.40.refs_0_), channel_id=1, source_target_pairs={{0,1},{1,0},{2,3},{3,2},{4,5},{5,4},{6,7},{7,6},{8,9},{9,8},{10,11... | collective-permute-start | bytes 798728 | tf_op jit(solution)/shard_map/ppermute | solution.py:129
  64.9 1.2 %collective-permute-done.24.refs_1_ = bf16[1040,128]{1,0:T(8,128)(2,1)S(1)} collective-permute-done((bf16[1040,128]{1,0:T(8,128)(2,1)S(1)}, bf16[1040,128]{1,0:T(8,128)(2,1)S(1)}, u32[]{:S(2)}, u32[]{:S(2)}) %collective-permute-start.24) | collective-permute-done | bytes 266272 | tf_op jit(solution)/shard_map/ppermute | solution.py:129
  66.5 1.4 %final_kernel.1 = f32[2,1024,128]{2,1,0:T(8,128)} custom-call(f32[2,1024,128]{2,1,0:T(8,128)S(1)} %bitcast.14, bf16[1040,128]{1,0:T(8,128)(2,1)S(1)} %get-tuple-element.40.refs_0_, bf16[1040,128]{1,0:T(8,128)(2,1)S(1)} %collective-permute-done.24.refs_1_, bf16[1040,128]{1,0:T(8,128)(2,1)S(1)} %collective-permute-done.22.refs_2_, ...), custom_call_target="tpu_custom_call" | custom-call | tf_op jit(solution)/shard_map/final_kernel/pallas_call | solution.py:156
  (48 shorter events, 4.8 us)
Async XLA Ops:
  2.0 10.3 %collective-permute-start.2 = (bf16[128,1024]{1,0:T(8,128)(2,1)S(1)}, bf16[128,1024]{1,0:T(8,128)(2,1)S(1)}, u32[]{:S(2)}, u32[]{:S(2)}) collective-permute-start(bf16[128,1024]{1,0:T(8,128)(2,1)S(1)} %get-tuple-element.24), channel_id=1, source_target_pairs={{24,1},{25,22},{26,13},{27,15},{28,9},{29,23},{30,3},{31,14}} | collective-permute-start | bytes 786440 | tf_op jit(solution)/shard_map/ppermute | solution.py:133
  2.8 9.5 %collective-permute-start.1 = (bf16[128,768]{1,0:T(8,128)(2,1)S(1)}, bf16[128,768]{1,0:T(8,128)(2,1)S(1)}, u32[]{:S(2)}, u32[]{:S(2)}) collective-permute-start(bf16[128,768]{1,0:T(8,128)(2,1)S(1)} %get-tuple-element.23), channel_id=1, source_target_pairs={{16,0},{17,13},{18,22},{19,15},{20,14},{21,9},{23,2}} | collective-permute-start | bytes 589832 | tf_op jit(solution)/shard_map/ppermute | solution.py:133
  3.6 8.6 %collective-permute-start = (bf16[128,512]{1,0:T(8,128)(2,1)S(1)}, bf16[128,512]{1,0:T(8,128)(2,1)S(1)}, u32[]{:S(2)}, u32[]{:S(2)}) collective-permute-start(bf16[128,512]{1,0:T(8,128)(2,1)S(1)} %get-tuple-element.22), channel_id=1, source_target_pairs={{4,0},{8,22},{10,2},{11,15},{12,1},{13,9},{14,23}} | collective-permute-start | bytes 393224 | tf_op jit(solution)/shard_map/ppermute | solution.py:133
  4.3 8.0 %collective-permute-start.9 = (bf16[128,256]{1,0:T(8,128)(2,1)S(1)}, bf16[128,256]{1,0:T(8,128)(2,1)S(1)}, u32[]{:S(2)}, u32[]{:S(2)}) collective-permute-start(bf16[128,256]{1,0:T(8,128)(2,1)S(1)} %get-tuple-element.27), channel_id=1, source_target_pairs={{5,9},{6,14},{7,23}} | collective-permute-start | bytes 196616 | tf_op jit(solution)/shard_map/ppermute | solution.py:133
  12.3 6.3 %collective-permute-start.10 = (bf16[128,2304]{1,0:T(8,128)(2,1)S(1)}, bf16[128,2304]{1,0:T(8,128)(2,1)S(1)}, u32[]{:S(2)}, u32[]{:S(2)}) collective-permute-start(bf16[128,2304]{1,0:T(8,128)(2,1)S(1)} %pack_kernel.1), channel_id=1, source_target_pairs={{0,1},{1,0},{2,3},{3,2},{4,5},{5,4},{6,7},{7,6},{8,12},{9,8},{10,1... | collective-permute-start | bytes 1769480 | tf_op jit(solution)/shard_map/ppermute | solution.py:129
  14.6 1.7 %collective-permute-start.3 = (bf16[256,128]{1,0:T(8,128)(2,1)S(1)}, bf16[256,128]{1,0:T(8,128)(2,1)S(1)}, u32[]{:S(2)}, u32[]{:S(2)}) collective-permute-start(bf16[256,128]{1,0:T(8,128)(2,1)S(1)} %first_kernel.1), channel_id=1, source_target_pairs={{0,4},{1,8},{2,12},{3,2},{4,5},{5,0},{6,7},{7,6},{8,9},{9,1},{10,1... | collective-permute-start | bytes 196616 | tf_op jit(solution)/shard_map/ppermute | solution.py:129
  14.7 1.6 %collective-permute-start.4 = (bf16[256,128]{1,0:T(8,128)(2,1)S(1)}, bf16[256,128]{1,0:T(8,128)(2,1)S(1)}, u32[]{:S(2)}, u32[]{:S(2)}) collective-permute-start(bf16[256,128]{1,0:T(8,128)(2,1)S(1)} %first_kernel.1), channel_id=1, source_target_pairs={{0,8},{1,12},{2,3},{3,4},{4,5},{5,0},{6,7},{7,6},{8,9},{9,1},{10,1... | collective-permute-start | bytes 196616 | tf_op jit(solution)/shard_map/ppermute | solution.py:129
  15.3 1.3 %collective-permute-start.6 = (bf16[256,128]{1,0:T(8,128)(2,1)S(1)}, bf16[256,128]{1,0:T(8,128)(2,1)S(1)}, u32[]{:S(2)}, u32[]{:S(2)}) collective-permute-start(bf16[256,128]{1,0:T(8,128)(2,1)S(1)} %first_kernel.1), channel_id=1, source_target_pairs={{0,1},{1,4},{2,8},{3,12},{4,5},{5,0},{6,7},{7,6},{8,9},{9,2},{10,1... | collective-permute-start | bytes 196616 | tf_op jit(solution)/shard_map/ppermute | solution.py:129
  16.6 2.1 %collective-permute-start.7 = (bf16[1024,128]{1,0:T(8,128)(2,1)S(1)}, bf16[1024,128]{1,0:T(8,128)(2,1)S(1)}, u32[]{:S(2)}, u32[]{:S(2)}) collective-permute-start(bf16[1024,128]{1,0:T(8,128)(2,1)S(1)} %get-tuple-element.25), channel_id=1, source_target_pairs={{0,1},{1,0},{2,3},{3,2},{4,9},{5,4},{6,7},{7,6},{8,5},{9,8},{10,11... | collective-permute-start | bytes 786440 | tf_op jit(solution)/shard_map/ppermute | solution.py:129
  17.0 1.8 %collective-permute-start.11 = (bf16[1024,128]{1,0:T(8,128)(2,1)S(1)}, bf16[1024,128]{1,0:T(8,128)(2,1)S(1)}, u32[]{:S(2)}, u32[]{:S(2)}) collective-permute-start(bf16[1024,128]{1,0:T(8,128)(2,1)S(1)} %get-tuple-element.29.s_prev), channel_id=1, source_target_pairs={{0,1},{1,0},{2,3},{3,2},{4,5},{5,4},{6,7},{7,6},{8,9},{9,8},{10,11... | collective-permute-start | bytes 786440 | tf_op jit(solution)/shard_map/ppermute | solution.py:129
  17.1 1.5 %collective-permute-start.8 = (bf16[128,256]{1,0:T(8,128)(2,1)S(1)}, bf16[128,256]{1,0:T(8,128)(2,1)S(1)}, u32[]{:S(2)}, u32[]{:S(2)}) collective-permute-start(bf16[128,256]{1,0:T(8,128)(2,1)S(1)} %get-tuple-element.27), channel_id=1, source_target_pairs={{0,1},{1,9},{2,14},{3,23},{4,5},{5,4},{6,7},{7,6},{8,0},{9,8},{10,... | collective-permute-start | bytes 196616 | tf_op jit(solution)/shard_map/ppermute | solution.py:129
  18.8 1.6 %collective-permute-start.12 = (bf16[1024,128]{1,0:T(8,128)(2,1)S(1)}, bf16[1024,128]{1,0:T(8,128)(2,1)S(1)}, u32[]{:S(2)}, u32[]{:S(2)}) collective-permute-start(bf16[1024,128]{1,0:T(8,128)(2,1)S(1)} %get-tuple-element.30), channel_id=1, source_target_pairs={{0,1},{1,0},{2,3},{3,2},{4,5},{5,4},{6,7},{7,6},{8,9},{9,14},{10,1... | collective-permute-start | bytes 786440 | tf_op jit(solution)/shard_map/ppermute | solution.py:129
  19.2 1.6 %collective-permute-start.13 = (bf16[1024,128]{1,0:T(8,128)(2,1)S(1)}, bf16[1024,128]{1,0:T(8,128)(2,1)S(1)}, u32[]{:S(2)}, u32[]{:S(2)}) collective-permute-start(bf16[1024,128]{1,0:T(8,128)(2,1)S(1)} %step1_kernel.1.q_in.q_prev), channel_id=1, source_target_pairs={{0,1},{1,5},{2,3},{3,2},{4,0},{5,4},{6,7},{7,6},{8,16},{9,17},{10,... | collective-permute-start | bytes 786440 | tf_op jit(solution)/shard_map/ppermute | solution.py:129
  19.4 1.8 %collective-permute-start.14 = (bf16[1024,128]{1,0:T(8,128)(2,1)S(1)}, bf16[1024,128]{1,0:T(8,128)(2,1)S(1)}, u32[]{:S(2)}, u32[]{:S(2)}) collective-permute-start(bf16[1024,128]{1,0:T(8,128)(2,1)S(1)} %step1_kernel.1.q_in.q_prev), channel_id=1, source_target_pairs={{0,1},{1,0},{2,3},{3,2},{4,5},{5,4},{6,7},{7,6},{8,9},{9,13},{10,1... | collective-permute-start | bytes 786440 | tf_op jit(solution)/shard_map/ppermute | solution.py:129
  21.2 1.6 %collective-permute-start.15 = (bf16[1024,128]{1,0:T(8,128)(2,1)S(1)}, bf16[1024,128]{1,0:T(8,128)(2,1)S(1)}, u32[]{:S(2)}, u32[]{:S(2)}) collective-permute-start(bf16[1024,128]{1,0:T(8,128)(2,1)S(1)} %get-tuple-element.33.s_ref), channel_id=1, source_target_pairs={{0,1},{1,0},{2,3},{3,2},{4,5},{5,4},{6,7},{7,6},{8,9},{9,8},{10,11... | collective-permute-start | bytes 786440 | tf_op jit(solution)/shard_map/ppermute | solution.py:129
  22.8 4.2 %collective-permute-start.17 = (bf16[1024,128]{1,0:T(8,128)(2,1)S(1)}, bf16[1024,128]{1,0:T(8,128)(2,1)S(1)}, u32[]{:S(2)}, u32[]{:S(2)}) collective-permute-start(bf16[1024,128]{1,0:T(8,128)(2,1)S(1)} %step3_kernel.1.q_prev), channel_id=1, source_target_pairs={{0,1},{1,0},{2,3},{3,2},{4,5},{5,4},{6,7},{7,6},{8,9},{9,8},{10,11... | collective-permute-start | bytes 786440 | tf_op jit(solution)/shard_map/ppermute | solution.py:129
  23.2 3.8 %collective-permute-start.18 = (bf16[1024,128]{1,0:T(8,128)(2,1)S(1)}, bf16[1024,128]{1,0:T(8,128)(2,1)S(1)}, u32[]{:S(2)}, u32[]{:S(2)}) collective-permute-start(bf16[1024,128]{1,0:T(8,128)(2,1)S(1)} %step3_kernel.1.q_prev), channel_id=1, source_target_pairs={{0,1},{1,0},{2,3},{3,2},{4,5},{5,4},{6,7},{7,6},{8,9},{9,8},{10,11... | collective-permute-start | bytes 786440 | tf_op jit(solution)/shard_map/ppermute | solution.py:129
  23.4 3.6 %collective-permute-start.19 = (bf16[1024,128]{1,0:T(8,128)(2,1)S(1)}, bf16[1024,128]{1,0:T(8,128)(2,1)S(1)}, u32[]{:S(2)}, u32[]{:S(2)}) collective-permute-start(bf16[1024,128]{1,0:T(8,128)(2,1)S(1)} %step3_kernel.1.q_prev), channel_id=1, source_target_pairs={{0,1},{1,0},{2,3},{3,2},{4,5},{5,4},{6,7},{7,6},{8,9},{9,8},{10,11... | collective-permute-start | bytes 786440 | tf_op jit(solution)/shard_map/ppermute | solution.py:129
  23.7 3.3 %collective-permute-start.20 = (bf16[1024,128]{1,0:T(8,128)(2,1)S(1)}, bf16[1024,128]{1,0:T(8,128)(2,1)S(1)}, u32[]{:S(2)}, u32[]{:S(2)}) collective-permute-start(bf16[1024,128]{1,0:T(8,128)(2,1)S(1)} %step3_kernel.1.q_prev), channel_id=1, source_target_pairs={{23,15},{10,26},{14,30},{16,24},{20,28},{17,25},{13,21},{9,1}} | collective-permute-start | bytes 786440 | tf_op jit(solution)/shard_map/ppermute | solution.py:133
  24.4 30.6 %collective-permute-start.21 = (bf16[1024,128]{1,0:T(8,128)(2,1)S(1)}, bf16[1024,128]{1,0:T(8,128)(2,1)S(1)}, u32[]{:S(2)}, u32[]{:S(2)}) collective-permute-start(bf16[1024,128]{1,0:T(8,128)(2,1)S(1)} %step3_kernel.1.q_prev), channel_id=1, source_target_pairs={{23,7},{10,18},{14,22},{17,29},{13,5}} | collective-permute-start | bytes 786440 | tf_op jit(solution)/shard_map/ppermute | solution.py:133
  55.1 5.5 %collective-permute-start.22 = (bf16[1040,128]{1,0:T(8,128)(2,1)S(1)}, bf16[1040,128]{1,0:T(8,128)(2,1)S(1)}, u32[]{:S(2)}, u32[]{:S(2)}) collective-permute-start(bf16[1040,128]{1,0:T(8,128)(2,1)S(1)} %get-tuple-element.40.refs_0_), channel_id=1, source_target_pairs={{0,2},{1,3},{2,0},{3,1},{4,6},{5,7},{6,4},{7,5},{8,10},{9,11},{10,... | collective-permute-start | bytes 798728 | tf_op jit(solution)/shard_map/ppermute | solution.py:129
  55.1 4.6 %collective-permute-start.23 = (bf16[1024,128]{1,0:T(8,128)(2,1)S(1)}, bf16[1024,128]{1,0:T(8,128)(2,1)S(1)}, u32[]{:S(2)}, u32[]{:S(2)}) collective-permute-start(bf16[1024,128]{1,0:T(8,128)(2,1)S(1)} %get-tuple-element.38.q_ref), channel_id=1, source_target_pairs={{15,11},{7,3},{10,2},{14,6}} | collective-permute-start | bytes 786440 | tf_op jit(solution)/shard_map/ppermute | solution.py:133
  60.6 5.5 %collective-permute-start.24 = (bf16[1040,128]{1,0:T(8,128)(2,1)S(1)}, bf16[1040,128]{1,0:T(8,128)(2,1)S(1)}, u32[]{:S(2)}, u32[]{:S(2)}) collective-permute-start(bf16[1040,128]{1,0:T(8,128)(2,1)S(1)} %get-tuple-element.40.refs_0_), channel_id=1, source_target_pairs={{0,1},{1,0},{2,3},{3,2},{4,5},{5,4},{6,7},{7,6},{8,9},{9,8},{10,11... | collective-permute-start | bytes 798728 | tf_op jit(solution)/shard_map/ppermute | solution.py:129
  64.9 1.5 %collective-permute-start.25 = (bf16[1040,128]{1,0:T(8,128)(2,1)S(1)}, bf16[1040,128]{1,0:T(8,128)(2,1)S(1)}, u32[]{:S(2)}, u32[]{:S(2)}) collective-permute-start(bf16[1040,128]{1,0:T(8,128)(2,1)S(1)} %collective-permute-done.22.refs_2_), channel_id=1, source_target_pairs={{0,1},{1,0},{2,3},{3,2},{4,5},{5,4},{6,7},{7,6},{8,9},{9,8},{10,11... | collective-permute-start | bytes 798728 | tf_op jit(solution)/shard_map/ppermute | solution.py:129
  (6 other events, 45.0 us)

commit v13 on v12

--- a/solution.py
+++ b/solution.py
@@ -78,7 +78,7 @@
     (0, 3, 1, 2),
     (1, 3, 0, 2),
 )
-REST = ((2, 3), (0, 3), (0, 2), (1, 2))
+REST = ((2, 3), (0, 3), (1, 3), (0, 2))
 
 
 def hops(a, b):
@@ -224,7 +224,7 @@
 
 
 def pack_kernel(*refs):
-    parts, out_ref, sem = refs[1:-2], refs[-2], refs[-1]
+    parts, out_ref, sem = refs[:-2], refs[-2], refs[-1]
 
     @pl.when(any_of(PARTNER[1:]))
     def _():
@@ -239,7 +239,7 @@
             copy.wait()
 
 
-def whole_kernel(diag_ref, top_ref, even_ref, *refs):
+def whole_kernel(diag_ref, even_ref, *refs):
     odd, out_ref, sem = refs[:-2], refs[-2], refs[-1]
     size = out_ref.shape[0]
     part = size // NR
@@ -256,11 +256,9 @@
             wide = pair_width(i // 2, part)
             if i % 2:
                 source = odd[i // 2]
-            elif i:
+            else:
                 source = even_ref.at[:, pl.ds(left, wide)]
                 left += wide
-            else:
-                source = top_ref
 
             @pl.when(row == i)
             def _():
@@ -354,7 +352,7 @@
         s_ref[...] = s_prev[...]
 
 
-def step3_kernel(takers, sum_ref, a_ref, *refs):
+def step3_kernel(takers, a_ref, sum_ref, *refs):
     came, (d_ref, q_prev, q_ref, p_v) = refs[:-4], refs[-4:]
     active = at(MAKER[3])
 
@@ -363,7 +361,7 @@
         p_v[...] = low(a_ref[...].astype(jnp.float32) - sum_ref[...].astype(jnp.float32))
         lower_dot(q_ref, d_ref, p_v)
 
-    for devices, source in zip(takers, (a_ref, *came)):
+    for devices, source in zip(takers, came):
 
         @pl.when(any_of(devices))
         def _():
@@ -448,9 +446,9 @@
     parts = []
     for m, cut in enumerate(cuts):
         pairs = []
-        for r in range(1, NR):
+        for r in range(NR):
             for c, k in enumerate(SENDS[r]):
-                if k == 0 and max(r // 2, 1) == m:
+                if k == 0 and r and max(r // 2, 1) == m:
                     pairs.append(((r, c), at_piece[r]))
                 if k and MAKER[k][0] != r and r // 2 == m:
                     pairs.append(((r, c), MAKER[k] if r % 2 else PARTNER[k]))
@@ -472,20 +470,18 @@
     got = [send(q, [((0, c), takers[(c + j) % 4]) for c in range(4) if (c + j) % 4 < 3]) for j in range(4)]
     even = call(
         pack_kernel,
-        jax.ShapeDtypeStruct((part, sum(wides[1:])), bf16),
+        jax.ShapeDtypeStruct((part, sum(wides)), bf16),
         parts,
         [ANY] * len(wides),
         VMEM,
-        [pltpu.SemaphoreType.DMA((len(wides) - 1,))],
+        [pltpu.SemaphoreType.DMA((len(wides),))],
     )
     even = send(even, [(PARTNER[k], MAKER[k]) for k in range(1, NC)])
-    top, _ = lax.optimization_barrier((cuts[0], q))
-    top = send(top, [((0, k), MAKER[k]) for k in range(1, NC)])
     diag = call(
         whole_kernel,
         jax.ShapeDtypeStruct((size, size), bf16),
-        [diag_inv, top, even, *parts],
-        [HBM] + [ANY] * (2 + len(wides)),
+        [diag_inv, even, *parts],
+        [HBM] + [ANY] * (1 + len(wides)),
         VMEM,
         [pltpu.SemaphoreType.DMA((NR,))],
     )
@@ -503,27 +499,30 @@
     p_in, came = lax.optimization_barrier((p_in, came))
 
     a, q, s = call(step2_kernel, [vec] * 3, [p_in, q_in, sums, rhs, diag, block, q, s], [VMEM] * 8, [VMEM] * 3)
+    from_c = a
+    a = send(a, [(BESIDE, MAKER[3])])
     sums = send(s, [(MAKER[2], MAKER[3])])
-    a = send_only(a, [(BESIDE, MAKER[3]), (MAKER[2], (2, 2))])
+    early = ((2, 2), (7, 2), (5, 2))
+    got = [send_only(from_c, [(MAKER[2], d)]) for d in early]
     q = call(
-        functools.partial(step3_kernel, [[(2, 2)], took]),
+        functools.partial(step3_kernel, [[d] for d in early] + [took]),
         vec,
-        [sums, a, came, diag, q],
-        [VMEM] * 5,
+        [a, sums, *got, came, diag, q],
+        [VMEM] * 8,
         VMEM,
         [pltpu.VMEM((size, width), bf16)],
     )
 
-    sends = [[(MAKER[3], (r, 3))] for r in (6, 7, 4)]
-    got = [send(q, pairs) for pairs in sends]
-    sends += [
+    sends = [
         [
-            (MAKER[3], (3, 3)), ((2, 2), (6, 2)), (MAKER[2], (7, 2)),
+            (MAKER[3], (6, 3)), ((2, 2), (6, 2)),
             ((4, 0), (6, 0)), ((5, 0), (7, 0)), ((4, 1), (6, 1)), ((3, 1), (5, 1)), ((2, 1), (0, 1)),
         ],
-        [(MAKER[3], (1, 3)), ((2, 2), (4, 2)), (MAKER[2], (5, 2)), ((4, 1), (7, 1)), ((3, 1), (1, 1))],
+        [(MAKER[3], (7, 3)), ((2, 2), (4, 2)), ((4, 1), (7, 1)), ((3, 1), (1, 1))],
+        [(MAKER[3], (4, 3))],
+        [(MAKER[3], (3, 3)), (MAKER[2], (1, 2))],
     ]
-    got += [send_only(q, pairs) for pairs in sends[3:]]
+    got = [send_only(q, pairs) for pairs in sends]
     takers = [[b for _, b in pairs] for pairs in sends]
     q, mine = call(
         functools.partial(update_kernel, takers),
@@ -537,7 +536,7 @@
         return send(value, [((r, c), (r, c ^ step)) for r in range(NR) for c in range(NC)])
 
     across = swap(mine, 2)
-    rest = send_only(q, list(zip(((3, 3), (1, 3), (2, 2), MAKER[2]), REST)))
+    rest = send_only(q, list(zip(((3, 3), (6, 3), (7, 3), (2, 2)), REST)))
     solved = call(solved_kernel, jax.ShapeDtypeStruct((size, width), jnp.float32), [q, rest], [VMEM] * 2, VMEM)
     beside, across, solved = lax.optimization_barrier((mine, across, solved))
     beside = swap(beside, 1)

time: 68.1 us -> 66.2 us (0.972)
  waiting for transfers between devices: 38.1 us -> 17.9 us
  starting transfers between devices: 23.7 us -> 41.3 us
    ppermute x8 -> x12, waiting for transfers between devices: 32.6 us -> 12.7 us  [send_only(): lax.ppermute(value, ('row', 'col'), [(a * NC + b, c * NC + d) for (a, b),...]
    ppermute x18 -> x15, starting transfers between devices: 10.9 us -> 26.4 us  [send(): lax.ppermute(value, ('row', 'col'), [(a * NC + b, c * NC + d) for (a, b),...]
    ppermute x8 -> x12, starting transfers between devices: 12.9 us -> 14.9 us  [send_only(): lax.ppermute(value, ('row', 'col'), [(a * NC + b, c * NC + d) for (a, b),...]
    ppermute x18 -> x15, waiting for transfers between devices: 5.53 us -> 5.2 us  [send(): lax.ppermute(value, ('row', 'col'), [(a * NC + b, c * NC + d) for (a, b),...]
  transfers between devices with their start and end apart: 26 -> 27, of which waited for: 14 -> 13; matrix products, arithmetic and copies ran while one was open for 0% -> 0% of each run, Pallas kernels for 1% -> 1%
where the time goes in v13:
time: 66.2 us; the launch traced here: 65.4 us
  starting transfers between devices  41.3 us (62%)
  waiting for transfers between devices  17.9 us (27%)
  Pallas kernels  2.65 us (4%)
  between operations  2.19 us (3%)
  local copies, waits for them, and re-layouts  1.32 us (2%)
    ppermute x15, starting transfers between devices, send(): lax.ppermute(value, ('row', 'col'), [(a * NC + b, c * NC + d) for (a, b),...  26.4 us
    ppermute x12, starting transfers between devices, send_only(): lax.ppermute(value, ('row', 'col'), [(a * NC + b, c * NC + d) for (a, b),...  14.9 us
    ppermute x12, waiting for transfers between devices, send_only(): lax.ppermute(value, ('row', 'col'), [(a * NC + b, c * NC + d) for (a, b),...  12.7 us
    ppermute x15, waiting for transfers between devices, send(): lax.ppermute(value, ('row', 'col'), [(a * NC + b, c * NC + d) for (a, b),...  5.2 us
    pallas_call x12, Pallas kernels, call(): pl.pallas_call(kernel, out_shape=outs, in_specs=in_specs, out_specs=out_s...  2.65 us
  transfers between devices with their start and end apart: 27, of which 13 were waited for; matrix products, arithmetic and copies ran while one was open for 0% of the time, Pallas kernels for 1%

profile of v13, /device:TPU:7, one launch (start us, length us, event | category | flops | bytes accessed | tf_op | source)
XLA Modules:
  0.0 65.4 jit_solution(6220531415782228554)
XLA Ops:
  0.6 1.3 %copy-done.2 = bf16[4,128,1024]{2,1,0:T(8,128)(2,1)S(1)} copy-done((bf16[4,128,1024]{2,1,0:T(8,128)(2,1)S(1)}, bf16[4,128,1024]{2,1,0:T(8,128)(2,1)}, u32[]{:S(2)}) %copy-start.2) | copy-done | bytes 1048600
  2.0 0.8 %collective-permute-start.2 = (bf16[128,1024]{1,0:T(8,128)(2,1)S(1)}, bf16[128,1024]{1,0:T(8,128)(2,1)S(1)}, u32[]{:S(2)}, u32[]{:S(2)}) collective-permute-start(bf16[128,1024]{1,0:T(8,128)(2,1)S(1)} %get-tuple-element.23), channel_id=1, source_target_pairs={{24,1},{25,22},{26,13},{27,15},{28,9},{29,23},{30,3},{31,14}} | collective-permute-start | bytes 786440 | tf_op jit(solution)/shard_map/ppermute | solution.py:133
  2.8 0.8 %collective-permute-start.1 = (bf16[128,768]{1,0:T(8,128)(2,1)S(1)}, bf16[128,768]{1,0:T(8,128)(2,1)S(1)}, u32[]{:S(2)}, u32[]{:S(2)}) collective-permute-start(bf16[128,768]{1,0:T(8,128)(2,1)S(1)} %get-tuple-element.22), channel_id=1, source_target_pairs={{16,0},{17,13},{18,22},{19,15},{20,14},{21,9},{23,2}} | collective-permute-start | bytes 589832 | tf_op jit(solution)/shard_map/ppermute | solution.py:133
  3.6 0.7 %collective-permute-start = (bf16[128,512]{1,0:T(8,128)(2,1)S(1)}, bf16[128,512]{1,0:T(8,128)(2,1)S(1)}, u32[]{:S(2)}, u32[]{:S(2)}) collective-permute-start(bf16[128,512]{1,0:T(8,128)(2,1)S(1)} %get-tuple-element.21), channel_id=1, source_target_pairs={{4,0},{8,22},{10,2},{11,15},{12,1},{13,9},{14,23}} | collective-permute-start | bytes 393224 | tf_op jit(solution)/shard_map/ppermute | solution.py:133
  4.3 6.6 %collective-permute-start.8 = (bf16[128,256]{1,0:T(8,128)(2,1)S(1)}, bf16[128,256]{1,0:T(8,128)(2,1)S(1)}, u32[]{:S(2)}, u32[]{:S(2)}) collective-permute-start(bf16[128,256]{1,0:T(8,128)(2,1)S(1)} %get-tuple-element.25), channel_id=1, source_target_pairs={{1,13},{2,15},{3,22},{5,9},{6,14},{7,23}} | collective-permute-start | bytes 196616 | tf_op jit(solution)/shard_map/ppermute | solution.py:133
  11.0 1.3 %collective-permute-done.8.refs_0_ = bf16[128,256]{1,0:T(8,128)(2,1)S(1)} collective-permute-done((bf16[128,256]{1,0:T(8,128)(2,1)S(1)}, bf16[128,256]{1,0:T(8,128)(2,1)S(1)}, u32[]{:S(2)}, u32[]{:S(2)}) %collective-permute-start.8) | collective-permute-done | bytes 65568 | tf_op jit(solution)/shard_map/ppermute | solution.py:133
  12.3 2.2 %collective-permute-start.9 = (bf16[128,2560]{1,0:T(8,128)(2,1)S(1)}, bf16[128,2560]{1,0:T(8,128)(2,1)S(1)}, u32[]{:S(2)}, u32[]{:S(2)}) collective-permute-start(bf16[128,2560]{1,0:T(8,128)(2,1)S(1)} %pack_kernel.1), channel_id=1, source_target_pairs={{0,1},{1,0},{2,3},{3,2},{4,5},{5,4},{6,7},{7,6},{8,12},{9,8},{10,1... | collective-permute-start | bytes 1966088 | tf_op jit(solution)/shard_map/ppermute | solution.py:129
  15.7 0.7 %collective-permute-done.3.g0 = bf16[256,128]{1,0:T(8,128)(2,1)S(1)} collective-permute-done((bf16[256,128]{1,0:T(8,128)(2,1)S(1)}, bf16[256,128]{1,0:T(8,128)(2,1)S(1)}, u32[]{:S(2)}, u32[]{:S(2)}) %collective-permute-start.3) | collective-permute-done | bytes 65568 | tf_op jit(solution)/shard_map/ppermute | solution.py:129
  17.3 0.9 %collective-permute-done.7.p_in = bf16[1024,128]{1,0:T(8,128)(2,1)S(1)} collective-permute-done((bf16[1024,128]{1,0:T(8,128)(2,1)S(1)}, bf16[1024,128]{1,0:T(8,128)(2,1)S(1)}, u32[]{:S(2)}, u32[]{:S(2)}) %collective-permute-start.7) | collective-permute-done | bytes 262176 | tf_op jit(solution)/shard_map/ppermute | solution.py:129
  19.6 0.7 collective-permute-done.11.p_in
  21.6 0.7 %collective-permute-start.16 = (bf16[1024,128]{1,0:T(8,128)(2,1)S(1)}, bf16[1024,128]{1,0:T(8,128)(2,1)S(1)}, u32[]{:S(2)}, u32[]{:S(2)}) collective-permute-start(bf16[1024,128]{1,0:T(8,128)(2,1)S(1)} %get-tuple-element.32), channel_id=1, source_target_pairs={{14,10}} | collective-permute-start | bytes 786440 | tf_op jit(solution)/shard_map/ppermute | solution.py:133
  22.2 0.7 %collective-permute-start.17 = (bf16[1024,128]{1,0:T(8,128)(2,1)S(1)}, bf16[1024,128]{1,0:T(8,128)(2,1)S(1)}, u32[]{:S(2)}, u32[]{:S(2)}) collective-permute-start(bf16[1024,128]{1,0:T(8,128)(2,1)S(1)} %get-tuple-element.32), channel_id=1, source_target_pairs={{14,30}} | collective-permute-start | bytes 786440 | tf_op jit(solution)/shard_map/ppermute | solution.py:133
  22.9 0.7 %collective-permute-start.18 = (bf16[1024,128]{1,0:T(8,128)(2,1)S(1)}, bf16[1024,128]{1,0:T(8,128)(2,1)S(1)}, u32[]{:S(2)}, u32[]{:S(2)}) collective-permute-start(bf16[1024,128]{1,0:T(8,128)(2,1)S(1)} %get-tuple-element.32), channel_id=1, source_target_pairs={{14,22}} | collective-permute-start | bytes 786440 | tf_op jit(solution)/shard_map/ppermute | solution.py:133
  23.7 0.7 %collective-permute-start.19 = (bf16[1024,128]{1,0:T(8,128)(2,1)S(1)}, bf16[1024,128]{1,0:T(8,128)(2,1)S(1)}, u32[]{:S(2)}, u32[]{:S(2)}) collective-permute-start(bf16[1024,128]{1,0:T(8,128)(2,1)S(1)} %step3_kernel.1.q_prev), channel_id=1, source_target_pairs={{23,27},{10,26},{16,24},{20,28},{17,25},{13,21},{9,1}} | collective-permute-start | bytes 786440 | tf_op jit(solution)/shard_map/ppermute | solution.py:133
  24.4 0.7 %collective-permute-start.20 = (bf16[1024,128]{1,0:T(8,128)(2,1)S(1)}, bf16[1024,128]{1,0:T(8,128)(2,1)S(1)}, u32[]{:S(2)}, u32[]{:S(2)}) collective-permute-start(bf16[1024,128]{1,0:T(8,128)(2,1)S(1)} %step3_kernel.1.q_prev), channel_id=1, source_target_pairs={{23,31},{10,18},{17,29},{13,5}} | collective-permute-start | bytes 786440 | tf_op jit(solution)/shard_map/ppermute | solution.py:133
  25.1 0.7 %collective-permute-start.21 = (bf16[1024,128]{1,0:T(8,128)(2,1)S(1)}, bf16[1024,128]{1,0:T(8,128)(2,1)S(1)}, u32[]{:S(2)}, u32[]{:S(2)}) collective-permute-start(bf16[1024,128]{1,0:T(8,128)(2,1)S(1)} %step3_kernel.1.q_prev), channel_id=1, source_target_pairs={{23,19}} | collective-permute-start | bytes 786440 | tf_op jit(solution)/shard_map/ppermute | solution.py:133
  25.8 0.7 %collective-permute-start.22 = (bf16[1024,128]{1,0:T(8,128)(2,1)S(1)}, bf16[1024,128]{1,0:T(8,128)(2,1)S(1)}, u32[]{:S(2)}, u32[]{:S(2)}) collective-permute-start(bf16[1024,128]{1,0:T(8,128)(2,1)S(1)} %step3_kernel.1.q_prev), channel_id=1, source_target_pairs={{23,15},{14,6}} | collective-permute-start | bytes 786440 | tf_op jit(solution)/shard_map/ppermute | solution.py:133
  27.9 19.8 %collective-permute-start.23 = (bf16[1040,128]{1,0:T(8,128)(2,1)S(1)}, bf16[1040,128]{1,0:T(8,128)(2,1)S(1)}, u32[]{:S(2)}, u32[]{:S(2)}) collective-permute-start(bf16[1040,128]{1,0:T(8,128)(2,1)S(1)} %get-tuple-element.38.refs_0_), channel_id=1, source_target_pairs={{0,2},{1,3},{2,0},{3,1},{4,6},{5,7},{6,4},{7,5},{8,10},{9,11},{10,... | collective-permute-start | bytes 798728 | tf_op jit(solution)/shard_map/ppermute | solution.py:129
  47.8 1.3 %collective-permute-start.24 = (bf16[1024,128]{1,0:T(8,128)(2,1)S(1)}, bf16[1024,128]{1,0:T(8,128)(2,1)S(1)}, u32[]{:S(2)}, u32[]{:S(2)}) collective-permute-start(bf16[1024,128]{1,0:T(8,128)(2,1)S(1)} %get-tuple-element.36.q_ref), channel_id=1, source_target_pairs={{15,11},{27,3},{31,7},{10,2}} | collective-permute-start | bytes 786440 | tf_op jit(solution)/shard_map/ppermute | solution.py:133
  49.1 11.4 %collective-permute-done.24.rest_ref = bf16[1024,128]{1,0:T(8,128)(2,1)S(1)} collective-permute-done((bf16[1024,128]{1,0:T(8,128)(2,1)S(1)}, bf16[1024,128]{1,0:T(8,128)(2,1)S(1)}, u32[]{:S(2)}, u32[]{:S(2)}) %collective-permute-start.24) | collective-permute-done | bytes 262176 | tf_op jit(solution)/shard_map/ppermute | solution.py:133
  60.4 0.8 %solved_kernel.1 = f32[1024,128]{1,0:T(8,128)} custom-call(bf16[1024,128]{1,0:T(8,128)(2,1)S(1)} %get-tuple-element.36.q_ref, bf16[1024,128]{1,0:T(8,128)(2,1)S(1)} %collective-permute-done.24.rest_ref), custom_call_target="tpu_custom_call" | custom-call | tf_op jit(solution)/shard_map/solved_kernel/pallas_call | solution.py:156
  61.3 1.2 %collective-permute-start.25 = (bf16[1040,128]{1,0:T(8,128)(2,1)S(1)}, bf16[1040,128]{1,0:T(8,128)(2,1)S(1)}, u32[]{:S(2)}, u32[]{:S(2)}) collective-permute-start(bf16[1040,128]{1,0:T(8,128)(2,1)S(1)} %get-tuple-element.38.refs_0_), channel_id=1, source_target_pairs={{0,1},{1,0},{2,3},{3,2},{4,5},{5,4},{6,7},{7,6},{8,9},{9,8},{10,11... | collective-permute-start | bytes 798728 | tf_op jit(solution)/shard_map/ppermute | solution.py:129
  62.5 1.2 %collective-permute-done.25.refs_1_ = bf16[1040,128]{1,0:T(8,128)(2,1)S(1)} collective-permute-done((bf16[1040,128]{1,0:T(8,128)(2,1)S(1)}, bf16[1040,128]{1,0:T(8,128)(2,1)S(1)}, u32[]{:S(2)}, u32[]{:S(2)}) %collective-permute-start.25) | collective-permute-done | bytes 266272 | tf_op jit(solution)/shard_map/ppermute | solution.py:129
  64.0 1.4 %final_kernel.1 = f32[2,1024,128]{2,1,0:T(8,128)} custom-call(f32[2,1024,128]{2,1,0:T(8,128)S(1)} %bitcast.14, bf16[1040,128]{1,0:T(8,128)(2,1)S(1)} %get-tuple-element.38.refs_0_, bf16[1040,128]{1,0:T(8,128)(2,1)S(1)} %collective-permute-done.25.refs_1_, bf16[1040,128]{1,0:T(8,128)(2,1)S(1)} %collective-permute-done.23.refs_2_, ...), custom_call_target="tpu_custom_call" | custom-call | tf_op jit(solution)/shard_map/final_kernel/pallas_call | solution.py:156
  (50 shorter events, 5.4 us)
Async XLA Ops:
  2.0 10.3 %collective-permute-start.2 = (bf16[128,1024]{1,0:T(8,128)(2,1)S(1)}, bf16[128,1024]{1,0:T(8,128)(2,1)S(1)}, u32[]{:S(2)}, u32[]{:S(2)}) collective-permute-start(bf16[128,1024]{1,0:T(8,128)(2,1)S(1)} %get-tuple-element.23), channel_id=1, source_target_pairs={{24,1},{25,22},{26,13},{27,15},{28,9},{29,23},{30,3},{31,14}} | collective-permute-start | bytes 786440 | tf_op jit(solution)/shard_map/ppermute | solution.py:133
  2.8 9.5 %collective-permute-start.1 = (bf16[128,768]{1,0:T(8,128)(2,1)S(1)}, bf16[128,768]{1,0:T(8,128)(2,1)S(1)}, u32[]{:S(2)}, u32[]{:S(2)}) collective-permute-start(bf16[128,768]{1,0:T(8,128)(2,1)S(1)} %get-tuple-element.22), channel_id=1, source_target_pairs={{16,0},{17,13},{18,22},{19,15},{20,14},{21,9},{23,2}} | collective-permute-start | bytes 589832 | tf_op jit(solution)/shard_map/ppermute | solution.py:133
  3.6 8.6 %collective-permute-start = (bf16[128,512]{1,0:T(8,128)(2,1)S(1)}, bf16[128,512]{1,0:T(8,128)(2,1)S(1)}, u32[]{:S(2)}, u32[]{:S(2)}) collective-permute-start(bf16[128,512]{1,0:T(8,128)(2,1)S(1)} %get-tuple-element.21), channel_id=1, source_target_pairs={{4,0},{8,22},{10,2},{11,15},{12,1},{13,9},{14,23}} | collective-permute-start | bytes 393224 | tf_op jit(solution)/shard_map/ppermute | solution.py:133
  4.3 8.0 %collective-permute-start.8 = (bf16[128,256]{1,0:T(8,128)(2,1)S(1)}, bf16[128,256]{1,0:T(8,128)(2,1)S(1)}, u32[]{:S(2)}, u32[]{:S(2)}) collective-permute-start(bf16[128,256]{1,0:T(8,128)(2,1)S(1)} %get-tuple-element.25), channel_id=1, source_target_pairs={{1,13},{2,15},{3,22},{5,9},{6,14},{7,23}} | collective-permute-start | bytes 196616 | tf_op jit(solution)/shard_map/ppermute | solution.py:133
  12.3 4.8 %collective-permute-start.9 = (bf16[128,2560]{1,0:T(8,128)(2,1)S(1)}, bf16[128,2560]{1,0:T(8,128)(2,1)S(1)}, u32[]{:S(2)}, u32[]{:S(2)}) collective-permute-start(bf16[128,2560]{1,0:T(8,128)(2,1)S(1)} %pack_kernel.1), channel_id=1, source_target_pairs={{0,1},{1,0},{2,3},{3,2},{4,5},{5,4},{6,7},{7,6},{8,12},{9,8},{10,1... | collective-permute-start | bytes 1966088 | tf_op jit(solution)/shard_map/ppermute | solution.py:129
  14.6 1.8 %collective-permute-start.3 = (bf16[256,128]{1,0:T(8,128)(2,1)S(1)}, bf16[256,128]{1,0:T(8,128)(2,1)S(1)}, u32[]{:S(2)}, u32[]{:S(2)}) collective-permute-start(bf16[256,128]{1,0:T(8,128)(2,1)S(1)} %first_kernel.1), channel_id=1, source_target_pairs={{0,4},{1,8},{2,12},{3,2},{4,5},{5,0},{6,7},{7,6},{8,9},{9,1},{10,1... | collective-permute-start | bytes 196616 | tf_op jit(solution)/shard_map/ppermute | solution.py:129
  14.7 1.7 %collective-permute-start.4 = (bf16[256,128]{1,0:T(8,128)(2,1)S(1)}, bf16[256,128]{1,0:T(8,128)(2,1)S(1)}, u32[]{:S(2)}, u32[]{:S(2)}) collective-permute-start(bf16[256,128]{1,0:T(8,128)(2,1)S(1)} %first_kernel.1), channel_id=1, source_target_pairs={{0,8},{1,12},{2,3},{3,4},{4,5},{5,0},{6,7},{7,6},{8,9},{9,1},{10,1... | collective-permute-start | bytes 196616 | tf_op jit(solution)/shard_map/ppermute | solution.py:129
  16.7 1.5 %collective-permute-start.7 = (bf16[1024,128]{1,0:T(8,128)(2,1)S(1)}, bf16[1024,128]{1,0:T(8,128)(2,1)S(1)}, u32[]{:S(2)}, u32[]{:S(2)}) collective-permute-start(bf16[1024,128]{1,0:T(8,128)(2,1)S(1)} %get-tuple-element.24), channel_id=1, source_target_pairs={{0,1},{1,0},{2,3},{3,2},{4,9},{5,4},{6,7},{7,6},{8,5},{9,8},{10,11... | collective-permute-start | bytes 786440 | tf_op jit(solution)/shard_map/ppermute | solution.py:129
  17.1 1.5 %collective-permute-start.10 = (bf16[1024,128]{1,0:T(8,128)(2,1)S(1)}, bf16[1024,128]{1,0:T(8,128)(2,1)S(1)}, u32[]{:S(2)}, u32[]{:S(2)}) collective-permute-start(bf16[1024,128]{1,0:T(8,128)(2,1)S(1)} %get-tuple-element.27.s_prev), channel_id=1, source_target_pairs={{0,1},{1,0},{2,3},{3,2},{4,5},{5,4},{6,7},{7,6},{8,9},{9,8},{10,11... | collective-permute-start | bytes 786440 | tf_op jit(solution)/shard_map/ppermute | solution.py:129
  18.6 1.6 %collective-permute-start.11 = (bf16[1024,128]{1,0:T(8,128)(2,1)S(1)}, bf16[1024,128]{1,0:T(8,128)(2,1)S(1)}, u32[]{:S(2)}, u32[]{:S(2)}) collective-permute-start(bf16[1024,128]{1,0:T(8,128)(2,1)S(1)} %get-tuple-element.28), channel_id=1, source_target_pairs={{0,1},{1,0},{2,3},{3,2},{4,5},{5,4},{6,7},{7,6},{8,9},{9,14},{10,1... | collective-permute-start | bytes 786440 | tf_op jit(solution)/shard_map/ppermute | solution.py:129
  19.1 1.5 %collective-permute-start.12 = (bf16[1024,128]{1,0:T(8,128)(2,1)S(1)}, bf16[1024,128]{1,0:T(8,128)(2,1)S(1)}, u32[]{:S(2)}, u32[]{:S(2)}) collective-permute-start(bf16[1024,128]{1,0:T(8,128)(2,1)S(1)} %step1_kernel.1.q_in.q_prev), channel_id=1, source_target_pairs={{0,1},{1,5},{2,3},{3,2},{4,0},{5,4},{6,7},{7,6},{8,16},{9,17},{10,... | collective-permute-start | bytes 786440 | tf_op jit(solution)/shard_map/ppermute | solution.py:129
  19.2 1.8 %collective-permute-start.13 = (bf16[1024,128]{1,0:T(8,128)(2,1)S(1)}, bf16[1024,128]{1,0:T(8,128)(2,1)S(1)}, u32[]{:S(2)}, u32[]{:S(2)}) collective-permute-start(bf16[1024,128]{1,0:T(8,128)(2,1)S(1)} %step1_kernel.1.q_in.q_prev), channel_id=1, source_target_pairs={{0,1},{1,0},{2,3},{3,2},{4,5},{5,4},{6,7},{7,6},{8,9},{9,13},{10,1... | collective-permute-start | bytes 786440 | tf_op jit(solution)/shard_map/ppermute | solution.py:129
  21.0 2.6 %collective-permute-start.14 = (bf16[1024,128]{1,0:T(8,128)(2,1)S(1)}, bf16[1024,128]{1,0:T(8,128)(2,1)S(1)}, u32[]{:S(2)}, u32[]{:S(2)}) collective-permute-start(bf16[1024,128]{1,0:T(8,128)(2,1)S(1)} %get-tuple-element.32), channel_id=1, source_target_pairs={{0,1},{1,0},{2,3},{3,2},{4,5},{5,4},{6,7},{7,6},{8,9},{9,8},{10,11... | collective-permute-start | bytes 786440 | tf_op jit(solution)/shard_map/ppermute | solution.py:129
  21.4 2.2 %collective-permute-start.15 = (bf16[1024,128]{1,0:T(8,128)(2,1)S(1)}, bf16[1024,128]{1,0:T(8,128)(2,1)S(1)}, u32[]{:S(2)}, u32[]{:S(2)}) collective-permute-start(bf16[1024,128]{1,0:T(8,128)(2,1)S(1)} %get-tuple-element.31.s_ref), channel_id=1, source_target_pairs={{0,1},{1,0},{2,3},{3,2},{4,5},{5,4},{6,7},{7,6},{8,9},{9,8},{10,11... | collective-permute-start | bytes 786440 | tf_op jit(solution)/shard_map/ppermute | solution.py:129
  21.6 2.1 %collective-permute-start.16 = (bf16[1024,128]{1,0:T(8,128)(2,1)S(1)}, bf16[1024,128]{1,0:T(8,128)(2,1)S(1)}, u32[]{:S(2)}, u32[]{:S(2)}) collective-permute-start(bf16[1024,128]{1,0:T(8,128)(2,1)S(1)} %get-tuple-element.32), channel_id=1, source_target_pairs={{14,10}} | collective-permute-start | bytes 786440 | tf_op jit(solution)/shard_map/ppermute | solution.py:133
  22.2 1.4 %collective-permute-start.17 = (bf16[1024,128]{1,0:T(8,128)(2,1)S(1)}, bf16[1024,128]{1,0:T(8,128)(2,1)S(1)}, u32[]{:S(2)}, u32[]{:S(2)}) collective-permute-start(bf16[1024,128]{1,0:T(8,128)(2,1)S(1)} %get-tuple-element.32), channel_id=1, source_target_pairs={{14,30}} | collective-permute-start | bytes 786440 | tf_op jit(solution)/shard_map/ppermute | solution.py:133
  23.7 4.0 %collective-permute-start.19 = (bf16[1024,128]{1,0:T(8,128)(2,1)S(1)}, bf16[1024,128]{1,0:T(8,128)(2,1)S(1)}, u32[]{:S(2)}, u32[]{:S(2)}) collective-permute-start(bf16[1024,128]{1,0:T(8,128)(2,1)S(1)} %step3_kernel.1.q_prev), channel_id=1, source_target_pairs={{23,27},{10,26},{16,24},{20,28},{17,25},{13,21},{9,1}} | collective-permute-start | bytes 786440 | tf_op jit(solution)/shard_map/ppermute | solution.py:133
  24.4 3.4 %collective-permute-start.20 = (bf16[1024,128]{1,0:T(8,128)(2,1)S(1)}, bf16[1024,128]{1,0:T(8,128)(2,1)S(1)}, u32[]{:S(2)}, u32[]{:S(2)}) collective-permute-start(bf16[1024,128]{1,0:T(8,128)(2,1)S(1)} %step3_kernel.1.q_prev), channel_id=1, source_target_pairs={{23,31},{10,18},{17,29},{13,5}} | collective-permute-start | bytes 786440 | tf_op jit(solution)/shard_map/ppermute | solution.py:133
  25.1 2.7 %collective-permute-start.21 = (bf16[1024,128]{1,0:T(8,128)(2,1)S(1)}, bf16[1024,128]{1,0:T(8,128)(2,1)S(1)}, u32[]{:S(2)}, u32[]{:S(2)}) collective-permute-start(bf16[1024,128]{1,0:T(8,128)(2,1)S(1)} %step3_kernel.1.q_prev), channel_id=1, source_target_pairs={{23,19}} | collective-permute-start | bytes 786440 | tf_op jit(solution)/shard_map/ppermute | solution.py:133
  25.8 2.0 %collective-permute-start.22 = (bf16[1024,128]{1,0:T(8,128)(2,1)S(1)}, bf16[1024,128]{1,0:T(8,128)(2,1)S(1)}, u32[]{:S(2)}, u32[]{:S(2)}) collective-permute-start(bf16[1024,128]{1,0:T(8,128)(2,1)S(1)} %step3_kernel.1.q_prev), channel_id=1, source_target_pairs={{23,15},{14,6}} | collective-permute-start | bytes 786440 | tf_op jit(solution)/shard_map/ppermute | solution.py:133
  27.9 33.3 %collective-permute-start.23 = (bf16[1040,128]{1,0:T(8,128)(2,1)S(1)}, bf16[1040,128]{1,0:T(8,128)(2,1)S(1)}, u32[]{:S(2)}, u32[]{:S(2)}) collective-permute-start(bf16[1040,128]{1,0:T(8,128)(2,1)S(1)} %get-tuple-element.38.refs_0_), channel_id=1, source_target_pairs={{0,2},{1,3},{2,0},{3,1},{4,6},{5,7},{6,4},{7,5},{8,10},{9,11},{10,... | collective-permute-start | bytes 798728 | tf_op jit(solution)/shard_map/ppermute | solution.py:129
  47.8 12.7 %collective-permute-start.24 = (bf16[1024,128]{1,0:T(8,128)(2,1)S(1)}, bf16[1024,128]{1,0:T(8,128)(2,1)S(1)}, u32[]{:S(2)}, u32[]{:S(2)}) collective-permute-start(bf16[1024,128]{1,0:T(8,128)(2,1)S(1)} %get-tuple-element.36.q_ref), channel_id=1, source_target_pairs={{15,11},{27,3},{31,7},{10,2}} | collective-permute-start | bytes 786440 | tf_op jit(solution)/shard_map/ppermute | solution.py:133
  61.3 2.4 %collective-permute-start.25 = (bf16[1040,128]{1,0:T(8,128)(2,1)S(1)}, bf16[1040,128]{1,0:T(8,128)(2,1)S(1)}, u32[]{:S(2)}, u32[]{:S(2)}) collective-permute-start(bf16[1040,128]{1,0:T(8,128)(2,1)S(1)} %get-tuple-element.38.refs_0_), channel_id=1, source_target_pairs={{0,1},{1,0},{2,3},{3,2},{4,5},{5,4},{6,7},{7,6},{8,9},{9,8},{10,11... | collective-permute-start | bytes 798728 | tf_op jit(solution)/shard_map/ppermute | solution.py:129
  62.5 1.5 %collective-permute-start.26 = (bf16[1040,128]{1,0:T(8,128)(2,1)S(1)}, bf16[1040,128]{1,0:T(8,128)(2,1)S(1)}, u32[]{:S(2)}, u32[]{:S(2)}) collective-permute-start(bf16[1040,128]{1,0:T(8,128)(2,1)S(1)} %collective-permute-done.23.refs_2_), channel_id=1, source_target_pairs={{0,1},{1,0},{2,3},{3,2},{4,5},{5,4},{6,7},{7,6},{8,9},{9,8},{10,11... | collective-permute-start | bytes 798728 | tf_op jit(solution)/shard_map/ppermute | solution.py:129
  (7 other events, 46.0 us)

commit v14 on v13

--- a/solution.py
+++ b/solution.py
@@ -67,18 +67,18 @@
 FIRST = (1, 0)
 BESIDE = (3, 1)
 PARTNER = (None, (3, 1), (3, 3), (5, 2))
-PIECES = ((4, 1), (6, 3), (5, 2), (7, 0))
+PIECES = ((6, 3), (7, 0), (4, 2), (5, 1))
 SENDS = (
     (0, 1, 2, 3),
-    (0, 1, 2, 3),
+    (2, 1, 0, 3),
     (3, 1, 0, 2),
     (0, 1, 3, 2),
-    (0, 1, 3, 2),
+    (1, 3, 0, 2),
     (2, 1, 3, 0),
-    (0, 3, 1, 2),
-    (1, 3, 0, 2),
+    (0, 1, 2, 3),
+    (1, 0, 2, 3),
 )
-REST = ((2, 3), (0, 3), (1, 3), (0, 2))
+REST = ((3, 3), (0, 3), (1, 3))
 
 
 def hops(a, b):
@@ -171,66 +171,55 @@
 def cut_kernel(diag_ref, *refs):
     cuts, sem = refs[:-1], refs[-1]
     row, col = lax.axis_index("row"), lax.axis_index("col")
-    part = diag_ref.shape[1]
     k = jnp.int32(0)
     for r in range(NR):
         for c in range(NC):
             k = jnp.where((row == r) & (col == c), SENDS[r][c], k)
-    for m in range(NR // 2):
-
-        @pl.when(jnp.where((row == 1) & (k == 0), 1, row // 2) == m)
+    place = jnp.where(k > 0, row // 2, jnp.where(row < 4, 1, len(cuts) - 1))
+    for m, out in enumerate(cuts):
+
+        @pl.when(place == m)
         def _():
-            copy = pltpu.make_async_copy(diag_ref.at[k, :, pl.ds(0, pair_width(m, part))], cuts[m], sem)
+            copy = pltpu.make_async_copy(diag_ref.at[k, :, pl.ds(0, out.shape[1])], out, sem)
             copy.start()
             copy.wait()
 
 
-def first_kernel(rhs_ref, diag_ref, *refs):
-    parts, (out_ref, rhs_v, d_v, rhs_sem, d_sem) = refs[:-5], refs[-5:]
-    n = out_ref.shape[0] // 2
-    col = lax.axis_index("col")
+def first_kernel(rhs_ref, diag_ref, hi_ref, lo_ref, out_ref, rhs_v, lo_v, rhs_sem, lo_sem):
+    n, half = lo_ref.shape
 
     @pl.when(lax.axis_index("row") == 0)
     def _():
-        rhs_copy = pltpu.make_async_copy(rhs_ref.at[0], rhs_v, rhs_sem)
-        rhs_copy.start()
-
-        def pieces(c):
-            copies = []
-            for i, r in enumerate(PIECES[c]):
-                m = max(r // 2, 1)
-                wide = pair_width(m, n)
-                source = parts[m - 1] if r else diag_ref.at[0, :, pl.ds(0, wide)]
-                copies.append(pltpu.make_async_copy(source, d_v.at[i, :, pl.ds(0, wide)], d_sem.at[i]))
-            return copies
-
-        for c in range(NC):
-
-            @pl.when(col == c)
-            def _():
-                for copy in pieces(c):
-                    copy.start()
-
-        rhs_copy.wait()
+        copy = pltpu.make_async_copy(rhs_ref.at[0], rhs_v, rhs_sem)
+        copy.start()
+        own = pltpu.make_async_copy(diag_ref.at[0, :, pl.ds(0, half)], lo_v, lo_sem)
+        has_own = lax.axis_index("col") == [lo for _, lo in PIECES].index(0)
+
+        @pl.when(has_own)
+        def _():
+            own.start()
+            own.wait()
+
+        @pl.when(jnp.logical_not(has_own))
+        def _():
+            lo_v[...] = lo_ref[...]
+
+        copy.wait()
         p = low(rhs_v[...])
-        for c in range(NC):
-
-            @pl.when(col == c)
-            def _():
-                for i, copy in enumerate(pieces(c)):
-                    copy.wait()
-                    wide = pair_width(max(PIECES[c][i] // 2, 1), n)
-                    out_ref[i * n : (i + 1) * n] = low(dot(d_v[i, :, :wide], p[:wide]))
+        out_ref[:n] = low(dot(hi_ref[...], p))
+        out_ref[n:] = low(dot(lo_v[...], p[:half]))
 
 
 def pack_kernel(*refs):
-    parts, out_ref, sem = refs[:-2], refs[-2], refs[-1]
+    parts, out_ref, sem = refs[: NR // 2], refs[-2], refs[-1]
+    part = out_ref.shape[0]
 
     @pl.when(any_of(PARTNER[1:]))
     def _():
         copies, left = [], 0
-        for m, source in enumerate(parts):
-            wide = source.shape[1]
+        for m in range(NR // 2):
+            wide = pair_width(m, part)
+            (source,) = [p for p in parts if p.shape[1] == wide]
             copies.append(pltpu.make_async_copy(source, out_ref.at[:, pl.ds(left, wide)], sem.at[m]))
             left += wide
         for copy in copies:
@@ -406,7 +395,9 @@
     out_ref[pl.ds(size, TAIL)] = low(jnp.where(flag, 1.0, 0.0))
 
 
-def solved_kernel(q_ref, rest_ref, solved_ref):
+def final_kernel(q_ref, rest_ref, rhs_ref, *refs):
+    sums, (solved_ref, out_ref) = refs[:NC], refs[NC:]
+    size = out_ref.shape[1]
     came = any_of(REST)
 
     @pl.when(came)
@@ -417,10 +408,6 @@
     def _():
         solved_ref[...] = q_ref[...].astype(jnp.float32)
 
-
-def final_kernel(rhs_ref, *refs):
-    sums, out_ref = refs[:NC], refs[NC]
-    size = out_ref.shape[1]
     for i in range(out_ref.shape[0]):
         acc = rhs_ref[i]
         for s in sums:
@@ -439,44 +426,46 @@
     dma = pltpu.SemaphoreType.DMA
 
     wides = [pair_width(m, part) for m in range(NR // 2)]
-    cuts = call(
-        cut_kernel, [jax.ShapeDtypeStruct((part, w), bf16) for w in wides], [diag_inv], [HBM], [ANY] * len(wides), [dma]
-    )
-    at_piece = {r: (0, c) for c, rows in enumerate(PIECES) for r in rows}
+    *cuts, hi = call(
+        cut_kernel,
+        [jax.ShapeDtypeStruct((part, w), bf16) for w in wides + [size]],
+        [diag_inv],
+        [HBM],
+        [ANY] * (len(wides) + 1),
+        [dma],
+    )
+    source = {(r, k): (r, c) for r in range(NR) for c, k in enumerate(SENDS[r])}
+    hi = send_only(hi, [(source[rows[0], 0], (0, c)) for c, rows in enumerate(PIECES)])
     parts = []
     for m, cut in enumerate(cuts):
-        pairs = []
-        for r in range(NR):
-            for c, k in enumerate(SENDS[r]):
-                if k == 0 and r and max(r // 2, 1) == m:
-                    pairs.append(((r, c), at_piece[r]))
-                if k and MAKER[k][0] != r and r // 2 == m:
-                    pairs.append(((r, c), MAKER[k] if r % 2 else PARTNER[k]))
+        pairs = [
+            (source[r, k], MAKER[k] if r % 2 else PARTNER[k])
+            for r in (2 * m, 2 * m + 1)
+            for k in range(1, NC)
+            if MAKER[k][0] != r
+        ]
+        if m == 1:
+            pairs += [(source[rows[1], 0], (0, c)) for c, rows in enumerate(PIECES) if rows[1]]
         parts.append(send_only(cut, pairs))
     q = call(
         first_kernel,
         jax.ShapeDtypeStruct((2 * part, width), bf16),
-        [rhs, diag_inv, *parts[1:]],
-        [HBM, HBM] + [ANY] * (len(wides) - 1),
+        [rhs, diag_inv, hi, parts[1]],
+        [HBM, HBM, VMEM, VMEM],
         VMEM,
-        [
-            pltpu.VMEM((size, width), jnp.float32),
-            pltpu.VMEM((2, part, size), bf16),
-            dma,
-            pltpu.SemaphoreType.DMA((2,)),
-        ],
+        [pltpu.VMEM((size, width), jnp.float32), pltpu.VMEM((part, size // 2), bf16), dma, dma],
     )
     takers = (FIRST, (2, 0), (3, 0))
     got = [send(q, [((0, c), takers[(c + j) % 4]) for c in range(4) if (c + j) % 4 < 3]) for j in range(4)]
     even = call(
         pack_kernel,
         jax.ShapeDtypeStruct((part, sum(wides)), bf16),
-        parts,
-        [ANY] * len(wides),
+        [parts[2], parts[3], parts[1], parts[0], hi],
+        [ANY] * (len(wides) + 1),
         VMEM,
         [pltpu.SemaphoreType.DMA((len(wides),))],
     )
-    even = send(even, [(PARTNER[k], MAKER[k]) for k in range(1, NC)])
+    even = send_only(even, [(PARTNER[k], MAKER[k]) for k in range(1, NC)])
     diag = call(
         whole_kernel,
         jax.ShapeDtypeStruct((size, size), bf16),
@@ -519,8 +508,8 @@
             ((4, 0), (6, 0)), ((5, 0), (7, 0)), ((4, 1), (6, 1)), ((3, 1), (5, 1)), ((2, 1), (0, 1)),
         ],
         [(MAKER[3], (7, 3)), ((2, 2), (4, 2)), ((4, 1), (7, 1)), ((3, 1), (1, 1))],
-        [(MAKER[3], (4, 3))],
-        [(MAKER[3], (3, 3)), (MAKER[2], (1, 2))],
+        [(MAKER[3], (4, 3)), ((2, 2), (0, 2)), (MAKER[2], (1, 2))],
+        [(MAKER[3], (2, 3))],
     ]
     got = [send_only(q, pairs) for pairs in sends]
     takers = [[b for _, b in pairs] for pairs in sends]
@@ -536,17 +525,16 @@
         return send(value, [((r, c), (r, c ^ step)) for r in range(NR) for c in range(NC)])
 
     across = swap(mine, 2)
-    rest = send_only(q, list(zip(((3, 3), (6, 3), (7, 3), (2, 2)), REST)))
-    solved = call(solved_kernel, jax.ShapeDtypeStruct((size, width), jnp.float32), [q, rest], [VMEM] * 2, VMEM)
-    beside, across, solved = lax.optimization_barrier((mine, across, solved))
+    rest = send_only(q, list(zip(((2, 3), (6, 3), (7, 3)), REST)))
+    beside, across, rest = lax.optimization_barrier((mine, across, rest))
     beside = swap(beside, 1)
     corner = swap(across, 1)
-    remainder = call(
+    solved, remainder = call(
         final_kernel,
-        jax.ShapeDtypeStruct(rhs.shape, jnp.float32),
-        [rhs, mine, beside, across, corner],
-        [VMEM] * 5,
-        VMEM,
+        [jax.ShapeDtypeStruct((size, width), jnp.float32), jax.ShapeDtypeStruct(rhs.shape, jnp.float32)],
+        [q, rest, rhs, mine, beside, across, corner],
+        [VMEM] * 7,
+        [VMEM] * 2,
     )
     return solved[None, None], remainder[:, None]
 

time: 66.2 us -> 68.1 us (1.029)
  starting transfers between devices: 41.3 us -> 43.5 us
  waiting for transfers between devices: 17.9 us -> 18.8 us
  Pallas kernels: 2.65 us -> 1.88 us
    ppermute x12 -> x14, starting transfers between devices: 14.9 us -> 16.4 us  [send_only(): lax.ppermute(value, ('row', 'col'), [(a * NC + b, c * NC + d) for (a, b),...]
    ppermute x12 -> x14, waiting for transfers between devices: 12.7 us -> 13.7 us  [send_only(): lax.ppermute(value, ('row', 'col'), [(a * NC + b, c * NC + d) for (a, b),...]
    pallas_call x12 -> x11, Pallas kernels: 2.65 us -> 1.88 us  [call(): pl.pallas_call(kernel, out_shape=outs, in_specs=in_specs, out_specs=out_s...]
    ppermute x15 -> x14, starting transfers between devices: 26.4 us -> 27.1 us  [send(): lax.ppermute(value, ('row', 'col'), [(a * NC + b, c * NC + d) for (a, b),...]
    ppermute x15 -> x14, waiting for transfers between devices: 5.2 us -> 5.17 us  [send(): lax.ppermute(value, ('row', 'col'), [(a * NC + b, c * NC + d) for (a, b),...]
  transfers between devices with their start and end apart: 27 -> 28, of which waited for: 13 -> 13; matrix products, arithmetic and copies ran while one was open for 0% -> 0% of each run, Pallas kernels for 1% -> 0%
where the time goes in v14:
time: 68.1 us; the launch traced here: 67.8 us
  starting transfers between devices  43.5 us (64%)
  waiting for transfers between devices  18.8 us (28%)
  between operations  2.24 us (3%)
  Pallas kernels  1.88 us (3%)
  local copies, waits for them, and re-layouts  1.32 us (2%)
    ppermute x14, starting transfers between devices, send(): lax.ppermute(value, ('row', 'col'), [(a * NC + b, c * NC + d) for (a, b),...  27.1 us
    ppermute x14, starting transfers between devices, send_only(): lax.ppermute(value, ('row', 'col'), [(a * NC + b, c * NC + d) for (a, b),...  16.4 us
    ppermute x14, waiting for transfers between devices, send_only(): lax.ppermute(value, ('row', 'col'), [(a * NC + b, c * NC + d) for (a, b),...  13.7 us
    ppermute x14, waiting for transfers between devices, send(): lax.ppermute(value, ('row', 'col'), [(a * NC + b, c * NC + d) for (a, b),...  5.17 us
    pallas_call x11, Pallas kernels, call(): pl.pallas_call(kernel, out_shape=outs, in_specs=in_specs, out_specs=out_s...  1.88 us
  transfers between devices with their start and end apart: 28, of which 13 were waited for; matrix products, arithmetic and copies ran while one was open for 0% of the time, Pallas kernels for 0%

profile of v14, /device:TPU:7, one launch (start us, length us, event | category | flops | bytes accessed | tf_op | source)
XLA Modules:
  0.0 67.8 jit_solution(3682421304136880963)
XLA Ops:
  0.6 1.3 %copy-done.2 = bf16[4,128,1024]{2,1,0:T(8,128)(2,1)S(1)} copy-done((bf16[4,128,1024]{2,1,0:T(8,128)(2,1)S(1)}, bf16[4,128,1024]{2,1,0:T(8,128)(2,1)}, u32[]{:S(2)}) %copy-start.2) | copy-done | bytes 1048600
  2.0 0.8 %collective-permute-start = (bf16[128,1024]{1,0:T(8,128)(2,1)S(1)}, bf16[128,1024]{1,0:T(8,128)(2,1)S(1)}, u32[]{:S(2)}, u32[]{:S(2)}) collective-permute-start(bf16[128,1024]{1,0:T(8,128)(2,1)S(1)} %get-tuple-element.24), channel_id=1, source_target_pairs={{24,0},{29,1},{18,2},{23,3}} | collective-permute-start | bytes 786440 | tf_op jit(solution)/shard_map/ppermute | solution.py:133
  2.8 0.8 %collective-permute-start.8 = (bf16[128,1024]{1,0:T(8,128)(2,1)S(1)}, bf16[128,1024]{1,0:T(8,128)(2,1)S(1)}, u32[]{:S(2)}, u32[]{:S(2)}) collective-permute-start(bf16[128,1024]{1,0:T(8,128)(2,1)S(1)} %get-tuple-element.28), channel_id=1, source_target_pairs={{25,13},{26,15},{27,22},{28,9},{30,14},{31,23}} | collective-permute-start | bytes 786440 | tf_op jit(solution)/shard_map/ppermute | solution.py:133
  3.6 0.7 collective-permute-start.7
  4.3 0.7 collective-permute-start.1
  5.0 6.7 %collective-permute-start.9 = (bf16[128,256]{1,0:T(8,128)(2,1)S(1)}, bf16[128,256]{1,0:T(8,128)(2,1)S(1)}, u32[]{:S(2)}, u32[]{:S(2)}) collective-permute-start(bf16[128,256]{1,0:T(8,128)(2,1)S(1)} %get-tuple-element.29), channel_id=1, source_target_pairs={{1,13},{2,15},{3,22},{5,9},{4,14},{7,23}} | collective-permute-start | bytes 196616 | tf_op jit(solution)/shard_map/ppermute | solution.py:133
  11.7 1.3 %collective-permute-done.9.refs_3_.refs_0_ = bf16[128,256]{1,0:T(8,128)(2,1)S(1)} collective-permute-done((bf16[128,256]{1,0:T(8,128)(2,1)S(1)}, bf16[128,256]{1,0:T(8,128)(2,1)S(1)}, u32[]{:S(2)}, u32[]{:S(2)}) %collective-permute-start.9) | collective-permute-done | bytes 65568 | tf_op jit(solution)/shard_map/ppermute | solution.py:133
  13.1 0.7 %collective-permute-start.10 = (bf16[128,2560]{1,0:T(8,128)(2,1)S(1)}, bf16[128,2560]{1,0:T(8,128)(2,1)S(1)}, u32[]{:S(2)}, u32[]{:S(2)}) collective-permute-start(bf16[128,2560]{1,0:T(8,128)(2,1)S(1)} %pack_kernel.1), channel_id=1, source_target_pairs={{13,9},{15,14},{22,23}} | collective-permute-start | bytes 1966088 | tf_op jit(solution)/shard_map/ppermute | solution.py:133
  14.0 0.5 collective-permute-start.3
  16.5 0.9 %collective-permute-done.6.p_in = bf16[1024,128]{1,0:T(8,128)(2,1)S(1)} collective-permute-done((bf16[1024,128]{1,0:T(8,128)(2,1)S(1)}, bf16[1024,128]{1,0:T(8,128)(2,1)S(1)}, u32[]{:S(2)}, u32[]{:S(2)}) %collective-permute-start.6) | collective-permute-done | bytes 262176 | tf_op jit(solution)/shard_map/ppermute | solution.py:129
  18.8 0.7 collective-permute-done.12.p_in
  20.8 0.7 collective-permute-start.17
  21.5 0.7 collective-permute-start.18
  22.1 0.7 collective-permute-start.19
  23.0 0.7 collective-permute-start.20
  23.6 0.7 collective-permute-start.21
  24.3 0.7 collective-permute-start.22
  25.0 0.7 collective-permute-start.23
  27.2 23.1 %collective-permute-start.24 = (bf16[1040,128]{1,0:T(8,128)(2,1)S(1)}, bf16[1040,128]{1,0:T(8,128)(2,1)S(1)}, u32[]{:S(2)}, u32[]{:S(2)}) collective-permute-start(bf16[1040,128]{1,0:T(8,128)(2,1)S(1)} %get-tuple-element.42.refs_0_), channel_id=1, source_target_pairs={{0,2},{1,3},{2,0},{3,1},{4,6},{5,7},{6,4},{7,5},{8,10},{9,11},{10,... | collective-permute-start | bytes 798728 | tf_op jit(solution)/shard_map/ppermute | solution.py:129
  50.2 1.3 %collective-permute-start.25 = (bf16[1024,128]{1,0:T(8,128)(2,1)S(1)}, bf16[1024,128]{1,0:T(8,128)(2,1)S(1)}, u32[]{:S(2)}, u32[]{:S(2)}) collective-permute-start(bf16[1024,128]{1,0:T(8,128)(2,1)S(1)} %get-tuple-element.39.q_ref), channel_id=1, source_target_pairs={{11,15},{27,3},{31,7}} | collective-permute-start | bytes 786440 | tf_op jit(solution)/shard_map/ppermute | solution.py:133
  51.5 12.3 %collective-permute-done.25.rest_ref = bf16[1024,128]{1,0:T(8,128)(2,1)S(1)} collective-permute-done((bf16[1024,128]{1,0:T(8,128)(2,1)S(1)}, bf16[1024,128]{1,0:T(8,128)(2,1)S(1)}, u32[]{:S(2)}, u32[]{:S(2)}) %collective-permute-start.25) | collective-permute-done | bytes 262176 | tf_op jit(solution)/shard_map/ppermute | solution.py:133
  63.8 0.9 %collective-permute-start.26 = (bf16[1040,128]{1,0:T(8,128)(2,1)S(1)}, bf16[1040,128]{1,0:T(8,128)(2,1)S(1)}, u32[]{:S(2)}, u32[]{:S(2)}) collective-permute-start(bf16[1040,128]{1,0:T(8,128)(2,1)S(1)} %get-tuple-element.42.refs_0_), channel_id=1, source_target_pairs={{0,1},{1,0},{2,3},{3,2},{4,5},{5,4},{6,7},{7,6},{8,9},{9,8},{10,11... | collective-permute-start | bytes 798728 | tf_op jit(solution)/shard_map/ppermute | solution.py:129
  64.8 1.2 %collective-permute-done.26.refs_1_ = bf16[1040,128]{1,0:T(8,128)(2,1)S(1)} collective-permute-done((bf16[1040,128]{1,0:T(8,128)(2,1)S(1)}, bf16[1040,128]{1,0:T(8,128)(2,1)S(1)}, u32[]{:S(2)}, u32[]{:S(2)}) %collective-permute-start.26) | collective-permute-done | bytes 266272 | tf_op jit(solution)/shard_map/ppermute | solution.py:129
  66.3 1.4 %final_kernel.1 = (f32[1024,128]{1,0:T(8,128)}, f32[2,1024,128]{2,1,0:T(8,128)}) custom-call(bf16[1024,128]{1,0:T(8,128)(2,1)S(1)} %get-tuple-element.39.q_ref, bf16[1024,128]{1,0:T(8,128)(2,1)S(1)} %collective-permute-done.25.rest_ref, f32[2,1024,128]{2,1,0:T(8,128)S(1)} %bitcast.14, bf16[1040,128]{1,0:T(8,128)(2,1)S(1)} %get-tuple-element.42.refs_0_, ...), custom_call_target="tpu_custom_call" | custom-call | tf_op jit(solution)/shard_map/final_kernel/pallas_call | solution.py:156
  (51 shorter events, 5.5 us)
Async XLA Ops:
  2.0 11.0 %collective-permute-start = (bf16[128,1024]{1,0:T(8,128)(2,1)S(1)}, bf16[128,1024]{1,0:T(8,128)(2,1)S(1)}, u32[]{:S(2)}, u32[]{:S(2)}) collective-permute-start(bf16[128,1024]{1,0:T(8,128)(2,1)S(1)} %get-tuple-element.24), channel_id=1, source_target_pairs={{24,0},{29,1},{18,2},{23,3}} | collective-permute-start | bytes 786440 | tf_op jit(solution)/shard_map/ppermute | solution.py:133
  2.8 10.2 %collective-permute-start.8 = (bf16[128,1024]{1,0:T(8,128)(2,1)S(1)}, bf16[128,1024]{1,0:T(8,128)(2,1)S(1)}, u32[]{:S(2)}, u32[]{:S(2)}) collective-permute-start(bf16[128,1024]{1,0:T(8,128)(2,1)S(1)} %get-tuple-element.28), channel_id=1, source_target_pairs={{25,13},{26,15},{27,22},{28,9},{30,14},{31,23}} | collective-permute-start | bytes 786440 | tf_op jit(solution)/shard_map/ppermute | solution.py:133
  3.6 9.4 %collective-permute-start.7 = (bf16[128,768]{1,0:T(8,128)(2,1)S(1)}, bf16[128,768]{1,0:T(8,128)(2,1)S(1)}, u32[]{:S(2)}, u32[]{:S(2)}) collective-permute-start(bf16[128,768]{1,0:T(8,128)(2,1)S(1)} %get-tuple-element.27), channel_id=1, source_target_pairs={{16,13},{19,15},{17,22},{21,9},{20,14}} | collective-permute-start | bytes 589832 | tf_op jit(solution)/shard_map/ppermute | solution.py:133
  4.3 8.7 %collective-permute-start.1 = (bf16[128,512]{1,0:T(8,128)(2,1)S(1)}, bf16[128,512]{1,0:T(8,128)(2,1)S(1)}, u32[]{:S(2)}, u32[]{:S(2)}) collective-permute-start(bf16[128,512]{1,0:T(8,128)(2,1)S(1)} %get-tuple-element.25), channel_id=1, source_target_pairs={{11,15},{8,22},{13,9},{14,23},{12,0},{10,2},{6,3}} | collective-permute-start | bytes 393224 | tf_op jit(solution)/shard_map/ppermute | solution.py:133
  5.0 8.0 %collective-permute-start.9 = (bf16[128,256]{1,0:T(8,128)(2,1)S(1)}, bf16[128,256]{1,0:T(8,128)(2,1)S(1)}, u32[]{:S(2)}, u32[]{:S(2)}) collective-permute-start(bf16[128,256]{1,0:T(8,128)(2,1)S(1)} %get-tuple-element.29), channel_id=1, source_target_pairs={{1,13},{2,15},{3,22},{5,9},{4,14},{7,23}} | collective-permute-start | bytes 196616 | tf_op jit(solution)/shard_map/ppermute | solution.py:133
  13.1 3.3 %collective-permute-start.10 = (bf16[128,2560]{1,0:T(8,128)(2,1)S(1)}, bf16[128,2560]{1,0:T(8,128)(2,1)S(1)}, u32[]{:S(2)}, u32[]{:S(2)}) collective-permute-start(bf16[128,2560]{1,0:T(8,128)(2,1)S(1)} %pack_kernel.1), channel_id=1, source_target_pairs={{13,9},{15,14},{22,23}} | collective-permute-start | bytes 1966088 | tf_op jit(solution)/shard_map/ppermute | solution.py:133
  14.0 1.4 %collective-permute-start.3 = (bf16[256,128]{1,0:T(8,128)(2,1)S(1)}, bf16[256,128]{1,0:T(8,128)(2,1)S(1)}, u32[]{:S(2)}, u32[]{:S(2)}) collective-permute-start(bf16[256,128]{1,0:T(8,128)(2,1)S(1)} %first_kernel.1), channel_id=1, source_target_pairs={{0,8},{1,12},{2,3},{3,4},{4,5},{5,0},{6,7},{7,6},{8,9},{9,1},{10,1... | collective-permute-start | bytes 196616 | tf_op jit(solution)/shard_map/ppermute | solution.py:129
  15.9 1.5 %collective-permute-start.6 = (bf16[1024,128]{1,0:T(8,128)(2,1)S(1)}, bf16[1024,128]{1,0:T(8,128)(2,1)S(1)}, u32[]{:S(2)}, u32[]{:S(2)}) collective-permute-start(bf16[1024,128]{1,0:T(8,128)(2,1)S(1)} %get-tuple-element.26), channel_id=1, source_target_pairs={{0,1},{1,0},{2,3},{3,2},{4,9},{5,4},{6,7},{7,6},{8,5},{9,8},{10,11... | collective-permute-start | bytes 786440 | tf_op jit(solution)/shard_map/ppermute | solution.py:129
  16.2 1.6 %collective-permute-start.11 = (bf16[1024,128]{1,0:T(8,128)(2,1)S(1)}, bf16[1024,128]{1,0:T(8,128)(2,1)S(1)}, u32[]{:S(2)}, u32[]{:S(2)}) collective-permute-start(bf16[1024,128]{1,0:T(8,128)(2,1)S(1)} %get-tuple-element.31.s_prev), channel_id=1, source_target_pairs={{0,1},{1,0},{2,3},{3,2},{4,5},{5,4},{6,7},{7,6},{8,9},{9,8},{10,11... | collective-permute-start | bytes 786440 | tf_op jit(solution)/shard_map/ppermute | solution.py:129
  17.8 1.6 %collective-permute-start.12 = (bf16[1024,128]{1,0:T(8,128)(2,1)S(1)}, bf16[1024,128]{1,0:T(8,128)(2,1)S(1)}, u32[]{:S(2)}, u32[]{:S(2)}) collective-permute-start(bf16[1024,128]{1,0:T(8,128)(2,1)S(1)} %get-tuple-element.32), channel_id=1, source_target_pairs={{0,1},{1,0},{2,3},{3,2},{4,5},{5,4},{6,7},{7,6},{8,9},{9,14},{10,1... | collective-permute-start | bytes 786440 | tf_op jit(solution)/shard_map/ppermute | solution.py:129
  18.2 1.6 %collective-permute-start.13 = (bf16[1024,128]{1,0:T(8,128)(2,1)S(1)}, bf16[1024,128]{1,0:T(8,128)(2,1)S(1)}, u32[]{:S(2)}, u32[]{:S(2)}) collective-permute-start(bf16[1024,128]{1,0:T(8,128)(2,1)S(1)} %step1_kernel.1.q_in.q_prev), channel_id=1, source_target_pairs={{0,1},{1,5},{2,3},{3,2},{4,0},{5,4},{6,7},{7,6},{8,16},{9,17},{10,... | collective-permute-start | bytes 786440 | tf_op jit(solution)/shard_map/ppermute | solution.py:129
  18.4 1.8 %collective-permute-start.14 = (bf16[1024,128]{1,0:T(8,128)(2,1)S(1)}, bf16[1024,128]{1,0:T(8,128)(2,1)S(1)}, u32[]{:S(2)}, u32[]{:S(2)}) collective-permute-start(bf16[1024,128]{1,0:T(8,128)(2,1)S(1)} %step1_kernel.1.q_in.q_prev), channel_id=1, source_target_pairs={{0,1},{1,0},{2,3},{3,2},{4,5},{5,4},{6,7},{7,6},{8,9},{9,13},{10,1... | collective-permute-start | bytes 786440 | tf_op jit(solution)/shard_map/ppermute | solution.py:129
  20.2 2.6 %collective-permute-start.15 = (bf16[1024,128]{1,0:T(8,128)(2,1)S(1)}, bf16[1024,128]{1,0:T(8,128)(2,1)S(1)}, u32[]{:S(2)}, u32[]{:S(2)}) collective-permute-start(bf16[1024,128]{1,0:T(8,128)(2,1)S(1)} %get-tuple-element.36), channel_id=1, source_target_pairs={{0,1},{1,0},{2,3},{3,2},{4,5},{5,4},{6,7},{7,6},{8,9},{9,8},{10,11... | collective-permute-start | bytes 786440 | tf_op jit(solution)/shard_map/ppermute | solution.py:129
  20.6 2.2 %collective-permute-start.16 = (bf16[1024,128]{1,0:T(8,128)(2,1)S(1)}, bf16[1024,128]{1,0:T(8,128)(2,1)S(1)}, u32[]{:S(2)}, u32[]{:S(2)}) collective-permute-start(bf16[1024,128]{1,0:T(8,128)(2,1)S(1)} %get-tuple-element.35.s_ref), channel_id=1, source_target_pairs={{0,1},{1,0},{2,3},{3,2},{4,5},{5,4},{6,7},{7,6},{8,9},{9,8},{10,11... | collective-permute-start | bytes 786440 | tf_op jit(solution)/shard_map/ppermute | solution.py:129
  20.8 2.1 %collective-permute-start.17 = (bf16[1024,128]{1,0:T(8,128)(2,1)S(1)}, bf16[1024,128]{1,0:T(8,128)(2,1)S(1)}, u32[]{:S(2)}, u32[]{:S(2)}) collective-permute-start(bf16[1024,128]{1,0:T(8,128)(2,1)S(1)} %get-tuple-element.36), channel_id=1, source_target_pairs={{14,10}} | collective-permute-start | bytes 786440 | tf_op jit(solution)/shard_map/ppermute | solution.py:133
  21.5 1.4 %collective-permute-start.18 = (bf16[1024,128]{1,0:T(8,128)(2,1)S(1)}, bf16[1024,128]{1,0:T(8,128)(2,1)S(1)}, u32[]{:S(2)}, u32[]{:S(2)}) collective-permute-start(bf16[1024,128]{1,0:T(8,128)(2,1)S(1)} %get-tuple-element.36), channel_id=1, source_target_pairs={{14,30}} | collective-permute-start | bytes 786440 | tf_op jit(solution)/shard_map/ppermute | solution.py:133
  23.0 4.0 %collective-permute-start.20 = (bf16[1024,128]{1,0:T(8,128)(2,1)S(1)}, bf16[1024,128]{1,0:T(8,128)(2,1)S(1)}, u32[]{:S(2)}, u32[]{:S(2)}) collective-permute-start(bf16[1024,128]{1,0:T(8,128)(2,1)S(1)} %step3_kernel.1.q_prev), channel_id=1, source_target_pairs={{23,27},{10,26},{16,24},{20,28},{17,25},{13,21},{9,1}} | collective-permute-start | bytes 786440 | tf_op jit(solution)/shard_map/ppermute | solution.py:133
  23.6 3.4 %collective-permute-start.21 = (bf16[1024,128]{1,0:T(8,128)(2,1)S(1)}, bf16[1024,128]{1,0:T(8,128)(2,1)S(1)}, u32[]{:S(2)}, u32[]{:S(2)}) collective-permute-start(bf16[1024,128]{1,0:T(8,128)(2,1)S(1)} %step3_kernel.1.q_prev), channel_id=1, source_target_pairs={{23,31},{10,18},{17,29},{13,5}} | collective-permute-start | bytes 786440 | tf_op jit(solution)/shard_map/ppermute | solution.py:133
  24.3 2.7 %collective-permute-start.22 = (bf16[1024,128]{1,0:T(8,128)(2,1)S(1)}, bf16[1024,128]{1,0:T(8,128)(2,1)S(1)}, u32[]{:S(2)}, u32[]{:S(2)}) collective-permute-start(bf16[1024,128]{1,0:T(8,128)(2,1)S(1)} %step3_kernel.1.q_prev), channel_id=1, source_target_pairs={{23,19},{10,2},{14,6}} | collective-permute-start | bytes 786440 | tf_op jit(solution)/shard_map/ppermute | solution.py:133
  25.0 2.0 %collective-permute-start.23 = (bf16[1024,128]{1,0:T(8,128)(2,1)S(1)}, bf16[1024,128]{1,0:T(8,128)(2,1)S(1)}, u32[]{:S(2)}, u32[]{:S(2)}) collective-permute-start(bf16[1024,128]{1,0:T(8,128)(2,1)S(1)} %step3_kernel.1.q_prev), channel_id=1, source_target_pairs={{23,11}} | collective-permute-start | bytes 786440 | tf_op jit(solution)/shard_map/ppermute | solution.py:133
  27.2 36.7 %collective-permute-start.24 = (bf16[1040,128]{1,0:T(8,128)(2,1)S(1)}, bf16[1040,128]{1,0:T(8,128)(2,1)S(1)}, u32[]{:S(2)}, u32[]{:S(2)}) collective-permute-start(bf16[1040,128]{1,0:T(8,128)(2,1)S(1)} %get-tuple-element.42.refs_0_), channel_id=1, source_target_pairs={{0,2},{1,3},{2,0},{3,1},{4,6},{5,7},{6,4},{7,5},{8,10},{9,11},{10,... | collective-permute-start | bytes 798728 | tf_op jit(solution)/shard_map/ppermute | solution.py:129
  50.2 13.6 %collective-permute-start.25 = (bf16[1024,128]{1,0:T(8,128)(2,1)S(1)}, bf16[1024,128]{1,0:T(8,128)(2,1)S(1)}, u32[]{:S(2)}, u32[]{:S(2)}) collective-permute-start(bf16[1024,128]{1,0:T(8,128)(2,1)S(1)} %get-tuple-element.39.q_ref), channel_id=1, source_target_pairs={{11,15},{27,3},{31,7}} | collective-permute-start | bytes 786440 | tf_op jit(solution)/shard_map/ppermute | solution.py:133
  63.8 2.1 %collective-permute-start.26 = (bf16[1040,128]{1,0:T(8,128)(2,1)S(1)}, bf16[1040,128]{1,0:T(8,128)(2,1)S(1)}, u32[]{:S(2)}, u32[]{:S(2)}) collective-permute-start(bf16[1040,128]{1,0:T(8,128)(2,1)S(1)} %get-tuple-element.42.refs_0_), channel_id=1, source_target_pairs={{0,1},{1,0},{2,3},{3,2},{4,5},{5,4},{6,7},{7,6},{8,9},{9,8},{10,11... | collective-permute-start | bytes 798728 | tf_op jit(solution)/shard_map/ppermute | solution.py:129
  64.8 1.5 %collective-permute-start.27 = (bf16[1040,128]{1,0:T(8,128)(2,1)S(1)}, bf16[1040,128]{1,0:T(8,128)(2,1)S(1)}, u32[]{:S(2)}, u32[]{:S(2)}) collective-permute-start(bf16[1040,128]{1,0:T(8,128)(2,1)S(1)} %collective-permute-done.24.refs_2_), channel_id=1, source_target_pairs={{0,1},{1,0},{2,3},{3,2},{4,5},{5,4},{6,7},{7,6},{8,9},{9,8},{10,11... | collective-permute-start | bytes 798728 | tf_op jit(solution)/shard_map/ppermute | solution.py:129
  (8 other events, 44.9 us)

commit v15 on v13

--- a/solution.py
+++ b/solution.py
@@ -78,7 +78,7 @@
     (0, 3, 1, 2),
     (1, 3, 0, 2),
 )
-REST = ((2, 3), (0, 3), (1, 3), (0, 2))
+REST = ((3, 3), (0, 3), (1, 3))
 
 
 def hops(a, b):
@@ -406,7 +406,9 @@
     out_ref[pl.ds(size, TAIL)] = low(jnp.where(flag, 1.0, 0.0))
 
 
-def solved_kernel(q_ref, rest_ref, solved_ref):
+def final_kernel(q_ref, rest_ref, rhs_ref, *refs):
+    sums, (solved_ref, out_ref) = refs[:NC], refs[NC:]
+    size = out_ref.shape[1]
     came = any_of(REST)
 
     @pl.when(came)
@@ -417,10 +419,6 @@
     def _():
         solved_ref[...] = q_ref[...].astype(jnp.float32)
 
-
-def final_kernel(rhs_ref, *refs):
-    sums, out_ref = refs[:NC], refs[NC]
-    size = out_ref.shape[1]
     for i in range(out_ref.shape[0]):
         acc = rhs_ref[i]
         for s in sums:
@@ -502,7 +500,7 @@
     from_c = a
     a = send(a, [(BESIDE, MAKER[3])])
     sums = send(s, [(MAKER[2], MAKER[3])])
-    early = ((2, 2), (7, 2), (5, 2))
+    early = ((2, 2), (7, 2), (4, 2))
     got = [send_only(from_c, [(MAKER[2], d)]) for d in early]
     q = call(
         functools.partial(step3_kernel, [[d] for d in early] + [took]),
@@ -515,12 +513,12 @@
 
     sends = [
         [
-            (MAKER[3], (6, 3)), ((2, 2), (6, 2)),
+            (MAKER[3], (6, 3)), ((2, 2), (6, 2)), ((4, 2), (5, 2)),
             ((4, 0), (6, 0)), ((5, 0), (7, 0)), ((4, 1), (6, 1)), ((3, 1), (5, 1)), ((2, 1), (0, 1)),
         ],
-        [(MAKER[3], (7, 3)), ((2, 2), (4, 2)), ((4, 1), (7, 1)), ((3, 1), (1, 1))],
+        [(MAKER[3], (7, 3)), ((2, 2), (0, 2)), (MAKER[2], (1, 2)), ((4, 1), (7, 1)), ((3, 1), (1, 1))],
         [(MAKER[3], (4, 3))],
-        [(MAKER[3], (3, 3)), (MAKER[2], (1, 2))],
+        [(MAKER[3], (2, 3))],
     ]
     got = [send_only(q, pairs) for pairs in sends]
     takers = [[b for _, b in pairs] for pairs in sends]
@@ -536,17 +534,16 @@
         return send(value, [((r, c), (r, c ^ step)) for r in range(NR) for c in range(NC)])
 
     across = swap(mine, 2)
-    rest = send_only(q, list(zip(((3, 3), (6, 3), (7, 3), (2, 2)), REST)))
-    solved = call(solved_kernel, jax.ShapeDtypeStruct((size, width), jnp.float32), [q, rest], [VMEM] * 2, VMEM)
-    beside, across, solved = lax.optimization_barrier((mine, across, solved))
+    rest = send_only(q, list(zip(((2, 3), (6, 3), (7, 3)), REST)))
+    beside, across, rest = lax.optimization_barrier((mine, across, rest))
     beside = swap(beside, 1)
     corner = swap(across, 1)
-    remainder = call(
+    solved, remainder = call(
         final_kernel,
-        jax.ShapeDtypeStruct(rhs.shape, jnp.float32),
-        [rhs, mine, beside, across, corner],
-        [VMEM] * 5,
-        VMEM,
+        [jax.ShapeDtypeStruct((size, width), jnp.float32), jax.ShapeDtypeStruct(rhs.shape, jnp.float32)],
+        [q, rest, rhs, mine, beside, across, corner],
+        [VMEM] * 7,
+        [VMEM] * 2,
     )
     return solved[None, None], remainder[:, None]
 

time: 66.2 us -> 64.8 us (0.979)
  Pallas kernels: 2.65 us -> 1.86 us
  starting transfers between devices: 41.3 us -> 40.6 us
    pallas_call x12 -> x11, Pallas kernels: 2.65 us -> 1.86 us  [call(): pl.pallas_call(kernel, out_shape=outs, in_specs=in_specs, out_specs=out_s...]
    ppermute x15, starting transfers between devices: 26.4 us -> 25.7 us  [send(): lax.ppermute(value, ('row', 'col'), [(a * NC + b, c * NC + d) for (a, b),...]
  transfers between devices with their start and end apart: 27 -> 27, of which waited for: 13 -> 13; matrix products, arithmetic and copies ran while one was open for 0% -> 0% of each run, Pallas kernels for 1% -> 0%
where the time goes in v15:
time: 64.8 us; the launch traced here: 63.8 us
  starting transfers between devices  40.6 us (63%)
  waiting for transfers between devices  17.8 us (27%)
  between operations  2.19 us (3%)
  Pallas kernels  1.86 us (3%)
  local copies, waits for them, and re-layouts  1.32 us (2%)
    ppermute x15, starting transfers between devices, send(): lax.ppermute(value, ('row', 'col'), [(a * NC + b, c * NC + d) for (a, b),...  25.7 us
    ppermute x12, starting transfers between devices, send_only(): lax.ppermute(value, ('row', 'col'), [(a * NC + b, c * NC + d) for (a, b),...  14.9 us
    ppermute x12, waiting for transfers between devices, send_only(): lax.ppermute(value, ('row', 'col'), [(a * NC + b, c * NC + d) for (a, b),...  12.7 us
    ppermute x15, waiting for transfers between devices, send(): lax.ppermute(value, ('row', 'col'), [(a * NC + b, c * NC + d) for (a, b),...  5.07 us
    pallas_call x11, Pallas kernels, call(): pl.pallas_call(kernel, out_shape=outs, in_specs=in_specs, out_specs=out_s...  1.86 us
    unnamed x8, local copies, waits for them, and re-layouts  1.32 us
  transfers between devices with their start and end apart: 27, of which 13 were waited for; matrix products, arithmetic and copies ran while one was open for 0% of the time, Pallas kernels for 0%

profile of v15, /device:TPU:7, one launch (start us, length us, event | category | flops | bytes accessed | tf_op | source)
XLA Modules:
  0.0 63.8 jit_solution(9855290670467691424)
XLA Ops:
  0.6 1.3 %copy-done.2 = bf16[4,128,1024]{2,1,0:T(8,128)(2,1)S(1)} copy-done((bf16[4,128,1024]{2,1,0:T(8,128)(2,1)S(1)}, bf16[4,128,1024]{2,1,0:T(8,128)(2,1)}, u32[]{:S(2)}) %copy-start.2) | copy-done | bytes 1048600
  2.0 0.8 %collective-permute-start.2 = (bf16[128,1024]{1,0:T(8,128)(2,1)S(1)}, bf16[128,1024]{1,0:T(8,128)(2,1)S(1)}, u32[]{:S(2)}, u32[]{:S(2)}) collective-permute-start(bf16[128,1024]{1,0:T(8,128)(2,1)S(1)} %get-tuple-element.25), channel_id=1, source_target_pairs={{24,1},{25,22},{26,13},{27,15},{28,9},{29,23},{30,3},{31,14}} | collective-permute-start | bytes 786440 | tf_op jit(solution)/shard_map/ppermute | solution.py:133
  2.8 0.8 %collective-permute-start.1 = (bf16[128,768]{1,0:T(8,128)(2,1)S(1)}, bf16[128,768]{1,0:T(8,128)(2,1)S(1)}, u32[]{:S(2)}, u32[]{:S(2)}) collective-permute-start(bf16[128,768]{1,0:T(8,128)(2,1)S(1)} %get-tuple-element.24), channel_id=1, source_target_pairs={{16,0},{17,13},{18,22},{19,15},{20,14},{21,9},{23,2}} | collective-permute-start | bytes 589832 | tf_op jit(solution)/shard_map/ppermute | solution.py:133
  3.6 0.7 %collective-permute-start = (bf16[128,512]{1,0:T(8,128)(2,1)S(1)}, bf16[128,512]{1,0:T(8,128)(2,1)S(1)}, u32[]{:S(2)}, u32[]{:S(2)}) collective-permute-start(bf16[128,512]{1,0:T(8,128)(2,1)S(1)} %get-tuple-element.23), channel_id=1, source_target_pairs={{4,0},{8,22},{10,2},{11,15},{12,1},{13,9},{14,23}} | collective-permute-start | bytes 393224 | tf_op jit(solution)/shard_map/ppermute | solution.py:133
  4.3 6.6 %collective-permute-start.8 = (bf16[128,256]{1,0:T(8,128)(2,1)S(1)}, bf16[128,256]{1,0:T(8,128)(2,1)S(1)}, u32[]{:S(2)}, u32[]{:S(2)}) collective-permute-start(bf16[128,256]{1,0:T(8,128)(2,1)S(1)} %get-tuple-element.27), channel_id=1, source_target_pairs={{1,13},{2,15},{3,22},{5,9},{6,14},{7,23}} | collective-permute-start | bytes 196616 | tf_op jit(solution)/shard_map/ppermute | solution.py:133
  11.0 1.3 %collective-permute-done.8.refs_0_ = bf16[128,256]{1,0:T(8,128)(2,1)S(1)} collective-permute-done((bf16[128,256]{1,0:T(8,128)(2,1)S(1)}, bf16[128,256]{1,0:T(8,128)(2,1)S(1)}, u32[]{:S(2)}, u32[]{:S(2)}) %collective-permute-start.8) | collective-permute-done | bytes 65568 | tf_op jit(solution)/shard_map/ppermute | solution.py:133
  12.3 2.2 %collective-permute-start.9 = (bf16[128,2560]{1,0:T(8,128)(2,1)S(1)}, bf16[128,2560]{1,0:T(8,128)(2,1)S(1)}, u32[]{:S(2)}, u32[]{:S(2)}) collective-permute-start(bf16[128,2560]{1,0:T(8,128)(2,1)S(1)} %pack_kernel.1), channel_id=1, source_target_pairs={{0,1},{1,0},{2,3},{3,2},{4,5},{5,4},{6,7},{7,6},{8,12},{9,8},{10,1... | collective-permute-start | bytes 1966088 | tf_op jit(solution)/shard_map/ppermute | solution.py:129
  14.7 0.5 collective-permute-start.4
  15.7 0.7 %collective-permute-done.3.g0 = bf16[256,128]{1,0:T(8,128)(2,1)S(1)} collective-permute-done((bf16[256,128]{1,0:T(8,128)(2,1)S(1)}, bf16[256,128]{1,0:T(8,128)(2,1)S(1)}, u32[]{:S(2)}, u32[]{:S(2)}) %collective-permute-start.3) | collective-permute-done | bytes 65568 | tf_op jit(solution)/shard_map/ppermute | solution.py:129
  17.3 0.9 %collective-permute-done.7.p_in = bf16[1024,128]{1,0:T(8,128)(2,1)S(1)} collective-permute-done((bf16[1024,128]{1,0:T(8,128)(2,1)S(1)}, bf16[1024,128]{1,0:T(8,128)(2,1)S(1)}, u32[]{:S(2)}, u32[]{:S(2)}) %collective-permute-start.7) | collective-permute-done | bytes 262176 | tf_op jit(solution)/shard_map/ppermute | solution.py:129
  18.6 0.4 collective-permute-start.11
  19.6 0.7 %collective-permute-done.11.p_in = bf16[1024,128]{1,0:T(8,128)(2,1)S(1)} collective-permute-done((bf16[1024,128]{1,0:T(8,128)(2,1)S(1)}, bf16[1024,128]{1,0:T(8,128)(2,1)S(1)}, u32[]{:S(2)}, u32[]{:S(2)}) %collective-permute-start.11) | collective-permute-done | bytes 262176 | tf_op jit(solution)/shard_map/ppermute | solution.py:129
  21.6 0.7 %collective-permute-start.16 = (bf16[1024,128]{1,0:T(8,128)(2,1)S(1)}, bf16[1024,128]{1,0:T(8,128)(2,1)S(1)}, u32[]{:S(2)}, u32[]{:S(2)}) collective-permute-start(bf16[1024,128]{1,0:T(8,128)(2,1)S(1)} %get-tuple-element.34), channel_id=1, source_target_pairs={{14,10}} | collective-permute-start | bytes 786440 | tf_op jit(solution)/shard_map/ppermute | solution.py:133
  22.2 0.7 %collective-permute-start.17 = (bf16[1024,128]{1,0:T(8,128)(2,1)S(1)}, bf16[1024,128]{1,0:T(8,128)(2,1)S(1)}, u32[]{:S(2)}, u32[]{:S(2)}) collective-permute-start(bf16[1024,128]{1,0:T(8,128)(2,1)S(1)} %get-tuple-element.34), channel_id=1, source_target_pairs={{14,30}} | collective-permute-start | bytes 786440 | tf_op jit(solution)/shard_map/ppermute | solution.py:133
  22.9 0.7 %collective-permute-start.18 = (bf16[1024,128]{1,0:T(8,128)(2,1)S(1)}, bf16[1024,128]{1,0:T(8,128)(2,1)S(1)}, u32[]{:S(2)}, u32[]{:S(2)}) collective-permute-start(bf16[1024,128]{1,0:T(8,128)(2,1)S(1)} %get-tuple-element.34), channel_id=1, source_target_pairs={{14,18}} | collective-permute-start | bytes 786440 | tf_op jit(solution)/shard_map/ppermute | solution.py:133
  23.7 0.7 %collective-permute-start.19 = (bf16[1024,128]{1,0:T(8,128)(2,1)S(1)}, bf16[1024,128]{1,0:T(8,128)(2,1)S(1)}, u32[]{:S(2)}, u32[]{:S(2)}) collective-permute-start(bf16[1024,128]{1,0:T(8,128)(2,1)S(1)} %step3_kernel.1.q_prev), channel_id=1, source_target_pairs={{23,27},{10,26},{18,22},{16,24},{20,28},{17,25},{13,21},{9,1}} | collective-permute-start | bytes 786440 | tf_op jit(solution)/shard_map/ppermute | solution.py:133
  24.4 0.7 %collective-permute-start.20 = (bf16[1024,128]{1,0:T(8,128)(2,1)S(1)}, bf16[1024,128]{1,0:T(8,128)(2,1)S(1)}, u32[]{:S(2)}, u32[]{:S(2)}) collective-permute-start(bf16[1024,128]{1,0:T(8,128)(2,1)S(1)} %step3_kernel.1.q_prev), channel_id=1, source_target_pairs={{23,31},{10,2},{14,6},{17,29},{13,5}} | collective-permute-start | bytes 786440 | tf_op jit(solution)/shard_map/ppermute | solution.py:133
  25.1 0.7 %collective-permute-start.21 = (bf16[1024,128]{1,0:T(8,128)(2,1)S(1)}, bf16[1024,128]{1,0:T(8,128)(2,1)S(1)}, u32[]{:S(2)}, u32[]{:S(2)}) collective-permute-start(bf16[1024,128]{1,0:T(8,128)(2,1)S(1)} %step3_kernel.1.q_prev), channel_id=1, source_target_pairs={{23,19}} | collective-permute-start | bytes 786440 | tf_op jit(solution)/shard_map/ppermute | solution.py:133
  25.8 0.7 %collective-permute-start.22 = (bf16[1024,128]{1,0:T(8,128)(2,1)S(1)}, bf16[1024,128]{1,0:T(8,128)(2,1)S(1)}, u32[]{:S(2)}, u32[]{:S(2)}) collective-permute-start(bf16[1024,128]{1,0:T(8,128)(2,1)S(1)} %step3_kernel.1.q_prev), channel_id=1, source_target_pairs={{23,11}} | collective-permute-start | bytes 786440 | tf_op jit(solution)/shard_map/ppermute | solution.py:133
  27.9 19.8 %collective-permute-start.23 = (bf16[1040,128]{1,0:T(8,128)(2,1)S(1)}, bf16[1040,128]{1,0:T(8,128)(2,1)S(1)}, u32[]{:S(2)}, u32[]{:S(2)}) collective-permute-start(bf16[1040,128]{1,0:T(8,128)(2,1)S(1)} %get-tuple-element.40.refs_0_), channel_id=1, source_target_pairs={{0,2},{1,3},{2,0},{3,1},{4,6},{5,7},{6,4},{7,5},{8,10},{9,11},{10,... | collective-permute-start | bytes 798728 | tf_op jit(solution)/shard_map/ppermute | solution.py:129
  47.8 1.3 %collective-permute-start.24 = (bf16[1024,128]{1,0:T(8,128)(2,1)S(1)}, bf16[1024,128]{1,0:T(8,128)(2,1)S(1)}, u32[]{:S(2)}, u32[]{:S(2)}) collective-permute-start(bf16[1024,128]{1,0:T(8,128)(2,1)S(1)} %get-tuple-element.37.q_ref), channel_id=1, source_target_pairs={{11,15},{27,3},{31,7}} | collective-permute-start | bytes 786440 | tf_op jit(solution)/shard_map/ppermute | solution.py:133
  49.1 11.4 %collective-permute-done.24.rest_ref = bf16[1024,128]{1,0:T(8,128)(2,1)S(1)} collective-permute-done((bf16[1024,128]{1,0:T(8,128)(2,1)S(1)}, bf16[1024,128]{1,0:T(8,128)(2,1)S(1)}, u32[]{:S(2)}, u32[]{:S(2)}) %collective-permute-start.24) | collective-permute-done | bytes 262176 | tf_op jit(solution)/shard_map/ppermute | solution.py:133
  61.0 1.0 %collective-permute-done.25.refs_1_ = bf16[1040,128]{1,0:T(8,128)(2,1)S(1)} collective-permute-done((bf16[1040,128]{1,0:T(8,128)(2,1)S(1)}, bf16[1040,128]{1,0:T(8,128)(2,1)S(1)}, u32[]{:S(2)}, u32[]{:S(2)}) %collective-permute-start.25) | collective-permute-done | bytes 266272 | tf_op jit(solution)/shard_map/ppermute | solution.py:129
  62.4 1.4 %final_kernel.1 = (f32[1024,128]{1,0:T(8,128)}, f32[2,1024,128]{2,1,0:T(8,128)}) custom-call(bf16[1024,128]{1,0:T(8,128)(2,1)S(1)} %get-tuple-element.37.q_ref, bf16[1024,128]{1,0:T(8,128)(2,1)S(1)} %collective-permute-done.24.rest_ref, f32[2,1024,128]{2,1,0:T(8,128)S(1)} %bitcast.14, bf16[1040,128]{1,0:T(8,128)(2,1)S(1)} %get-tuple-element.40.refs_0_, ...), custom_call_target="tpu_custom_call" | custom-call | tf_op jit(solution)/shard_map/final_kernel/pallas_call | solution.py:156
  (49 shorter events, 5.0 us)
Async XLA Ops:
  2.0 10.3 %collective-permute-start.2 = (bf16[128,1024]{1,0:T(8,128)(2,1)S(1)}, bf16[128,1024]{1,0:T(8,128)(2,1)S(1)}, u32[]{:S(2)}, u32[]{:S(2)}) collective-permute-start(bf16[128,1024]{1,0:T(8,128)(2,1)S(1)} %get-tuple-element.25), channel_id=1, source_target_pairs={{24,1},{25,22},{26,13},{27,15},{28,9},{29,23},{30,3},{31,14}} | collective-permute-start | bytes 786440 | tf_op jit(solution)/shard_map/ppermute | solution.py:133
  2.8 9.5 %collective-permute-start.1 = (bf16[128,768]{1,0:T(8,128)(2,1)S(1)}, bf16[128,768]{1,0:T(8,128)(2,1)S(1)}, u32[]{:S(2)}, u32[]{:S(2)}) collective-permute-start(bf16[128,768]{1,0:T(8,128)(2,1)S(1)} %get-tuple-element.24), channel_id=1, source_target_pairs={{16,0},{17,13},{18,22},{19,15},{20,14},{21,9},{23,2}} | collective-permute-start | bytes 589832 | tf_op jit(solution)/shard_map/ppermute | solution.py:133
  3.6 8.6 %collective-permute-start = (bf16[128,512]{1,0:T(8,128)(2,1)S(1)}, bf16[128,512]{1,0:T(8,128)(2,1)S(1)}, u32[]{:S(2)}, u32[]{:S(2)}) collective-permute-start(bf16[128,512]{1,0:T(8,128)(2,1)S(1)} %get-tuple-element.23), channel_id=1, source_target_pairs={{4,0},{8,22},{10,2},{11,15},{12,1},{13,9},{14,23}} | collective-permute-start | bytes 393224 | tf_op jit(solution)/shard_map/ppermute | solution.py:133
  4.3 8.0 %collective-permute-start.8 = (bf16[128,256]{1,0:T(8,128)(2,1)S(1)}, bf16[128,256]{1,0:T(8,128)(2,1)S(1)}, u32[]{:S(2)}, u32[]{:S(2)}) collective-permute-start(bf16[128,256]{1,0:T(8,128)(2,1)S(1)} %get-tuple-element.27), channel_id=1, source_target_pairs={{1,13},{2,15},{3,22},{5,9},{6,14},{7,23}} | collective-permute-start | bytes 196616 | tf_op jit(solution)/shard_map/ppermute | solution.py:133
  12.3 4.8 %collective-permute-start.9 = (bf16[128,2560]{1,0:T(8,128)(2,1)S(1)}, bf16[128,2560]{1,0:T(8,128)(2,1)S(1)}, u32[]{:S(2)}, u32[]{:S(2)}) collective-permute-start(bf16[128,2560]{1,0:T(8,128)(2,1)S(1)} %pack_kernel.1), channel_id=1, source_target_pairs={{0,1},{1,0},{2,3},{3,2},{4,5},{5,4},{6,7},{7,6},{8,12},{9,8},{10,1... | collective-permute-start | bytes 1966088 | tf_op jit(solution)/shard_map/ppermute | solution.py:129
  14.6 1.8 %collective-permute-start.3 = (bf16[256,128]{1,0:T(8,128)(2,1)S(1)}, bf16[256,128]{1,0:T(8,128)(2,1)S(1)}, u32[]{:S(2)}, u32[]{:S(2)}) collective-permute-start(bf16[256,128]{1,0:T(8,128)(2,1)S(1)} %first_kernel.1), channel_id=1, source_target_pairs={{0,4},{1,8},{2,12},{3,2},{4,5},{5,0},{6,7},{7,6},{8,9},{9,1},{10,1... | collective-permute-start | bytes 196616 | tf_op jit(solution)/shard_map/ppermute | solution.py:129
  14.7 1.7 %collective-permute-start.4 = (bf16[256,128]{1,0:T(8,128)(2,1)S(1)}, bf16[256,128]{1,0:T(8,128)(2,1)S(1)}, u32[]{:S(2)}, u32[]{:S(2)}) collective-permute-start(bf16[256,128]{1,0:T(8,128)(2,1)S(1)} %first_kernel.1), channel_id=1, source_target_pairs={{0,8},{1,12},{2,3},{3,4},{4,5},{5,0},{6,7},{7,6},{8,9},{9,1},{10,1... | collective-permute-start | bytes 196616 | tf_op jit(solution)/shard_map/ppermute | solution.py:129
  16.7 1.5 %collective-permute-start.7 = (bf16[1024,128]{1,0:T(8,128)(2,1)S(1)}, bf16[1024,128]{1,0:T(8,128)(2,1)S(1)}, u32[]{:S(2)}, u32[]{:S(2)}) collective-permute-start(bf16[1024,128]{1,0:T(8,128)(2,1)S(1)} %get-tuple-element.26), channel_id=1, source_target_pairs={{0,1},{1,0},{2,3},{3,2},{4,9},{5,4},{6,7},{7,6},{8,5},{9,8},{10,11... | collective-permute-start | bytes 786440 | tf_op jit(solution)/shard_map/ppermute | solution.py:129
  17.1 1.5 %collective-permute-start.10 = (bf16[1024,128]{1,0:T(8,128)(2,1)S(1)}, bf16[1024,128]{1,0:T(8,128)(2,1)S(1)}, u32[]{:S(2)}, u32[]{:S(2)}) collective-permute-start(bf16[1024,128]{1,0:T(8,128)(2,1)S(1)} %get-tuple-element.29.s_prev), channel_id=1, source_target_pairs={{0,1},{1,0},{2,3},{3,2},{4,5},{5,4},{6,7},{7,6},{8,9},{9,8},{10,11... | collective-permute-start | bytes 786440 | tf_op jit(solution)/shard_map/ppermute | solution.py:129
  18.6 1.6 %collective-permute-start.11 = (bf16[1024,128]{1,0:T(8,128)(2,1)S(1)}, bf16[1024,128]{1,0:T(8,128)(2,1)S(1)}, u32[]{:S(2)}, u32[]{:S(2)}) collective-permute-start(bf16[1024,128]{1,0:T(8,128)(2,1)S(1)} %get-tuple-element.30), channel_id=1, source_target_pairs={{0,1},{1,0},{2,3},{3,2},{4,5},{5,4},{6,7},{7,6},{8,9},{9,14},{10,1... | collective-permute-start | bytes 786440 | tf_op jit(solution)/shard_map/ppermute | solution.py:129
  19.1 1.5 %collective-permute-start.12 = (bf16[1024,128]{1,0:T(8,128)(2,1)S(1)}, bf16[1024,128]{1,0:T(8,128)(2,1)S(1)}, u32[]{:S(2)}, u32[]{:S(2)}) collective-permute-start(bf16[1024,128]{1,0:T(8,128)(2,1)S(1)} %step1_kernel.1.q_in.q_prev), channel_id=1, source_target_pairs={{0,1},{1,5},{2,3},{3,2},{4,0},{5,4},{6,7},{7,6},{8,16},{9,17},{10,... | collective-permute-start | bytes 786440 | tf_op jit(solution)/shard_map/ppermute | solution.py:129
  19.2 1.8 %collective-permute-start.13 = (bf16[1024,128]{1,0:T(8,128)(2,1)S(1)}, bf16[1024,128]{1,0:T(8,128)(2,1)S(1)}, u32[]{:S(2)}, u32[]{:S(2)}) collective-permute-start(bf16[1024,128]{1,0:T(8,128)(2,1)S(1)} %step1_kernel.1.q_in.q_prev), channel_id=1, source_target_pairs={{0,1},{1,0},{2,3},{3,2},{4,5},{5,4},{6,7},{7,6},{8,9},{9,13},{10,1... | collective-permute-start | bytes 786440 | tf_op jit(solution)/shard_map/ppermute | solution.py:129
  21.0 2.6 %collective-permute-start.14 = (bf16[1024,128]{1,0:T(8,128)(2,1)S(1)}, bf16[1024,128]{1,0:T(8,128)(2,1)S(1)}, u32[]{:S(2)}, u32[]{:S(2)}) collective-permute-start(bf16[1024,128]{1,0:T(8,128)(2,1)S(1)} %get-tuple-element.34), channel_id=1, source_target_pairs={{0,1},{1,0},{2,3},{3,2},{4,5},{5,4},{6,7},{7,6},{8,9},{9,8},{10,11... | collective-permute-start | bytes 786440 | tf_op jit(solution)/shard_map/ppermute | solution.py:129
  21.4 2.2 %collective-permute-start.15 = (bf16[1024,128]{1,0:T(8,128)(2,1)S(1)}, bf16[1024,128]{1,0:T(8,128)(2,1)S(1)}, u32[]{:S(2)}, u32[]{:S(2)}) collective-permute-start(bf16[1024,128]{1,0:T(8,128)(2,1)S(1)} %get-tuple-element.33.s_ref), channel_id=1, source_target_pairs={{0,1},{1,0},{2,3},{3,2},{4,5},{5,4},{6,7},{7,6},{8,9},{9,8},{10,11... | collective-permute-start | bytes 786440 | tf_op jit(solution)/shard_map/ppermute | solution.py:129
  21.6 2.1 %collective-permute-start.16 = (bf16[1024,128]{1,0:T(8,128)(2,1)S(1)}, bf16[1024,128]{1,0:T(8,128)(2,1)S(1)}, u32[]{:S(2)}, u32[]{:S(2)}) collective-permute-start(bf16[1024,128]{1,0:T(8,128)(2,1)S(1)} %get-tuple-element.34), channel_id=1, source_target_pairs={{14,10}} | collective-permute-start | bytes 786440 | tf_op jit(solution)/shard_map/ppermute | solution.py:133
  22.2 1.4 %collective-permute-start.17 = (bf16[1024,128]{1,0:T(8,128)(2,1)S(1)}, bf16[1024,128]{1,0:T(8,128)(2,1)S(1)}, u32[]{:S(2)}, u32[]{:S(2)}) collective-permute-start(bf16[1024,128]{1,0:T(8,128)(2,1)S(1)} %get-tuple-element.34), channel_id=1, source_target_pairs={{14,30}} | collective-permute-start | bytes 786440 | tf_op jit(solution)/shard_map/ppermute | solution.py:133
  23.7 4.0 %collective-permute-start.19 = (bf16[1024,128]{1,0:T(8,128)(2,1)S(1)}, bf16[1024,128]{1,0:T(8,128)(2,1)S(1)}, u32[]{:S(2)}, u32[]{:S(2)}) collective-permute-start(bf16[1024,128]{1,0:T(8,128)(2,1)S(1)} %step3_kernel.1.q_prev), channel_id=1, source_target_pairs={{23,27},{10,26},{18,22},{16,24},{20,28},{17,25},{13,21},{9,1}} | collective-permute-start | bytes 786440 | tf_op jit(solution)/shard_map/ppermute | solution.py:133
  24.4 3.4 %collective-permute-start.20 = (bf16[1024,128]{1,0:T(8,128)(2,1)S(1)}, bf16[1024,128]{1,0:T(8,128)(2,1)S(1)}, u32[]{:S(2)}, u32[]{:S(2)}) collective-permute-start(bf16[1024,128]{1,0:T(8,128)(2,1)S(1)} %step3_kernel.1.q_prev), channel_id=1, source_target_pairs={{23,31},{10,2},{14,6},{17,29},{13,5}} | collective-permute-start | bytes 786440 | tf_op jit(solution)/shard_map/ppermute | solution.py:133
  25.1 2.7 %collective-permute-start.21 = (bf16[1024,128]{1,0:T(8,128)(2,1)S(1)}, bf16[1024,128]{1,0:T(8,128)(2,1)S(1)}, u32[]{:S(2)}, u32[]{:S(2)}) collective-permute-start(bf16[1024,128]{1,0:T(8,128)(2,1)S(1)} %step3_kernel.1.q_prev), channel_id=1, source_target_pairs={{23,19}} | collective-permute-start | bytes 786440 | tf_op jit(solution)/shard_map/ppermute | solution.py:133
  25.8 2.0 %collective-permute-start.22 = (bf16[1024,128]{1,0:T(8,128)(2,1)S(1)}, bf16[1024,128]{1,0:T(8,128)(2,1)S(1)}, u32[]{:S(2)}, u32[]{:S(2)}) collective-permute-start(bf16[1024,128]{1,0:T(8,128)(2,1)S(1)} %step3_kernel.1.q_prev), channel_id=1, source_target_pairs={{23,11}} | collective-permute-start | bytes 786440 | tf_op jit(solution)/shard_map/ppermute | solution.py:133
  27.9 32.5 %collective-permute-start.23 = (bf16[1040,128]{1,0:T(8,128)(2,1)S(1)}, bf16[1040,128]{1,0:T(8,128)(2,1)S(1)}, u32[]{:S(2)}, u32[]{:S(2)}) collective-permute-start(bf16[1040,128]{1,0:T(8,128)(2,1)S(1)} %get-tuple-element.40.refs_0_), channel_id=1, source_target_pairs={{0,2},{1,3},{2,0},{3,1},{4,6},{5,7},{6,4},{7,5},{8,10},{9,11},{10,... | collective-permute-start | bytes 798728 | tf_op jit(solution)/shard_map/ppermute | solution.py:129
  47.8 12.7 %collective-permute-start.24 = (bf16[1024,128]{1,0:T(8,128)(2,1)S(1)}, bf16[1024,128]{1,0:T(8,128)(2,1)S(1)}, u32[]{:S(2)}, u32[]{:S(2)}) collective-permute-start(bf16[1024,128]{1,0:T(8,128)(2,1)S(1)} %get-tuple-element.37.q_ref), channel_id=1, source_target_pairs={{11,15},{27,3},{31,7}} | collective-permute-start | bytes 786440 | tf_op jit(solution)/shard_map/ppermute | solution.py:133
  60.4 1.5 %collective-permute-start.25 = (bf16[1040,128]{1,0:T(8,128)(2,1)S(1)}, bf16[1040,128]{1,0:T(8,128)(2,1)S(1)}, u32[]{:S(2)}, u32[]{:S(2)}) collective-permute-start(bf16[1040,128]{1,0:T(8,128)(2,1)S(1)} %get-tuple-element.40.refs_0_), channel_id=1, source_target_pairs={{0,1},{1,0},{2,3},{3,2},{4,5},{5,4},{6,7},{7,6},{8,9},{9,8},{10,11... | collective-permute-start | bytes 798728 | tf_op jit(solution)/shard_map/ppermute | solution.py:129
  60.7 1.6 %collective-permute-start.26 = (bf16[1040,128]{1,0:T(8,128)(2,1)S(1)}, bf16[1040,128]{1,0:T(8,128)(2,1)S(1)}, u32[]{:S(2)}, u32[]{:S(2)}) collective-permute-start(bf16[1040,128]{1,0:T(8,128)(2,1)S(1)} %collective-permute-done.23.refs_2_), channel_id=1, source_target_pairs={{0,1},{1,0},{2,3},{3,2},{4,5},{5,4},{6,7},{7,6},{8,9},{9,8},{10,11... | collective-permute-start | bytes 798728 | tf_op jit(solution)/shard_map/ppermute | solution.py:129
  (7 other events, 46.0 us)

commit v16 on v15

--- a/solution.py
+++ b/solution.py
@@ -406,9 +406,15 @@
     out_ref[pl.ds(size, TAIL)] = low(jnp.where(flag, 1.0, 0.0))
 
 
-def final_kernel(q_ref, rest_ref, rhs_ref, *refs):
-    sums, (solved_ref, out_ref) = refs[:NC], refs[NC:]
-    size = out_ref.shape[1]
+def minus(acc, sums, i):
+    size = acc.shape[0]
+    for s in sums:
+        keep = s[pl.ds(size, TAIL)].astype(jnp.float32)[i : i + 1] > 0.5
+        acc = acc - jnp.where(keep, s[pl.ds(0, size)].astype(jnp.float32), 0.0)
+    return acc
+
+
+def half_kernel(q_ref, rest_ref, rhs_ref, mine_ref, across_ref, solved_ref, out_ref):
     came = any_of(REST)
 
     @pl.when(came)
@@ -420,11 +426,12 @@
         solved_ref[...] = q_ref[...].astype(jnp.float32)
 
     for i in range(out_ref.shape[0]):
-        acc = rhs_ref[i]
-        for s in sums:
-            keep = s[pl.ds(size, TAIL)].astype(jnp.float32)[i : i + 1] > 0.5
-            acc = acc - jnp.where(keep, s[pl.ds(0, size)].astype(jnp.float32), 0.0)
-        out_ref[i] = acc
+        out_ref[i] = minus(rhs_ref[i], (mine_ref, across_ref), i)
+
+
+def final_kernel(half_ref, beside_ref, corner_ref, out_ref):
+    for i in range(out_ref.shape[0]):
+        out_ref[i] = minus(half_ref[i], (beside_ref, corner_ref), i)
 
 
 def on_device_8x4(rhs, diag_inv, blocks, block_rows, counts):
@@ -513,7 +520,7 @@
 
     sends = [
         [
-            (MAKER[3], (6, 3)), ((2, 2), (6, 2)), ((4, 2), (5, 2)),
+            (MAKER[3], (6, 3)), ((2, 2), (6, 2)), ((7, 2), (5, 2)),
             ((4, 0), (6, 0)), ((5, 0), (7, 0)), ((4, 1), (6, 1)), ((3, 1), (5, 1)), ((2, 1), (0, 1)),
         ],
         [(MAKER[3], (7, 3)), ((2, 2), (0, 2)), (MAKER[2], (1, 2)), ((4, 1), (7, 1)), ((3, 1), (1, 1))],
@@ -535,16 +542,18 @@
 
     across = swap(mine, 2)
     rest = send_only(q, list(zip(((2, 3), (6, 3), (7, 3)), REST)))
-    beside, across, rest = lax.optimization_barrier((mine, across, rest))
-    beside = swap(beside, 1)
+    beside = swap(mine, 1)
+    across, rest = lax.optimization_barrier((across, rest))
     corner = swap(across, 1)
-    solved, remainder = call(
-        final_kernel,
-        [jax.ShapeDtypeStruct((size, width), jnp.float32), jax.ShapeDtypeStruct(rhs.shape, jnp.float32)],
-        [q, rest, rhs, mine, beside, across, corner],
-        [VMEM] * 7,
+    whole_rhs = jax.ShapeDtypeStruct(rhs.shape, jnp.float32)
+    solved, half = call(
+        half_kernel,
+        [jax.ShapeDtypeStruct((size, width), jnp.float32), whole_rhs],
+        [q, rest, rhs, mine, across],
+        [VMEM] * 5,
         [VMEM] * 2,
     )
+    remainder = call(final_kernel, whole_rhs, [half, beside, corner], [VMEM] * 3, VMEM)
     return solved[None, None], remainder[:, None]
 
 

time: 64.8 us -> 63.5 us (0.980); the launches traced: 63.8 us -> 63.2 us
  waiting for transfers between devices: 17.8 us -> 10.8 us
  starting transfers between devices: 40.6 us -> 46.4 us
    ppermute x12, waiting for transfers between devices: 12.7 us -> 6.71 us  [send_only(): lax.ppermute(value, ('row', 'col'), [(a * NC + b, c * NC + d) for (a, b),...]
    ppermute x15, starting transfers between devices: 25.7 us -> 31.5 us  [send(): lax.ppermute(value, ('row', 'col'), [(a * NC + b, c * NC + d) for (a, b),...]
    ppermute x15, waiting for transfers between devices: 5.07 us -> 4.08 us  [send(): lax.ppermute(value, ('row', 'col'), [(a * NC + b, c * NC + d) for (a, b),...]
    pallas_call x11 -> x12, Pallas kernels: 1.86 us -> 2.48 us  [call(): pl.pallas_call(kernel, out_shape=outs, in_specs=in_specs, out_specs=out_s...]
  transfers between devices with their start and end apart: 27 -> 27, of which waited for: 13 -> 12; matrix products, arithmetic and copies ran while one was open for 0% -> 0% of each run, Pallas kernels for 0% -> 2%
where the time goes in v16:
time: 63.5 us; the launch traced here: 63.2 us
  starting transfers between devices  46.4 us (73%)
  waiting for transfers between devices  10.8 us (17%)
  Pallas kernels  2.48 us (4%)
  between operations  2.19 us (3%)
  local copies, waits for them, and re-layouts  1.32 us (2%)
    ppermute x15, starting transfers between devices, send(): lax.ppermute(value, ('row', 'col'), [(a * NC + b, c * NC + d) for (a, b),...  31.5 us
    ppermute x12, starting transfers between devices, send_only(): lax.ppermute(value, ('row', 'col'), [(a * NC + b, c * NC + d) for (a, b),...  14.9 us
    ppermute x12, waiting for transfers between devices, send_only(): lax.ppermute(value, ('row', 'col'), [(a * NC + b, c * NC + d) for (a, b),...  6.71 us
    ppermute x15, waiting for transfers between devices, send(): lax.ppermute(value, ('row', 'col'), [(a * NC + b, c * NC + d) for (a, b),...  4.08 us
    pallas_call x12, Pallas kernels, call(): pl.pallas_call(kernel, out_shape=outs, in_specs=in_specs, out_specs=out_s...  2.48 us
    unnamed x8, local copies, waits for them, and re-layouts  1.32 us
  transfers between devices with their start and end apart: 27, of which 12 were waited for; matrix products, arithmetic and copies ran while one was open for 0% of the time, Pallas kernels for 2%

profile of v16, /device:TPU:7, one launch (start us, length us, event | category | flops | bytes accessed | tf_op | source)
XLA Modules:
  0.0 63.2 jit_solution(11503848777533281547)
XLA Ops:
  0.6 1.3 %copy-done.2 = bf16[4,128,1024]{2,1,0:T(8,128)(2,1)S(1)} copy-done((bf16[4,128,1024]{2,1,0:T(8,128)(2,1)S(1)}, bf16[4,128,1024]{2,1,0:T(8,128)(2,1)}, u32[]{:S(2)}) %copy-start.2) | copy-done | bytes 1048600
  2.0 0.8 %collective-permute-start.2 = (bf16[128,1024]{1,0:T(8,128)(2,1)S(1)}, bf16[128,1024]{1,0:T(8,128)(2,1)S(1)}, u32[]{:S(2)}, u32[]{:S(2)}) collective-permute-start(bf16[128,1024]{1,0:T(8,128)(2,1)S(1)} %get-tuple-element.24), channel_id=1, source_target_pairs={{24,1},{25,22},{26,13},{27,15},{28,9},{29,23},{30,3},{31,14}} | collective-permute-start | bytes 786440 | tf_op jit(solution)/shard_map/ppermute | solution.py:133
  2.8 0.8 %collective-permute-start.1 = (bf16[128,768]{1,0:T(8,128)(2,1)S(1)}, bf16[128,768]{1,0:T(8,128)(2,1)S(1)}, u32[]{:S(2)}, u32[]{:S(2)}) collective-permute-start(bf16[128,768]{1,0:T(8,128)(2,1)S(1)} %get-tuple-element.23), channel_id=1, source_target_pairs={{16,0},{17,13},{18,22},{19,15},{20,14},{21,9},{23,2}} | collective-permute-start | bytes 589832 | tf_op jit(solution)/shard_map/ppermute | solution.py:133
  3.6 0.7 %collective-permute-start = (bf16[128,512]{1,0:T(8,128)(2,1)S(1)}, bf16[128,512]{1,0:T(8,128)(2,1)S(1)}, u32[]{:S(2)}, u32[]{:S(2)}) collective-permute-start(bf16[128,512]{1,0:T(8,128)(2,1)S(1)} %get-tuple-element.22), channel_id=1, source_target_pairs={{4,0},{8,22},{10,2},{11,15},{12,1},{13,9},{14,23}} | collective-permute-start | bytes 393224 | tf_op jit(solution)/shard_map/ppermute | solution.py:133
  4.3 6.6 %collective-permute-start.8 = (bf16[128,256]{1,0:T(8,128)(2,1)S(1)}, bf16[128,256]{1,0:T(8,128)(2,1)S(1)}, u32[]{:S(2)}, u32[]{:S(2)}) collective-permute-start(bf16[128,256]{1,0:T(8,128)(2,1)S(1)} %get-tuple-element.26), channel_id=1, source_target_pairs={{1,13},{2,15},{3,22},{5,9},{6,14},{7,23}} | collective-permute-start | bytes 196616 | tf_op jit(solution)/shard_map/ppermute | solution.py:133
  11.0 1.3 %collective-permute-done.8.refs_0_ = bf16[128,256]{1,0:T(8,128)(2,1)S(1)} collective-permute-done((bf16[128,256]{1,0:T(8,128)(2,1)S(1)}, bf16[128,256]{1,0:T(8,128)(2,1)S(1)}, u32[]{:S(2)}, u32[]{:S(2)}) %collective-permute-start.8) | collective-permute-done | bytes 65568 | tf_op jit(solution)/shard_map/ppermute | solution.py:133
  12.3 2.2 %collective-permute-start.9 = (bf16[128,2560]{1,0:T(8,128)(2,1)S(1)}, bf16[128,2560]{1,0:T(8,128)(2,1)S(1)}, u32[]{:S(2)}, u32[]{:S(2)}) collective-permute-start(bf16[128,2560]{1,0:T(8,128)(2,1)S(1)} %pack_kernel.1), channel_id=1, source_target_pairs={{0,1},{1,0},{2,3},{3,2},{4,5},{5,4},{6,7},{7,6},{8,12},{9,8},{10,1... | collective-permute-start | bytes 1966088 | tf_op jit(solution)/shard_map/ppermute | solution.py:129
  14.7 0.5 collective-permute-start.4
  15.7 0.7 %collective-permute-done.3.g0 = bf16[256,128]{1,0:T(8,128)(2,1)S(1)} collective-permute-done((bf16[256,128]{1,0:T(8,128)(2,1)S(1)}, bf16[256,128]{1,0:T(8,128)(2,1)S(1)}, u32[]{:S(2)}, u32[]{:S(2)}) %collective-permute-start.3) | collective-permute-done | bytes 65568 | tf_op jit(solution)/shard_map/ppermute | solution.py:129
  17.3 0.9 %collective-permute-done.7.p_in = bf16[1024,128]{1,0:T(8,128)(2,1)S(1)} collective-permute-done((bf16[1024,128]{1,0:T(8,128)(2,1)S(1)}, bf16[1024,128]{1,0:T(8,128)(2,1)S(1)}, u32[]{:S(2)}, u32[]{:S(2)}) %collective-permute-start.7) | collective-permute-done | bytes 262176 | tf_op jit(solution)/shard_map/ppermute | solution.py:129
  19.6 0.7 %collective-permute-done.11.p_in = bf16[1024,128]{1,0:T(8,128)(2,1)S(1)} collective-permute-done((bf16[1024,128]{1,0:T(8,128)(2,1)S(1)}, bf16[1024,128]{1,0:T(8,128)(2,1)S(1)}, u32[]{:S(2)}, u32[]{:S(2)}) %collective-permute-start.11) | collective-permute-done | bytes 262176 | tf_op jit(solution)/shard_map/ppermute | solution.py:129
  21.6 0.7 %collective-permute-start.16 = (bf16[1024,128]{1,0:T(8,128)(2,1)S(1)}, bf16[1024,128]{1,0:T(8,128)(2,1)S(1)}, u32[]{:S(2)}, u32[]{:S(2)}) collective-permute-start(bf16[1024,128]{1,0:T(8,128)(2,1)S(1)} %get-tuple-element.33), channel_id=1, source_target_pairs={{14,10}} | collective-permute-start | bytes 786440 | tf_op jit(solution)/shard_map/ppermute | solution.py:133
  22.2 0.7 %collective-permute-start.17 = (bf16[1024,128]{1,0:T(8,128)(2,1)S(1)}, bf16[1024,128]{1,0:T(8,128)(2,1)S(1)}, u32[]{:S(2)}, u32[]{:S(2)}) collective-permute-start(bf16[1024,128]{1,0:T(8,128)(2,1)S(1)} %get-tuple-element.33), channel_id=1, source_target_pairs={{14,30}} | collective-permute-start | bytes 786440 | tf_op jit(solution)/shard_map/ppermute | solution.py:133
  22.9 0.7 %collective-permute-start.18 = (bf16[1024,128]{1,0:T(8,128)(2,1)S(1)}, bf16[1024,128]{1,0:T(8,128)(2,1)S(1)}, u32[]{:S(2)}, u32[]{:S(2)}) collective-permute-start(bf16[1024,128]{1,0:T(8,128)(2,1)S(1)} %get-tuple-element.33), channel_id=1, source_target_pairs={{14,18}} | collective-permute-start | bytes 786440 | tf_op jit(solution)/shard_map/ppermute | solution.py:133
  23.7 0.7 %collective-permute-start.19 = (bf16[1024,128]{1,0:T(8,128)(2,1)S(1)}, bf16[1024,128]{1,0:T(8,128)(2,1)S(1)}, u32[]{:S(2)}, u32[]{:S(2)}) collective-permute-start(bf16[1024,128]{1,0:T(8,128)(2,1)S(1)} %step3_kernel.1.q_prev), channel_id=1, source_target_pairs={{23,27},{10,26},{30,22},{16,24},{20,28},{17,25},{13,21},{9,1}} | collective-permute-start | bytes 786440 | tf_op jit(solution)/shard_map/ppermute | solution.py:133
  24.4 0.7 %collective-permute-start.20 = (bf16[1024,128]{1,0:T(8,128)(2,1)S(1)}, bf16[1024,128]{1,0:T(8,128)(2,1)S(1)}, u32[]{:S(2)}, u32[]{:S(2)}) collective-permute-start(bf16[1024,128]{1,0:T(8,128)(2,1)S(1)} %step3_kernel.1.q_prev), channel_id=1, source_target_pairs={{23,31},{10,2},{14,6},{17,29},{13,5}} | collective-permute-start | bytes 786440 | tf_op jit(solution)/shard_map/ppermute | solution.py:133
  25.1 0.7 %collective-permute-start.21 = (bf16[1024,128]{1,0:T(8,128)(2,1)S(1)}, bf16[1024,128]{1,0:T(8,128)(2,1)S(1)}, u32[]{:S(2)}, u32[]{:S(2)}) collective-permute-start(bf16[1024,128]{1,0:T(8,128)(2,1)S(1)} %step3_kernel.1.q_prev), channel_id=1, source_target_pairs={{23,19}} | collective-permute-start | bytes 786440 | tf_op jit(solution)/shard_map/ppermute | solution.py:133
  25.8 0.7 %collective-permute-start.22 = (bf16[1024,128]{1,0:T(8,128)(2,1)S(1)}, bf16[1024,128]{1,0:T(8,128)(2,1)S(1)}, u32[]{:S(2)}, u32[]{:S(2)}) collective-permute-start(bf16[1024,128]{1,0:T(8,128)(2,1)S(1)} %step3_kernel.1.q_prev), channel_id=1, source_target_pairs={{23,11}} | collective-permute-start | bytes 786440 | tf_op jit(solution)/shard_map/ppermute | solution.py:133
  27.9 19.8 %collective-permute-start.23 = (bf16[1040,128]{1,0:T(8,128)(2,1)S(1)}, bf16[1040,128]{1,0:T(8,128)(2,1)S(1)}, u32[]{:S(2)}, u32[]{:S(2)}) collective-permute-start(bf16[1040,128]{1,0:T(8,128)(2,1)S(1)} %get-tuple-element.37.mine_ref), channel_id=1, source_target_pairs={{0,2},{1,3},{2,0},{3,1},{4,6},{5,7},{6,4},{7,5},{8,10},{9,11},{10,... | collective-permute-start | bytes 798728 | tf_op jit(solution)/shard_map/ppermute | solution.py:129
  47.8 1.3 %collective-permute-start.24 = (bf16[1024,128]{1,0:T(8,128)(2,1)S(1)}, bf16[1024,128]{1,0:T(8,128)(2,1)S(1)}, u32[]{:S(2)}, u32[]{:S(2)}) collective-permute-start(bf16[1024,128]{1,0:T(8,128)(2,1)S(1)} %get-tuple-element.36.q_ref), channel_id=1, source_target_pairs={{11,15},{27,3},{31,7}} | collective-permute-start | bytes 786440 | tf_op jit(solution)/shard_map/ppermute | solution.py:133
  49.1 6.0 %collective-permute-start.25 = (bf16[1040,128]{1,0:T(8,128)(2,1)S(1)}, bf16[1040,128]{1,0:T(8,128)(2,1)S(1)}, u32[]{:S(2)}, u32[]{:S(2)}) collective-permute-start(bf16[1040,128]{1,0:T(8,128)(2,1)S(1)} %get-tuple-element.37.mine_ref), channel_id=1, source_target_pairs={{0,1},{1,0},{2,3},{3,2},{4,5},{5,4},{6,7},{7,6},{8,9},{9,8},{10,11... | collective-permute-start | bytes 798728 | tf_op jit(solution)/shard_map/ppermute | solution.py:129
  55.1 5.4 %collective-permute-done.24.rest_ref = bf16[1024,128]{1,0:T(8,128)(2,1)S(1)} collective-permute-done((bf16[1024,128]{1,0:T(8,128)(2,1)S(1)}, bf16[1024,128]{1,0:T(8,128)(2,1)S(1)}, u32[]{:S(2)}, u32[]{:S(2)}) %collective-permute-start.24) | collective-permute-done | bytes 262176 | tf_op jit(solution)/shard_map/ppermute | solution.py:133
  60.7 0.8 %half_kernel.1 = (f32[1024,128]{1,0:T(8,128)}, f32[2,1024,128]{2,1,0:T(8,128)S(1)}) custom-call(bf16[1024,128]{1,0:T(8,128)(2,1)S(1)} %get-tuple-element.36.q_ref, bf16[1024,128]{1,0:T(8,128)(2,1)S(1)} %collective-permute-done.24.rest_ref, f32[2,1024,128]{2,1,0:T(8,128)S(1)} %bitcast.14, bf16[1040,128]{1,0:T(8,128)(2,1)S(1)} %get-tuple-element.37.mine_ref, ...), custom_call_target="tpu_custom_call" | custom-call | tf_op jit(solution)/shard_map/half_kernel/pallas_call | solution.py:156
  62.0 1.2 %final_kernel.1 = f32[2,1024,128]{2,1,0:T(8,128)} custom-call(f32[2,1024,128]{2,1,0:T(8,128)S(1)} %get-tuple-element.41.half_ref, bf16[1040,128]{1,0:T(8,128)(2,1)S(1)} %collective-permute-done.25.beside_ref, bf16[1040,128]{1,0:T(8,128)(2,1)S(1)} %collective-permute-done.26.corner_ref), custom_call_target="tpu_custom_call" | custom-call | tf_op jit(solution)/shard_map/final_kernel/pallas_call | solution.py:156
  (50 shorter events, 5.2 us)
Async XLA Ops:
  2.0 10.3 %collective-permute-start.2 = (bf16[128,1024]{1,0:T(8,128)(2,1)S(1)}, bf16[128,1024]{1,0:T(8,128)(2,1)S(1)}, u32[]{:S(2)}, u32[]{:S(2)}) collective-permute-start(bf16[128,1024]{1,0:T(8,128)(2,1)S(1)} %get-tuple-element.24), channel_id=1, source_target_pairs={{24,1},{25,22},{26,13},{27,15},{28,9},{29,23},{30,3},{31,14}} | collective-permute-start | bytes 786440 | tf_op jit(solution)/shard_map/ppermute | solution.py:133
  2.8 9.5 %collective-permute-start.1 = (bf16[128,768]{1,0:T(8,128)(2,1)S(1)}, bf16[128,768]{1,0:T(8,128)(2,1)S(1)}, u32[]{:S(2)}, u32[]{:S(2)}) collective-permute-start(bf16[128,768]{1,0:T(8,128)(2,1)S(1)} %get-tuple-element.23), channel_id=1, source_target_pairs={{16,0},{17,13},{18,22},{19,15},{20,14},{21,9},{23,2}} | collective-permute-start | bytes 589832 | tf_op jit(solution)/shard_map/ppermute | solution.py:133
  3.6 8.6 %collective-permute-start = (bf16[128,512]{1,0:T(8,128)(2,1)S(1)}, bf16[128,512]{1,0:T(8,128)(2,1)S(1)}, u32[]{:S(2)}, u32[]{:S(2)}) collective-permute-start(bf16[128,512]{1,0:T(8,128)(2,1)S(1)} %get-tuple-element.22), channel_id=1, source_target_pairs={{4,0},{8,22},{10,2},{11,15},{12,1},{13,9},{14,23}} | collective-permute-start | bytes 393224 | tf_op jit(solution)/shard_map/ppermute | solution.py:133
  4.3 8.0 %collective-permute-start.8 = (bf16[128,256]{1,0:T(8,128)(2,1)S(1)}, bf16[128,256]{1,0:T(8,128)(2,1)S(1)}, u32[]{:S(2)}, u32[]{:S(2)}) collective-permute-start(bf16[128,256]{1,0:T(8,128)(2,1)S(1)} %get-tuple-element.26), channel_id=1, source_target_pairs={{1,13},{2,15},{3,22},{5,9},{6,14},{7,23}} | collective-permute-start | bytes 196616 | tf_op jit(solution)/shard_map/ppermute | solution.py:133
  12.3 4.8 %collective-permute-start.9 = (bf16[128,2560]{1,0:T(8,128)(2,1)S(1)}, bf16[128,2560]{1,0:T(8,128)(2,1)S(1)}, u32[]{:S(2)}, u32[]{:S(2)}) collective-permute-start(bf16[128,2560]{1,0:T(8,128)(2,1)S(1)} %pack_kernel.1), channel_id=1, source_target_pairs={{0,1},{1,0},{2,3},{3,2},{4,5},{5,4},{6,7},{7,6},{8,12},{9,8},{10,1... | collective-permute-start | bytes 1966088 | tf_op jit(solution)/shard_map/ppermute | solution.py:129
  14.6 1.8 %collective-permute-start.3 = (bf16[256,128]{1,0:T(8,128)(2,1)S(1)}, bf16[256,128]{1,0:T(8,128)(2,1)S(1)}, u32[]{:S(2)}, u32[]{:S(2)}) collective-permute-start(bf16[256,128]{1,0:T(8,128)(2,1)S(1)} %first_kernel.1), channel_id=1, source_target_pairs={{0,4},{1,8},{2,12},{3,2},{4,5},{5,0},{6,7},{7,6},{8,9},{9,1},{10,1... | collective-permute-start | bytes 196616 | tf_op jit(solution)/shard_map/ppermute | solution.py:129
  14.7 1.7 %collective-permute-start.4 = (bf16[256,128]{1,0:T(8,128)(2,1)S(1)}, bf16[256,128]{1,0:T(8,128)(2,1)S(1)}, u32[]{:S(2)}, u32[]{:S(2)}) collective-permute-start(bf16[256,128]{1,0:T(8,128)(2,1)S(1)} %first_kernel.1), channel_id=1, source_target_pairs={{0,8},{1,12},{2,3},{3,4},{4,5},{5,0},{6,7},{7,6},{8,9},{9,1},{10,1... | collective-permute-start | bytes 196616 | tf_op jit(solution)/shard_map/ppermute | solution.py:129
  16.7 1.5 %collective-permute-start.7 = (bf16[1024,128]{1,0:T(8,128)(2,1)S(1)}, bf16[1024,128]{1,0:T(8,128)(2,1)S(1)}, u32[]{:S(2)}, u32[]{:S(2)}) collective-permute-start(bf16[1024,128]{1,0:T(8,128)(2,1)S(1)} %get-tuple-element.25), channel_id=1, source_target_pairs={{0,1},{1,0},{2,3},{3,2},{4,9},{5,4},{6,7},{7,6},{8,5},{9,8},{10,11... | collective-permute-start | bytes 786440 | tf_op jit(solution)/shard_map/ppermute | solution.py:129
  17.1 1.5 %collective-permute-start.10 = (bf16[1024,128]{1,0:T(8,128)(2,1)S(1)}, bf16[1024,128]{1,0:T(8,128)(2,1)S(1)}, u32[]{:S(2)}, u32[]{:S(2)}) collective-permute-start(bf16[1024,128]{1,0:T(8,128)(2,1)S(1)} %get-tuple-element.28.s_prev), channel_id=1, source_target_pairs={{0,1},{1,0},{2,3},{3,2},{4,5},{5,4},{6,7},{7,6},{8,9},{9,8},{10,11... | collective-permute-start | bytes 786440 | tf_op jit(solution)/shard_map/ppermute | solution.py:129
  18.6 1.6 %collective-permute-start.11 = (bf16[1024,128]{1,0:T(8,128)(2,1)S(1)}, bf16[1024,128]{1,0:T(8,128)(2,1)S(1)}, u32[]{:S(2)}, u32[]{:S(2)}) collective-permute-start(bf16[1024,128]{1,0:T(8,128)(2,1)S(1)} %get-tuple-element.29), channel_id=1, source_target_pairs={{0,1},{1,0},{2,3},{3,2},{4,5},{5,4},{6,7},{7,6},{8,9},{9,14},{10,1... | collective-permute-start | bytes 786440 | tf_op jit(solution)/shard_map/ppermute | solution.py:129
  19.1 1.5 %collective-permute-start.12 = (bf16[1024,128]{1,0:T(8,128)(2,1)S(1)}, bf16[1024,128]{1,0:T(8,128)(2,1)S(1)}, u32[]{:S(2)}, u32[]{:S(2)}) collective-permute-start(bf16[1024,128]{1,0:T(8,128)(2,1)S(1)} %step1_kernel.1.q_in.q_prev), channel_id=1, source_target_pairs={{0,1},{1,5},{2,3},{3,2},{4,0},{5,4},{6,7},{7,6},{8,16},{9,17},{10,... | collective-permute-start | bytes 786440 | tf_op jit(solution)/shard_map/ppermute | solution.py:129
  19.2 1.8 %collective-permute-start.13 = (bf16[1024,128]{1,0:T(8,128)(2,1)S(1)}, bf16[1024,128]{1,0:T(8,128)(2,1)S(1)}, u32[]{:S(2)}, u32[]{:S(2)}) collective-permute-start(bf16[1024,128]{1,0:T(8,128)(2,1)S(1)} %step1_kernel.1.q_in.q_prev), channel_id=1, source_target_pairs={{0,1},{1,0},{2,3},{3,2},{4,5},{5,4},{6,7},{7,6},{8,9},{9,13},{10,1... | collective-permute-start | bytes 786440 | tf_op jit(solution)/shard_map/ppermute | solution.py:129
  21.0 2.6 %collective-permute-start.14 = (bf16[1024,128]{1,0:T(8,128)(2,1)S(1)}, bf16[1024,128]{1,0:T(8,128)(2,1)S(1)}, u32[]{:S(2)}, u32[]{:S(2)}) collective-permute-start(bf16[1024,128]{1,0:T(8,128)(2,1)S(1)} %get-tuple-element.33), channel_id=1, source_target_pairs={{0,1},{1,0},{2,3},{3,2},{4,5},{5,4},{6,7},{7,6},{8,9},{9,8},{10,11... | collective-permute-start | bytes 786440 | tf_op jit(solution)/shard_map/ppermute | solution.py:129
  21.4 2.2 %collective-permute-start.15 = (bf16[1024,128]{1,0:T(8,128)(2,1)S(1)}, bf16[1024,128]{1,0:T(8,128)(2,1)S(1)}, u32[]{:S(2)}, u32[]{:S(2)}) collective-permute-start(bf16[1024,128]{1,0:T(8,128)(2,1)S(1)} %get-tuple-element.32.s_ref), channel_id=1, source_target_pairs={{0,1},{1,0},{2,3},{3,2},{4,5},{5,4},{6,7},{7,6},{8,9},{9,8},{10,11... | collective-permute-start | bytes 786440 | tf_op jit(solution)/shard_map/ppermute | solution.py:129
  21.6 2.1 %collective-permute-start.16 = (bf16[1024,128]{1,0:T(8,128)(2,1)S(1)}, bf16[1024,128]{1,0:T(8,128)(2,1)S(1)}, u32[]{:S(2)}, u32[]{:S(2)}) collective-permute-start(bf16[1024,128]{1,0:T(8,128)(2,1)S(1)} %get-tuple-element.33), channel_id=1, source_target_pairs={{14,10}} | collective-permute-start | bytes 786440 | tf_op jit(solution)/shard_map/ppermute | solution.py:133
  22.2 1.4 %collective-permute-start.17 = (bf16[1024,128]{1,0:T(8,128)(2,1)S(1)}, bf16[1024,128]{1,0:T(8,128)(2,1)S(1)}, u32[]{:S(2)}, u32[]{:S(2)}) collective-permute-start(bf16[1024,128]{1,0:T(8,128)(2,1)S(1)} %get-tuple-element.33), channel_id=1, source_target_pairs={{14,30}} | collective-permute-start | bytes 786440 | tf_op jit(solution)/shard_map/ppermute | solution.py:133
  23.7 4.0 %collective-permute-start.19 = (bf16[1024,128]{1,0:T(8,128)(2,1)S(1)}, bf16[1024,128]{1,0:T(8,128)(2,1)S(1)}, u32[]{:S(2)}, u32[]{:S(2)}) collective-permute-start(bf16[1024,128]{1,0:T(8,128)(2,1)S(1)} %step3_kernel.1.q_prev), channel_id=1, source_target_pairs={{23,27},{10,26},{30,22},{16,24},{20,28},{17,25},{13,21},{9,1}} | collective-permute-start | bytes 786440 | tf_op jit(solution)/shard_map/ppermute | solution.py:133
  24.4 3.4 %collective-permute-start.20 = (bf16[1024,128]{1,0:T(8,128)(2,1)S(1)}, bf16[1024,128]{1,0:T(8,128)(2,1)S(1)}, u32[]{:S(2)}, u32[]{:S(2)}) collective-permute-start(bf16[1024,128]{1,0:T(8,128)(2,1)S(1)} %step3_kernel.1.q_prev), channel_id=1, source_target_pairs={{23,31},{10,2},{14,6},{17,29},{13,5}} | collective-permute-start | bytes 786440 | tf_op jit(solution)/shard_map/ppermute | solution.py:133
  25.1 2.7 %collective-permute-start.21 = (bf16[1024,128]{1,0:T(8,128)(2,1)S(1)}, bf16[1024,128]{1,0:T(8,128)(2,1)S(1)}, u32[]{:S(2)}, u32[]{:S(2)}) collective-permute-start(bf16[1024,128]{1,0:T(8,128)(2,1)S(1)} %step3_kernel.1.q_prev), channel_id=1, source_target_pairs={{23,19}} | collective-permute-start | bytes 786440 | tf_op jit(solution)/shard_map/ppermute | solution.py:133
  25.8 2.0 %collective-permute-start.22 = (bf16[1024,128]{1,0:T(8,128)(2,1)S(1)}, bf16[1024,128]{1,0:T(8,128)(2,1)S(1)}, u32[]{:S(2)}, u32[]{:S(2)}) collective-permute-start(bf16[1024,128]{1,0:T(8,128)(2,1)S(1)} %step3_kernel.1.q_prev), channel_id=1, source_target_pairs={{23,11}} | collective-permute-start | bytes 786440 | tf_op jit(solution)/shard_map/ppermute | solution.py:133
  27.9 32.5 %collective-permute-start.23 = (bf16[1040,128]{1,0:T(8,128)(2,1)S(1)}, bf16[1040,128]{1,0:T(8,128)(2,1)S(1)}, u32[]{:S(2)}, u32[]{:S(2)}) collective-permute-start(bf16[1040,128]{1,0:T(8,128)(2,1)S(1)} %get-tuple-element.37.mine_ref), channel_id=1, source_target_pairs={{0,2},{1,3},{2,0},{3,1},{4,6},{5,7},{6,4},{7,5},{8,10},{9,11},{10,... | collective-permute-start | bytes 798728 | tf_op jit(solution)/shard_map/ppermute | solution.py:129
  47.8 12.7 %collective-permute-start.24 = (bf16[1024,128]{1,0:T(8,128)(2,1)S(1)}, bf16[1024,128]{1,0:T(8,128)(2,1)S(1)}, u32[]{:S(2)}, u32[]{:S(2)}) collective-permute-start(bf16[1024,128]{1,0:T(8,128)(2,1)S(1)} %get-tuple-element.36.q_ref), channel_id=1, source_target_pairs={{11,15},{27,3},{31,7}} | collective-permute-start | bytes 786440 | tf_op jit(solution)/shard_map/ppermute | solution.py:133
  49.1 12.5 %collective-permute-start.25 = (bf16[1040,128]{1,0:T(8,128)(2,1)S(1)}, bf16[1040,128]{1,0:T(8,128)(2,1)S(1)}, u32[]{:S(2)}, u32[]{:S(2)}) collective-permute-start(bf16[1040,128]{1,0:T(8,128)(2,1)S(1)} %get-tuple-element.37.mine_ref), channel_id=1, source_target_pairs={{0,1},{1,0},{2,3},{3,2},{4,5},{5,4},{6,7},{7,6},{8,9},{9,8},{10,11... | collective-permute-start | bytes 798728 | tf_op jit(solution)/shard_map/ppermute | solution.py:129
  60.4 1.5 %collective-permute-start.26 = (bf16[1040,128]{1,0:T(8,128)(2,1)S(1)}, bf16[1040,128]{1,0:T(8,128)(2,1)S(1)}, u32[]{:S(2)}, u32[]{:S(2)}) collective-permute-start(bf16[1040,128]{1,0:T(8,128)(2,1)S(1)} %collective-permute-done.23.across_ref), channel_id=1, source_target_pairs={{0,1},{1,0},{2,3},{3,2},{4,5},{5,4},{6,7},{7,6},{8,9},{9,8},{10,11... | collective-permute-start | bytes 798728 | tf_op jit(solution)/shard_map/ppermute | solution.py:129
  (7 other events, 46.0 us)

commit v17 on v16

--- a/solution.py
+++ b/solution.py
@@ -78,7 +78,7 @@
     (0, 3, 1, 2),
     (1, 3, 0, 2),
 )
-REST = ((3, 3), (0, 3), (1, 3))
+REST = ((2, 3), (3, 3), (0, 3), (1, 3), (0, 2), (1, 2))
 
 
 def hops(a, b):
@@ -239,11 +239,19 @@
             copy.wait()
 
 
-def whole_kernel(diag_ref, even_ref, *refs):
-    odd, out_ref, sem = refs[:-2], refs[-2], refs[-1]
+def whole_kernel(rows_ref, counts_ref, diag_ref, even_ref, *refs):
+    odd, (out_ref, tail_ref, sem) = refs[:-3], refs[-3:]
     size = out_ref.shape[0]
     part = size // NR
     row, col = lax.axis_index("row"), lax.axis_index("col")
+    listed = rows_ref[0, 0, 0, 0]
+    there = (row >= NC) & (counts_ref[0, 0, 0] > 0)
+    done = at(FIRST) | at(MAKER[1]) | at(BESIDE) | at(MAKER[2])
+    first = (there & (listed == 0)) | done
+    second = there & (listed == 1)
+    ids = lax.broadcasted_iota(jnp.int32, tail_ref.shape, 0)
+    flag = ((ids == 0) & first) | ((ids == 1) & second)
+    tail_ref[...] = low(jnp.where(flag, 1.0, 0.0))
 
     @pl.when(any_of(MAKER[1:]))
     def _():
@@ -372,7 +380,7 @@
         q_ref[...] = q_prev[...]
 
 
-def update_kernel(takers, rows_ref, counts_ref, s_ref, l_ref, q_prev, *refs):
+def update_kernel(takers, tail_ref, s_ref, l_ref, q_prev, *refs):
     got, q_ref, out_ref = refs[:-2], refs[-2], refs[-1]
     size = l_ref.shape[0]
     row, col = lax.axis_index("row"), lax.axis_index("col")
@@ -396,14 +404,7 @@
     def _():
         out_ref[pl.ds(0, size)] = s_ref[...]
 
-    listed = rows_ref[0, 0, 0, 0]
-    there = below & (counts_ref[0, 0, 0] > 0)
-    done = at(FIRST) | at(MAKER[1]) | at(BESIDE) | at(MAKER[2])
-    first = (there & (listed == 0)) | done
-    second = there & (listed == 1)
-    ids = lax.broadcasted_iota(jnp.int32, (TAIL, out_ref.shape[1]), 0)
-    flag = ((ids == 0) & first) | ((ids == 1) & second)
-    out_ref[pl.ds(size, TAIL)] = low(jnp.where(flag, 1.0, 0.0))
+    out_ref[pl.ds(size, TAIL)] = tail_ref[...]
 
 
 def minus(acc, sums, i):
@@ -482,12 +483,12 @@
         [pltpu.SemaphoreType.DMA((len(wides),))],
     )
     even = send(even, [(PARTNER[k], MAKER[k]) for k in range(1, NC)])
-    diag = call(
+    diag, tail = call(
         whole_kernel,
-        jax.ShapeDtypeStruct((size, size), bf16),
-        [diag_inv, even, *parts],
-        [HBM] + [ANY] * (1 + len(wides)),
-        VMEM,
+        [jax.ShapeDtypeStruct((size, size), bf16), jax.ShapeDtypeStruct((TAIL, width), bf16)],
+        [block_rows, counts, diag_inv, even, *parts],
+        [SMEM, SMEM, HBM] + [ANY] * (1 + len(wides)),
+        [VMEM, VMEM],
         [pltpu.SemaphoreType.DMA((NR,))],
     )
 
@@ -504,11 +505,10 @@
     p_in, came = lax.optimization_barrier((p_in, came))
 
     a, q, s = call(step2_kernel, [vec] * 3, [p_in, q_in, sums, rhs, diag, block, q, s], [VMEM] * 8, [VMEM] * 3)
-    from_c = a
     a = send(a, [(BESIDE, MAKER[3])])
     sums = send(s, [(MAKER[2], MAKER[3])])
-    early = ((2, 2), (7, 2), (4, 2))
-    got = [send_only(from_c, [(MAKER[2], d)]) for d in early]
+    early = ((2, 2), (7, 2), (5, 2))
+    got = [send_only(q, [(MAKER[2], d)]) for d in early]
     q = call(
         functools.partial(step3_kernel, [[d] for d in early] + [took]),
         vec,
@@ -520,20 +520,19 @@
 
     sends = [
         [
-            (MAKER[3], (6, 3)), ((2, 2), (6, 2)), ((7, 2), (5, 2)),
+            (MAKER[3], (6, 3)), ((2, 2), (4, 2)),
             ((4, 0), (6, 0)), ((5, 0), (7, 0)), ((4, 1), (6, 1)), ((3, 1), (5, 1)), ((2, 1), (0, 1)),
         ],
-        [(MAKER[3], (7, 3)), ((2, 2), (0, 2)), (MAKER[2], (1, 2)), ((4, 1), (7, 1)), ((3, 1), (1, 1))],
+        [(MAKER[3], (7, 3)), ((2, 2), (6, 2)), ((4, 1), (7, 1)), ((3, 1), (1, 1))],
         [(MAKER[3], (4, 3))],
-        [(MAKER[3], (2, 3))],
     ]
     got = [send_only(q, pairs) for pairs in sends]
     takers = [[b for _, b in pairs] for pairs in sends]
     q, mine = call(
         functools.partial(update_kernel, takers),
         [vec, jax.ShapeDtypeStruct((size + TAIL, width), bf16)],
-        [block_rows, counts, s, block, q, *got],
-        [SMEM] * 2 + [VMEM] * (3 + len(got)),
+        [tail, s, block, q, *got],
+        [VMEM] * (4 + len(got)),
         [VMEM] * 2,
     )
 
@@ -541,7 +540,7 @@
         return send(value, [((r, c), (r, c ^ step)) for r in range(NR) for c in range(NC)])
 
     across = swap(mine, 2)
-    rest = send_only(q, list(zip(((2, 3), (6, 3), (7, 3)), REST)))
+    rest = send_only(q, list(zip(((4, 3), (5, 3), (6, 3), (7, 3), (2, 2), MAKER[2]), REST)))
     beside = swap(mine, 1)
     across, rest = lax.optimization_barrier((across, rest))
     corner = swap(across, 1)

time: 63.5 us -> 63.8 us (level)
  starting transfers between devices: 46.4 us -> 41.6 us
  waiting for transfers between devices: 10.8 us -> 15.5 us
    ppermute x12 -> x11, waiting for transfers between devices: 6.71 us -> 12.4 us  [send_only(): lax.ppermute(value, ('row', 'col'), [(a * NC + b, c * NC + d) for (a, b),...]
    ppermute x15, starting transfers between devices: 31.5 us -> 27.3 us  [send(): lax.ppermute(value, ('row', 'col'), [(a * NC + b, c * NC + d) for (a, b),...]
    ppermute x15, waiting for transfers between devices: 4.08 us -> 3.06 us  [send(): lax.ppermute(value, ('row', 'col'), [(a * NC + b, c * NC + d) for (a, b),...]
    ppermute x12 -> x11, starting transfers between devices: 14.9 us -> 14.3 us  [send_only(): lax.ppermute(value, ('row', 'col'), [(a * NC + b, c * NC + d) for (a, b),...]
  transfers between devices with their start and end apart: 27 -> 26, of which waited for: 12 -> 10; matrix products, arithmetic and copies ran while one was open for 0% -> 0% of each run, Pallas kernels for 2% -> 2%
where the time goes in v17:
time: 63.8 us; the launch traced here: 63.2 us
  starting transfers between devices  41.6 us (65%)
  waiting for transfers between devices  15.5 us (24%)
  Pallas kernels  2.51 us (4%)
  between operations  2.22 us (3%)
  local copies, waits for them, and re-layouts  1.32 us (2%)
    ppermute x15, starting transfers between devices, send(): lax.ppermute(value, ('row', 'col'), [(a * NC + b, c * NC + d) for (a, b),...  27.3 us
    ppermute x11, starting transfers between devices, send_only(): lax.ppermute(value, ('row', 'col'), [(a * NC + b, c * NC + d) for (a, b),...  14.3 us
    ppermute x11, waiting for transfers between devices, send_only(): lax.ppermute(value, ('row', 'col'), [(a * NC + b, c * NC + d) for (a, b),...  12.4 us
    ppermute x15, waiting for transfers between devices, send(): lax.ppermute(value, ('row', 'col'), [(a * NC + b, c * NC + d) for (a, b),...  3.06 us
    pallas_call x12, Pallas kernels, call(): pl.pallas_call(kernel, out_shape=outs, in_specs=in_specs, out_specs=out_s...  2.51 us
    unnamed x8, local copies, waits for them, and re-layouts  1.32 us
  transfers between devices with their start and end apart: 26, of which 10 were waited for; matrix products, arithmetic and copies ran while one was open for 0% of the time, Pallas kernels for 2%

profile of v17, /device:TPU:7, one launch (start us, length us, event | category | flops | bytes accessed | tf_op | source)
XLA Modules:
  0.0 63.2 jit_solution(9410362356840200606)
XLA Ops:
  0.6 1.3 %copy-done.2 = bf16[4,128,1024]{2,1,0:T(8,128)(2,1)S(1)} copy-done((bf16[4,128,1024]{2,1,0:T(8,128)(2,1)S(1)}, bf16[4,128,1024]{2,1,0:T(8,128)(2,1)}, u32[]{:S(2)}) %copy-start.2) | copy-done | bytes 1048600
  2.0 0.8 %collective-permute-start.3 = (bf16[128,1024]{1,0:T(8,128)(2,1)S(1)}, bf16[128,1024]{1,0:T(8,128)(2,1)S(1)}, u32[]{:S(2)}, u32[]{:S(2)}) collective-permute-start(bf16[128,1024]{1,0:T(8,128)(2,1)S(1)} %get-tuple-element.27), channel_id=1, source_target_pairs={{24,1},{25,22},{26,13},{27,15},{28,9},{29,23},{30,3},{31,14}} | collective-permute-start | bytes 786440 | tf_op jit(solution)/shard_map/ppermute | solution.py:133
  2.8 0.8 %collective-permute-start.2 = (bf16[128,768]{1,0:T(8,128)(2,1)S(1)}, bf16[128,768]{1,0:T(8,128)(2,1)S(1)}, u32[]{:S(2)}, u32[]{:S(2)}) collective-permute-start(bf16[128,768]{1,0:T(8,128)(2,1)S(1)} %get-tuple-element.26), channel_id=1, source_target_pairs={{16,0},{17,13},{18,22},{19,15},{20,14},{21,9},{23,2}} | collective-permute-start | bytes 589832 | tf_op jit(solution)/shard_map/ppermute | solution.py:133
  3.6 0.7 %collective-permute-start.1 = (bf16[128,512]{1,0:T(8,128)(2,1)S(1)}, bf16[128,512]{1,0:T(8,128)(2,1)S(1)}, u32[]{:S(2)}, u32[]{:S(2)}) collective-permute-start(bf16[128,512]{1,0:T(8,128)(2,1)S(1)} %get-tuple-element.25), channel_id=1, source_target_pairs={{4,0},{8,22},{10,2},{11,15},{12,1},{13,9},{14,23}} | collective-permute-start | bytes 393224 | tf_op jit(solution)/shard_map/ppermute | solution.py:133
  4.3 6.6 %collective-permute-start = (bf16[128,256]{1,0:T(8,128)(2,1)S(1)}, bf16[128,256]{1,0:T(8,128)(2,1)S(1)}, u32[]{:S(2)}, u32[]{:S(2)}) collective-permute-start(bf16[128,256]{1,0:T(8,128)(2,1)S(1)} %get-tuple-element.24), channel_id=1, source_target_pairs={{1,13},{2,15},{3,22},{5,9},{6,14},{7,23}} | collective-permute-start | bytes 196616 | tf_op jit(solution)/shard_map/ppermute | solution.py:133
  11.0 1.3 %collective-permute-done.refs_0_ = bf16[128,256]{1,0:T(8,128)(2,1)S(1)} collective-permute-done((bf16[128,256]{1,0:T(8,128)(2,1)S(1)}, bf16[128,256]{1,0:T(8,128)(2,1)S(1)}, u32[]{:S(2)}, u32[]{:S(2)}) %collective-permute-start) | collective-permute-done | bytes 65568 | tf_op jit(solution)/shard_map/ppermute | solution.py:133
  12.3 2.2 %collective-permute-start.4 = (bf16[128,2560]{1,0:T(8,128)(2,1)S(1)}, bf16[128,2560]{1,0:T(8,128)(2,1)S(1)}, u32[]{:S(2)}, u32[]{:S(2)}) collective-permute-start(bf16[128,2560]{1,0:T(8,128)(2,1)S(1)} %pack_kernel.1), channel_id=1, source_target_pairs={{0,1},{1,0},{2,3},{3,2},{4,5},{5,4},{6,7},{7,6},{8,12},{9,8},{10,1... | collective-permute-start | bytes 1966088 | tf_op jit(solution)/shard_map/ppermute | solution.py:129
  14.7 0.5 collective-permute-start.6
  15.7 0.7 %collective-permute-done.5.g0 = bf16[256,128]{1,0:T(8,128)(2,1)S(1)} collective-permute-done((bf16[256,128]{1,0:T(8,128)(2,1)S(1)}, bf16[256,128]{1,0:T(8,128)(2,1)S(1)}, u32[]{:S(2)}, u32[]{:S(2)}) %collective-permute-start.5) | collective-permute-done | bytes 65568 | tf_op jit(solution)/shard_map/ppermute | solution.py:129
  18.7 0.4 collective-permute-start.11
  19.7 0.7 %collective-permute-done.11.p_in = bf16[1024,128]{1,0:T(8,128)(2,1)S(1)} collective-permute-done((bf16[1024,128]{1,0:T(8,128)(2,1)S(1)}, bf16[1024,128]{1,0:T(8,128)(2,1)S(1)}, u32[]{:S(2)}, u32[]{:S(2)}) %collective-permute-start.11) | collective-permute-done | bytes 262176 | tf_op jit(solution)/shard_map/ppermute | solution.py:129
  21.1 0.4 collective-permute-start.14
  21.7 0.7 %collective-permute-start.16 = (bf16[1024,128]{1,0:T(8,128)(2,1)S(1)}, bf16[1024,128]{1,0:T(8,128)(2,1)S(1)}, u32[]{:S(2)}, u32[]{:S(2)}) collective-permute-start(bf16[1024,128]{1,0:T(8,128)(2,1)S(1)} %get-tuple-element.38.refs_5_), channel_id=1, source_target_pairs={{14,10}} | collective-permute-start | bytes 786440 | tf_op jit(solution)/shard_map/ppermute | solution.py:133
  22.3 0.7 %collective-permute-start.17 = (bf16[1024,128]{1,0:T(8,128)(2,1)S(1)}, bf16[1024,128]{1,0:T(8,128)(2,1)S(1)}, u32[]{:S(2)}, u32[]{:S(2)}) collective-permute-start(bf16[1024,128]{1,0:T(8,128)(2,1)S(1)} %get-tuple-element.38.refs_5_), channel_id=1, source_target_pairs={{14,30}} | collective-permute-start | bytes 786440 | tf_op jit(solution)/shard_map/ppermute | solution.py:133
  23.0 0.7 %collective-permute-start.18 = (bf16[1024,128]{1,0:T(8,128)(2,1)S(1)}, bf16[1024,128]{1,0:T(8,128)(2,1)S(1)}, u32[]{:S(2)}, u32[]{:S(2)}) collective-permute-start(bf16[1024,128]{1,0:T(8,128)(2,1)S(1)} %get-tuple-element.38.refs_5_), channel_id=1, source_target_pairs={{14,22}} | collective-permute-start | bytes 786440 | tf_op jit(solution)/shard_map/ppermute | solution.py:133
  23.8 0.7 %collective-permute-start.19 = (bf16[1024,128]{1,0:T(8,128)(2,1)S(1)}, bf16[1024,128]{1,0:T(8,128)(2,1)S(1)}, u32[]{:S(2)}, u32[]{:S(2)}) collective-permute-start(bf16[1024,128]{1,0:T(8,128)(2,1)S(1)} %step3_kernel.1.q_prev), channel_id=1, source_target_pairs={{23,27},{10,18},{16,24},{20,28},{17,25},{13,21},{9,1}} | collective-permute-start | bytes 786440 | tf_op jit(solution)/shard_map/ppermute | solution.py:133
  24.5 0.7 %collective-permute-start.20 = (bf16[1024,128]{1,0:T(8,128)(2,1)S(1)}, bf16[1024,128]{1,0:T(8,128)(2,1)S(1)}, u32[]{:S(2)}, u32[]{:S(2)}) collective-permute-start(bf16[1024,128]{1,0:T(8,128)(2,1)S(1)} %step3_kernel.1.q_prev), channel_id=1, source_target_pairs={{23,31},{10,26},{17,29},{13,5}} | collective-permute-start | bytes 786440 | tf_op jit(solution)/shard_map/ppermute | solution.py:133
  25.2 0.7 %collective-permute-start.21 = (bf16[1024,128]{1,0:T(8,128)(2,1)S(1)}, bf16[1024,128]{1,0:T(8,128)(2,1)S(1)}, u32[]{:S(2)}, u32[]{:S(2)}) collective-permute-start(bf16[1024,128]{1,0:T(8,128)(2,1)S(1)} %step3_kernel.1.q_prev), channel_id=1, source_target_pairs={{23,19}} | collective-permute-start | bytes 786440 | tf_op jit(solution)/shard_map/ppermute | solution.py:133
  26.0 21.9 %collective-permute-start.22 = (bf16[1040,128]{1,0:T(8,128)(2,1)S(1)}, bf16[1040,128]{1,0:T(8,128)(2,1)S(1)}, u32[]{:S(2)}, u32[]{:S(2)}) collective-permute-start(bf16[1040,128]{1,0:T(8,128)(2,1)S(1)} %get-tuple-element.41.mine_ref), channel_id=1, source_target_pairs={{0,2},{1,3},{2,0},{3,1},{4,6},{5,7},{6,4},{7,5},{8,10},{9,11},{10,... | collective-permute-start | bytes 798728 | tf_op jit(solution)/shard_map/ppermute | solution.py:129
  47.9 1.3 %collective-permute-start.23 = (bf16[1024,128]{1,0:T(8,128)(2,1)S(1)}, bf16[1024,128]{1,0:T(8,128)(2,1)S(1)}, u32[]{:S(2)}, u32[]{:S(2)}) collective-permute-start(bf16[1024,128]{1,0:T(8,128)(2,1)S(1)} %get-tuple-element.40.q_ref), channel_id=1, source_target_pairs={{19,11},{23,15},{27,3},{31,7},{10,2},{14,6}} | collective-permute-start | bytes 786440 | tf_op jit(solution)/shard_map/ppermute | solution.py:133
  49.3 11.1 %collective-permute-done.23.rest_ref = bf16[1024,128]{1,0:T(8,128)(2,1)S(1)} collective-permute-done((bf16[1024,128]{1,0:T(8,128)(2,1)S(1)}, bf16[1024,128]{1,0:T(8,128)(2,1)S(1)}, u32[]{:S(2)}, u32[]{:S(2)}) %collective-permute-start.23) | collective-permute-done | bytes 262176 | tf_op jit(solution)/shard_map/ppermute | solution.py:133
  60.4 0.8 %half_kernel.1 = (f32[1024,128]{1,0:T(8,128)}, f32[2,1024,128]{2,1,0:T(8,128)S(1)}) custom-call(bf16[1024,128]{1,0:T(8,128)(2,1)S(1)} %get-tuple-element.40.q_ref, bf16[1024,128]{1,0:T(8,128)(2,1)S(1)} %collective-permute-done.23.rest_ref, f32[2,1024,128]{2,1,0:T(8,128)S(1)} %bitcast.14, bf16[1040,128]{1,0:T(8,128)(2,1)S(1)} %get-tuple-element.41.mine_ref, ...), custom_call_target="tpu_custom_call" | custom-call | tf_op jit(solution)/shard_map/half_kernel/pallas_call | solution.py:156
  61.3 0.7 %collective-permute-done.25.corner_ref = bf16[1040,128]{1,0:T(8,128)(2,1)S(1)} collective-permute-done((bf16[1040,128]{1,0:T(8,128)(2,1)S(1)}, bf16[1040,128]{1,0:T(8,128)(2,1)S(1)}, u32[]{:S(2)}, u32[]{:S(2)}) %collective-permute-start.25) | collective-permute-done | bytes 266272 | tf_op jit(solution)/shard_map/ppermute | solution.py:129
  62.0 1.2 %final_kernel.1 = f32[2,1024,128]{2,1,0:T(8,128)} custom-call(f32[2,1024,128]{2,1,0:T(8,128)S(1)} %get-tuple-element.45.half_ref, bf16[1040,128]{1,0:T(8,128)(2,1)S(1)} %collective-permute-done.24.beside_ref, bf16[1040,128]{1,0:T(8,128)(2,1)S(1)} %collective-permute-done.25.corner_ref), custom_call_target="tpu_custom_call" | custom-call | tf_op jit(solution)/shard_map/final_kernel/pallas_call | solution.py:156
  (48 shorter events, 3.4 us)
Async XLA Ops:
  2.0 10.3 %collective-permute-start.3 = (bf16[128,1024]{1,0:T(8,128)(2,1)S(1)}, bf16[128,1024]{1,0:T(8,128)(2,1)S(1)}, u32[]{:S(2)}, u32[]{:S(2)}) collective-permute-start(bf16[128,1024]{1,0:T(8,128)(2,1)S(1)} %get-tuple-element.27), channel_id=1, source_target_pairs={{24,1},{25,22},{26,13},{27,15},{28,9},{29,23},{30,3},{31,14}} | collective-permute-start | bytes 786440 | tf_op jit(solution)/shard_map/ppermute | solution.py:133
  2.8 9.5 %collective-permute-start.2 = (bf16[128,768]{1,0:T(8,128)(2,1)S(1)}, bf16[128,768]{1,0:T(8,128)(2,1)S(1)}, u32[]{:S(2)}, u32[]{:S(2)}) collective-permute-start(bf16[128,768]{1,0:T(8,128)(2,1)S(1)} %get-tuple-element.26), channel_id=1, source_target_pairs={{16,0},{17,13},{18,22},{19,15},{20,14},{21,9},{23,2}} | collective-permute-start | bytes 589832 | tf_op jit(solution)/shard_map/ppermute | solution.py:133
  3.6 8.6 %collective-permute-start.1 = (bf16[128,512]{1,0:T(8,128)(2,1)S(1)}, bf16[128,512]{1,0:T(8,128)(2,1)S(1)}, u32[]{:S(2)}, u32[]{:S(2)}) collective-permute-start(bf16[128,512]{1,0:T(8,128)(2,1)S(1)} %get-tuple-element.25), channel_id=1, source_target_pairs={{4,0},{8,22},{10,2},{11,15},{12,1},{13,9},{14,23}} | collective-permute-start | bytes 393224 | tf_op jit(solution)/shard_map/ppermute | solution.py:133
  4.3 8.0 %collective-permute-start = (bf16[128,256]{1,0:T(8,128)(2,1)S(1)}, bf16[128,256]{1,0:T(8,128)(2,1)S(1)}, u32[]{:S(2)}, u32[]{:S(2)}) collective-permute-start(bf16[128,256]{1,0:T(8,128)(2,1)S(1)} %get-tuple-element.24), channel_id=1, source_target_pairs={{1,13},{2,15},{3,22},{5,9},{6,14},{7,23}} | collective-permute-start | bytes 196616 | tf_op jit(solution)/shard_map/ppermute | solution.py:133
  12.3 6.1 %collective-permute-start.4 = (bf16[128,2560]{1,0:T(8,128)(2,1)S(1)}, bf16[128,2560]{1,0:T(8,128)(2,1)S(1)}, u32[]{:S(2)}, u32[]{:S(2)}) collective-permute-start(bf16[128,2560]{1,0:T(8,128)(2,1)S(1)} %pack_kernel.1), channel_id=1, source_target_pairs={{0,1},{1,0},{2,3},{3,2},{4,5},{5,4},{6,7},{7,6},{8,12},{9,8},{10,1... | collective-permute-start | bytes 1966088 | tf_op jit(solution)/shard_map/ppermute | solution.py:129
  14.6 1.8 %collective-permute-start.5 = (bf16[256,128]{1,0:T(8,128)(2,1)S(1)}, bf16[256,128]{1,0:T(8,128)(2,1)S(1)}, u32[]{:S(2)}, u32[]{:S(2)}) collective-permute-start(bf16[256,128]{1,0:T(8,128)(2,1)S(1)} %first_kernel.1), channel_id=1, source_target_pairs={{0,4},{1,8},{2,12},{3,2},{4,5},{5,0},{6,7},{7,6},{8,9},{9,1},{10,1... | collective-permute-start | bytes 196616 | tf_op jit(solution)/shard_map/ppermute | solution.py:129
  14.7 1.7 %collective-permute-start.6 = (bf16[256,128]{1,0:T(8,128)(2,1)S(1)}, bf16[256,128]{1,0:T(8,128)(2,1)S(1)}, u32[]{:S(2)}, u32[]{:S(2)}) collective-permute-start(bf16[256,128]{1,0:T(8,128)(2,1)S(1)} %first_kernel.1), channel_id=1, source_target_pairs={{0,8},{1,12},{2,3},{3,4},{4,5},{5,0},{6,7},{7,6},{8,9},{9,1},{10,1... | collective-permute-start | bytes 196616 | tf_op jit(solution)/shard_map/ppermute | solution.py:129
  15.2 1.4 %collective-permute-start.7 = (bf16[256,128]{1,0:T(8,128)(2,1)S(1)}, bf16[256,128]{1,0:T(8,128)(2,1)S(1)}, u32[]{:S(2)}, u32[]{:S(2)}) collective-permute-start(bf16[256,128]{1,0:T(8,128)(2,1)S(1)} %first_kernel.1), channel_id=1, source_target_pairs={{0,12},{1,0},{2,4},{3,8},{4,5},{5,1},{6,7},{7,6},{8,9},{9,2},{10,1... | collective-permute-start | bytes 196616 | tf_op jit(solution)/shard_map/ppermute | solution.py:129
  15.3 1.4 %collective-permute-start.8 = (bf16[256,128]{1,0:T(8,128)(2,1)S(1)}, bf16[256,128]{1,0:T(8,128)(2,1)S(1)}, u32[]{:S(2)}, u32[]{:S(2)}) collective-permute-start(bf16[256,128]{1,0:T(8,128)(2,1)S(1)} %first_kernel.1), channel_id=1, source_target_pairs={{0,1},{1,4},{2,8},{3,12},{4,5},{5,0},{6,7},{7,6},{8,9},{9,2},{10,1... | collective-permute-start | bytes 196616 | tf_op jit(solution)/shard_map/ppermute | solution.py:129
  16.7 1.9 %collective-permute-start.9 = (bf16[1024,128]{1,0:T(8,128)(2,1)S(1)}, bf16[1024,128]{1,0:T(8,128)(2,1)S(1)}, u32[]{:S(2)}, u32[]{:S(2)}) collective-permute-start(bf16[1024,128]{1,0:T(8,128)(2,1)S(1)} %get-tuple-element.29), channel_id=1, source_target_pairs={{0,1},{1,0},{2,3},{3,2},{4,9},{5,4},{6,7},{7,6},{8,5},{9,8},{10,11... | collective-permute-start | bytes 786440 | tf_op jit(solution)/shard_map/ppermute | solution.py:129
  17.1 1.6 %collective-permute-start.10 = (bf16[1024,128]{1,0:T(8,128)(2,1)S(1)}, bf16[1024,128]{1,0:T(8,128)(2,1)S(1)}, u32[]{:S(2)}, u32[]{:S(2)}) collective-permute-start(bf16[1024,128]{1,0:T(8,128)(2,1)S(1)} %get-tuple-element.32.s_prev), channel_id=1, source_target_pairs={{0,1},{1,0},{2,3},{3,2},{4,5},{5,4},{6,7},{7,6},{8,9},{9,8},{10,11... | collective-permute-start | bytes 786440 | tf_op jit(solution)/shard_map/ppermute | solution.py:129
  18.7 1.6 %collective-permute-start.11 = (bf16[1024,128]{1,0:T(8,128)(2,1)S(1)}, bf16[1024,128]{1,0:T(8,128)(2,1)S(1)}, u32[]{:S(2)}, u32[]{:S(2)}) collective-permute-start(bf16[1024,128]{1,0:T(8,128)(2,1)S(1)} %get-tuple-element.33), channel_id=1, source_target_pairs={{0,1},{1,0},{2,3},{3,2},{4,5},{5,4},{6,7},{7,6},{8,9},{9,14},{10,1... | collective-permute-start | bytes 786440 | tf_op jit(solution)/shard_map/ppermute | solution.py:129
  19.2 1.5 %collective-permute-start.12 = (bf16[1024,128]{1,0:T(8,128)(2,1)S(1)}, bf16[1024,128]{1,0:T(8,128)(2,1)S(1)}, u32[]{:S(2)}, u32[]{:S(2)}) collective-permute-start(bf16[1024,128]{1,0:T(8,128)(2,1)S(1)} %step1_kernel.1.q_in.q_prev), channel_id=1, source_target_pairs={{0,1},{1,5},{2,3},{3,2},{4,0},{5,4},{6,7},{7,6},{8,16},{9,17},{10,... | collective-permute-start | bytes 786440 | tf_op jit(solution)/shard_map/ppermute | solution.py:129
  19.3 1.8 %collective-permute-start.13 = (bf16[1024,128]{1,0:T(8,128)(2,1)S(1)}, bf16[1024,128]{1,0:T(8,128)(2,1)S(1)}, u32[]{:S(2)}, u32[]{:S(2)}) collective-permute-start(bf16[1024,128]{1,0:T(8,128)(2,1)S(1)} %step1_kernel.1.q_in.q_prev), channel_id=1, source_target_pairs={{0,1},{1,0},{2,3},{3,2},{4,5},{5,4},{6,7},{7,6},{8,9},{9,13},{10,1... | collective-permute-start | bytes 786440 | tf_op jit(solution)/shard_map/ppermute | solution.py:129
  21.1 2.6 %collective-permute-start.14 = (bf16[1024,128]{1,0:T(8,128)(2,1)S(1)}, bf16[1024,128]{1,0:T(8,128)(2,1)S(1)}, u32[]{:S(2)}, u32[]{:S(2)}) collective-permute-start(bf16[1024,128]{1,0:T(8,128)(2,1)S(1)} %get-tuple-element.37), channel_id=1, source_target_pairs={{0,1},{1,0},{2,3},{3,2},{4,5},{5,4},{6,7},{7,6},{8,9},{9,8},{10,11... | collective-permute-start | bytes 786440 | tf_op jit(solution)/shard_map/ppermute | solution.py:129
  21.5 2.2 %collective-permute-start.15 = (bf16[1024,128]{1,0:T(8,128)(2,1)S(1)}, bf16[1024,128]{1,0:T(8,128)(2,1)S(1)}, u32[]{:S(2)}, u32[]{:S(2)}) collective-permute-start(bf16[1024,128]{1,0:T(8,128)(2,1)S(1)} %get-tuple-element.36.s_ref), channel_id=1, source_target_pairs={{0,1},{1,0},{2,3},{3,2},{4,5},{5,4},{6,7},{7,6},{8,9},{9,8},{10,11... | collective-permute-start | bytes 786440 | tf_op jit(solution)/shard_map/ppermute | solution.py:129
  21.7 2.1 %collective-permute-start.16 = (bf16[1024,128]{1,0:T(8,128)(2,1)S(1)}, bf16[1024,128]{1,0:T(8,128)(2,1)S(1)}, u32[]{:S(2)}, u32[]{:S(2)}) collective-permute-start(bf16[1024,128]{1,0:T(8,128)(2,1)S(1)} %get-tuple-element.38.refs_5_), channel_id=1, source_target_pairs={{14,10}} | collective-permute-start | bytes 786440 | tf_op jit(solution)/shard_map/ppermute | solution.py:133
  22.3 1.4 %collective-permute-start.17 = (bf16[1024,128]{1,0:T(8,128)(2,1)S(1)}, bf16[1024,128]{1,0:T(8,128)(2,1)S(1)}, u32[]{:S(2)}, u32[]{:S(2)}) collective-permute-start(bf16[1024,128]{1,0:T(8,128)(2,1)S(1)} %get-tuple-element.38.refs_5_), channel_id=1, source_target_pairs={{14,30}} | collective-permute-start | bytes 786440 | tf_op jit(solution)/shard_map/ppermute | solution.py:133
  23.8 2.1 %collective-permute-start.19 = (bf16[1024,128]{1,0:T(8,128)(2,1)S(1)}, bf16[1024,128]{1,0:T(8,128)(2,1)S(1)}, u32[]{:S(2)}, u32[]{:S(2)}) collective-permute-start(bf16[1024,128]{1,0:T(8,128)(2,1)S(1)} %step3_kernel.1.q_prev), channel_id=1, source_target_pairs={{23,27},{10,18},{16,24},{20,28},{17,25},{13,21},{9,1}} | collective-permute-start | bytes 786440 | tf_op jit(solution)/shard_map/ppermute | solution.py:133
  24.5 1.4 %collective-permute-start.20 = (bf16[1024,128]{1,0:T(8,128)(2,1)S(1)}, bf16[1024,128]{1,0:T(8,128)(2,1)S(1)}, u32[]{:S(2)}, u32[]{:S(2)}) collective-permute-start(bf16[1024,128]{1,0:T(8,128)(2,1)S(1)} %step3_kernel.1.q_prev), channel_id=1, source_target_pairs={{23,31},{10,26},{17,29},{13,5}} | collective-permute-start | bytes 786440 | tf_op jit(solution)/shard_map/ppermute | solution.py:133
  26.0 34.4 %collective-permute-start.22 = (bf16[1040,128]{1,0:T(8,128)(2,1)S(1)}, bf16[1040,128]{1,0:T(8,128)(2,1)S(1)}, u32[]{:S(2)}, u32[]{:S(2)}) collective-permute-start(bf16[1040,128]{1,0:T(8,128)(2,1)S(1)} %get-tuple-element.41.mine_ref), channel_id=1, source_target_pairs={{0,2},{1,3},{2,0},{3,1},{4,6},{5,7},{6,4},{7,5},{8,10},{9,11},{10,... | collective-permute-start | bytes 798728 | tf_op jit(solution)/shard_map/ppermute | solution.py:129
  47.9 12.5 %collective-permute-start.23 = (bf16[1024,128]{1,0:T(8,128)(2,1)S(1)}, bf16[1024,128]{1,0:T(8,128)(2,1)S(1)}, u32[]{:S(2)}, u32[]{:S(2)}) collective-permute-start(bf16[1024,128]{1,0:T(8,128)(2,1)S(1)} %get-tuple-element.40.q_ref), channel_id=1, source_target_pairs={{19,11},{23,15},{27,3},{31,7},{10,2},{14,6}} | collective-permute-start | bytes 786440 | tf_op jit(solution)/shard_map/ppermute | solution.py:133
  49.2 12.0 %collective-permute-start.24 = (bf16[1040,128]{1,0:T(8,128)(2,1)S(1)}, bf16[1040,128]{1,0:T(8,128)(2,1)S(1)}, u32[]{:S(2)}, u32[]{:S(2)}) collective-permute-start(bf16[1040,128]{1,0:T(8,128)(2,1)S(1)} %get-tuple-element.41.mine_ref), channel_id=1, source_target_pairs={{0,1},{1,0},{2,3},{3,2},{4,5},{5,4},{6,7},{7,6},{8,9},{9,8},{10,11... | collective-permute-start | bytes 798728 | tf_op jit(solution)/shard_map/ppermute | solution.py:129
  60.4 1.5 %collective-permute-start.25 = (bf16[1040,128]{1,0:T(8,128)(2,1)S(1)}, bf16[1040,128]{1,0:T(8,128)(2,1)S(1)}, u32[]{:S(2)}, u32[]{:S(2)}) collective-permute-start(bf16[1040,128]{1,0:T(8,128)(2,1)S(1)} %collective-permute-done.22.across_ref), channel_id=1, source_target_pairs={{0,1},{1,0},{2,3},{3,2},{4,5},{5,4},{6,7},{7,6},{8,9},{9,8},{10,11... | collective-permute-start | bytes 798728 | tf_op jit(solution)/shard_map/ppermute | solution.py:129
  (6 other events, 44.0 us)

commit v18 on v17

--- a/solution.py
+++ b/solution.py
@@ -338,13 +338,12 @@
         s_ref[...] = s_prev[...]
 
 
-def step2_kernel(p_in, q_in, sum_ref, rhs_ref, d_ref, l_ref, q_prev, s_prev, a_ref, q_ref, s_ref):
-    active, beside = at(MAKER[2]), at(BESIDE)
+def step2_kernel(takers, p_in, q_in, came_ref, sum_ref, rhs_ref, d_ref, l_ref, q_prev, s_prev, a_ref, q_ref, s_ref):
+    active, beside, taken = at(MAKER[2]), at(BESIDE), any_of(takers)
 
     @pl.when(active)
     def _():
         lower_dot(q_ref, d_ref, p_in)
-        a_ref[...] = q_ref[...]
         s_ref[...] = low(dot(l_ref[...], q_ref[...]))
 
     @pl.when(beside)
@@ -356,8 +355,15 @@
 
     @pl.when(jnp.logical_not(active | beside))
     def _():
+        s_ref[...] = s_prev[...]
+
+    @pl.when(taken)
+    def _():
+        q_ref[...] = came_ref[...]
+
+    @pl.when(jnp.logical_not(active | beside | taken))
+    def _():
         q_ref[...] = q_prev[...]
-        s_ref[...] = s_prev[...]
 
 
 def step3_kernel(takers, a_ref, sum_ref, *refs):
@@ -502,28 +508,33 @@
 
     came = send(q, [((2, 0), (4, 0)), ((3, 0), (5, 0)), ((1, 0), (0, 0)), ((2, 1), (4, 1))])
     took = [(4, 0), (5, 0), (0, 0), (4, 1)]
-    p_in, came = lax.optimization_barrier((p_in, came))
-
-    a, q, s = call(step2_kernel, [vec] * 3, [p_in, q_in, sums, rhs, diag, block, q, s], [VMEM] * 8, [VMEM] * 3)
+    a, q, s = call(
+        functools.partial(step2_kernel, took),
+        [vec] * 3,
+        [p_in, q_in, came, sums, rhs, diag, block, q, s],
+        [VMEM] * 9,
+        [VMEM] * 3,
+    )
     a = send(a, [(BESIDE, MAKER[3])])
     sums = send(s, [(MAKER[2], MAKER[3])])
-    early = ((2, 2), (7, 2), (5, 2))
-    got = [send_only(q, [(MAKER[2], d)]) for d in early]
+    sends = [
+        [(MAKER[2], (2, 2))],
+        [(MAKER[2], (7, 2)), ((4, 0), (6, 0)), ((5, 0), (7, 0)), ((4, 1), (6, 1)), ((3, 1), (5, 1)), ((2, 1), (0, 1))],
+        [(MAKER[2], (5, 2)), ((4, 1), (7, 1)), ((3, 1), (1, 1))],
+    ]
+    got = [send(q, sends[0])] + [send_only(q, pairs) for pairs in sends[1:]]
     q = call(
-        functools.partial(step3_kernel, [[d] for d in early] + [took]),
+        functools.partial(step3_kernel, [[b for _, b in pairs] for pairs in sends]),
         vec,
-        [a, sums, *got, came, diag, q],
-        [VMEM] * 8,
+        [a, sums, *got, diag, q],
+        [VMEM] * 7,
         VMEM,
         [pltpu.VMEM((size, width), bf16)],
     )
 
     sends = [
-        [
-            (MAKER[3], (6, 3)), ((2, 2), (4, 2)),
-            ((4, 0), (6, 0)), ((5, 0), (7, 0)), ((4, 1), (6, 1)), ((3, 1), (5, 1)), ((2, 1), (0, 1)),
-        ],
-        [(MAKER[3], (7, 3)), ((2, 2), (6, 2)), ((4, 1), (7, 1)), ((3, 1), (1, 1))],
+        [(MAKER[3], (6, 3)), ((2, 2), (6, 2))],
+        [(MAKER[3], (7, 3)), ((2, 2), (4, 2))],
         [(MAKER[3], (4, 3))],
     ]
     got = [send_only(q, pairs) for pairs in sends]

time: 63.8 us -> 63.9 us (level)
  starting transfers between devices: 41.6 us -> 42.9 us
  waiting for transfers between devices: 15.5 us -> 14.8 us
    ppermute x15 -> x16, starting transfers between devices: 27.3 us -> 29.3 us  [send(): lax.ppermute(value, ('row', 'col'), [(a * NC + b, c * NC + d) for (a, b),...]
    ppermute x11 -> x10, waiting for transfers between devices: 12.4 us -> 11.7 us  [send_only(): lax.ppermute(value, ('row', 'col'), [(a * NC + b, c * NC + d) for (a, b),...]
    ppermute x11 -> x10, starting transfers between devices: 14.3 us -> 13.6 us  [send_only(): lax.ppermute(value, ('row', 'col'), [(a * NC + b, c * NC + d) for (a, b),...]
    ppermute x15 -> x16, waiting for transfers between devices: 3.06 us -> 3.08 us  [send(): lax.ppermute(value, ('row', 'col'), [(a * NC + b, c * NC + d) for (a, b),...]
where the time goes in v18:
time: 63.9 us; the launch traced here: 63.7 us
  starting transfers between devices  42.9 us (67%)
  waiting for transfers between devices  14.8 us (23%)
  Pallas kernels  2.5 us (4%)
  between operations  2.2 us (3%)
  local copies, waits for them, and re-layouts  1.32 us (2%)
    ppermute x16, starting transfers between devices, send(): lax.ppermute(value, ('row', 'col'), [(a * NC + b, c * NC + d) for (a, b),...  29.3 us
    ppermute x10, starting transfers between devices, send_only(): lax.ppermute(value, ('row', 'col'), [(a * NC + b, c * NC + d) for (a, b),...  13.6 us
    ppermute x10, waiting for transfers between devices, send_only(): lax.ppermute(value, ('row', 'col'), [(a * NC + b, c * NC + d) for (a, b),...  11.7 us
    ppermute x16, waiting for transfers between devices, send(): lax.ppermute(value, ('row', 'col'), [(a * NC + b, c * NC + d) for (a, b),...  3.08 us
    pallas_call x12, Pallas kernels, call(): pl.pallas_call(kernel, out_shape=outs, in_specs=in_specs, out_specs=out_s...  2.5 us
    unnamed x8, local copies, waits for them, and re-layouts  1.32 us
  transfers between devices with their start and end apart: 26, of which 10 were waited for; matrix products, arithmetic and copies ran while one was open for 0% of the time, Pallas kernels for 2%

profile of v18, /device:TPU:7, one launch (start us, length us, event | category | flops | bytes accessed | tf_op | source)
XLA Modules:
  0.0 63.7 jit_solution(340631867330474313)
XLA Ops:
  0.6 1.3 %copy-done.2 = bf16[4,128,1024]{2,1,0:T(8,128)(2,1)S(1)} copy-done((bf16[4,128,1024]{2,1,0:T(8,128)(2,1)S(1)}, bf16[4,128,1024]{2,1,0:T(8,128)(2,1)}, u32[]{:S(2)}) %copy-start.2) | copy-done | bytes 1048600
  2.0 0.8 %collective-permute-start.3 = (bf16[128,1024]{1,0:T(8,128)(2,1)S(1)}, bf16[128,1024]{1,0:T(8,128)(2,1)S(1)}, u32[]{:S(2)}, u32[]{:S(2)}) collective-permute-start(bf16[128,1024]{1,0:T(8,128)(2,1)S(1)} %get-tuple-element.25), channel_id=1, source_target_pairs={{24,1},{25,22},{26,13},{27,15},{28,9},{29,23},{30,3},{31,14}} | collective-permute-start | bytes 786440 | tf_op jit(solution)/shard_map/ppermute | solution.py:133
  2.8 0.8 %collective-permute-start.2 = (bf16[128,768]{1,0:T(8,128)(2,1)S(1)}, bf16[128,768]{1,0:T(8,128)(2,1)S(1)}, u32[]{:S(2)}, u32[]{:S(2)}) collective-permute-start(bf16[128,768]{1,0:T(8,128)(2,1)S(1)} %get-tuple-element.24), channel_id=1, source_target_pairs={{16,0},{17,13},{18,22},{19,15},{20,14},{21,9},{23,2}} | collective-permute-start | bytes 589832 | tf_op jit(solution)/shard_map/ppermute | solution.py:133
  3.6 0.7 %collective-permute-start.1 = (bf16[128,512]{1,0:T(8,128)(2,1)S(1)}, bf16[128,512]{1,0:T(8,128)(2,1)S(1)}, u32[]{:S(2)}, u32[]{:S(2)}) collective-permute-start(bf16[128,512]{1,0:T(8,128)(2,1)S(1)} %get-tuple-element.23), channel_id=1, source_target_pairs={{4,0},{8,22},{10,2},{11,15},{12,1},{13,9},{14,23}} | collective-permute-start | bytes 393224 | tf_op jit(solution)/shard_map/ppermute | solution.py:133
  4.3 6.6 %collective-permute-start = (bf16[128,256]{1,0:T(8,128)(2,1)S(1)}, bf16[128,256]{1,0:T(8,128)(2,1)S(1)}, u32[]{:S(2)}, u32[]{:S(2)}) collective-permute-start(bf16[128,256]{1,0:T(8,128)(2,1)S(1)} %get-tuple-element.22), channel_id=1, source_target_pairs={{1,13},{2,15},{3,22},{5,9},{6,14},{7,23}} | collective-permute-start | bytes 196616 | tf_op jit(solution)/shard_map/ppermute | solution.py:133
  11.0 1.3 %collective-permute-done.refs_0_ = bf16[128,256]{1,0:T(8,128)(2,1)S(1)} collective-permute-done((bf16[128,256]{1,0:T(8,128)(2,1)S(1)}, bf16[128,256]{1,0:T(8,128)(2,1)S(1)}, u32[]{:S(2)}, u32[]{:S(2)}) %collective-permute-start) | collective-permute-done | bytes 65568 | tf_op jit(solution)/shard_map/ppermute | solution.py:133
  12.3 2.2 %collective-permute-start.4 = (bf16[128,2560]{1,0:T(8,128)(2,1)S(1)}, bf16[128,2560]{1,0:T(8,128)(2,1)S(1)}, u32[]{:S(2)}, u32[]{:S(2)}) collective-permute-start(bf16[128,2560]{1,0:T(8,128)(2,1)S(1)} %pack_kernel.1), channel_id=1, source_target_pairs={{0,1},{1,0},{2,3},{3,2},{4,5},{5,4},{6,7},{7,6},{8,12},{9,8},{10,1... | collective-permute-start | bytes 1966088 | tf_op jit(solution)/shard_map/ppermute | solution.py:129
  14.7 0.5 collective-permute-start.6
  15.3 0.4 collective-permute-start.8
  15.7 0.7 %collective-permute-done.5.g0 = bf16[256,128]{1,0:T(8,128)(2,1)S(1)} collective-permute-done((bf16[256,128]{1,0:T(8,128)(2,1)S(1)}, bf16[256,128]{1,0:T(8,128)(2,1)S(1)}, u32[]{:S(2)}, u32[]{:S(2)}) %collective-permute-start.5) | collective-permute-done | bytes 65568 | tf_op jit(solution)/shard_map/ppermute | solution.py:129
  18.7 0.4 collective-permute-start.11
  19.7 0.7 %collective-permute-done.11.p_in = bf16[1024,128]{1,0:T(8,128)(2,1)S(1)} collective-permute-done((bf16[1024,128]{1,0:T(8,128)(2,1)S(1)}, bf16[1024,128]{1,0:T(8,128)(2,1)S(1)}, u32[]{:S(2)}, u32[]{:S(2)}) %collective-permute-start.11) | collective-permute-done | bytes 262176 | tf_op jit(solution)/shard_map/ppermute | solution.py:129
  21.1 0.4 collective-permute-start.14
  22.1 0.7 %collective-permute-start.17 = (bf16[1024,128]{1,0:T(8,128)(2,1)S(1)}, bf16[1024,128]{1,0:T(8,128)(2,1)S(1)}, u32[]{:S(2)}, u32[]{:S(2)}) collective-permute-start(bf16[1024,128]{1,0:T(8,128)(2,1)S(1)} %get-tuple-element.35.refs_4_), channel_id=1, source_target_pairs={{14,30},{16,24},{20,28},{17,25},{13,21},{9,1}} | collective-permute-start | bytes 786440 | tf_op jit(solution)/shard_map/ppermute | solution.py:133
  22.7 0.7 %collective-permute-start.18 = (bf16[1024,128]{1,0:T(8,128)(2,1)S(1)}, bf16[1024,128]{1,0:T(8,128)(2,1)S(1)}, u32[]{:S(2)}, u32[]{:S(2)}) collective-permute-start(bf16[1024,128]{1,0:T(8,128)(2,1)S(1)} %get-tuple-element.35.refs_4_), channel_id=1, source_target_pairs={{14,22},{17,29},{13,5}} | collective-permute-start | bytes 786440 | tf_op jit(solution)/shard_map/ppermute | solution.py:133
  23.5 0.7 %collective-permute-start.19 = (bf16[1024,128]{1,0:T(8,128)(2,1)S(1)}, bf16[1024,128]{1,0:T(8,128)(2,1)S(1)}, u32[]{:S(2)}, u32[]{:S(2)}) collective-permute-start(bf16[1024,128]{1,0:T(8,128)(2,1)S(1)} %step3_kernel.1.q_prev), channel_id=1, source_target_pairs={{23,27},{10,26}} | collective-permute-start | bytes 786440 | tf_op jit(solution)/shard_map/ppermute | solution.py:133
  24.2 0.7 %collective-permute-start.20 = (bf16[1024,128]{1,0:T(8,128)(2,1)S(1)}, bf16[1024,128]{1,0:T(8,128)(2,1)S(1)}, u32[]{:S(2)}, u32[]{:S(2)}) collective-permute-start(bf16[1024,128]{1,0:T(8,128)(2,1)S(1)} %step3_kernel.1.q_prev), channel_id=1, source_target_pairs={{23,31},{10,18}} | collective-permute-start | bytes 786440 | tf_op jit(solution)/shard_map/ppermute | solution.py:133
  24.9 0.7 %collective-permute-start.21 = (bf16[1024,128]{1,0:T(8,128)(2,1)S(1)}, bf16[1024,128]{1,0:T(8,128)(2,1)S(1)}, u32[]{:S(2)}, u32[]{:S(2)}) collective-permute-start(bf16[1024,128]{1,0:T(8,128)(2,1)S(1)} %step3_kernel.1.q_prev), channel_id=1, source_target_pairs={{23,19}} | collective-permute-start | bytes 786440 | tf_op jit(solution)/shard_map/ppermute | solution.py:133
  25.7 23.5 %collective-permute-start.22 = (bf16[1040,128]{1,0:T(8,128)(2,1)S(1)}, bf16[1040,128]{1,0:T(8,128)(2,1)S(1)}, u32[]{:S(2)}, u32[]{:S(2)}) collective-permute-start(bf16[1040,128]{1,0:T(8,128)(2,1)S(1)} %get-tuple-element.37.mine_ref), channel_id=1, source_target_pairs={{0,2},{1,3},{2,0},{3,1},{4,6},{5,7},{6,4},{7,5},{8,10},{9,11},{10,... | collective-permute-start | bytes 798728 | tf_op jit(solution)/shard_map/ppermute | solution.py:129
  49.2 1.3 %collective-permute-start.23 = (bf16[1024,128]{1,0:T(8,128)(2,1)S(1)}, bf16[1024,128]{1,0:T(8,128)(2,1)S(1)}, u32[]{:S(2)}, u32[]{:S(2)}) collective-permute-start(bf16[1024,128]{1,0:T(8,128)(2,1)S(1)} %get-tuple-element.36.q_ref), channel_id=1, source_target_pairs={{19,11},{23,15},{27,3},{31,7},{10,2},{14,6}} | collective-permute-start | bytes 786440 | tf_op jit(solution)/shard_map/ppermute | solution.py:133
  50.6 10.3 %collective-permute-done.23.rest_ref = bf16[1024,128]{1,0:T(8,128)(2,1)S(1)} collective-permute-done((bf16[1024,128]{1,0:T(8,128)(2,1)S(1)}, bf16[1024,128]{1,0:T(8,128)(2,1)S(1)}, u32[]{:S(2)}, u32[]{:S(2)}) %collective-permute-start.23) | collective-permute-done | bytes 262176 | tf_op jit(solution)/shard_map/ppermute | solution.py:133
  60.9 0.8 %half_kernel.1 = (f32[1024,128]{1,0:T(8,128)}, f32[2,1024,128]{2,1,0:T(8,128)S(1)}) custom-call(bf16[1024,128]{1,0:T(8,128)(2,1)S(1)} %get-tuple-element.36.q_ref, bf16[1024,128]{1,0:T(8,128)(2,1)S(1)} %collective-permute-done.23.rest_ref, f32[2,1024,128]{2,1,0:T(8,128)S(1)} %bitcast.14, bf16[1040,128]{1,0:T(8,128)(2,1)S(1)} %get-tuple-element.37.mine_ref, ...), custom_call_target="tpu_custom_call" | custom-call | tf_op jit(solution)/shard_map/half_kernel/pallas_call | solution.py:156
  61.8 0.7 %collective-permute-done.25.corner_ref = bf16[1040,128]{1,0:T(8,128)(2,1)S(1)} collective-permute-done((bf16[1040,128]{1,0:T(8,128)(2,1)S(1)}, bf16[1040,128]{1,0:T(8,128)(2,1)S(1)}, u32[]{:S(2)}, u32[]{:S(2)}) %collective-permute-start.25) | collective-permute-done | bytes 266272 | tf_op jit(solution)/shard_map/ppermute | solution.py:129
  62.5 1.2 %final_kernel.1 = f32[2,1024,128]{2,1,0:T(8,128)} custom-call(f32[2,1024,128]{2,1,0:T(8,128)S(1)} %get-tuple-element.41.half_ref, bf16[1040,128]{1,0:T(8,128)(2,1)S(1)} %collective-permute-done.24.beside_ref, bf16[1040,128]{1,0:T(8,128)(2,1)S(1)} %collective-permute-done.25.corner_ref), custom_call_target="tpu_custom_call" | custom-call | tf_op jit(solution)/shard_map/final_kernel/pallas_call | solution.py:156
  (48 shorter events, 3.4 us)
Async XLA Ops:
  2.0 10.3 %collective-permute-start.3 = (bf16[128,1024]{1,0:T(8,128)(2,1)S(1)}, bf16[128,1024]{1,0:T(8,128)(2,1)S(1)}, u32[]{:S(2)}, u32[]{:S(2)}) collective-permute-start(bf16[128,1024]{1,0:T(8,128)(2,1)S(1)} %get-tuple-element.25), channel_id=1, source_target_pairs={{24,1},{25,22},{26,13},{27,15},{28,9},{29,23},{30,3},{31,14}} | collective-permute-start | bytes 786440 | tf_op jit(solution)/shard_map/ppermute | solution.py:133
  2.8 9.5 %collective-permute-start.2 = (bf16[128,768]{1,0:T(8,128)(2,1)S(1)}, bf16[128,768]{1,0:T(8,128)(2,1)S(1)}, u32[]{:S(2)}, u32[]{:S(2)}) collective-permute-start(bf16[128,768]{1,0:T(8,128)(2,1)S(1)} %get-tuple-element.24), channel_id=1, source_target_pairs={{16,0},{17,13},{18,22},{19,15},{20,14},{21,9},{23,2}} | collective-permute-start | bytes 589832 | tf_op jit(solution)/shard_map/ppermute | solution.py:133
  3.6 8.6 %collective-permute-start.1 = (bf16[128,512]{1,0:T(8,128)(2,1)S(1)}, bf16[128,512]{1,0:T(8,128)(2,1)S(1)}, u32[]{:S(2)}, u32[]{:S(2)}) collective-permute-start(bf16[128,512]{1,0:T(8,128)(2,1)S(1)} %get-tuple-element.23), channel_id=1, source_target_pairs={{4,0},{8,22},{10,2},{11,15},{12,1},{13,9},{14,23}} | collective-permute-start | bytes 393224 | tf_op jit(solution)/shard_map/ppermute | solution.py:133
  4.3 8.0 %collective-permute-start = (bf16[128,256]{1,0:T(8,128)(2,1)S(1)}, bf16[128,256]{1,0:T(8,128)(2,1)S(1)}, u32[]{:S(2)}, u32[]{:S(2)}) collective-permute-start(bf16[128,256]{1,0:T(8,128)(2,1)S(1)} %get-tuple-element.22), channel_id=1, source_target_pairs={{1,13},{2,15},{3,22},{5,9},{6,14},{7,23}} | collective-permute-start | bytes 196616 | tf_op jit(solution)/shard_map/ppermute | solution.py:133
  12.3 6.1 %collective-permute-start.4 = (bf16[128,2560]{1,0:T(8,128)(2,1)S(1)}, bf16[128,2560]{1,0:T(8,128)(2,1)S(1)}, u32[]{:S(2)}, u32[]{:S(2)}) collective-permute-start(bf16[128,2560]{1,0:T(8,128)(2,1)S(1)} %pack_kernel.1), channel_id=1, source_target_pairs={{0,1},{1,0},{2,3},{3,2},{4,5},{5,4},{6,7},{7,6},{8,12},{9,8},{10,1... | collective-permute-start | bytes 1966088 | tf_op jit(solution)/shard_map/ppermute | solution.py:129
  14.6 1.8 %collective-permute-start.5 = (bf16[256,128]{1,0:T(8,128)(2,1)S(1)}, bf16[256,128]{1,0:T(8,128)(2,1)S(1)}, u32[]{:S(2)}, u32[]{:S(2)}) collective-permute-start(bf16[256,128]{1,0:T(8,128)(2,1)S(1)} %first_kernel.1), channel_id=1, source_target_pairs={{0,4},{1,8},{2,12},{3,2},{4,5},{5,0},{6,7},{7,6},{8,9},{9,1},{10,1... | collective-permute-start | bytes 196616 | tf_op jit(solution)/shard_map/ppermute | solution.py:129
  14.7 1.7 %collective-permute-start.6 = (bf16[256,128]{1,0:T(8,128)(2,1)S(1)}, bf16[256,128]{1,0:T(8,128)(2,1)S(1)}, u32[]{:S(2)}, u32[]{:S(2)}) collective-permute-start(bf16[256,128]{1,0:T(8,128)(2,1)S(1)} %first_kernel.1), channel_id=1, source_target_pairs={{0,8},{1,12},{2,3},{3,4},{4,5},{5,0},{6,7},{7,6},{8,9},{9,1},{10,1... | collective-permute-start | bytes 196616 | tf_op jit(solution)/shard_map/ppermute | solution.py:129
  15.2 1.4 %collective-permute-start.7 = (bf16[256,128]{1,0:T(8,128)(2,1)S(1)}, bf16[256,128]{1,0:T(8,128)(2,1)S(1)}, u32[]{:S(2)}, u32[]{:S(2)}) collective-permute-start(bf16[256,128]{1,0:T(8,128)(2,1)S(1)} %first_kernel.1), channel_id=1, source_target_pairs={{0,12},{1,0},{2,4},{3,8},{4,5},{5,1},{6,7},{7,6},{8,9},{9,2},{10,1... | collective-permute-start | bytes 196616 | tf_op jit(solution)/shard_map/ppermute | solution.py:129
  15.3 1.4 %collective-permute-start.8 = (bf16[256,128]{1,0:T(8,128)(2,1)S(1)}, bf16[256,128]{1,0:T(8,128)(2,1)S(1)}, u32[]{:S(2)}, u32[]{:S(2)}) collective-permute-start(bf16[256,128]{1,0:T(8,128)(2,1)S(1)} %first_kernel.1), channel_id=1, source_target_pairs={{0,1},{1,4},{2,8},{3,12},{4,5},{5,0},{6,7},{7,6},{8,9},{9,2},{10,1... | collective-permute-start | bytes 196616 | tf_op jit(solution)/shard_map/ppermute | solution.py:129
  16.7 1.9 %collective-permute-start.9 = (bf16[1024,128]{1,0:T(8,128)(2,1)S(1)}, bf16[1024,128]{1,0:T(8,128)(2,1)S(1)}, u32[]{:S(2)}, u32[]{:S(2)}) collective-permute-start(bf16[1024,128]{1,0:T(8,128)(2,1)S(1)} %get-tuple-element.27), channel_id=1, source_target_pairs={{0,1},{1,0},{2,3},{3,2},{4,9},{5,4},{6,7},{7,6},{8,5},{9,8},{10,11... | collective-permute-start | bytes 786440 | tf_op jit(solution)/shard_map/ppermute | solution.py:129
  17.1 1.6 %collective-permute-start.10 = (bf16[1024,128]{1,0:T(8,128)(2,1)S(1)}, bf16[1024,128]{1,0:T(8,128)(2,1)S(1)}, u32[]{:S(2)}, u32[]{:S(2)}) collective-permute-start(bf16[1024,128]{1,0:T(8,128)(2,1)S(1)} %get-tuple-element.30.s_prev), channel_id=1, source_target_pairs={{0,1},{1,0},{2,3},{3,2},{4,5},{5,4},{6,7},{7,6},{8,9},{9,8},{10,11... | collective-permute-start | bytes 786440 | tf_op jit(solution)/shard_map/ppermute | solution.py:129
  18.7 1.6 %collective-permute-start.11 = (bf16[1024,128]{1,0:T(8,128)(2,1)S(1)}, bf16[1024,128]{1,0:T(8,128)(2,1)S(1)}, u32[]{:S(2)}, u32[]{:S(2)}) collective-permute-start(bf16[1024,128]{1,0:T(8,128)(2,1)S(1)} %get-tuple-element.31), channel_id=1, source_target_pairs={{0,1},{1,0},{2,3},{3,2},{4,5},{5,4},{6,7},{7,6},{8,9},{9,14},{10,1... | collective-permute-start | bytes 786440 | tf_op jit(solution)/shard_map/ppermute | solution.py:129
  19.2 1.5 %collective-permute-start.12 = (bf16[1024,128]{1,0:T(8,128)(2,1)S(1)}, bf16[1024,128]{1,0:T(8,128)(2,1)S(1)}, u32[]{:S(2)}, u32[]{:S(2)}) collective-permute-start(bf16[1024,128]{1,0:T(8,128)(2,1)S(1)} %step1_kernel.1.q_in.q_prev), channel_id=1, source_target_pairs={{0,1},{1,0},{2,3},{3,2},{4,5},{5,4},{6,7},{7,6},{8,9},{9,13},{10,1... | collective-permute-start | bytes 786440 | tf_op jit(solution)/shard_map/ppermute | solution.py:129
  19.3 1.8 %collective-permute-start.13 = (bf16[1024,128]{1,0:T(8,128)(2,1)S(1)}, bf16[1024,128]{1,0:T(8,128)(2,1)S(1)}, u32[]{:S(2)}, u32[]{:S(2)}) collective-permute-start(bf16[1024,128]{1,0:T(8,128)(2,1)S(1)} %step1_kernel.1.q_in.q_prev), channel_id=1, source_target_pairs={{0,1},{1,5},{2,3},{3,2},{4,0},{5,4},{6,7},{7,6},{8,16},{9,17},{10,... | collective-permute-start | bytes 786440 | tf_op jit(solution)/shard_map/ppermute | solution.py:129
  21.1 2.3 %collective-permute-start.14 = (bf16[1024,128]{1,0:T(8,128)(2,1)S(1)}, bf16[1024,128]{1,0:T(8,128)(2,1)S(1)}, u32[]{:S(2)}, u32[]{:S(2)}) collective-permute-start(bf16[1024,128]{1,0:T(8,128)(2,1)S(1)} %get-tuple-element.34), channel_id=1, source_target_pairs={{0,1},{1,0},{2,3},{3,2},{4,5},{5,4},{6,7},{7,6},{8,9},{9,8},{10,11... | collective-permute-start | bytes 786440 | tf_op jit(solution)/shard_map/ppermute | solution.py:129
  21.5 1.9 %collective-permute-start.15 = (bf16[1024,128]{1,0:T(8,128)(2,1)S(1)}, bf16[1024,128]{1,0:T(8,128)(2,1)S(1)}, u32[]{:S(2)}, u32[]{:S(2)}) collective-permute-start(bf16[1024,128]{1,0:T(8,128)(2,1)S(1)} %get-tuple-element.33.s_ref), channel_id=1, source_target_pairs={{0,1},{1,0},{2,3},{3,2},{4,5},{5,4},{6,7},{7,6},{8,9},{9,8},{10,11... | collective-permute-start | bytes 786440 | tf_op jit(solution)/shard_map/ppermute | solution.py:129
  21.7 1.8 %collective-permute-start.16 = (bf16[1024,128]{1,0:T(8,128)(2,1)S(1)}, bf16[1024,128]{1,0:T(8,128)(2,1)S(1)}, u32[]{:S(2)}, u32[]{:S(2)}) collective-permute-start(bf16[1024,128]{1,0:T(8,128)(2,1)S(1)} %get-tuple-element.35.refs_4_), channel_id=1, source_target_pairs={{0,1},{1,0},{2,3},{3,2},{4,5},{5,4},{6,7},{7,6},{8,9},{9,8},{10,11... | collective-permute-start | bytes 786440 | tf_op jit(solution)/shard_map/ppermute | solution.py:129
  22.1 1.4 %collective-permute-start.17 = (bf16[1024,128]{1,0:T(8,128)(2,1)S(1)}, bf16[1024,128]{1,0:T(8,128)(2,1)S(1)}, u32[]{:S(2)}, u32[]{:S(2)}) collective-permute-start(bf16[1024,128]{1,0:T(8,128)(2,1)S(1)} %get-tuple-element.35.refs_4_), channel_id=1, source_target_pairs={{14,30},{16,24},{20,28},{17,25},{13,21},{9,1}} | collective-permute-start | bytes 786440 | tf_op jit(solution)/shard_map/ppermute | solution.py:133
  23.5 2.1 %collective-permute-start.19 = (bf16[1024,128]{1,0:T(8,128)(2,1)S(1)}, bf16[1024,128]{1,0:T(8,128)(2,1)S(1)}, u32[]{:S(2)}, u32[]{:S(2)}) collective-permute-start(bf16[1024,128]{1,0:T(8,128)(2,1)S(1)} %step3_kernel.1.q_prev), channel_id=1, source_target_pairs={{23,27},{10,26}} | collective-permute-start | bytes 786440 | tf_op jit(solution)/shard_map/ppermute | solution.py:133
  24.2 1.4 %collective-permute-start.20 = (bf16[1024,128]{1,0:T(8,128)(2,1)S(1)}, bf16[1024,128]{1,0:T(8,128)(2,1)S(1)}, u32[]{:S(2)}, u32[]{:S(2)}) collective-permute-start(bf16[1024,128]{1,0:T(8,128)(2,1)S(1)} %step3_kernel.1.q_prev), channel_id=1, source_target_pairs={{23,31},{10,18}} | collective-permute-start | bytes 786440 | tf_op jit(solution)/shard_map/ppermute | solution.py:133
  25.7 35.2 %collective-permute-start.22 = (bf16[1040,128]{1,0:T(8,128)(2,1)S(1)}, bf16[1040,128]{1,0:T(8,128)(2,1)S(1)}, u32[]{:S(2)}, u32[]{:S(2)}) collective-permute-start(bf16[1040,128]{1,0:T(8,128)(2,1)S(1)} %get-tuple-element.37.mine_ref), channel_id=1, source_target_pairs={{0,2},{1,3},{2,0},{3,1},{4,6},{5,7},{6,4},{7,5},{8,10},{9,11},{10,... | collective-permute-start | bytes 798728 | tf_op jit(solution)/shard_map/ppermute | solution.py:129
  49.2 11.7 %collective-permute-start.23 = (bf16[1024,128]{1,0:T(8,128)(2,1)S(1)}, bf16[1024,128]{1,0:T(8,128)(2,1)S(1)}, u32[]{:S(2)}, u32[]{:S(2)}) collective-permute-start(bf16[1024,128]{1,0:T(8,128)(2,1)S(1)} %get-tuple-element.36.q_ref), channel_id=1, source_target_pairs={{19,11},{23,15},{27,3},{31,7},{10,2},{14,6}} | collective-permute-start | bytes 786440 | tf_op jit(solution)/shard_map/ppermute | solution.py:133
  50.5 11.3 %collective-permute-start.24 = (bf16[1040,128]{1,0:T(8,128)(2,1)S(1)}, bf16[1040,128]{1,0:T(8,128)(2,1)S(1)}, u32[]{:S(2)}, u32[]{:S(2)}) collective-permute-start(bf16[1040,128]{1,0:T(8,128)(2,1)S(1)} %get-tuple-element.37.mine_ref), channel_id=1, source_target_pairs={{0,1},{1,0},{2,3},{3,2},{4,5},{5,4},{6,7},{7,6},{8,9},{9,8},{10,11... | collective-permute-start | bytes 798728 | tf_op jit(solution)/shard_map/ppermute | solution.py:129
  60.9 1.5 %collective-permute-start.25 = (bf16[1040,128]{1,0:T(8,128)(2,1)S(1)}, bf16[1040,128]{1,0:T(8,128)(2,1)S(1)}, u32[]{:S(2)}, u32[]{:S(2)}) collective-permute-start(bf16[1040,128]{1,0:T(8,128)(2,1)S(1)} %collective-permute-done.22.across_ref), channel_id=1, source_target_pairs={{0,1},{1,0},{2,3},{3,2},{4,5},{5,4},{6,7},{7,6},{8,9},{9,8},{10,11... | collective-permute-start | bytes 798728 | tf_op jit(solution)/shard_map/ppermute | solution.py:129
  (6 other events, 44.0 us)

commit v19 on v18

--- a/solution.py
+++ b/solution.py
@@ -78,7 +78,7 @@
     (0, 3, 1, 2),
     (1, 3, 0, 2),
 )
-REST = ((2, 3), (3, 3), (0, 3), (1, 3), (0, 2), (1, 2))
+REST = ((2, 3), (1, 3), (0, 3), (1, 2))
 
 
 def hops(a, b):
@@ -520,7 +520,7 @@
     sends = [
         [(MAKER[2], (2, 2))],
         [(MAKER[2], (7, 2)), ((4, 0), (6, 0)), ((5, 0), (7, 0)), ((4, 1), (6, 1)), ((3, 1), (5, 1)), ((2, 1), (0, 1))],
-        [(MAKER[2], (5, 2)), ((4, 1), (7, 1)), ((3, 1), (1, 1))],
+        [(MAKER[2], (5, 2)), ((3, 1), (7, 1)), ((2, 1), (1, 1))],
     ]
     got = [send(q, sends[0])] + [send_only(q, pairs) for pairs in sends[1:]]
     q = call(
@@ -533,9 +533,10 @@
     )
 
     sends = [
-        [(MAKER[3], (6, 3)), ((2, 2), (6, 2))],
-        [(MAKER[3], (7, 3)), ((2, 2), (4, 2))],
-        [(MAKER[3], (4, 3))],
+        [(MAKER[3], (6, 3)), ((2, 2), (4, 2))],
+        [(MAKER[3], (7, 3)), ((2, 2), (6, 2))],
+        [(MAKER[3], (4, 3)), ((2, 2), (0, 2))],
+        [(MAKER[3], (3, 3))],
     ]
     got = [send_only(q, pairs) for pairs in sends]
     takers = [[b for _, b in pairs] for pairs in sends]
@@ -551,7 +552,7 @@
         return send(value, [((r, c), (r, c ^ step)) for r in range(NR) for c in range(NC)])
 
     across = swap(mine, 2)
-    rest = send_only(q, list(zip(((4, 3), (5, 3), (6, 3), (7, 3), (2, 2), MAKER[2]), REST)))
+    rest = send_only(q, list(zip(((3, 3), MAKER[3], (6, 3), MAKER[2]), REST)))
     beside = swap(mine, 1)
     across, rest = lax.optimization_barrier((across, rest))
     corner = swap(across, 1)

time: 63.9 us -> 64.9 us (1.016)
  starting transfers between devices: 42.9 us -> 45.9 us
  waiting for transfers between devices: 14.8 us -> 12.4 us
    ppermute x16, starting transfers between devices: 29.3 us -> 31.7 us  [send(): lax.ppermute(value, ('row', 'col'), [(a * NC + b, c * NC + d) for (a, b),...]
    ppermute x10 -> x11, waiting for transfers between devices: 11.7 us -> 9.35 us  [send_only(): lax.ppermute(value, ('row', 'col'), [(a * NC + b, c * NC + d) for (a, b),...]
    ppermute x10 -> x11, starting transfers between devices: 13.6 us -> 14.3 us  [send_only(): lax.ppermute(value, ('row', 'col'), [(a * NC + b, c * NC + d) for (a, b),...]
  transfers between devices with their start and end apart: 26 -> 27, of which waited for: 10 -> 10; matrix products, arithmetic and copies ran while one was open for 0% -> 0% of each run, Pallas kernels for 2% -> 2%
where the time goes in v19:
time: 64.9 us; the launch traced here: 64.4 us
  starting transfers between devices  45.9 us (71%)
  waiting for transfers between devices  12.4 us (19%)
  Pallas kernels  2.51 us (4%)
  between operations  2.21 us (3%)
  local copies, waits for them, and re-layouts  1.32 us (2%)
    ppermute x16, starting transfers between devices, send(): lax.ppermute(value, ('row', 'col'), [(a * NC + b, c * NC + d) for (a, b),...  31.7 us
    ppermute x11, starting transfers between devices, send_only(): lax.ppermute(value, ('row', 'col'), [(a * NC + b, c * NC + d) for (a, b),...  14.3 us
    ppermute x11, waiting for transfers between devices, send_only(): lax.ppermute(value, ('row', 'col'), [(a * NC + b, c * NC + d) for (a, b),...  9.35 us
    ppermute x16, waiting for transfers between devices, send(): lax.ppermute(value, ('row', 'col'), [(a * NC + b, c * NC + d) for (a, b),...  3.08 us
    pallas_call x12, Pallas kernels, call(): pl.pallas_call(kernel, out_shape=outs, in_specs=in_specs, out_specs=out_s...  2.51 us
    unnamed x8, local copies, waits for them, and re-layouts  1.32 us
  transfers between devices with their start and end apart: 27, of which 10 were waited for; matrix products, arithmetic and copies ran while one was open for 0% of the time, Pallas kernels for 2%

profile of v19, /device:TPU:7, one launch (start us, length us, event | category | flops | bytes accessed | tf_op | source)
XLA Modules:
  0.0 64.4 jit_solution(13358492186077468934)
XLA Ops:
  0.6 1.3 %copy-done.2 = bf16[4,128,1024]{2,1,0:T(8,128)(2,1)S(1)} copy-done((bf16[4,128,1024]{2,1,0:T(8,128)(2,1)S(1)}, bf16[4,128,1024]{2,1,0:T(8,128)(2,1)}, u32[]{:S(2)}) %copy-start.2) | copy-done | bytes 1048600
  2.0 0.8 %collective-permute-start.3 = (bf16[128,1024]{1,0:T(8,128)(2,1)S(1)}, bf16[128,1024]{1,0:T(8,128)(2,1)S(1)}, u32[]{:S(2)}, u32[]{:S(2)}) collective-permute-start(bf16[128,1024]{1,0:T(8,128)(2,1)S(1)} %get-tuple-element.25), channel_id=1, source_target_pairs={{24,1},{25,22},{26,13},{27,15},{28,9},{29,23},{30,3},{31,14}} | collective-permute-start | bytes 786440 | tf_op jit(solution)/shard_map/ppermute | solution.py:133
  2.8 0.8 %collective-permute-start.2 = (bf16[128,768]{1,0:T(8,128)(2,1)S(1)}, bf16[128,768]{1,0:T(8,128)(2,1)S(1)}, u32[]{:S(2)}, u32[]{:S(2)}) collective-permute-start(bf16[128,768]{1,0:T(8,128)(2,1)S(1)} %get-tuple-element.24), channel_id=1, source_target_pairs={{16,0},{17,13},{18,22},{19,15},{20,14},{21,9},{23,2}} | collective-permute-start | bytes 589832 | tf_op jit(solution)/shard_map/ppermute | solution.py:133
  3.6 0.7 %collective-permute-start.1 = (bf16[128,512]{1,0:T(8,128)(2,1)S(1)}, bf16[128,512]{1,0:T(8,128)(2,1)S(1)}, u32[]{:S(2)}, u32[]{:S(2)}) collective-permute-start(bf16[128,512]{1,0:T(8,128)(2,1)S(1)} %get-tuple-element.23), channel_id=1, source_target_pairs={{4,0},{8,22},{10,2},{11,15},{12,1},{13,9},{14,23}} | collective-permute-start | bytes 393224 | tf_op jit(solution)/shard_map/ppermute | solution.py:133
  4.3 6.6 %collective-permute-start = (bf16[128,256]{1,0:T(8,128)(2,1)S(1)}, bf16[128,256]{1,0:T(8,128)(2,1)S(1)}, u32[]{:S(2)}, u32[]{:S(2)}) collective-permute-start(bf16[128,256]{1,0:T(8,128)(2,1)S(1)} %get-tuple-element.22), channel_id=1, source_target_pairs={{1,13},{2,15},{3,22},{5,9},{6,14},{7,23}} | collective-permute-start | bytes 196616 | tf_op jit(solution)/shard_map/ppermute | solution.py:133
  11.0 1.3 %collective-permute-done.refs_0_ = bf16[128,256]{1,0:T(8,128)(2,1)S(1)} collective-permute-done((bf16[128,256]{1,0:T(8,128)(2,1)S(1)}, bf16[128,256]{1,0:T(8,128)(2,1)S(1)}, u32[]{:S(2)}, u32[]{:S(2)}) %collective-permute-start) | collective-permute-done | bytes 65568 | tf_op jit(solution)/shard_map/ppermute | solution.py:133
  12.3 2.2 %collective-permute-start.4 = (bf16[128,2560]{1,0:T(8,128)(2,1)S(1)}, bf16[128,2560]{1,0:T(8,128)(2,1)S(1)}, u32[]{:S(2)}, u32[]{:S(2)}) collective-permute-start(bf16[128,2560]{1,0:T(8,128)(2,1)S(1)} %pack_kernel.1), channel_id=1, source_target_pairs={{0,1},{1,0},{2,3},{3,2},{4,5},{5,4},{6,7},{7,6},{8,12},{9,8},{10,1... | collective-permute-start | bytes 1966088 | tf_op jit(solution)/shard_map/ppermute | solution.py:129
  14.7 0.5 collective-permute-start.6
  15.7 0.7 %collective-permute-done.5.g0 = bf16[256,128]{1,0:T(8,128)(2,1)S(1)} collective-permute-done((bf16[256,128]{1,0:T(8,128)(2,1)S(1)}, bf16[256,128]{1,0:T(8,128)(2,1)S(1)}, u32[]{:S(2)}, u32[]{:S(2)}) %collective-permute-start.5) | collective-permute-done | bytes 65568 | tf_op jit(solution)/shard_map/ppermute | solution.py:129
  18.7 0.4 collective-permute-start.11
  19.7 0.7 %collective-permute-done.11.p_in = bf16[1024,128]{1,0:T(8,128)(2,1)S(1)} collective-permute-done((bf16[1024,128]{1,0:T(8,128)(2,1)S(1)}, bf16[1024,128]{1,0:T(8,128)(2,1)S(1)}, u32[]{:S(2)}, u32[]{:S(2)}) %collective-permute-start.11) | collective-permute-done | bytes 262176 | tf_op jit(solution)/shard_map/ppermute | solution.py:129
  21.1 0.4 collective-permute-start.14
  22.1 0.7 %collective-permute-start.17 = (bf16[1024,128]{1,0:T(8,128)(2,1)S(1)}, bf16[1024,128]{1,0:T(8,128)(2,1)S(1)}, u32[]{:S(2)}, u32[]{:S(2)}) collective-permute-start(bf16[1024,128]{1,0:T(8,128)(2,1)S(1)} %get-tuple-element.35.refs_4_), channel_id=1, source_target_pairs={{14,30},{16,24},{20,28},{17,25},{13,21},{9,1}} | collective-permute-start | bytes 786440 | tf_op jit(solution)/shard_map/ppermute | solution.py:133
  22.7 0.7 %collective-permute-start.18 = (bf16[1024,128]{1,0:T(8,128)(2,1)S(1)}, bf16[1024,128]{1,0:T(8,128)(2,1)S(1)}, u32[]{:S(2)}, u32[]{:S(2)}) collective-permute-start(bf16[1024,128]{1,0:T(8,128)(2,1)S(1)} %get-tuple-element.35.refs_4_), channel_id=1, source_target_pairs={{14,22},{13,29},{9,5}} | collective-permute-start | bytes 786440 | tf_op jit(solution)/shard_map/ppermute | solution.py:133
  23.5 0.7 %collective-permute-start.19 = (bf16[1024,128]{1,0:T(8,128)(2,1)S(1)}, bf16[1024,128]{1,0:T(8,128)(2,1)S(1)}, u32[]{:S(2)}, u32[]{:S(2)}) collective-permute-start(bf16[1024,128]{1,0:T(8,128)(2,1)S(1)} %step3_kernel.1.q_prev), channel_id=1, source_target_pairs={{23,27},{10,18}} | collective-permute-start | bytes 786440 | tf_op jit(solution)/shard_map/ppermute | solution.py:133
  24.2 0.7 %collective-permute-start.20 = (bf16[1024,128]{1,0:T(8,128)(2,1)S(1)}, bf16[1024,128]{1,0:T(8,128)(2,1)S(1)}, u32[]{:S(2)}, u32[]{:S(2)}) collective-permute-start(bf16[1024,128]{1,0:T(8,128)(2,1)S(1)} %step3_kernel.1.q_prev), channel_id=1, source_target_pairs={{23,31},{10,26}} | collective-permute-start | bytes 786440 | tf_op jit(solution)/shard_map/ppermute | solution.py:133
  24.9 0.7 %collective-permute-start.21 = (bf16[1024,128]{1,0:T(8,128)(2,1)S(1)}, bf16[1024,128]{1,0:T(8,128)(2,1)S(1)}, u32[]{:S(2)}, u32[]{:S(2)}) collective-permute-start(bf16[1024,128]{1,0:T(8,128)(2,1)S(1)} %step3_kernel.1.q_prev), channel_id=1, source_target_pairs={{23,19},{10,2}} | collective-permute-start | bytes 786440 | tf_op jit(solution)/shard_map/ppermute | solution.py:133
  25.6 0.7 %collective-permute-start.22 = (bf16[1024,128]{1,0:T(8,128)(2,1)S(1)}, bf16[1024,128]{1,0:T(8,128)(2,1)S(1)}, u32[]{:S(2)}, u32[]{:S(2)}) collective-permute-start(bf16[1024,128]{1,0:T(8,128)(2,1)S(1)} %step3_kernel.1.q_prev), channel_id=1, source_target_pairs={{23,15}} | collective-permute-start | bytes 786440 | tf_op jit(solution)/shard_map/ppermute | solution.py:133
  26.4 25.9 %collective-permute-start.23 = (bf16[1040,128]{1,0:T(8,128)(2,1)S(1)}, bf16[1040,128]{1,0:T(8,128)(2,1)S(1)}, u32[]{:S(2)}, u32[]{:S(2)}) collective-permute-start(bf16[1040,128]{1,0:T(8,128)(2,1)S(1)} %get-tuple-element.37.mine_ref), channel_id=1, source_target_pairs={{0,2},{1,3},{2,0},{3,1},{4,6},{5,7},{6,4},{7,5},{8,10},{9,11},{10,... | collective-permute-start | bytes 798728 | tf_op jit(solution)/shard_map/ppermute | solution.py:129
  52.3 1.3 %collective-permute-start.24 = (bf16[1024,128]{1,0:T(8,128)(2,1)S(1)}, bf16[1024,128]{1,0:T(8,128)(2,1)S(1)}, u32[]{:S(2)}, u32[]{:S(2)}) collective-permute-start(bf16[1024,128]{1,0:T(8,128)(2,1)S(1)} %get-tuple-element.36.q_ref), channel_id=1, source_target_pairs={{15,11},{23,7},{27,3},{14,6}} | collective-permute-start | bytes 786440 | tf_op jit(solution)/shard_map/ppermute | solution.py:133
  53.7 8.0 %collective-permute-done.24.rest_ref = bf16[1024,128]{1,0:T(8,128)(2,1)S(1)} collective-permute-done((bf16[1024,128]{1,0:T(8,128)(2,1)S(1)}, bf16[1024,128]{1,0:T(8,128)(2,1)S(1)}, u32[]{:S(2)}, u32[]{:S(2)}) %collective-permute-start.24) | collective-permute-done | bytes 262176 | tf_op jit(solution)/shard_map/ppermute | solution.py:133
  61.7 0.8 %half_kernel.1 = (f32[1024,128]{1,0:T(8,128)}, f32[2,1024,128]{2,1,0:T(8,128)S(1)}) custom-call(bf16[1024,128]{1,0:T(8,128)(2,1)S(1)} %get-tuple-element.36.q_ref, bf16[1024,128]{1,0:T(8,128)(2,1)S(1)} %collective-permute-done.24.rest_ref, f32[2,1024,128]{2,1,0:T(8,128)S(1)} %bitcast.14, bf16[1040,128]{1,0:T(8,128)(2,1)S(1)} %get-tuple-element.37.mine_ref, ...), custom_call_target="tpu_custom_call" | custom-call | tf_op jit(solution)/shard_map/half_kernel/pallas_call | solution.py:156
  62.5 0.7 %collective-permute-done.26.corner_ref = bf16[1040,128]{1,0:T(8,128)(2,1)S(1)} collective-permute-done((bf16[1040,128]{1,0:T(8,128)(2,1)S(1)}, bf16[1040,128]{1,0:T(8,128)(2,1)S(1)}, u32[]{:S(2)}, u32[]{:S(2)}) %collective-permute-start.26) | collective-permute-done | bytes 266272 | tf_op jit(solution)/shard_map/ppermute | solution.py:129
  63.2 1.2 %final_kernel.1 = f32[2,1024,128]{2,1,0:T(8,128)} custom-call(f32[2,1024,128]{2,1,0:T(8,128)S(1)} %get-tuple-element.41.half_ref, bf16[1040,128]{1,0:T(8,128)(2,1)S(1)} %collective-permute-done.25.beside_ref, bf16[1040,128]{1,0:T(8,128)(2,1)S(1)} %collective-permute-done.26.corner_ref), custom_call_target="tpu_custom_call" | custom-call | tf_op jit(solution)/shard_map/final_kernel/pallas_call | solution.py:156
  (50 shorter events, 3.8 us)
Async XLA Ops:
  2.0 10.3 %collective-permute-start.3 = (bf16[128,1024]{1,0:T(8,128)(2,1)S(1)}, bf16[128,1024]{1,0:T(8,128)(2,1)S(1)}, u32[]{:S(2)}, u32[]{:S(2)}) collective-permute-start(bf16[128,1024]{1,0:T(8,128)(2,1)S(1)} %get-tuple-element.25), channel_id=1, source_target_pairs={{24,1},{25,22},{26,13},{27,15},{28,9},{29,23},{30,3},{31,14}} | collective-permute-start | bytes 786440 | tf_op jit(solution)/shard_map/ppermute | solution.py:133
  2.8 9.5 %collective-permute-start.2 = (bf16[128,768]{1,0:T(8,128)(2,1)S(1)}, bf16[128,768]{1,0:T(8,128)(2,1)S(1)}, u32[]{:S(2)}, u32[]{:S(2)}) collective-permute-start(bf16[128,768]{1,0:T(8,128)(2,1)S(1)} %get-tuple-element.24), channel_id=1, source_target_pairs={{16,0},{17,13},{18,22},{19,15},{20,14},{21,9},{23,2}} | collective-permute-start | bytes 589832 | tf_op jit(solution)/shard_map/ppermute | solution.py:133
  3.6 8.6 %collective-permute-start.1 = (bf16[128,512]{1,0:T(8,128)(2,1)S(1)}, bf16[128,512]{1,0:T(8,128)(2,1)S(1)}, u32[]{:S(2)}, u32[]{:S(2)}) collective-permute-start(bf16[128,512]{1,0:T(8,128)(2,1)S(1)} %get-tuple-element.23), channel_id=1, source_target_pairs={{4,0},{8,22},{10,2},{11,15},{12,1},{13,9},{14,23}} | collective-permute-start | bytes 393224 | tf_op jit(solution)/shard_map/ppermute | solution.py:133
  4.3 8.0 %collective-permute-start = (bf16[128,256]{1,0:T(8,128)(2,1)S(1)}, bf16[128,256]{1,0:T(8,128)(2,1)S(1)}, u32[]{:S(2)}, u32[]{:S(2)}) collective-permute-start(bf16[128,256]{1,0:T(8,128)(2,1)S(1)} %get-tuple-element.22), channel_id=1, source_target_pairs={{1,13},{2,15},{3,22},{5,9},{6,14},{7,23}} | collective-permute-start | bytes 196616 | tf_op jit(solution)/shard_map/ppermute | solution.py:133
  12.3 6.1 %collective-permute-start.4 = (bf16[128,2560]{1,0:T(8,128)(2,1)S(1)}, bf16[128,2560]{1,0:T(8,128)(2,1)S(1)}, u32[]{:S(2)}, u32[]{:S(2)}) collective-permute-start(bf16[128,2560]{1,0:T(8,128)(2,1)S(1)} %pack_kernel.1), channel_id=1, source_target_pairs={{0,1},{1,0},{2,3},{3,2},{4,5},{5,4},{6,7},{7,6},{8,12},{9,8},{10,1... | collective-permute-start | bytes 1966088 | tf_op jit(solution)/shard_map/ppermute | solution.py:129
  14.6 1.8 %collective-permute-start.5 = (bf16[256,128]{1,0:T(8,128)(2,1)S(1)}, bf16[256,128]{1,0:T(8,128)(2,1)S(1)}, u32[]{:S(2)}, u32[]{:S(2)}) collective-permute-start(bf16[256,128]{1,0:T(8,128)(2,1)S(1)} %first_kernel.1), channel_id=1, source_target_pairs={{0,4},{1,8},{2,12},{3,2},{4,5},{5,0},{6,7},{7,6},{8,9},{9,1},{10,1... | collective-permute-start | bytes 196616 | tf_op jit(solution)/shard_map/ppermute | solution.py:129
  14.7 1.7 %collective-permute-start.6 = (bf16[256,128]{1,0:T(8,128)(2,1)S(1)}, bf16[256,128]{1,0:T(8,128)(2,1)S(1)}, u32[]{:S(2)}, u32[]{:S(2)}) collective-permute-start(bf16[256,128]{1,0:T(8,128)(2,1)S(1)} %first_kernel.1), channel_id=1, source_target_pairs={{0,8},{1,12},{2,3},{3,4},{4,5},{5,0},{6,7},{7,6},{8,9},{9,1},{10,1... | collective-permute-start | bytes 196616 | tf_op jit(solution)/shard_map/ppermute | solution.py:129
  15.2 1.4 %collective-permute-start.7 = (bf16[256,128]{1,0:T(8,128)(2,1)S(1)}, bf16[256,128]{1,0:T(8,128)(2,1)S(1)}, u32[]{:S(2)}, u32[]{:S(2)}) collective-permute-start(bf16[256,128]{1,0:T(8,128)(2,1)S(1)} %first_kernel.1), channel_id=1, source_target_pairs={{0,12},{1,0},{2,4},{3,8},{4,5},{5,1},{6,7},{7,6},{8,9},{9,2},{10,1... | collective-permute-start | bytes 196616 | tf_op jit(solution)/shard_map/ppermute | solution.py:129
  16.7 1.9 %collective-permute-start.9 = (bf16[1024,128]{1,0:T(8,128)(2,1)S(1)}, bf16[1024,128]{1,0:T(8,128)(2,1)S(1)}, u32[]{:S(2)}, u32[]{:S(2)}) collective-permute-start(bf16[1024,128]{1,0:T(8,128)(2,1)S(1)} %get-tuple-element.27), channel_id=1, source_target_pairs={{0,1},{1,0},{2,3},{3,2},{4,9},{5,4},{6,7},{7,6},{8,5},{9,8},{10,11... | collective-permute-start | bytes 786440 | tf_op jit(solution)/shard_map/ppermute | solution.py:129
  17.1 1.6 %collective-permute-start.10 = (bf16[1024,128]{1,0:T(8,128)(2,1)S(1)}, bf16[1024,128]{1,0:T(8,128)(2,1)S(1)}, u32[]{:S(2)}, u32[]{:S(2)}) collective-permute-start(bf16[1024,128]{1,0:T(8,128)(2,1)S(1)} %get-tuple-element.30.s_prev), channel_id=1, source_target_pairs={{0,1},{1,0},{2,3},{3,2},{4,5},{5,4},{6,7},{7,6},{8,9},{9,8},{10,11... | collective-permute-start | bytes 786440 | tf_op jit(solution)/shard_map/ppermute | solution.py:129
  18.7 1.6 %collective-permute-start.11 = (bf16[1024,128]{1,0:T(8,128)(2,1)S(1)}, bf16[1024,128]{1,0:T(8,128)(2,1)S(1)}, u32[]{:S(2)}, u32[]{:S(2)}) collective-permute-start(bf16[1024,128]{1,0:T(8,128)(2,1)S(1)} %get-tuple-element.31), channel_id=1, source_target_pairs={{0,1},{1,0},{2,3},{3,2},{4,5},{5,4},{6,7},{7,6},{8,9},{9,14},{10,1... | collective-permute-start | bytes 786440 | tf_op jit(solution)/shard_map/ppermute | solution.py:129
  19.2 1.5 %collective-permute-start.12 = (bf16[1024,128]{1,0:T(8,128)(2,1)S(1)}, bf16[1024,128]{1,0:T(8,128)(2,1)S(1)}, u32[]{:S(2)}, u32[]{:S(2)}) collective-permute-start(bf16[1024,128]{1,0:T(8,128)(2,1)S(1)} %step1_kernel.1.q_in.q_prev), channel_id=1, source_target_pairs={{0,1},{1,0},{2,3},{3,2},{4,5},{5,4},{6,7},{7,6},{8,9},{9,13},{10,1... | collective-permute-start | bytes 786440 | tf_op jit(solution)/shard_map/ppermute | solution.py:129
  19.3 1.8 %collective-permute-start.13 = (bf16[1024,128]{1,0:T(8,128)(2,1)S(1)}, bf16[1024,128]{1,0:T(8,128)(2,1)S(1)}, u32[]{:S(2)}, u32[]{:S(2)}) collective-permute-start(bf16[1024,128]{1,0:T(8,128)(2,1)S(1)} %step1_kernel.1.q_in.q_prev), channel_id=1, source_target_pairs={{0,1},{1,5},{2,3},{3,2},{4,0},{5,4},{6,7},{7,6},{8,16},{9,17},{10,... | collective-permute-start | bytes 786440 | tf_op jit(solution)/shard_map/ppermute | solution.py:129
  21.1 2.3 %collective-permute-start.14 = (bf16[1024,128]{1,0:T(8,128)(2,1)S(1)}, bf16[1024,128]{1,0:T(8,128)(2,1)S(1)}, u32[]{:S(2)}, u32[]{:S(2)}) collective-permute-start(bf16[1024,128]{1,0:T(8,128)(2,1)S(1)} %get-tuple-element.34), channel_id=1, source_target_pairs={{0,1},{1,0},{2,3},{3,2},{4,5},{5,4},{6,7},{7,6},{8,9},{9,8},{10,11... | collective-permute-start | bytes 786440 | tf_op jit(solution)/shard_map/ppermute | solution.py:129
  21.5 1.9 %collective-permute-start.15 = (bf16[1024,128]{1,0:T(8,128)(2,1)S(1)}, bf16[1024,128]{1,0:T(8,128)(2,1)S(1)}, u32[]{:S(2)}, u32[]{:S(2)}) collective-permute-start(bf16[1024,128]{1,0:T(8,128)(2,1)S(1)} %get-tuple-element.33.s_ref), channel_id=1, source_target_pairs={{0,1},{1,0},{2,3},{3,2},{4,5},{5,4},{6,7},{7,6},{8,9},{9,8},{10,11... | collective-permute-start | bytes 786440 | tf_op jit(solution)/shard_map/ppermute | solution.py:129
  21.7 1.8 %collective-permute-start.16 = (bf16[1024,128]{1,0:T(8,128)(2,1)S(1)}, bf16[1024,128]{1,0:T(8,128)(2,1)S(1)}, u32[]{:S(2)}, u32[]{:S(2)}) collective-permute-start(bf16[1024,128]{1,0:T(8,128)(2,1)S(1)} %get-tuple-element.35.refs_4_), channel_id=1, source_target_pairs={{0,1},{1,0},{2,3},{3,2},{4,5},{5,4},{6,7},{7,6},{8,9},{9,8},{10,11... | collective-permute-start | bytes 786440 | tf_op jit(solution)/shard_map/ppermute | solution.py:129
  22.1 1.4 %collective-permute-start.17 = (bf16[1024,128]{1,0:T(8,128)(2,1)S(1)}, bf16[1024,128]{1,0:T(8,128)(2,1)S(1)}, u32[]{:S(2)}, u32[]{:S(2)}) collective-permute-start(bf16[1024,128]{1,0:T(8,128)(2,1)S(1)} %get-tuple-element.35.refs_4_), channel_id=1, source_target_pairs={{14,30},{16,24},{20,28},{17,25},{13,21},{9,1}} | collective-permute-start | bytes 786440 | tf_op jit(solution)/shard_map/ppermute | solution.py:133
  23.5 2.7 %collective-permute-start.19 = (bf16[1024,128]{1,0:T(8,128)(2,1)S(1)}, bf16[1024,128]{1,0:T(8,128)(2,1)S(1)}, u32[]{:S(2)}, u32[]{:S(2)}) collective-permute-start(bf16[1024,128]{1,0:T(8,128)(2,1)S(1)} %step3_kernel.1.q_prev), channel_id=1, source_target_pairs={{23,27},{10,18}} | collective-permute-start | bytes 786440 | tf_op jit(solution)/shard_map/ppermute | solution.py:133
  24.2 2.1 %collective-permute-start.20 = (bf16[1024,128]{1,0:T(8,128)(2,1)S(1)}, bf16[1024,128]{1,0:T(8,128)(2,1)S(1)}, u32[]{:S(2)}, u32[]{:S(2)}) collective-permute-start(bf16[1024,128]{1,0:T(8,128)(2,1)S(1)} %step3_kernel.1.q_prev), channel_id=1, source_target_pairs={{23,31},{10,26}} | collective-permute-start | bytes 786440 | tf_op jit(solution)/shard_map/ppermute | solution.py:133
  24.9 1.4 %collective-permute-start.21 = (bf16[1024,128]{1,0:T(8,128)(2,1)S(1)}, bf16[1024,128]{1,0:T(8,128)(2,1)S(1)}, u32[]{:S(2)}, u32[]{:S(2)}) collective-permute-start(bf16[1024,128]{1,0:T(8,128)(2,1)S(1)} %step3_kernel.1.q_prev), channel_id=1, source_target_pairs={{23,19},{10,2}} | collective-permute-start | bytes 786440 | tf_op jit(solution)/shard_map/ppermute | solution.py:133
  26.4 35.3 %collective-permute-start.23 = (bf16[1040,128]{1,0:T(8,128)(2,1)S(1)}, bf16[1040,128]{1,0:T(8,128)(2,1)S(1)}, u32[]{:S(2)}, u32[]{:S(2)}) collective-permute-start(bf16[1040,128]{1,0:T(8,128)(2,1)S(1)} %get-tuple-element.37.mine_ref), channel_id=1, source_target_pairs={{0,2},{1,3},{2,0},{3,1},{4,6},{5,7},{6,4},{7,5},{8,10},{9,11},{10,... | collective-permute-start | bytes 798728 | tf_op jit(solution)/shard_map/ppermute | solution.py:129
  52.3 9.4 %collective-permute-start.24 = (bf16[1024,128]{1,0:T(8,128)(2,1)S(1)}, bf16[1024,128]{1,0:T(8,128)(2,1)S(1)}, u32[]{:S(2)}, u32[]{:S(2)}) collective-permute-start(bf16[1024,128]{1,0:T(8,128)(2,1)S(1)} %get-tuple-element.36.q_ref), channel_id=1, source_target_pairs={{15,11},{23,7},{27,3},{14,6}} | collective-permute-start | bytes 786440 | tf_op jit(solution)/shard_map/ppermute | solution.py:133
  53.6 8.9 %collective-permute-start.25 = (bf16[1040,128]{1,0:T(8,128)(2,1)S(1)}, bf16[1040,128]{1,0:T(8,128)(2,1)S(1)}, u32[]{:S(2)}, u32[]{:S(2)}) collective-permute-start(bf16[1040,128]{1,0:T(8,128)(2,1)S(1)} %get-tuple-element.37.mine_ref), channel_id=1, source_target_pairs={{0,1},{1,0},{2,3},{3,2},{4,5},{5,4},{6,7},{7,6},{8,9},{9,8},{10,11... | collective-permute-start | bytes 798728 | tf_op jit(solution)/shard_map/ppermute | solution.py:129
  61.7 1.5 %collective-permute-start.26 = (bf16[1040,128]{1,0:T(8,128)(2,1)S(1)}, bf16[1040,128]{1,0:T(8,128)(2,1)S(1)}, u32[]{:S(2)}, u32[]{:S(2)}) collective-permute-start(bf16[1040,128]{1,0:T(8,128)(2,1)S(1)} %collective-permute-done.23.across_ref), channel_id=1, source_target_pairs={{0,1},{1,0},{2,3},{3,2},{4,5},{5,4},{6,7},{7,6},{8,9},{9,8},{10,11... | collective-permute-start | bytes 798728 | tf_op jit(solution)/shard_map/ppermute | solution.py:129
  (7 other events, 45.4 us)

commit v20 on v19

--- a/solution.py
+++ b/solution.py
@@ -78,7 +78,7 @@
     (0, 3, 1, 2),
     (1, 3, 0, 2),
 )
-REST = ((2, 3), (1, 3), (0, 3), (1, 2))
+REST = ((2, 3), (3, 3), (0, 3), (1, 3), (1, 2))
 
 
 def hops(a, b):
@@ -536,7 +536,6 @@
         [(MAKER[3], (6, 3)), ((2, 2), (4, 2))],
         [(MAKER[3], (7, 3)), ((2, 2), (6, 2))],
         [(MAKER[3], (4, 3)), ((2, 2), (0, 2))],
-        [(MAKER[3], (3, 3))],
     ]
     got = [send_only(q, pairs) for pairs in sends]
     takers = [[b for _, b in pairs] for pairs in sends]
@@ -552,7 +551,7 @@
         return send(value, [((r, c), (r, c ^ step)) for r in range(NR) for c in range(NC)])
 
     across = swap(mine, 2)
-    rest = send_only(q, list(zip(((3, 3), MAKER[3], (6, 3), MAKER[2]), REST)))
+    rest = send_only(q, list(zip(((4, 3), (5, 3), (6, 3), (7, 3), MAKER[2]), REST)))
     beside = swap(mine, 1)
     across, rest = lax.optimization_barrier((across, rest))
     corner = swap(across, 1)

time: 64.9 us -> 63.5 us (0.978)
    ppermute x11 -> x10, starting transfers between devices: 14.3 us -> 13.6 us  [send_only(): lax.ppermute(value, ('row', 'col'), [(a * NC + b, c * NC + d) for (a, b),...]
    ppermute x11 -> x10, waiting for transfers between devices: 9.35 us -> 8.87 us  [send_only(): lax.ppermute(value, ('row', 'col'), [(a * NC + b, c * NC + d) for (a, b),...]
  transfers between devices with their start and end apart: 27 -> 26, of which waited for: 10 -> 10; matrix products, arithmetic and copies ran while one was open for 0% -> 0% of each run, Pallas kernels for 2% -> 2%
where the time goes in v20:
time: 63.5 us; the launch traced here: 63.2 us
  starting transfers between devices  45.3 us (71%)
  waiting for transfers between devices  12 us (19%)
  Pallas kernels  2.51 us (4%)
  between operations  2.2 us (3%)
  local copies, waits for them, and re-layouts  1.32 us (2%)
    ppermute x16, starting transfers between devices, send(): lax.ppermute(value, ('row', 'col'), [(a * NC + b, c * NC + d) for (a, b),...  31.7 us
    ppermute x10, starting transfers between devices, send_only(): lax.ppermute(value, ('row', 'col'), [(a * NC + b, c * NC + d) for (a, b),...  13.6 us
    ppermute x10, waiting for transfers between devices, send_only(): lax.ppermute(value, ('row', 'col'), [(a * NC + b, c * NC + d) for (a, b),...  8.87 us
    ppermute x16, waiting for transfers between devices, send(): lax.ppermute(value, ('row', 'col'), [(a * NC + b, c * NC + d) for (a, b),...  3.08 us
    pallas_call x12, Pallas kernels, call(): pl.pallas_call(kernel, out_shape=outs, in_specs=in_specs, out_specs=out_s...  2.51 us
    unnamed x8, local copies, waits for them, and re-layouts  1.32 us
  transfers between devices with their start and end apart: 26, of which 10 were waited for; matrix products, arithmetic and copies ran while one was open for 0% of the time, Pallas kernels for 2%

profile of v20, /device:TPU:7, one launch (start us, length us, event | category | flops | bytes accessed | tf_op | source)
XLA Modules:
  0.0 63.2 jit_solution(6007300458656696653)
XLA Ops:
  0.6 1.3 %copy-done.2 = bf16[4,128,1024]{2,1,0:T(8,128)(2,1)S(1)} copy-done((bf16[4,128,1024]{2,1,0:T(8,128)(2,1)S(1)}, bf16[4,128,1024]{2,1,0:T(8,128)(2,1)}, u32[]{:S(2)}) %copy-start.2) | copy-done | bytes 1048600
  2.0 0.8 %collective-permute-start.3 = (bf16[128,1024]{1,0:T(8,128)(2,1)S(1)}, bf16[128,1024]{1,0:T(8,128)(2,1)S(1)}, u32[]{:S(2)}, u32[]{:S(2)}) collective-permute-start(bf16[128,1024]{1,0:T(8,128)(2,1)S(1)} %get-tuple-element.25), channel_id=1, source_target_pairs={{24,1},{25,22},{26,13},{27,15},{28,9},{29,23},{30,3},{31,14}} | collective-permute-start | bytes 786440 | tf_op jit(solution)/shard_map/ppermute | solution.py:133
  2.8 0.8 %collective-permute-start.2 = (bf16[128,768]{1,0:T(8,128)(2,1)S(1)}, bf16[128,768]{1,0:T(8,128)(2,1)S(1)}, u32[]{:S(2)}, u32[]{:S(2)}) collective-permute-start(bf16[128,768]{1,0:T(8,128)(2,1)S(1)} %get-tuple-element.24), channel_id=1, source_target_pairs={{16,0},{17,13},{18,22},{19,15},{20,14},{21,9},{23,2}} | collective-permute-start | bytes 589832 | tf_op jit(solution)/shard_map/ppermute | solution.py:133
  3.6 0.7 %collective-permute-start.1 = (bf16[128,512]{1,0:T(8,128)(2,1)S(1)}, bf16[128,512]{1,0:T(8,128)(2,1)S(1)}, u32[]{:S(2)}, u32[]{:S(2)}) collective-permute-start(bf16[128,512]{1,0:T(8,128)(2,1)S(1)} %get-tuple-element.23), channel_id=1, source_target_pairs={{4,0},{8,22},{10,2},{11,15},{12,1},{13,9},{14,23}} | collective-permute-start | bytes 393224 | tf_op jit(solution)/shard_map/ppermute | solution.py:133
  4.3 6.6 %collective-permute-start = (bf16[128,256]{1,0:T(8,128)(2,1)S(1)}, bf16[128,256]{1,0:T(8,128)(2,1)S(1)}, u32[]{:S(2)}, u32[]{:S(2)}) collective-permute-start(bf16[128,256]{1,0:T(8,128)(2,1)S(1)} %get-tuple-element.22), channel_id=1, source_target_pairs={{1,13},{2,15},{3,22},{5,9},{6,14},{7,23}} | collective-permute-start | bytes 196616 | tf_op jit(solution)/shard_map/ppermute | solution.py:133
  11.0 1.3 %collective-permute-done.refs_0_ = bf16[128,256]{1,0:T(8,128)(2,1)S(1)} collective-permute-done((bf16[128,256]{1,0:T(8,128)(2,1)S(1)}, bf16[128,256]{1,0:T(8,128)(2,1)S(1)}, u32[]{:S(2)}, u32[]{:S(2)}) %collective-permute-start) | collective-permute-done | bytes 65568 | tf_op jit(solution)/shard_map/ppermute | solution.py:133
  12.3 2.2 %collective-permute-start.4 = (bf16[128,2560]{1,0:T(8,128)(2,1)S(1)}, bf16[128,2560]{1,0:T(8,128)(2,1)S(1)}, u32[]{:S(2)}, u32[]{:S(2)}) collective-permute-start(bf16[128,2560]{1,0:T(8,128)(2,1)S(1)} %pack_kernel.1), channel_id=1, source_target_pairs={{0,1},{1,0},{2,3},{3,2},{4,5},{5,4},{6,7},{7,6},{8,12},{9,8},{10,1... | collective-permute-start | bytes 1966088 | tf_op jit(solution)/shard_map/ppermute | solution.py:129
  14.7 0.5 collective-permute-start.6
  15.3 0.4 collective-permute-start.8
  15.7 0.7 %collective-permute-done.5.g0 = bf16[256,128]{1,0:T(8,128)(2,1)S(1)} collective-permute-done((bf16[256,128]{1,0:T(8,128)(2,1)S(1)}, bf16[256,128]{1,0:T(8,128)(2,1)S(1)}, u32[]{:S(2)}, u32[]{:S(2)}) %collective-permute-start.5) | collective-permute-done | bytes 65568 | tf_op jit(solution)/shard_map/ppermute | solution.py:129
  18.7 0.4 collective-permute-start.11
  19.7 0.7 %collective-permute-done.11.p_in = bf16[1024,128]{1,0:T(8,128)(2,1)S(1)} collective-permute-done((bf16[1024,128]{1,0:T(8,128)(2,1)S(1)}, bf16[1024,128]{1,0:T(8,128)(2,1)S(1)}, u32[]{:S(2)}, u32[]{:S(2)}) %collective-permute-start.11) | collective-permute-done | bytes 262176 | tf_op jit(solution)/shard_map/ppermute | solution.py:129
  21.1 0.4 collective-permute-start.14
  22.1 0.7 %collective-permute-start.17 = (bf16[1024,128]{1,0:T(8,128)(2,1)S(1)}, bf16[1024,128]{1,0:T(8,128)(2,1)S(1)}, u32[]{:S(2)}, u32[]{:S(2)}) collective-permute-start(bf16[1024,128]{1,0:T(8,128)(2,1)S(1)} %get-tuple-element.35.refs_4_), channel_id=1, source_target_pairs={{14,30},{16,24},{20,28},{17,25},{13,21},{9,1}} | collective-permute-start | bytes 786440 | tf_op jit(solution)/shard_map/ppermute | solution.py:133
  22.7 0.7 %collective-permute-start.18 = (bf16[1024,128]{1,0:T(8,128)(2,1)S(1)}, bf16[1024,128]{1,0:T(8,128)(2,1)S(1)}, u32[]{:S(2)}, u32[]{:S(2)}) collective-permute-start(bf16[1024,128]{1,0:T(8,128)(2,1)S(1)} %get-tuple-element.35.refs_4_), channel_id=1, source_target_pairs={{14,22},{13,29},{9,5}} | collective-permute-start | bytes 786440 | tf_op jit(solution)/shard_map/ppermute | solution.py:133
  23.5 0.7 %collective-permute-start.19 = (bf16[1024,128]{1,0:T(8,128)(2,1)S(1)}, bf16[1024,128]{1,0:T(8,128)(2,1)S(1)}, u32[]{:S(2)}, u32[]{:S(2)}) collective-permute-start(bf16[1024,128]{1,0:T(8,128)(2,1)S(1)} %step3_kernel.1.q_prev), channel_id=1, source_target_pairs={{23,27},{10,18}} | collective-permute-start | bytes 786440 | tf_op jit(solution)/shard_map/ppermute | solution.py:133
  24.2 0.7 %collective-permute-start.20 = (bf16[1024,128]{1,0:T(8,128)(2,1)S(1)}, bf16[1024,128]{1,0:T(8,128)(2,1)S(1)}, u32[]{:S(2)}, u32[]{:S(2)}) collective-permute-start(bf16[1024,128]{1,0:T(8,128)(2,1)S(1)} %step3_kernel.1.q_prev), channel_id=1, source_target_pairs={{23,31},{10,26}} | collective-permute-start | bytes 786440 | tf_op jit(solution)/shard_map/ppermute | solution.py:133
  24.9 0.7 %collective-permute-start.21 = (bf16[1024,128]{1,0:T(8,128)(2,1)S(1)}, bf16[1024,128]{1,0:T(8,128)(2,1)S(1)}, u32[]{:S(2)}, u32[]{:S(2)}) collective-permute-start(bf16[1024,128]{1,0:T(8,128)(2,1)S(1)} %step3_kernel.1.q_prev), channel_id=1, source_target_pairs={{23,19},{10,2}} | collective-permute-start | bytes 786440 | tf_op jit(solution)/shard_map/ppermute | solution.py:133
  25.7 25.9 %collective-permute-start.22 = (bf16[1040,128]{1,0:T(8,128)(2,1)S(1)}, bf16[1040,128]{1,0:T(8,128)(2,1)S(1)}, u32[]{:S(2)}, u32[]{:S(2)}) collective-permute-start(bf16[1040,128]{1,0:T(8,128)(2,1)S(1)} %get-tuple-element.37.mine_ref), channel_id=1, source_target_pairs={{0,2},{1,3},{2,0},{3,1},{4,6},{5,7},{6,4},{7,5},{8,10},{9,11},{10,... | collective-permute-start | bytes 798728 | tf_op jit(solution)/shard_map/ppermute | solution.py:129
  51.6 1.3 %collective-permute-start.23 = (bf16[1024,128]{1,0:T(8,128)(2,1)S(1)}, bf16[1024,128]{1,0:T(8,128)(2,1)S(1)}, u32[]{:S(2)}, u32[]{:S(2)}) collective-permute-start(bf16[1024,128]{1,0:T(8,128)(2,1)S(1)} %get-tuple-element.36.q_ref), channel_id=1, source_target_pairs={{19,11},{23,15},{27,3},{31,7},{14,6}} | collective-permute-start | bytes 786440 | tf_op jit(solution)/shard_map/ppermute | solution.py:133
  53.0 7.5 %collective-permute-done.23.rest_ref = bf16[1024,128]{1,0:T(8,128)(2,1)S(1)} collective-permute-done((bf16[1024,128]{1,0:T(8,128)(2,1)S(1)}, bf16[1024,128]{1,0:T(8,128)(2,1)S(1)}, u32[]{:S(2)}, u32[]{:S(2)}) %collective-permute-start.23) | collective-permute-done | bytes 262176 | tf_op jit(solution)/shard_map/ppermute | solution.py:133
  60.5 0.8 %half_kernel.1 = (f32[1024,128]{1,0:T(8,128)}, f32[2,1024,128]{2,1,0:T(8,128)S(1)}) custom-call(bf16[1024,128]{1,0:T(8,128)(2,1)S(1)} %get-tuple-element.36.q_ref, bf16[1024,128]{1,0:T(8,128)(2,1)S(1)} %collective-permute-done.23.rest_ref, f32[2,1024,128]{2,1,0:T(8,128)S(1)} %bitcast.14, bf16[1040,128]{1,0:T(8,128)(2,1)S(1)} %get-tuple-element.37.mine_ref, ...), custom_call_target="tpu_custom_call" | custom-call | tf_op jit(solution)/shard_map/half_kernel/pallas_call | solution.py:156
  61.4 0.7 %collective-permute-done.25.corner_ref = bf16[1040,128]{1,0:T(8,128)(2,1)S(1)} collective-permute-done((bf16[1040,128]{1,0:T(8,128)(2,1)S(1)}, bf16[1040,128]{1,0:T(8,128)(2,1)S(1)}, u32[]{:S(2)}, u32[]{:S(2)}) %collective-permute-start.25) | collective-permute-done | bytes 266272 | tf_op jit(solution)/shard_map/ppermute | solution.py:129
  62.0 1.2 %final_kernel.1 = f32[2,1024,128]{2,1,0:T(8,128)} custom-call(f32[2,1024,128]{2,1,0:T(8,128)S(1)} %get-tuple-element.41.half_ref, bf16[1040,128]{1,0:T(8,128)(2,1)S(1)} %collective-permute-done.24.beside_ref, bf16[1040,128]{1,0:T(8,128)(2,1)S(1)} %collective-permute-done.25.corner_ref), custom_call_target="tpu_custom_call" | custom-call | tf_op jit(solution)/shard_map/final_kernel/pallas_call | solution.py:156
  (48 shorter events, 3.4 us)
Async XLA Ops:
  2.0 10.3 %collective-permute-start.3 = (bf16[128,1024]{1,0:T(8,128)(2,1)S(1)}, bf16[128,1024]{1,0:T(8,128)(2,1)S(1)}, u32[]{:S(2)}, u32[]{:S(2)}) collective-permute-start(bf16[128,1024]{1,0:T(8,128)(2,1)S(1)} %get-tuple-element.25), channel_id=1, source_target_pairs={{24,1},{25,22},{26,13},{27,15},{28,9},{29,23},{30,3},{31,14}} | collective-permute-start | bytes 786440 | tf_op jit(solution)/shard_map/ppermute | solution.py:133
  2.8 9.5 %collective-permute-start.2 = (bf16[128,768]{1,0:T(8,128)(2,1)S(1)}, bf16[128,768]{1,0:T(8,128)(2,1)S(1)}, u32[]{:S(2)}, u32[]{:S(2)}) collective-permute-start(bf16[128,768]{1,0:T(8,128)(2,1)S(1)} %get-tuple-element.24), channel_id=1, source_target_pairs={{16,0},{17,13},{18,22},{19,15},{20,14},{21,9},{23,2}} | collective-permute-start | bytes 589832 | tf_op jit(solution)/shard_map/ppermute | solution.py:133
  3.6 8.6 %collective-permute-start.1 = (bf16[128,512]{1,0:T(8,128)(2,1)S(1)}, bf16[128,512]{1,0:T(8,128)(2,1)S(1)}, u32[]{:S(2)}, u32[]{:S(2)}) collective-permute-start(bf16[128,512]{1,0:T(8,128)(2,1)S(1)} %get-tuple-element.23), channel_id=1, source_target_pairs={{4,0},{8,22},{10,2},{11,15},{12,1},{13,9},{14,23}} | collective-permute-start | bytes 393224 | tf_op jit(solution)/shard_map/ppermute | solution.py:133
  4.3 8.0 %collective-permute-start = (bf16[128,256]{1,0:T(8,128)(2,1)S(1)}, bf16[128,256]{1,0:T(8,128)(2,1)S(1)}, u32[]{:S(2)}, u32[]{:S(2)}) collective-permute-start(bf16[128,256]{1,0:T(8,128)(2,1)S(1)} %get-tuple-element.22), channel_id=1, source_target_pairs={{1,13},{2,15},{3,22},{5,9},{6,14},{7,23}} | collective-permute-start | bytes 196616 | tf_op jit(solution)/shard_map/ppermute | solution.py:133
  12.3 6.1 %collective-permute-start.4 = (bf16[128,2560]{1,0:T(8,128)(2,1)S(1)}, bf16[128,2560]{1,0:T(8,128)(2,1)S(1)}, u32[]{:S(2)}, u32[]{:S(2)}) collective-permute-start(bf16[128,2560]{1,0:T(8,128)(2,1)S(1)} %pack_kernel.1), channel_id=1, source_target_pairs={{0,1},{1,0},{2,3},{3,2},{4,5},{5,4},{6,7},{7,6},{8,12},{9,8},{10,1... | collective-permute-start | bytes 1966088 | tf_op jit(solution)/shard_map/ppermute | solution.py:129
  14.6 1.8 %collective-permute-start.5 = (bf16[256,128]{1,0:T(8,128)(2,1)S(1)}, bf16[256,128]{1,0:T(8,128)(2,1)S(1)}, u32[]{:S(2)}, u32[]{:S(2)}) collective-permute-start(bf16[256,128]{1,0:T(8,128)(2,1)S(1)} %first_kernel.1), channel_id=1, source_target_pairs={{0,4},{1,8},{2,12},{3,2},{4,5},{5,0},{6,7},{7,6},{8,9},{9,1},{10,1... | collective-permute-start | bytes 196616 | tf_op jit(solution)/shard_map/ppermute | solution.py:129
  14.7 1.7 %collective-permute-start.6 = (bf16[256,128]{1,0:T(8,128)(2,1)S(1)}, bf16[256,128]{1,0:T(8,128)(2,1)S(1)}, u32[]{:S(2)}, u32[]{:S(2)}) collective-permute-start(bf16[256,128]{1,0:T(8,128)(2,1)S(1)} %first_kernel.1), channel_id=1, source_target_pairs={{0,8},{1,12},{2,3},{3,4},{4,5},{5,0},{6,7},{7,6},{8,9},{9,1},{10,1... | collective-permute-start | bytes 196616 | tf_op jit(solution)/shard_map/ppermute | solution.py:129
  15.2 1.4 %collective-permute-start.7 = (bf16[256,128]{1,0:T(8,128)(2,1)S(1)}, bf16[256,128]{1,0:T(8,128)(2,1)S(1)}, u32[]{:S(2)}, u32[]{:S(2)}) collective-permute-start(bf16[256,128]{1,0:T(8,128)(2,1)S(1)} %first_kernel.1), channel_id=1, source_target_pairs={{0,12},{1,0},{2,4},{3,8},{4,5},{5,1},{6,7},{7,6},{8,9},{9,2},{10,1... | collective-permute-start | bytes 196616 | tf_op jit(solution)/shard_map/ppermute | solution.py:129
  15.3 1.4 %collective-permute-start.8 = (bf16[256,128]{1,0:T(8,128)(2,1)S(1)}, bf16[256,128]{1,0:T(8,128)(2,1)S(1)}, u32[]{:S(2)}, u32[]{:S(2)}) collective-permute-start(bf16[256,128]{1,0:T(8,128)(2,1)S(1)} %first_kernel.1), channel_id=1, source_target_pairs={{0,1},{1,4},{2,8},{3,12},{4,5},{5,0},{6,7},{7,6},{8,9},{9,2},{10,1... | collective-permute-start | bytes 196616 | tf_op jit(solution)/shard_map/ppermute | solution.py:129
  16.7 1.9 %collective-permute-start.9 = (bf16[1024,128]{1,0:T(8,128)(2,1)S(1)}, bf16[1024,128]{1,0:T(8,128)(2,1)S(1)}, u32[]{:S(2)}, u32[]{:S(2)}) collective-permute-start(bf16[1024,128]{1,0:T(8,128)(2,1)S(1)} %get-tuple-element.27), channel_id=1, source_target_pairs={{0,1},{1,0},{2,3},{3,2},{4,9},{5,4},{6,7},{7,6},{8,5},{9,8},{10,11... | collective-permute-start | bytes 786440 | tf_op jit(solution)/shard_map/ppermute | solution.py:129
  17.1 1.6 %collective-permute-start.10 = (bf16[1024,128]{1,0:T(8,128)(2,1)S(1)}, bf16[1024,128]{1,0:T(8,128)(2,1)S(1)}, u32[]{:S(2)}, u32[]{:S(2)}) collective-permute-start(bf16[1024,128]{1,0:T(8,128)(2,1)S(1)} %get-tuple-element.30.s_prev), channel_id=1, source_target_pairs={{0,1},{1,0},{2,3},{3,2},{4,5},{5,4},{6,7},{7,6},{8,9},{9,8},{10,11... | collective-permute-start | bytes 786440 | tf_op jit(solution)/shard_map/ppermute | solution.py:129
  18.7 1.6 %collective-permute-start.11 = (bf16[1024,128]{1,0:T(8,128)(2,1)S(1)}, bf16[1024,128]{1,0:T(8,128)(2,1)S(1)}, u32[]{:S(2)}, u32[]{:S(2)}) collective-permute-start(bf16[1024,128]{1,0:T(8,128)(2,1)S(1)} %get-tuple-element.31), channel_id=1, source_target_pairs={{0,1},{1,0},{2,3},{3,2},{4,5},{5,4},{6,7},{7,6},{8,9},{9,14},{10,1... | collective-permute-start | bytes 786440 | tf_op jit(solution)/shard_map/ppermute | solution.py:129
  19.2 1.5 %collective-permute-start.12 = (bf16[1024,128]{1,0:T(8,128)(2,1)S(1)}, bf16[1024,128]{1,0:T(8,128)(2,1)S(1)}, u32[]{:S(2)}, u32[]{:S(2)}) collective-permute-start(bf16[1024,128]{1,0:T(8,128)(2,1)S(1)} %step1_kernel.1.q_in.q_prev), channel_id=1, source_target_pairs={{0,1},{1,0},{2,3},{3,2},{4,5},{5,4},{6,7},{7,6},{8,9},{9,13},{10,1... | collective-permute-start | bytes 786440 | tf_op jit(solution)/shard_map/ppermute | solution.py:129
  19.3 1.8 %collective-permute-start.13 = (bf16[1024,128]{1,0:T(8,128)(2,1)S(1)}, bf16[1024,128]{1,0:T(8,128)(2,1)S(1)}, u32[]{:S(2)}, u32[]{:S(2)}) collective-permute-start(bf16[1024,128]{1,0:T(8,128)(2,1)S(1)} %step1_kernel.1.q_in.q_prev), channel_id=1, source_target_pairs={{0,1},{1,5},{2,3},{3,2},{4,0},{5,4},{6,7},{7,6},{8,16},{9,17},{10,... | collective-permute-start | bytes 786440 | tf_op jit(solution)/shard_map/ppermute | solution.py:129
  21.1 2.3 %collective-permute-start.14 = (bf16[1024,128]{1,0:T(8,128)(2,1)S(1)}, bf16[1024,128]{1,0:T(8,128)(2,1)S(1)}, u32[]{:S(2)}, u32[]{:S(2)}) collective-permute-start(bf16[1024,128]{1,0:T(8,128)(2,1)S(1)} %get-tuple-element.34), channel_id=1, source_target_pairs={{0,1},{1,0},{2,3},{3,2},{4,5},{5,4},{6,7},{7,6},{8,9},{9,8},{10,11... | collective-permute-start | bytes 786440 | tf_op jit(solution)/shard_map/ppermute | solution.py:129
  21.5 1.9 %collective-permute-start.15 = (bf16[1024,128]{1,0:T(8,128)(2,1)S(1)}, bf16[1024,128]{1,0:T(8,128)(2,1)S(1)}, u32[]{:S(2)}, u32[]{:S(2)}) collective-permute-start(bf16[1024,128]{1,0:T(8,128)(2,1)S(1)} %get-tuple-element.33.s_ref), channel_id=1, source_target_pairs={{0,1},{1,0},{2,3},{3,2},{4,5},{5,4},{6,7},{7,6},{8,9},{9,8},{10,11... | collective-permute-start | bytes 786440 | tf_op jit(solution)/shard_map/ppermute | solution.py:129
  21.7 1.8 %collective-permute-start.16 = (bf16[1024,128]{1,0:T(8,128)(2,1)S(1)}, bf16[1024,128]{1,0:T(8,128)(2,1)S(1)}, u32[]{:S(2)}, u32[]{:S(2)}) collective-permute-start(bf16[1024,128]{1,0:T(8,128)(2,1)S(1)} %get-tuple-element.35.refs_4_), channel_id=1, source_target_pairs={{0,1},{1,0},{2,3},{3,2},{4,5},{5,4},{6,7},{7,6},{8,9},{9,8},{10,11... | collective-permute-start | bytes 786440 | tf_op jit(solution)/shard_map/ppermute | solution.py:129
  22.1 1.4 %collective-permute-start.17 = (bf16[1024,128]{1,0:T(8,128)(2,1)S(1)}, bf16[1024,128]{1,0:T(8,128)(2,1)S(1)}, u32[]{:S(2)}, u32[]{:S(2)}) collective-permute-start(bf16[1024,128]{1,0:T(8,128)(2,1)S(1)} %get-tuple-element.35.refs_4_), channel_id=1, source_target_pairs={{14,30},{16,24},{20,28},{17,25},{13,21},{9,1}} | collective-permute-start | bytes 786440 | tf_op jit(solution)/shard_map/ppermute | solution.py:133
  23.5 2.1 %collective-permute-start.19 = (bf16[1024,128]{1,0:T(8,128)(2,1)S(1)}, bf16[1024,128]{1,0:T(8,128)(2,1)S(1)}, u32[]{:S(2)}, u32[]{:S(2)}) collective-permute-start(bf16[1024,128]{1,0:T(8,128)(2,1)S(1)} %step3_kernel.1.q_prev), channel_id=1, source_target_pairs={{23,27},{10,18}} | collective-permute-start | bytes 786440 | tf_op jit(solution)/shard_map/ppermute | solution.py:133
  24.2 1.4 %collective-permute-start.20 = (bf16[1024,128]{1,0:T(8,128)(2,1)S(1)}, bf16[1024,128]{1,0:T(8,128)(2,1)S(1)}, u32[]{:S(2)}, u32[]{:S(2)}) collective-permute-start(bf16[1024,128]{1,0:T(8,128)(2,1)S(1)} %step3_kernel.1.q_prev), channel_id=1, source_target_pairs={{23,31},{10,26}} | collective-permute-start | bytes 786440 | tf_op jit(solution)/shard_map/ppermute | solution.py:133
  25.7 34.8 %collective-permute-start.22 = (bf16[1040,128]{1,0:T(8,128)(2,1)S(1)}, bf16[1040,128]{1,0:T(8,128)(2,1)S(1)}, u32[]{:S(2)}, u32[]{:S(2)}) collective-permute-start(bf16[1040,128]{1,0:T(8,128)(2,1)S(1)} %get-tuple-element.37.mine_ref), channel_id=1, source_target_pairs={{0,2},{1,3},{2,0},{3,1},{4,6},{5,7},{6,4},{7,5},{8,10},{9,11},{10,... | collective-permute-start | bytes 798728 | tf_op jit(solution)/shard_map/ppermute | solution.py:129
  51.6 8.9 %collective-permute-start.23 = (bf16[1024,128]{1,0:T(8,128)(2,1)S(1)}, bf16[1024,128]{1,0:T(8,128)(2,1)S(1)}, u32[]{:S(2)}, u32[]{:S(2)}) collective-permute-start(bf16[1024,128]{1,0:T(8,128)(2,1)S(1)} %get-tuple-element.36.q_ref), channel_id=1, source_target_pairs={{19,11},{23,15},{27,3},{31,7},{14,6}} | collective-permute-start | bytes 786440 | tf_op jit(solution)/shard_map/ppermute | solution.py:133
  52.9 8.5 %collective-permute-start.24 = (bf16[1040,128]{1,0:T(8,128)(2,1)S(1)}, bf16[1040,128]{1,0:T(8,128)(2,1)S(1)}, u32[]{:S(2)}, u32[]{:S(2)}) collective-permute-start(bf16[1040,128]{1,0:T(8,128)(2,1)S(1)} %get-tuple-element.37.mine_ref), channel_id=1, source_target_pairs={{0,1},{1,0},{2,3},{3,2},{4,5},{5,4},{6,7},{7,6},{8,9},{9,8},{10,11... | collective-permute-start | bytes 798728 | tf_op jit(solution)/shard_map/ppermute | solution.py:129
  60.5 1.5 %collective-permute-start.25 = (bf16[1040,128]{1,0:T(8,128)(2,1)S(1)}, bf16[1040,128]{1,0:T(8,128)(2,1)S(1)}, u32[]{:S(2)}, u32[]{:S(2)}) collective-permute-start(bf16[1040,128]{1,0:T(8,128)(2,1)S(1)} %collective-permute-done.22.across_ref), channel_id=1, source_target_pairs={{0,1},{1,0},{2,3},{3,2},{4,5},{5,4},{6,7},{7,6},{8,9},{9,8},{10,11... | collective-permute-start | bytes 798728 | tf_op jit(solution)/shard_map/ppermute | solution.py:129
  (6 other events, 44.0 us)

commit v21 on v20

--- a/solution.py
+++ b/solution.py
@@ -519,8 +519,8 @@
     sums = send(s, [(MAKER[2], MAKER[3])])
     sends = [
         [(MAKER[2], (2, 2))],
-        [(MAKER[2], (7, 2)), ((4, 0), (6, 0)), ((5, 0), (7, 0)), ((4, 1), (6, 1)), ((3, 1), (5, 1)), ((2, 1), (0, 1))],
-        [(MAKER[2], (5, 2)), ((3, 1), (7, 1)), ((2, 1), (1, 1))],
+        [(MAKER[2], (7, 2)), ((4, 0), (6, 0)), ((5, 0), (7, 0)), ((4, 1), (6, 1)), ((3, 1), (1, 1)), ((2, 1), (0, 1))],
+        [(MAKER[2], (5, 2)), ((3, 1), (7, 1)), ((4, 1), (5, 1))],
     ]
     got = [send(q, sends[0])] + [send_only(q, pairs) for pairs in sends[1:]]
     q = call(
@@ -533,9 +533,9 @@
     )
 
     sends = [
-        [(MAKER[3], (6, 3)), ((2, 2), (4, 2))],
-        [(MAKER[3], (7, 3)), ((2, 2), (6, 2))],
+        [(MAKER[3], (6, 3)), ((2, 2), (4, 2)), ((7, 2), (6, 2))],
         [(MAKER[3], (4, 3)), ((2, 2), (0, 2))],
+        [(MAKER[3], (7, 3))],
     ]
     got = [send_only(q, pairs) for pairs in sends]
     takers = [[b for _, b in pairs] for pairs in sends]

time: 63.5 us -> 62.1 us (0.978)
  starting transfers between devices: 45.3 us -> 41.2 us
  waiting for transfers between devices: 12 us -> 14.4 us
    ppermute x16, starting transfers between devices: 31.7 us -> 27.6 us  [send(): lax.ppermute(value, ('row', 'col'), [(a * NC + b, c * NC + d) for (a, b),...]
    ppermute x10, waiting for transfers between devices: 8.87 us -> 11.3 us  [send_only(): lax.ppermute(value, ('row', 'col'), [(a * NC + b, c * NC + d) for (a, b),...]
where the time goes in v21:
time: 62.1 us; the launch traced here: 61.6 us
  starting transfers between devices  41.2 us (66%)
  waiting for transfers between devices  14.4 us (23%)
  Pallas kernels  2.51 us (4%)
  between operations  2.2 us (4%)
  local copies, waits for them, and re-layouts  1.32 us (2%)
    ppermute x16, starting transfers between devices, send(): lax.ppermute(value, ('row', 'col'), [(a * NC + b, c * NC + d) for (a, b),...  27.6 us
    ppermute x10, starting transfers between devices, send_only(): lax.ppermute(value, ('row', 'col'), [(a * NC + b, c * NC + d) for (a, b),...  13.6 us
    ppermute x10, waiting for transfers between devices, send_only(): lax.ppermute(value, ('row', 'col'), [(a * NC + b, c * NC + d) for (a, b),...  11.3 us
    ppermute x16, waiting for transfers between devices, send(): lax.ppermute(value, ('row', 'col'), [(a * NC + b, c * NC + d) for (a, b),...  3.08 us
    pallas_call x12, Pallas kernels, call(): pl.pallas_call(kernel, out_shape=outs, in_specs=in_specs, out_specs=out_s...  2.51 us
    unnamed x8, local copies, waits for them, and re-layouts  1.32 us
  transfers between devices with their start and end apart: 26, of which 10 were waited for; matrix products, arithmetic and copies ran while one was open for 0% of the time, Pallas kernels for 2%

profile of v21, /device:TPU:7, one launch (start us, length us, event | category | flops | bytes accessed | tf_op | source)
XLA Modules:
  0.0 61.6 jit_solution(12116182625781212735)
XLA Ops:
  0.6 1.3 %copy-done.2 = bf16[4,128,1024]{2,1,0:T(8,128)(2,1)S(1)} copy-done((bf16[4,128,1024]{2,1,0:T(8,128)(2,1)S(1)}, bf16[4,128,1024]{2,1,0:T(8,128)(2,1)}, u32[]{:S(2)}) %copy-start.2) | copy-done | bytes 1048600
  2.0 0.8 %collective-permute-start.3 = (bf16[128,1024]{1,0:T(8,128)(2,1)S(1)}, bf16[128,1024]{1,0:T(8,128)(2,1)S(1)}, u32[]{:S(2)}, u32[]{:S(2)}) collective-permute-start(bf16[128,1024]{1,0:T(8,128)(2,1)S(1)} %get-tuple-element.25), channel_id=1, source_target_pairs={{24,1},{25,22},{26,13},{27,15},{28,9},{29,23},{30,3},{31,14}} | collective-permute-start | bytes 786440 | tf_op jit(solution)/shard_map/ppermute | solution.py:133
  2.8 0.8 %collective-permute-start.2 = (bf16[128,768]{1,0:T(8,128)(2,1)S(1)}, bf16[128,768]{1,0:T(8,128)(2,1)S(1)}, u32[]{:S(2)}, u32[]{:S(2)}) collective-permute-start(bf16[128,768]{1,0:T(8,128)(2,1)S(1)} %get-tuple-element.24), channel_id=1, source_target_pairs={{16,0},{17,13},{18,22},{19,15},{20,14},{21,9},{23,2}} | collective-permute-start | bytes 589832 | tf_op jit(solution)/shard_map/ppermute | solution.py:133
  3.6 0.7 %collective-permute-start.1 = (bf16[128,512]{1,0:T(8,128)(2,1)S(1)}, bf16[128,512]{1,0:T(8,128)(2,1)S(1)}, u32[]{:S(2)}, u32[]{:S(2)}) collective-permute-start(bf16[128,512]{1,0:T(8,128)(2,1)S(1)} %get-tuple-element.23), channel_id=1, source_target_pairs={{4,0},{8,22},{10,2},{11,15},{12,1},{13,9},{14,23}} | collective-permute-start | bytes 393224 | tf_op jit(solution)/shard_map/ppermute | solution.py:133
  4.3 6.6 %collective-permute-start = (bf16[128,256]{1,0:T(8,128)(2,1)S(1)}, bf16[128,256]{1,0:T(8,128)(2,1)S(1)}, u32[]{:S(2)}, u32[]{:S(2)}) collective-permute-start(bf16[128,256]{1,0:T(8,128)(2,1)S(1)} %get-tuple-element.22), channel_id=1, source_target_pairs={{1,13},{2,15},{3,22},{5,9},{6,14},{7,23}} | collective-permute-start | bytes 196616 | tf_op jit(solution)/shard_map/ppermute | solution.py:133
  11.0 1.3 %collective-permute-done.refs_0_ = bf16[128,256]{1,0:T(8,128)(2,1)S(1)} collective-permute-done((bf16[128,256]{1,0:T(8,128)(2,1)S(1)}, bf16[128,256]{1,0:T(8,128)(2,1)S(1)}, u32[]{:S(2)}, u32[]{:S(2)}) %collective-permute-start) | collective-permute-done | bytes 65568 | tf_op jit(solution)/shard_map/ppermute | solution.py:133
  12.3 2.2 %collective-permute-start.4 = (bf16[128,2560]{1,0:T(8,128)(2,1)S(1)}, bf16[128,2560]{1,0:T(8,128)(2,1)S(1)}, u32[]{:S(2)}, u32[]{:S(2)}) collective-permute-start(bf16[128,2560]{1,0:T(8,128)(2,1)S(1)} %pack_kernel.1), channel_id=1, source_target_pairs={{0,1},{1,0},{2,3},{3,2},{4,5},{5,4},{6,7},{7,6},{8,12},{9,8},{10,1... | collective-permute-start | bytes 1966088 | tf_op jit(solution)/shard_map/ppermute | solution.py:129
  14.7 0.5 collective-permute-start.6
  15.3 0.4 collective-permute-start.8
  15.7 0.7 %collective-permute-done.5.g0 = bf16[256,128]{1,0:T(8,128)(2,1)S(1)} collective-permute-done((bf16[256,128]{1,0:T(8,128)(2,1)S(1)}, bf16[256,128]{1,0:T(8,128)(2,1)S(1)}, u32[]{:S(2)}, u32[]{:S(2)}) %collective-permute-start.5) | collective-permute-done | bytes 65568 | tf_op jit(solution)/shard_map/ppermute | solution.py:129
  18.7 0.4 collective-permute-start.11
  19.7 0.7 %collective-permute-done.11.p_in = bf16[1024,128]{1,0:T(8,128)(2,1)S(1)} collective-permute-done((bf16[1024,128]{1,0:T(8,128)(2,1)S(1)}, bf16[1024,128]{1,0:T(8,128)(2,1)S(1)}, u32[]{:S(2)}, u32[]{:S(2)}) %collective-permute-start.11) | collective-permute-done | bytes 262176 | tf_op jit(solution)/shard_map/ppermute | solution.py:129
  21.1 0.4 collective-permute-start.14
  22.1 0.7 %collective-permute-start.17 = (bf16[1024,128]{1,0:T(8,128)(2,1)S(1)}, bf16[1024,128]{1,0:T(8,128)(2,1)S(1)}, u32[]{:S(2)}, u32[]{:S(2)}) collective-permute-start(bf16[1024,128]{1,0:T(8,128)(2,1)S(1)} %get-tuple-element.35.refs_4_), channel_id=1, source_target_pairs={{14,30},{16,24},{20,28},{17,25},{13,5},{9,1}} | collective-permute-start | bytes 786440 | tf_op jit(solution)/shard_map/ppermute | solution.py:133
  22.7 0.7 %collective-permute-start.18 = (bf16[1024,128]{1,0:T(8,128)(2,1)S(1)}, bf16[1024,128]{1,0:T(8,128)(2,1)S(1)}, u32[]{:S(2)}, u32[]{:S(2)}) collective-permute-start(bf16[1024,128]{1,0:T(8,128)(2,1)S(1)} %get-tuple-element.35.refs_4_), channel_id=1, source_target_pairs={{14,22},{13,29},{17,21}} | collective-permute-start | bytes 786440 | tf_op jit(solution)/shard_map/ppermute | solution.py:133
  23.5 0.7 %collective-permute-start.19 = (bf16[1024,128]{1,0:T(8,128)(2,1)S(1)}, bf16[1024,128]{1,0:T(8,128)(2,1)S(1)}, u32[]{:S(2)}, u32[]{:S(2)}) collective-permute-start(bf16[1024,128]{1,0:T(8,128)(2,1)S(1)} %step3_kernel.1.q_prev), channel_id=1, source_target_pairs={{23,27},{10,18},{30,26}} | collective-permute-start | bytes 786440 | tf_op jit(solution)/shard_map/ppermute | solution.py:133
  24.2 0.7 %collective-permute-start.20 = (bf16[1024,128]{1,0:T(8,128)(2,1)S(1)}, bf16[1024,128]{1,0:T(8,128)(2,1)S(1)}, u32[]{:S(2)}, u32[]{:S(2)}) collective-permute-start(bf16[1024,128]{1,0:T(8,128)(2,1)S(1)} %step3_kernel.1.q_prev), channel_id=1, source_target_pairs={{23,19},{10,2}} | collective-permute-start | bytes 786440 | tf_op jit(solution)/shard_map/ppermute | solution.py:133
  24.9 0.7 %collective-permute-start.21 = (bf16[1024,128]{1,0:T(8,128)(2,1)S(1)}, bf16[1024,128]{1,0:T(8,128)(2,1)S(1)}, u32[]{:S(2)}, u32[]{:S(2)}) collective-permute-start(bf16[1024,128]{1,0:T(8,128)(2,1)S(1)} %step3_kernel.1.q_prev), channel_id=1, source_target_pairs={{23,31}} | collective-permute-start | bytes 786440 | tf_op jit(solution)/shard_map/ppermute | solution.py:133
  25.7 21.8 %collective-permute-start.22 = (bf16[1040,128]{1,0:T(8,128)(2,1)S(1)}, bf16[1040,128]{1,0:T(8,128)(2,1)S(1)}, u32[]{:S(2)}, u32[]{:S(2)}) collective-permute-start(bf16[1040,128]{1,0:T(8,128)(2,1)S(1)} %get-tuple-element.37.mine_ref), channel_id=1, source_target_pairs={{0,2},{1,3},{2,0},{3,1},{4,6},{5,7},{6,4},{7,5},{8,10},{9,11},{10,... | collective-permute-start | bytes 798728 | tf_op jit(solution)/shard_map/ppermute | solution.py:129
  47.5 1.3 %collective-permute-start.23 = (bf16[1024,128]{1,0:T(8,128)(2,1)S(1)}, bf16[1024,128]{1,0:T(8,128)(2,1)S(1)}, u32[]{:S(2)}, u32[]{:S(2)}) collective-permute-start(bf16[1024,128]{1,0:T(8,128)(2,1)S(1)} %get-tuple-element.36.q_ref), channel_id=1, source_target_pairs={{19,11},{23,15},{27,3},{31,7},{14,6}} | collective-permute-start | bytes 786440 | tf_op jit(solution)/shard_map/ppermute | solution.py:133
  48.9 9.9 %collective-permute-done.23.rest_ref = bf16[1024,128]{1,0:T(8,128)(2,1)S(1)} collective-permute-done((bf16[1024,128]{1,0:T(8,128)(2,1)S(1)}, bf16[1024,128]{1,0:T(8,128)(2,1)S(1)}, u32[]{:S(2)}, u32[]{:S(2)}) %collective-permute-start.23) | collective-permute-done | bytes 262176 | tf_op jit(solution)/shard_map/ppermute | solution.py:133
  58.8 0.8 %half_kernel.1 = (f32[1024,128]{1,0:T(8,128)}, f32[2,1024,128]{2,1,0:T(8,128)S(1)}) custom-call(bf16[1024,128]{1,0:T(8,128)(2,1)S(1)} %get-tuple-element.36.q_ref, bf16[1024,128]{1,0:T(8,128)(2,1)S(1)} %collective-permute-done.23.rest_ref, f32[2,1024,128]{2,1,0:T(8,128)S(1)} %bitcast.14, bf16[1040,128]{1,0:T(8,128)(2,1)S(1)} %get-tuple-element.37.mine_ref, ...), custom_call_target="tpu_custom_call" | custom-call | tf_op jit(solution)/shard_map/half_kernel/pallas_call | solution.py:156
  59.7 0.7 %collective-permute-done.25.corner_ref = bf16[1040,128]{1,0:T(8,128)(2,1)S(1)} collective-permute-done((bf16[1040,128]{1,0:T(8,128)(2,1)S(1)}, bf16[1040,128]{1,0:T(8,128)(2,1)S(1)}, u32[]{:S(2)}, u32[]{:S(2)}) %collective-permute-start.25) | collective-permute-done | bytes 266272 | tf_op jit(solution)/shard_map/ppermute | solution.py:129
  60.4 1.2 %final_kernel.1 = f32[2,1024,128]{2,1,0:T(8,128)} custom-call(f32[2,1024,128]{2,1,0:T(8,128)S(1)} %get-tuple-element.41.half_ref, bf16[1040,128]{1,0:T(8,128)(2,1)S(1)} %collective-permute-done.24.beside_ref, bf16[1040,128]{1,0:T(8,128)(2,1)S(1)} %collective-permute-done.25.corner_ref), custom_call_target="tpu_custom_call" | custom-call | tf_op jit(solution)/shard_map/final_kernel/pallas_call | solution.py:156
  (48 shorter events, 3.4 us)
Async XLA Ops:
  2.0 10.3 %collective-permute-start.3 = (bf16[128,1024]{1,0:T(8,128)(2,1)S(1)}, bf16[128,1024]{1,0:T(8,128)(2,1)S(1)}, u32[]{:S(2)}, u32[]{:S(2)}) collective-permute-start(bf16[128,1024]{1,0:T(8,128)(2,1)S(1)} %get-tuple-element.25), channel_id=1, source_target_pairs={{24,1},{25,22},{26,13},{27,15},{28,9},{29,23},{30,3},{31,14}} | collective-permute-start | bytes 786440 | tf_op jit(solution)/shard_map/ppermute | solution.py:133
  2.8 9.5 %collective-permute-start.2 = (bf16[128,768]{1,0:T(8,128)(2,1)S(1)}, bf16[128,768]{1,0:T(8,128)(2,1)S(1)}, u32[]{:S(2)}, u32[]{:S(2)}) collective-permute-start(bf16[128,768]{1,0:T(8,128)(2,1)S(1)} %get-tuple-element.24), channel_id=1, source_target_pairs={{16,0},{17,13},{18,22},{19,15},{20,14},{21,9},{23,2}} | collective-permute-start | bytes 589832 | tf_op jit(solution)/shard_map/ppermute | solution.py:133
  3.6 8.6 %collective-permute-start.1 = (bf16[128,512]{1,0:T(8,128)(2,1)S(1)}, bf16[128,512]{1,0:T(8,128)(2,1)S(1)}, u32[]{:S(2)}, u32[]{:S(2)}) collective-permute-start(bf16[128,512]{1,0:T(8,128)(2,1)S(1)} %get-tuple-element.23), channel_id=1, source_target_pairs={{4,0},{8,22},{10,2},{11,15},{12,1},{13,9},{14,23}} | collective-permute-start | bytes 393224 | tf_op jit(solution)/shard_map/ppermute | solution.py:133
  4.3 8.0 %collective-permute-start = (bf16[128,256]{1,0:T(8,128)(2,1)S(1)}, bf16[128,256]{1,0:T(8,128)(2,1)S(1)}, u32[]{:S(2)}, u32[]{:S(2)}) collective-permute-start(bf16[128,256]{1,0:T(8,128)(2,1)S(1)} %get-tuple-element.22), channel_id=1, source_target_pairs={{1,13},{2,15},{3,22},{5,9},{6,14},{7,23}} | collective-permute-start | bytes 196616 | tf_op jit(solution)/shard_map/ppermute | solution.py:133
  12.3 6.1 %collective-permute-start.4 = (bf16[128,2560]{1,0:T(8,128)(2,1)S(1)}, bf16[128,2560]{1,0:T(8,128)(2,1)S(1)}, u32[]{:S(2)}, u32[]{:S(2)}) collective-permute-start(bf16[128,2560]{1,0:T(8,128)(2,1)S(1)} %pack_kernel.1), channel_id=1, source_target_pairs={{0,1},{1,0},{2,3},{3,2},{4,5},{5,4},{6,7},{7,6},{8,12},{9,8},{10,1... | collective-permute-start | bytes 1966088 | tf_op jit(solution)/shard_map/ppermute | solution.py:129
  14.6 1.8 %collective-permute-start.5 = (bf16[256,128]{1,0:T(8,128)(2,1)S(1)}, bf16[256,128]{1,0:T(8,128)(2,1)S(1)}, u32[]{:S(2)}, u32[]{:S(2)}) collective-permute-start(bf16[256,128]{1,0:T(8,128)(2,1)S(1)} %first_kernel.1), channel_id=1, source_target_pairs={{0,4},{1,8},{2,12},{3,2},{4,5},{5,0},{6,7},{7,6},{8,9},{9,1},{10,1... | collective-permute-start | bytes 196616 | tf_op jit(solution)/shard_map/ppermute | solution.py:129
  14.7 1.7 %collective-permute-start.6 = (bf16[256,128]{1,0:T(8,128)(2,1)S(1)}, bf16[256,128]{1,0:T(8,128)(2,1)S(1)}, u32[]{:S(2)}, u32[]{:S(2)}) collective-permute-start(bf16[256,128]{1,0:T(8,128)(2,1)S(1)} %first_kernel.1), channel_id=1, source_target_pairs={{0,8},{1,12},{2,3},{3,4},{4,5},{5,0},{6,7},{7,6},{8,9},{9,1},{10,1... | collective-permute-start | bytes 196616 | tf_op jit(solution)/shard_map/ppermute | solution.py:129
  15.2 1.4 %collective-permute-start.7 = (bf16[256,128]{1,0:T(8,128)(2,1)S(1)}, bf16[256,128]{1,0:T(8,128)(2,1)S(1)}, u32[]{:S(2)}, u32[]{:S(2)}) collective-permute-start(bf16[256,128]{1,0:T(8,128)(2,1)S(1)} %first_kernel.1), channel_id=1, source_target_pairs={{0,12},{1,0},{2,4},{3,8},{4,5},{5,1},{6,7},{7,6},{8,9},{9,2},{10,1... | collective-permute-start | bytes 196616 | tf_op jit(solution)/shard_map/ppermute | solution.py:129
  15.3 1.4 %collective-permute-start.8 = (bf16[256,128]{1,0:T(8,128)(2,1)S(1)}, bf16[256,128]{1,0:T(8,128)(2,1)S(1)}, u32[]{:S(2)}, u32[]{:S(2)}) collective-permute-start(bf16[256,128]{1,0:T(8,128)(2,1)S(1)} %first_kernel.1), channel_id=1, source_target_pairs={{0,1},{1,4},{2,8},{3,12},{4,5},{5,0},{6,7},{7,6},{8,9},{9,2},{10,1... | collective-permute-start | bytes 196616 | tf_op jit(solution)/shard_map/ppermute | solution.py:129
  16.7 1.9 %collective-permute-start.9 = (bf16[1024,128]{1,0:T(8,128)(2,1)S(1)}, bf16[1024,128]{1,0:T(8,128)(2,1)S(1)}, u32[]{:S(2)}, u32[]{:S(2)}) collective-permute-start(bf16[1024,128]{1,0:T(8,128)(2,1)S(1)} %get-tuple-element.27), channel_id=1, source_target_pairs={{0,1},{1,0},{2,3},{3,2},{4,9},{5,4},{6,7},{7,6},{8,5},{9,8},{10,11... | collective-permute-start | bytes 786440 | tf_op jit(solution)/shard_map/ppermute | solution.py:129
  17.1 1.6 %collective-permute-start.10 = (bf16[1024,128]{1,0:T(8,128)(2,1)S(1)}, bf16[1024,128]{1,0:T(8,128)(2,1)S(1)}, u32[]{:S(2)}, u32[]{:S(2)}) collective-permute-start(bf16[1024,128]{1,0:T(8,128)(2,1)S(1)} %get-tuple-element.30.s_prev), channel_id=1, source_target_pairs={{0,1},{1,0},{2,3},{3,2},{4,5},{5,4},{6,7},{7,6},{8,9},{9,8},{10,11... | collective-permute-start | bytes 786440 | tf_op jit(solution)/shard_map/ppermute | solution.py:129
  18.7 1.6 %collective-permute-start.11 = (bf16[1024,128]{1,0:T(8,128)(2,1)S(1)}, bf16[1024,128]{1,0:T(8,128)(2,1)S(1)}, u32[]{:S(2)}, u32[]{:S(2)}) collective-permute-start(bf16[1024,128]{1,0:T(8,128)(2,1)S(1)} %get-tuple-element.31), channel_id=1, source_target_pairs={{0,1},{1,0},{2,3},{3,2},{4,5},{5,4},{6,7},{7,6},{8,9},{9,14},{10,1... | collective-permute-start | bytes 786440 | tf_op jit(solution)/shard_map/ppermute | solution.py:129
  19.2 1.5 %collective-permute-start.12 = (bf16[1024,128]{1,0:T(8,128)(2,1)S(1)}, bf16[1024,128]{1,0:T(8,128)(2,1)S(1)}, u32[]{:S(2)}, u32[]{:S(2)}) collective-permute-start(bf16[1024,128]{1,0:T(8,128)(2,1)S(1)} %step1_kernel.1.q_in.q_prev), channel_id=1, source_target_pairs={{0,1},{1,0},{2,3},{3,2},{4,5},{5,4},{6,7},{7,6},{8,9},{9,13},{10,1... | collective-permute-start | bytes 786440 | tf_op jit(solution)/shard_map/ppermute | solution.py:129
  19.3 1.8 %collective-permute-start.13 = (bf16[1024,128]{1,0:T(8,128)(2,1)S(1)}, bf16[1024,128]{1,0:T(8,128)(2,1)S(1)}, u32[]{:S(2)}, u32[]{:S(2)}) collective-permute-start(bf16[1024,128]{1,0:T(8,128)(2,1)S(1)} %step1_kernel.1.q_in.q_prev), channel_id=1, source_target_pairs={{0,1},{1,5},{2,3},{3,2},{4,0},{5,4},{6,7},{7,6},{8,16},{9,17},{10,... | collective-permute-start | bytes 786440 | tf_op jit(solution)/shard_map/ppermute | solution.py:129
  21.1 2.3 %collective-permute-start.14 = (bf16[1024,128]{1,0:T(8,128)(2,1)S(1)}, bf16[1024,128]{1,0:T(8,128)(2,1)S(1)}, u32[]{:S(2)}, u32[]{:S(2)}) collective-permute-start(bf16[1024,128]{1,0:T(8,128)(2,1)S(1)} %get-tuple-element.34), channel_id=1, source_target_pairs={{0,1},{1,0},{2,3},{3,2},{4,5},{5,4},{6,7},{7,6},{8,9},{9,8},{10,11... | collective-permute-start | bytes 786440 | tf_op jit(solution)/shard_map/ppermute | solution.py:129
  21.5 1.9 %collective-permute-start.15 = (bf16[1024,128]{1,0:T(8,128)(2,1)S(1)}, bf16[1024,128]{1,0:T(8,128)(2,1)S(1)}, u32[]{:S(2)}, u32[]{:S(2)}) collective-permute-start(bf16[1024,128]{1,0:T(8,128)(2,1)S(1)} %get-tuple-element.33.s_ref), channel_id=1, source_target_pairs={{0,1},{1,0},{2,3},{3,2},{4,5},{5,4},{6,7},{7,6},{8,9},{9,8},{10,11... | collective-permute-start | bytes 786440 | tf_op jit(solution)/shard_map/ppermute | solution.py:129
  21.7 1.8 %collective-permute-start.16 = (bf16[1024,128]{1,0:T(8,128)(2,1)S(1)}, bf16[1024,128]{1,0:T(8,128)(2,1)S(1)}, u32[]{:S(2)}, u32[]{:S(2)}) collective-permute-start(bf16[1024,128]{1,0:T(8,128)(2,1)S(1)} %get-tuple-element.35.refs_4_), channel_id=1, source_target_pairs={{0,1},{1,0},{2,3},{3,2},{4,5},{5,4},{6,7},{7,6},{8,9},{9,8},{10,11... | collective-permute-start | bytes 786440 | tf_op jit(solution)/shard_map/ppermute | solution.py:129
  22.1 1.4 %collective-permute-start.17 = (bf16[1024,128]{1,0:T(8,128)(2,1)S(1)}, bf16[1024,128]{1,0:T(8,128)(2,1)S(1)}, u32[]{:S(2)}, u32[]{:S(2)}) collective-permute-start(bf16[1024,128]{1,0:T(8,128)(2,1)S(1)} %get-tuple-element.35.refs_4_), channel_id=1, source_target_pairs={{14,30},{16,24},{20,28},{17,25},{13,5},{9,1}} | collective-permute-start | bytes 786440 | tf_op jit(solution)/shard_map/ppermute | solution.py:133
  23.5 2.1 %collective-permute-start.19 = (bf16[1024,128]{1,0:T(8,128)(2,1)S(1)}, bf16[1024,128]{1,0:T(8,128)(2,1)S(1)}, u32[]{:S(2)}, u32[]{:S(2)}) collective-permute-start(bf16[1024,128]{1,0:T(8,128)(2,1)S(1)} %step3_kernel.1.q_prev), channel_id=1, source_target_pairs={{23,27},{10,18},{30,26}} | collective-permute-start | bytes 786440 | tf_op jit(solution)/shard_map/ppermute | solution.py:133
  24.2 1.4 %collective-permute-start.20 = (bf16[1024,128]{1,0:T(8,128)(2,1)S(1)}, bf16[1024,128]{1,0:T(8,128)(2,1)S(1)}, u32[]{:S(2)}, u32[]{:S(2)}) collective-permute-start(bf16[1024,128]{1,0:T(8,128)(2,1)S(1)} %step3_kernel.1.q_prev), channel_id=1, source_target_pairs={{23,19},{10,2}} | collective-permute-start | bytes 786440 | tf_op jit(solution)/shard_map/ppermute | solution.py:133
  25.7 33.1 %collective-permute-start.22 = (bf16[1040,128]{1,0:T(8,128)(2,1)S(1)}, bf16[1040,128]{1,0:T(8,128)(2,1)S(1)}, u32[]{:S(2)}, u32[]{:S(2)}) collective-permute-start(bf16[1040,128]{1,0:T(8,128)(2,1)S(1)} %get-tuple-element.37.mine_ref), channel_id=1, source_target_pairs={{0,2},{1,3},{2,0},{3,1},{4,6},{5,7},{6,4},{7,5},{8,10},{9,11},{10,... | collective-permute-start | bytes 798728 | tf_op jit(solution)/shard_map/ppermute | solution.py:129
  47.5 11.3 %collective-permute-start.23 = (bf16[1024,128]{1,0:T(8,128)(2,1)S(1)}, bf16[1024,128]{1,0:T(8,128)(2,1)S(1)}, u32[]{:S(2)}, u32[]{:S(2)}) collective-permute-start(bf16[1024,128]{1,0:T(8,128)(2,1)S(1)} %get-tuple-element.36.q_ref), channel_id=1, source_target_pairs={{19,11},{23,15},{27,3},{31,7},{14,6}} | collective-permute-start | bytes 786440 | tf_op jit(solution)/shard_map/ppermute | solution.py:133
  48.8 10.9 %collective-permute-start.24 = (bf16[1040,128]{1,0:T(8,128)(2,1)S(1)}, bf16[1040,128]{1,0:T(8,128)(2,1)S(1)}, u32[]{:S(2)}, u32[]{:S(2)}) collective-permute-start(bf16[1040,128]{1,0:T(8,128)(2,1)S(1)} %get-tuple-element.37.mine_ref), channel_id=1, source_target_pairs={{0,1},{1,0},{2,3},{3,2},{4,5},{5,4},{6,7},{7,6},{8,9},{9,8},{10,11... | collective-permute-start | bytes 798728 | tf_op jit(solution)/shard_map/ppermute | solution.py:129
  58.8 1.5 %collective-permute-start.25 = (bf16[1040,128]{1,0:T(8,128)(2,1)S(1)}, bf16[1040,128]{1,0:T(8,128)(2,1)S(1)}, u32[]{:S(2)}, u32[]{:S(2)}) collective-permute-start(bf16[1040,128]{1,0:T(8,128)(2,1)S(1)} %collective-permute-done.22.across_ref), channel_id=1, source_target_pairs={{0,1},{1,0},{2,3},{3,2},{4,5},{5,4},{6,7},{7,6},{8,9},{9,8},{10,11... | collective-permute-start | bytes 798728 | tf_op jit(solution)/shard_map/ppermute | solution.py:129
  (6 other events, 44.0 us)

commit v22 on v21

--- a/solution.py
+++ b/solution.py
@@ -78,7 +78,7 @@
     (0, 3, 1, 2),
     (1, 3, 0, 2),
 )
-REST = ((2, 3), (3, 3), (0, 3), (1, 3), (1, 2))
+REST = ((3, 3), (0, 3), (1, 3), (1, 2))
 
 
 def hops(a, b):
@@ -152,13 +152,14 @@
     return flag
 
 
-def call(kernel, outs, ins, in_specs, out_specs, scratch=(), limit=16):
+def call(kernel, outs, ins, in_specs, out_specs, scratch=(), limit=16, aliases=None):
     return pl.pallas_call(
         kernel,
         out_shape=outs,
         in_specs=in_specs,
         out_specs=out_specs,
         scratch_shapes=list(scratch),
+        input_output_aliases=aliases or {},
         compiler_params=pltpu.CompilerParams(vmem_limit_bytes=limit << 20),
         name=kernel.func.__name__ if isinstance(kernel, functools.partial) else kernel.__name__,
     )(*ins)
@@ -421,7 +422,7 @@
     return acc
 
 
-def half_kernel(q_ref, rest_ref, rhs_ref, mine_ref, across_ref, solved_ref, out_ref):
+def half_kernel(q_ref, rest_ref, rhs_ref, mine_ref, across_ref, beside_ref, solved_ref, out_ref, acc_ref):
     came = any_of(REST)
 
     @pl.when(came)
@@ -433,12 +434,21 @@
         solved_ref[...] = q_ref[...].astype(jnp.float32)
 
     for i in range(out_ref.shape[0]):
-        out_ref[i] = minus(rhs_ref[i], (mine_ref, across_ref), i)
-
-
-def final_kernel(half_ref, beside_ref, corner_ref, out_ref):
-    for i in range(out_ref.shape[0]):
-        out_ref[i] = minus(half_ref[i], (beside_ref, corner_ref), i)
+        acc_ref[i] = minus(rhs_ref[i], (mine_ref, across_ref, beside_ref), i)
+        out_ref[i] = acc_ref[i]
+
+
+def final_kernel(whole_ref, acc_ref, corner_ref, out_ref, new_v, sem):
+    size = new_v.shape[0]
+    tail = corner_ref[pl.ds(size, TAIL)].astype(jnp.float32)
+    for i in range(acc_ref.shape[0]):
+
+        @pl.when(jnp.max(tail[i : i + 1]) > 0.5)
+        def _():
+            new_v[...] = acc_ref[i] - corner_ref[pl.ds(0, size)].astype(jnp.float32)
+            copy = pltpu.make_async_copy(new_v, out_ref.at[i], sem)
+            copy.start()
+            copy.wait()
 
 
 def on_device_8x4(rhs, diag_inv, blocks, block_rows, counts):
@@ -536,6 +546,7 @@
         [(MAKER[3], (6, 3)), ((2, 2), (4, 2)), ((7, 2), (6, 2))],
         [(MAKER[3], (4, 3)), ((2, 2), (0, 2))],
         [(MAKER[3], (7, 3))],
+        [(MAKER[3], (2, 3))],
     ]
     got = [send_only(q, pairs) for pairs in sends]
     takers = [[b for _, b in pairs] for pairs in sends]
@@ -551,19 +562,27 @@
         return send(value, [((r, c), (r, c ^ step)) for r in range(NR) for c in range(NC)])
 
     across = swap(mine, 2)
-    rest = send_only(q, list(zip(((4, 3), (5, 3), (6, 3), (7, 3), MAKER[2]), REST)))
+    rest = send_only(q, list(zip(((2, 3), (6, 3), (7, 3), MAKER[2]), REST)))
     beside = swap(mine, 1)
     across, rest = lax.optimization_barrier((across, rest))
     corner = swap(across, 1)
     whole_rhs = jax.ShapeDtypeStruct(rhs.shape, jnp.float32)
-    solved, half = call(
+    solved, half, acc = call(
         half_kernel,
-        [jax.ShapeDtypeStruct((size, width), jnp.float32), whole_rhs],
-        [q, rest, rhs, mine, across],
-        [VMEM] * 5,
-        [VMEM] * 2,
-    )
-    remainder = call(final_kernel, whole_rhs, [half, beside, corner], [VMEM] * 3, VMEM)
+        [jax.ShapeDtypeStruct((size, width), jnp.float32), whole_rhs, whole_rhs],
+        [q, rest, rhs, mine, across, beside],
+        [VMEM] * 6,
+        [VMEM] * 3,
+    )
+    remainder = call(
+        final_kernel,
+        whole_rhs,
+        [half, acc, corner],
+        [ANY, VMEM, VMEM],
+        ANY,
+        [pltpu.VMEM((size, width), jnp.float32), dma],
+        aliases={0: 0},
+    )
     return solved[None, None], remainder[:, None]
 
 

time: 62.1 us -> 62.4 us (level)
  waiting for transfers between devices: 14.4 us -> 13.2 us
  Pallas kernels: 2.51 us -> 3.23 us
    pallas_call x12, Pallas kernels: 2.51 us -> 3.23 us  [call(): pl.pallas_call(kernel, out_shape=outs, in_specs=in_specs, out_specs=out_s...]
    ppermute x16, waiting for transfers between devices: 3.08 us -> 2.39 us  [send(): lax.ppermute(value, ('row', 'col'), [(a * NC + b, c * NC + d) for (a, b),...]
    ppermute x10 -> x11, starting transfers between devices: 13.6 us -> 14.3 us  [send_only(): lax.ppermute(value, ('row', 'col'), [(a * NC + b, c * NC + d) for (a, b),...]
    ppermute x10 -> x11, waiting for transfers between devices: 11.3 us -> 10.8 us  [send_only(): lax.ppermute(value, ('row', 'col'), [(a * NC + b, c * NC + d) for (a, b),...]
  transfers between devices with their start and end apart: 26 -> 27, of which waited for: 10 -> 9; matrix products, arithmetic and copies ran while one was open for 0% -> 0% of each run, Pallas kernels for 2% -> 3%
where the time goes in v22:
time: 62.4 us; the launch traced here: 61.5 us
  starting transfers between devices  41.6 us (67%)
  waiting for transfers between devices  13.2 us (21%)
  Pallas kernels  3.23 us (5%)
  between operations  2.22 us (4%)
  local copies, waits for them, and re-layouts  1.32 us (2%)
    ppermute x16, starting transfers between devices, send(): lax.ppermute(value, ('row', 'col'), [(a * NC + b, c * NC + d) for (a, b),...  27.3 us
    ppermute x11, starting transfers between devices, send_only(): lax.ppermute(value, ('row', 'col'), [(a * NC + b, c * NC + d) for (a, b),...  14.3 us
    ppermute x11, waiting for transfers between devices, send_only(): lax.ppermute(value, ('row', 'col'), [(a * NC + b, c * NC + d) for (a, b),...  10.8 us
    pallas_call x12, Pallas kernels, call(): pl.pallas_call(kernel, out_shape=outs, in_specs=in_specs, out_specs=out_s...  3.23 us
    ppermute x16, waiting for transfers between devices, send(): lax.ppermute(value, ('row', 'col'), [(a * NC + b, c * NC + d) for (a, b),...  2.39 us
    unnamed x8, local copies, waits for them, and re-layouts  1.32 us
  transfers between devices with their start and end apart: 27, of which 9 were waited for; matrix products, arithmetic and copies ran while one was open for 0% of the time, Pallas kernels for 3%

profile of v22, /device:TPU:7, one launch (start us, length us, event | category | flops | bytes accessed | tf_op | source)
XLA Modules:
  0.0 61.5 jit_solution(7906385192342635665)
XLA Ops:
  0.6 1.3 %copy-done.2 = bf16[4,128,1024]{2,1,0:T(8,128)(2,1)S(1)} copy-done((bf16[4,128,1024]{2,1,0:T(8,128)(2,1)S(1)}, bf16[4,128,1024]{2,1,0:T(8,128)(2,1)}, u32[]{:S(2)}) %copy-start.2) | copy-done | bytes 1048600
  2.0 0.8 %collective-permute-start.3 = (bf16[128,1024]{1,0:T(8,128)(2,1)S(1)}, bf16[128,1024]{1,0:T(8,128)(2,1)S(1)}, u32[]{:S(2)}, u32[]{:S(2)}) collective-permute-start(bf16[128,1024]{1,0:T(8,128)(2,1)S(1)} %get-tuple-element.26), channel_id=1, source_target_pairs={{24,1},{25,22},{26,13},{27,15},{28,9},{29,23},{30,3},{31,14}} | collective-permute-start | bytes 786440 | tf_op jit(solution)/shard_map/ppermute | solution.py:133
  2.8 0.8 %collective-permute-start.2 = (bf16[128,768]{1,0:T(8,128)(2,1)S(1)}, bf16[128,768]{1,0:T(8,128)(2,1)S(1)}, u32[]{:S(2)}, u32[]{:S(2)}) collective-permute-start(bf16[128,768]{1,0:T(8,128)(2,1)S(1)} %get-tuple-element.25), channel_id=1, source_target_pairs={{16,0},{17,13},{18,22},{19,15},{20,14},{21,9},{23,2}} | collective-permute-start | bytes 589832 | tf_op jit(solution)/shard_map/ppermute | solution.py:133
  3.6 0.7 %collective-permute-start.1 = (bf16[128,512]{1,0:T(8,128)(2,1)S(1)}, bf16[128,512]{1,0:T(8,128)(2,1)S(1)}, u32[]{:S(2)}, u32[]{:S(2)}) collective-permute-start(bf16[128,512]{1,0:T(8,128)(2,1)S(1)} %get-tuple-element.24), channel_id=1, source_target_pairs={{4,0},{8,22},{10,2},{11,15},{12,1},{13,9},{14,23}} | collective-permute-start | bytes 393224 | tf_op jit(solution)/shard_map/ppermute | solution.py:133
  4.3 6.6 %collective-permute-start = (bf16[128,256]{1,0:T(8,128)(2,1)S(1)}, bf16[128,256]{1,0:T(8,128)(2,1)S(1)}, u32[]{:S(2)}, u32[]{:S(2)}) collective-permute-start(bf16[128,256]{1,0:T(8,128)(2,1)S(1)} %get-tuple-element.23), channel_id=1, source_target_pairs={{1,13},{2,15},{3,22},{5,9},{6,14},{7,23}} | collective-permute-start | bytes 196616 | tf_op jit(solution)/shard_map/ppermute | solution.py:133
  11.0 1.3 %collective-permute-done.refs_0_ = bf16[128,256]{1,0:T(8,128)(2,1)S(1)} collective-permute-done((bf16[128,256]{1,0:T(8,128)(2,1)S(1)}, bf16[128,256]{1,0:T(8,128)(2,1)S(1)}, u32[]{:S(2)}, u32[]{:S(2)}) %collective-permute-start) | collective-permute-done | bytes 65568 | tf_op jit(solution)/shard_map/ppermute | solution.py:133
  12.3 2.2 %collective-permute-start.4 = (bf16[128,2560]{1,0:T(8,128)(2,1)S(1)}, bf16[128,2560]{1,0:T(8,128)(2,1)S(1)}, u32[]{:S(2)}, u32[]{:S(2)}) collective-permute-start(bf16[128,2560]{1,0:T(8,128)(2,1)S(1)} %pack_kernel.1), channel_id=1, source_target_pairs={{0,1},{1,0},{2,3},{3,2},{4,5},{5,4},{6,7},{7,6},{8,12},{9,8},{10,1... | collective-permute-start | bytes 1966088 | tf_op jit(solution)/shard_map/ppermute | solution.py:129
  14.7 0.5 collective-permute-start.6
  15.3 0.4 collective-permute-start.8
  15.7 0.7 %collective-permute-done.5.g0 = bf16[256,128]{1,0:T(8,128)(2,1)S(1)} collective-permute-done((bf16[256,128]{1,0:T(8,128)(2,1)S(1)}, bf16[256,128]{1,0:T(8,128)(2,1)S(1)}, u32[]{:S(2)}, u32[]{:S(2)}) %collective-permute-start.5) | collective-permute-done | bytes 65568 | tf_op jit(solution)/shard_map/ppermute | solution.py:129
  18.7 0.4 collective-permute-start.11
  19.7 0.7 %collective-permute-done.11.p_in = bf16[1024,128]{1,0:T(8,128)(2,1)S(1)} collective-permute-done((bf16[1024,128]{1,0:T(8,128)(2,1)S(1)}, bf16[1024,128]{1,0:T(8,128)(2,1)S(1)}, u32[]{:S(2)}, u32[]{:S(2)}) %collective-permute-start.11) | collective-permute-done | bytes 262176 | tf_op jit(solution)/shard_map/ppermute | solution.py:129
  21.1 0.4 collective-permute-start.14
  22.1 0.7 %collective-permute-start.17 = (bf16[1024,128]{1,0:T(8,128)(2,1)S(1)}, bf16[1024,128]{1,0:T(8,128)(2,1)S(1)}, u32[]{:S(2)}, u32[]{:S(2)}) collective-permute-start(bf16[1024,128]{1,0:T(8,128)(2,1)S(1)} %get-tuple-element.36.refs_4_), channel_id=1, source_target_pairs={{14,30},{16,24},{20,28},{17,25},{13,5},{9,1}} | collective-permute-start | bytes 786440 | tf_op jit(solution)/shard_map/ppermute | solution.py:133
  22.7 0.7 %collective-permute-start.18 = (bf16[1024,128]{1,0:T(8,128)(2,1)S(1)}, bf16[1024,128]{1,0:T(8,128)(2,1)S(1)}, u32[]{:S(2)}, u32[]{:S(2)}) collective-permute-start(bf16[1024,128]{1,0:T(8,128)(2,1)S(1)} %get-tuple-element.36.refs_4_), channel_id=1, source_target_pairs={{14,22},{13,29},{17,21}} | collective-permute-start | bytes 786440 | tf_op jit(solution)/shard_map/ppermute | solution.py:133
  23.5 0.7 %collective-permute-start.19 = (bf16[1024,128]{1,0:T(8,128)(2,1)S(1)}, bf16[1024,128]{1,0:T(8,128)(2,1)S(1)}, u32[]{:S(2)}, u32[]{:S(2)}) collective-permute-start(bf16[1024,128]{1,0:T(8,128)(2,1)S(1)} %step3_kernel.1.q_prev), channel_id=1, source_target_pairs={{23,27},{10,18},{30,26}} | collective-permute-start | bytes 786440 | tf_op jit(solution)/shard_map/ppermute | solution.py:133
  24.2 0.7 %collective-permute-start.20 = (bf16[1024,128]{1,0:T(8,128)(2,1)S(1)}, bf16[1024,128]{1,0:T(8,128)(2,1)S(1)}, u32[]{:S(2)}, u32[]{:S(2)}) collective-permute-start(bf16[1024,128]{1,0:T(8,128)(2,1)S(1)} %step3_kernel.1.q_prev), channel_id=1, source_target_pairs={{23,19},{10,2}} | collective-permute-start | bytes 786440 | tf_op jit(solution)/shard_map/ppermute | solution.py:133
  24.9 0.7 %collective-permute-start.21 = (bf16[1024,128]{1,0:T(8,128)(2,1)S(1)}, bf16[1024,128]{1,0:T(8,128)(2,1)S(1)}, u32[]{:S(2)}, u32[]{:S(2)}) collective-permute-start(bf16[1024,128]{1,0:T(8,128)(2,1)S(1)} %step3_kernel.1.q_prev), channel_id=1, source_target_pairs={{23,31}} | collective-permute-start | bytes 786440 | tf_op jit(solution)/shard_map/ppermute | solution.py:133
  25.6 0.7 %collective-permute-start.22 = (bf16[1024,128]{1,0:T(8,128)(2,1)S(1)}, bf16[1024,128]{1,0:T(8,128)(2,1)S(1)}, u32[]{:S(2)}, u32[]{:S(2)}) collective-permute-start(bf16[1024,128]{1,0:T(8,128)(2,1)S(1)} %step3_kernel.1.q_prev), channel_id=1, source_target_pairs={{23,11}} | collective-permute-start | bytes 786440 | tf_op jit(solution)/shard_map/ppermute | solution.py:133
  26.4 21.5 %collective-permute-start.23 = (bf16[1040,128]{1,0:T(8,128)(2,1)S(1)}, bf16[1040,128]{1,0:T(8,128)(2,1)S(1)}, u32[]{:S(2)}, u32[]{:S(2)}) collective-permute-start(bf16[1040,128]{1,0:T(8,128)(2,1)S(1)} %get-tuple-element.38.mine_ref), channel_id=1, source_target_pairs={{0,2},{1,3},{2,0},{3,1},{4,6},{5,7},{6,4},{7,5},{8,10},{9,11},{10,... | collective-permute-start | bytes 798728 | tf_op jit(solution)/shard_map/ppermute | solution.py:129
  47.9 1.3 %collective-permute-start.24 = (bf16[1024,128]{1,0:T(8,128)(2,1)S(1)}, bf16[1024,128]{1,0:T(8,128)(2,1)S(1)}, u32[]{:S(2)}, u32[]{:S(2)}) collective-permute-start(bf16[1024,128]{1,0:T(8,128)(2,1)S(1)} %get-tuple-element.37.q_ref), channel_id=1, source_target_pairs={{11,15},{27,3},{31,7},{14,6}} | collective-permute-start | bytes 786440 | tf_op jit(solution)/shard_map/ppermute | solution.py:133
  49.3 9.5 %collective-permute-done.24.rest_ref = bf16[1024,128]{1,0:T(8,128)(2,1)S(1)} collective-permute-done((bf16[1024,128]{1,0:T(8,128)(2,1)S(1)}, bf16[1024,128]{1,0:T(8,128)(2,1)S(1)}, u32[]{:S(2)}, u32[]{:S(2)}) %collective-permute-start.24) | collective-permute-done | bytes 262176 | tf_op jit(solution)/shard_map/ppermute | solution.py:133
  58.8 1.7 %half_kernel.1 = (f32[1024,128]{1,0:T(8,128)}, f32[2,1024,128]{2,1,0:T(8,128)}, f32[2,1024,128]{2,1,0:T(8,128)S(1)}) custom-call(bf16[1024,128]{1,0:T(8,128)(2,1)S(1)} %get-tuple-element.37.q_ref, bf16[1024,128]{1,0:T(8,128)(2,1)S(1)} %collective-permute-done.24.rest_ref, f32[2,1024,128]{2,1,0:T(8,128)S(1)} %bitcast.14, ...), custom_call_target="tpu_custom_call" | custom-call | tf_op jit(solution)/shard_map/half_kernel/pallas_call | solution.py:156
  60.4 1.1 %final_kernel.1 = f32[2,1024,128]{2,1,0:T(8,128)} custom-call(f32[2,1024,128]{2,1,0:T(8,128)} %get-tuple-element.42.whole_ref, f32[2,1024,128]{2,1,0:T(8,128)S(1)} %get-tuple-element.43.acc_ref, bf16[1040,128]{1,0:T(8,128)(2,1)S(1)} %collective-permute-done.26.corner_ref), custom_call_target="tpu_custom_call", output_to_operand_aliasing={{}: (0, {})} | custom-call | tf_op jit(solution)/shard_map/final_kernel/pallas_call | solution.py:156
  (50 shorter events, 3.4 us)
Async XLA Ops:
  2.0 10.3 %collective-permute-start.3 = (bf16[128,1024]{1,0:T(8,128)(2,1)S(1)}, bf16[128,1024]{1,0:T(8,128)(2,1)S(1)}, u32[]{:S(2)}, u32[]{:S(2)}) collective-permute-start(bf16[128,1024]{1,0:T(8,128)(2,1)S(1)} %get-tuple-element.26), channel_id=1, source_target_pairs={{24,1},{25,22},{26,13},{27,15},{28,9},{29,23},{30,3},{31,14}} | collective-permute-start | bytes 786440 | tf_op jit(solution)/shard_map/ppermute | solution.py:133
  2.8 9.5 %collective-permute-start.2 = (bf16[128,768]{1,0:T(8,128)(2,1)S(1)}, bf16[128,768]{1,0:T(8,128)(2,1)S(1)}, u32[]{:S(2)}, u32[]{:S(2)}) collective-permute-start(bf16[128,768]{1,0:T(8,128)(2,1)S(1)} %get-tuple-element.25), channel_id=1, source_target_pairs={{16,0},{17,13},{18,22},{19,15},{20,14},{21,9},{23,2}} | collective-permute-start | bytes 589832 | tf_op jit(solution)/shard_map/ppermute | solution.py:133
  3.6 8.6 %collective-permute-start.1 = (bf16[128,512]{1,0:T(8,128)(2,1)S(1)}, bf16[128,512]{1,0:T(8,128)(2,1)S(1)}, u32[]{:S(2)}, u32[]{:S(2)}) collective-permute-start(bf16[128,512]{1,0:T(8,128)(2,1)S(1)} %get-tuple-element.24), channel_id=1, source_target_pairs={{4,0},{8,22},{10,2},{11,15},{12,1},{13,9},{14,23}} | collective-permute-start | bytes 393224 | tf_op jit(solution)/shard_map/ppermute | solution.py:133
  4.3 8.0 %collective-permute-start = (bf16[128,256]{1,0:T(8,128)(2,1)S(1)}, bf16[128,256]{1,0:T(8,128)(2,1)S(1)}, u32[]{:S(2)}, u32[]{:S(2)}) collective-permute-start(bf16[128,256]{1,0:T(8,128)(2,1)S(1)} %get-tuple-element.23), channel_id=1, source_target_pairs={{1,13},{2,15},{3,22},{5,9},{6,14},{7,23}} | collective-permute-start | bytes 196616 | tf_op jit(solution)/shard_map/ppermute | solution.py:133
  12.3 6.1 %collective-permute-start.4 = (bf16[128,2560]{1,0:T(8,128)(2,1)S(1)}, bf16[128,2560]{1,0:T(8,128)(2,1)S(1)}, u32[]{:S(2)}, u32[]{:S(2)}) collective-permute-start(bf16[128,2560]{1,0:T(8,128)(2,1)S(1)} %pack_kernel.1), channel_id=1, source_target_pairs={{0,1},{1,0},{2,3},{3,2},{4,5},{5,4},{6,7},{7,6},{8,12},{9,8},{10,1... | collective-permute-start | bytes 1966088 | tf_op jit(solution)/shard_map/ppermute | solution.py:129
  14.6 1.8 %collective-permute-start.5 = (bf16[256,128]{1,0:T(8,128)(2,1)S(1)}, bf16[256,128]{1,0:T(8,128)(2,1)S(1)}, u32[]{:S(2)}, u32[]{:S(2)}) collective-permute-start(bf16[256,128]{1,0:T(8,128)(2,1)S(1)} %first_kernel.1), channel_id=1, source_target_pairs={{0,4},{1,8},{2,12},{3,2},{4,5},{5,0},{6,7},{7,6},{8,9},{9,1},{10,1... | collective-permute-start | bytes 196616 | tf_op jit(solution)/shard_map/ppermute | solution.py:129
  14.7 1.7 %collective-permute-start.6 = (bf16[256,128]{1,0:T(8,128)(2,1)S(1)}, bf16[256,128]{1,0:T(8,128)(2,1)S(1)}, u32[]{:S(2)}, u32[]{:S(2)}) collective-permute-start(bf16[256,128]{1,0:T(8,128)(2,1)S(1)} %first_kernel.1), channel_id=1, source_target_pairs={{0,8},{1,12},{2,3},{3,4},{4,5},{5,0},{6,7},{7,6},{8,9},{9,1},{10,1... | collective-permute-start | bytes 196616 | tf_op jit(solution)/shard_map/ppermute | solution.py:129
  15.2 1.4 %collective-permute-start.7 = (bf16[256,128]{1,0:T(8,128)(2,1)S(1)}, bf16[256,128]{1,0:T(8,128)(2,1)S(1)}, u32[]{:S(2)}, u32[]{:S(2)}) collective-permute-start(bf16[256,128]{1,0:T(8,128)(2,1)S(1)} %first_kernel.1), channel_id=1, source_target_pairs={{0,12},{1,0},{2,4},{3,8},{4,5},{5,1},{6,7},{7,6},{8,9},{9,2},{10,1... | collective-permute-start | bytes 196616 | tf_op jit(solution)/shard_map/ppermute | solution.py:129
  16.7 1.9 %collective-permute-start.9 = (bf16[1024,128]{1,0:T(8,128)(2,1)S(1)}, bf16[1024,128]{1,0:T(8,128)(2,1)S(1)}, u32[]{:S(2)}, u32[]{:S(2)}) collective-permute-start(bf16[1024,128]{1,0:T(8,128)(2,1)S(1)} %get-tuple-element.28), channel_id=1, source_target_pairs={{0,1},{1,0},{2,3},{3,2},{4,9},{5,4},{6,7},{7,6},{8,5},{9,8},{10,11... | collective-permute-start | bytes 786440 | tf_op jit(solution)/shard_map/ppermute | solution.py:129
  17.1 1.6 %collective-permute-start.10 = (bf16[1024,128]{1,0:T(8,128)(2,1)S(1)}, bf16[1024,128]{1,0:T(8,128)(2,1)S(1)}, u32[]{:S(2)}, u32[]{:S(2)}) collective-permute-start(bf16[1024,128]{1,0:T(8,128)(2,1)S(1)} %get-tuple-element.31.s_prev), channel_id=1, source_target_pairs={{0,1},{1,0},{2,3},{3,2},{4,5},{5,4},{6,7},{7,6},{8,9},{9,8},{10,11... | collective-permute-start | bytes 786440 | tf_op jit(solution)/shard_map/ppermute | solution.py:129
  18.7 1.6 %collective-permute-start.11 = (bf16[1024,128]{1,0:T(8,128)(2,1)S(1)}, bf16[1024,128]{1,0:T(8,128)(2,1)S(1)}, u32[]{:S(2)}, u32[]{:S(2)}) collective-permute-start(bf16[1024,128]{1,0:T(8,128)(2,1)S(1)} %get-tuple-element.32), channel_id=1, source_target_pairs={{0,1},{1,0},{2,3},{3,2},{4,5},{5,4},{6,7},{7,6},{8,9},{9,14},{10,1... | collective-permute-start | bytes 786440 | tf_op jit(solution)/shard_map/ppermute | solution.py:129
  19.2 1.5 %collective-permute-start.12 = (bf16[1024,128]{1,0:T(8,128)(2,1)S(1)}, bf16[1024,128]{1,0:T(8,128)(2,1)S(1)}, u32[]{:S(2)}, u32[]{:S(2)}) collective-permute-start(bf16[1024,128]{1,0:T(8,128)(2,1)S(1)} %step1_kernel.1.q_in.q_prev), channel_id=1, source_target_pairs={{0,1},{1,0},{2,3},{3,2},{4,5},{5,4},{6,7},{7,6},{8,9},{9,13},{10,1... | collective-permute-start | bytes 786440 | tf_op jit(solution)/shard_map/ppermute | solution.py:129
  19.3 1.8 %collective-permute-start.13 = (bf16[1024,128]{1,0:T(8,128)(2,1)S(1)}, bf16[1024,128]{1,0:T(8,128)(2,1)S(1)}, u32[]{:S(2)}, u32[]{:S(2)}) collective-permute-start(bf16[1024,128]{1,0:T(8,128)(2,1)S(1)} %step1_kernel.1.q_in.q_prev), channel_id=1, source_target_pairs={{0,1},{1,5},{2,3},{3,2},{4,0},{5,4},{6,7},{7,6},{8,16},{9,17},{10,... | collective-permute-start | bytes 786440 | tf_op jit(solution)/shard_map/ppermute | solution.py:129
  21.1 2.3 %collective-permute-start.14 = (bf16[1024,128]{1,0:T(8,128)(2,1)S(1)}, bf16[1024,128]{1,0:T(8,128)(2,1)S(1)}, u32[]{:S(2)}, u32[]{:S(2)}) collective-permute-start(bf16[1024,128]{1,0:T(8,128)(2,1)S(1)} %get-tuple-element.35), channel_id=1, source_target_pairs={{0,1},{1,0},{2,3},{3,2},{4,5},{5,4},{6,7},{7,6},{8,9},{9,8},{10,11... | collective-permute-start | bytes 786440 | tf_op jit(solution)/shard_map/ppermute | solution.py:129
  21.5 1.9 %collective-permute-start.15 = (bf16[1024,128]{1,0:T(8,128)(2,1)S(1)}, bf16[1024,128]{1,0:T(8,128)(2,1)S(1)}, u32[]{:S(2)}, u32[]{:S(2)}) collective-permute-start(bf16[1024,128]{1,0:T(8,128)(2,1)S(1)} %get-tuple-element.34.s_ref), channel_id=1, source_target_pairs={{0,1},{1,0},{2,3},{3,2},{4,5},{5,4},{6,7},{7,6},{8,9},{9,8},{10,11... | collective-permute-start | bytes 786440 | tf_op jit(solution)/shard_map/ppermute | solution.py:129
  21.7 1.8 %collective-permute-start.16 = (bf16[1024,128]{1,0:T(8,128)(2,1)S(1)}, bf16[1024,128]{1,0:T(8,128)(2,1)S(1)}, u32[]{:S(2)}, u32[]{:S(2)}) collective-permute-start(bf16[1024,128]{1,0:T(8,128)(2,1)S(1)} %get-tuple-element.36.refs_4_), channel_id=1, source_target_pairs={{0,1},{1,0},{2,3},{3,2},{4,5},{5,4},{6,7},{7,6},{8,9},{9,8},{10,11... | collective-permute-start | bytes 786440 | tf_op jit(solution)/shard_map/ppermute | solution.py:129
  22.1 1.4 %collective-permute-start.17 = (bf16[1024,128]{1,0:T(8,128)(2,1)S(1)}, bf16[1024,128]{1,0:T(8,128)(2,1)S(1)}, u32[]{:S(2)}, u32[]{:S(2)}) collective-permute-start(bf16[1024,128]{1,0:T(8,128)(2,1)S(1)} %get-tuple-element.36.refs_4_), channel_id=1, source_target_pairs={{14,30},{16,24},{20,28},{17,25},{13,5},{9,1}} | collective-permute-start | bytes 786440 | tf_op jit(solution)/shard_map/ppermute | solution.py:133
  23.5 2.7 %collective-permute-start.19 = (bf16[1024,128]{1,0:T(8,128)(2,1)S(1)}, bf16[1024,128]{1,0:T(8,128)(2,1)S(1)}, u32[]{:S(2)}, u32[]{:S(2)}) collective-permute-start(bf16[1024,128]{1,0:T(8,128)(2,1)S(1)} %step3_kernel.1.q_prev), channel_id=1, source_target_pairs={{23,27},{10,18},{30,26}} | collective-permute-start | bytes 786440 | tf_op jit(solution)/shard_map/ppermute | solution.py:133
  24.2 2.1 %collective-permute-start.20 = (bf16[1024,128]{1,0:T(8,128)(2,1)S(1)}, bf16[1024,128]{1,0:T(8,128)(2,1)S(1)}, u32[]{:S(2)}, u32[]{:S(2)}) collective-permute-start(bf16[1024,128]{1,0:T(8,128)(2,1)S(1)} %step3_kernel.1.q_prev), channel_id=1, source_target_pairs={{23,19},{10,2}} | collective-permute-start | bytes 786440 | tf_op jit(solution)/shard_map/ppermute | solution.py:133
  24.9 1.4 %collective-permute-start.21 = (bf16[1024,128]{1,0:T(8,128)(2,1)S(1)}, bf16[1024,128]{1,0:T(8,128)(2,1)S(1)}, u32[]{:S(2)}, u32[]{:S(2)}) collective-permute-start(bf16[1024,128]{1,0:T(8,128)(2,1)S(1)} %step3_kernel.1.q_prev), channel_id=1, source_target_pairs={{23,31}} | collective-permute-start | bytes 786440 | tf_op jit(solution)/shard_map/ppermute | solution.py:133
  26.4 32.4 %collective-permute-start.23 = (bf16[1040,128]{1,0:T(8,128)(2,1)S(1)}, bf16[1040,128]{1,0:T(8,128)(2,1)S(1)}, u32[]{:S(2)}, u32[]{:S(2)}) collective-permute-start(bf16[1040,128]{1,0:T(8,128)(2,1)S(1)} %get-tuple-element.38.mine_ref), channel_id=1, source_target_pairs={{0,2},{1,3},{2,0},{3,1},{4,6},{5,7},{6,4},{7,5},{8,10},{9,11},{10,... | collective-permute-start | bytes 798728 | tf_op jit(solution)/shard_map/ppermute | solution.py:129
  47.9 10.9 %collective-permute-start.24 = (bf16[1024,128]{1,0:T(8,128)(2,1)S(1)}, bf16[1024,128]{1,0:T(8,128)(2,1)S(1)}, u32[]{:S(2)}, u32[]{:S(2)}) collective-permute-start(bf16[1024,128]{1,0:T(8,128)(2,1)S(1)} %get-tuple-element.37.q_ref), channel_id=1, source_target_pairs={{11,15},{27,3},{31,7},{14,6}} | collective-permute-start | bytes 786440 | tf_op jit(solution)/shard_map/ppermute | solution.py:133
  49.2 9.6 %collective-permute-start.25 = (bf16[1040,128]{1,0:T(8,128)(2,1)S(1)}, bf16[1040,128]{1,0:T(8,128)(2,1)S(1)}, u32[]{:S(2)}, u32[]{:S(2)}) collective-permute-start(bf16[1040,128]{1,0:T(8,128)(2,1)S(1)} %get-tuple-element.38.mine_ref), channel_id=1, source_target_pairs={{0,1},{1,0},{2,3},{3,2},{4,5},{5,4},{6,7},{7,6},{8,9},{9,8},{10,11... | collective-permute-start | bytes 798728 | tf_op jit(solution)/shard_map/ppermute | solution.py:129
  58.8 1.7 %collective-permute-start.26 = (bf16[1040,128]{1,0:T(8,128)(2,1)S(1)}, bf16[1040,128]{1,0:T(8,128)(2,1)S(1)}, u32[]{:S(2)}, u32[]{:S(2)}) collective-permute-start(bf16[1040,128]{1,0:T(8,128)(2,1)S(1)} %collective-permute-done.23.across_ref), channel_id=1, source_target_pairs={{0,1},{1,0},{2,3},{3,2},{4,5},{5,4},{6,7},{7,6},{8,9},{9,8},{10,11... | collective-permute-start | bytes 798728 | tf_op jit(solution)/shard_map/ppermute | solution.py:129
  (7 other events, 45.4 us)

commit v23 on v21

--- a/solution.py
+++ b/solution.py
@@ -78,7 +78,7 @@
     (0, 3, 1, 2),
     (1, 3, 0, 2),
 )
-REST = ((2, 3), (3, 3), (0, 3), (1, 3), (1, 2))
+REST = ((3, 3), (0, 3), (1, 3), (1, 2))
 
 
 def hops(a, b):
@@ -386,6 +386,18 @@
         q_ref[...] = q_prev[...]
 
 
+def relay_kernel(takers, q_ref, got_ref, out_ref):
+    taken = any_of(takers)
+
+    @pl.when(taken)
+    def _():
+        out_ref[...] = got_ref[...]
+
+    @pl.when(jnp.logical_not(taken))
+    def _():
+        out_ref[...] = q_ref[...]
+
+
 def update_kernel(takers, tail_ref, s_ref, l_ref, q_prev, *refs):
     got, q_ref, out_ref = refs[:-2], refs[-2], refs[-1]
     size = l_ref.shape[0]
@@ -421,7 +433,7 @@
     return acc
 
 
-def half_kernel(q_ref, rest_ref, rhs_ref, mine_ref, across_ref, solved_ref, out_ref):
+def half_kernel(q_ref, rest_ref, rhs_ref, mine_ref, across_ref, beside_ref, solved_ref, out_ref):
     came = any_of(REST)
 
     @pl.when(came)
@@ -433,12 +445,12 @@
         solved_ref[...] = q_ref[...].astype(jnp.float32)
 
     for i in range(out_ref.shape[0]):
-        out_ref[i] = minus(rhs_ref[i], (mine_ref, across_ref), i)
-
-
-def final_kernel(half_ref, beside_ref, corner_ref, out_ref):
+        out_ref[i] = minus(rhs_ref[i], (mine_ref, across_ref, beside_ref), i)
+
+
+def final_kernel(half_ref, corner_ref, out_ref):
     for i in range(out_ref.shape[0]):
-        out_ref[i] = minus(half_ref[i], (beside_ref, corner_ref), i)
+        out_ref[i] = minus(half_ref[i], (corner_ref,), i)
 
 
 def on_device_8x4(rhs, diag_inv, blocks, block_rows, counts):
@@ -538,6 +550,8 @@
         [(MAKER[3], (7, 3))],
     ]
     got = [send_only(q, pairs) for pairs in sends]
+    above = [(2, 3)]
+    came = send_only(q, [(MAKER[3], d) for d in above])
     takers = [[b for _, b in pairs] for pairs in sends]
     q, mine = call(
         functools.partial(update_kernel, takers),
@@ -551,7 +565,8 @@
         return send(value, [((r, c), (r, c ^ step)) for r in range(NR) for c in range(NC)])
 
     across = swap(mine, 2)
-    rest = send_only(q, list(zip(((4, 3), (5, 3), (6, 3), (7, 3), MAKER[2]), REST)))
+    q = call(functools.partial(relay_kernel, above), vec, [q, came], [VMEM] * 2, VMEM)
+    rest = send_only(q, list(zip(((2, 3), (6, 3), (7, 3), MAKER[2]), REST)))
     beside = swap(mine, 1)
     across, rest = lax.optimization_barrier((across, rest))
     corner = swap(across, 1)
@@ -559,11 +574,11 @@
     solved, half = call(
         half_kernel,
         [jax.ShapeDtypeStruct((size, width), jnp.float32), whole_rhs],
-        [q, rest, rhs, mine, across],
-        [VMEM] * 5,
+        [q, rest, rhs, mine, across, beside],
+        [VMEM] * 6,
         [VMEM] * 2,
     )
-    remainder = call(final_kernel, whole_rhs, [half, beside, corner], [VMEM] * 3, VMEM)
+    remainder = call(final_kernel, whole_rhs, [half, corner], [VMEM] * 2, VMEM)
     return solved[None, None], remainder[:, None]
 
 

time: 62.1 us -> 61.9 us (level)
    ppermute x10 -> x11, starting transfers between devices: 13.6 us -> 14.3 us  [send_only(): lax.ppermute(value, ('row', 'col'), [(a * NC + b, c * NC + d) for (a, b),...]
    ppermute x10 -> x11, waiting for transfers between devices: 11.3 us -> 10.8 us  [send_only(): lax.ppermute(value, ('row', 'col'), [(a * NC + b, c * NC + d) for (a, b),...]
    pallas_call x12 -> x13, Pallas kernels: 2.51 us -> 2.42 us  [call(): pl.pallas_call(kernel, out_shape=outs, in_specs=in_specs, out_specs=out_s...]
  transfers between devices with their start and end apart: 26 -> 27, of which waited for: 10 -> 10; matrix products, arithmetic and copies ran while one was open for 0% -> 0% of each run, Pallas kernels for 2% -> 2%
where the time goes in v23:
time: 61.9 us; the launch traced here: 61.4 us
  starting transfers between devices  41.6 us (67%)
  waiting for transfers between devices  13.9 us (22%)
  Pallas kernels  2.42 us (4%)
  between operations  2.22 us (4%)
  local copies, waits for them, and re-layouts  1.32 us (2%)
    ppermute x16, starting transfers between devices, send(): lax.ppermute(value, ('row', 'col'), [(a * NC + b, c * NC + d) for (a, b),...  27.3 us
    ppermute x11, starting transfers between devices, send_only(): lax.ppermute(value, ('row', 'col'), [(a * NC + b, c * NC + d) for (a, b),...  14.3 us
    ppermute x11, waiting for transfers between devices, send_only(): lax.ppermute(value, ('row', 'col'), [(a * NC + b, c * NC + d) for (a, b),...  10.8 us
    ppermute x16, waiting for transfers between devices, send(): lax.ppermute(value, ('row', 'col'), [(a * NC + b, c * NC + d) for (a, b),...  3.07 us
    pallas_call x13, Pallas kernels, call(): pl.pallas_call(kernel, out_shape=outs, in_specs=in_specs, out_specs=out_s...  2.42 us
    unnamed x8, local copies, waits for them, and re-layouts  1.32 us
  transfers between devices with their start and end apart: 27, of which 10 were waited for; matrix products, arithmetic and copies ran while one was open for 0% of the time, Pallas kernels for 2%

profile of v23, /device:TPU:7, one launch (start us, length us, event | category | flops | bytes accessed | tf_op | source)
XLA Modules:
  0.0 61.4 jit_solution(15402239747986502310)
XLA Ops:
  0.6 1.3 %copy-done.2 = bf16[4,128,1024]{2,1,0:T(8,128)(2,1)S(1)} copy-done((bf16[4,128,1024]{2,1,0:T(8,128)(2,1)S(1)}, bf16[4,128,1024]{2,1,0:T(8,128)(2,1)}, u32[]{:S(2)}) %copy-start.2) | copy-done | bytes 1048600
  2.0 0.8 %collective-permute-start.3 = (bf16[128,1024]{1,0:T(8,128)(2,1)S(1)}, bf16[128,1024]{1,0:T(8,128)(2,1)S(1)}, u32[]{:S(2)}, u32[]{:S(2)}) collective-permute-start(bf16[128,1024]{1,0:T(8,128)(2,1)S(1)} %get-tuple-element.25), channel_id=1, source_target_pairs={{24,1},{25,22},{26,13},{27,15},{28,9},{29,23},{30,3},{31,14}} | collective-permute-start | bytes 786440 | tf_op jit(solution)/shard_map/ppermute | solution.py:133
  2.8 0.8 %collective-permute-start.2 = (bf16[128,768]{1,0:T(8,128)(2,1)S(1)}, bf16[128,768]{1,0:T(8,128)(2,1)S(1)}, u32[]{:S(2)}, u32[]{:S(2)}) collective-permute-start(bf16[128,768]{1,0:T(8,128)(2,1)S(1)} %get-tuple-element.24), channel_id=1, source_target_pairs={{16,0},{17,13},{18,22},{19,15},{20,14},{21,9},{23,2}} | collective-permute-start | bytes 589832 | tf_op jit(solution)/shard_map/ppermute | solution.py:133
  3.6 0.7 %collective-permute-start.1 = (bf16[128,512]{1,0:T(8,128)(2,1)S(1)}, bf16[128,512]{1,0:T(8,128)(2,1)S(1)}, u32[]{:S(2)}, u32[]{:S(2)}) collective-permute-start(bf16[128,512]{1,0:T(8,128)(2,1)S(1)} %get-tuple-element.23), channel_id=1, source_target_pairs={{4,0},{8,22},{10,2},{11,15},{12,1},{13,9},{14,23}} | collective-permute-start | bytes 393224 | tf_op jit(solution)/shard_map/ppermute | solution.py:133
  4.3 6.6 %collective-permute-start = (bf16[128,256]{1,0:T(8,128)(2,1)S(1)}, bf16[128,256]{1,0:T(8,128)(2,1)S(1)}, u32[]{:S(2)}, u32[]{:S(2)}) collective-permute-start(bf16[128,256]{1,0:T(8,128)(2,1)S(1)} %get-tuple-element.22), channel_id=1, source_target_pairs={{1,13},{2,15},{3,22},{5,9},{6,14},{7,23}} | collective-permute-start | bytes 196616 | tf_op jit(solution)/shard_map/ppermute | solution.py:133
  11.0 1.3 %collective-permute-done.refs_0_ = bf16[128,256]{1,0:T(8,128)(2,1)S(1)} collective-permute-done((bf16[128,256]{1,0:T(8,128)(2,1)S(1)}, bf16[128,256]{1,0:T(8,128)(2,1)S(1)}, u32[]{:S(2)}, u32[]{:S(2)}) %collective-permute-start) | collective-permute-done | bytes 65568 | tf_op jit(solution)/shard_map/ppermute | solution.py:133
  12.3 2.2 %collective-permute-start.4 = (bf16[128,2560]{1,0:T(8,128)(2,1)S(1)}, bf16[128,2560]{1,0:T(8,128)(2,1)S(1)}, u32[]{:S(2)}, u32[]{:S(2)}) collective-permute-start(bf16[128,2560]{1,0:T(8,128)(2,1)S(1)} %pack_kernel.1), channel_id=1, source_target_pairs={{0,1},{1,0},{2,3},{3,2},{4,5},{5,4},{6,7},{7,6},{8,12},{9,8},{10,1... | collective-permute-start | bytes 1966088 | tf_op jit(solution)/shard_map/ppermute | solution.py:129
  14.7 0.5 collective-permute-start.6
  15.7 0.7 %collective-permute-done.5.g0 = bf16[256,128]{1,0:T(8,128)(2,1)S(1)} collective-permute-done((bf16[256,128]{1,0:T(8,128)(2,1)S(1)}, bf16[256,128]{1,0:T(8,128)(2,1)S(1)}, u32[]{:S(2)}, u32[]{:S(2)}) %collective-permute-start.5) | collective-permute-done | bytes 65568 | tf_op jit(solution)/shard_map/ppermute | solution.py:129
  18.7 0.4 collective-permute-start.11
  19.7 0.7 %collective-permute-done.11.p_in = bf16[1024,128]{1,0:T(8,128)(2,1)S(1)} collective-permute-done((bf16[1024,128]{1,0:T(8,128)(2,1)S(1)}, bf16[1024,128]{1,0:T(8,128)(2,1)S(1)}, u32[]{:S(2)}, u32[]{:S(2)}) %collective-permute-start.11) | collective-permute-done | bytes 262176 | tf_op jit(solution)/shard_map/ppermute | solution.py:129
  21.1 0.4 collective-permute-start.14
  22.1 0.7 %collective-permute-start.17 = (bf16[1024,128]{1,0:T(8,128)(2,1)S(1)}, bf16[1024,128]{1,0:T(8,128)(2,1)S(1)}, u32[]{:S(2)}, u32[]{:S(2)}) collective-permute-start(bf16[1024,128]{1,0:T(8,128)(2,1)S(1)} %get-tuple-element.35.refs_4_), channel_id=1, source_target_pairs={{14,30},{16,24},{20,28},{17,25},{13,5},{9,1}} | collective-permute-start | bytes 786440 | tf_op jit(solution)/shard_map/ppermute | solution.py:133
  22.7 0.7 %collective-permute-start.18 = (bf16[1024,128]{1,0:T(8,128)(2,1)S(1)}, bf16[1024,128]{1,0:T(8,128)(2,1)S(1)}, u32[]{:S(2)}, u32[]{:S(2)}) collective-permute-start(bf16[1024,128]{1,0:T(8,128)(2,1)S(1)} %get-tuple-element.35.refs_4_), channel_id=1, source_target_pairs={{14,22},{13,29},{17,21}} | collective-permute-start | bytes 786440 | tf_op jit(solution)/shard_map/ppermute | solution.py:133
  23.5 0.7 %collective-permute-start.19 = (bf16[1024,128]{1,0:T(8,128)(2,1)S(1)}, bf16[1024,128]{1,0:T(8,128)(2,1)S(1)}, u32[]{:S(2)}, u32[]{:S(2)}) collective-permute-start(bf16[1024,128]{1,0:T(8,128)(2,1)S(1)} %step3_kernel.1.q_prev), channel_id=1, source_target_pairs={{23,27},{10,18},{30,26}} | collective-permute-start | bytes 786440 | tf_op jit(solution)/shard_map/ppermute | solution.py:133
  24.2 0.7 %collective-permute-start.20 = (bf16[1024,128]{1,0:T(8,128)(2,1)S(1)}, bf16[1024,128]{1,0:T(8,128)(2,1)S(1)}, u32[]{:S(2)}, u32[]{:S(2)}) collective-permute-start(bf16[1024,128]{1,0:T(8,128)(2,1)S(1)} %step3_kernel.1.q_prev), channel_id=1, source_target_pairs={{23,19},{10,2}} | collective-permute-start | bytes 786440 | tf_op jit(solution)/shard_map/ppermute | solution.py:133
  24.9 0.7 %collective-permute-start.21 = (bf16[1024,128]{1,0:T(8,128)(2,1)S(1)}, bf16[1024,128]{1,0:T(8,128)(2,1)S(1)}, u32[]{:S(2)}, u32[]{:S(2)}) collective-permute-start(bf16[1024,128]{1,0:T(8,128)(2,1)S(1)} %step3_kernel.1.q_prev), channel_id=1, source_target_pairs={{23,31}} | collective-permute-start | bytes 786440 | tf_op jit(solution)/shard_map/ppermute | solution.py:133
  25.6 0.7 %collective-permute-start.22 = (bf16[1024,128]{1,0:T(8,128)(2,1)S(1)}, bf16[1024,128]{1,0:T(8,128)(2,1)S(1)}, u32[]{:S(2)}, u32[]{:S(2)}) collective-permute-start(bf16[1024,128]{1,0:T(8,128)(2,1)S(1)} %step3_kernel.1.q_prev), channel_id=1, source_target_pairs={{23,11}} | collective-permute-start | bytes 786440 | tf_op jit(solution)/shard_map/ppermute | solution.py:133
  26.4 21.5 %collective-permute-start.23 = (bf16[1040,128]{1,0:T(8,128)(2,1)S(1)}, bf16[1040,128]{1,0:T(8,128)(2,1)S(1)}, u32[]{:S(2)}, u32[]{:S(2)}) collective-permute-start(bf16[1040,128]{1,0:T(8,128)(2,1)S(1)} %get-tuple-element.37.mine_ref), channel_id=1, source_target_pairs={{0,2},{1,3},{2,0},{3,1},{4,6},{5,7},{6,4},{7,5},{8,10},{9,11},{10,... | collective-permute-start | bytes 798728 | tf_op jit(solution)/shard_map/ppermute | solution.py:129
  47.9 1.3 %collective-permute-start.24 = (bf16[1024,128]{1,0:T(8,128)(2,1)S(1)}, bf16[1024,128]{1,0:T(8,128)(2,1)S(1)}, u32[]{:S(2)}, u32[]{:S(2)}) collective-permute-start(bf16[1024,128]{1,0:T(8,128)(2,1)S(1)} %relay_kernel.1.q_ref), channel_id=1, source_target_pairs={{11,15},{27,3},{31,7},{14,6}} | collective-permute-start | bytes 786440 | tf_op jit(solution)/shard_map/ppermute | solution.py:133
  49.3 9.5 %collective-permute-done.24.rest_ref = bf16[1024,128]{1,0:T(8,128)(2,1)S(1)} collective-permute-done((bf16[1024,128]{1,0:T(8,128)(2,1)S(1)}, bf16[1024,128]{1,0:T(8,128)(2,1)S(1)}, u32[]{:S(2)}, u32[]{:S(2)}) %collective-permute-start.24) | collective-permute-done | bytes 262176 | tf_op jit(solution)/shard_map/ppermute | solution.py:133
  58.8 0.9 %half_kernel.1 = (f32[1024,128]{1,0:T(8,128)}, f32[2,1024,128]{2,1,0:T(8,128)S(1)}) custom-call(bf16[1024,128]{1,0:T(8,128)(2,1)S(1)} %relay_kernel.1.q_ref, bf16[1024,128]{1,0:T(8,128)(2,1)S(1)} %collective-permute-done.24.rest_ref, f32[2,1024,128]{2,1,0:T(8,128)S(1)} %bitcast.14, bf16[1040,128]{1,0:T(8,128)(2,1)S(1)} %get-tuple-element.37.mine_ref, ...), custom_call_target="tpu_custom_call" | custom-call | tf_op jit(solution)/shard_map/half_kernel/pallas_call | solution.py:156
  59.7 0.7 %collective-permute-done.26.corner_ref = bf16[1040,128]{1,0:T(8,128)(2,1)S(1)} collective-permute-done((bf16[1040,128]{1,0:T(8,128)(2,1)S(1)}, bf16[1040,128]{1,0:T(8,128)(2,1)S(1)}, u32[]{:S(2)}, u32[]{:S(2)}) %collective-permute-start.26) | collective-permute-done | bytes 266272 | tf_op jit(solution)/shard_map/ppermute | solution.py:129
  60.4 1.1 %final_kernel.1 = f32[2,1024,128]{2,1,0:T(8,128)} custom-call(f32[2,1024,128]{2,1,0:T(8,128)S(1)} %get-tuple-element.41.half_ref, bf16[1040,128]{1,0:T(8,128)(2,1)S(1)} %collective-permute-done.26.corner_ref), custom_call_target="tpu_custom_call" | custom-call | tf_op jit(solution)/shard_map/final_kernel/pallas_call | solution.py:156
  (51 shorter events, 3.8 us)
Async XLA Ops:
  2.0 10.3 %collective-permute-start.3 = (bf16[128,1024]{1,0:T(8,128)(2,1)S(1)}, bf16[128,1024]{1,0:T(8,128)(2,1)S(1)}, u32[]{:S(2)}, u32[]{:S(2)}) collective-permute-start(bf16[128,1024]{1,0:T(8,128)(2,1)S(1)} %get-tuple-element.25), channel_id=1, source_target_pairs={{24,1},{25,22},{26,13},{27,15},{28,9},{29,23},{30,3},{31,14}} | collective-permute-start | bytes 786440 | tf_op jit(solution)/shard_map/ppermute | solution.py:133
  2.8 9.5 %collective-permute-start.2 = (bf16[128,768]{1,0:T(8,128)(2,1)S(1)}, bf16[128,768]{1,0:T(8,128)(2,1)S(1)}, u32[]{:S(2)}, u32[]{:S(2)}) collective-permute-start(bf16[128,768]{1,0:T(8,128)(2,1)S(1)} %get-tuple-element.24), channel_id=1, source_target_pairs={{16,0},{17,13},{18,22},{19,15},{20,14},{21,9},{23,2}} | collective-permute-start | bytes 589832 | tf_op jit(solution)/shard_map/ppermute | solution.py:133
  3.6 8.6 %collective-permute-start.1 = (bf16[128,512]{1,0:T(8,128)(2,1)S(1)}, bf16[128,512]{1,0:T(8,128)(2,1)S(1)}, u32[]{:S(2)}, u32[]{:S(2)}) collective-permute-start(bf16[128,512]{1,0:T(8,128)(2,1)S(1)} %get-tuple-element.23), channel_id=1, source_target_pairs={{4,0},{8,22},{10,2},{11,15},{12,1},{13,9},{14,23}} | collective-permute-start | bytes 393224 | tf_op jit(solution)/shard_map/ppermute | solution.py:133
  4.3 8.0 %collective-permute-start = (bf16[128,256]{1,0:T(8,128)(2,1)S(1)}, bf16[128,256]{1,0:T(8,128)(2,1)S(1)}, u32[]{:S(2)}, u32[]{:S(2)}) collective-permute-start(bf16[128,256]{1,0:T(8,128)(2,1)S(1)} %get-tuple-element.22), channel_id=1, source_target_pairs={{1,13},{2,15},{3,22},{5,9},{6,14},{7,23}} | collective-permute-start | bytes 196616 | tf_op jit(solution)/shard_map/ppermute | solution.py:133
  12.3 6.1 %collective-permute-start.4 = (bf16[128,2560]{1,0:T(8,128)(2,1)S(1)}, bf16[128,2560]{1,0:T(8,128)(2,1)S(1)}, u32[]{:S(2)}, u32[]{:S(2)}) collective-permute-start(bf16[128,2560]{1,0:T(8,128)(2,1)S(1)} %pack_kernel.1), channel_id=1, source_target_pairs={{0,1},{1,0},{2,3},{3,2},{4,5},{5,4},{6,7},{7,6},{8,12},{9,8},{10,1... | collective-permute-start | bytes 1966088 | tf_op jit(solution)/shard_map/ppermute | solution.py:129
  14.6 1.8 %collective-permute-start.5 = (bf16[256,128]{1,0:T(8,128)(2,1)S(1)}, bf16[256,128]{1,0:T(8,128)(2,1)S(1)}, u32[]{:S(2)}, u32[]{:S(2)}) collective-permute-start(bf16[256,128]{1,0:T(8,128)(2,1)S(1)} %first_kernel.1), channel_id=1, source_target_pairs={{0,4},{1,8},{2,12},{3,2},{4,5},{5,0},{6,7},{7,6},{8,9},{9,1},{10,1... | collective-permute-start | bytes 196616 | tf_op jit(solution)/shard_map/ppermute | solution.py:129
  14.7 1.7 %collective-permute-start.6 = (bf16[256,128]{1,0:T(8,128)(2,1)S(1)}, bf16[256,128]{1,0:T(8,128)(2,1)S(1)}, u32[]{:S(2)}, u32[]{:S(2)}) collective-permute-start(bf16[256,128]{1,0:T(8,128)(2,1)S(1)} %first_kernel.1), channel_id=1, source_target_pairs={{0,8},{1,12},{2,3},{3,4},{4,5},{5,0},{6,7},{7,6},{8,9},{9,1},{10,1... | collective-permute-start | bytes 196616 | tf_op jit(solution)/shard_map/ppermute | solution.py:129
  16.7 1.9 %collective-permute-start.9 = (bf16[1024,128]{1,0:T(8,128)(2,1)S(1)}, bf16[1024,128]{1,0:T(8,128)(2,1)S(1)}, u32[]{:S(2)}, u32[]{:S(2)}) collective-permute-start(bf16[1024,128]{1,0:T(8,128)(2,1)S(1)} %get-tuple-element.27), channel_id=1, source_target_pairs={{0,1},{1,0},{2,3},{3,2},{4,9},{5,4},{6,7},{7,6},{8,5},{9,8},{10,11... | collective-permute-start | bytes 786440 | tf_op jit(solution)/shard_map/ppermute | solution.py:129
  17.1 1.6 %collective-permute-start.10 = (bf16[1024,128]{1,0:T(8,128)(2,1)S(1)}, bf16[1024,128]{1,0:T(8,128)(2,1)S(1)}, u32[]{:S(2)}, u32[]{:S(2)}) collective-permute-start(bf16[1024,128]{1,0:T(8,128)(2,1)S(1)} %get-tuple-element.30.s_prev), channel_id=1, source_target_pairs={{0,1},{1,0},{2,3},{3,2},{4,5},{5,4},{6,7},{7,6},{8,9},{9,8},{10,11... | collective-permute-start | bytes 786440 | tf_op jit(solution)/shard_map/ppermute | solution.py:129
  18.7 1.6 %collective-permute-start.11 = (bf16[1024,128]{1,0:T(8,128)(2,1)S(1)}, bf16[1024,128]{1,0:T(8,128)(2,1)S(1)}, u32[]{:S(2)}, u32[]{:S(2)}) collective-permute-start(bf16[1024,128]{1,0:T(8,128)(2,1)S(1)} %get-tuple-element.31), channel_id=1, source_target_pairs={{0,1},{1,0},{2,3},{3,2},{4,5},{5,4},{6,7},{7,6},{8,9},{9,14},{10,1... | collective-permute-start | bytes 786440 | tf_op jit(solution)/shard_map/ppermute | solution.py:129
  19.2 1.5 %collective-permute-start.12 = (bf16[1024,128]{1,0:T(8,128)(2,1)S(1)}, bf16[1024,128]{1,0:T(8,128)(2,1)S(1)}, u32[]{:S(2)}, u32[]{:S(2)}) collective-permute-start(bf16[1024,128]{1,0:T(8,128)(2,1)S(1)} %step1_kernel.1.q_in.q_prev), channel_id=1, source_target_pairs={{0,1},{1,0},{2,3},{3,2},{4,5},{5,4},{6,7},{7,6},{8,9},{9,13},{10,1... | collective-permute-start | bytes 786440 | tf_op jit(solution)/shard_map/ppermute | solution.py:129
  19.3 1.8 %collective-permute-start.13 = (bf16[1024,128]{1,0:T(8,128)(2,1)S(1)}, bf16[1024,128]{1,0:T(8,128)(2,1)S(1)}, u32[]{:S(2)}, u32[]{:S(2)}) collective-permute-start(bf16[1024,128]{1,0:T(8,128)(2,1)S(1)} %step1_kernel.1.q_in.q_prev), channel_id=1, source_target_pairs={{0,1},{1,5},{2,3},{3,2},{4,0},{5,4},{6,7},{7,6},{8,16},{9,17},{10,... | collective-permute-start | bytes 786440 | tf_op jit(solution)/shard_map/ppermute | solution.py:129
  21.1 2.3 %collective-permute-start.14 = (bf16[1024,128]{1,0:T(8,128)(2,1)S(1)}, bf16[1024,128]{1,0:T(8,128)(2,1)S(1)}, u32[]{:S(2)}, u32[]{:S(2)}) collective-permute-start(bf16[1024,128]{1,0:T(8,128)(2,1)S(1)} %get-tuple-element.34), channel_id=1, source_target_pairs={{0,1},{1,0},{2,3},{3,2},{4,5},{5,4},{6,7},{7,6},{8,9},{9,8},{10,11... | collective-permute-start | bytes 786440 | tf_op jit(solution)/shard_map/ppermute | solution.py:129
  21.5 1.9 %collective-permute-start.15 = (bf16[1024,128]{1,0:T(8,128)(2,1)S(1)}, bf16[1024,128]{1,0:T(8,128)(2,1)S(1)}, u32[]{:S(2)}, u32[]{:S(2)}) collective-permute-start(bf16[1024,128]{1,0:T(8,128)(2,1)S(1)} %get-tuple-element.33.s_ref), channel_id=1, source_target_pairs={{0,1},{1,0},{2,3},{3,2},{4,5},{5,4},{6,7},{7,6},{8,9},{9,8},{10,11... | collective-permute-start | bytes 786440 | tf_op jit(solution)/shard_map/ppermute | solution.py:129
  21.7 1.8 %collective-permute-start.16 = (bf16[1024,128]{1,0:T(8,128)(2,1)S(1)}, bf16[1024,128]{1,0:T(8,128)(2,1)S(1)}, u32[]{:S(2)}, u32[]{:S(2)}) collective-permute-start(bf16[1024,128]{1,0:T(8,128)(2,1)S(1)} %get-tuple-element.35.refs_4_), channel_id=1, source_target_pairs={{0,1},{1,0},{2,3},{3,2},{4,5},{5,4},{6,7},{7,6},{8,9},{9,8},{10,11... | collective-permute-start | bytes 786440 | tf_op jit(solution)/shard_map/ppermute | solution.py:129
  22.1 1.4 %collective-permute-start.17 = (bf16[1024,128]{1,0:T(8,128)(2,1)S(1)}, bf16[1024,128]{1,0:T(8,128)(2,1)S(1)}, u32[]{:S(2)}, u32[]{:S(2)}) collective-permute-start(bf16[1024,128]{1,0:T(8,128)(2,1)S(1)} %get-tuple-element.35.refs_4_), channel_id=1, source_target_pairs={{14,30},{16,24},{20,28},{17,25},{13,5},{9,1}} | collective-permute-start | bytes 786440 | tf_op jit(solution)/shard_map/ppermute | solution.py:133
  23.5 2.7 %collective-permute-start.19 = (bf16[1024,128]{1,0:T(8,128)(2,1)S(1)}, bf16[1024,128]{1,0:T(8,128)(2,1)S(1)}, u32[]{:S(2)}, u32[]{:S(2)}) collective-permute-start(bf16[1024,128]{1,0:T(8,128)(2,1)S(1)} %step3_kernel.1.q_prev), channel_id=1, source_target_pairs={{23,27},{10,18},{30,26}} | collective-permute-start | bytes 786440 | tf_op jit(solution)/shard_map/ppermute | solution.py:133
  24.2 2.1 %collective-permute-start.20 = (bf16[1024,128]{1,0:T(8,128)(2,1)S(1)}, bf16[1024,128]{1,0:T(8,128)(2,1)S(1)}, u32[]{:S(2)}, u32[]{:S(2)}) collective-permute-start(bf16[1024,128]{1,0:T(8,128)(2,1)S(1)} %step3_kernel.1.q_prev), channel_id=1, source_target_pairs={{23,19},{10,2}} | collective-permute-start | bytes 786440 | tf_op jit(solution)/shard_map/ppermute | solution.py:133
  24.9 1.4 %collective-permute-start.21 = (bf16[1024,128]{1,0:T(8,128)(2,1)S(1)}, bf16[1024,128]{1,0:T(8,128)(2,1)S(1)}, u32[]{:S(2)}, u32[]{:S(2)}) collective-permute-start(bf16[1024,128]{1,0:T(8,128)(2,1)S(1)} %step3_kernel.1.q_prev), channel_id=1, source_target_pairs={{23,31}} | collective-permute-start | bytes 786440 | tf_op jit(solution)/shard_map/ppermute | solution.py:133
  25.6 22.3 %collective-permute-start.22 = (bf16[1024,128]{1,0:T(8,128)(2,1)S(1)}, bf16[1024,128]{1,0:T(8,128)(2,1)S(1)}, u32[]{:S(2)}, u32[]{:S(2)}) collective-permute-start(bf16[1024,128]{1,0:T(8,128)(2,1)S(1)} %step3_kernel.1.q_prev), channel_id=1, source_target_pairs={{23,11}} | collective-permute-start | bytes 786440 | tf_op jit(solution)/shard_map/ppermute | solution.py:133
  26.4 32.4 %collective-permute-start.23 = (bf16[1040,128]{1,0:T(8,128)(2,1)S(1)}, bf16[1040,128]{1,0:T(8,128)(2,1)S(1)}, u32[]{:S(2)}, u32[]{:S(2)}) collective-permute-start(bf16[1040,128]{1,0:T(8,128)(2,1)S(1)} %get-tuple-element.37.mine_ref), channel_id=1, source_target_pairs={{0,2},{1,3},{2,0},{3,1},{4,6},{5,7},{6,4},{7,5},{8,10},{9,11},{10,... | collective-permute-start | bytes 798728 | tf_op jit(solution)/shard_map/ppermute | solution.py:129
  47.9 10.9 %collective-permute-start.24 = (bf16[1024,128]{1,0:T(8,128)(2,1)S(1)}, bf16[1024,128]{1,0:T(8,128)(2,1)S(1)}, u32[]{:S(2)}, u32[]{:S(2)}) collective-permute-start(bf16[1024,128]{1,0:T(8,128)(2,1)S(1)} %relay_kernel.1.q_ref), channel_id=1, source_target_pairs={{11,15},{27,3},{31,7},{14,6}} | collective-permute-start | bytes 786440 | tf_op jit(solution)/shard_map/ppermute | solution.py:133
  49.2 9.6 %collective-permute-start.25 = (bf16[1040,128]{1,0:T(8,128)(2,1)S(1)}, bf16[1040,128]{1,0:T(8,128)(2,1)S(1)}, u32[]{:S(2)}, u32[]{:S(2)}) collective-permute-start(bf16[1040,128]{1,0:T(8,128)(2,1)S(1)} %get-tuple-element.37.mine_ref), channel_id=1, source_target_pairs={{0,1},{1,0},{2,3},{3,2},{4,5},{5,4},{6,7},{7,6},{8,9},{9,8},{10,11... | collective-permute-start | bytes 798728 | tf_op jit(solution)/shard_map/ppermute | solution.py:129
  58.8 1.5 %collective-permute-start.26 = (bf16[1040,128]{1,0:T(8,128)(2,1)S(1)}, bf16[1040,128]{1,0:T(8,128)(2,1)S(1)}, u32[]{:S(2)}, u32[]{:S(2)}) collective-permute-start(bf16[1040,128]{1,0:T(8,128)(2,1)S(1)} %collective-permute-done.23.across_ref), channel_id=1, source_target_pairs={{0,1},{1,0},{2,3},{3,2},{4,5},{5,4},{6,7},{7,6},{8,9},{9,8},{10,11... | collective-permute-start | bytes 798728 | tf_op jit(solution)/shard_map/ppermute | solution.py:129
  (7 other events, 46.1 us)

commit v24 on v23

--- a/solution.py
+++ b/solution.py
@@ -545,13 +545,13 @@
     )
 
     sends = [
-        [(MAKER[3], (6, 3)), ((2, 2), (4, 2)), ((7, 2), (6, 2))],
-        [(MAKER[3], (4, 3)), ((2, 2), (0, 2))],
+        [(MAKER[3], (6, 3)), ((2, 2), (4, 2))],
+        [(MAKER[3], (4, 3)), ((2, 2), (6, 2))],
         [(MAKER[3], (7, 3))],
     ]
     got = [send_only(q, pairs) for pairs in sends]
-    above = [(2, 3)]
-    came = send_only(q, [(MAKER[3], d) for d in above])
+    above = [(2, 3), (0, 2)]
+    came = send_only(q, list(zip((MAKER[3], (2, 2)), above)))
     takers = [[b for _, b in pairs] for pairs in sends]
     q, mine = call(
         functools.partial(update_kernel, takers),

time: 61.9 us -> 61.9 us (level)
  no operation moved by 1% of the time
where the time goes in v24:
time: 61.9 us; the launch traced here: 61.4 us
  starting transfers between devices  41.6 us (67%)
  waiting for transfers between devices  13.9 us (22%)
  Pallas kernels  2.42 us (4%)
  between operations  2.22 us (4%)
  local copies, waits for them, and re-layouts  1.32 us (2%)
    ppermute x16, starting transfers between devices, send(): lax.ppermute(value, ('row', 'col'), [(a * NC + b, c * NC + d) for (a, b),...  27.3 us
    ppermute x11, starting transfers between devices, send_only(): lax.ppermute(value, ('row', 'col'), [(a * NC + b, c * NC + d) for (a, b),...  14.3 us
    ppermute x11, waiting for transfers between devices, send_only(): lax.ppermute(value, ('row', 'col'), [(a * NC + b, c * NC + d) for (a, b),...  10.8 us
    ppermute x16, waiting for transfers between devices, send(): lax.ppermute(value, ('row', 'col'), [(a * NC + b, c * NC + d) for (a, b),...  3.07 us
    pallas_call x13, Pallas kernels, call(): pl.pallas_call(kernel, out_shape=outs, in_specs=in_specs, out_specs=out_s...  2.42 us
    unnamed x8, local copies, waits for them, and re-layouts  1.32 us
  transfers between devices with their start and end apart: 27, of which 10 were waited for; matrix products, arithmetic and copies ran while one was open for 0% of the time, Pallas kernels for 2%

profile of v24, /device:TPU:7, one launch (start us, length us, event | category | flops | bytes accessed | tf_op | source)
XLA Modules:
  0.0 61.4 jit_solution(17970474744460627203)
XLA Ops:
  0.6 1.3 %copy-done.2 = bf16[4,128,1024]{2,1,0:T(8,128)(2,1)S(1)} copy-done((bf16[4,128,1024]{2,1,0:T(8,128)(2,1)S(1)}, bf16[4,128,1024]{2,1,0:T(8,128)(2,1)}, u32[]{:S(2)}) %copy-start.2) | copy-done | bytes 1048600
  2.0 0.8 %collective-permute-start.3 = (bf16[128,1024]{1,0:T(8,128)(2,1)S(1)}, bf16[128,1024]{1,0:T(8,128)(2,1)S(1)}, u32[]{:S(2)}, u32[]{:S(2)}) collective-permute-start(bf16[128,1024]{1,0:T(8,128)(2,1)S(1)} %get-tuple-element.25), channel_id=1, source_target_pairs={{24,1},{25,22},{26,13},{27,15},{28,9},{29,23},{30,3},{31,14}} | collective-permute-start | bytes 786440 | tf_op jit(solution)/shard_map/ppermute | solution.py:133
  2.8 0.8 %collective-permute-start.2 = (bf16[128,768]{1,0:T(8,128)(2,1)S(1)}, bf16[128,768]{1,0:T(8,128)(2,1)S(1)}, u32[]{:S(2)}, u32[]{:S(2)}) collective-permute-start(bf16[128,768]{1,0:T(8,128)(2,1)S(1)} %get-tuple-element.24), channel_id=1, source_target_pairs={{16,0},{17,13},{18,22},{19,15},{20,14},{21,9},{23,2}} | collective-permute-start | bytes 589832 | tf_op jit(solution)/shard_map/ppermute | solution.py:133
  3.6 0.7 %collective-permute-start.1 = (bf16[128,512]{1,0:T(8,128)(2,1)S(1)}, bf16[128,512]{1,0:T(8,128)(2,1)S(1)}, u32[]{:S(2)}, u32[]{:S(2)}) collective-permute-start(bf16[128,512]{1,0:T(8,128)(2,1)S(1)} %get-tuple-element.23), channel_id=1, source_target_pairs={{4,0},{8,22},{10,2},{11,15},{12,1},{13,9},{14,23}} | collective-permute-start | bytes 393224 | tf_op jit(solution)/shard_map/ppermute | solution.py:133
  4.3 6.6 %collective-permute-start = (bf16[128,256]{1,0:T(8,128)(2,1)S(1)}, bf16[128,256]{1,0:T(8,128)(2,1)S(1)}, u32[]{:S(2)}, u32[]{:S(2)}) collective-permute-start(bf16[128,256]{1,0:T(8,128)(2,1)S(1)} %get-tuple-element.22), channel_id=1, source_target_pairs={{1,13},{2,15},{3,22},{5,9},{6,14},{7,23}} | collective-permute-start | bytes 196616 | tf_op jit(solution)/shard_map/ppermute | solution.py:133
  11.0 1.3 %collective-permute-done.refs_0_ = bf16[128,256]{1,0:T(8,128)(2,1)S(1)} collective-permute-done((bf16[128,256]{1,0:T(8,128)(2,1)S(1)}, bf16[128,256]{1,0:T(8,128)(2,1)S(1)}, u32[]{:S(2)}, u32[]{:S(2)}) %collective-permute-start) | collective-permute-done | bytes 65568 | tf_op jit(solution)/shard_map/ppermute | solution.py:133
  12.3 2.2 %collective-permute-start.4 = (bf16[128,2560]{1,0:T(8,128)(2,1)S(1)}, bf16[128,2560]{1,0:T(8,128)(2,1)S(1)}, u32[]{:S(2)}, u32[]{:S(2)}) collective-permute-start(bf16[128,2560]{1,0:T(8,128)(2,1)S(1)} %pack_kernel.1), channel_id=1, source_target_pairs={{0,1},{1,0},{2,3},{3,2},{4,5},{5,4},{6,7},{7,6},{8,12},{9,8},{10,1... | collective-permute-start | bytes 1966088 | tf_op jit(solution)/shard_map/ppermute | solution.py:129
  14.7 0.5 collective-permute-start.6
  15.7 0.7 %collective-permute-done.5.g0 = bf16[256,128]{1,0:T(8,128)(2,1)S(1)} collective-permute-done((bf16[256,128]{1,0:T(8,128)(2,1)S(1)}, bf16[256,128]{1,0:T(8,128)(2,1)S(1)}, u32[]{:S(2)}, u32[]{:S(2)}) %collective-permute-start.5) | collective-permute-done | bytes 65568 | tf_op jit(solution)/shard_map/ppermute | solution.py:129
  18.7 0.4 collective-permute-start.11
  19.7 0.7 %collective-permute-done.11.p_in = bf16[1024,128]{1,0:T(8,128)(2,1)S(1)} collective-permute-done((bf16[1024,128]{1,0:T(8,128)(2,1)S(1)}, bf16[1024,128]{1,0:T(8,128)(2,1)S(1)}, u32[]{:S(2)}, u32[]{:S(2)}) %collective-permute-start.11) | collective-permute-done | bytes 262176 | tf_op jit(solution)/shard_map/ppermute | solution.py:129
  21.1 0.4 collective-permute-start.14
  22.1 0.7 %collective-permute-start.17 = (bf16[1024,128]{1,0:T(8,128)(2,1)S(1)}, bf16[1024,128]{1,0:T(8,128)(2,1)S(1)}, u32[]{:S(2)}, u32[]{:S(2)}) collective-permute-start(bf16[1024,128]{1,0:T(8,128)(2,1)S(1)} %get-tuple-element.35.refs_4_), channel_id=1, source_target_pairs={{14,30},{16,24},{20,28},{17,25},{13,5},{9,1}} | collective-permute-start | bytes 786440 | tf_op jit(solution)/shard_map/ppermute | solution.py:133
  22.7 0.7 %collective-permute-start.18 = (bf16[1024,128]{1,0:T(8,128)(2,1)S(1)}, bf16[1024,128]{1,0:T(8,128)(2,1)S(1)}, u32[]{:S(2)}, u32[]{:S(2)}) collective-permute-start(bf16[1024,128]{1,0:T(8,128)(2,1)S(1)} %get-tuple-element.35.refs_4_), channel_id=1, source_target_pairs={{14,22},{13,29},{17,21}} | collective-permute-start | bytes 786440 | tf_op jit(solution)/shard_map/ppermute | solution.py:133
  23.5 0.7 %collective-permute-start.19 = (bf16[1024,128]{1,0:T(8,128)(2,1)S(1)}, bf16[1024,128]{1,0:T(8,128)(2,1)S(1)}, u32[]{:S(2)}, u32[]{:S(2)}) collective-permute-start(bf16[1024,128]{1,0:T(8,128)(2,1)S(1)} %step3_kernel.1.q_prev), channel_id=1, source_target_pairs={{23,27},{10,18}} | collective-permute-start | bytes 786440 | tf_op jit(solution)/shard_map/ppermute | solution.py:133
  24.2 0.7 %collective-permute-start.20 = (bf16[1024,128]{1,0:T(8,128)(2,1)S(1)}, bf16[1024,128]{1,0:T(8,128)(2,1)S(1)}, u32[]{:S(2)}, u32[]{:S(2)}) collective-permute-start(bf16[1024,128]{1,0:T(8,128)(2,1)S(1)} %step3_kernel.1.q_prev), channel_id=1, source_target_pairs={{23,19},{10,26}} | collective-permute-start | bytes 786440 | tf_op jit(solution)/shard_map/ppermute | solution.py:133
  24.9 0.7 %collective-permute-start.21 = (bf16[1024,128]{1,0:T(8,128)(2,1)S(1)}, bf16[1024,128]{1,0:T(8,128)(2,1)S(1)}, u32[]{:S(2)}, u32[]{:S(2)}) collective-permute-start(bf16[1024,128]{1,0:T(8,128)(2,1)S(1)} %step3_kernel.1.q_prev), channel_id=1, source_target_pairs={{23,31}} | collective-permute-start | bytes 786440 | tf_op jit(solution)/shard_map/ppermute | solution.py:133
  25.6 0.7 %collective-permute-start.22 = (bf16[1024,128]{1,0:T(8,128)(2,1)S(1)}, bf16[1024,128]{1,0:T(8,128)(2,1)S(1)}, u32[]{:S(2)}, u32[]{:S(2)}) collective-permute-start(bf16[1024,128]{1,0:T(8,128)(2,1)S(1)} %step3_kernel.1.q_prev), channel_id=1, source_target_pairs={{23,11},{10,2}} | collective-permute-start | bytes 786440 | tf_op jit(solution)/shard_map/ppermute | solution.py:133
  26.4 21.5 %collective-permute-start.23 = (bf16[1040,128]{1,0:T(8,128)(2,1)S(1)}, bf16[1040,128]{1,0:T(8,128)(2,1)S(1)}, u32[]{:S(2)}, u32[]{:S(2)}) collective-permute-start(bf16[1040,128]{1,0:T(8,128)(2,1)S(1)} %get-tuple-element.37.mine_ref), channel_id=1, source_target_pairs={{0,2},{1,3},{2,0},{3,1},{4,6},{5,7},{6,4},{7,5},{8,10},{9,11},{10,... | collective-permute-start | bytes 798728 | tf_op jit(solution)/shard_map/ppermute | solution.py:129
  47.9 1.3 %collective-permute-start.24 = (bf16[1024,128]{1,0:T(8,128)(2,1)S(1)}, bf16[1024,128]{1,0:T(8,128)(2,1)S(1)}, u32[]{:S(2)}, u32[]{:S(2)}) collective-permute-start(bf16[1024,128]{1,0:T(8,128)(2,1)S(1)} %relay_kernel.1.q_ref), channel_id=1, source_target_pairs={{11,15},{27,3},{31,7},{14,6}} | collective-permute-start | bytes 786440 | tf_op jit(solution)/shard_map/ppermute | solution.py:133
  49.3 9.5 %collective-permute-done.24.rest_ref = bf16[1024,128]{1,0:T(8,128)(2,1)S(1)} collective-permute-done((bf16[1024,128]{1,0:T(8,128)(2,1)S(1)}, bf16[1024,128]{1,0:T(8,128)(2,1)S(1)}, u32[]{:S(2)}, u32[]{:S(2)}) %collective-permute-start.24) | collective-permute-done | bytes 262176 | tf_op jit(solution)/shard_map/ppermute | solution.py:133
  58.8 0.9 %half_kernel.1 = (f32[1024,128]{1,0:T(8,128)}, f32[2,1024,128]{2,1,0:T(8,128)S(1)}) custom-call(bf16[1024,128]{1,0:T(8,128)(2,1)S(1)} %relay_kernel.1.q_ref, bf16[1024,128]{1,0:T(8,128)(2,1)S(1)} %collective-permute-done.24.rest_ref, f32[2,1024,128]{2,1,0:T(8,128)S(1)} %bitcast.14, bf16[1040,128]{1,0:T(8,128)(2,1)S(1)} %get-tuple-element.37.mine_ref, ...), custom_call_target="tpu_custom_call" | custom-call | tf_op jit(solution)/shard_map/half_kernel/pallas_call | solution.py:156
  59.7 0.7 %collective-permute-done.26.corner_ref = bf16[1040,128]{1,0:T(8,128)(2,1)S(1)} collective-permute-done((bf16[1040,128]{1,0:T(8,128)(2,1)S(1)}, bf16[1040,128]{1,0:T(8,128)(2,1)S(1)}, u32[]{:S(2)}, u32[]{:S(2)}) %collective-permute-start.26) | collective-permute-done | bytes 266272 | tf_op jit(solution)/shard_map/ppermute | solution.py:129
  60.4 1.1 %final_kernel.1 = f32[2,1024,128]{2,1,0:T(8,128)} custom-call(f32[2,1024,128]{2,1,0:T(8,128)S(1)} %get-tuple-element.41.half_ref, bf16[1040,128]{1,0:T(8,128)(2,1)S(1)} %collective-permute-done.26.corner_ref), custom_call_target="tpu_custom_call" | custom-call | tf_op jit(solution)/shard_map/final_kernel/pallas_call | solution.py:156
  (51 shorter events, 3.8 us)
Async XLA Ops:
  2.0 10.3 %collective-permute-start.3 = (bf16[128,1024]{1,0:T(8,128)(2,1)S(1)}, bf16[128,1024]{1,0:T(8,128)(2,1)S(1)}, u32[]{:S(2)}, u32[]{:S(2)}) collective-permute-start(bf16[128,1024]{1,0:T(8,128)(2,1)S(1)} %get-tuple-element.25), channel_id=1, source_target_pairs={{24,1},{25,22},{26,13},{27,15},{28,9},{29,23},{30,3},{31,14}} | collective-permute-start | bytes 786440 | tf_op jit(solution)/shard_map/ppermute | solution.py:133
  2.8 9.5 %collective-permute-start.2 = (bf16[128,768]{1,0:T(8,128)(2,1)S(1)}, bf16[128,768]{1,0:T(8,128)(2,1)S(1)}, u32[]{:S(2)}, u32[]{:S(2)}) collective-permute-start(bf16[128,768]{1,0:T(8,128)(2,1)S(1)} %get-tuple-element.24), channel_id=1, source_target_pairs={{16,0},{17,13},{18,22},{19,15},{20,14},{21,9},{23,2}} | collective-permute-start | bytes 589832 | tf_op jit(solution)/shard_map/ppermute | solution.py:133
  3.6 8.6 %collective-permute-start.1 = (bf16[128,512]{1,0:T(8,128)(2,1)S(1)}, bf16[128,512]{1,0:T(8,128)(2,1)S(1)}, u32[]{:S(2)}, u32[]{:S(2)}) collective-permute-start(bf16[128,512]{1,0:T(8,128)(2,1)S(1)} %get-tuple-element.23), channel_id=1, source_target_pairs={{4,0},{8,22},{10,2},{11,15},{12,1},{13,9},{14,23}} | collective-permute-start | bytes 393224 | tf_op jit(solution)/shard_map/ppermute | solution.py:133
  4.3 8.0 %collective-permute-start = (bf16[128,256]{1,0:T(8,128)(2,1)S(1)}, bf16[128,256]{1,0:T(8,128)(2,1)S(1)}, u32[]{:S(2)}, u32[]{:S(2)}) collective-permute-start(bf16[128,256]{1,0:T(8,128)(2,1)S(1)} %get-tuple-element.22), channel_id=1, source_target_pairs={{1,13},{2,15},{3,22},{5,9},{6,14},{7,23}} | collective-permute-start | bytes 196616 | tf_op jit(solution)/shard_map/ppermute | solution.py:133
  12.3 6.1 %collective-permute-start.4 = (bf16[128,2560]{1,0:T(8,128)(2,1)S(1)}, bf16[128,2560]{1,0:T(8,128)(2,1)S(1)}, u32[]{:S(2)}, u32[]{:S(2)}) collective-permute-start(bf16[128,2560]{1,0:T(8,128)(2,1)S(1)} %pack_kernel.1), channel_id=1, source_target_pairs={{0,1},{1,0},{2,3},{3,2},{4,5},{5,4},{6,7},{7,6},{8,12},{9,8},{10,1... | collective-permute-start | bytes 1966088 | tf_op jit(solution)/shard_map/ppermute | solution.py:129
  14.6 1.8 %collective-permute-start.5 = (bf16[256,128]{1,0:T(8,128)(2,1)S(1)}, bf16[256,128]{1,0:T(8,128)(2,1)S(1)}, u32[]{:S(2)}, u32[]{:S(2)}) collective-permute-start(bf16[256,128]{1,0:T(8,128)(2,1)S(1)} %first_kernel.1), channel_id=1, source_target_pairs={{0,4},{1,8},{2,12},{3,2},{4,5},{5,0},{6,7},{7,6},{8,9},{9,1},{10,1... | collective-permute-start | bytes 196616 | tf_op jit(solution)/shard_map/ppermute | solution.py:129
  14.7 1.7 %collective-permute-start.6 = (bf16[256,128]{1,0:T(8,128)(2,1)S(1)}, bf16[256,128]{1,0:T(8,128)(2,1)S(1)}, u32[]{:S(2)}, u32[]{:S(2)}) collective-permute-start(bf16[256,128]{1,0:T(8,128)(2,1)S(1)} %first_kernel.1), channel_id=1, source_target_pairs={{0,8},{1,12},{2,3},{3,4},{4,5},{5,0},{6,7},{7,6},{8,9},{9,1},{10,1... | collective-permute-start | bytes 196616 | tf_op jit(solution)/shard_map/ppermute | solution.py:129
  16.7 1.9 %collective-permute-start.9 = (bf16[1024,128]{1,0:T(8,128)(2,1)S(1)}, bf16[1024,128]{1,0:T(8,128)(2,1)S(1)}, u32[]{:S(2)}, u32[]{:S(2)}) collective-permute-start(bf16[1024,128]{1,0:T(8,128)(2,1)S(1)} %get-tuple-element.27), channel_id=1, source_target_pairs={{0,1},{1,0},{2,3},{3,2},{4,9},{5,4},{6,7},{7,6},{8,5},{9,8},{10,11... | collective-permute-start | bytes 786440 | tf_op jit(solution)/shard_map/ppermute | solution.py:129
  17.1 1.6 %collective-permute-start.10 = (bf16[1024,128]{1,0:T(8,128)(2,1)S(1)}, bf16[1024,128]{1,0:T(8,128)(2,1)S(1)}, u32[]{:S(2)}, u32[]{:S(2)}) collective-permute-start(bf16[1024,128]{1,0:T(8,128)(2,1)S(1)} %get-tuple-element.30.s_prev), channel_id=1, source_target_pairs={{0,1},{1,0},{2,3},{3,2},{4,5},{5,4},{6,7},{7,6},{8,9},{9,8},{10,11... | collective-permute-start | bytes 786440 | tf_op jit(solution)/shard_map/ppermute | solution.py:129
  18.7 1.6 %collective-permute-start.11 = (bf16[1024,128]{1,0:T(8,128)(2,1)S(1)}, bf16[1024,128]{1,0:T(8,128)(2,1)S(1)}, u32[]{:S(2)}, u32[]{:S(2)}) collective-permute-start(bf16[1024,128]{1,0:T(8,128)(2,1)S(1)} %get-tuple-element.31), channel_id=1, source_target_pairs={{0,1},{1,0},{2,3},{3,2},{4,5},{5,4},{6,7},{7,6},{8,9},{9,14},{10,1... | collective-permute-start | bytes 786440 | tf_op jit(solution)/shard_map/ppermute | solution.py:129
  19.2 1.5 %collective-permute-start.12 = (bf16[1024,128]{1,0:T(8,128)(2,1)S(1)}, bf16[1024,128]{1,0:T(8,128)(2,1)S(1)}, u32[]{:S(2)}, u32[]{:S(2)}) collective-permute-start(bf16[1024,128]{1,0:T(8,128)(2,1)S(1)} %step1_kernel.1.q_in.q_prev), channel_id=1, source_target_pairs={{0,1},{1,0},{2,3},{3,2},{4,5},{5,4},{6,7},{7,6},{8,9},{9,13},{10,1... | collective-permute-start | bytes 786440 | tf_op jit(solution)/shard_map/ppermute | solution.py:129
  19.3 1.8 %collective-permute-start.13 = (bf16[1024,128]{1,0:T(8,128)(2,1)S(1)}, bf16[1024,128]{1,0:T(8,128)(2,1)S(1)}, u32[]{:S(2)}, u32[]{:S(2)}) collective-permute-start(bf16[1024,128]{1,0:T(8,128)(2,1)S(1)} %step1_kernel.1.q_in.q_prev), channel_id=1, source_target_pairs={{0,1},{1,5},{2,3},{3,2},{4,0},{5,4},{6,7},{7,6},{8,16},{9,17},{10,... | collective-permute-start | bytes 786440 | tf_op jit(solution)/shard_map/ppermute | solution.py:129
  21.1 2.3 %collective-permute-start.14 = (bf16[1024,128]{1,0:T(8,128)(2,1)S(1)}, bf16[1024,128]{1,0:T(8,128)(2,1)S(1)}, u32[]{:S(2)}, u32[]{:S(2)}) collective-permute-start(bf16[1024,128]{1,0:T(8,128)(2,1)S(1)} %get-tuple-element.34), channel_id=1, source_target_pairs={{0,1},{1,0},{2,3},{3,2},{4,5},{5,4},{6,7},{7,6},{8,9},{9,8},{10,11... | collective-permute-start | bytes 786440 | tf_op jit(solution)/shard_map/ppermute | solution.py:129
  21.5 1.9 %collective-permute-start.15 = (bf16[1024,128]{1,0:T(8,128)(2,1)S(1)}, bf16[1024,128]{1,0:T(8,128)(2,1)S(1)}, u32[]{:S(2)}, u32[]{:S(2)}) collective-permute-start(bf16[1024,128]{1,0:T(8,128)(2,1)S(1)} %get-tuple-element.33.s_ref), channel_id=1, source_target_pairs={{0,1},{1,0},{2,3},{3,2},{4,5},{5,4},{6,7},{7,6},{8,9},{9,8},{10,11... | collective-permute-start | bytes 786440 | tf_op jit(solution)/shard_map/ppermute | solution.py:129
  21.7 1.8 %collective-permute-start.16 = (bf16[1024,128]{1,0:T(8,128)(2,1)S(1)}, bf16[1024,128]{1,0:T(8,128)(2,1)S(1)}, u32[]{:S(2)}, u32[]{:S(2)}) collective-permute-start(bf16[1024,128]{1,0:T(8,128)(2,1)S(1)} %get-tuple-element.35.refs_4_), channel_id=1, source_target_pairs={{0,1},{1,0},{2,3},{3,2},{4,5},{5,4},{6,7},{7,6},{8,9},{9,8},{10,11... | collective-permute-start | bytes 786440 | tf_op jit(solution)/shard_map/ppermute | solution.py:129
  22.1 1.4 %collective-permute-start.17 = (bf16[1024,128]{1,0:T(8,128)(2,1)S(1)}, bf16[1024,128]{1,0:T(8,128)(2,1)S(1)}, u32[]{:S(2)}, u32[]{:S(2)}) collective-permute-start(bf16[1024,128]{1,0:T(8,128)(2,1)S(1)} %get-tuple-element.35.refs_4_), channel_id=1, source_target_pairs={{14,30},{16,24},{20,28},{17,25},{13,5},{9,1}} | collective-permute-start | bytes 786440 | tf_op jit(solution)/shard_map/ppermute | solution.py:133
  23.5 2.7 %collective-permute-start.19 = (bf16[1024,128]{1,0:T(8,128)(2,1)S(1)}, bf16[1024,128]{1,0:T(8,128)(2,1)S(1)}, u32[]{:S(2)}, u32[]{:S(2)}) collective-permute-start(bf16[1024,128]{1,0:T(8,128)(2,1)S(1)} %step3_kernel.1.q_prev), channel_id=1, source_target_pairs={{23,27},{10,18}} | collective-permute-start | bytes 786440 | tf_op jit(solution)/shard_map/ppermute | solution.py:133
  24.2 2.1 %collective-permute-start.20 = (bf16[1024,128]{1,0:T(8,128)(2,1)S(1)}, bf16[1024,128]{1,0:T(8,128)(2,1)S(1)}, u32[]{:S(2)}, u32[]{:S(2)}) collective-permute-start(bf16[1024,128]{1,0:T(8,128)(2,1)S(1)} %step3_kernel.1.q_prev), channel_id=1, source_target_pairs={{23,19},{10,26}} | collective-permute-start | bytes 786440 | tf_op jit(solution)/shard_map/ppermute | solution.py:133
  24.9 1.4 %collective-permute-start.21 = (bf16[1024,128]{1,0:T(8,128)(2,1)S(1)}, bf16[1024,128]{1,0:T(8,128)(2,1)S(1)}, u32[]{:S(2)}, u32[]{:S(2)}) collective-permute-start(bf16[1024,128]{1,0:T(8,128)(2,1)S(1)} %step3_kernel.1.q_prev), channel_id=1, source_target_pairs={{23,31}} | collective-permute-start | bytes 786440 | tf_op jit(solution)/shard_map/ppermute | solution.py:133
  25.6 22.3 %collective-permute-start.22 = (bf16[1024,128]{1,0:T(8,128)(2,1)S(1)}, bf16[1024,128]{1,0:T(8,128)(2,1)S(1)}, u32[]{:S(2)}, u32[]{:S(2)}) collective-permute-start(bf16[1024,128]{1,0:T(8,128)(2,1)S(1)} %step3_kernel.1.q_prev), channel_id=1, source_target_pairs={{23,11},{10,2}} | collective-permute-start | bytes 786440 | tf_op jit(solution)/shard_map/ppermute | solution.py:133
  26.4 32.4 %collective-permute-start.23 = (bf16[1040,128]{1,0:T(8,128)(2,1)S(1)}, bf16[1040,128]{1,0:T(8,128)(2,1)S(1)}, u32[]{:S(2)}, u32[]{:S(2)}) collective-permute-start(bf16[1040,128]{1,0:T(8,128)(2,1)S(1)} %get-tuple-element.37.mine_ref), channel_id=1, source_target_pairs={{0,2},{1,3},{2,0},{3,1},{4,6},{5,7},{6,4},{7,5},{8,10},{9,11},{10,... | collective-permute-start | bytes 798728 | tf_op jit(solution)/shard_map/ppermute | solution.py:129
  47.9 10.9 %collective-permute-start.24 = (bf16[1024,128]{1,0:T(8,128)(2,1)S(1)}, bf16[1024,128]{1,0:T(8,128)(2,1)S(1)}, u32[]{:S(2)}, u32[]{:S(2)}) collective-permute-start(bf16[1024,128]{1,0:T(8,128)(2,1)S(1)} %relay_kernel.1.q_ref), channel_id=1, source_target_pairs={{11,15},{27,3},{31,7},{14,6}} | collective-permute-start | bytes 786440 | tf_op jit(solution)/shard_map/ppermute | solution.py:133
  49.2 9.6 %collective-permute-start.25 = (bf16[1040,128]{1,0:T(8,128)(2,1)S(1)}, bf16[1040,128]{1,0:T(8,128)(2,1)S(1)}, u32[]{:S(2)}, u32[]{:S(2)}) collective-permute-start(bf16[1040,128]{1,0:T(8,128)(2,1)S(1)} %get-tuple-element.37.mine_ref), channel_id=1, source_target_pairs={{0,1},{1,0},{2,3},{3,2},{4,5},{5,4},{6,7},{7,6},{8,9},{9,8},{10,11... | collective-permute-start | bytes 798728 | tf_op jit(solution)/shard_map/ppermute | solution.py:129
  58.8 1.5 %collective-permute-start.26 = (bf16[1040,128]{1,0:T(8,128)(2,1)S(1)}, bf16[1040,128]{1,0:T(8,128)(2,1)S(1)}, u32[]{:S(2)}, u32[]{:S(2)}) collective-permute-start(bf16[1040,128]{1,0:T(8,128)(2,1)S(1)} %collective-permute-done.23.across_ref), channel_id=1, source_target_pairs={{0,1},{1,0},{2,3},{3,2},{4,5},{5,4},{6,7},{7,6},{8,9},{9,8},{10,11... | collective-permute-start | bytes 798728 | tf_op jit(solution)/shard_map/ppermute | solution.py:129
  (7 other events, 46.1 us)

commit v25 on v24

--- a/solution.py
+++ b/solution.py
@@ -566,7 +566,7 @@
 
     across = swap(mine, 2)
     q = call(functools.partial(relay_kernel, above), vec, [q, came], [VMEM] * 2, VMEM)
-    rest = send_only(q, list(zip(((2, 3), (6, 3), (7, 3), MAKER[2]), REST)))
+    rest = send_only(q, list(zip(((2, 3), (4, 3), MAKER[3], MAKER[2]), REST)))
     beside = swap(mine, 1)
     across, rest = lax.optimization_barrier((across, rest))
     corner = swap(across, 1)

time: 61.9 us -> 62 us (level)
  starting transfers between devices: 41.6 us -> 43.5 us
  waiting for transfers between devices: 13.9 us -> 12.3 us
    ppermute x16, starting transfers between devices: 27.3 us -> 29.3 us  [send(): lax.ppermute(value, ('row', 'col'), [(a * NC + b, c * NC + d) for (a, b),...]
    ppermute x11, waiting for transfers between devices: 10.8 us -> 9.56 us  [send_only(): lax.ppermute(value, ('row', 'col'), [(a * NC + b, c * NC + d) for (a, b),...]
where the time goes in v25:
time: 62 us; the launch traced here: 61.8 us
  starting transfers between devices  43.5 us (70%)
  waiting for transfers between devices  12.3 us (20%)
  Pallas kernels  2.4 us (4%)
  between operations  2.21 us (4%)
  local copies, waits for them, and re-layouts  1.32 us (2%)
    ppermute x16, starting transfers between devices, send(): lax.ppermute(value, ('row', 'col'), [(a * NC + b, c * NC + d) for (a, b),...  29.3 us
    ppermute x11, starting transfers between devices, send_only(): lax.ppermute(value, ('row', 'col'), [(a * NC + b, c * NC + d) for (a, b),...  14.3 us
    ppermute x11, waiting for transfers between devices, send_only(): lax.ppermute(value, ('row', 'col'), [(a * NC + b, c * NC + d) for (a, b),...  9.56 us
    ppermute x16, waiting for transfers between devices, send(): lax.ppermute(value, ('row', 'col'), [(a * NC + b, c * NC + d) for (a, b),...  2.72 us
    pallas_call x13, Pallas kernels, call(): pl.pallas_call(kernel, out_shape=outs, in_specs=in_specs, out_specs=out_s...  2.4 us
    unnamed x8, local copies, waits for them, and re-layouts  1.32 us
  transfers between devices with their start and end apart: 27, of which 10 were waited for; matrix products, arithmetic and copies ran while one was open for 0% of the time, Pallas kernels for 2%

profile of v25, /device:TPU:7, one launch (start us, length us, event | category | flops | bytes accessed | tf_op | source)
XLA Modules:
  0.0 61.8 jit_solution(9291613970742849833)
XLA Ops:
  0.6 1.3 %copy-done.2 = bf16[4,128,1024]{2,1,0:T(8,128)(2,1)S(1)} copy-done((bf16[4,128,1024]{2,1,0:T(8,128)(2,1)S(1)}, bf16[4,128,1024]{2,1,0:T(8,128)(2,1)}, u32[]{:S(2)}) %copy-start.2) | copy-done | bytes 1048600
  2.0 0.8 %collective-permute-start.3 = (bf16[128,1024]{1,0:T(8,128)(2,1)S(1)}, bf16[128,1024]{1,0:T(8,128)(2,1)S(1)}, u32[]{:S(2)}, u32[]{:S(2)}) collective-permute-start(bf16[128,1024]{1,0:T(8,128)(2,1)S(1)} %get-tuple-element.25), channel_id=1, source_target_pairs={{24,1},{25,22},{26,13},{27,15},{28,9},{29,23},{30,3},{31,14}} | collective-permute-start | bytes 786440 | tf_op jit(solution)/shard_map/ppermute | solution.py:133
  2.8 0.8 %collective-permute-start.2 = (bf16[128,768]{1,0:T(8,128)(2,1)S(1)}, bf16[128,768]{1,0:T(8,128)(2,1)S(1)}, u32[]{:S(2)}, u32[]{:S(2)}) collective-permute-start(bf16[128,768]{1,0:T(8,128)(2,1)S(1)} %get-tuple-element.24), channel_id=1, source_target_pairs={{16,0},{17,13},{18,22},{19,15},{20,14},{21,9},{23,2}} | collective-permute-start | bytes 589832 | tf_op jit(solution)/shard_map/ppermute | solution.py:133
  3.6 0.7 %collective-permute-start.1 = (bf16[128,512]{1,0:T(8,128)(2,1)S(1)}, bf16[128,512]{1,0:T(8,128)(2,1)S(1)}, u32[]{:S(2)}, u32[]{:S(2)}) collective-permute-start(bf16[128,512]{1,0:T(8,128)(2,1)S(1)} %get-tuple-element.23), channel_id=1, source_target_pairs={{4,0},{8,22},{10,2},{11,15},{12,1},{13,9},{14,23}} | collective-permute-start | bytes 393224 | tf_op jit(solution)/shard_map/ppermute | solution.py:133
  4.3 6.6 %collective-permute-start = (bf16[128,256]{1,0:T(8,128)(2,1)S(1)}, bf16[128,256]{1,0:T(8,128)(2,1)S(1)}, u32[]{:S(2)}, u32[]{:S(2)}) collective-permute-start(bf16[128,256]{1,0:T(8,128)(2,1)S(1)} %get-tuple-element.22), channel_id=1, source_target_pairs={{1,13},{2,15},{3,22},{5,9},{6,14},{7,23}} | collective-permute-start | bytes 196616 | tf_op jit(solution)/shard_map/ppermute | solution.py:133
  11.0 1.3 %collective-permute-done.refs_0_ = bf16[128,256]{1,0:T(8,128)(2,1)S(1)} collective-permute-done((bf16[128,256]{1,0:T(8,128)(2,1)S(1)}, bf16[128,256]{1,0:T(8,128)(2,1)S(1)}, u32[]{:S(2)}, u32[]{:S(2)}) %collective-permute-start) | collective-permute-done | bytes 65568 | tf_op jit(solution)/shard_map/ppermute | solution.py:133
  12.3 2.2 %collective-permute-start.4 = (bf16[128,2560]{1,0:T(8,128)(2,1)S(1)}, bf16[128,2560]{1,0:T(8,128)(2,1)S(1)}, u32[]{:S(2)}, u32[]{:S(2)}) collective-permute-start(bf16[128,2560]{1,0:T(8,128)(2,1)S(1)} %pack_kernel.1), channel_id=1, source_target_pairs={{0,1},{1,0},{2,3},{3,2},{4,5},{5,4},{6,7},{7,6},{8,12},{9,8},{10,1... | collective-permute-start | bytes 1966088 | tf_op jit(solution)/shard_map/ppermute | solution.py:129
  14.7 0.5 collective-permute-start.6
  15.7 0.7 %collective-permute-done.5.g0 = bf16[256,128]{1,0:T(8,128)(2,1)S(1)} collective-permute-done((bf16[256,128]{1,0:T(8,128)(2,1)S(1)}, bf16[256,128]{1,0:T(8,128)(2,1)S(1)}, u32[]{:S(2)}, u32[]{:S(2)}) %collective-permute-start.5) | collective-permute-done | bytes 65568 | tf_op jit(solution)/shard_map/ppermute | solution.py:129
  18.7 0.4 collective-permute-start.11
  19.7 0.7 %collective-permute-done.11.p_in = bf16[1024,128]{1,0:T(8,128)(2,1)S(1)} collective-permute-done((bf16[1024,128]{1,0:T(8,128)(2,1)S(1)}, bf16[1024,128]{1,0:T(8,128)(2,1)S(1)}, u32[]{:S(2)}, u32[]{:S(2)}) %collective-permute-start.11) | collective-permute-done | bytes 262176 | tf_op jit(solution)/shard_map/ppermute | solution.py:129
  21.1 0.4 collective-permute-start.14
  22.1 0.7 %collective-permute-start.17 = (bf16[1024,128]{1,0:T(8,128)(2,1)S(1)}, bf16[1024,128]{1,0:T(8,128)(2,1)S(1)}, u32[]{:S(2)}, u32[]{:S(2)}) collective-permute-start(bf16[1024,128]{1,0:T(8,128)(2,1)S(1)} %get-tuple-element.35.refs_4_), channel_id=1, source_target_pairs={{14,30},{16,24},{20,28},{17,25},{13,5},{9,1}} | collective-permute-start | bytes 786440 | tf_op jit(solution)/shard_map/ppermute | solution.py:133
  22.7 0.7 %collective-permute-start.18 = (bf16[1024,128]{1,0:T(8,128)(2,1)S(1)}, bf16[1024,128]{1,0:T(8,128)(2,1)S(1)}, u32[]{:S(2)}, u32[]{:S(2)}) collective-permute-start(bf16[1024,128]{1,0:T(8,128)(2,1)S(1)} %get-tuple-element.35.refs_4_), channel_id=1, source_target_pairs={{14,22},{13,29},{17,21}} | collective-permute-start | bytes 786440 | tf_op jit(solution)/shard_map/ppermute | solution.py:133
  23.5 0.7 %collective-permute-start.19 = (bf16[1024,128]{1,0:T(8,128)(2,1)S(1)}, bf16[1024,128]{1,0:T(8,128)(2,1)S(1)}, u32[]{:S(2)}, u32[]{:S(2)}) collective-permute-start(bf16[1024,128]{1,0:T(8,128)(2,1)S(1)} %step3_kernel.1.q_prev), channel_id=1, source_target_pairs={{23,27},{10,18}} | collective-permute-start | bytes 786440 | tf_op jit(solution)/shard_map/ppermute | solution.py:133
  24.2 0.7 %collective-permute-start.20 = (bf16[1024,128]{1,0:T(8,128)(2,1)S(1)}, bf16[1024,128]{1,0:T(8,128)(2,1)S(1)}, u32[]{:S(2)}, u32[]{:S(2)}) collective-permute-start(bf16[1024,128]{1,0:T(8,128)(2,1)S(1)} %step3_kernel.1.q_prev), channel_id=1, source_target_pairs={{23,19},{10,26}} | collective-permute-start | bytes 786440 | tf_op jit(solution)/shard_map/ppermute | solution.py:133
  24.9 0.7 %collective-permute-start.21 = (bf16[1024,128]{1,0:T(8,128)(2,1)S(1)}, bf16[1024,128]{1,0:T(8,128)(2,1)S(1)}, u32[]{:S(2)}, u32[]{:S(2)}) collective-permute-start(bf16[1024,128]{1,0:T(8,128)(2,1)S(1)} %step3_kernel.1.q_prev), channel_id=1, source_target_pairs={{23,31}} | collective-permute-start | bytes 786440 | tf_op jit(solution)/shard_map/ppermute | solution.py:133
  25.6 0.7 %collective-permute-start.22 = (bf16[1024,128]{1,0:T(8,128)(2,1)S(1)}, bf16[1024,128]{1,0:T(8,128)(2,1)S(1)}, u32[]{:S(2)}, u32[]{:S(2)}) collective-permute-start(bf16[1024,128]{1,0:T(8,128)(2,1)S(1)} %step3_kernel.1.q_prev), channel_id=1, source_target_pairs={{23,11},{10,2}} | collective-permute-start | bytes 786440 | tf_op jit(solution)/shard_map/ppermute | solution.py:133
  26.4 21.5 %collective-permute-start.23 = (bf16[1040,128]{1,0:T(8,128)(2,1)S(1)}, bf16[1040,128]{1,0:T(8,128)(2,1)S(1)}, u32[]{:S(2)}, u32[]{:S(2)}) collective-permute-start(bf16[1040,128]{1,0:T(8,128)(2,1)S(1)} %get-tuple-element.37.mine_ref), channel_id=1, source_target_pairs={{0,2},{1,3},{2,0},{3,1},{4,6},{5,7},{6,4},{7,5},{8,10},{9,11},{10,... | collective-permute-start | bytes 798728 | tf_op jit(solution)/shard_map/ppermute | solution.py:129
  47.9 1.3 %collective-permute-start.24 = (bf16[1024,128]{1,0:T(8,128)(2,1)S(1)}, bf16[1024,128]{1,0:T(8,128)(2,1)S(1)}, u32[]{:S(2)}, u32[]{:S(2)}) collective-permute-start(bf16[1024,128]{1,0:T(8,128)(2,1)S(1)} %relay_kernel.1.q_ref), channel_id=1, source_target_pairs={{11,15},{19,3},{23,7},{14,6}} | collective-permute-start | bytes 786440 | tf_op jit(solution)/shard_map/ppermute | solution.py:133
  49.3 8.2 %collective-permute-done.24.rest_ref = bf16[1024,128]{1,0:T(8,128)(2,1)S(1)} collective-permute-done((bf16[1024,128]{1,0:T(8,128)(2,1)S(1)}, bf16[1024,128]{1,0:T(8,128)(2,1)S(1)}, u32[]{:S(2)}, u32[]{:S(2)}) %collective-permute-start.24) | collective-permute-done | bytes 262176 | tf_op jit(solution)/shard_map/ppermute | solution.py:133
  57.5 2.0 %collective-permute-start.26 = (bf16[1040,128]{1,0:T(8,128)(2,1)S(1)}, bf16[1040,128]{1,0:T(8,128)(2,1)S(1)}, u32[]{:S(2)}, u32[]{:S(2)}) collective-permute-start(bf16[1040,128]{1,0:T(8,128)(2,1)S(1)} %collective-permute-done.23.across_ref), channel_id=1, source_target_pairs={{0,1},{1,0},{2,3},{3,2},{4,5},{5,4},{6,7},{7,6},{8,9},{9,8},{10,11... | collective-permute-start | bytes 798728 | tf_op jit(solution)/shard_map/ppermute | solution.py:129
  59.5 0.8 %half_kernel.1 = (f32[1024,128]{1,0:T(8,128)}, f32[2,1024,128]{2,1,0:T(8,128)S(1)}) custom-call(bf16[1024,128]{1,0:T(8,128)(2,1)S(1)} %relay_kernel.1.q_ref, bf16[1024,128]{1,0:T(8,128)(2,1)S(1)} %collective-permute-done.24.rest_ref, f32[2,1024,128]{2,1,0:T(8,128)S(1)} %bitcast.14, bf16[1040,128]{1,0:T(8,128)(2,1)S(1)} %get-tuple-element.37.mine_ref, ...), custom_call_target="tpu_custom_call" | custom-call | tf_op jit(solution)/shard_map/half_kernel/pallas_call | solution.py:156
  60.7 1.1 %final_kernel.1 = f32[2,1024,128]{2,1,0:T(8,128)} custom-call(f32[2,1024,128]{2,1,0:T(8,128)S(1)} %get-tuple-element.41.half_ref, bf16[1040,128]{1,0:T(8,128)(2,1)S(1)} %collective-permute-done.26.corner_ref), custom_call_target="tpu_custom_call" | custom-call | tf_op jit(solution)/shard_map/final_kernel/pallas_call | solution.py:156
  (51 shorter events, 4.2 us)
Async XLA Ops:
  2.0 10.3 %collective-permute-start.3 = (bf16[128,1024]{1,0:T(8,128)(2,1)S(1)}, bf16[128,1024]{1,0:T(8,128)(2,1)S(1)}, u32[]{:S(2)}, u32[]{:S(2)}) collective-permute-start(bf16[128,1024]{1,0:T(8,128)(2,1)S(1)} %get-tuple-element.25), channel_id=1, source_target_pairs={{24,1},{25,22},{26,13},{27,15},{28,9},{29,23},{30,3},{31,14}} | collective-permute-start | bytes 786440 | tf_op jit(solution)/shard_map/ppermute | solution.py:133
  2.8 9.5 %collective-permute-start.2 = (bf16[128,768]{1,0:T(8,128)(2,1)S(1)}, bf16[128,768]{1,0:T(8,128)(2,1)S(1)}, u32[]{:S(2)}, u32[]{:S(2)}) collective-permute-start(bf16[128,768]{1,0:T(8,128)(2,1)S(1)} %get-tuple-element.24), channel_id=1, source_target_pairs={{16,0},{17,13},{18,22},{19,15},{20,14},{21,9},{23,2}} | collective-permute-start | bytes 589832 | tf_op jit(solution)/shard_map/ppermute | solution.py:133
  3.6 8.6 %collective-permute-start.1 = (bf16[128,512]{1,0:T(8,128)(2,1)S(1)}, bf16[128,512]{1,0:T(8,128)(2,1)S(1)}, u32[]{:S(2)}, u32[]{:S(2)}) collective-permute-start(bf16[128,512]{1,0:T(8,128)(2,1)S(1)} %get-tuple-element.23), channel_id=1, source_target_pairs={{4,0},{8,22},{10,2},{11,15},{12,1},{13,9},{14,23}} | collective-permute-start | bytes 393224 | tf_op jit(solution)/shard_map/ppermute | solution.py:133
  4.3 8.0 %collective-permute-start = (bf16[128,256]{1,0:T(8,128)(2,1)S(1)}, bf16[128,256]{1,0:T(8,128)(2,1)S(1)}, u32[]{:S(2)}, u32[]{:S(2)}) collective-permute-start(bf16[128,256]{1,0:T(8,128)(2,1)S(1)} %get-tuple-element.22), channel_id=1, source_target_pairs={{1,13},{2,15},{3,22},{5,9},{6,14},{7,23}} | collective-permute-start | bytes 196616 | tf_op jit(solution)/shard_map/ppermute | solution.py:133
  12.3 6.1 %collective-permute-start.4 = (bf16[128,2560]{1,0:T(8,128)(2,1)S(1)}, bf16[128,2560]{1,0:T(8,128)(2,1)S(1)}, u32[]{:S(2)}, u32[]{:S(2)}) collective-permute-start(bf16[128,2560]{1,0:T(8,128)(2,1)S(1)} %pack_kernel.1), channel_id=1, source_target_pairs={{0,1},{1,0},{2,3},{3,2},{4,5},{5,4},{6,7},{7,6},{8,12},{9,8},{10,1... | collective-permute-start | bytes 1966088 | tf_op jit(solution)/shard_map/ppermute | solution.py:129
  14.6 1.8 %collective-permute-start.5 = (bf16[256,128]{1,0:T(8,128)(2,1)S(1)}, bf16[256,128]{1,0:T(8,128)(2,1)S(1)}, u32[]{:S(2)}, u32[]{:S(2)}) collective-permute-start(bf16[256,128]{1,0:T(8,128)(2,1)S(1)} %first_kernel.1), channel_id=1, source_target_pairs={{0,4},{1,8},{2,12},{3,2},{4,5},{5,0},{6,7},{7,6},{8,9},{9,1},{10,1... | collective-permute-start | bytes 196616 | tf_op jit(solution)/shard_map/ppermute | solution.py:129
  14.7 1.7 %collective-permute-start.6 = (bf16[256,128]{1,0:T(8,128)(2,1)S(1)}, bf16[256,128]{1,0:T(8,128)(2,1)S(1)}, u32[]{:S(2)}, u32[]{:S(2)}) collective-permute-start(bf16[256,128]{1,0:T(8,128)(2,1)S(1)} %first_kernel.1), channel_id=1, source_target_pairs={{0,8},{1,12},{2,3},{3,4},{4,5},{5,0},{6,7},{7,6},{8,9},{9,1},{10,1... | collective-permute-start | bytes 196616 | tf_op jit(solution)/shard_map/ppermute | solution.py:129
  16.7 1.9 %collective-permute-start.9 = (bf16[1024,128]{1,0:T(8,128)(2,1)S(1)}, bf16[1024,128]{1,0:T(8,128)(2,1)S(1)}, u32[]{:S(2)}, u32[]{:S(2)}) collective-permute-start(bf16[1024,128]{1,0:T(8,128)(2,1)S(1)} %get-tuple-element.27), channel_id=1, source_target_pairs={{0,1},{1,0},{2,3},{3,2},{4,9},{5,4},{6,7},{7,6},{8,5},{9,8},{10,11... | collective-permute-start | bytes 786440 | tf_op jit(solution)/shard_map/ppermute | solution.py:129
  17.1 1.6 %collective-permute-start.10 = (bf16[1024,128]{1,0:T(8,128)(2,1)S(1)}, bf16[1024,128]{1,0:T(8,128)(2,1)S(1)}, u32[]{:S(2)}, u32[]{:S(2)}) collective-permute-start(bf16[1024,128]{1,0:T(8,128)(2,1)S(1)} %get-tuple-element.30.s_prev), channel_id=1, source_target_pairs={{0,1},{1,0},{2,3},{3,2},{4,5},{5,4},{6,7},{7,6},{8,9},{9,8},{10,11... | collective-permute-start | bytes 786440 | tf_op jit(solution)/shard_map/ppermute | solution.py:129
  18.7 1.6 %collective-permute-start.11 = (bf16[1024,128]{1,0:T(8,128)(2,1)S(1)}, bf16[1024,128]{1,0:T(8,128)(2,1)S(1)}, u32[]{:S(2)}, u32[]{:S(2)}) collective-permute-start(bf16[1024,128]{1,0:T(8,128)(2,1)S(1)} %get-tuple-element.31), channel_id=1, source_target_pairs={{0,1},{1,0},{2,3},{3,2},{4,5},{5,4},{6,7},{7,6},{8,9},{9,14},{10,1... | collective-permute-start | bytes 786440 | tf_op jit(solution)/shard_map/ppermute | solution.py:129
  19.2 1.5 %collective-permute-start.12 = (bf16[1024,128]{1,0:T(8,128)(2,1)S(1)}, bf16[1024,128]{1,0:T(8,128)(2,1)S(1)}, u32[]{:S(2)}, u32[]{:S(2)}) collective-permute-start(bf16[1024,128]{1,0:T(8,128)(2,1)S(1)} %step1_kernel.1.q_in.q_prev), channel_id=1, source_target_pairs={{0,1},{1,0},{2,3},{3,2},{4,5},{5,4},{6,7},{7,6},{8,9},{9,13},{10,1... | collective-permute-start | bytes 786440 | tf_op jit(solution)/shard_map/ppermute | solution.py:129
  19.3 1.8 %collective-permute-start.13 = (bf16[1024,128]{1,0:T(8,128)(2,1)S(1)}, bf16[1024,128]{1,0:T(8,128)(2,1)S(1)}, u32[]{:S(2)}, u32[]{:S(2)}) collective-permute-start(bf16[1024,128]{1,0:T(8,128)(2,1)S(1)} %step1_kernel.1.q_in.q_prev), channel_id=1, source_target_pairs={{0,1},{1,5},{2,3},{3,2},{4,0},{5,4},{6,7},{7,6},{8,16},{9,17},{10,... | collective-permute-start | bytes 786440 | tf_op jit(solution)/shard_map/ppermute | solution.py:129
  21.1 2.3 %collective-permute-start.14 = (bf16[1024,128]{1,0:T(8,128)(2,1)S(1)}, bf16[1024,128]{1,0:T(8,128)(2,1)S(1)}, u32[]{:S(2)}, u32[]{:S(2)}) collective-permute-start(bf16[1024,128]{1,0:T(8,128)(2,1)S(1)} %get-tuple-element.34), channel_id=1, source_target_pairs={{0,1},{1,0},{2,3},{3,2},{4,5},{5,4},{6,7},{7,6},{8,9},{9,8},{10,11... | collective-permute-start | bytes 786440 | tf_op jit(solution)/shard_map/ppermute | solution.py:129
  21.5 1.9 %collective-permute-start.15 = (bf16[1024,128]{1,0:T(8,128)(2,1)S(1)}, bf16[1024,128]{1,0:T(8,128)(2,1)S(1)}, u32[]{:S(2)}, u32[]{:S(2)}) collective-permute-start(bf16[1024,128]{1,0:T(8,128)(2,1)S(1)} %get-tuple-element.33.s_ref), channel_id=1, source_target_pairs={{0,1},{1,0},{2,3},{3,2},{4,5},{5,4},{6,7},{7,6},{8,9},{9,8},{10,11... | collective-permute-start | bytes 786440 | tf_op jit(solution)/shard_map/ppermute | solution.py:129
  21.7 1.8 %collective-permute-start.16 = (bf16[1024,128]{1,0:T(8,128)(2,1)S(1)}, bf16[1024,128]{1,0:T(8,128)(2,1)S(1)}, u32[]{:S(2)}, u32[]{:S(2)}) collective-permute-start(bf16[1024,128]{1,0:T(8,128)(2,1)S(1)} %get-tuple-element.35.refs_4_), channel_id=1, source_target_pairs={{0,1},{1,0},{2,3},{3,2},{4,5},{5,4},{6,7},{7,6},{8,9},{9,8},{10,11... | collective-permute-start | bytes 786440 | tf_op jit(solution)/shard_map/ppermute | solution.py:129
  22.1 1.4 %collective-permute-start.17 = (bf16[1024,128]{1,0:T(8,128)(2,1)S(1)}, bf16[1024,128]{1,0:T(8,128)(2,1)S(1)}, u32[]{:S(2)}, u32[]{:S(2)}) collective-permute-start(bf16[1024,128]{1,0:T(8,128)(2,1)S(1)} %get-tuple-element.35.refs_4_), channel_id=1, source_target_pairs={{14,30},{16,24},{20,28},{17,25},{13,5},{9,1}} | collective-permute-start | bytes 786440 | tf_op jit(solution)/shard_map/ppermute | solution.py:133
  23.5 2.7 %collective-permute-start.19 = (bf16[1024,128]{1,0:T(8,128)(2,1)S(1)}, bf16[1024,128]{1,0:T(8,128)(2,1)S(1)}, u32[]{:S(2)}, u32[]{:S(2)}) collective-permute-start(bf16[1024,128]{1,0:T(8,128)(2,1)S(1)} %step3_kernel.1.q_prev), channel_id=1, source_target_pairs={{23,27},{10,18}} | collective-permute-start | bytes 786440 | tf_op jit(solution)/shard_map/ppermute | solution.py:133
  24.2 2.1 %collective-permute-start.20 = (bf16[1024,128]{1,0:T(8,128)(2,1)S(1)}, bf16[1024,128]{1,0:T(8,128)(2,1)S(1)}, u32[]{:S(2)}, u32[]{:S(2)}) collective-permute-start(bf16[1024,128]{1,0:T(8,128)(2,1)S(1)} %step3_kernel.1.q_prev), channel_id=1, source_target_pairs={{23,19},{10,26}} | collective-permute-start | bytes 786440 | tf_op jit(solution)/shard_map/ppermute | solution.py:133
  24.9 1.4 %collective-permute-start.21 = (bf16[1024,128]{1,0:T(8,128)(2,1)S(1)}, bf16[1024,128]{1,0:T(8,128)(2,1)S(1)}, u32[]{:S(2)}, u32[]{:S(2)}) collective-permute-start(bf16[1024,128]{1,0:T(8,128)(2,1)S(1)} %step3_kernel.1.q_prev), channel_id=1, source_target_pairs={{23,31}} | collective-permute-start | bytes 786440 | tf_op jit(solution)/shard_map/ppermute | solution.py:133
  25.6 22.3 %collective-permute-start.22 = (bf16[1024,128]{1,0:T(8,128)(2,1)S(1)}, bf16[1024,128]{1,0:T(8,128)(2,1)S(1)}, u32[]{:S(2)}, u32[]{:S(2)}) collective-permute-start(bf16[1024,128]{1,0:T(8,128)(2,1)S(1)} %step3_kernel.1.q_prev), channel_id=1, source_target_pairs={{23,11},{10,2}} | collective-permute-start | bytes 786440 | tf_op jit(solution)/shard_map/ppermute | solution.py:133
  26.4 31.1 %collective-permute-start.23 = (bf16[1040,128]{1,0:T(8,128)(2,1)S(1)}, bf16[1040,128]{1,0:T(8,128)(2,1)S(1)}, u32[]{:S(2)}, u32[]{:S(2)}) collective-permute-start(bf16[1040,128]{1,0:T(8,128)(2,1)S(1)} %get-tuple-element.37.mine_ref), channel_id=1, source_target_pairs={{0,2},{1,3},{2,0},{3,1},{4,6},{5,7},{6,4},{7,5},{8,10},{9,11},{10,... | collective-permute-start | bytes 798728 | tf_op jit(solution)/shard_map/ppermute | solution.py:129
  47.9 9.6 %collective-permute-start.24 = (bf16[1024,128]{1,0:T(8,128)(2,1)S(1)}, bf16[1024,128]{1,0:T(8,128)(2,1)S(1)}, u32[]{:S(2)}, u32[]{:S(2)}) collective-permute-start(bf16[1024,128]{1,0:T(8,128)(2,1)S(1)} %relay_kernel.1.q_ref), channel_id=1, source_target_pairs={{11,15},{19,3},{23,7},{14,6}} | collective-permute-start | bytes 786440 | tf_op jit(solution)/shard_map/ppermute | solution.py:133
  49.2 10.3 %collective-permute-start.25 = (bf16[1040,128]{1,0:T(8,128)(2,1)S(1)}, bf16[1040,128]{1,0:T(8,128)(2,1)S(1)}, u32[]{:S(2)}, u32[]{:S(2)}) collective-permute-start(bf16[1040,128]{1,0:T(8,128)(2,1)S(1)} %get-tuple-element.37.mine_ref), channel_id=1, source_target_pairs={{0,1},{1,0},{2,3},{3,2},{4,5},{5,4},{6,7},{7,6},{8,9},{9,8},{10,11... | collective-permute-start | bytes 798728 | tf_op jit(solution)/shard_map/ppermute | solution.py:129
  57.5 3.1 %collective-permute-start.26 = (bf16[1040,128]{1,0:T(8,128)(2,1)S(1)}, bf16[1040,128]{1,0:T(8,128)(2,1)S(1)}, u32[]{:S(2)}, u32[]{:S(2)}) collective-permute-start(bf16[1040,128]{1,0:T(8,128)(2,1)S(1)} %collective-permute-done.23.across_ref), channel_id=1, source_target_pairs={{0,1},{1,0},{2,3},{3,2},{4,5},{5,4},{6,7},{7,6},{8,9},{9,8},{10,11... | collective-permute-start | bytes 798728 | tf_op jit(solution)/shard_map/ppermute | solution.py:129
  (7 other events, 46.1 us)

commit v26 on v25

--- a/solution.py
+++ b/solution.py
@@ -566,7 +566,7 @@
 
     across = swap(mine, 2)
     q = call(functools.partial(relay_kernel, above), vec, [q, came], [VMEM] * 2, VMEM)
-    rest = send_only(q, list(zip(((2, 3), (4, 3), MAKER[3], MAKER[2]), REST)))
+    rest = send_only(q, list(zip(((2, 3), (4, 3), (7, 3), MAKER[2]), REST)))
     beside = swap(mine, 1)
     across, rest = lax.optimization_barrier((across, rest))
     corner = swap(across, 1)

time: 62 us -> 61.7 us (level)
  starting transfers between devices: 43.5 us -> 41.6 us
  waiting for transfers between devices: 12.3 us -> 13.9 us
    ppermute x16, starting transfers between devices: 29.3 us -> 27.3 us  [send(): lax.ppermute(value, ('row', 'col'), [(a * NC + b, c * NC + d) for (a, b),...]
    ppermute x11, waiting for transfers between devices: 9.56 us -> 10.8 us  [send_only(): lax.ppermute(value, ('row', 'col'), [(a * NC + b, c * NC + d) for (a, b),...]
where the time goes in v26:
time: 61.7 us; the launch traced here: 61.4 us
  starting transfers between devices  41.6 us (67%)
  waiting for transfers between devices  13.9 us (23%)
  Pallas kernels  2.42 us (4%)
  between operations  2.22 us (4%)
  local copies, waits for them, and re-layouts  1.32 us (2%)
    ppermute x16, starting transfers between devices, send(): lax.ppermute(value, ('row', 'col'), [(a * NC + b, c * NC + d) for (a, b),...  27.3 us
    ppermute x11, starting transfers between devices, send_only(): lax.ppermute(value, ('row', 'col'), [(a * NC + b, c * NC + d) for (a, b),...  14.3 us
    ppermute x11, waiting for transfers between devices, send_only(): lax.ppermute(value, ('row', 'col'), [(a * NC + b, c * NC + d) for (a, b),...  10.8 us
    ppermute x16, waiting for transfers between devices, send(): lax.ppermute(value, ('row', 'col'), [(a * NC + b, c * NC + d) for (a, b),...  3.07 us
    pallas_call x13, Pallas kernels, call(): pl.pallas_call(kernel, out_shape=outs, in_specs=in_specs, out_specs=out_s...  2.42 us
    unnamed x8, local copies, waits for them, and re-layouts  1.32 us
  transfers between devices with their start and end apart: 27, of which 10 were waited for; matrix products, arithmetic and copies ran while one was open for 0% of the time, Pallas kernels for 2%

profile of v26, /device:TPU:7, one launch (start us, length us, event | category | flops | bytes accessed | tf_op | source)
XLA Modules:
  0.0 61.4 jit_solution(3267178207698309078)
XLA Ops:
  0.6 1.3 %copy-done.2 = bf16[4,128,1024]{2,1,0:T(8,128)(2,1)S(1)} copy-done((bf16[4,128,1024]{2,1,0:T(8,128)(2,1)S(1)}, bf16[4,128,1024]{2,1,0:T(8,128)(2,1)}, u32[]{:S(2)}) %copy-start.2) | copy-done | bytes 1048600
  2.0 0.8 %collective-permute-start.3 = (bf16[128,1024]{1,0:T(8,128)(2,1)S(1)}, bf16[128,1024]{1,0:T(8,128)(2,1)S(1)}, u32[]{:S(2)}, u32[]{:S(2)}) collective-permute-start(bf16[128,1024]{1,0:T(8,128)(2,1)S(1)} %get-tuple-element.25), channel_id=1, source_target_pairs={{24,1},{25,22},{26,13},{27,15},{28,9},{29,23},{30,3},{31,14}} | collective-permute-start | bytes 786440 | tf_op jit(solution)/shard_map/ppermute | solution.py:133
  2.8 0.8 %collective-permute-start.2 = (bf16[128,768]{1,0:T(8,128)(2,1)S(1)}, bf16[128,768]{1,0:T(8,128)(2,1)S(1)}, u32[]{:S(2)}, u32[]{:S(2)}) collective-permute-start(bf16[128,768]{1,0:T(8,128)(2,1)S(1)} %get-tuple-element.24), channel_id=1, source_target_pairs={{16,0},{17,13},{18,22},{19,15},{20,14},{21,9},{23,2}} | collective-permute-start | bytes 589832 | tf_op jit(solution)/shard_map/ppermute | solution.py:133
  3.6 0.7 %collective-permute-start.1 = (bf16[128,512]{1,0:T(8,128)(2,1)S(1)}, bf16[128,512]{1,0:T(8,128)(2,1)S(1)}, u32[]{:S(2)}, u32[]{:S(2)}) collective-permute-start(bf16[128,512]{1,0:T(8,128)(2,1)S(1)} %get-tuple-element.23), channel_id=1, source_target_pairs={{4,0},{8,22},{10,2},{11,15},{12,1},{13,9},{14,23}} | collective-permute-start | bytes 393224 | tf_op jit(solution)/shard_map/ppermute | solution.py:133
  4.3 6.6 %collective-permute-start = (bf16[128,256]{1,0:T(8,128)(2,1)S(1)}, bf16[128,256]{1,0:T(8,128)(2,1)S(1)}, u32[]{:S(2)}, u32[]{:S(2)}) collective-permute-start(bf16[128,256]{1,0:T(8,128)(2,1)S(1)} %get-tuple-element.22), channel_id=1, source_target_pairs={{1,13},{2,15},{3,22},{5,9},{6,14},{7,23}} | collective-permute-start | bytes 196616 | tf_op jit(solution)/shard_map/ppermute | solution.py:133
  11.0 1.3 %collective-permute-done.refs_0_ = bf16[128,256]{1,0:T(8,128)(2,1)S(1)} collective-permute-done((bf16[128,256]{1,0:T(8,128)(2,1)S(1)}, bf16[128,256]{1,0:T(8,128)(2,1)S(1)}, u32[]{:S(2)}, u32[]{:S(2)}) %collective-permute-start) | collective-permute-done | bytes 65568 | tf_op jit(solution)/shard_map/ppermute | solution.py:133
  12.3 2.2 %collective-permute-start.4 = (bf16[128,2560]{1,0:T(8,128)(2,1)S(1)}, bf16[128,2560]{1,0:T(8,128)(2,1)S(1)}, u32[]{:S(2)}, u32[]{:S(2)}) collective-permute-start(bf16[128,2560]{1,0:T(8,128)(2,1)S(1)} %pack_kernel.1), channel_id=1, source_target_pairs={{0,1},{1,0},{2,3},{3,2},{4,5},{5,4},{6,7},{7,6},{8,12},{9,8},{10,1... | collective-permute-start | bytes 1966088 | tf_op jit(solution)/shard_map/ppermute | solution.py:129
  14.7 0.5 collective-permute-start.6
  15.7 0.7 %collective-permute-done.5.g0 = bf16[256,128]{1,0:T(8,128)(2,1)S(1)} collective-permute-done((bf16[256,128]{1,0:T(8,128)(2,1)S(1)}, bf16[256,128]{1,0:T(8,128)(2,1)S(1)}, u32[]{:S(2)}, u32[]{:S(2)}) %collective-permute-start.5) | collective-permute-done | bytes 65568 | tf_op jit(solution)/shard_map/ppermute | solution.py:129
  18.7 0.4 collective-permute-start.11
  19.7 0.7 %collective-permute-done.11.p_in = bf16[1024,128]{1,0:T(8,128)(2,1)S(1)} collective-permute-done((bf16[1024,128]{1,0:T(8,128)(2,1)S(1)}, bf16[1024,128]{1,0:T(8,128)(2,1)S(1)}, u32[]{:S(2)}, u32[]{:S(2)}) %collective-permute-start.11) | collective-permute-done | bytes 262176 | tf_op jit(solution)/shard_map/ppermute | solution.py:129
  21.1 0.4 collective-permute-start.14
  22.1 0.7 %collective-permute-start.17 = (bf16[1024,128]{1,0:T(8,128)(2,1)S(1)}, bf16[1024,128]{1,0:T(8,128)(2,1)S(1)}, u32[]{:S(2)}, u32[]{:S(2)}) collective-permute-start(bf16[1024,128]{1,0:T(8,128)(2,1)S(1)} %get-tuple-element.35.refs_4_), channel_id=1, source_target_pairs={{14,30},{16,24},{20,28},{17,25},{13,5},{9,1}} | collective-permute-start | bytes 786440 | tf_op jit(solution)/shard_map/ppermute | solution.py:133
  22.7 0.7 %collective-permute-start.18 = (bf16[1024,128]{1,0:T(8,128)(2,1)S(1)}, bf16[1024,128]{1,0:T(8,128)(2,1)S(1)}, u32[]{:S(2)}, u32[]{:S(2)}) collective-permute-start(bf16[1024,128]{1,0:T(8,128)(2,1)S(1)} %get-tuple-element.35.refs_4_), channel_id=1, source_target_pairs={{14,22},{13,29},{17,21}} | collective-permute-start | bytes 786440 | tf_op jit(solution)/shard_map/ppermute | solution.py:133
  23.5 0.7 %collective-permute-start.19 = (bf16[1024,128]{1,0:T(8,128)(2,1)S(1)}, bf16[1024,128]{1,0:T(8,128)(2,1)S(1)}, u32[]{:S(2)}, u32[]{:S(2)}) collective-permute-start(bf16[1024,128]{1,0:T(8,128)(2,1)S(1)} %step3_kernel.1.q_prev), channel_id=1, source_target_pairs={{23,27},{10,18}} | collective-permute-start | bytes 786440 | tf_op jit(solution)/shard_map/ppermute | solution.py:133
  24.2 0.7 %collective-permute-start.20 = (bf16[1024,128]{1,0:T(8,128)(2,1)S(1)}, bf16[1024,128]{1,0:T(8,128)(2,1)S(1)}, u32[]{:S(2)}, u32[]{:S(2)}) collective-permute-start(bf16[1024,128]{1,0:T(8,128)(2,1)S(1)} %step3_kernel.1.q_prev), channel_id=1, source_target_pairs={{23,19},{10,26}} | collective-permute-start | bytes 786440 | tf_op jit(solution)/shard_map/ppermute | solution.py:133
  24.9 0.7 %collective-permute-start.21 = (bf16[1024,128]{1,0:T(8,128)(2,1)S(1)}, bf16[1024,128]{1,0:T(8,128)(2,1)S(1)}, u32[]{:S(2)}, u32[]{:S(2)}) collective-permute-start(bf16[1024,128]{1,0:T(8,128)(2,1)S(1)} %step3_kernel.1.q_prev), channel_id=1, source_target_pairs={{23,31}} | collective-permute-start | bytes 786440 | tf_op jit(solution)/shard_map/ppermute | solution.py:133
  25.6 0.7 %collective-permute-start.22 = (bf16[1024,128]{1,0:T(8,128)(2,1)S(1)}, bf16[1024,128]{1,0:T(8,128)(2,1)S(1)}, u32[]{:S(2)}, u32[]{:S(2)}) collective-permute-start(bf16[1024,128]{1,0:T(8,128)(2,1)S(1)} %step3_kernel.1.q_prev), channel_id=1, source_target_pairs={{23,11},{10,2}} | collective-permute-start | bytes 786440 | tf_op jit(solution)/shard_map/ppermute | solution.py:133
  26.4 21.5 %collective-permute-start.23 = (bf16[1040,128]{1,0:T(8,128)(2,1)S(1)}, bf16[1040,128]{1,0:T(8,128)(2,1)S(1)}, u32[]{:S(2)}, u32[]{:S(2)}) collective-permute-start(bf16[1040,128]{1,0:T(8,128)(2,1)S(1)} %get-tuple-element.37.mine_ref), channel_id=1, source_target_pairs={{0,2},{1,3},{2,0},{3,1},{4,6},{5,7},{6,4},{7,5},{8,10},{9,11},{10,... | collective-permute-start | bytes 798728 | tf_op jit(solution)/shard_map/ppermute | solution.py:129
  47.9 1.3 %collective-permute-start.24 = (bf16[1024,128]{1,0:T(8,128)(2,1)S(1)}, bf16[1024,128]{1,0:T(8,128)(2,1)S(1)}, u32[]{:S(2)}, u32[]{:S(2)}) collective-permute-start(bf16[1024,128]{1,0:T(8,128)(2,1)S(1)} %relay_kernel.1.q_ref), channel_id=1, source_target_pairs={{11,15},{19,3},{31,7},{14,6}} | collective-permute-start | bytes 786440 | tf_op jit(solution)/shard_map/ppermute | solution.py:133
  49.3 9.5 %collective-permute-done.24.rest_ref = bf16[1024,128]{1,0:T(8,128)(2,1)S(1)} collective-permute-done((bf16[1024,128]{1,0:T(8,128)(2,1)S(1)}, bf16[1024,128]{1,0:T(8,128)(2,1)S(1)}, u32[]{:S(2)}, u32[]{:S(2)}) %collective-permute-start.24) | collective-permute-done | bytes 262176 | tf_op jit(solution)/shard_map/ppermute | solution.py:133
  58.8 0.9 %half_kernel.1 = (f32[1024,128]{1,0:T(8,128)}, f32[2,1024,128]{2,1,0:T(8,128)S(1)}) custom-call(bf16[1024,128]{1,0:T(8,128)(2,1)S(1)} %relay_kernel.1.q_ref, bf16[1024,128]{1,0:T(8,128)(2,1)S(1)} %collective-permute-done.24.rest_ref, f32[2,1024,128]{2,1,0:T(8,128)S(1)} %bitcast.14, bf16[1040,128]{1,0:T(8,128)(2,1)S(1)} %get-tuple-element.37.mine_ref, ...), custom_call_target="tpu_custom_call" | custom-call | tf_op jit(solution)/shard_map/half_kernel/pallas_call | solution.py:156
  59.7 0.7 %collective-permute-done.26.corner_ref = bf16[1040,128]{1,0:T(8,128)(2,1)S(1)} collective-permute-done((bf16[1040,128]{1,0:T(8,128)(2,1)S(1)}, bf16[1040,128]{1,0:T(8,128)(2,1)S(1)}, u32[]{:S(2)}, u32[]{:S(2)}) %collective-permute-start.26) | collective-permute-done | bytes 266272 | tf_op jit(solution)/shard_map/ppermute | solution.py:129
  60.4 1.1 %final_kernel.1 = f32[2,1024,128]{2,1,0:T(8,128)} custom-call(f32[2,1024,128]{2,1,0:T(8,128)S(1)} %get-tuple-element.41.half_ref, bf16[1040,128]{1,0:T(8,128)(2,1)S(1)} %collective-permute-done.26.corner_ref), custom_call_target="tpu_custom_call" | custom-call | tf_op jit(solution)/shard_map/final_kernel/pallas_call | solution.py:156
  (51 shorter events, 3.8 us)
Async XLA Ops:
  2.0 10.3 %collective-permute-start.3 = (bf16[128,1024]{1,0:T(8,128)(2,1)S(1)}, bf16[128,1024]{1,0:T(8,128)(2,1)S(1)}, u32[]{:S(2)}, u32[]{:S(2)}) collective-permute-start(bf16[128,1024]{1,0:T(8,128)(2,1)S(1)} %get-tuple-element.25), channel_id=1, source_target_pairs={{24,1},{25,22},{26,13},{27,15},{28,9},{29,23},{30,3},{31,14}} | collective-permute-start | bytes 786440 | tf_op jit(solution)/shard_map/ppermute | solution.py:133
  2.8 9.5 %collective-permute-start.2 = (bf16[128,768]{1,0:T(8,128)(2,1)S(1)}, bf16[128,768]{1,0:T(8,128)(2,1)S(1)}, u32[]{:S(2)}, u32[]{:S(2)}) collective-permute-start(bf16[128,768]{1,0:T(8,128)(2,1)S(1)} %get-tuple-element.24), channel_id=1, source_target_pairs={{16,0},{17,13},{18,22},{19,15},{20,14},{21,9},{23,2}} | collective-permute-start | bytes 589832 | tf_op jit(solution)/shard_map/ppermute | solution.py:133
  3.6 8.6 %collective-permute-start.1 = (bf16[128,512]{1,0:T(8,128)(2,1)S(1)}, bf16[128,512]{1,0:T(8,128)(2,1)S(1)}, u32[]{:S(2)}, u32[]{:S(2)}) collective-permute-start(bf16[128,512]{1,0:T(8,128)(2,1)S(1)} %get-tuple-element.23), channel_id=1, source_target_pairs={{4,0},{8,22},{10,2},{11,15},{12,1},{13,9},{14,23}} | collective-permute-start | bytes 393224 | tf_op jit(solution)/shard_map/ppermute | solution.py:133
  4.3 8.0 %collective-permute-start = (bf16[128,256]{1,0:T(8,128)(2,1)S(1)}, bf16[128,256]{1,0:T(8,128)(2,1)S(1)}, u32[]{:S(2)}, u32[]{:S(2)}) collective-permute-start(bf16[128,256]{1,0:T(8,128)(2,1)S(1)} %get-tuple-element.22), channel_id=1, source_target_pairs={{1,13},{2,15},{3,22},{5,9},{6,14},{7,23}} | collective-permute-start | bytes 196616 | tf_op jit(solution)/shard_map/ppermute | solution.py:133
  12.3 6.1 %collective-permute-start.4 = (bf16[128,2560]{1,0:T(8,128)(2,1)S(1)}, bf16[128,2560]{1,0:T(8,128)(2,1)S(1)}, u32[]{:S(2)}, u32[]{:S(2)}) collective-permute-start(bf16[128,2560]{1,0:T(8,128)(2,1)S(1)} %pack_kernel.1), channel_id=1, source_target_pairs={{0,1},{1,0},{2,3},{3,2},{4,5},{5,4},{6,7},{7,6},{8,12},{9,8},{10,1... | collective-permute-start | bytes 1966088 | tf_op jit(solution)/shard_map/ppermute | solution.py:129
  14.6 1.8 %collective-permute-start.5 = (bf16[256,128]{1,0:T(8,128)(2,1)S(1)}, bf16[256,128]{1,0:T(8,128)(2,1)S(1)}, u32[]{:S(2)}, u32[]{:S(2)}) collective-permute-start(bf16[256,128]{1,0:T(8,128)(2,1)S(1)} %first_kernel.1), channel_id=1, source_target_pairs={{0,4},{1,8},{2,12},{3,2},{4,5},{5,0},{6,7},{7,6},{8,9},{9,1},{10,1... | collective-permute-start | bytes 196616 | tf_op jit(solution)/shard_map/ppermute | solution.py:129
  14.7 1.7 %collective-permute-start.6 = (bf16[256,128]{1,0:T(8,128)(2,1)S(1)}, bf16[256,128]{1,0:T(8,128)(2,1)S(1)}, u32[]{:S(2)}, u32[]{:S(2)}) collective-permute-start(bf16[256,128]{1,0:T(8,128)(2,1)S(1)} %first_kernel.1), channel_id=1, source_target_pairs={{0,8},{1,12},{2,3},{3,4},{4,5},{5,0},{6,7},{7,6},{8,9},{9,1},{10,1... | collective-permute-start | bytes 196616 | tf_op jit(solution)/shard_map/ppermute | solution.py:129
  16.7 1.9 %collective-permute-start.9 = (bf16[1024,128]{1,0:T(8,128)(2,1)S(1)}, bf16[1024,128]{1,0:T(8,128)(2,1)S(1)}, u32[]{:S(2)}, u32[]{:S(2)}) collective-permute-start(bf16[1024,128]{1,0:T(8,128)(2,1)S(1)} %get-tuple-element.27), channel_id=1, source_target_pairs={{0,1},{1,0},{2,3},{3,2},{4,9},{5,4},{6,7},{7,6},{8,5},{9,8},{10,11... | collective-permute-start | bytes 786440 | tf_op jit(solution)/shard_map/ppermute | solution.py:129
  17.1 1.6 %collective-permute-start.10 = (bf16[1024,128]{1,0:T(8,128)(2,1)S(1)}, bf16[1024,128]{1,0:T(8,128)(2,1)S(1)}, u32[]{:S(2)}, u32[]{:S(2)}) collective-permute-start(bf16[1024,128]{1,0:T(8,128)(2,1)S(1)} %get-tuple-element.30.s_prev), channel_id=1, source_target_pairs={{0,1},{1,0},{2,3},{3,2},{4,5},{5,4},{6,7},{7,6},{8,9},{9,8},{10,11... | collective-permute-start | bytes 786440 | tf_op jit(solution)/shard_map/ppermute | solution.py:129
  18.7 1.6 %collective-permute-start.11 = (bf16[1024,128]{1,0:T(8,128)(2,1)S(1)}, bf16[1024,128]{1,0:T(8,128)(2,1)S(1)}, u32[]{:S(2)}, u32[]{:S(2)}) collective-permute-start(bf16[1024,128]{1,0:T(8,128)(2,1)S(1)} %get-tuple-element.31), channel_id=1, source_target_pairs={{0,1},{1,0},{2,3},{3,2},{4,5},{5,4},{6,7},{7,6},{8,9},{9,14},{10,1... | collective-permute-start | bytes 786440 | tf_op jit(solution)/shard_map/ppermute | solution.py:129
  19.2 1.5 %collective-permute-start.12 = (bf16[1024,128]{1,0:T(8,128)(2,1)S(1)}, bf16[1024,128]{1,0:T(8,128)(2,1)S(1)}, u32[]{:S(2)}, u32[]{:S(2)}) collective-permute-start(bf16[1024,128]{1,0:T(8,128)(2,1)S(1)} %step1_kernel.1.q_in.q_prev), channel_id=1, source_target_pairs={{0,1},{1,0},{2,3},{3,2},{4,5},{5,4},{6,7},{7,6},{8,9},{9,13},{10,1... | collective-permute-start | bytes 786440 | tf_op jit(solution)/shard_map/ppermute | solution.py:129
  19.3 1.8 %collective-permute-start.13 = (bf16[1024,128]{1,0:T(8,128)(2,1)S(1)}, bf16[1024,128]{1,0:T(8,128)(2,1)S(1)}, u32[]{:S(2)}, u32[]{:S(2)}) collective-permute-start(bf16[1024,128]{1,0:T(8,128)(2,1)S(1)} %step1_kernel.1.q_in.q_prev), channel_id=1, source_target_pairs={{0,1},{1,5},{2,3},{3,2},{4,0},{5,4},{6,7},{7,6},{8,16},{9,17},{10,... | collective-permute-start | bytes 786440 | tf_op jit(solution)/shard_map/ppermute | solution.py:129
  21.1 2.3 %collective-permute-start.14 = (bf16[1024,128]{1,0:T(8,128)(2,1)S(1)}, bf16[1024,128]{1,0:T(8,128)(2,1)S(1)}, u32[]{:S(2)}, u32[]{:S(2)}) collective-permute-start(bf16[1024,128]{1,0:T(8,128)(2,1)S(1)} %get-tuple-element.34), channel_id=1, source_target_pairs={{0,1},{1,0},{2,3},{3,2},{4,5},{5,4},{6,7},{7,6},{8,9},{9,8},{10,11... | collective-permute-start | bytes 786440 | tf_op jit(solution)/shard_map/ppermute | solution.py:129
  21.5 1.9 %collective-permute-start.15 = (bf16[1024,128]{1,0:T(8,128)(2,1)S(1)}, bf16[1024,128]{1,0:T(8,128)(2,1)S(1)}, u32[]{:S(2)}, u32[]{:S(2)}) collective-permute-start(bf16[1024,128]{1,0:T(8,128)(2,1)S(1)} %get-tuple-element.33.s_ref), channel_id=1, source_target_pairs={{0,1},{1,0},{2,3},{3,2},{4,5},{5,4},{6,7},{7,6},{8,9},{9,8},{10,11... | collective-permute-start | bytes 786440 | tf_op jit(solution)/shard_map/ppermute | solution.py:129
  21.7 1.8 %collective-permute-start.16 = (bf16[1024,128]{1,0:T(8,128)(2,1)S(1)}, bf16[1024,128]{1,0:T(8,128)(2,1)S(1)}, u32[]{:S(2)}, u32[]{:S(2)}) collective-permute-start(bf16[1024,128]{1,0:T(8,128)(2,1)S(1)} %get-tuple-element.35.refs_4_), channel_id=1, source_target_pairs={{0,1},{1,0},{2,3},{3,2},{4,5},{5,4},{6,7},{7,6},{8,9},{9,8},{10,11... | collective-permute-start | bytes 786440 | tf_op jit(solution)/shard_map/ppermute | solution.py:129
  22.1 1.4 %collective-permute-start.17 = (bf16[1024,128]{1,0:T(8,128)(2,1)S(1)}, bf16[1024,128]{1,0:T(8,128)(2,1)S(1)}, u32[]{:S(2)}, u32[]{:S(2)}) collective-permute-start(bf16[1024,128]{1,0:T(8,128)(2,1)S(1)} %get-tuple-element.35.refs_4_), channel_id=1, source_target_pairs={{14,30},{16,24},{20,28},{17,25},{13,5},{9,1}} | collective-permute-start | bytes 786440 | tf_op jit(solution)/shard_map/ppermute | solution.py:133
  23.5 2.7 %collective-permute-start.19 = (bf16[1024,128]{1,0:T(8,128)(2,1)S(1)}, bf16[1024,128]{1,0:T(8,128)(2,1)S(1)}, u32[]{:S(2)}, u32[]{:S(2)}) collective-permute-start(bf16[1024,128]{1,0:T(8,128)(2,1)S(1)} %step3_kernel.1.q_prev), channel_id=1, source_target_pairs={{23,27},{10,18}} | collective-permute-start | bytes 786440 | tf_op jit(solution)/shard_map/ppermute | solution.py:133
  24.2 2.1 %collective-permute-start.20 = (bf16[1024,128]{1,0:T(8,128)(2,1)S(1)}, bf16[1024,128]{1,0:T(8,128)(2,1)S(1)}, u32[]{:S(2)}, u32[]{:S(2)}) collective-permute-start(bf16[1024,128]{1,0:T(8,128)(2,1)S(1)} %step3_kernel.1.q_prev), channel_id=1, source_target_pairs={{23,19},{10,26}} | collective-permute-start | bytes 786440 | tf_op jit(solution)/shard_map/ppermute | solution.py:133
  24.9 1.4 %collective-permute-start.21 = (bf16[1024,128]{1,0:T(8,128)(2,1)S(1)}, bf16[1024,128]{1,0:T(8,128)(2,1)S(1)}, u32[]{:S(2)}, u32[]{:S(2)}) collective-permute-start(bf16[1024,128]{1,0:T(8,128)(2,1)S(1)} %step3_kernel.1.q_prev), channel_id=1, source_target_pairs={{23,31}} | collective-permute-start | bytes 786440 | tf_op jit(solution)/shard_map/ppermute | solution.py:133
  25.6 22.3 %collective-permute-start.22 = (bf16[1024,128]{1,0:T(8,128)(2,1)S(1)}, bf16[1024,128]{1,0:T(8,128)(2,1)S(1)}, u32[]{:S(2)}, u32[]{:S(2)}) collective-permute-start(bf16[1024,128]{1,0:T(8,128)(2,1)S(1)} %step3_kernel.1.q_prev), channel_id=1, source_target_pairs={{23,11},{10,2}} | collective-permute-start | bytes 786440 | tf_op jit(solution)/shard_map/ppermute | solution.py:133
  26.4 32.4 %collective-permute-start.23 = (bf16[1040,128]{1,0:T(8,128)(2,1)S(1)}, bf16[1040,128]{1,0:T(8,128)(2,1)S(1)}, u32[]{:S(2)}, u32[]{:S(2)}) collective-permute-start(bf16[1040,128]{1,0:T(8,128)(2,1)S(1)} %get-tuple-element.37.mine_ref), channel_id=1, source_target_pairs={{0,2},{1,3},{2,0},{3,1},{4,6},{5,7},{6,4},{7,5},{8,10},{9,11},{10,... | collective-permute-start | bytes 798728 | tf_op jit(solution)/shard_map/ppermute | solution.py:129
  47.9 10.9 %collective-permute-start.24 = (bf16[1024,128]{1,0:T(8,128)(2,1)S(1)}, bf16[1024,128]{1,0:T(8,128)(2,1)S(1)}, u32[]{:S(2)}, u32[]{:S(2)}) collective-permute-start(bf16[1024,128]{1,0:T(8,128)(2,1)S(1)} %relay_kernel.1.q_ref), channel_id=1, source_target_pairs={{11,15},{19,3},{31,7},{14,6}} | collective-permute-start | bytes 786440 | tf_op jit(solution)/shard_map/ppermute | solution.py:133
  49.2 9.6 %collective-permute-start.25 = (bf16[1040,128]{1,0:T(8,128)(2,1)S(1)}, bf16[1040,128]{1,0:T(8,128)(2,1)S(1)}, u32[]{:S(2)}, u32[]{:S(2)}) collective-permute-start(bf16[1040,128]{1,0:T(8,128)(2,1)S(1)} %get-tuple-element.37.mine_ref), channel_id=1, source_target_pairs={{0,1},{1,0},{2,3},{3,2},{4,5},{5,4},{6,7},{7,6},{8,9},{9,8},{10,11... | collective-permute-start | bytes 798728 | tf_op jit(solution)/shard_map/ppermute | solution.py:129
  58.8 1.5 %collective-permute-start.26 = (bf16[1040,128]{1,0:T(8,128)(2,1)S(1)}, bf16[1040,128]{1,0:T(8,128)(2,1)S(1)}, u32[]{:S(2)}, u32[]{:S(2)}) collective-permute-start(bf16[1040,128]{1,0:T(8,128)(2,1)S(1)} %collective-permute-done.23.across_ref), channel_id=1, source_target_pairs={{0,1},{1,0},{2,3},{3,2},{4,5},{5,4},{6,7},{7,6},{8,9},{9,8},{10,11... | collective-permute-start | bytes 798728 | tf_op jit(solution)/shard_map/ppermute | solution.py:129
  (7 other events, 46.1 us)

commit v27 on v26

--- a/solution.py
+++ b/solution.py
@@ -464,7 +464,13 @@
 
     wides = [pair_width(m, part) for m in range(NR // 2)]
     cuts = call(
-        cut_kernel, [jax.ShapeDtypeStruct((part, w), bf16) for w in wides], [diag_inv], [HBM], [ANY] * len(wides), [dma]
+        cut_kernel,
+        [jax.ShapeDtypeStruct((part, w), bf16) for w in wides],
+        [diag_inv],
+        [HBM],
+        [ANY] * len(wides),
+        [dma],
+        limit=60,
     )
     at_piece = {r: (0, c) for c, rows in enumerate(PIECES) for r in rows}
     parts = []

time: 61.7 us -> 67.4 us (1.092)
  starting transfers between devices: 41.6 us -> 44.8 us
  Pallas kernels: 2.42 us -> 5.53 us
  local copies, waits for them, and re-layouts: 1.32 us -> 0.01 us
  waiting for transfers between devices: 13.9 us -> 14.6 us
    ppermute x11, starting transfers between devices: 14.3 us -> 17.6 us  [send_only(): lax.ppermute(value, ('row', 'col'), [(a * NC + b, c * NC + d) for (a, b),...]
    pallas_call x13, Pallas kernels: 2.42 us -> 5.53 us  [call(): pl.pallas_call(kernel, out_shape=outs, in_specs=in_specs, out_specs=out_s...]
    unnamed x8 -> x6, local copies, waits for them, and re-layouts: 1.32 us -> 0.01 us
    ppermute x11, waiting for transfers between devices: 10.8 us -> 11.6 us  [send_only(): lax.ppermute(value, ('row', 'col'), [(a * NC + b, c * NC + d) for (a, b),...]
where the time goes in v27:
time: 67.4 us; the launch traced here: 67.1 us
  starting transfers between devices  44.8 us (66%)
  waiting for transfers between devices  14.6 us (22%)
  Pallas kernels  5.53 us (8%)
  between operations  2.21 us (3%)
    ppermute x16, starting transfers between devices, send(): lax.ppermute(value, ('row', 'col'), [(a * NC + b, c * NC + d) for (a, b),...  27.2 us
    ppermute x11, starting transfers between devices, send_only(): lax.ppermute(value, ('row', 'col'), [(a * NC + b, c * NC + d) for (a, b),...  17.6 us
    ppermute x11, waiting for transfers between devices, send_only(): lax.ppermute(value, ('row', 'col'), [(a * NC + b, c * NC + d) for (a, b),...  11.6 us
    pallas_call x13, Pallas kernels, call(): pl.pallas_call(kernel, out_shape=outs, in_specs=in_specs, out_specs=out_s...  5.53 us
    ppermute x16, waiting for transfers between devices, send(): lax.ppermute(value, ('row', 'col'), [(a * NC + b, c * NC + d) for (a, b),...  3.07 us
  transfers between devices with their start and end apart: 27, of which 10 were waited for; matrix products, arithmetic and copies ran while one was open for 0% of the time, Pallas kernels for 2%

profile of v27, /device:TPU:7, one launch (start us, length us, event | category | flops | bytes accessed | tf_op | source)
XLA Modules:
  0.0 67.1 jit_solution(4597830170218178041)
XLA Ops:
  0.6 3.1 %cut_kernel.1 = (bf16[128,256]{1,0:T(8,128)(2,1)}, bf16[128,512]{1,0:T(8,128)(2,1)}, bf16[128,768]{1,0:T(8,128)(2,1)}, bf16[128,1024]{1,0:T(8,128)(2,1)}) custom-call(bf16[4,128,1024]{2,1,0:T(8,128)(2,1)} %diag_ref.5), custom_call_target="tpu_custom_call" | custom-call | tf_op jit(solution)/shard_map/cut_kernel/pallas_call | solution.py:156
  3.8 0.8 %collective-permute-start.3 = (bf16[128,1024]{1,0:T(8,128)(2,1)}, bf16[128,1024]{1,0:T(8,128)(2,1)S(1)}, u32[]{:S(2)}, u32[]{:S(2)}) collective-permute-start(bf16[128,1024]{1,0:T(8,128)(2,1)} %get-tuple-element.25), channel_id=1, source_target_pairs={{24,1},{25,22},{26,13},{27,15},{28,9},{29,23},{30,3},{31,14}} | collective-permute-start | bytes 786440 | tf_op jit(solution)/shard_map/ppermute | solution.py:133
  4.6 0.7 %collective-permute-start.2 = (bf16[128,768]{1,0:T(8,128)(2,1)}, bf16[128,768]{1,0:T(8,128)(2,1)S(1)}, u32[]{:S(2)}, u32[]{:S(2)}) collective-permute-start(bf16[128,768]{1,0:T(8,128)(2,1)} %get-tuple-element.24), channel_id=1, source_target_pairs={{16,0},{17,13},{18,22},{19,15},{20,14},{21,9},{23,2}} | collective-permute-start | bytes 589832 | tf_op jit(solution)/shard_map/ppermute | solution.py:133
  5.3 0.7 collective-permute-start.1
  6.0 10.1 %collective-permute-start = (bf16[128,256]{1,0:T(8,128)(2,1)}, bf16[128,256]{1,0:T(8,128)(2,1)S(1)}, u32[]{:S(2)}, u32[]{:S(2)}) collective-permute-start(bf16[128,256]{1,0:T(8,128)(2,1)} %get-tuple-element.22), channel_id=1, source_target_pairs={{1,13},{2,15},{3,22},{5,9},{6,14},{7,23}} | collective-permute-start | bytes 196616 | tf_op jit(solution)/shard_map/ppermute | solution.py:133
  16.0 1.6 %collective-permute-done.refs_0_ = bf16[128,256]{1,0:T(8,128)(2,1)S(1)} collective-permute-done((bf16[128,256]{1,0:T(8,128)(2,1)}, bf16[128,256]{1,0:T(8,128)(2,1)S(1)}, u32[]{:S(2)}, u32[]{:S(2)}) %collective-permute-start) | collective-permute-done | bytes 65568 | tf_op jit(solution)/shard_map/ppermute | solution.py:133
  17.8 2.2 %collective-permute-start.4 = (bf16[128,2560]{1,0:T(8,128)(2,1)S(1)}, bf16[128,2560]{1,0:T(8,128)(2,1)S(1)}, u32[]{:S(2)}, u32[]{:S(2)}) collective-permute-start(bf16[128,2560]{1,0:T(8,128)(2,1)S(1)} %pack_kernel.1), channel_id=1, source_target_pairs={{0,1},{1,0},{2,3},{3,2},{4,5},{5,4},{6,7},{7,6},{8,12},{9,8},{10,1... | collective-permute-start | bytes 1966088 | tf_op jit(solution)/shard_map/ppermute | solution.py:129
  20.1 0.5 collective-permute-start.6
  21.1 0.7 collective-permute-done.5.g0
  24.1 0.4 collective-permute-start.11
  25.1 0.7 collective-permute-done.11.p_in
  26.5 0.4 collective-permute-start.14
  27.5 0.7 collective-permute-start.17
  28.1 0.7 %collective-permute-start.18 = (bf16[1024,128]{1,0:T(8,128)(2,1)S(1)}, bf16[1024,128]{1,0:T(8,128)(2,1)S(1)}, u32[]{:S(2)}, u32[]{:S(2)}) collective-permute-start(bf16[1024,128]{1,0:T(8,128)(2,1)S(1)} %get-tuple-element.35.refs_4_), channel_id=1, source_target_pairs={{14,22},{13,29},{17,21}} | collective-permute-start | bytes 786440 | tf_op jit(solution)/shard_map/ppermute | solution.py:133
  28.9 0.7 %collective-permute-start.19 = (bf16[1024,128]{1,0:T(8,128)(2,1)S(1)}, bf16[1024,128]{1,0:T(8,128)(2,1)S(1)}, u32[]{:S(2)}, u32[]{:S(2)}) collective-permute-start(bf16[1024,128]{1,0:T(8,128)(2,1)S(1)} %step3_kernel.1.q_prev), channel_id=1, source_target_pairs={{23,27},{10,18}} | collective-permute-start | bytes 786440 | tf_op jit(solution)/shard_map/ppermute | solution.py:133
  29.6 0.7 %collective-permute-start.20 = (bf16[1024,128]{1,0:T(8,128)(2,1)S(1)}, bf16[1024,128]{1,0:T(8,128)(2,1)S(1)}, u32[]{:S(2)}, u32[]{:S(2)}) collective-permute-start(bf16[1024,128]{1,0:T(8,128)(2,1)S(1)} %step3_kernel.1.q_prev), channel_id=1, source_target_pairs={{23,19},{10,26}} | collective-permute-start | bytes 786440 | tf_op jit(solution)/shard_map/ppermute | solution.py:133
  30.3 0.7 %collective-permute-start.21 = (bf16[1024,128]{1,0:T(8,128)(2,1)S(1)}, bf16[1024,128]{1,0:T(8,128)(2,1)S(1)}, u32[]{:S(2)}, u32[]{:S(2)}) collective-permute-start(bf16[1024,128]{1,0:T(8,128)(2,1)S(1)} %step3_kernel.1.q_prev), channel_id=1, source_target_pairs={{23,31}} | collective-permute-start | bytes 786440 | tf_op jit(solution)/shard_map/ppermute | solution.py:133
  31.0 0.7 %collective-permute-start.22 = (bf16[1024,128]{1,0:T(8,128)(2,1)S(1)}, bf16[1024,128]{1,0:T(8,128)(2,1)S(1)}, u32[]{:S(2)}, u32[]{:S(2)}) collective-permute-start(bf16[1024,128]{1,0:T(8,128)(2,1)S(1)} %step3_kernel.1.q_prev), channel_id=1, source_target_pairs={{23,11},{10,2}} | collective-permute-start | bytes 786440 | tf_op jit(solution)/shard_map/ppermute | solution.py:133
  31.8 21.4 %collective-permute-start.23 = (bf16[1040,128]{1,0:T(8,128)(2,1)S(1)}, bf16[1040,128]{1,0:T(8,128)(2,1)S(1)}, u32[]{:S(2)}, u32[]{:S(2)}) collective-permute-start(bf16[1040,128]{1,0:T(8,128)(2,1)S(1)} %get-tuple-element.37.mine_ref), channel_id=1, source_target_pairs={{0,2},{1,3},{2,0},{3,1},{4,6},{5,7},{6,4},{7,5},{8,10},{9,11},{10,... | collective-permute-start | bytes 798728 | tf_op jit(solution)/shard_map/ppermute | solution.py:129
  53.2 1.3 %collective-permute-start.24 = (bf16[1024,128]{1,0:T(8,128)(2,1)S(1)}, bf16[1024,128]{1,0:T(8,128)(2,1)S(1)}, u32[]{:S(2)}, u32[]{:S(2)}) collective-permute-start(bf16[1024,128]{1,0:T(8,128)(2,1)S(1)} %relay_kernel.1.q_ref), channel_id=1, source_target_pairs={{11,15},{19,3},{31,7},{14,6}} | collective-permute-start | bytes 786440 | tf_op jit(solution)/shard_map/ppermute | solution.py:133
  54.6 9.9 %collective-permute-done.24.rest_ref = bf16[1024,128]{1,0:T(8,128)(2,1)S(1)} collective-permute-done((bf16[1024,128]{1,0:T(8,128)(2,1)S(1)}, bf16[1024,128]{1,0:T(8,128)(2,1)S(1)}, u32[]{:S(2)}, u32[]{:S(2)}) %collective-permute-start.24) | collective-permute-done | bytes 262176 | tf_op jit(solution)/shard_map/ppermute | solution.py:133
  64.5 0.9 %half_kernel.1 = (f32[1024,128]{1,0:T(8,128)}, f32[2,1024,128]{2,1,0:T(8,128)S(1)}) custom-call(bf16[1024,128]{1,0:T(8,128)(2,1)S(1)} %relay_kernel.1.q_ref, bf16[1024,128]{1,0:T(8,128)(2,1)S(1)} %collective-permute-done.24.rest_ref, f32[2,1024,128]{2,1,0:T(8,128)S(1)} %bitcast.14, bf16[1040,128]{1,0:T(8,128)(2,1)S(1)} %get-tuple-element.37.mine_ref, ...), custom_call_target="tpu_custom_call" | custom-call | tf_op jit(solution)/shard_map/half_kernel/pallas_call | solution.py:156
  65.4 0.7 %collective-permute-done.26.corner_ref = bf16[1040,128]{1,0:T(8,128)(2,1)S(1)} collective-permute-done((bf16[1040,128]{1,0:T(8,128)(2,1)S(1)}, bf16[1040,128]{1,0:T(8,128)(2,1)S(1)}, u32[]{:S(2)}, u32[]{:S(2)}) %collective-permute-start.26) | collective-permute-done | bytes 266272 | tf_op jit(solution)/shard_map/ppermute | solution.py:129
  66.1 1.1 %final_kernel.1 = f32[2,1024,128]{2,1,0:T(8,128)} custom-call(f32[2,1024,128]{2,1,0:T(8,128)S(1)} %get-tuple-element.41.half_ref, bf16[1040,128]{1,0:T(8,128)(2,1)S(1)} %collective-permute-done.26.corner_ref), custom_call_target="tpu_custom_call" | custom-call | tf_op jit(solution)/shard_map/final_kernel/pallas_call | solution.py:156
  (49 shorter events, 3.8 us)
Async XLA Ops:
  3.8 13.9 %collective-permute-start.3 = (bf16[128,1024]{1,0:T(8,128)(2,1)}, bf16[128,1024]{1,0:T(8,128)(2,1)S(1)}, u32[]{:S(2)}, u32[]{:S(2)}) collective-permute-start(bf16[128,1024]{1,0:T(8,128)(2,1)} %get-tuple-element.25), channel_id=1, source_target_pairs={{24,1},{25,22},{26,13},{27,15},{28,9},{29,23},{30,3},{31,14}} | collective-permute-start | bytes 786440 | tf_op jit(solution)/shard_map/ppermute | solution.py:133
  4.6 13.1 %collective-permute-start.2 = (bf16[128,768]{1,0:T(8,128)(2,1)}, bf16[128,768]{1,0:T(8,128)(2,1)S(1)}, u32[]{:S(2)}, u32[]{:S(2)}) collective-permute-start(bf16[128,768]{1,0:T(8,128)(2,1)} %get-tuple-element.24), channel_id=1, source_target_pairs={{16,0},{17,13},{18,22},{19,15},{20,14},{21,9},{23,2}} | collective-permute-start | bytes 589832 | tf_op jit(solution)/shard_map/ppermute | solution.py:133
  5.3 12.4 %collective-permute-start.1 = (bf16[128,512]{1,0:T(8,128)(2,1)}, bf16[128,512]{1,0:T(8,128)(2,1)S(1)}, u32[]{:S(2)}, u32[]{:S(2)}) collective-permute-start(bf16[128,512]{1,0:T(8,128)(2,1)} %get-tuple-element.23), channel_id=1, source_target_pairs={{4,0},{8,22},{10,2},{11,15},{12,1},{13,9},{14,23}} | collective-permute-start | bytes 393224 | tf_op jit(solution)/shard_map/ppermute | solution.py:133
  6.0 11.7 %collective-permute-start = (bf16[128,256]{1,0:T(8,128)(2,1)}, bf16[128,256]{1,0:T(8,128)(2,1)S(1)}, u32[]{:S(2)}, u32[]{:S(2)}) collective-permute-start(bf16[128,256]{1,0:T(8,128)(2,1)} %get-tuple-element.22), channel_id=1, source_target_pairs={{1,13},{2,15},{3,22},{5,9},{6,14},{7,23}} | collective-permute-start | bytes 196616 | tf_op jit(solution)/shard_map/ppermute | solution.py:133
  17.8 6.1 %collective-permute-start.4 = (bf16[128,2560]{1,0:T(8,128)(2,1)S(1)}, bf16[128,2560]{1,0:T(8,128)(2,1)S(1)}, u32[]{:S(2)}, u32[]{:S(2)}) collective-permute-start(bf16[128,2560]{1,0:T(8,128)(2,1)S(1)} %pack_kernel.1), channel_id=1, source_target_pairs={{0,1},{1,0},{2,3},{3,2},{4,5},{5,4},{6,7},{7,6},{8,12},{9,8},{10,1... | collective-permute-start | bytes 1966088 | tf_op jit(solution)/shard_map/ppermute | solution.py:129
  20.0 1.8 %collective-permute-start.5 = (bf16[256,128]{1,0:T(8,128)(2,1)S(1)}, bf16[256,128]{1,0:T(8,128)(2,1)S(1)}, u32[]{:S(2)}, u32[]{:S(2)}) collective-permute-start(bf16[256,128]{1,0:T(8,128)(2,1)S(1)} %first_kernel.1), channel_id=1, source_target_pairs={{0,4},{1,8},{2,12},{3,2},{4,5},{5,0},{6,7},{7,6},{8,9},{9,1},{10,1... | collective-permute-start | bytes 196616 | tf_op jit(solution)/shard_map/ppermute | solution.py:129
  20.1 1.7 %collective-permute-start.6 = (bf16[256,128]{1,0:T(8,128)(2,1)S(1)}, bf16[256,128]{1,0:T(8,128)(2,1)S(1)}, u32[]{:S(2)}, u32[]{:S(2)}) collective-permute-start(bf16[256,128]{1,0:T(8,128)(2,1)S(1)} %first_kernel.1), channel_id=1, source_target_pairs={{0,8},{1,12},{2,3},{3,4},{4,5},{5,0},{6,7},{7,6},{8,9},{9,1},{10,1... | collective-permute-start | bytes 196616 | tf_op jit(solution)/shard_map/ppermute | solution.py:129
  22.1 1.9 %collective-permute-start.9 = (bf16[1024,128]{1,0:T(8,128)(2,1)S(1)}, bf16[1024,128]{1,0:T(8,128)(2,1)S(1)}, u32[]{:S(2)}, u32[]{:S(2)}) collective-permute-start(bf16[1024,128]{1,0:T(8,128)(2,1)S(1)} %get-tuple-element.27), channel_id=1, source_target_pairs={{0,1},{1,0},{2,3},{3,2},{4,9},{5,4},{6,7},{7,6},{8,5},{9,8},{10,11... | collective-permute-start | bytes 786440 | tf_op jit(solution)/shard_map/ppermute | solution.py:129
  22.5 1.6 %collective-permute-start.10 = (bf16[1024,128]{1,0:T(8,128)(2,1)S(1)}, bf16[1024,128]{1,0:T(8,128)(2,1)S(1)}, u32[]{:S(2)}, u32[]{:S(2)}) collective-permute-start(bf16[1024,128]{1,0:T(8,128)(2,1)S(1)} %get-tuple-element.30.s_prev), channel_id=1, source_target_pairs={{0,1},{1,0},{2,3},{3,2},{4,5},{5,4},{6,7},{7,6},{8,9},{9,8},{10,11... | collective-permute-start | bytes 786440 | tf_op jit(solution)/shard_map/ppermute | solution.py:129
  24.1 1.6 %collective-permute-start.11 = (bf16[1024,128]{1,0:T(8,128)(2,1)S(1)}, bf16[1024,128]{1,0:T(8,128)(2,1)S(1)}, u32[]{:S(2)}, u32[]{:S(2)}) collective-permute-start(bf16[1024,128]{1,0:T(8,128)(2,1)S(1)} %get-tuple-element.31), channel_id=1, source_target_pairs={{0,1},{1,0},{2,3},{3,2},{4,5},{5,4},{6,7},{7,6},{8,9},{9,14},{10,1... | collective-permute-start | bytes 786440 | tf_op jit(solution)/shard_map/ppermute | solution.py:129
  24.6 1.5 %collective-permute-start.12 = (bf16[1024,128]{1,0:T(8,128)(2,1)S(1)}, bf16[1024,128]{1,0:T(8,128)(2,1)S(1)}, u32[]{:S(2)}, u32[]{:S(2)}) collective-permute-start(bf16[1024,128]{1,0:T(8,128)(2,1)S(1)} %step1_kernel.1.q_in.q_prev), channel_id=1, source_target_pairs={{0,1},{1,0},{2,3},{3,2},{4,5},{5,4},{6,7},{7,6},{8,9},{9,13},{10,1... | collective-permute-start | bytes 786440 | tf_op jit(solution)/shard_map/ppermute | solution.py:129
  24.7 1.8 %collective-permute-start.13 = (bf16[1024,128]{1,0:T(8,128)(2,1)S(1)}, bf16[1024,128]{1,0:T(8,128)(2,1)S(1)}, u32[]{:S(2)}, u32[]{:S(2)}) collective-permute-start(bf16[1024,128]{1,0:T(8,128)(2,1)S(1)} %step1_kernel.1.q_in.q_prev), channel_id=1, source_target_pairs={{0,1},{1,5},{2,3},{3,2},{4,0},{5,4},{6,7},{7,6},{8,16},{9,17},{10,... | collective-permute-start | bytes 786440 | tf_op jit(solution)/shard_map/ppermute | solution.py:129
  26.5 2.3 %collective-permute-start.14 = (bf16[1024,128]{1,0:T(8,128)(2,1)S(1)}, bf16[1024,128]{1,0:T(8,128)(2,1)S(1)}, u32[]{:S(2)}, u32[]{:S(2)}) collective-permute-start(bf16[1024,128]{1,0:T(8,128)(2,1)S(1)} %get-tuple-element.34), channel_id=1, source_target_pairs={{0,1},{1,0},{2,3},{3,2},{4,5},{5,4},{6,7},{7,6},{8,9},{9,8},{10,11... | collective-permute-start | bytes 786440 | tf_op jit(solution)/shard_map/ppermute | solution.py:129
  26.9 1.9 %collective-permute-start.15 = (bf16[1024,128]{1,0:T(8,128)(2,1)S(1)}, bf16[1024,128]{1,0:T(8,128)(2,1)S(1)}, u32[]{:S(2)}, u32[]{:S(2)}) collective-permute-start(bf16[1024,128]{1,0:T(8,128)(2,1)S(1)} %get-tuple-element.33.s_ref), channel_id=1, source_target_pairs={{0,1},{1,0},{2,3},{3,2},{4,5},{5,4},{6,7},{7,6},{8,9},{9,8},{10,11... | collective-permute-start | bytes 786440 | tf_op jit(solution)/shard_map/ppermute | solution.py:129
  27.1 1.8 %collective-permute-start.16 = (bf16[1024,128]{1,0:T(8,128)(2,1)S(1)}, bf16[1024,128]{1,0:T(8,128)(2,1)S(1)}, u32[]{:S(2)}, u32[]{:S(2)}) collective-permute-start(bf16[1024,128]{1,0:T(8,128)(2,1)S(1)} %get-tuple-element.35.refs_4_), channel_id=1, source_target_pairs={{0,1},{1,0},{2,3},{3,2},{4,5},{5,4},{6,7},{7,6},{8,9},{9,8},{10,11... | collective-permute-start | bytes 786440 | tf_op jit(solution)/shard_map/ppermute | solution.py:129
  27.5 1.4 %collective-permute-start.17 = (bf16[1024,128]{1,0:T(8,128)(2,1)S(1)}, bf16[1024,128]{1,0:T(8,128)(2,1)S(1)}, u32[]{:S(2)}, u32[]{:S(2)}) collective-permute-start(bf16[1024,128]{1,0:T(8,128)(2,1)S(1)} %get-tuple-element.35.refs_4_), channel_id=1, source_target_pairs={{14,30},{16,24},{20,28},{17,25},{13,5},{9,1}} | collective-permute-start | bytes 786440 | tf_op jit(solution)/shard_map/ppermute | solution.py:133
  28.9 2.7 %collective-permute-start.19 = (bf16[1024,128]{1,0:T(8,128)(2,1)S(1)}, bf16[1024,128]{1,0:T(8,128)(2,1)S(1)}, u32[]{:S(2)}, u32[]{:S(2)}) collective-permute-start(bf16[1024,128]{1,0:T(8,128)(2,1)S(1)} %step3_kernel.1.q_prev), channel_id=1, source_target_pairs={{23,27},{10,18}} | collective-permute-start | bytes 786440 | tf_op jit(solution)/shard_map/ppermute | solution.py:133
  29.6 2.1 %collective-permute-start.20 = (bf16[1024,128]{1,0:T(8,128)(2,1)S(1)}, bf16[1024,128]{1,0:T(8,128)(2,1)S(1)}, u32[]{:S(2)}, u32[]{:S(2)}) collective-permute-start(bf16[1024,128]{1,0:T(8,128)(2,1)S(1)} %step3_kernel.1.q_prev), channel_id=1, source_target_pairs={{23,19},{10,26}} | collective-permute-start | bytes 786440 | tf_op jit(solution)/shard_map/ppermute | solution.py:133
  30.3 1.4 %collective-permute-start.21 = (bf16[1024,128]{1,0:T(8,128)(2,1)S(1)}, bf16[1024,128]{1,0:T(8,128)(2,1)S(1)}, u32[]{:S(2)}, u32[]{:S(2)}) collective-permute-start(bf16[1024,128]{1,0:T(8,128)(2,1)S(1)} %step3_kernel.1.q_prev), channel_id=1, source_target_pairs={{23,31}} | collective-permute-start | bytes 786440 | tf_op jit(solution)/shard_map/ppermute | solution.py:133
  31.0 22.2 %collective-permute-start.22 = (bf16[1024,128]{1,0:T(8,128)(2,1)S(1)}, bf16[1024,128]{1,0:T(8,128)(2,1)S(1)}, u32[]{:S(2)}, u32[]{:S(2)}) collective-permute-start(bf16[1024,128]{1,0:T(8,128)(2,1)S(1)} %step3_kernel.1.q_prev), channel_id=1, source_target_pairs={{23,11},{10,2}} | collective-permute-start | bytes 786440 | tf_op jit(solution)/shard_map/ppermute | solution.py:133
  31.8 32.7 %collective-permute-start.23 = (bf16[1040,128]{1,0:T(8,128)(2,1)S(1)}, bf16[1040,128]{1,0:T(8,128)(2,1)S(1)}, u32[]{:S(2)}, u32[]{:S(2)}) collective-permute-start(bf16[1040,128]{1,0:T(8,128)(2,1)S(1)} %get-tuple-element.37.mine_ref), channel_id=1, source_target_pairs={{0,2},{1,3},{2,0},{3,1},{4,6},{5,7},{6,4},{7,5},{8,10},{9,11},{10,... | collective-permute-start | bytes 798728 | tf_op jit(solution)/shard_map/ppermute | solution.py:129
  53.2 11.3 %collective-permute-start.24 = (bf16[1024,128]{1,0:T(8,128)(2,1)S(1)}, bf16[1024,128]{1,0:T(8,128)(2,1)S(1)}, u32[]{:S(2)}, u32[]{:S(2)}) collective-permute-start(bf16[1024,128]{1,0:T(8,128)(2,1)S(1)} %relay_kernel.1.q_ref), channel_id=1, source_target_pairs={{11,15},{19,3},{31,7},{14,6}} | collective-permute-start | bytes 786440 | tf_op jit(solution)/shard_map/ppermute | solution.py:133
  54.5 10.0 %collective-permute-start.25 = (bf16[1040,128]{1,0:T(8,128)(2,1)S(1)}, bf16[1040,128]{1,0:T(8,128)(2,1)S(1)}, u32[]{:S(2)}, u32[]{:S(2)}) collective-permute-start(bf16[1040,128]{1,0:T(8,128)(2,1)S(1)} %get-tuple-element.37.mine_ref), channel_id=1, source_target_pairs={{0,1},{1,0},{2,3},{3,2},{4,5},{5,4},{6,7},{7,6},{8,9},{9,8},{10,11... | collective-permute-start | bytes 798728 | tf_op jit(solution)/shard_map/ppermute | solution.py:129
  64.5 1.5 %collective-permute-start.26 = (bf16[1040,128]{1,0:T(8,128)(2,1)S(1)}, bf16[1040,128]{1,0:T(8,128)(2,1)S(1)}, u32[]{:S(2)}, u32[]{:S(2)}) collective-permute-start(bf16[1040,128]{1,0:T(8,128)(2,1)S(1)} %collective-permute-done.23.across_ref), channel_id=1, source_target_pairs={{0,1},{1,0},{2,3},{3,2},{4,5},{5,4},{6,7},{7,6},{8,9},{9,8},{10,11... | collective-permute-start | bytes 798728 | tf_op jit(solution)/shard_map/ppermute | solution.py:129
  (6 other events, 60.5 us)
